TPU v7x, 32 devices: a whole 2x2x4 slice. The times are simulated.
32 devices in a mesh: groups: 2 (over x), req: 4 (over y, core), tp: 4 (over z).
Axes of the slice: x: 2, y: 2, z: 4, core: 2. Of those that a mesh axis runs over, the one named last changes fastest.
Arguments:
- attention_rows: bfloat16 [4096, 8192], P(('groups', 'req'), 'tp'), parts along dimension 0, may hold values from -6 to 6
- output_weight_matrix: bfloat16 [8192, 4096], P('tp'), may hold values from -0.0625 to 0.0625
- adapter_down_maps: bfloat16 [1024, 16, 8192], P(('groups', 'req'), None, 'tp'), parts along dimension 0, may hold values from -0.0625 to 0.0625
- adapter_up_maps: bfloat16 [1024, 16, 4096], P(('groups', 'req'), None, 'tp'), parts along dimension 0, may hold values from -1.5 to 1.5
- adapter_pool_slot: int32 [1024], P('groups'), parts along dimension 0, may hold values from 0 to 511, as said below
- segment_adapter_ids: int32 [8, 12], P(('groups', 'req')), parts along dimension 0, may hold values from 0 to 511, as said below
- segment_row_count: int32 [8, 12], P(('groups', 'req')), parts along dimension 0, may hold values from 1 to 128, 512 in all within a row
Outputs:
- mixed: bfloat16 [4096, 4096], P(('groups', 'req'), 'tp'), parts along dimension 0
There are 2 independent parts, one for each index of `groups`. A program takes and returns all parts, laid end to end along the dimension named above; an argument that names none is the same for every part. Nothing has to cross between parts.
Inputs may be any that keep to these rules, and one draw needn't show every extreme that they name: adapter_pool_slot is a permutation of the slots; slots j * 128 to (j + 1) * 128 - 1 form pool share j. `segment_adapter_ids`: in each request group, at most 6 segments name adapters whose slots lie in any one pool share, and exactly 6 for some share. `segment_row_count`: each request group's lengths sum to 512, the longest exactly 128.
All inputs are finite; a program needn't handle non-finite values.
Results may differ from a plain program's by a relative error of at most 0.014.
Values may be sent and summed in bfloat16 or wider, within the bound.
No kernel may reach another device: no remote copies, remote signals or barrier semaphores. Data moves between devices by JAX's collectives and lax.ppermute only.
A program may use at most 192 MiB of HBM per device.

v0:
```python
import jax
import jax.numpy as jnp
from jax import lax
from jax.sharding import PartitionSpec as P


def local(
    attention_rows,
    output_weight_matrix,
    adapter_down_maps,
    adapter_up_maps,
    adapter_pool_slot,
    segment_adapter_ids,
    segment_row_count,
):
    row_total = attention_rows.shape[0]
    seg_total = segment_row_count.shape[1]
    rank_extent = adapter_down_maps.shape[1]
    table_size = adapter_pool_slot.shape[0]
    lengths = segment_row_count[0]
    wanted_adapter = segment_adapter_ids[0]
    seg_ends = jnp.cumsum(lengths)
    row_segment = jnp.sum(
        (seg_ends[None, :] <= jnp.arange(row_total)[:, None]).astype(jnp.int32), axis=1
    )
    member = row_segment[:, None] == jnp.arange(seg_total)[None, :]
    slot_ids = jnp.sum(
        jnp.where(
            wanted_adapter[:, None] == jnp.arange(table_size)[None, :],
            adapter_pool_slot[None, :],
            0,
        ),
        axis=1,
    )
    pieces = (
        lax.all_gather(adapter_down_maps, "req", axis=0, tiled=True),
        lax.all_gather(adapter_up_maps, "req", axis=0, tiled=True),
    )
    piece_rows = pieces[0].shape[0]
    picker = (slot_ids[:, None] == jnp.arange(piece_rows)[None, :]).astype(jnp.bfloat16)
    next_down = jnp.einsum("sn,nrd->srd", picker, pieces[0], preferred_element_type=jnp.float32)
    next_up = jnp.einsum("sn,nrd->srd", picker, pieces[1], preferred_element_type=jnp.float32)
    sel_down = next_down
    sel_up = next_up
    sel_down = sel_down.astype(jnp.bfloat16)
    sel_up = sel_up.astype(jnp.bfloat16)
    all_low = jnp.einsum(
        "id,srd->isr", attention_rows, sel_down, preferred_element_type=jnp.float32
    )
    low_part = jnp.sum(jnp.where(member[:, :, None], all_low, jnp.zeros((), jnp.float32)), axis=1)
    rank_reduced = lax.psum(low_part.astype(jnp.bfloat16), "tp")
    spread = jnp.where(member[:, :, None], rank_reduced[:, None, :], jnp.zeros((), jnp.bfloat16))
    spread = spread.reshape(row_total, seg_total * rank_extent)
    adapter_term = jnp.dot(
        spread, sel_up.reshape(seg_total * rank_extent, -1), preferred_element_type=jnp.float32
    )
    base_part = jnp.dot(attention_rows, output_weight_matrix, preferred_element_type=jnp.float32)
    base_product = lax.psum_scatter(
        base_part.astype(jnp.bfloat16), "tp", scatter_dimension=1, tiled=True
    ).astype(jnp.float32)
    return (base_product + adapter_term).astype(jnp.bfloat16)


def solution(mesh):
    return jax.shard_map(
        local,
        mesh=mesh,
        in_specs=(
            P(("groups", "req"), "tp"),
            P("tp", None),
            P(("groups", "req"), None, "tp"),
            P(("groups", "req"), None, "tp"),
            P("groups"),
            P(("groups", "req"), None),
            P(("groups", "req"), None),
        ),
        out_specs=P(("groups", "req"), "tp"),
        check_vma=False,
    )
```

profile of v0, /device:TPU:0, one launch (start us, length us, event | category | flops | bytes accessed | tf_op | source)
XLA Modules:
  0.0 429.6 jit_solution(12857870627794645139)
XLA Ops:
  7.4 0.0 copy-start
  7.4 0.0 all-gather.5.cloned.1.call-start
  7.4 0.7 all-gather.5.cloned.1.call-update
  8.1 0.0 all-gather.3.cloned.1.call-start
  8.1 0.7 all-gather.3.cloned.1.call-update
  8.8 0.0 copy-start.3
  8.9 0.0 copy-start.1
  8.9 0.0 copy-start.2
  8.9 0.0 reduce-scatter.2.cloned.1.call-start
  8.9 0.0 copy-done
  9.0 13.8 %convolution_convert_fusion = bf16[512,4096]{1,0:T(8,128)(2,1)} fusion(bf16[512,2048]{1,0:T(8,128)(2,1)S(1)} %copy-done, bf16[2048,4096]{1,0:T(8,128)(2,1)} %param.8), kind=kOutput, calls=%fused_computation.4 | convolution fusion | flops 8592031744 | bytes 23068672 | tf_op jit(solution)/shard_map/dot_general | solution.py:57
  22.7 0.0 reduce-scatter.2.cloned.1.call-update
  22.8 0.0 copy-done.3
  22.8 0.2 reduce-window.8
  23.0 0.1 convert_reduce_fusion
  23.0 0.0 copy-done.1
  23.1 0.0 copy-done.2
  23.1 0.2 select_reduce_fusion
  23.3 95.3 %all-gather.5.cloned.1.call-done = bf16[512,16,1024]{2,1,0:T(8,128)(2,1)} async-done(((bf16[128,16,1024]{2,1,0:T(8,128)(2,1)}), bf16[512,16,1024]{2,1,0:T(8,128)(2,1)}) %all-gather.5.cloned.1.call-update) | async-done | bytes 16777232 | tf_op jit(solution)/shard_map/all_gather | solution.py:37
  118.5 27.6 %fusion.10 = bf16[12,16,1024]{2,0,1:T(8,128)(2,1)S(1)} fusion(bf16[512,16,1024]{2,1,0:T(8,128)(2,1)} %all-gather.5.cloned.1.call-done, s32[12]{0:T(128)S(1)} %select_reduce_fusion), kind=kOutput, calls=%fused_computation.10 | convolution fusion | flops 201529344 | bytes 17170480 | tf_op jit(solution)/shard_map/sn,nrd->srd/dot_general | solution.py:42
  146.2 175.5 %all-gather.3.cloned.1.call-done = bf16[512,16,2048]{2,1,0:T(8,128)(2,1)} async-done(((bf16[128,16,2048]{2,1,0:T(8,128)(2,1)}), bf16[512,16,2048]{2,1,0:T(8,128)(2,1)}) %all-gather.3.cloned.1.call-update) | async-done | bytes 33554448 | tf_op jit(solution)/shard_map/all_gather | solution.py:36
  321.7 78.6 %fusion.8 = f32[12,16,512]{2,0,1:T(8,128)S(1)} fusion(bf16[512,2048]{1,0:T(8,128)(2,1)S(1)} %copy-done, bf16[512,16,2048]{2,1,0:T(8,128)(2,1)} %all-gather.3.cloned.1.call-done, s32[12]{0:T(128)S(1)} %select_reduce_fusion), kind=kOutput, calls=%fused_computation.8 | convolution fusion | flops 805705728 | bytes 36044848 | tf_op jit(solution)/shard_map/id,srd->isr/dot_general | solution.py:47
  400.2 0.2 fusion.15
  400.5 18.7 %psum.7 = bf16[512,16]{0,1:T(8,128)(2,1)S(1)} all-reduce(bf16[512,16]{0,1:T(8,128)(2,1)S(1)} %fusion.15), channel_id=1, replica_groups=mesh['groups'=2,'req'=4,'tp'=4] {'tp'}, use_global_device_ids=true, to_apply=%region_5.6 | all-reduce | flops 8192 | bytes 32768 | tf_op jit(solution)/shard_map/psum | solution.py:51
  419.2 0.0 reduce-scatter.2.cloned.1.call-done
  419.2 2.8 fusion.7
  (1 shorter events, 0.0 us)
Async XLA Ops:
  7.4 1.6 copy-start
  7.4 111.2 %all-gather.5.cloned.1.call-start = ((), (), s32[]{:S(2)}) async-start(), calls=%async_computation.3 | async-start | bytes 20971520 | tf_op jit(solution)/shard_map/all_gather | solution.py:37
  8.1 313.6 %all-gather.3.cloned.1.call-start = ((), (), s32[]{:S(2)}) async-start(), calls=%async_computation.2 | async-start | bytes 41943040 | tf_op jit(solution)/shard_map/all_gather | solution.py:36
  8.8 13.9 %copy-start.3 = (s32[1,12]{1,0:T(1,128)S(1)}, s32[1,12]{1,0:T(1,128)}, u32[]{:S(2)}) copy-start(s32[1,12]{1,0:T(1,128)} %param.13) | copy-start | bytes 148
  8.9 14.2 %copy-start.1 = (s32[512]{0:T(512)S(1)}, s32[512]{0:T(512)}, u32[]{:S(2)}) copy-start(s32[512]{0:T(512)} %param.11) | copy-start | bytes 6148
  8.9 14.2 %copy-start.2 = (s32[1,12]{1,0:T(1,128)S(1)}, s32[1,12]{1,0:T(1,128)}, u32[]{:S(2)}) copy-start(s32[1,12]{1,0:T(1,128)} %param.12) | copy-start | bytes 148
  8.9 410.4 %reduce-scatter.2.cloned.1.call-start = ((), (), s32[]{:S(2)}) async-start(), calls=%async_computation.1 | async-start | bytes 5242880 | tf_op jit(solution)/shard_map/reduce_scatter | solution.py:58
Sparse Core Ops, SparseCore 0:
  9.8 108.6 all-gather.4
  120.2 201.4 all-gather.2
Sparse Core Ops, SparseCore 1:
  22.8 79.4 reduce-scatter.1
where the time goes:
time: 433 us; the launch traced here: 430 us
  waiting for transfers between devices  272 us (63%)
  matrix products  123 us (28%)
  blocking collectives  18.7 us (4%)
  between operations  15.1 us (3%)
    all_gather x1, waiting for transfers between devices, local(): lax.all_gather(adapter_down_maps, 'req', axis=0, tiled=True)  175 us
    all_gather x1, waiting for transfers between devices, local(): lax.all_gather(adapter_up_maps, 'req', axis=0, tiled=True)  95.3 us
    dot_general x1, matrix products, local(): jnp.einsum('id,srd->isr', attention_rows, sel_down, preferred_element_typ...  78.6 us
    dot_general x1, matrix products, local(): jnp.einsum('sn,nrd->srd', picker, pieces[1], preferred_element_type=jnp.f...  27.6 us
    psum x1, blocking collectives, local(): rank_reduced = lax.psum(low_part.astype(jnp.bfloat16), 'tp')  18.7 us
    dot_general x1, matrix products, local(): jnp.dot(attention_rows, output_weight_matrix, preferred_element_type=jnp....  13.8 us
  transfers between devices with their start and end apart: 3, of which 2 were waited for; matrix products, arithmetic and copies ran while one was open for 28% of the time, Pallas kernels for 0%

commit v1 on v0

v1 whole, which is shorter than its diff:
```python
import functools

import jax
import jax.numpy as jnp
from jax import lax
from jax.experimental import pallas as pl
from jax.experimental.pallas import tpu as pltpu
from jax.sharding import PartitionSpec as P

CAP = 6
CHUNKS = 2
VMEM_LIMIT = 48 * 1024 * 1024
F32 = jnp.float32
BF16 = jnp.bfloat16


def product_kernel(tile_ref, rows_ref, weight_ref, out_ref):
    out_ref[...] = jnp.dot(
        rows_ref[...], weight_ref[...], preferred_element_type=F32
    ).astype(out_ref.dtype)


def block_product(rows, weight, first_tile, width, tile):
    row_total, depth = rows.shape
    tiles = width // tile
    return pl.pallas_call(
        product_kernel,
        grid_spec=pltpu.PrefetchScalarGridSpec(
            num_scalar_prefetch=1,
            grid=(tiles,),
            in_specs=[
                pl.BlockSpec((row_total, depth), lambda j, t: (0, 0)),
                pl.BlockSpec((depth, tile), lambda j, t: (0, t[0] + j)),
            ],
            out_specs=pl.BlockSpec((row_total, tile), lambda j, t: (0, j)),
        ),
        out_shape=jax.ShapeDtypeStruct((row_total, width), BF16),
        compiler_params=pltpu.CompilerParams(vmem_limit_bytes=VMEM_LIMIT),
        cost_estimate=pl.CostEstimate(
            flops=2 * row_total * depth * width,
            bytes_accessed=2 * (row_total * depth + depth * width + row_total * width),
            transcendentals=0,
        ),
        name="block_product",
    )(first_tile.reshape(1), rows, weight)


def pick_kernel(me_ref, table_ref, ids_ref, lens_ref, down_ref, up_ref, *rest):
    peers = ids_ref.shape[0]
    segs = ids_ref.shape[1]
    share = down_ref.shape[0]
    downs, ups = rest[:peers], rest[peers : 2 * peers]
    start_ref, end_ref, pick_ref, sem = rest[2 * peers :]
    me = me_ref[0]

    def clear(q, carry):
        pick_ref[q] = 0
        start_ref[q] = 0
        end_ref[q] = 0
        return carry

    lax.fori_loop(0, peers * CAP, clear, 0)

    for k in range(peers):

        def choose(s, count):
            slot = table_ref[ids_ref[k, s]]
            local = slot - me * share
            mine = jnp.logical_and(local >= 0, local < share)

            @pl.when(jnp.logical_and(mine, count < CAP))
            def _():
                pick_ref[k * CAP + count] = local

            return count + mine.astype(jnp.int32)

        lax.fori_loop(0, segs, choose, 0)
        for c in range(CAP):
            source = pick_ref[k * CAP + c]
            pltpu.make_async_copy(down_ref.at[source], downs[k].at[c], sem).start()
            pltpu.make_async_copy(up_ref.at[source], ups[k].at[c], sem).start()

    for k in range(peers):
        owner = lax.rem(me + peers - k, peers)

        def place(s, carry):
            count, first = carry
            local = table_ref[ids_ref[0, s]] - owner * share
            theirs = jnp.logical_and(local >= 0, local < share)
            last = first + lens_ref[0, s]

            @pl.when(jnp.logical_and(theirs, count < CAP))
            def _():
                start_ref[k * CAP + count] = first
                end_ref[k * CAP + count] = last

            return count + theirs.astype(jnp.int32), last

        lax.fori_loop(0, segs, place, (0, 0))

    for k in range(peers):
        for c in range(CAP):
            pltpu.make_async_copy(down_ref.at[0], downs[k].at[c], sem).wait()
            pltpu.make_async_copy(up_ref.at[0], ups[k].at[c], sem).wait()


def pick_adapters(me, table, ids, lens, down, up):
    peers = ids.shape[0]
    _, rank, depth = down.shape
    cols = up.shape[2]
    smem = pl.BlockSpec(memory_space=pltpu.SMEM)
    hbm = pl.BlockSpec(memory_space=pl.ANY)
    out = pl.pallas_call(
        pick_kernel,
        in_specs=[smem, smem, smem, smem, hbm, hbm],
        out_specs=[hbm] * (2 * peers) + [smem, smem],
        out_shape=[jax.ShapeDtypeStruct((CAP, rank, depth), BF16)] * peers
        + [jax.ShapeDtypeStruct((CAP, rank, cols), BF16)] * peers
        + [jax.ShapeDtypeStruct((peers * CAP,), jnp.int32)] * 2,
        scratch_shapes=[pltpu.SMEM((peers * CAP,), jnp.int32), pltpu.SemaphoreType.DMA],
        cost_estimate=pl.CostEstimate(
            flops=0, bytes_accessed=4 * peers * CAP * rank * (depth + cols), transcendentals=0
        ),
        name="pick_adapters",
    )(me.reshape(1), table, ids, lens, down, up)
    return out[:peers], out[peers : 2 * peers], out[2 * peers], out[2 * peers + 1]


def low_kernel(start_ref, end_ref, rows_ref, *rest):
    downs, out_ref = rest[:-1], rest[-1]
    row_total = rows_ref.shape[0]
    rank = out_ref.shape[0]
    place = lax.broadcasted_iota(jnp.int32, (rank, row_total), 1)
    total = jnp.zeros((rank, row_total), F32)
    for k, down_ref in enumerate(downs):
        part = lax.dot_general(
            down_ref[...], rows_ref[...], (((1,), (1,)), ((), ())), preferred_element_type=F32
        )
        for c in range(CAP):
            q = k * CAP + c
            member = jnp.logical_and(place >= start_ref[q], place < end_ref[q])
            total = jnp.where(member, part[c * rank : (c + 1) * rank], total)
    out_ref[...] = total.astype(BF16)


def low_sums(starts, ends, rows, downs, rank):
    row_total, depth = rows.shape
    smem = pl.BlockSpec(memory_space=pltpu.SMEM)
    vmem = pl.BlockSpec(memory_space=pltpu.VMEM)
    return pl.pallas_call(
        low_kernel,
        in_specs=[smem, smem] + [vmem] * (1 + len(downs)),
        out_specs=vmem,
        out_shape=jax.ShapeDtypeStruct((rank, row_total), BF16),
        compiler_params=pltpu.CompilerParams(vmem_limit_bytes=VMEM_LIMIT),
        cost_estimate=pl.CostEstimate(
            flops=2 * row_total * depth * CAP * rank * len(downs),
            bytes_accessed=2 * depth * (row_total + CAP * rank * len(downs)),
            transcendentals=0,
        ),
        name="low_sums",
    )(starts, ends, rows, *[d.reshape(CAP * rank, depth) for d in downs])


def finish_kernel(lows, ups_total, own_total, start_ref, end_ref, *rest):
    low_refs = rest[:lows]
    up_refs = rest[lows : lows + ups_total]
    base_refs = rest[lows + ups_total : -1]
    out_ref = rest[-1]
    rank, row_total = low_refs[0].shape
    low = low_refs[0][...].astype(F32)
    for ref in low_refs[1:]:
        low = low + ref[...].astype(F32)
    low = low.astype(BF16).astype(F32)
    place = lax.broadcasted_iota(jnp.int32, (rank, row_total), 1)
    term = jnp.zeros(out_ref.shape, F32)
    for k, up_ref in enumerate(up_refs):
        spread = []
        for c in range(CAP):
            q = k * CAP + c
            member = jnp.logical_and(place >= start_ref[q], place < end_ref[q])
            spread.append(jnp.where(member, low, 0.0))
        spread = jnp.concatenate(spread, axis=0).astype(BF16)
        term = term + lax.dot_general(
            spread, up_ref[...], (((0,), (0,)), ((), ())), preferred_element_type=F32
        )
    width = base_refs[0].shape[1]
    for c in range(out_ref.shape[1] // width):
        cols = slice(c * width, (c + 1) * width)
        base = base_refs[c * own_total][...].astype(F32)
        for ref in base_refs[c * own_total + 1 : (c + 1) * own_total]:
            base = base + ref[...].astype(F32)
        out_ref[:, cols] = (base + term[:, cols]).astype(out_ref.dtype)


def finish(starts, ends, lows, ups, bases):
    rank, row_total = lows[0].shape
    cols = ups[0].shape[2]
    smem = pl.BlockSpec(memory_space=pltpu.SMEM)
    vmem = pl.BlockSpec(memory_space=pltpu.VMEM)
    flat = [b for chunk in bases for b in chunk]
    return pl.pallas_call(
        functools.partial(finish_kernel, len(lows), len(ups), len(bases[0])),
        in_specs=[smem, smem] + [vmem] * (len(lows) + len(ups) + len(flat)),
        out_specs=vmem,
        out_shape=jax.ShapeDtypeStruct((row_total, cols), BF16),
        compiler_params=pltpu.CompilerParams(vmem_limit_bytes=VMEM_LIMIT),
        cost_estimate=pl.CostEstimate(
            flops=2 * row_total * cols * CAP * rank * len(ups),
            bytes_accessed=2 * row_total * cols * 5,
            transcendentals=0,
        ),
        name="finish",
    )(starts, ends, *lows, *[u.reshape(CAP * rank, cols) for u in ups], *flat)


def add(a, b):
    return (a.astype(F32) + b.astype(F32)).astype(BF16)


def local(req_total, tp_total, rows, weight, down, up, table, ids, lens):
    rank = down.shape[1]
    cols = weight.shape[1] // tp_total
    width = cols // CHUNKS
    tile = min(256, width)
    me_req = lax.axis_index("req").astype(jnp.int32)
    me = lax.axis_index("tp").astype(jnp.int32)
    lower = me < tp_total // 2

    all_ids = [ids]
    for k in range(1, req_total):
        back = [((i + k) % req_total, i) for i in range(req_total)]
        all_ids.append(lax.ppermute(ids, "req", back))
    all_ids = jnp.concatenate(all_ids, axis=0)
    downs, ups, starts, ends = pick_adapters(me_req, table, all_ids, lens, down, up)
    held_down, held_up = [downs[0]], [ups[0]]
    for k in range(1, req_total):
        ahead = [(i, (i + k) % req_total) for i in range(req_total)]
        held_down.append(lax.ppermute(downs[k], "req", ahead))
    for k in range(1, req_total):
        ahead = [(i, (i + k) % req_total) for i in range(req_total)]
        held_up.append(lax.ppermute(ups[k], "req", ahead))

    def partial(block, chunk):
        first = (jnp.clip(block, 0, tp_total - 1) * cols + chunk * width) // tile
        return block_product(rows, weight, first, width, tile)

    arrived = [[] for _ in range(CHUNKS)]
    for step in range(tp_total - 1):
        ahead = tp_total - 1 - step
        for chunk in range(CHUNKS):
            near = partial(jnp.where(lower, me + ahead, me - ahead), chunk)
            far = None
            if 2 * ahead < tp_total:
                far = partial(jnp.where(lower, me - ahead, me + ahead), chunk)
            sent = []
            for k in range(step + 1):
                value = near if k < tp_total // 2 else far
                if k > 0:
                    value = add(value, arrived[chunk][k - 1])
                m = tp_total - 1 - k
                sent.append(lax.ppermute(value, "tp", [(k, k + 1), (m, m - 1)]))
            arrived[chunk] = sent

    low = low_sums(starts, ends, rows, held_down, rank)
    lows = [low]
    for k in range(1, tp_total):
        lows.append(lax.ppermute(low, "tp", [(i, (i + k) % tp_total) for i in range(tp_total)]))
    bases = [[partial(me, chunk)] + arrived[chunk] for chunk in range(CHUNKS)]
    return finish(starts, ends, lows, held_up, bases)


def solution(mesh):
    return jax.shard_map(
        functools.partial(local, mesh.shape["req"], mesh.shape["tp"]),
        mesh=mesh,
        in_specs=(
            P(("groups", "req"), "tp"),
            P("tp", None),
            P(("groups", "req"), None, "tp"),
            P(("groups", "req"), None, "tp"),
            P("groups"),
            P(("groups", "req"), None),
            P(("groups", "req"), None),
        ),
        out_specs=P(("groups", "req"), "tp"),
        check_vma=False,
    )
```

time: 433 us -> 217 us (0.50)
  waiting for transfers between devices: 272 us -> 38 us
  matrix products: 123 us -> 0 us
  Pallas kernels: 0 us -> 110 us
  starting transfers between devices: 0.08 us -> 53.9 us
  blocking collectives: 18.7 us -> 0 us
  between operations: 15.1 us -> 0.54 us
  other arithmetic: 0.71 us -> 7.75 us
  local copies, waits for them, and re-layouts: 0.05 us -> 5.73 us
    all_gather x2 -> x0, waiting for transfers between devices: 271 us -> none  [the longest x1 175 us: local(): lax.all_gather(adapter_down_maps, 'req', axis=0, tiled=True)]
    dot_general x4 -> x0, matrix products: 123 us -> none  [the longest x1 78.6 us: local(): jnp.einsum('id,srd->isr', attention_rows, sel_down, preferred_element_typ...]
    pallas_call x0 -> x13, Pallas kernels: none -> 110 us  [the longest x1 74.2 us: pick_adapters(): pl.pallas_call(pick_kernel, in_specs=[smem, smem, smem, smem, hbm, hbm],...]
    ppermute x0 -> x24, starting transfers between devices: none -> 53.9 us  [the longest x12 24.8 us: local(): sent.append(lax.ppermute(value, 'tp', [(k, k + 1), (m, m - 1)]))]
    ppermute x0 -> x24, waiting for transfers between devices: none -> 38 us  [the longest x12 36.3 us: local(): sent.append(lax.ppermute(value, 'tp', [(k, k + 1), (m, m - 1)]))]
    psum x1 -> x0, blocking collectives: 18.7 us -> none  [local(): rank_reduced = lax.psum(low_part.astype(jnp.bfloat16), 'tp')]
    convert_element_type x0 -> x6, other arithmetic: none -> 7.15 us  [add(): return (a.astype(F32) + b.astype(F32)).astype(BF16)]
    unnamed x8 -> x48, local copies, waits for them, and re-layouts: 0.05 us -> 5.73 us
  transfers between devices with their start and end apart: 3 -> 24, of which waited for: 2 -> 4; matrix products, arithmetic and copies ran while one was open for 28% -> 4% of each run, Pallas kernels for 0% -> 49%
where the time goes in v1:
time: 217 us; the launch traced here: 216 us
  Pallas kernels  110 us (51%)
  starting transfers between devices  53.9 us (25%)
  waiting for transfers between devices  38 us (18%)
  other arithmetic  7.75 us (4%)
  local copies, waits for them, and re-layouts  5.73 us (3%)
    pallas_call x1, Pallas kernels, pick_adapters(): pl.pallas_call(pick_kernel, in_specs=[smem, smem, smem, smem, hbm, hbm],...  74.2 us
    ppermute x12, waiting for transfers between devices, local(): sent.append(lax.ppermute(value, 'tp', [(k, k + 1), (m, m - 1)]))  36.3 us
    pallas_call x10, Pallas kernels, block_product(): pl.pallas_call(product_kernel, grid_spec=pltpu.PrefetchScalarGridSpec(num...  28.7 us
    ppermute x12, starting transfers between devices, local(): sent.append(lax.ppermute(value, 'tp', [(k, k + 1), (m, m - 1)]))  24.8 us
    ppermute x3, starting transfers between devices, local(): lax.ppermute(low, 'tp', [(i, (i + k) % tp_total) for i in range(tp_total)])  19.6 us
    convert_element_type x6, other arithmetic, add(): return (a.astype(F32) + b.astype(F32)).astype(BF16)  7.15 us
    unnamed x48, local copies, waits for them, and re-layouts  5.73 us
    ppermute x3, starting transfers between devices, local(): all_ids.append(lax.ppermute(ids, 'req', back))  4.43 us
  transfers between devices with their start and end apart: 24, of which 4 were waited for; matrix products, arithmetic and copies ran while one was open for 4% of the time, Pallas kernels for 49%

profile of v1, /device:TPU:0, one launch (start us, length us, event | category | flops | bytes accessed | tf_op | source)
XLA Modules:
  0.0 215.9 jit_solution(6267660983647885935)
XLA Ops:
  0.0 0.5 collective-permute-start.2
  0.5 2.5 %collective-permute-start.1 = (s32[1,12]{1,0:T(1,128)}, s32[1,12]{1,0:T(1,128)S(1)}, u32[]{:S(2)}, u32[]{:S(2)}) collective-permute-start(s32[1,12]{1,0:T(1,128)} %param.12), channel_id=1, source_target_pairs={{8,0},{12,4},{0,8},{4,12},{9,1},{13,5},{1,9},{5,13},{10,2},{14,6},... | collective-permute-start | bytes 152 | tf_op jit(solution)/shard_map/ppermute | solution.py:233
  3.0 1.4 collective-permute-start
  4.4 1.6 copy-done
  6.0 2.8 %block_product.12 = bf16[512,512]{1,0:T(8,128)(2,1)S(1)} custom-call(s32[1]{0:T(128)} %bitcast.11.tile_ref, bf16[512,2048]{1,0:T(8,128)(2,1)S(1)} %copy-done, bf16[2048,4096]{1,0:T(8,128)(2,1)} %weight_ref.19), custom_call_target="tpu_custom_call" | custom-call | flops 1073741824 | bytes 4718592 | tf_op jit(solution)/shard_map/block_product/pallas_call | solution.py:26
  8.9 4.3 %collective-permute-start.13 = (bf16[512,512]{1,0:T(8,128)(2,1)S(1)}, bf16[512,512]{1,0:T(8,128)(2,1)}, u32[]{:S(2)}, u32[]{:S(2)}) collective-permute-start(bf16[512,512]{1,0:T(8,128)(2,1)S(1)} %block_product.12), channel_id=1, source_target_pairs={{0,1},{3,2},{4,5},{7,6},{8,9},{11,10},{12,13},{15,14},{16,17},{19,... | collective-permute-start | bytes 1572872 | tf_op jit(solution)/shard_map/ppermute | solution.py:262
  13.2 3.4 %block_product.14 = bf16[512,512]{1,0:T(8,128)(2,1)} custom-call(s32[1]{0:T(128)} %bitcast.13.tile_ref, bf16[512,2048]{1,0:T(8,128)(2,1)S(1)} %copy-done.1, bf16[2048,4096]{1,0:T(8,128)(2,1)} %weight_ref.19), custom_call_target="tpu_custom_call" | custom-call | flops 1073741824 | bytes 4718592 | tf_op jit(solution)/shard_map/block_product/pallas_call | solution.py:26
  16.5 2.1 collective-permute-start.15
  18.7 2.7 %block_product.11 = bf16[512,512]{1,0:T(8,128)(2,1)S(1)} custom-call(s32[1]{0:T(128)} %bitcast.10.tile_ref, bf16[512,2048]{1,0:T(8,128)(2,1)S(1)} %copy-done.1, bf16[2048,4096]{1,0:T(8,128)(2,1)} %weight_ref.19), custom_call_target="tpu_custom_call" | custom-call | flops 1073741824 | bytes 4718592 | tf_op jit(solution)/shard_map/block_product/pallas_call | solution.py:26
  21.4 0.0 copy-start.20
  21.4 2.7 %block_product.13 = bf16[512,512]{1,0:T(8,128)(2,1)S(1)} custom-call(s32[1]{0:T(128)} %bitcast.12.tile_ref, bf16[512,2048]{1,0:T(8,128)(2,1)S(1)} %copy-done.1, bf16[2048,4096]{1,0:T(8,128)(2,1)} %weight_ref.19), custom_call_target="tpu_custom_call" | custom-call | flops 1073741824 | bytes 4718592 | tf_op jit(solution)/shard_map/block_product/pallas_call | solution.py:26
  24.1 0.8 copy-done.2
  24.9 0.0 collective-permute-done.2
  25.0 0.6 pad_add_fusion.ids_ref
  25.6 74.2 %pick_adapters.1 = (bf16[6,16,2048]{2,1,0:T(8,128)(2,1)}, bf16[6,16,2048]{2,1,0:T(8,128)(2,1)}, bf16[6,16,2048]{2,1,0:T(8,128)(2,1)}, bf16[6,16,2048]{2,1,0:T(8,...) custom-call(s32[1]{0:T(128)} %bitcast.me_ref, ...), custom_call_target="tpu_custom_call" | custom-call | bytes 4718592 | tf_op jit(solution)/shard_map/pick_adapters/pallas_call | solution.py:113
  99.7 0.1 collective-permute-start.3
  99.8 0.6 collective-permute-start.4
  100.4 1.4 collective-permute-start.5
  101.7 3.4 %block_product.16 = bf16[512,512]{1,0:T(8,128)(2,1)} custom-call(s32[1]{0:T(128)} %bitcast.15.tile_ref, bf16[512,2048]{1,0:T(8,128)(2,1)S(1)} %copy-done.1, bf16[2048,4096]{1,0:T(8,128)(2,1)} %weight_ref.19), custom_call_target="tpu_custom_call" | custom-call | flops 1073741824 | bytes 4718592 | tf_op jit(solution)/shard_map/block_product/pallas_call | solution.py:26
  105.1 2.7 %block_product.17 = bf16[512,512]{1,0:T(8,128)(2,1)S(1)} custom-call(s32[1]{0:T(128)} %bitcast.16.tile_ref, bf16[512,2048]{1,0:T(8,128)(2,1)S(1)} %copy-done.1, bf16[2048,4096]{1,0:T(8,128)(2,1)} %weight_ref.19), custom_call_target="tpu_custom_call" | custom-call | flops 1073741824 | bytes 4718592 | tf_op jit(solution)/shard_map/block_product/pallas_call | solution.py:26
  107.8 2.7 %block_product.19 = bf16[512,512]{1,0:T(8,128)(2,1)S(1)} custom-call(s32[1]{0:T(128)} %bitcast.18.tile_ref, bf16[512,2048]{1,0:T(8,128)(2,1)S(1)} %copy-done.1, bf16[2048,4096]{1,0:T(8,128)(2,1)} %weight_ref.19), custom_call_target="tpu_custom_call" | custom-call | flops 1073741824 | bytes 4718592 | tf_op jit(solution)/shard_map/block_product/pallas_call | solution.py:26
  110.6 2.8 %block_product.18 = bf16[512,512]{1,0:T(8,128)(2,1)S(1)} custom-call(s32[1]{0:T(128)} %bitcast.17.tile_ref, bf16[512,2048]{1,0:T(8,128)(2,1)S(1)} %copy-done.1, bf16[2048,4096]{1,0:T(8,128)(2,1)} %weight_ref.19), custom_call_target="tpu_custom_call" | custom-call | flops 1073741824 | bytes 4718592 | tf_op jit(solution)/shard_map/block_product/pallas_call | solution.py:26
  113.4 0.0 collective-permute-done.3
  113.4 1.5 collective-permute-start.12
  114.9 0.0 collective-permute-done.4
  114.9 1.3 collective-permute-start.19
  116.2 1.7 collective-permute-done.5
  118.0 1.3 collective-permute-start.21
  119.3 3.2 %low_sums.1.rest_0_ = bf16[16,512]{1,0:T(8,128)(2,1)S(1)} custom-call(s32[24]{0:T(128)S(1)} %copy-done.16, s32[24]{0:T(128)S(1)} %copy-done.18, bf16[512,2048]{1,0:T(8,128)(2,1)S(1)} %copy-done.1, bf16[96,2048]{1,0:T(8,128)(2,1)S(1)} %bitcast.19, bf16[96,2048]{1,0:T(8,128)(2,1)S(1)} %bitcast.20, bf16[96,2048]{1,0:T(8,128)(2,1)S(1)} %bitcast.21, ...), custom_call_target="tpu_custom_call" | custom-call | flops 805306368 | bytes 3670016 | tf_op jit(solution)/shard_map/low_sums/pallas_call | solution.py:150
  122.5 0.0 collective-permute-done.13
  122.5 2.5 %collective-permute-start.9 = (bf16[6,16,1024]{2,1,0:T(8,128)(2,1)S(1)}, bf16[6,16,1024]{2,1,0:T(8,128)(2,1)S(1)}, u32[]{:S(2)}, u32[]{:S(2)}) collective-permute-start(bf16[6,16,1024]{2,1,0:T(8,128)(2,1)S(1)} %copy-done.23), channel_id=1, source_target_pairs={{0,4},{4,8},{8,12},{12,0},{1,5},{5,9},{9,13},{13,1},{2,6},{6,10},{... | collective-permute-start | bytes 589832 | tf_op jit(solution)/shard_map/ppermute | solution.py:242
  125.0 2.0 add_convert_fusion.5
  127.0 0.0 collective-permute-done.15
  127.0 0.5 collective-permute-start.10
  127.5 1.2 add_convert_fusion.4
  128.7 20.2 %collective-permute-done.21 = bf16[512,512]{1,0:T(8,128)(2,1)S(1)} collective-permute-done((bf16[512,512]{1,0:T(8,128)(2,1)S(1)}, bf16[512,512]{1,0:T(8,128)(2,1)S(1)}, u32[]{:S(2)}, u32[]{:S(2)}) %collective-permute-start.21) | collective-permute-done | bytes 524320 | tf_op jit(solution)/shard_map/ppermute | solution.py:262
  148.8 0.7 collective-permute-start.16
  149.5 0.1 add_convert_fusion.1
  149.7 0.7 collective-permute-start.22
  150.4 2.0 add_convert_fusion.2
  152.4 0.0 collective-permute-done.16
  152.4 0.0 collective-permute-start.11
  152.4 0.9 add_convert_fusion.3
  153.3 16.0 %collective-permute-start.6 = (bf16[16,512]{1,0:T(8,128)(2,1)S(1)}, bf16[16,512]{1,0:T(8,128)(2,1)S(1)}, u32[]{:S(2)}, u32[]{:S(2)}) collective-permute-start(bf16[16,512]{1,0:T(8,128)(2,1)S(1)} %low_sums.1.rest_0_), channel_id=1, source_target_pairs={{0,1},{1,2},{2,3},{3,0},{4,5},{5,6},{6,7},{7,4},{8,9},{9,10},{10,1... | collective-permute-start | bytes 49160 | tf_op jit(solution)/shard_map/ppermute | solution.py:268
  169.4 0.7 collective-permute-start.7
  170.1 2.9 %collective-permute-start.8 = (bf16[16,512]{1,0:T(8,128)(2,1)S(1)}, bf16[16,512]{1,0:T(8,128)(2,1)S(1)}, u32[]{:S(2)}, u32[]{:S(2)}) collective-permute-start(bf16[16,512]{1,0:T(8,128)(2,1)S(1)} %low_sums.1.rest_0_), channel_id=1, source_target_pairs={{0,3},{1,0},{2,1},{3,2},{4,7},{5,4},{6,5},{7,6},{8,11},{9,8},{10,9... | collective-permute-start | bytes 49160 | tf_op jit(solution)/shard_map/ppermute | solution.py:268
  173.0 0.9 add_convert_fusion
  173.9 0.7 copy-done.8
  174.6 7.4 %collective-permute-start.18 = (bf16[512,512]{1,0:T(8,128)(2,1)}, bf16[512,512]{1,0:T(8,128)(2,1)S(1)}, u32[]{:S(2)}, u32[]{:S(2)}) collective-permute-start(bf16[512,512]{1,0:T(8,128)(2,1)} %block_product.16), channel_id=1, source_target_pairs={{0,1},{3,2},{4,5},{7,6},{8,9},{11,10},{12,13},{15,14},{16,17},{19,... | collective-permute-start | bytes 1572872 | tf_op jit(solution)/shard_map/ppermute | solution.py:262
  182.1 0.6 copy-done.10
  182.7 1.5 collective-permute-start.14
  184.1 0.6 copy-done.12
  184.7 1.5 collective-permute-start.20
  186.2 0.6 copy-done.14
  186.8 1.3 collective-permute-start.17
  188.1 0.0 copy-start.4
  188.1 0.8 copy-done.4
  188.9 1.3 collective-permute-start.23
  190.2 2.7 %block_product.10.rest_8_ = bf16[512,512]{1,0:T(8,128)(2,1)S(1)} custom-call(s32[1]{0:T(128)} %bitcast.9.tile_ref, bf16[512,2048]{1,0:T(8,128)(2,1)S(1)} %copy-done.1, bf16[2048,4096]{1,0:T(8,128)(2,1)} %weight_ref.19), custom_call_target="tpu_custom_call" | custom-call | flops 1073741824 | bytes 4718592 | tf_op jit(solution)/shard_map/block_product/pallas_call | solution.py:26
  192.9 0.0 copy-start.5
  193.0 2.8 %block_product.15.rest_12_ = bf16[512,512]{1,0:T(8,128)(2,1)S(1)} custom-call(s32[1]{0:T(128)} %bitcast.14.tile_ref, bf16[512,2048]{1,0:T(8,128)(2,1)S(1)} %copy-done.1, bf16[2048,4096]{1,0:T(8,128)(2,1)} %weight_ref.19), custom_call_target="tpu_custom_call" | custom-call | flops 1073741824 | bytes 4718592 | tf_op jit(solution)/shard_map/block_product/pallas_call | solution.py:26
  195.8 8.0 %collective-permute-done.17.rest_11_ = bf16[512,512]{1,0:T(8,128)(2,1)} collective-permute-done((bf16[512,512]{1,0:T(8,128)(2,1)}, bf16[512,512]{1,0:T(8,128)(2,1)}, u32[]{:S(2)}, u32[]{:S(2)}) %collective-permute-start.17) | collective-permute-done | bytes 524320 | tf_op jit(solution)/shard_map/ppermute | solution.py:262
  203.9 8.1 %collective-permute-done.23.rest_15_ = bf16[512,512]{1,0:T(8,128)(2,1)S(1)} collective-permute-done((bf16[512,512]{1,0:T(8,128)(2,1)}, bf16[512,512]{1,0:T(8,128)(2,1)S(1)}, u32[]{:S(2)}, u32[]{:S(2)}) %collective-permute-start.23) | collective-permute-done | bytes 524320 | tf_op jit(solution)/shard_map/ppermute | solution.py:262
  212.0 3.9 %finish.1 = bf16[512,1024]{1,0:T(8,128)(2,1)} custom-call(s32[24]{0:T(128)S(1)} %copy-done.17, s32[24]{0:T(128)S(1)} %copy-done.19, bf16[16,512]{1,0:T(8,128)(2,1)S(1)} %low_sums.1.rest_0_, bf16[16,512]{1,0:T(8,128)(2,1)S(1)} %copy-done.11, bf16[16,512]{1,0:T(8,128)(2,1)S(1)} %copy-done.13, bf16[16,512]{1,0:T(8,128)(2,1)S(1)} %copy-done.15, ...), custom_call_target="tpu_custom_call" | custom-call | flops 402653184 | bytes 5242880 | tf_op jit(solution)/shard_map/finish/pallas_call | solution.py:202
  (52 shorter events, 0.1 us)
Async XLA Ops:
  0.0 24.9 %collective-permute-start.2 = (s32[1,12]{1,0:T(1,128)}, s32[1,12]{1,0:T(1,128)S(1)}, u32[]{:S(2)}, u32[]{:S(2)}) collective-permute-start(s32[1,12]{1,0:T(1,128)} %param.12), channel_id=1, source_target_pairs={{12,0},{0,4},{4,8},{8,12},{13,1},{1,5},{5,9},{9,13},{14,2},{2,6},{... | collective-permute-start | bytes 152 | tf_op jit(solution)/shard_map/ppermute | solution.py:233
  0.5 24.5 %collective-permute-start.1 = (s32[1,12]{1,0:T(1,128)}, s32[1,12]{1,0:T(1,128)S(1)}, u32[]{:S(2)}, u32[]{:S(2)}) collective-permute-start(s32[1,12]{1,0:T(1,128)} %param.12), channel_id=1, source_target_pairs={{8,0},{12,4},{0,8},{4,12},{9,1},{13,5},{1,9},{5,13},{10,2},{14,6},... | collective-permute-start | bytes 152 | tf_op jit(solution)/shard_map/ppermute | solution.py:233
  3.0 21.9 %collective-permute-start = (s32[1,12]{1,0:T(1,128)}, s32[1,12]{1,0:T(1,128)S(1)}, u32[]{:S(2)}, u32[]{:S(2)}) collective-permute-start(s32[1,12]{1,0:T(1,128)} %param.12), channel_id=1, source_target_pairs={{4,0},{8,4},{12,8},{0,12},{5,1},{9,5},{13,9},{1,13},{6,2},{10,6},{... | collective-permute-start | bytes 152 | tf_op jit(solution)/shard_map/ppermute | solution.py:233
  4.4 1.6 copy-start
  6.0 7.1 %copy-start.1 = (bf16[512,2048]{1,0:T(8,128)(2,1)S(1)}, bf16[512,2048]{1,0:T(8,128)(2,1)}, u32[]{:S(2)}) copy-start(bf16[512,2048]{1,0:T(8,128)(2,1)} %rows_ref.21) | copy-start | bytes 6291460
  8.9 113.6 %collective-permute-start.13 = (bf16[512,512]{1,0:T(8,128)(2,1)S(1)}, bf16[512,512]{1,0:T(8,128)(2,1)}, u32[]{:S(2)}, u32[]{:S(2)}) collective-permute-start(bf16[512,512]{1,0:T(8,128)(2,1)S(1)} %block_product.12), channel_id=1, source_target_pairs={{0,1},{3,2},{4,5},{7,6},{8,9},{11,10},{12,13},{15,14},{16,17},{19,... | collective-permute-start | bytes 1572872 | tf_op jit(solution)/shard_map/ppermute | solution.py:262
  16.5 110.4 %collective-permute-start.15 = (bf16[512,512]{1,0:T(8,128)(2,1)}, bf16[512,512]{1,0:T(8,128)(2,1)}, u32[]{:S(2)}, u32[]{:S(2)}) collective-permute-start(bf16[512,512]{1,0:T(8,128)(2,1)} %block_product.14), channel_id=1, source_target_pairs={{0,1},{3,2},{4,5},{7,6},{8,9},{11,10},{12,13},{15,14},{16,17},{19,... | collective-permute-start | bytes 1572872 | tf_op jit(solution)/shard_map/ppermute | solution.py:262
  21.4 3.6 %copy-start.20 = (s32[1,12]{1,0:T(1,128)S(1)}, s32[1,12]{1,0:T(1,128)}, u32[]{:S(2)}) copy-start(s32[1,12]{1,0:T(1,128)} %param.12) | copy-start | bytes 148
  24.1 0.8 copy-start.2
  99.7 13.7 %collective-permute-start.3 = (bf16[6,16,2048]{2,1,0:T(8,128)(2,1)}, bf16[6,16,2048]{2,1,0:T(8,128)(2,1)S(1)}, u32[]{:S(2)}, u32[]{:S(2)}) collective-permute-start(bf16[6,16,2048]{2,1,0:T(8,128)(2,1)} %get-tuple-element.18), channel_id=1, source_target_pairs={{0,4},{4,8},{8,12},{12,0},{1,5},{5,9},{9,13},{13,1},{2,6},{6,10},{... | collective-permute-start | bytes 1179656 | tf_op jit(solution)/shard_map/ppermute | solution.py:239
  99.8 15.1 %collective-permute-start.4 = (bf16[6,16,2048]{2,1,0:T(8,128)(2,1)}, bf16[6,16,2048]{2,1,0:T(8,128)(2,1)S(1)}, u32[]{:S(2)}, u32[]{:S(2)}) collective-permute-start(bf16[6,16,2048]{2,1,0:T(8,128)(2,1)} %get-tuple-element.19), channel_id=1, source_target_pairs={{0,8},{4,12},{8,0},{12,4},{1,9},{5,13},{9,1},{13,5},{2,10},{6,14},... | collective-permute-start | bytes 1179656 | tf_op jit(solution)/shard_map/ppermute | solution.py:239
  100.4 17.6 %collective-permute-start.5 = (bf16[6,16,2048]{2,1,0:T(8,128)(2,1)}, bf16[6,16,2048]{2,1,0:T(8,128)(2,1)S(1)}, u32[]{:S(2)}, u32[]{:S(2)}) collective-permute-start(bf16[6,16,2048]{2,1,0:T(8,128)(2,1)} %get-tuple-element.20), channel_id=1, source_target_pairs={{0,12},{4,0},{8,4},{12,8},{1,13},{5,1},{9,5},{13,9},{2,14},{6,2},{... | collective-permute-start | bytes 1179656 | tf_op jit(solution)/shard_map/ppermute | solution.py:239
  110.6 8.7 %copy-start.6 = (bf16[6,16,2048]{2,1,0:T(8,128)(2,1)S(1)}, bf16[6,16,2048]{2,1,0:T(8,128)(2,1)}, u32[]{:S(2)}) copy-start(bf16[6,16,2048]{2,1,0:T(8,128)(2,1)} %get-tuple-element.17) | copy-start | bytes 1179652
  110.6 8.7 %copy-start.16 = (s32[24]{0:T(128)S(1)}, s32[24]{0:T(128)}, u32[]{:S(2)}) copy-start(s32[24]{0:T(128)} %get-tuple-element.15.start_ref) | copy-start | bytes 292
  110.6 8.7 %copy-start.18 = (s32[24]{0:T(128)S(1)}, s32[24]{0:T(128)}, u32[]{:S(2)}) copy-start(s32[24]{0:T(128)} %get-tuple-element.16.end_ref) | copy-start | bytes 292
  110.6 11.9 %copy-start.23 = (bf16[6,16,1024]{2,1,0:T(8,128)(2,1)S(1)}, bf16[6,16,1024]{2,1,0:T(8,128)(2,1)}, u32[]{:S(2)}) copy-start(bf16[6,16,1024]{2,1,0:T(8,128)(2,1)} %get-tuple-element.22) | copy-start | bytes 589828
  110.6 16.4 %copy-start.22 = (bf16[6,16,1024]{2,1,0:T(8,128)(2,1)S(1)}, bf16[6,16,1024]{2,1,0:T(8,128)(2,1)}, u32[]{:S(2)}) copy-start(bf16[6,16,1024]{2,1,0:T(8,128)(2,1)} %get-tuple-element.23) | copy-start | bytes 589828
  113.4 39.0 %copy-start.21 = (bf16[6,16,1024]{2,1,0:T(8,128)(2,1)S(1)}, bf16[6,16,1024]{2,1,0:T(8,128)(2,1)}, u32[]{:S(2)}) copy-start(bf16[6,16,1024]{2,1,0:T(8,128)(2,1)} %get-tuple-element.24) | copy-start | bytes 589828
  113.4 39.0 %copy-start.3 = (bf16[512,512]{1,0:T(8,128)(2,1)S(1)}, bf16[512,512]{1,0:T(8,128)(2,1)}, u32[]{:S(2)}) copy-start(bf16[512,512]{1,0:T(8,128)(2,1)} %copy-done.2) | copy-start | bytes 1572868
  113.4 74.7 %collective-permute-start.12 = (bf16[512,512]{1,0:T(8,128)(2,1)S(1)}, bf16[512,512]{1,0:T(8,128)(2,1)S(1)}, u32[]{:S(2)}, u32[]{:S(2)}) collective-permute-start(bf16[512,512]{1,0:T(8,128)(2,1)S(1)} %block_product.11), channel_id=1, source_target_pairs={{0,1},{3,2},{4,5},{7,6},{8,9},{11,10},{12,13},{15,14},{16,17},{19,... | collective-permute-start | bytes 1572872 | tf_op jit(solution)/shard_map/ppermute | solution.py:262
  114.9 34.8 %collective-permute-start.19 = (bf16[512,512]{1,0:T(8,128)(2,1)S(1)}, bf16[512,512]{1,0:T(8,128)(2,1)S(1)}, u32[]{:S(2)}, u32[]{:S(2)}) collective-permute-start(bf16[512,512]{1,0:T(8,128)(2,1)S(1)} %block_product.17), channel_id=1, source_target_pairs={{0,1},{3,2},{4,5},{7,6},{8,9},{11,10},{12,13},{15,14},{16,17},{19,... | collective-permute-start | bytes 1572872 | tf_op jit(solution)/shard_map/ppermute | solution.py:262
  118.0 30.9 %collective-permute-start.21 = (bf16[512,512]{1,0:T(8,128)(2,1)S(1)}, bf16[512,512]{1,0:T(8,128)(2,1)S(1)}, u32[]{:S(2)}, u32[]{:S(2)}) collective-permute-start(bf16[512,512]{1,0:T(8,128)(2,1)S(1)} %block_product.19), channel_id=1, source_target_pairs={{0,1},{3,2},{4,5},{7,6},{8,9},{11,10},{12,13},{15,14},{16,17},{19,... | collective-permute-start | bytes 1572872 | tf_op jit(solution)/shard_map/ppermute | solution.py:262
  122.5 30.8 %collective-permute-start.9 = (bf16[6,16,1024]{2,1,0:T(8,128)(2,1)S(1)}, bf16[6,16,1024]{2,1,0:T(8,128)(2,1)S(1)}, u32[]{:S(2)}, u32[]{:S(2)}) collective-permute-start(bf16[6,16,1024]{2,1,0:T(8,128)(2,1)S(1)} %copy-done.23), channel_id=1, source_target_pairs={{0,4},{4,8},{8,12},{12,0},{1,5},{5,9},{9,13},{13,1},{2,6},{6,10},{... | collective-permute-start | bytes 589832 | tf_op jit(solution)/shard_map/ppermute | solution.py:242
  127.0 42.4 %collective-permute-start.10 = (bf16[6,16,1024]{2,1,0:T(8,128)(2,1)S(1)}, bf16[6,16,1024]{2,1,0:T(8,128)(2,1)S(1)}, u32[]{:S(2)}, u32[]{:S(2)}) collective-permute-start(bf16[6,16,1024]{2,1,0:T(8,128)(2,1)S(1)} %copy-done.22), channel_id=1, source_target_pairs={{0,8},{4,12},{8,0},{12,4},{1,9},{5,13},{9,1},{13,5},{2,10},{6,14},... | collective-permute-start | bytes 589832 | tf_op jit(solution)/shard_map/ppermute | solution.py:242
  148.8 3.5 %collective-permute-start.16 = (bf16[512,512]{1,0:T(8,128)(2,1)S(1)}, bf16[512,512]{1,0:T(8,128)(2,1)S(1)}, u32[]{:S(2)}, u32[]{:S(2)}) collective-permute-start(bf16[512,512]{1,0:T(8,128)(2,1)S(1)} %add_convert_fusion.4), channel_id=1, source_target_pairs={{1,2},{2,1},{5,6},{6,5},{9,10},{10,9},{13,14},{14,13},{17,18},{18,... | collective-permute-start | bytes 1572872 | tf_op jit(solution)/shard_map/ppermute | solution.py:262
  149.7 20.4 %collective-permute-start.22 = (bf16[512,512]{1,0:T(8,128)(2,1)S(1)}, bf16[512,512]{1,0:T(8,128)(2,1)S(1)}, u32[]{:S(2)}, u32[]{:S(2)}) collective-permute-start(bf16[512,512]{1,0:T(8,128)(2,1)S(1)} %add_convert_fusion.1), channel_id=1, source_target_pairs={{1,2},{2,1},{5,6},{6,5},{9,10},{10,9},{13,14},{14,13},{17,18},{18,... | collective-permute-start | bytes 1572872 | tf_op jit(solution)/shard_map/ppermute | solution.py:262
  152.4 21.5 %collective-permute-start.11 = (bf16[6,16,1024]{2,1,0:T(8,128)(2,1)S(1)}, bf16[6,16,1024]{2,1,0:T(8,128)(2,1)S(1)}, u32[]{:S(2)}, u32[]{:S(2)}) collective-permute-start(bf16[6,16,1024]{2,1,0:T(8,128)(2,1)S(1)} %copy-done.21), channel_id=1, source_target_pairs={{0,12},{4,0},{8,4},{12,8},{1,13},{5,1},{9,5},{13,9},{2,14},{6,2},{... | collective-permute-start | bytes 589832 | tf_op jit(solution)/shard_map/ppermute | solution.py:242
  153.3 28.7 %collective-permute-start.6 = (bf16[16,512]{1,0:T(8,128)(2,1)S(1)}, bf16[16,512]{1,0:T(8,128)(2,1)S(1)}, u32[]{:S(2)}, u32[]{:S(2)}) collective-permute-start(bf16[16,512]{1,0:T(8,128)(2,1)S(1)} %low_sums.1.rest_0_), channel_id=1, source_target_pairs={{0,1},{1,2},{2,3},{3,0},{4,5},{5,6},{6,7},{7,4},{8,9},{9,10},{10,1... | collective-permute-start | bytes 49160 | tf_op jit(solution)/shard_map/ppermute | solution.py:268
  169.4 14.7 %collective-permute-start.7 = (bf16[16,512]{1,0:T(8,128)(2,1)S(1)}, bf16[16,512]{1,0:T(8,128)(2,1)S(1)}, u32[]{:S(2)}, u32[]{:S(2)}) collective-permute-start(bf16[16,512]{1,0:T(8,128)(2,1)S(1)} %low_sums.1.rest_0_), channel_id=1, source_target_pairs={{0,2},{1,3},{2,0},{3,1},{4,6},{5,7},{6,4},{7,5},{8,10},{9,11},{10,... | collective-permute-start | bytes 49160 | tf_op jit(solution)/shard_map/ppermute | solution.py:268
  170.1 16.1 %collective-permute-start.8 = (bf16[16,512]{1,0:T(8,128)(2,1)S(1)}, bf16[16,512]{1,0:T(8,128)(2,1)S(1)}, u32[]{:S(2)}, u32[]{:S(2)}) collective-permute-start(bf16[16,512]{1,0:T(8,128)(2,1)S(1)} %low_sums.1.rest_0_), channel_id=1, source_target_pairs={{0,3},{1,0},{2,1},{3,2},{4,7},{5,4},{6,5},{7,6},{8,11},{9,8},{10,9... | collective-permute-start | bytes 49160 | tf_op jit(solution)/shard_map/ppermute | solution.py:268
  173.9 0.7 copy-start.8
  174.6 21.2 %collective-permute-start.18 = (bf16[512,512]{1,0:T(8,128)(2,1)}, bf16[512,512]{1,0:T(8,128)(2,1)S(1)}, u32[]{:S(2)}, u32[]{:S(2)}) collective-permute-start(bf16[512,512]{1,0:T(8,128)(2,1)} %block_product.16), channel_id=1, source_target_pairs={{0,1},{3,2},{4,5},{7,6},{8,9},{11,10},{12,13},{15,14},{16,17},{19,... | collective-permute-start | bytes 1572872 | tf_op jit(solution)/shard_map/ppermute | solution.py:262
  182.1 0.6 copy-start.10
  182.7 13.1 %collective-permute-start.14 = (bf16[512,512]{1,0:T(8,128)(2,1)}, bf16[512,512]{1,0:T(8,128)(2,1)}, u32[]{:S(2)}, u32[]{:S(2)}) collective-permute-start(bf16[512,512]{1,0:T(8,128)(2,1)} %add_convert_fusion.5), channel_id=1, source_target_pairs={{1,2},{2,1},{5,6},{6,5},{9,10},{10,9},{13,14},{14,13},{17,18},{18,... | collective-permute-start | bytes 1572872 | tf_op jit(solution)/shard_map/ppermute | solution.py:262
  184.1 0.6 copy-start.12
  184.7 11.1 %collective-permute-start.20 = (bf16[512,512]{1,0:T(8,128)(2,1)}, bf16[512,512]{1,0:T(8,128)(2,1)}, u32[]{:S(2)}, u32[]{:S(2)}) collective-permute-start(bf16[512,512]{1,0:T(8,128)(2,1)} %add_convert_fusion.2), channel_id=1, source_target_pairs={{1,2},{2,1},{5,6},{6,5},{9,10},{10,9},{13,14},{14,13},{17,18},{18,... | collective-permute-start | bytes 1572872 | tf_op jit(solution)/shard_map/ppermute | solution.py:262
  186.2 0.6 copy-start.14
  186.8 17.1 %collective-permute-start.17 = (bf16[512,512]{1,0:T(8,128)(2,1)}, bf16[512,512]{1,0:T(8,128)(2,1)}, u32[]{:S(2)}, u32[]{:S(2)}) collective-permute-start(bf16[512,512]{1,0:T(8,128)(2,1)} %add_convert_fusion.3), channel_id=1, source_target_pairs={{2,3},{1,0},{6,7},{5,4},{10,11},{9,8},{14,15},{13,12},{18,19},{17,... | collective-permute-start | bytes 1572872 | tf_op jit(solution)/shard_map/ppermute | solution.py:262
  188.1 0.8 copy-start.4
  188.9 23.0 %collective-permute-start.23 = (bf16[512,512]{1,0:T(8,128)(2,1)}, bf16[512,512]{1,0:T(8,128)(2,1)S(1)}, u32[]{:S(2)}, u32[]{:S(2)}) collective-permute-start(bf16[512,512]{1,0:T(8,128)(2,1)} %add_convert_fusion), channel_id=1, source_target_pairs={{2,3},{1,0},{6,7},{5,4},{10,11},{9,8},{14,15},{13,12},{18,19},{17,... | collective-permute-start | bytes 1572872 | tf_op jit(solution)/shard_map/ppermute | solution.py:262
  192.9 19.0 %copy-start.5 = (bf16[512,512]{1,0:T(8,128)(2,1)S(1)}, bf16[512,512]{1,0:T(8,128)(2,1)}, u32[]{:S(2)}) copy-start(bf16[512,512]{1,0:T(8,128)(2,1)} %copy-done.4) | copy-start | bytes 1572868
  192.9 19.0 %copy-start.7 = (bf16[6,16,1024]{2,1,0:T(8,128)(2,1)S(1)}, bf16[6,16,1024]{2,1,0:T(8,128)(2,1)}, u32[]{:S(2)}) copy-start(bf16[6,16,1024]{2,1,0:T(8,128)(2,1)} %get-tuple-element.21) | copy-start | bytes 589828
  192.9 19.0 %copy-start.9 = (bf16[6,16,1024]{2,1,0:T(8,128)(2,1)S(1)}, bf16[6,16,1024]{2,1,0:T(8,128)(2,1)}, u32[]{:S(2)}) copy-start(bf16[6,16,1024]{2,1,0:T(8,128)(2,1)} %copy-done.8) | copy-start | bytes 589828
  192.9 19.0 %copy-start.11 = (bf16[16,512]{1,0:T(8,128)(2,1)S(1)}, bf16[16,512]{1,0:T(8,128)(2,1)}, u32[]{:S(2)}) copy-start(bf16[16,512]{1,0:T(8,128)(2,1)} %copy-done.10) | copy-start | bytes 49156
  193.0 19.0 %copy-start.13 = (bf16[16,512]{1,0:T(8,128)(2,1)S(1)}, bf16[16,512]{1,0:T(8,128)(2,1)}, u32[]{:S(2)}) copy-start(bf16[16,512]{1,0:T(8,128)(2,1)} %copy-done.12) | copy-start | bytes 49156
  193.0 19.0 %copy-start.15 = (bf16[16,512]{1,0:T(8,128)(2,1)S(1)}, bf16[16,512]{1,0:T(8,128)(2,1)}, u32[]{:S(2)}) copy-start(bf16[16,512]{1,0:T(8,128)(2,1)} %copy-done.14) | copy-start | bytes 49156
  193.0 19.0 %copy-start.17 = (s32[24]{0:T(128)S(1)}, s32[24]{0:T(128)}, u32[]{:S(2)}) copy-start(s32[24]{0:T(128)} %get-tuple-element.15.start_ref) | copy-start | bytes 292
  193.0 19.0 %copy-start.19 = (s32[24]{0:T(128)S(1)}, s32[24]{0:T(128)}, u32[]{:S(2)}) copy-start(s32[24]{0:T(128)} %get-tuple-element.16.end_ref) | copy-start | bytes 292

commit v2 on v1

v2 whole, which is shorter than its diff:
```python
import functools

import jax
import jax.numpy as jnp
from jax import lax
from jax.experimental import pallas as pl
from jax.experimental.pallas import tpu as pltpu
from jax.sharding import PartitionSpec as P

CAP = 6
PIECES = 2
VMEM_LIMIT = 48 * 1024 * 1024
F32 = jnp.float32
BF16 = jnp.bfloat16


def product_kernel(rows_ref, weight_ref, ids_ref, out_ref, ids_out_ref):
    out_ref[0] = jnp.dot(
        rows_ref[...], weight_ref[...], preferred_element_type=F32
    ).astype(out_ref.dtype)

    @pl.when(jnp.logical_and(pl.program_id(0) == 0, pl.program_id(1) == 0))
    def _():
        for s in range(ids_ref.shape[1]):
            ids_out_ref[0, s] = ids_ref[0, s]


def base_piece(rows, weight, ids, blocks, piece, pieces, tile):
    row_total, depth = rows.shape
    cols = weight.shape[1] // blocks
    width = cols // pieces
    tiles = width // tile
    return pl.pallas_call(
        product_kernel,
        grid=(blocks, tiles),
        in_specs=[
            pl.BlockSpec((row_total, depth), lambda d, j: (0, 0)),
            pl.BlockSpec((depth, tile), lambda d, j: (0, (d * pieces + piece) * tiles + j)),
            pl.BlockSpec(memory_space=pltpu.SMEM),
        ],
        out_specs=[
            pl.BlockSpec((1, row_total, tile), lambda d, j: (d, 0, j)),
            pl.BlockSpec(memory_space=pltpu.SMEM),
        ],
        out_shape=[
            jax.ShapeDtypeStruct((blocks, row_total, width), BF16),
            jax.ShapeDtypeStruct(ids.shape, ids.dtype),
        ],
        compiler_params=pltpu.CompilerParams(vmem_limit_bytes=VMEM_LIMIT),
        cost_estimate=pl.CostEstimate(
            flops=2 * row_total * depth * width * blocks,
            bytes_accessed=2 * (row_total * depth + (depth + row_total) * width * blocks),
            transcendentals=0,
        ),
        name="base_piece",
    )(rows, weight, ids)


def pick_kernel(peers, me_ref, table_ref, lens_ref, *rest):
    ids_refs = rest[:peers]
    down_ref, up_ref = rest[peers : peers + 2]
    packs = rest[peers + 2 : 2 * peers + 2]
    start_ref, end_ref, pick_ref, sem = rest[2 * peers + 2 :]
    segs = lens_ref.shape[1]
    share, _, depth = down_ref.shape
    cols = up_ref.shape[2]
    me = me_ref[0]

    def clear(q, carry):
        pick_ref[q] = 0
        start_ref[q] = 0
        end_ref[q] = 0
        return carry

    lax.fori_loop(0, peers * CAP, clear, 0)

    def copies(k, c, source):
        return (
            pltpu.make_async_copy(down_ref.at[source], packs[k].at[c, :, pl.ds(0, depth)], sem),
            pltpu.make_async_copy(up_ref.at[source], packs[k].at[c, :, pl.ds(depth, cols)], sem),
        )

    for k in range(peers):

        def choose(s, count):
            local = table_ref[ids_refs[k][0, s]] - me * share
            mine = jnp.logical_and(local >= 0, local < share)

            @pl.when(jnp.logical_and(mine, count < CAP))
            def _():
                pick_ref[k * CAP + count] = local

            return count + mine.astype(jnp.int32)

        lax.fori_loop(0, segs, choose, 0)
        for c in range(CAP):
            for copy in copies(k, c, pick_ref[k * CAP + c]):
                copy.start()

    for k in range(peers):
        owner = lax.rem(me + peers - k, peers)

        def place(s, carry):
            count, first = carry
            local = table_ref[ids_refs[0][0, s]] - owner * share
            theirs = jnp.logical_and(local >= 0, local < share)
            last = first + lens_ref[0, s]

            @pl.when(jnp.logical_and(theirs, count < CAP))
            def _():
                start_ref[k * CAP + count] = first
                end_ref[k * CAP + count] = last

            return count + theirs.astype(jnp.int32), last

        lax.fori_loop(0, segs, place, (0, 0))

    for k in range(peers):
        for c in range(CAP):
            for copy in copies(k, c, 0):
                copy.wait()


def pick_adapters(me, table, all_ids, lens, down, up):
    peers = len(all_ids)
    _, rank, depth = down.shape
    cols = up.shape[2]
    smem = pl.BlockSpec(memory_space=pltpu.SMEM)
    vmem = pl.BlockSpec(memory_space=pltpu.VMEM)
    hbm = pl.BlockSpec(memory_space=pl.ANY)
    out = pl.pallas_call(
        functools.partial(pick_kernel, peers),
        in_specs=[smem] * (3 + peers) + [hbm, hbm],
        out_specs=[vmem] * peers + [smem, smem],
        out_shape=[jax.ShapeDtypeStruct((CAP, rank, depth + cols), BF16)] * peers
        + [jax.ShapeDtypeStruct((peers * CAP,), jnp.int32)] * 2,
        scratch_shapes=[pltpu.SMEM((peers * CAP,), jnp.int32), pltpu.SemaphoreType.DMA],
        compiler_params=pltpu.CompilerParams(vmem_limit_bytes=VMEM_LIMIT),
        cost_estimate=pl.CostEstimate(
            flops=0, bytes_accessed=4 * peers * CAP * rank * (depth + cols), transcendentals=0
        ),
        name="pick_adapters",
    )(me.reshape(1), table, lens, *all_ids, down, up)
    return out[:peers], out[peers], out[peers + 1]


def low_kernel(start_ref, end_ref, rows_ref, *rest):
    packs, out_ref = rest[:-1], rest[-1]
    row_total, depth = rows_ref.shape
    rank = out_ref.shape[0]
    place = lax.broadcasted_iota(jnp.int32, (rank, row_total), 1)
    total = jnp.zeros((rank, row_total), F32)
    for k, pack_ref in enumerate(packs):
        part = lax.dot_general(
            pack_ref[:, :, :depth].reshape(CAP * rank, depth),
            rows_ref[...],
            (((1,), (1,)), ((), ())),
            preferred_element_type=F32,
        )
        for c in range(CAP):
            q = k * CAP + c
            member = jnp.logical_and(place >= start_ref[q], place < end_ref[q])
            total = jnp.where(member, part[c * rank : (c + 1) * rank], total)
    out_ref[...] = total.astype(BF16)


def low_sums(starts, ends, rows, packs, rank):
    row_total, depth = rows.shape
    smem = pl.BlockSpec(memory_space=pltpu.SMEM)
    vmem = pl.BlockSpec(memory_space=pltpu.VMEM)
    return pl.pallas_call(
        low_kernel,
        in_specs=[smem, smem] + [vmem] * (1 + len(packs)),
        out_specs=vmem,
        out_shape=jax.ShapeDtypeStruct((rank, row_total), BF16),
        compiler_params=pltpu.CompilerParams(vmem_limit_bytes=VMEM_LIMIT),
        cost_estimate=pl.CostEstimate(
            flops=2 * row_total * depth * CAP * rank * len(packs),
            bytes_accessed=2 * depth * (row_total + CAP * rank * len(packs)),
            transcendentals=0,
        ),
        name="low_sums",
    )(starts, ends, rows, *packs)


def term_kernel(lows, start_ref, end_ref, *rest):
    low_refs, pack_refs, out_ref = rest[:lows], rest[lows:-1], rest[-1]
    rank, row_total = low_refs[0].shape
    cols = out_ref.shape[1]
    low = low_refs[0][...].astype(F32)
    for ref in low_refs[1:]:
        low = low + ref[...].astype(F32)
    low = low.astype(BF16).astype(F32)
    place = lax.broadcasted_iota(jnp.int32, (rank, row_total), 1)
    term = jnp.zeros(out_ref.shape, F32)
    for k, pack_ref in enumerate(pack_refs):
        spread = []
        for c in range(CAP):
            q = k * CAP + c
            member = jnp.logical_and(place >= start_ref[q], place < end_ref[q])
            spread.append(jnp.where(member, low, 0.0))
        spread = jnp.concatenate(spread, axis=0).astype(BF16)
        ups = pack_ref[:, :, pack_ref.shape[2] - cols :].reshape(CAP * rank, cols)
        term = term + lax.dot_general(
            spread, ups, (((0,), (0,)), ((), ())), preferred_element_type=F32
        )
    out_ref[...] = term


def adapter_term(starts, ends, lows, packs, cols):
    rank, row_total = lows[0].shape
    smem = pl.BlockSpec(memory_space=pltpu.SMEM)
    vmem = pl.BlockSpec(memory_space=pltpu.VMEM)
    return pl.pallas_call(
        functools.partial(term_kernel, len(lows)),
        in_specs=[smem, smem] + [vmem] * (len(lows) + len(packs)),
        out_specs=vmem,
        out_shape=jax.ShapeDtypeStruct((row_total, cols), F32),
        compiler_params=pltpu.CompilerParams(vmem_limit_bytes=VMEM_LIMIT),
        cost_estimate=pl.CostEstimate(
            flops=2 * row_total * cols * CAP * rank * len(packs),
            bytes_accessed=4 * row_total * cols,
            transcendentals=0,
        ),
        name="adapter_term",
    )(starts, ends, *lows, *packs)


def finish_kernel(term_ref, *rest):
    base_refs, out_ref = rest[:-1], rest[-1]
    width = base_refs[0].shape[1]
    for p, ref in enumerate(base_refs):
        cols = slice(p * width, (p + 1) * width)
        out_ref[:, cols] = (ref[...].astype(F32) + term_ref[:, cols]).astype(out_ref.dtype)


def finish(term, bases):
    row_total, cols = term.shape
    height = min(row_total, 128)
    return pl.pallas_call(
        finish_kernel,
        grid=(row_total // height,),
        in_specs=[pl.BlockSpec((height, cols), lambda i: (i, 0))]
        + [pl.BlockSpec((height, b.shape[1]), lambda i: (i, 0)) for b in bases],
        out_specs=pl.BlockSpec((height, cols), lambda i: (i, 0)),
        out_shape=jax.ShapeDtypeStruct((row_total, cols), BF16),
        compiler_params=pltpu.CompilerParams(vmem_limit_bytes=VMEM_LIMIT),
        cost_estimate=pl.CostEstimate(
            flops=row_total * cols, bytes_accessed=8 * row_total * cols, transcendentals=0
        ),
        name="finish",
    )(term, *bases)


def local(req_total, tp_total, rows, weight, down, up, table, ids, lens):
    rank = down.shape[1]
    cols = up.shape[2]
    tile = min(256, cols // PIECES)
    me_req = lax.axis_index("req").astype(jnp.int32)

    bases = []
    for piece in range(PIECES):
        product, ids = base_piece(rows, weight, ids, tp_total, piece, PIECES, tile)
        if piece == 0:
            first_ids = ids
        bases.append(lax.psum_scatter(product, "tp", scatter_dimension=0, tiled=False))

    all_ids = [first_ids]
    for k in range(1, req_total):
        back = [((i + k) % req_total, i) for i in range(req_total)]
        all_ids.append(lax.ppermute(first_ids, "req", back))
    packs, starts, ends = pick_adapters(me_req, table, all_ids, lens, down, up)
    held = [packs[0]]
    for k in range(1, req_total):
        ahead = [(i, (i + k) % req_total) for i in range(req_total)]
        held.append(lax.ppermute(packs[k], "req", ahead))

    low = low_sums(starts, ends, rows, held, rank)
    lows = [low]
    for k in range(1, tp_total):
        lows.append(lax.ppermute(low, "tp", [(i, (i + k) % tp_total) for i in range(tp_total)]))
    term = adapter_term(starts, ends, lows, held, cols)
    return finish(term, bases)


def solution(mesh):
    return jax.shard_map(
        functools.partial(local, mesh.shape["req"], mesh.shape["tp"]),
        mesh=mesh,
        in_specs=(
            P(("groups", "req"), "tp"),
            P("tp", None),
            P(("groups", "req"), None, "tp"),
            P(("groups", "req"), None, "tp"),
            P("groups"),
            P(("groups", "req"), None),
            P(("groups", "req"), None),
        ),
        out_specs=P(("groups", "req"), "tp"),
        check_vma=False,
    )
```

time: 217 us -> 124 us (0.57)
  Pallas kernels: 110 us -> 29.3 us
  starting transfers between devices: 53.9 us -> 12.1 us
  waiting for transfers between devices: 38 us -> 59.8 us
  between operations: 0.54 us -> 13.5 us
  other arithmetic: 7.75 us -> 0 us
  local copies, waits for them, and re-layouts: 5.73 us -> 8.48 us
    pallas_call x13 -> x6, Pallas kernels: 110 us -> 29.3 us  [the longest x2 19.1 us: base_piece(): pl.pallas_call(product_kernel, grid=(blocks, tiles), in_specs=[pl.BlockSp...]
    reduce_scatter x0 -> x2, waiting for transfers between devices: none -> 29.1 us  [local(): lax.psum_scatter(product, 'tp', scatter_dimension=0, tiled=False)]
    ppermute x21 -> x6, starting transfers between devices: 34.2 us -> 7.35 us  [the longest x3 4.39 us: local(): all_ids.append(lax.ppermute(first_ids, 'req', back))]
    ppermute x3, starting transfers between devices: 19.6 us -> 4.75 us  [local(): lax.ppermute(low, 'tp', [(i, (i + k) % tp_total) for i in range(tp_total)])]
    ppermute x21 -> x6, waiting for transfers between devices: 38 us -> 25.6 us  [the longest x3 24.3 us: local(): held.append(lax.ppermute(packs[k], 'req', ahead))]
    convert_element_type x6 -> x0, other arithmetic: 7.15 us -> none  [add(): return (a.astype(F32) + b.astype(F32)).astype(BF16)]
    ppermute x3, waiting for transfers between devices: 0.01 us -> 5.09 us  [local(): lax.ppermute(low, 'tp', [(i, (i + k) % tp_total) for i in range(tp_total)])]
    unnamed x48 -> x18, local copies, waits for them, and re-layouts: 5.73 us -> 8.48 us
  transfers between devices with their start and end apart: 24 -> 11, of which waited for: 4 -> 9; matrix products, arithmetic and copies ran while one was open for 4% -> 0% of each run, Pallas kernels for 49% -> 15%
where the time goes in v2:
time: 124 us; the launch traced here: 123 us
  waiting for transfers between devices  59.8 us (48%)
  Pallas kernels  29.3 us (24%)
  between operations  13.5 us (11%)
  starting transfers between devices  12.1 us (10%)
  local copies, waits for them, and re-layouts  8.48 us (7%)
    reduce_scatter x2, waiting for transfers between devices, local(): lax.psum_scatter(product, 'tp', scatter_dimension=0, tiled=False)  29.1 us
    ppermute x3, waiting for transfers between devices, local(): held.append(lax.ppermute(packs[k], 'req', ahead))  24.3 us
    pallas_call x2, Pallas kernels, base_piece(): pl.pallas_call(product_kernel, grid=(blocks, tiles), in_specs=[pl.BlockSp...  19.1 us
    unnamed x18, local copies, waits for them, and re-layouts  8.48 us
    ppermute x3, waiting for transfers between devices, local(): lax.ppermute(low, 'tp', [(i, (i + k) % tp_total) for i in range(tp_total)])  5.09 us
    ppermute x3, starting transfers between devices, local(): lax.ppermute(low, 'tp', [(i, (i + k) % tp_total) for i in range(tp_total)])  4.75 us
    ppermute x3, starting transfers between devices, local(): all_ids.append(lax.ppermute(first_ids, 'req', back))  4.39 us
    pallas_call x1, Pallas kernels, pick_adapters(): pl.pallas_call(functools.partial(pick_kernel, peers), in_specs=[smem] * (...  3.61 us
  transfers between devices with their start and end apart: 11, of which 9 were waited for; matrix products, arithmetic and copies ran while one was open for 0% of the time, Pallas kernels for 15%

profile of v2, /device:TPU:0, one launch (start us, length us, event | category | flops | bytes accessed | tf_op | source)
XLA Modules:
  0.0 123.2 jit_solution(16464933664727687817)
XLA Ops:
  6.5 0.0 reduce-scatter.3.cloned.1.call-start
  6.5 0.0 copy-start
  6.5 1.6 %copy-done = bf16[512,2048]{1,0:T(8,128)(2,1)S(1)} copy-done((bf16[512,2048]{1,0:T(8,128)(2,1)S(1)}, bf16[512,2048]{1,0:T(8,128)(2,1)}, u32[]{:S(2)}) %copy-start) | copy-done | bytes 2097176
  8.1 0.0 copy-start.7
  8.1 0.7 copy-done.7
  8.8 9.5 %base_piece.2 = (bf16[4,512,512]{2,1,0:T(8,128)(2,1)S(1)}, s32[1,12]{1,0:T(1,128)S(1)}) custom-call(bf16[512,2048]{1,0:T(8,128)(2,1)S(1)} %copy-done, bf16[2048,4096]{1,0:T(8,128)(2,1)} %weight_ref.3, s32[1,12]{1,0:T(1,128)S(1)} %copy-done.7), custom_call_target="tpu_custom_call" | custom-call | flops 4294967296 | bytes 12582912 | tf_op jit(solution)/shard_map/base_piece/pallas_call | solution.py:33
  18.3 0.0 copy-start.2
  18.3 1.3 %copy-done.2 = bf16[4,512,512]{2,1,0:T(8,128)(2,1)} copy-done((bf16[4,512,512]{2,1,0:T(8,128)(2,1)}, bf16[4,512,512]{2,1,0:T(8,128)(2,1)S(1)}, u32[]{:S(2)}) %copy-start.2) | copy-done | bytes 2097176
  19.7 0.0 copy-start.1
  19.7 0.0 reduce-scatter.3.cloned.1.call-update
  19.7 0.0 reduce-scatter.5.cloned.1.call-start
  19.7 1.5 %copy-done.1 = bf16[512,2048]{1,0:T(8,128)(2,1)S(1)} copy-done((bf16[512,2048]{1,0:T(8,128)(2,1)S(1)}, bf16[512,2048]{1,0:T(8,128)(2,1)}, u32[]{:S(2)}) %copy-start.1) | copy-done | bytes 2097176
  21.3 9.6 %base_piece.3 = (bf16[4,512,512]{2,1,0:T(8,128)(2,1)S(1)}, s32[1,12]{1,0:T(1,128)}) custom-call(bf16[512,2048]{1,0:T(8,128)(2,1)S(1)} %copy-done.1, bf16[2048,4096]{1,0:T(8,128)(2,1)} %weight_ref.3, s32[1,12]{1,0:T(1,128)S(1)} %get-tuple-element.14.rest_0_.ids_ref), custom_call_target="tpu_custom_call" | custom-call | flops 4294967296 | bytes 12582912 | tf_op jit(solution)/shard_map/base_piece/pallas_call | solution.py:33
  30.8 0.0 copy-start.3
  30.9 1.3 %copy-done.3 = bf16[4,512,512]{2,1,0:T(8,128)(2,1)} copy-done((bf16[4,512,512]{2,1,0:T(8,128)(2,1)}, bf16[4,512,512]{2,1,0:T(8,128)(2,1)S(1)}, u32[]{:S(2)}) %copy-start.3) | copy-done | bytes 2097176
  32.2 0.0 copy-start.6
  32.2 0.0 copy-start.8
  32.2 0.0 reduce-scatter.5.cloned.1.call-update
  32.2 0.5 collective-permute-start.2
  32.6 2.5 %collective-permute-start.1 = (s32[1,12]{1,0:T(1,128)S(1)}, s32[1,12]{1,0:T(1,128)S(1)}, u32[]{:S(2)}, u32[]{:S(2)}) collective-permute-start(s32[1,12]{1,0:T(1,128)S(1)} %get-tuple-element.14.rest_0_.ids_ref), channel_id=1, source_target_pairs={{8,0},{12,4},{0,8},{4,12},{9,1},{13,5},{1,9},{5,13},{10,2},{14,6},... | collective-permute-start | bytes 152 | tf_op jit(solution)/shard_map/ppermute | solution.py:271
  35.2 1.4 %collective-permute-start = (s32[1,12]{1,0:T(1,128)S(1)}, s32[1,12]{1,0:T(1,128)S(1)}, u32[]{:S(2)}, u32[]{:S(2)}) collective-permute-start(s32[1,12]{1,0:T(1,128)S(1)} %get-tuple-element.14.rest_0_.ids_ref), channel_id=1, source_target_pairs={{4,0},{8,4},{12,8},{0,12},{5,1},{9,5},{13,9},{1,13},{6,2},{10,6},{... | collective-permute-start | bytes 152 | tf_op jit(solution)/shard_map/ppermute | solution.py:271
  36.6 0.0 collective-permute-done.2.rest_3_
  36.6 0.1 collective-permute-done.1.rest_2_
  36.7 1.2 collective-permute-done.rest_1_
  37.9 0.0 copy-done.6
  37.9 0.0 copy-done.8
  37.9 3.6 %pick_adapters.1 = (bf16[6,16,3072]{2,1,0:T(8,128)(2,1)S(1)}, bf16[6,16,3072]{2,1,0:T(8,128)(2,1)S(1)}, bf16[6,16,3072]{2,1,0:T(8,128)(2,1)S(1)}, bf16[6,16,3072...) custom-call(s32[1]{0:T(128)} %bitcast.me_ref, s32[512]{0:T(512)S(1)} %copy-done.6, s32[1,12]{1,0:T(1,128)S(1)} %copy-done.8, ...), custom_call_target="tpu_custom_call" | custom-call | bytes 4718592 | tf_op jit(solution)/shard_map/pick_adapters/pallas_call | solution.py:131
  41.5 0.8 collective-permute-start.3
  42.3 1.8 %collective-permute-start.4 = (bf16[6,16,3072]{2,1,0:T(8,128)(2,1)S(1)}, bf16[6,16,3072]{2,1,0:T(8,128)(2,1)S(1)}, u32[]{:S(2)}, u32[]{:S(2)}) collective-permute-start(bf16[6,16,3072]{2,1,0:T(8,128)(2,1)S(1)} %get-tuple-element.19), channel_id=1, source_target_pairs={{0,8},{4,12},{8,0},{12,4},{1,9},{5,13},{9,1},{13,5},{2,10},{6,14},... | collective-permute-start | bytes 1769480 | tf_op jit(solution)/shard_map/ppermute | solution.py:276
  44.1 0.4 collective-permute-start.5
  44.5 12.2 %collective-permute-done.3.rest_1_.rest_5_ = bf16[6,16,3072]{2,1,0:T(8,128)(2,1)S(1)} collective-permute-done((bf16[6,16,3072]{2,1,0:T(8,128)(2,1)S(1)}, bf16[6,16,3072]{2,1,0:T(8,128)(2,1)S(1)}, u32[]{:S(2)}, u32[]{:S(2)}) %collective-permute-start.3) | collective-permute-done | bytes 589856 | tf_op jit(solution)/shard_map/ppermute | solution.py:276
  56.7 1.8 %collective-permute-done.4.rest_2_.rest_6_ = bf16[6,16,3072]{2,1,0:T(8,128)(2,1)S(1)} collective-permute-done((bf16[6,16,3072]{2,1,0:T(8,128)(2,1)S(1)}, bf16[6,16,3072]{2,1,0:T(8,128)(2,1)S(1)}, u32[]{:S(2)}, u32[]{:S(2)}) %collective-permute-start.4) | collective-permute-done | bytes 589856 | tf_op jit(solution)/shard_map/ppermute | solution.py:276
  58.5 10.3 %collective-permute-done.5.rest_3_.rest_7_ = bf16[6,16,3072]{2,1,0:T(8,128)(2,1)S(1)} collective-permute-done((bf16[6,16,3072]{2,1,0:T(8,128)(2,1)S(1)}, bf16[6,16,3072]{2,1,0:T(8,128)(2,1)S(1)}, u32[]{:S(2)}, u32[]{:S(2)}) %collective-permute-start.5) | collective-permute-done | bytes 589856 | tf_op jit(solution)/shard_map/ppermute | solution.py:276
  68.8 3.2 %low_sums.1.rest_0_ = bf16[16,512]{1,0:T(8,128)(2,1)S(1)} custom-call(s32[24]{0:T(128)S(1)} %get-tuple-element.15.start_ref, s32[24]{0:T(128)S(1)} %get-tuple-element.16.end_ref, bf16[512,2048]{1,0:T(8,128)(2,1)S(1)} %copy-done.1, bf16[6,16,3072]{2,1,0:T(8,128)(2,1)S(1)} %get-tuple-element.17.rest_0_.rest_4_, ...), custom_call_target="tpu_custom_call" | custom-call | flops 805306368 | bytes 3670016 | tf_op jit(solution)/shard_map/low_sums/pallas_call | solution.py:171
  72.0 3.8 %collective-permute-start.8 = (bf16[16,512]{1,0:T(8,128)(2,1)S(1)}, bf16[16,512]{1,0:T(8,128)(2,1)S(1)}, u32[]{:S(2)}, u32[]{:S(2)}) collective-permute-start(bf16[16,512]{1,0:T(8,128)(2,1)S(1)} %low_sums.1.rest_0_), channel_id=1, source_target_pairs={{0,3},{1,0},{2,1},{3,2},{4,7},{5,4},{6,5},{7,6},{8,11},{9,8},{10,9... | collective-permute-start | bytes 49160 | tf_op jit(solution)/shard_map/ppermute | solution.py:281
  75.7 0.0 collective-permute-start.7
  75.7 1.0 collective-permute-start.6
  76.7 0.7 collective-permute-done.8.rest_3_
  77.4 3.5 %collective-permute-done.7.rest_2_ = bf16[16,512]{1,0:T(8,128)(2,1)S(1)} collective-permute-done((bf16[16,512]{1,0:T(8,128)(2,1)S(1)}, bf16[16,512]{1,0:T(8,128)(2,1)S(1)}, u32[]{:S(2)}, u32[]{:S(2)}) %collective-permute-start.7) | collective-permute-done | bytes 16416 | tf_op jit(solution)/shard_map/ppermute | solution.py:281
  80.9 0.9 collective-permute-done.6.rest_1_
  81.8 1.8 %adapter_term.1.term_ref = f32[512,1024]{1,0:T(8,128)S(1)} custom-call(s32[24]{0:T(128)S(1)} %get-tuple-element.15.start_ref, s32[24]{0:T(128)S(1)} %get-tuple-element.16.end_ref, bf16[16,512]{1,0:T(8,128)(2,1)S(1)} %low_sums.1.rest_0_, bf16[16,512]{1,0:T(8,128)(2,1)S(1)} %collective-permute-done.6.rest_1_, ...), custom_call_target="tpu_custom_call" | custom-call | flops 402653184 | bytes 2097152 | tf_op jit(solution)/shard_map/adapter_term/pallas_call | solution.py:214
  83.6 0.0 reduce-scatter.3.cloned.1.call-done
  83.7 29.1 %reduce-scatter.5.cloned.1.call-done = bf16[1,512,512]{2,1,0:T(8,128)(2,1)} async-done(((bf16[4,512,512]{2,1,0:T(8,128)(2,1)}), bf16[1,512,512]{2,1,0:T(8,128)(2,1)}) %reduce-scatter.5.cloned.1.call-update) | async-done | bytes 524304 | tf_op jit(solution)/shard_map/reduce_scatter | solution.py:266
  112.7 0.0 copy-start.4
  112.7 1.0 copy-done.4
  113.8 0.0 copy-start.5
  113.8 1.0 copy-done.5
  114.8 1.6 %finish.1 = bf16[512,1024]{1,0:T(8,128)(2,1)} custom-call(f32[512,1024]{1,0:T(8,128)S(1)} %adapter_term.1.term_ref, bf16[512,512]{1,0:T(8,128)(2,1)S(1)} %bitcast.3, bf16[512,512]{1,0:T(8,128)(2,1)S(1)} %bitcast.4), custom_call_target="tpu_custom_call" | custom-call | flops 524288 | bytes 4194304 | tf_op jit(solution)/shard_map/finish/pallas_call | solution.py:240
Async XLA Ops:
  6.5 77.1 %reduce-scatter.3.cloned.1.call-start = ((), (), s32[]{:S(2)}) async-start(), calls=%async_computation.2 | async-start | bytes 2621440 | tf_op jit(solution)/shard_map/reduce_scatter | solution.py:266
  6.5 1.6 %copy-start = (bf16[512,2048]{1,0:T(8,128)(2,1)S(1)}, bf16[512,2048]{1,0:T(8,128)(2,1)}, u32[]{:S(2)}) copy-start(bf16[512,2048]{1,0:T(8,128)(2,1)} %rows_ref.5) | copy-start | bytes 6291460
  8.1 0.7 copy-start.7
  18.3 1.3 %copy-start.2 = (bf16[4,512,512]{2,1,0:T(8,128)(2,1)}, bf16[4,512,512]{2,1,0:T(8,128)(2,1)S(1)}, u32[]{:S(2)}) copy-start(bf16[4,512,512]{2,1,0:T(8,128)(2,1)S(1)} %get-tuple-element.21) | copy-start | bytes 6291460
  19.7 1.6 %copy-start.1 = (bf16[512,2048]{1,0:T(8,128)(2,1)S(1)}, bf16[512,2048]{1,0:T(8,128)(2,1)}, u32[]{:S(2)}) copy-start(bf16[512,2048]{1,0:T(8,128)(2,1)} %rows_ref.5) | copy-start | bytes 6291460
  19.7 93.0 %reduce-scatter.5.cloned.1.call-start = ((), (), s32[]{:S(2)}) async-start(), calls=%async_computation.3 | async-start | bytes 2621440 | tf_op jit(solution)/shard_map/reduce_scatter | solution.py:266
  30.8 1.3 %copy-start.3 = (bf16[4,512,512]{2,1,0:T(8,128)(2,1)}, bf16[4,512,512]{2,1,0:T(8,128)(2,1)S(1)}, u32[]{:S(2)}) copy-start(bf16[4,512,512]{2,1,0:T(8,128)(2,1)S(1)} %get-tuple-element.22) | copy-start | bytes 6291460
  32.2 5.7 %copy-start.6 = (s32[512]{0:T(512)S(1)}, s32[512]{0:T(512)}, u32[]{:S(2)}) copy-start(s32[512]{0:T(512)} %table_ref.1) | copy-start | bytes 6148
  32.2 5.7 %copy-start.8 = (s32[1,12]{1,0:T(1,128)S(1)}, s32[1,12]{1,0:T(1,128)}, u32[]{:S(2)}) copy-start(s32[1,12]{1,0:T(1,128)} %lens_ref.1) | copy-start | bytes 148
  32.2 4.4 %collective-permute-start.2 = (s32[1,12]{1,0:T(1,128)S(1)}, s32[1,12]{1,0:T(1,128)S(1)}, u32[]{:S(2)}, u32[]{:S(2)}) collective-permute-start(s32[1,12]{1,0:T(1,128)S(1)} %get-tuple-element.14.rest_0_.ids_ref), channel_id=1, source_target_pairs={{12,0},{0,4},{4,8},{8,12},{13,1},{1,5},{5,9},{9,13},{14,2},{2,6},{... | collective-permute-start | bytes 152 | tf_op jit(solution)/shard_map/ppermute | solution.py:271
  32.6 4.1 %collective-permute-start.1 = (s32[1,12]{1,0:T(1,128)S(1)}, s32[1,12]{1,0:T(1,128)S(1)}, u32[]{:S(2)}, u32[]{:S(2)}) collective-permute-start(s32[1,12]{1,0:T(1,128)S(1)} %get-tuple-element.14.rest_0_.ids_ref), channel_id=1, source_target_pairs={{8,0},{12,4},{0,8},{4,12},{9,1},{13,5},{1,9},{5,13},{10,2},{14,6},... | collective-permute-start | bytes 152 | tf_op jit(solution)/shard_map/ppermute | solution.py:271
  35.2 2.7 %collective-permute-start = (s32[1,12]{1,0:T(1,128)S(1)}, s32[1,12]{1,0:T(1,128)S(1)}, u32[]{:S(2)}, u32[]{:S(2)}) collective-permute-start(s32[1,12]{1,0:T(1,128)S(1)} %get-tuple-element.14.rest_0_.ids_ref), channel_id=1, source_target_pairs={{4,0},{8,4},{12,8},{0,12},{5,1},{9,5},{13,9},{1,13},{6,2},{10,6},{... | collective-permute-start | bytes 152 | tf_op jit(solution)/shard_map/ppermute | solution.py:271
  41.5 15.2 %collective-permute-start.3 = (bf16[6,16,3072]{2,1,0:T(8,128)(2,1)S(1)}, bf16[6,16,3072]{2,1,0:T(8,128)(2,1)S(1)}, u32[]{:S(2)}, u32[]{:S(2)}) collective-permute-start(bf16[6,16,3072]{2,1,0:T(8,128)(2,1)S(1)} %get-tuple-element.18), channel_id=1, source_target_pairs={{0,4},{4,8},{8,12},{12,0},{1,5},{5,9},{9,13},{13,1},{2,6},{6,10},{... | collective-permute-start | bytes 1769480 | tf_op jit(solution)/shard_map/ppermute | solution.py:276
  42.3 16.2 %collective-permute-start.4 = (bf16[6,16,3072]{2,1,0:T(8,128)(2,1)S(1)}, bf16[6,16,3072]{2,1,0:T(8,128)(2,1)S(1)}, u32[]{:S(2)}, u32[]{:S(2)}) collective-permute-start(bf16[6,16,3072]{2,1,0:T(8,128)(2,1)S(1)} %get-tuple-element.19), channel_id=1, source_target_pairs={{0,8},{4,12},{8,0},{12,4},{1,9},{5,13},{9,1},{13,5},{2,10},{6,14},... | collective-permute-start | bytes 1769480 | tf_op jit(solution)/shard_map/ppermute | solution.py:276
  44.1 24.7 %collective-permute-start.5 = (bf16[6,16,3072]{2,1,0:T(8,128)(2,1)S(1)}, bf16[6,16,3072]{2,1,0:T(8,128)(2,1)S(1)}, u32[]{:S(2)}, u32[]{:S(2)}) collective-permute-start(bf16[6,16,3072]{2,1,0:T(8,128)(2,1)S(1)} %get-tuple-element.20), channel_id=1, source_target_pairs={{0,12},{4,0},{8,4},{12,8},{1,13},{5,1},{9,5},{13,9},{2,14},{6,2},{... | collective-permute-start | bytes 1769480 | tf_op jit(solution)/shard_map/ppermute | solution.py:276
  72.0 5.4 %collective-permute-start.8 = (bf16[16,512]{1,0:T(8,128)(2,1)S(1)}, bf16[16,512]{1,0:T(8,128)(2,1)S(1)}, u32[]{:S(2)}, u32[]{:S(2)}) collective-permute-start(bf16[16,512]{1,0:T(8,128)(2,1)S(1)} %low_sums.1.rest_0_), channel_id=1, source_target_pairs={{0,3},{1,0},{2,1},{3,2},{4,7},{5,4},{6,5},{7,6},{8,11},{9,8},{10,9... | collective-permute-start | bytes 49160 | tf_op jit(solution)/shard_map/ppermute | solution.py:281
  75.7 5.1 %collective-permute-start.7 = (bf16[16,512]{1,0:T(8,128)(2,1)S(1)}, bf16[16,512]{1,0:T(8,128)(2,1)S(1)}, u32[]{:S(2)}, u32[]{:S(2)}) collective-permute-start(bf16[16,512]{1,0:T(8,128)(2,1)S(1)} %low_sums.1.rest_0_), channel_id=1, source_target_pairs={{0,2},{1,3},{2,0},{3,1},{4,6},{5,7},{6,4},{7,5},{8,10},{9,11},{10,... | collective-permute-start | bytes 49160 | tf_op jit(solution)/shard_map/ppermute | solution.py:281
  75.7 6.1 %collective-permute-start.6 = (bf16[16,512]{1,0:T(8,128)(2,1)S(1)}, bf16[16,512]{1,0:T(8,128)(2,1)S(1)}, u32[]{:S(2)}, u32[]{:S(2)}) collective-permute-start(bf16[16,512]{1,0:T(8,128)(2,1)S(1)} %low_sums.1.rest_0_), channel_id=1, source_target_pairs={{0,1},{1,2},{2,3},{3,0},{4,5},{5,6},{6,7},{7,4},{8,9},{9,10},{10,1... | collective-permute-start | bytes 49160 | tf_op jit(solution)/shard_map/ppermute | solution.py:281
  112.7 1.0 copy-start.4
  113.8 1.0 copy-start.5
Sparse Core Ops, SparseCore 0:
  19.8 46.5 reduce-scatter.2
  68.8 43.8 reduce-scatter.4

commit v3 on v2

v3 whole, which is shorter than its diff:
```python
import functools

import jax
import jax.numpy as jnp
from jax import lax
from jax.experimental import pallas as pl
from jax.experimental.pallas import tpu as pltpu
from jax.sharding import PartitionSpec as P

CAP = 6
PIECES = 2
VMEM_LIMIT = 48 * 1024 * 1024
F32 = jnp.float32
BF16 = jnp.bfloat16
SMALL = pl.CostEstimate(flops=1000, bytes_accessed=1000, transcendentals=0)


def product_kernel(tile_ref, rows_ref, weight_ref, *rest):
    out_ref = rest[-1]
    out_ref[...] = jnp.dot(
        rows_ref[...], weight_ref[...], preferred_element_type=F32
    ).astype(out_ref.dtype)


def block_product(rows, weight, first, width, after=()):
    row_total, depth = rows.shape
    tile = min(256, width)
    return pl.pallas_call(
        product_kernel,
        grid_spec=pltpu.PrefetchScalarGridSpec(
            num_scalar_prefetch=1,
            grid=(width // tile,),
            in_specs=[
                pl.BlockSpec((row_total, depth), lambda j, t: (0, 0)),
                pl.BlockSpec((depth, tile), lambda j, t: (0, t[0] + j)),
            ]
            + [pl.BlockSpec(memory_space=pl.ANY)] * len(after),
            out_specs=pl.BlockSpec((row_total, tile), lambda j, t: (0, j)),
        ),
        out_shape=jax.ShapeDtypeStruct((row_total, width), BF16),
        compiler_params=pltpu.CompilerParams(vmem_limit_bytes=VMEM_LIMIT),
        cost_estimate=SMALL,
        name="block_product",
    )((first // tile).reshape(1), rows, weight, *after)


def pick_kernel(peers, me_ref, table_ref, lens_ref, *rest):
    ids_refs = rest[:peers]
    down_ref, up_ref = rest[peers : peers + 2]
    near_ref, away_ref, start_ref, end_ref, pick_ref, sem = rest[peers + 2 :]
    segs = lens_ref.shape[1]
    share, _, depth = down_ref.shape
    cols = up_ref.shape[2]
    half = near_ref.shape[0]
    me = me_ref[0]

    def clear(q, carry):
        pick_ref[q] = 0
        start_ref[q] = 0
        end_ref[q] = 0
        return carry

    lax.fori_loop(0, peers * CAP, clear, 0)

    def copies(x, c, source):
        pack = near_ref.at[x, c] if x < half else away_ref.at[x - half, c]
        return (
            pltpu.make_async_copy(down_ref.at[source], pack.at[:, pl.ds(0, depth)], sem),
            pltpu.make_async_copy(up_ref.at[source], pack.at[:, pl.ds(depth, cols)], sem),
        )

    for x in reversed(range(peers)):

        def choose(s, count):
            local = table_ref[ids_refs[x][0, s]] - me * share
            mine = jnp.logical_and(local >= 0, local < share)

            @pl.when(jnp.logical_and(mine, count < CAP))
            def _():
                pick_ref[x * CAP + count] = local

            return count + mine.astype(jnp.int32)

        lax.fori_loop(0, segs, choose, 0)
        for c in range(CAP):
            for copy in copies(x, c, pick_ref[x * CAP + c]):
                copy.start()

    for x in range(peers):
        owner = lax.bitwise_xor(me, jnp.int32(x))

        def place(s, carry):
            count, first = carry
            local = table_ref[ids_refs[0][0, s]] - owner * share
            theirs = jnp.logical_and(local >= 0, local < share)
            last = first + lens_ref[0, s]

            @pl.when(jnp.logical_and(theirs, count < CAP))
            def _():
                start_ref[x * CAP + count] = first
                end_ref[x * CAP + count] = last

            return count + theirs.astype(jnp.int32), last

        lax.fori_loop(0, segs, place, (0, 0))

    for x in range(peers):
        for c in range(CAP):
            for copy in copies(x, c, 0):
                copy.wait()


def pick_adapters(me, table, all_ids, lens, down, up):
    peers = len(all_ids)
    _, rank, depth = down.shape
    cols = up.shape[2]
    smem = pl.BlockSpec(memory_space=pltpu.SMEM)
    vmem = pl.BlockSpec(memory_space=pltpu.VMEM)
    hbm = pl.BlockSpec(memory_space=pl.ANY)
    return pl.pallas_call(
        functools.partial(pick_kernel, peers),
        in_specs=[smem] * (3 + peers) + [hbm, hbm],
        out_specs=[vmem] * 2 + [smem, smem],
        out_shape=[jax.ShapeDtypeStruct((peers // 2, CAP, rank, depth + cols), BF16)] * 2
        + [jax.ShapeDtypeStruct((peers * CAP,), jnp.int32)] * 2,
        scratch_shapes=[pltpu.SMEM((peers * CAP,), jnp.int32), pltpu.SemaphoreType.DMA],
        compiler_params=pltpu.CompilerParams(vmem_limit_bytes=VMEM_LIMIT),
        cost_estimate=SMALL,
        name="pick_adapters",
    )(me.reshape(1), table, lens, *all_ids, down, up)


def exchange(near, away, peers):
    half = peers // 2
    held = {x: [(0, near if x < half else away, x % half)] for x in range(peers)}
    bit = half
    while bit:
        leaving = [(x, *entry) for x in sorted(held) if x & bit for entry in held.pop(x)]
        if bit == half:
            packed = away
        else:
            packed = jnp.stack([array[place] for _, _, array, place in leaving])
        came = lax.ppermute(packed, "req", [(i, i ^ bit) for i in range(peers)])
        for place, (x, origin, _, _) in enumerate(leaving):
            held[x ^ bit].append((origin ^ bit, came, place))
        bit //= 2
    return [(array, place) for _, array, place in sorted(held[0], key=lambda e: e[0])]


def pack_spec(pack, first, width):
    array, place = pack
    block = (1,) + array.shape[1:3] + (width,)
    return pl.BlockSpec(block, lambda i: (place, 0, 0, first // width))


def low_kernel(start_ref, end_ref, rows_ref, *rest):
    down_refs, out_ref = rest[:-1], rest[-1]
    row_total, depth = rows_ref.shape
    rank = out_ref.shape[0]
    place = lax.broadcasted_iota(jnp.int32, (rank, row_total), 1)
    total = jnp.zeros((rank, row_total), F32)
    for x, down_ref in enumerate(down_refs):
        part = lax.dot_general(
            down_ref[...].reshape(CAP * rank, depth),
            rows_ref[...],
            (((1,), (1,)), ((), ())),
            preferred_element_type=F32,
        )
        for c in range(CAP):
            q = x * CAP + c
            member = jnp.logical_and(place >= start_ref[q], place < end_ref[q])
            total = jnp.where(member, part[c * rank : (c + 1) * rank], total)
    out_ref[...] = total


def low_sums(starts, ends, rows, packs, rank):
    row_total, depth = rows.shape
    smem = pl.BlockSpec(memory_space=pltpu.SMEM)
    vmem = pl.BlockSpec(memory_space=pltpu.VMEM)
    return pl.pallas_call(
        low_kernel,
        grid=(1,),
        in_specs=[smem, smem, vmem] + [pack_spec(p, 0, depth) for p in packs],
        out_specs=vmem,
        out_shape=jax.ShapeDtypeStruct((rank, row_total), F32),
        compiler_params=pltpu.CompilerParams(vmem_limit_bytes=VMEM_LIMIT),
        cost_estimate=SMALL,
        name="low_sums",
    )(starts, ends, rows, *[array for array, _ in packs])


def term_kernel(start_ref, end_ref, low_ref, came_ref, *rest):
    up_refs, out_ref = rest[:-1], rest[-1]
    rank, row_total = low_ref.shape
    cols = out_ref.shape[1]
    low = (low_ref[...] + came_ref[...]).astype(BF16).astype(F32)
    place = lax.broadcasted_iota(jnp.int32, (rank, row_total), 1)
    term = jnp.zeros(out_ref.shape, F32)
    for x, up_ref in enumerate(up_refs):
        spread = []
        for c in range(CAP):
            q = x * CAP + c
            member = jnp.logical_and(place >= start_ref[q], place < end_ref[q])
            spread.append(jnp.where(member, low, 0.0))
        spread = jnp.concatenate(spread, axis=0).astype(BF16)
        term = term + lax.dot_general(
            spread,
            up_ref[...].reshape(CAP * rank, cols),
            (((0,), (0,)), ((), ())),
            preferred_element_type=F32,
        )
    out_ref[...] = term


def adapter_term(starts, ends, low, came, packs, cols):
    _, row_total = low.shape
    smem = pl.BlockSpec(memory_space=pltpu.SMEM)
    vmem = pl.BlockSpec(memory_space=pltpu.VMEM)
    depth = packs[0][0].shape[3] - cols
    return pl.pallas_call(
        term_kernel,
        grid=(1,),
        in_specs=[smem, smem, vmem, vmem] + [pack_spec(p, depth, cols) for p in packs],
        out_specs=vmem,
        out_shape=jax.ShapeDtypeStruct((row_total, cols), F32),
        compiler_params=pltpu.CompilerParams(vmem_limit_bytes=VMEM_LIMIT),
        cost_estimate=SMALL,
        name="adapter_term",
    )(starts, ends, low, came, *[array for array, _ in packs])


def finish_kernel(pieces, term_ref, *rest):
    base_refs, out_ref = rest[:-1], rest[-1]
    parts = len(base_refs) // pieces
    width = base_refs[0].shape[1]
    for p in range(pieces):
        cols = slice(p * width, (p + 1) * width)
        total = base_refs[p * parts][...].astype(F32)
        for ref in base_refs[p * parts + 1 : (p + 1) * parts]:
            total = total + ref[...].astype(F32)
        out_ref[:, cols] = (total + term_ref[:, cols]).astype(out_ref.dtype)


def finish(term, bases):
    row_total, cols = term.shape
    height = min(row_total, 128)
    flat = [b for piece in bases for b in piece]
    return pl.pallas_call(
        functools.partial(finish_kernel, len(bases)),
        grid=(row_total // height,),
        in_specs=[pl.BlockSpec((height, cols), lambda i: (i, 0))]
        + [pl.BlockSpec((height, b.shape[1]), lambda i: (i, 0)) for b in flat],
        out_specs=pl.BlockSpec((height, cols), lambda i: (i, 0)),
        out_shape=jax.ShapeDtypeStruct((row_total, cols), BF16),
        compiler_params=pltpu.CompilerParams(vmem_limit_bytes=VMEM_LIMIT),
        cost_estimate=SMALL,
        name="finish",
    )(term, *flat)


def chain_steps(total):
    steps = []
    for t in range(total - 1):
        ahead = total - 1 - t
        moves = [(i, i + 1, i + ahead) for i in range(t + 1)]
        moves += [(total - 1 - i, total - 2 - i, total - 1 - i - ahead) for i in range(t + 1)]
        moves.sort(key=lambda m: min(m[0], total - 1 - m[0]))
        permutes = []
        for move in moves:
            for permute in permutes:
                if all(move[0] != m[0] and move[1] != m[1] for m in permute):
                    permute.append(move)
                    break
            else:
                permutes.append([move])
        operands = []
        for permute in permutes:
            sources = {m[0] for m in permute}
            for operand in operands:
                if not any(m[0] in sources for other in operand for m in other):
                    operand.append(permute)
                    break
            else:
                operands.append([permute])
        steps.append(operands)
    return steps


def by_device(me, values, other):
    result = other
    for device, value in values.items():
        result = jnp.where(me == device, value, result)
    return result


def add(a, *others):
    total = a.astype(F32)
    for other in others:
        total = total + other.astype(F32)
    return total.astype(BF16)


def local(req_total, tp_total, rows, weight, down, up, table, ids, lens):
    rank = down.shape[1]
    cols = up.shape[2]
    width = cols // PIECES
    me_req = lax.axis_index("req").astype(jnp.int32)
    me = lax.axis_index("tp").astype(jnp.int32)

    def partial(block, piece, after=()):
        return block_product(rows, weight, block * cols + piece * width, width, after)

    steps = chain_steps(tp_total)
    arrived = [[] for _ in range(PIECES)]
    order = ()
    for t, operands in enumerate(steps):
        moves = [[m for permute in operand for m in permute] for operand in operands]
        products = [
            [
                partial(by_device(me, {m[0]: m[2] for m in operand}, me), piece, order)
                for operand in moves
            ]
            for piece in range(PIECES)
        ]
        before = [permute for operand in steps[t - 1] for permute in operand] if t else []
        for piece in range(PIECES):
            came = []
            for operand, product in enumerate(products[piece]):
                addends = []
                for number, permute in enumerate(before):
                    needed = {
                        m[0]
                        for m in moves[operand]
                        for b in permute
                        if b[1] == m[0] and b[0] - b[1] == m[0] - m[1]
                    }
                    received = {m[0] for m in moves[operand] for b in permute if b[1] == m[0]}
                    if needed:
                        addend = arrived[piece][number]
                        if needed != received:
                            inside = by_device(me, {d: True for d in needed}, False)
                            addend = jnp.where(inside, addend, jnp.zeros_like(addend))
                        addends.append(addend)
                value = add(product, *addends) if addends else product
                for permute in operands[operand]:
                    came.append(lax.ppermute(value, "tp", [(m[0], m[1]) for m in permute]))
                last = value
            arrived[piece] = came
        order = (last,)
    bases = [[partial(me, piece, order)] + arrived[piece] for piece in range(PIECES)]

    all_ids = [ids]
    for x in range(1, req_total):
        all_ids.append(lax.ppermute(ids, "req", [(i, i ^ x) for i in range(req_total)]))
    near, away, starts, ends = pick_adapters(me_req, table, all_ids, lens, down, up)
    packs = exchange(near, away, req_total)

    low = low_sums(starts, ends, rows, packs, rank)
    bit = 1
    while 2 * bit < tp_total:
        low = low + lax.ppermute(low, "tp", [(i, i ^ bit) for i in range(tp_total)])
        bit *= 2
    came = lax.ppermute(low, "tp", [(i, i ^ bit) for i in range(tp_total)])
    term = adapter_term(starts, ends, low, came, packs, cols)
    return finish(term, bases)


def solution(mesh):
    return jax.shard_map(
        functools.partial(local, mesh.shape["req"], mesh.shape["tp"]),
        mesh=mesh,
        in_specs=(
            P(("groups", "req"), "tp"),
            P("tp", None),
            P(("groups", "req"), None, "tp"),
            P(("groups", "req"), None, "tp"),
            P("groups"),
            P(("groups", "req"), None),
            P(("groups", "req"), None),
        ),
        out_specs=P(("groups", "req"), "tp"),
        check_vma=False,
    )
```

time: 124 us -> 99.2 us (0.80)
  waiting for transfers between devices: 59.8 us -> 14.2 us
  starting transfers between devices: 12.1 us -> 29.5 us
  Pallas kernels: 29.3 us -> 42.6 us
  between operations: 13.5 us -> 0.26 us
  other arithmetic: 0 us -> 8.09 us
  local copies, waits for them, and re-layouts: 8.48 us -> 3.56 us
    reduce_scatter x2 -> x0, waiting for transfers between devices: 29.1 us -> none  [local(): lax.psum_scatter(product, 'tp', scatter_dimension=0, tiled=False)]
    ppermute x9 -> x17, starting transfers between devices: 12.1 us -> 29.5 us  [the longest x10 23 us: local(): came.append(lax.ppermute(value, 'tp', [(m[0], m[1]) for m in permute]))]
    ppermute x9 -> x17, waiting for transfers between devices: 30.7 us -> 14.2 us  [the longest x1 11.5 us: local(): low = low + lax.ppermute(low, 'tp', [(i, i ^ bit) for i in range(tp_total)])]
    pallas_call x5 -> x13, Pallas kernels: 25.7 us -> 38.4 us  [the longest x10 28.6 us: block_product(): pl.pallas_call(product_kernel, grid_spec=pltpu.PrefetchScalarGridSpec(num...]
    convert_element_type x0 -> x6, other arithmetic: none -> 7.97 us  [add(): return total.astype(BF16)]
    unnamed x18 -> x20, local copies, waits for them, and re-layouts: 8.48 us -> 2.41 us
  transfers between devices with their start and end apart: 11 -> 17, of which waited for: 9 -> 3; matrix products, arithmetic and copies ran while one was open for 0% -> 9% of each run, Pallas kernels for 15% -> 36%
where the time goes in v3:
time: 99.2 us; the launch traced here: 98.2 us
  Pallas kernels  42.6 us (43%)
  starting transfers between devices  29.5 us (30%)
  waiting for transfers between devices  14.2 us (14%)
  other arithmetic  8.09 us (8%)
  local copies, waits for them, and re-layouts  3.56 us (4%)
    pallas_call x10, Pallas kernels, block_product(): pl.pallas_call(product_kernel, grid_spec=pltpu.PrefetchScalarGridSpec(num...  28.6 us
    ppermute x10, starting transfers between devices, local(): came.append(lax.ppermute(value, 'tp', [(m[0], m[1]) for m in permute]))  23 us
    ppermute x1, waiting for transfers between devices, local(): low = low + lax.ppermute(low, 'tp', [(i, i ^ bit) for i in range(tp_total)])  11.5 us
    convert_element_type x6, other arithmetic, add(): return total.astype(BF16)  7.97 us
    pallas_call x1, Pallas kernels, pick_adapters(): pl.pallas_call(functools.partial(pick_kernel, peers), in_specs=[smem] * (...  4.26 us
    pallas_call x1, Pallas kernels, finish(): pl.pallas_call(functools.partial(finish_kernel, len(bases)), grid=(row_to...  3.82 us
    pallas_call x1, Pallas kernels, low_sums(): pl.pallas_call(low_kernel, grid=(1,), in_specs=[smem, smem, vmem] + [pack...  3.7 us
    ppermute x1, starting transfers between devices, local(): came = lax.ppermute(low, 'tp', [(i, i ^ bit) for i in range(tp_total)])  3.1 us
  transfers between devices with their start and end apart: 17, of which 3 were waited for; matrix products, arithmetic and copies ran while one was open for 9% of the time, Pallas kernels for 36%

profile of v3, /device:TPU:0, one launch (start us, length us, event | category | flops | bytes accessed | tf_op | source)
XLA Modules:
  0.0 98.2 jit_solution(3668379077595014626)
XLA Ops:
  0.0 1.6 %copy-done = bf16[512,2048]{1,0:T(8,128)(2,1)S(1)} copy-done((bf16[512,2048]{1,0:T(8,128)(2,1)S(1)}, bf16[512,2048]{1,0:T(8,128)(2,1)}, u32[]{:S(2)}) %copy-start) | copy-done | bytes 2097176
  1.6 3.4 %block_product.16 = bf16[512,512]{1,0:T(8,128)(2,1)} custom-call(s32[1]{0:T(128)} %bitcast.7.tile_ref, bf16[512,2048]{1,0:T(8,128)(2,1)S(1)} %copy-done, bf16[2048,4096]{1,0:T(8,128)(2,1)} %weight_ref.19), custom_call_target="tpu_custom_call" | custom-call | flops 1000 | bytes 1000 | tf_op jit(solution)/shard_map/block_product/pallas_call | solution.py:28
  5.0 5.7 %collective-permute-start.9 = (bf16[512,512]{1,0:T(8,128)(2,1)}, bf16[512,512]{1,0:T(8,128)(2,1)}, u32[]{:S(2)}, u32[]{:S(2)}) collective-permute-start(bf16[512,512]{1,0:T(8,128)(2,1)} %block_product.16), channel_id=1, source_target_pairs={{0,1},{3,2},{4,5},{7,6},{8,9},{11,10},{12,13},{15,14},{16,17},{19,... | collective-permute-start | bytes 1572872 | tf_op jit(solution)/shard_map/ppermute | solution.py:346
  10.8 0.0 copy-done.9
  10.8 0.0 collective-permute-start
  10.8 1.5 %collective-permute-start.1 = (s32[1,12]{1,0:T(1,128)S(1)}, s32[1,12]{1,0:T(1,128)S(1)}, u32[]{:S(2)}, u32[]{:S(2)}) collective-permute-start(s32[1,12]{1,0:T(1,128)S(1)} %copy-done.9), channel_id=1, source_target_pairs={{0,8},{4,12},{8,0},{12,4},{1,9},{5,13},{9,1},{13,5},{2,10},{6,14},... | collective-permute-start | bytes 152 | tf_op jit(solution)/shard_map/ppermute | solution.py:354
  12.3 0.3 collective-permute-start.2
  12.6 0.0 collective-permute-done.rest_1_
  12.6 1.7 %collective-permute-done.1.rest_2_ = s32[1,12]{1,0:T(1,128)S(1)} collective-permute-done((s32[1,12]{1,0:T(1,128)S(1)}, s32[1,12]{1,0:T(1,128)S(1)}, u32[]{:S(2)}, u32[]{:S(2)}) %collective-permute-start.1) | collective-permute-done | bytes 80 | tf_op jit(solution)/shard_map/ppermute | solution.py:354
  14.3 0.9 collective-permute-done.2.rest_3_
  15.2 0.0 copy-done.7
  15.3 0.0 copy-done.8
  15.3 4.3 %pick_adapters.1 = (bf16[2,6,16,3072]{3,2,1,0:T(8,128)(2,1)S(1)}, bf16[2,6,16,3072]{3,2,1,0:T(8,128)(2,1)}, s32[24]{0:T(128)S(1)}, s32[24]{0:T(128)S(1)}) custom-call(s32[1]{0:T(128)} %bitcast.me_ref, s32[512]{0:T(512)S(1)} %copy-done.7, s32[1,12]{1,0:T(1,128)S(1)} %copy-done.8, s32[1,12]{1,0:T(1,128)S(1)} %copy-done.9, ...), custom_call_target="tpu_custom_call" | custom-call | flops 1000 | bytes 1000 | tf_op jit(solution)/shard_map/pick_adapters/pallas_call | solution.py:120
  19.5 0.0 copy-start.2
  19.5 0.3 collective-permute-start.3
  19.8 3.5 %block_product.10.rest_0_ = bf16[512,512]{1,0:T(8,128)(2,1)} custom-call(s32[1]{0:T(128)} %bitcast.4.tile_ref, bf16[512,2048]{1,0:T(8,128)(2,1)S(1)} %copy-done.1, bf16[2048,4096]{1,0:T(8,128)(2,1)} %weight_ref.19), custom_call_target="tpu_custom_call" | custom-call | flops 1000 | bytes 1000 | tf_op jit(solution)/shard_map/block_product/pallas_call | solution.py:28
  23.3 2.1 %collective-permute-start.7 = (bf16[512,512]{1,0:T(8,128)(2,1)}, bf16[512,512]{1,0:T(8,128)(2,1)}, u32[]{:S(2)}, u32[]{:S(2)}) collective-permute-start(bf16[512,512]{1,0:T(8,128)(2,1)} %block_product.10.rest_0_), channel_id=1, source_target_pairs={{0,1},{3,2},{4,5},{7,6},{8,9},{11,10},{12,13},{15,14},{16,17},{19,... | collective-permute-start | bytes 1572872 | tf_op jit(solution)/shard_map/ppermute | solution.py:346
  25.4 2.7 %block_product.15 = bf16[512,512]{1,0:T(8,128)(2,1)S(1)} custom-call(s32[1]{0:T(128)} %bitcast.6.tile_ref, bf16[512,2048]{1,0:T(8,128)(2,1)S(1)} %copy-done.1, bf16[2048,4096]{1,0:T(8,128)(2,1)} %weight_ref.19, bf16[512,512]{1,0:T(8,128)(2,1)} %block_product.10.rest_0_), custom_call_target="tpu_custom_call" | custom-call | flops 1000 | bytes 1000 | tf_op jit(solution)/shard_map/block_product/pallas_call | solution.py:28
  28.1 0.0 collective-permute-done.9
  28.1 2.0 %add_convert_fusion.3 = bf16[512,512]{1,0:T(8,128)(2,1)} fusion(bf16[512,512]{1,0:T(8,128)(2,1)} %collective-permute-done.9, bf16[512,512]{1,0:T(8,128)(2,1)S(1)} %block_product.15), kind=kLoop, calls=%fused_computation.4 | loop fusion | flops 1048576 | bytes 1572864 | tf_op jit(solution)/shard_map/convert_element_type | solution.py:300
  30.1 1.5 %collective-permute-start.10 = (bf16[512,512]{1,0:T(8,128)(2,1)}, bf16[512,512]{1,0:T(8,128)(2,1)}, u32[]{:S(2)}, u32[]{:S(2)}) collective-permute-start(bf16[512,512]{1,0:T(8,128)(2,1)} %add_convert_fusion.3), channel_id=1, source_target_pairs={{1,2},{2,1},{5,6},{6,5},{9,10},{10,9},{13,14},{14,13},{17,18},{18,... | collective-permute-start | bytes 1572872 | tf_op jit(solution)/shard_map/ppermute | solution.py:346
  31.6 2.7 %block_product.11 = bf16[512,512]{1,0:T(8,128)(2,1)S(1)} custom-call(s32[1]{0:T(128)} %bitcast.3.tile_ref, bf16[512,2048]{1,0:T(8,128)(2,1)S(1)} %copy-done.1, bf16[2048,4096]{1,0:T(8,128)(2,1)} %weight_ref.19, bf16[512,512]{1,0:T(8,128)(2,1)} %block_product.10.rest_0_), custom_call_target="tpu_custom_call" | custom-call | flops 1000 | bytes 1000 | tf_op jit(solution)/shard_map/block_product/pallas_call | solution.py:28
  34.3 0.8 copy-done.5
  35.1 2.1 %collective-permute-start.12 = (bf16[512,512]{1,0:T(8,128)(2,1)}, bf16[512,512]{1,0:T(8,128)(2,1)S(1)}, u32[]{:S(2)}, u32[]{:S(2)}) collective-permute-start(bf16[512,512]{1,0:T(8,128)(2,1)} %add_convert_fusion.3), channel_id=1, source_target_pairs={{0,1},{3,2},{4,5},{7,6},{8,9},{11,10},{12,13},{15,14},{16,17},{19,... | collective-permute-start | bytes 1572872 | tf_op jit(solution)/shard_map/ppermute | solution.py:346
  37.2 0.0 collective-permute-done.7
  37.2 0.0 copy-done.6
  37.2 1.2 %add_convert_fusion.5.rest_0_ = bf16[512,512]{1,0:T(8,128)(2,1)S(1)} fusion(bf16[512,512]{1,0:T(8,128)(2,1)} %collective-permute-done.7, bf16[512,512]{1,0:T(8,128)(2,1)S(1)} %copy-done.6), kind=kLoop, calls=%fused_computation.6 | loop fusion | flops 1048576 | bytes 1572864 | tf_op jit(solution)/shard_map/convert_element_type | solution.py:300
  38.4 4.0 %collective-permute-start.8 = (bf16[512,512]{1,0:T(8,128)(2,1)S(1)}, bf16[512,512]{1,0:T(8,128)(2,1)S(1)}, u32[]{:S(2)}, u32[]{:S(2)}) collective-permute-start(bf16[512,512]{1,0:T(8,128)(2,1)S(1)} %add_convert_fusion.5.rest_0_), channel_id=1, source_target_pairs={{0,1},{3,2},{4,5},{7,6},{8,9},{11,10},{12,13},{15,14},{16,17},{19,... | collective-permute-start | bytes 1572872 | tf_op jit(solution)/shard_map/ppermute | solution.py:346
  42.4 0.7 collective-permute-start.14
  43.1 2.7 %block_product.12 = bf16[512,512]{1,0:T(8,128)(2,1)S(1)} custom-call(s32[1]{0:T(128)} %bitcast.2.tile_ref, bf16[512,2048]{1,0:T(8,128)(2,1)S(1)} %copy-done.1, bf16[2048,4096]{1,0:T(8,128)(2,1)} %weight_ref.19, bf16[512,512]{1,0:T(8,128)(2,1)S(1)} %add_convert_fusion.5.rest_0_), custom_call_target="tpu_custom_call" | custom-call | flops 1000 | bytes 1000 | tf_op jit(solution)/shard_map/block_product/pallas_call | solution.py:28
  45.8 2.7 %block_product.14 = bf16[512,512]{1,0:T(8,128)(2,1)S(1)} custom-call(s32[1]{0:T(128)} %bitcast.5.tile_ref, bf16[512,2048]{1,0:T(8,128)(2,1)S(1)} %copy-done.1, bf16[2048,4096]{1,0:T(8,128)(2,1)} %weight_ref.19, bf16[512,512]{1,0:T(8,128)(2,1)S(1)} %add_convert_fusion.5.rest_0_), custom_call_target="tpu_custom_call" | custom-call | flops 1000 | bytes 1000 | tf_op jit(solution)/shard_map/block_product/pallas_call | solution.py:28
  48.6 2.7 %block_product.17 = bf16[512,512]{1,0:T(8,128)(2,1)S(1)} custom-call(s32[1]{0:T(128)} %bitcast.8.tile_ref, bf16[512,2048]{1,0:T(8,128)(2,1)S(1)} %copy-done.1, bf16[2048,4096]{1,0:T(8,128)(2,1)} %weight_ref.19, bf16[512,512]{1,0:T(8,128)(2,1)S(1)} %add_convert_fusion.5.rest_0_), custom_call_target="tpu_custom_call" | custom-call | flops 1000 | bytes 1000 | tf_op jit(solution)/shard_map/block_product/pallas_call | solution.py:28
  51.3 2.7 %block_product.19 = bf16[512,512]{1,0:T(8,128)(2,1)S(1)} custom-call(s32[1]{0:T(128)} %bitcast.10.tile_ref, bf16[512,2048]{1,0:T(8,128)(2,1)S(1)} %copy-done.1, bf16[2048,4096]{1,0:T(8,128)(2,1)} %weight_ref.19, bf16[512,512]{1,0:T(8,128)(2,1)S(1)} %add_convert_fusion.5.rest_0_), custom_call_target="tpu_custom_call" | custom-call | flops 1000 | bytes 1000 | tf_op jit(solution)/shard_map/block_product/pallas_call | solution.py:28
  54.0 0.0 collective-permute-done.10
  54.0 2.0 %add_convert_fusion.2 = bf16[512,512]{1,0:T(8,128)(2,1)} fusion(bf16[512,512]{1,0:T(8,128)(2,1)} %collective-permute-done.10, bf16[512,512]{1,0:T(8,128)(2,1)S(1)} %block_product.14), kind=kLoop, calls=%fused_computation.3 | loop fusion | flops 1048576 | bytes 1572864 | tf_op jit(solution)/shard_map/convert_element_type | solution.py:300
  56.0 2.1 %collective-permute-start.11 = (bf16[512,512]{1,0:T(8,128)(2,1)}, bf16[512,512]{1,0:T(8,128)(2,1)}, u32[]{:S(2)}, u32[]{:S(2)}) collective-permute-start(bf16[512,512]{1,0:T(8,128)(2,1)} %add_convert_fusion.2), channel_id=1, source_target_pairs={{0,1},{3,2},{2,3},{1,0},{4,5},{7,6},{6,7},{5,4},{8,9},{11,10},{10,... | collective-permute-start | bytes 1572872 | tf_op jit(solution)/shard_map/ppermute | solution.py:346
  58.1 0.0 collective-permute-done.3.rest_2_
  58.1 1.1 %slice.8 = bf16[1,6,16,3072]{3,2,1,0:T(8,128)(2,1)S(1)} slice(bf16[2,6,16,3072]{3,2,1,0:T(8,128)(2,1)} %collective-permute-done.3.rest_2_), slice={[1:2], [0:6], [0:16], [0:3072]} | slice | bytes 1179648 | tf_op jit(solution)/shard_map/slice | solution.py:142
  59.2 0.1 pad_maximum_fusion
  59.4 0.1 collective-permute-start.4
  59.4 0.0 collective-permute-done.12
  59.4 1.0 add_convert_fusion.1
  60.4 1.5 %collective-permute-start.13 = (bf16[512,512]{1,0:T(8,128)(2,1)}, bf16[512,512]{1,0:T(8,128)(2,1)}, u32[]{:S(2)}, u32[]{:S(2)}) collective-permute-start(bf16[512,512]{1,0:T(8,128)(2,1)} %add_convert_fusion.1), channel_id=1, source_target_pairs={{1,2},{2,1},{5,6},{6,5},{9,10},{10,9},{13,14},{14,13},{17,18},{18,... | collective-permute-start | bytes 1572872 | tf_op jit(solution)/shard_map/ppermute | solution.py:346
  61.9 0.0 collective-permute-done.14
  61.9 0.9 add_convert_fusion
  62.8 1.9 %collective-permute-start.15 = (bf16[512,512]{1,0:T(8,128)(2,1)}, bf16[512,512]{1,0:T(8,128)(2,1)}, u32[]{:S(2)}, u32[]{:S(2)}) collective-permute-start(bf16[512,512]{1,0:T(8,128)(2,1)} %add_convert_fusion), channel_id=1, source_target_pairs={{0,1},{3,2},{2,3},{1,0},{4,5},{7,6},{6,7},{5,4},{8,9},{11,10},{10,... | collective-permute-start | bytes 1572872 | tf_op jit(solution)/shard_map/ppermute | solution.py:346
  64.7 0.0 collective-permute-done.8
  64.7 0.9 add_convert_fusion.4.rest_0_
  65.7 1.5 %collective-permute-start.16 = (bf16[512,512]{1,0:T(8,128)(2,1)}, bf16[512,512]{1,0:T(8,128)(2,1)}, u32[]{:S(2)}, u32[]{:S(2)}) collective-permute-start(bf16[512,512]{1,0:T(8,128)(2,1)} %add_convert_fusion.4.rest_0_), channel_id=1, source_target_pairs={{1,2},{2,1},{5,6},{6,5},{9,10},{10,9},{13,14},{14,13},{17,18},{18,... | collective-permute-start | bytes 1572872 | tf_op jit(solution)/shard_map/ppermute | solution.py:346
  67.1 0.0 collective-permute-done.4.rest_1_.rest_3_
  67.1 0.0 copy-done.3
  67.1 3.7 %low_sums.1 = f32[16,512]{1,0:T(8,128)S(1)} custom-call(s32[24]{0:T(128)S(1)} %get-tuple-element.9.start_ref, s32[24]{0:T(128)S(1)} %get-tuple-element.10.end_ref, bf16[512,2048]{1,0:T(8,128)(2,1)S(1)} %copy-done.1, bf16[2,6,16,3072]{3,2,1,0:T(8,128)(2,1)S(1)} %copy-done.3, bf16[2,6,16,3072]{3,2,1,0:T(8,128)(2,1)S(1)} %collective-permute-done.4.rest_1_.rest_3_, ...), custom_call_target="tpu_custom_call" | custom-call | flops 1000 | bytes 1000 | tf_op jit(solution)/shard_map/low_sums/pallas_call | solution.py:180
  70.8 1.1 %collective-permute-start.5 = (f32[16,512]{1,0:T(8,128)S(1)}, f32[16,512]{1,0:T(8,128)S(1)}, u32[]{:S(2)}, u32[]{:S(2)}) collective-permute-start(f32[16,512]{1,0:T(8,128)S(1)} %low_sums.1), channel_id=1, source_target_pairs={{0,1},{1,0},{2,3},{3,2},{4,5},{5,4},{6,7},{7,6},{8,9},{9,8},{10,11... | collective-permute-start | bytes 98312 | tf_op jit(solution)/shard_map/ppermute | solution.py:361
  71.9 11.5 %collective-permute-done.5 = f32[16,512]{1,0:T(8,128)S(1)} collective-permute-done((f32[16,512]{1,0:T(8,128)S(1)}, f32[16,512]{1,0:T(8,128)S(1)}, u32[]{:S(2)}, u32[]{:S(2)}) %collective-permute-start.5) | collective-permute-done | bytes 32800 | tf_op jit(solution)/shard_map/ppermute | solution.py:361
  83.5 3.1 %collective-permute-start.6 = (f32[16,512]{1,0:T(8,128)S(1)}, f32[16,512]{1,0:T(8,128)S(1)}, u32[]{:S(2)}, u32[]{:S(2)}) collective-permute-start(f32[16,512]{1,0:T(8,128)S(1)} %add.46.low_ref), channel_id=1, source_target_pairs={{0,2},{1,3},{2,0},{3,1},{4,6},{5,7},{6,4},{7,5},{8,10},{9,11},{10,... | collective-permute-start | bytes 98312 | tf_op jit(solution)/shard_map/ppermute | solution.py:363
  86.6 2.7 %block_product.13.rest_0_ = bf16[512,512]{1,0:T(8,128)(2,1)S(1)} custom-call(s32[1]{0:T(128)} %bitcast.1.tile_ref, bf16[512,2048]{1,0:T(8,128)(2,1)S(1)} %copy-done.1, bf16[2048,4096]{1,0:T(8,128)(2,1)} %weight_ref.19, bf16[512,512]{1,0:T(8,128)(2,1)} %add_convert_fusion.4.rest_0_), custom_call_target="tpu_custom_call" | custom-call | flops 1000 | bytes 1000 | tf_op jit(solution)/shard_map/block_product/pallas_call | solution.py:28
  89.3 2.8 %block_product.18.rest_3_ = bf16[512,512]{1,0:T(8,128)(2,1)S(1)} custom-call(s32[1]{0:T(128)} %bitcast.9.tile_ref, bf16[512,2048]{1,0:T(8,128)(2,1)S(1)} %copy-done.1, bf16[2048,4096]{1,0:T(8,128)(2,1)} %weight_ref.19, bf16[512,512]{1,0:T(8,128)(2,1)} %add_convert_fusion.4.rest_0_), custom_call_target="tpu_custom_call" | custom-call | flops 1000 | bytes 1000 | tf_op jit(solution)/shard_map/block_product/pallas_call | solution.py:28
  92.1 0.0 collective-permute-done.6.came_ref
  92.1 2.2 %adapter_term.1.term_ref = f32[512,1024]{1,0:T(8,128)S(1)} custom-call(s32[24]{0:T(128)S(1)} %get-tuple-element.9.start_ref, s32[24]{0:T(128)S(1)} %get-tuple-element.10.end_ref, f32[16,512]{1,0:T(8,128)S(1)} %add.46.low_ref, f32[16,512]{1,0:T(8,128)S(1)} %collective-permute-done.6.came_ref, bf16[2,6,16,3072]{3,2,1,0:T(8,128)(2,1)S(1)} %copy-done.4, ...), custom_call_target="tpu_custom_call" | custom-call | flops 1000 | bytes 1000 | tf_op jit(solution)/shard_map/adapter_term/pallas_call | solution.py:220
  94.3 0.0 collective-permute-done.11.rest_1_
  94.3 0.0 collective-permute-done.13.rest_2_
  94.4 0.0 collective-permute-done.15.rest_4_
  94.4 0.0 collective-permute-done.16.rest_5_
  94.4 3.8 %finish.1 = bf16[512,1024]{1,0:T(8,128)(2,1)} custom-call(f32[512,1024]{1,0:T(8,128)S(1)} %adapter_term.1.term_ref, bf16[512,512]{1,0:T(8,128)(2,1)S(1)} %block_product.13.rest_0_, bf16[512,512]{1,0:T(8,128)(2,1)} %collective-permute-done.11.rest_1_, bf16[512,512]{1,0:T(8,128)(2,1)} %collective-permute-done.13.rest_2_, ...), custom_call_target="tpu_custom_call" | custom-call | flops 1000 | bytes 1000 | tf_op jit(solution)/shard_map/finish/pallas_call | solution.py:248
  (14 shorter events, 0.1 us)
Async XLA Ops:
  0.0 1.6 %copy-start = (bf16[512,2048]{1,0:T(8,128)(2,1)S(1)}, bf16[512,2048]{1,0:T(8,128)(2,1)}, u32[]{:S(2)}) copy-start(bf16[512,2048]{1,0:T(8,128)(2,1)} %rows_ref.21) | copy-start | bytes 6291460
  1.6 9.2 %copy-start.9 = (s32[1,12]{1,0:T(1,128)S(1)}, s32[1,12]{1,0:T(1,128)}, u32[]{:S(2)}) copy-start(s32[1,12]{1,0:T(1,128)} %rest_0_.1) | copy-start | bytes 148
  1.6 13.7 %copy-start.7 = (s32[512]{0:T(512)S(1)}, s32[512]{0:T(512)}, u32[]{:S(2)}) copy-start(s32[512]{0:T(512)} %table_ref.1) | copy-start | bytes 6148
  1.6 13.7 %copy-start.8 = (s32[1,12]{1,0:T(1,128)S(1)}, s32[1,12]{1,0:T(1,128)}, u32[]{:S(2)}) copy-start(s32[1,12]{1,0:T(1,128)} %lens_ref.1) | copy-start | bytes 148
  5.0 23.1 %collective-permute-start.9 = (bf16[512,512]{1,0:T(8,128)(2,1)}, bf16[512,512]{1,0:T(8,128)(2,1)}, u32[]{:S(2)}, u32[]{:S(2)}) collective-permute-start(bf16[512,512]{1,0:T(8,128)(2,1)} %block_product.16), channel_id=1, source_target_pairs={{0,1},{3,2},{4,5},{7,6},{8,9},{11,10},{12,13},{15,14},{16,17},{19,... | collective-permute-start | bytes 1572872 | tf_op jit(solution)/shard_map/ppermute | solution.py:346
  10.8 1.9 %collective-permute-start = (s32[1,12]{1,0:T(1,128)S(1)}, s32[1,12]{1,0:T(1,128)S(1)}, u32[]{:S(2)}, u32[]{:S(2)}) collective-permute-start(s32[1,12]{1,0:T(1,128)S(1)} %copy-done.9), channel_id=1, source_target_pairs={{0,4},{4,0},{8,12},{12,8},{1,5},{5,1},{9,13},{13,9},{2,6},{6,2},{1... | collective-permute-start | bytes 152 | tf_op jit(solution)/shard_map/ppermute | solution.py:354
  10.8 3.5 %collective-permute-start.1 = (s32[1,12]{1,0:T(1,128)S(1)}, s32[1,12]{1,0:T(1,128)S(1)}, u32[]{:S(2)}, u32[]{:S(2)}) collective-permute-start(s32[1,12]{1,0:T(1,128)S(1)} %copy-done.9), channel_id=1, source_target_pairs={{0,8},{4,12},{8,0},{12,4},{1,9},{5,13},{9,1},{13,5},{2,10},{6,14},... | collective-permute-start | bytes 152 | tf_op jit(solution)/shard_map/ppermute | solution.py:354
  12.3 3.0 %collective-permute-start.2 = (s32[1,12]{1,0:T(1,128)S(1)}, s32[1,12]{1,0:T(1,128)S(1)}, u32[]{:S(2)}, u32[]{:S(2)}) collective-permute-start(s32[1,12]{1,0:T(1,128)S(1)} %copy-done.9), channel_id=1, source_target_pairs={{0,12},{4,8},{8,4},{12,0},{1,13},{5,9},{9,5},{13,1},{2,14},{6,10},... | collective-permute-start | bytes 152 | tf_op jit(solution)/shard_map/ppermute | solution.py:354
  15.3 4.6 %copy-start.1 = (bf16[512,2048]{1,0:T(8,128)(2,1)S(1)}, bf16[512,2048]{1,0:T(8,128)(2,1)}, u32[]{:S(2)}) copy-start(bf16[512,2048]{1,0:T(8,128)(2,1)} %rows_ref.21) | copy-start | bytes 6291460
  19.5 15.6 %copy-start.2 = (bf16[2,6,16,3072]{3,2,1,0:T(8,128)(2,1)}, bf16[2,6,16,3072]{3,2,1,0:T(8,128)(2,1)S(1)}, u32[]{:S(2)}) copy-start(bf16[2,6,16,3072]{3,2,1,0:T(8,128)(2,1)S(1)} %get-tuple-element.11.rest_0_) | copy-start | bytes 3538948
  19.5 38.6 %collective-permute-start.3 = (bf16[2,6,16,3072]{3,2,1,0:T(8,128)(2,1)}, bf16[2,6,16,3072]{3,2,1,0:T(8,128)(2,1)}, u32[]{:S(2)}, u32[]{:S(2)}) collective-permute-start(bf16[2,6,16,3072]{3,2,1,0:T(8,128)(2,1)} %get-tuple-element.12), channel_id=1, source_target_pairs={{0,8},{4,12},{8,0},{12,4},{1,9},{5,13},{9,1},{13,5},{2,10},{6,14},... | collective-permute-start | bytes 3538952 | tf_op jit(solution)/shard_map/ppermute | solution.py:143
  23.3 13.9 %collective-permute-start.7 = (bf16[512,512]{1,0:T(8,128)(2,1)}, bf16[512,512]{1,0:T(8,128)(2,1)}, u32[]{:S(2)}, u32[]{:S(2)}) collective-permute-start(bf16[512,512]{1,0:T(8,128)(2,1)} %block_product.10.rest_0_), channel_id=1, source_target_pairs={{0,1},{3,2},{4,5},{7,6},{8,9},{11,10},{12,13},{15,14},{16,17},{19,... | collective-permute-start | bytes 1572872 | tf_op jit(solution)/shard_map/ppermute | solution.py:346
  30.1 23.9 %collective-permute-start.10 = (bf16[512,512]{1,0:T(8,128)(2,1)}, bf16[512,512]{1,0:T(8,128)(2,1)}, u32[]{:S(2)}, u32[]{:S(2)}) collective-permute-start(bf16[512,512]{1,0:T(8,128)(2,1)} %add_convert_fusion.3), channel_id=1, source_target_pairs={{1,2},{2,1},{5,6},{6,5},{9,10},{10,9},{13,14},{14,13},{17,18},{18,... | collective-permute-start | bytes 1572872 | tf_op jit(solution)/shard_map/ppermute | solution.py:346
  34.3 0.8 copy-start.5
  35.1 2.1 %copy-start.6 = (bf16[512,512]{1,0:T(8,128)(2,1)S(1)}, bf16[512,512]{1,0:T(8,128)(2,1)}, u32[]{:S(2)}) copy-start(bf16[512,512]{1,0:T(8,128)(2,1)} %copy-done.5) | copy-start | bytes 1572868
  35.1 24.3 %collective-permute-start.12 = (bf16[512,512]{1,0:T(8,128)(2,1)}, bf16[512,512]{1,0:T(8,128)(2,1)S(1)}, u32[]{:S(2)}, u32[]{:S(2)}) collective-permute-start(bf16[512,512]{1,0:T(8,128)(2,1)} %add_convert_fusion.3), channel_id=1, source_target_pairs={{0,1},{3,2},{4,5},{7,6},{8,9},{11,10},{12,13},{15,14},{16,17},{19,... | collective-permute-start | bytes 1572872 | tf_op jit(solution)/shard_map/ppermute | solution.py:346
  38.4 26.3 %collective-permute-start.8 = (bf16[512,512]{1,0:T(8,128)(2,1)S(1)}, bf16[512,512]{1,0:T(8,128)(2,1)S(1)}, u32[]{:S(2)}, u32[]{:S(2)}) collective-permute-start(bf16[512,512]{1,0:T(8,128)(2,1)S(1)} %add_convert_fusion.5.rest_0_), channel_id=1, source_target_pairs={{0,1},{3,2},{4,5},{7,6},{8,9},{11,10},{12,13},{15,14},{16,17},{19,... | collective-permute-start | bytes 1572872 | tf_op jit(solution)/shard_map/ppermute | solution.py:346
  42.4 19.5 %collective-permute-start.14 = (bf16[512,512]{1,0:T(8,128)(2,1)S(1)}, bf16[512,512]{1,0:T(8,128)(2,1)S(1)}, u32[]{:S(2)}, u32[]{:S(2)}) collective-permute-start(bf16[512,512]{1,0:T(8,128)(2,1)S(1)} %add_convert_fusion.5.rest_0_), channel_id=1, source_target_pairs={{1,2},{2,1},{5,6},{6,5},{9,10},{10,9},{13,14},{14,13},{17,18},{18,... | collective-permute-start | bytes 1572872 | tf_op jit(solution)/shard_map/ppermute | solution.py:346
  56.0 38.4 %collective-permute-start.11 = (bf16[512,512]{1,0:T(8,128)(2,1)}, bf16[512,512]{1,0:T(8,128)(2,1)}, u32[]{:S(2)}, u32[]{:S(2)}) collective-permute-start(bf16[512,512]{1,0:T(8,128)(2,1)} %add_convert_fusion.2), channel_id=1, source_target_pairs={{0,1},{3,2},{2,3},{1,0},{4,5},{7,6},{6,7},{5,4},{8,9},{11,10},{10,... | collective-permute-start | bytes 1572872 | tf_op jit(solution)/shard_map/ppermute | solution.py:346
  59.4 7.8 %collective-permute-start.4 = (bf16[2,6,16,3072]{3,2,1,0:T(8,128)(2,1)S(1)}, bf16[2,6,16,3072]{3,2,1,0:T(8,128)(2,1)S(1)}, u32[]{:S(2)}, u32[]{:S(2)}) collective-permute-start(bf16[2,6,16,3072]{3,2,1,0:T(8,128)(2,1)S(1)} %pad_maximum_fusion), channel_id=1, source_target_pairs={{0,4},{4,0},{8,12},{12,8},{1,5},{5,1},{9,13},{13,9},{2,6},{6,2},{1... | collective-permute-start | bytes 3538952 | tf_op jit(solution)/shard_map/ppermute | solution.py:143
  60.4 33.9 %collective-permute-start.13 = (bf16[512,512]{1,0:T(8,128)(2,1)}, bf16[512,512]{1,0:T(8,128)(2,1)}, u32[]{:S(2)}, u32[]{:S(2)}) collective-permute-start(bf16[512,512]{1,0:T(8,128)(2,1)} %add_convert_fusion.1), channel_id=1, source_target_pairs={{1,2},{2,1},{5,6},{6,5},{9,10},{10,9},{13,14},{14,13},{17,18},{18,... | collective-permute-start | bytes 1572872 | tf_op jit(solution)/shard_map/ppermute | solution.py:346
  62.8 4.3 %copy-start.3 = (bf16[2,6,16,3072]{3,2,1,0:T(8,128)(2,1)S(1)}, bf16[2,6,16,3072]{3,2,1,0:T(8,128)(2,1)}, u32[]{:S(2)}) copy-start(bf16[2,6,16,3072]{3,2,1,0:T(8,128)(2,1)} %copy-done.2) | copy-start | bytes 3538948
  62.8 31.5 %collective-permute-start.15 = (bf16[512,512]{1,0:T(8,128)(2,1)}, bf16[512,512]{1,0:T(8,128)(2,1)}, u32[]{:S(2)}, u32[]{:S(2)}) collective-permute-start(bf16[512,512]{1,0:T(8,128)(2,1)} %add_convert_fusion), channel_id=1, source_target_pairs={{0,1},{3,2},{2,3},{1,0},{4,5},{7,6},{6,7},{5,4},{8,9},{11,10},{10,... | collective-permute-start | bytes 1572872 | tf_op jit(solution)/shard_map/ppermute | solution.py:346
  65.7 28.7 %collective-permute-start.16 = (bf16[512,512]{1,0:T(8,128)(2,1)}, bf16[512,512]{1,0:T(8,128)(2,1)}, u32[]{:S(2)}, u32[]{:S(2)}) collective-permute-start(bf16[512,512]{1,0:T(8,128)(2,1)} %add_convert_fusion.4.rest_0_), channel_id=1, source_target_pairs={{1,2},{2,1},{5,6},{6,5},{9,10},{10,9},{13,14},{14,13},{17,18},{18,... | collective-permute-start | bytes 1572872 | tf_op jit(solution)/shard_map/ppermute | solution.py:346
  70.8 12.6 %collective-permute-start.5 = (f32[16,512]{1,0:T(8,128)S(1)}, f32[16,512]{1,0:T(8,128)S(1)}, u32[]{:S(2)}, u32[]{:S(2)}) collective-permute-start(f32[16,512]{1,0:T(8,128)S(1)} %low_sums.1), channel_id=1, source_target_pairs={{0,1},{1,0},{2,3},{3,2},{4,5},{5,4},{6,7},{7,6},{8,9},{9,8},{10,11... | collective-permute-start | bytes 98312 | tf_op jit(solution)/shard_map/ppermute | solution.py:361
  83.5 8.6 %collective-permute-start.6 = (f32[16,512]{1,0:T(8,128)S(1)}, f32[16,512]{1,0:T(8,128)S(1)}, u32[]{:S(2)}, u32[]{:S(2)}) collective-permute-start(f32[16,512]{1,0:T(8,128)S(1)} %add.46.low_ref), channel_id=1, source_target_pairs={{0,2},{1,3},{2,0},{3,1},{4,6},{5,7},{6,4},{7,5},{8,10},{9,11},{10,... | collective-permute-start | bytes 98312 | tf_op jit(solution)/shard_map/ppermute | solution.py:363
  89.3 2.8 %copy-start.4 = (bf16[2,6,16,3072]{3,2,1,0:T(8,128)(2,1)S(1)}, bf16[2,6,16,3072]{3,2,1,0:T(8,128)(2,1)}, u32[]{:S(2)}) copy-start(bf16[2,6,16,3072]{3,2,1,0:T(8,128)(2,1)} %copy-done.2) | copy-start | bytes 3538948

commit v4 on v2

v4 whole, which is shorter than its diff:
```python
import functools

import jax
import jax.numpy as jnp
from jax import lax
from jax.experimental import pallas as pl
from jax.experimental.pallas import tpu as pltpu
from jax.sharding import PartitionSpec as P

CAP = 6
PIECES = 2
VMEM_LIMIT = 48 * 1024 * 1024
F32 = jnp.float32
BF16 = jnp.bfloat16
SMALL = pl.CostEstimate(flops=1000, bytes_accessed=1000, transcendentals=0)


def product_kernel(tile, addends, afters, first_call, first_ref, rows_ref, weight_ref, *rest):
    addend_refs, rest = rest[:addends], rest[addends + afters :]
    if first_call:
        ids_ref, out_ref, ids_out_ref, tiles_ref, tile_sems, held_ref, held_sem = rest
    else:
        out_ref, tiles_ref, tile_sems = rest
    tiles = out_ref.shape[1] // tile
    first = first_ref[0]

    def weight_copy(j):
        columns = pl.ds(pl.multiple_of(first + j * tile, 128), tile)
        return pltpu.make_async_copy(
            weight_ref.at[:, columns], tiles_ref.at[j], tile_sems.at[j]
        )

    if first_call:
        rows_copy = pltpu.make_async_copy(rows_ref, held_ref, held_sem)
        rows_copy.start()
    for j in range(tiles):
        weight_copy(j).start()
    if first_call:
        for s in range(ids_ref.shape[1]):
            ids_out_ref[0, s] = ids_ref[0, s]
        rows_copy.wait()
        rows_ref = held_ref
    for j in range(tiles):
        weight_copy(j).wait()
        columns = slice(j * tile, (j + 1) * tile)
        total = jnp.dot(rows_ref[...], tiles_ref[j], preferred_element_type=F32)
        for ref in addend_refs:
            total = total + ref[:, columns].astype(F32)
        out_ref[:, columns] = total.astype(out_ref.dtype)


def block_product(rows, weight, first, width, addends=(), after=(), ids=None):
    row_total, depth = rows.shape
    tile = min(256, width)
    first_call = ids is not None
    smem = pl.BlockSpec(memory_space=pltpu.SMEM)
    vmem = pl.BlockSpec(memory_space=pltpu.VMEM)
    hbm = pl.BlockSpec(memory_space=pl.ANY)
    out_specs, out_shape = [vmem], [jax.ShapeDtypeStruct((row_total, width), BF16)]
    scratch = [
        pltpu.VMEM((width // tile, depth, tile), BF16),
        pltpu.SemaphoreType.DMA((width // tile,)),
    ]
    if first_call:
        out_specs.append(smem)
        out_shape.append(jax.ShapeDtypeStruct(ids.shape, ids.dtype))
        scratch += [pltpu.VMEM((row_total, depth), BF16), pltpu.SemaphoreType.DMA]
    out = pl.pallas_call(
        functools.partial(product_kernel, tile, len(addends), len(after), first_call),
        in_specs=[smem, hbm if first_call else vmem, hbm]
        + [vmem] * len(addends)
        + [hbm] * len(after)
        + [smem] * first_call,
        out_specs=out_specs,
        out_shape=out_shape,
        scratch_shapes=scratch,
        compiler_params=pltpu.CompilerParams(vmem_limit_bytes=VMEM_LIMIT),
        cost_estimate=SMALL,
        name="block_product",
    )(first.reshape(1), rows, weight, *addends, *after, *([ids] if first_call else []))
    return out if first_call else out[0]


def pick_kernel(peers, afters, me_ref, table_ref, lens_ref, *rest):
    ids_refs = rest[:peers]
    down_ref, up_ref = rest[peers : peers + 2]
    rest = rest[peers + 2 + afters :]
    packs, (start_ref, end_ref, pick_ref, sem) = rest[:peers], rest[peers:]
    segs = lens_ref.shape[1]
    share, _, depth = down_ref.shape
    cols = up_ref.shape[2]
    me = me_ref[0]

    def clear(q, carry):
        pick_ref[q] = 0
        start_ref[q] = 0
        end_ref[q] = 0
        return carry

    lax.fori_loop(0, peers * CAP, clear, 0)

    def copies(x, c, source):
        pack = packs[x].at[c]
        return (
            pltpu.make_async_copy(down_ref.at[source], pack.at[:, pl.ds(0, depth)], sem),
            pltpu.make_async_copy(up_ref.at[source], pack.at[:, pl.ds(depth, cols)], sem),
        )

    for x in reversed(range(peers)):

        def choose(s, count):
            local = table_ref[ids_refs[x][0, s]] - me * share
            mine = jnp.logical_and(local >= 0, local < share)

            @pl.when(jnp.logical_and(mine, count < CAP))
            def _():
                pick_ref[x * CAP + count] = local

            return count + mine.astype(jnp.int32)

        lax.fori_loop(0, segs, choose, 0)
        for c in range(CAP):
            for copy in copies(x, c, pick_ref[x * CAP + c]):
                copy.start()

    for x in range(peers):
        owner = lax.bitwise_xor(me, jnp.int32(x))

        def place(s, carry):
            count, first = carry
            local = table_ref[ids_refs[0][0, s]] - owner * share
            theirs = jnp.logical_and(local >= 0, local < share)
            last = first + lens_ref[0, s]

            @pl.when(jnp.logical_and(theirs, count < CAP))
            def _():
                start_ref[x * CAP + count] = first
                end_ref[x * CAP + count] = last

            return count + theirs.astype(jnp.int32), last

        lax.fori_loop(0, segs, place, (0, 0))

    for x in range(peers):
        for c in range(CAP):
            for copy in copies(x, c, 0):
                copy.wait()


def pick_adapters(me, table, all_ids, lens, down, up, after):
    peers = len(all_ids)
    _, rank, depth = down.shape
    cols = up.shape[2]
    smem = pl.BlockSpec(memory_space=pltpu.SMEM)
    vmem = pl.BlockSpec(memory_space=pltpu.VMEM)
    hbm = pl.BlockSpec(memory_space=pl.ANY)
    out = pl.pallas_call(
        functools.partial(pick_kernel, peers, len(after)),
        in_specs=[smem] * (3 + peers) + [hbm] * (2 + len(after)),
        out_specs=[vmem] * peers + [smem, smem],
        out_shape=[jax.ShapeDtypeStruct((CAP, rank, depth + cols), BF16)] * peers
        + [jax.ShapeDtypeStruct((peers * CAP,), jnp.int32)] * 2,
        scratch_shapes=[pltpu.SMEM((peers * CAP,), jnp.int32), pltpu.SemaphoreType.DMA],
        compiler_params=pltpu.CompilerParams(vmem_limit_bytes=VMEM_LIMIT),
        cost_estimate=SMALL,
        name="pick_adapters",
    )(me.reshape(1), table, lens, *all_ids, down, up, *after)
    return list(out[:-2]), out[-2], out[-1]


def pack_spec(pack, first, width):
    return pl.BlockSpec(pack.shape[:2] + (width,), lambda i: (0, 0, first // width))


def low_kernel(peers, start_ref, end_ref, rows_ref, *rest):
    down_refs, out_ref = rest[:peers], rest[-1]
    row_total, depth = rows_ref.shape
    rank = out_ref.shape[0]
    place = lax.broadcasted_iota(jnp.int32, (rank, row_total), 1)
    total = jnp.zeros((rank, row_total), F32)
    for x, down_ref in enumerate(down_refs):
        part = lax.dot_general(
            down_ref[...].reshape(CAP * rank, depth),
            rows_ref[...],
            (((1,), (1,)), ((), ())),
            preferred_element_type=F32,
        )
        for c in range(CAP):
            q = x * CAP + c
            member = jnp.logical_and(place >= start_ref[q], place < end_ref[q])
            total = jnp.where(member, part[c * rank : (c + 1) * rank], total)
    out_ref[...] = total


def low_sums(starts, ends, rows, packs, rank, after):
    row_total, depth = rows.shape
    smem = pl.BlockSpec(memory_space=pltpu.SMEM)
    vmem = pl.BlockSpec(memory_space=pltpu.VMEM)
    return pl.pallas_call(
        functools.partial(low_kernel, len(packs)),
        grid=(1,),
        in_specs=[smem, smem, vmem]
        + [pack_spec(p, 0, depth) for p in packs]
        + [pl.BlockSpec(memory_space=pl.ANY)] * len(after),
        out_specs=vmem,
        out_shape=jax.ShapeDtypeStruct((rank, row_total), F32),
        compiler_params=pltpu.CompilerParams(vmem_limit_bytes=VMEM_LIMIT),
        cost_estimate=SMALL,
        name="low_sums",
    )(starts, ends, rows, *packs, *after)


def term_kernel(lows, pieces, peers, start_ref, end_ref, *rest):
    low_refs, rest = rest[:lows], rest[lows:]
    own_refs, rest = rest[:pieces], rest[pieces:]
    up_refs, out_refs = rest[:peers], rest[-pieces:]
    rank, row_total = low_refs[0].shape
    width = out_refs[0].shape[1]
    cols = width * pieces
    low = low_refs[0][...]
    for ref in low_refs[1:]:
        low = low + ref[...]
    low = low.astype(BF16).astype(F32)
    place = lax.broadcasted_iota(jnp.int32, (rank, row_total), 1)
    spread = []
    for q in range(len(up_refs) * CAP):
        member = jnp.logical_and(place >= start_ref[q], place < end_ref[q])
        spread.append(jnp.where(member, low, 0.0))
    spread = jnp.concatenate(spread, axis=0).astype(BF16)
    ups = jnp.concatenate([ref[...].reshape(CAP * rank, cols) for ref in up_refs], axis=0)
    for piece in range(pieces):
        columns = slice(piece * width, (piece + 1) * width)
        term = lax.dot_general(
            spread, ups[:, columns], (((0,), (0,)), ((), ())), preferred_element_type=F32
        )
        out_refs[piece][...] = own_refs[piece][...].astype(F32) + term


def adapter_term(starts, ends, lows, owns, packs, after):
    row_total, width = owns[0].shape
    cols = width * len(owns)
    smem = pl.BlockSpec(memory_space=pltpu.SMEM)
    vmem = pl.BlockSpec(memory_space=pltpu.VMEM)
    depth = packs[0].shape[2] - cols
    return pl.pallas_call(
        functools.partial(term_kernel, len(lows), len(owns), len(packs)),
        grid=(1,),
        in_specs=[smem, smem]
        + [vmem] * (len(lows) + len(owns))
        + [pack_spec(p, depth, cols) for p in packs]
        + [pl.BlockSpec(memory_space=pl.ANY)] * len(after),
        out_specs=[vmem] * len(owns),
        out_shape=[jax.ShapeDtypeStruct((row_total, width), F32)] * len(owns),
        compiler_params=pltpu.CompilerParams(vmem_limit_bytes=VMEM_LIMIT),
        cost_estimate=SMALL,
        name="adapter_term",
    )(starts, ends, *lows, *owns, *packs, *after)


def finish_kernel(addends, term_ref, *rest):
    total = term_ref[...]
    for ref in rest[:addends]:
        total = total + ref[...].astype(F32)
    rest[-1][...] = total.astype(rest[-1].dtype)


def finish(term, arrivals, piece, pieces, result):
    row_total, width = term.shape
    height = min(row_total, 128)
    block = pl.BlockSpec((height, width), lambda i: (i, 0))
    held = [] if result is None else [result]
    return pl.pallas_call(
        functools.partial(finish_kernel, len(arrivals)),
        grid=(row_total // height,),
        in_specs=[block] * (1 + len(arrivals)) + [pl.BlockSpec(memory_space=pl.ANY)] * len(held),
        out_specs=pl.BlockSpec((height, width), lambda i: (i, piece)),
        out_shape=jax.ShapeDtypeStruct((row_total, width * pieces), BF16),
        input_output_aliases={1 + len(arrivals): 0} if held else {},
        compiler_params=pltpu.CompilerParams(vmem_limit_bytes=VMEM_LIMIT),
        cost_estimate=SMALL,
        name="finish",
    )(term, *arrivals, *held)


def local(req_total, tp_total, rows, weight, down, up, table, ids, lens):
    rank = down.shape[1]
    cols = up.shape[2]
    width = cols // PIECES
    me_req = lax.axis_index("req").astype(jnp.int32)
    me = lax.axis_index("tp").astype(jnp.int32)
    right = [(i, (i + 1) % tp_total) for i in range(tp_total)]
    steps = tp_total - 1

    def partial(back, piece, **options):
        block = lax.rem(me + (tp_total - back), tp_total)
        return block_product(rows, weight, block * cols + piece * width, width, **options)

    moving, owns = [None] * PIECES, [None] * PIECES
    last, ids = partial(1, 0, ids=ids)
    moving[0] = lax.ppermute(last, "tp", right)

    all_ids = [ids]
    for x in range(1, req_total):
        all_ids.append(lax.ppermute(ids, "req", [(i, i ^ x) for i in range(req_total)]))
    for piece in range(1, PIECES):
        last = partial(1, piece, after=[last])
        moving[piece] = lax.ppermute(last, "tp", right)
    packs, starts, ends = pick_adapters(me_req, table, all_ids, lens, down, up, [last])
    for x in range(1, req_total):
        packs[x] = lax.ppermute(packs[x], "req", [(i, i ^ x) for i in range(req_total)])

    last = starts
    for step in range(1, steps):
        for piece in range(PIECES):
            if step == steps - 1 and piece == PIECES - 1:
                low = low_sums(starts, ends, rows, packs, rank, [last])
                lows = [low]
                for x in range(1, tp_total):
                    pairs = [(i, i ^ x) for i in range(tp_total)]
                    lows.append(lax.ppermute(low, "tp", pairs))
                last = low
            last = partial(1 + step, piece, addends=[moving[piece]], after=[last])
            moving[piece] = lax.ppermute(last, "tp", right)
            if step == 1:
                last = owns[piece] = partial(0, piece, after=[last])

    terms = adapter_term(starts, ends, lows, owns, packs, [last])
    result = None
    for piece in range(PIECES):
        result = finish(terms[piece], [moving[piece]], piece, PIECES, result)
    return result


def solution(mesh):
    return jax.shard_map(
        functools.partial(local, mesh.shape["req"], mesh.shape["tp"]),
        mesh=mesh,
        in_specs=(
            P(("groups", "req"), "tp"),
            P("tp", None),
            P(("groups", "req"), None, "tp"),
            P(("groups", "req"), None, "tp"),
            P("groups"),
            P(("groups", "req"), None),
            P(("groups", "req"), None),
        ),
        out_specs=P(("groups", "req"), "tp"),
        check_vma=False,
    )
```

time: 124 us -> 90 us (0.73)
  waiting for transfers between devices: 59.8 us -> 22.1 us
  Pallas kernels: 29.3 us -> 49.2 us
  between operations: 13.5 us -> 0.16 us
  local copies, waits for them, and re-layouts: 8.48 us -> 2.26 us
  starting transfers between devices: 12.1 us -> 16 us
    reduce_scatter x2 -> x0, waiting for transfers between devices: 29.1 us -> none  [local(): lax.psum_scatter(product, 'tp', scatter_dimension=0, tiled=False)]
    pallas_call x6 -> x13, Pallas kernels: 29.3 us -> 49.2 us  [the longest x8 36.6 us: block_product(): pl.pallas_call(functools.partial(product_kernel, tile, len(addends), len(...]
    ppermute x9 -> x15, waiting for transfers between devices: 30.7 us -> 22.1 us  [the longest x3 15.6 us: local(): lows.append(lax.ppermute(low, 'tp', pairs))]
    unnamed x18 -> x10, local copies, waits for them, and re-layouts: 8.48 us -> 2.26 us
    ppermute x9 -> x15, starting transfers between devices: 12.1 us -> 16 us  [the longest x3 4.45 us: local(): lows.append(lax.ppermute(low, 'tp', pairs))]
  transfers between devices with their start and end apart: 11 -> 15, of which waited for: 9 -> 6; matrix products, arithmetic and copies ran while one was open for 0% -> 0% of each run, Pallas kernels for 15% -> 47%
where the time goes in v4:
time: 90 us; the launch traced here: 89.7 us
  Pallas kernels  49.2 us (55%)
  waiting for transfers between devices  22.1 us (25%)
  starting transfers between devices  16 us (18%)
  local copies, waits for them, and re-layouts  2.26 us (3%)
    pallas_call x8, Pallas kernels, block_product(): pl.pallas_call(functools.partial(product_kernel, tile, len(addends), len(...  36.6 us
    ppermute x3, waiting for transfers between devices, local(): lows.append(lax.ppermute(low, 'tp', pairs))  15.6 us
    ppermute x3, starting transfers between devices, local(): lows.append(lax.ppermute(low, 'tp', pairs))  4.45 us
    ppermute x5, waiting for transfers between devices, local(): moving[piece] = lax.ppermute(last, 'tp', right)  4.4 us
    pallas_call x1, Pallas kernels, low_sums(): pl.pallas_call(functools.partial(low_kernel, len(packs)), grid=(1,), in_s...  3.9 us
    pallas_call x1, Pallas kernels, pick_adapters(): pl.pallas_call(functools.partial(pick_kernel, peers, len(after)), in_spec...  3.88 us
    ppermute x5, starting transfers between devices, local(): moving[piece] = lax.ppermute(last, 'tp', right)  3.83 us
    ppermute x1, starting transfers between devices, local(): moving[0] = lax.ppermute(last, 'tp', right)  3.08 us
  transfers between devices with their start and end apart: 15, of which 6 were waited for; matrix products, arithmetic and copies ran while one was open for 0% of the time, Pallas kernels for 47%

profile of v4, /device:TPU:0, one launch (start us, length us, event | category | flops | bytes accessed | tf_op | source)
XLA Modules:
  0.0 89.7 jit_solution(3183993917500682708)
XLA Ops:
  0.0 0.0 copy-start
  0.0 1.6 %copy-done = bf16[512,2048]{1,0:T(8,128)(2,1)S(1)} copy-done((bf16[512,2048]{1,0:T(8,128)(2,1)S(1)}, bf16[512,2048]{1,0:T(8,128)(2,1)}, u32[]{:S(2)}) %copy-start) | copy-done | bytes 2097176
  1.6 0.0 copy-start.3
  1.6 0.7 copy-done.3
  2.2 0.0 copy-start.1
  2.2 5.2 %block_product.8 = (bf16[512,512]{1,0:T(8,128)(2,1)}, s32[1,12]{1,0:T(1,128)S(1)}) custom-call(s32[1]{0:T(128)} %bitcast.1.first_ref, bf16[512,2048]{1,0:T(8,128)(2,1)S(1)} %copy-done, bf16[2048,4096]{1,0:T(8,128)(2,1)} %weight_ref.15, s32[1,12]{1,0:T(1,128)S(1)} %copy-done.3), custom_call_target="tpu_custom_call" | custom-call | flops 1000 | bytes 1000 | tf_op jit(solution)/shard_map/block_product/pallas_call | solution.py:68
  7.5 3.1 %collective-permute-start.6 = (bf16[512,512]{1,0:T(8,128)(2,1)}, bf16[512,512]{1,0:T(8,128)(2,1)S(1)}, u32[]{:S(2)}, u32[]{:S(2)}) collective-permute-start(bf16[512,512]{1,0:T(8,128)(2,1)} %get-tuple-element.16.rest_0_), channel_id=1, source_target_pairs={{0,1},{1,2},{2,3},{3,0},{4,5},{5,6},{6,7},{7,4},{8,9},{9,10},{10,1... | collective-permute-start | bytes 1572872 | tf_op jit(solution)/shard_map/ppermute | solution.py:300
  10.5 0.0 copy-done.1
  10.5 0.0 copy-start.2
  10.5 0.0 copy-start.4
  10.5 4.5 %block_product.9.rest_6_ = bf16[512,512]{1,0:T(8,128)(2,1)} custom-call(s32[1]{0:T(128)} %bitcast.2.first_ref, bf16[512,2048]{1,0:T(8,128)(2,1)S(1)} %copy-done.1, bf16[2048,4096]{1,0:T(8,128)(2,1)} %weight_ref.15, bf16[512,512]{1,0:T(8,128)(2,1)} %get-tuple-element.16.rest_0_), custom_call_target="tpu_custom_call" | custom-call | flops 1000 | bytes 1000 | tf_op jit(solution)/shard_map/block_product/pallas_call | solution.py:68
  15.1 1.6 %collective-permute-start.8 = (bf16[512,512]{1,0:T(8,128)(2,1)}, bf16[512,512]{1,0:T(8,128)(2,1)}, u32[]{:S(2)}, u32[]{:S(2)}) collective-permute-start(bf16[512,512]{1,0:T(8,128)(2,1)} %block_product.9.rest_6_), channel_id=1, source_target_pairs={{0,1},{1,2},{2,3},{3,0},{4,5},{5,6},{6,7},{7,4},{8,9},{9,10},{10,1... | collective-permute-start | bytes 1572872 | tf_op jit(solution)/shard_map/ppermute | solution.py:307
  16.7 0.4 collective-permute-start.2
  17.1 1.2 %collective-permute-start.1 = (s32[1,12]{1,0:T(1,128)S(1)}, s32[1,12]{1,0:T(1,128)S(1)}, u32[]{:S(2)}, u32[]{:S(2)}) collective-permute-start(s32[1,12]{1,0:T(1,128)S(1)} %get-tuple-element.15.rest_0_), channel_id=1, source_target_pairs={{0,8},{4,12},{8,0},{12,4},{1,9},{5,13},{9,1},{13,5},{2,10},{6,14},... | collective-permute-start | bytes 152 | tf_op jit(solution)/shard_map/ppermute | solution.py:304
  18.3 0.3 collective-permute-start
  18.6 1.1 %collective-permute-done.2.rest_3_ = s32[1,12]{1,0:T(1,128)S(1)} collective-permute-done((s32[1,12]{1,0:T(1,128)S(1)}, s32[1,12]{1,0:T(1,128)S(1)}, u32[]{:S(2)}, u32[]{:S(2)}) %collective-permute-start.2) | collective-permute-done | bytes 80 | tf_op jit(solution)/shard_map/ppermute | solution.py:304
  19.7 1.0 %collective-permute-done.1.rest_2_ = s32[1,12]{1,0:T(1,128)S(1)} collective-permute-done((s32[1,12]{1,0:T(1,128)S(1)}, s32[1,12]{1,0:T(1,128)S(1)}, u32[]{:S(2)}, u32[]{:S(2)}) %collective-permute-start.1) | collective-permute-done | bytes 80 | tf_op jit(solution)/shard_map/ppermute | solution.py:304
  20.6 0.0 collective-permute-done.rest_1_
  20.6 0.0 copy-done.2
  20.6 0.0 copy-done.4
  20.6 3.9 %pick_adapters.1 = (bf16[6,16,3072]{2,1,0:T(8,128)(2,1)S(1)}, bf16[6,16,3072]{2,1,0:T(8,128)(2,1)}, bf16[6,16,3072]{2,1,0:T(8,128)(2,1)}, bf16[6,16,3072]{2,1,0:...) custom-call(s32[1]{0:T(128)} %bitcast.me_ref, s32[512]{0:T(512)S(1)} %copy-done.2, s32[1,12]{1,0:T(1,128)S(1)} %copy-done.4, ...), custom_call_target="tpu_custom_call" | custom-call | flops 1000 | bytes 1000 | tf_op jit(solution)/shard_map/pick_adapters/pallas_call | solution.py:157
  24.5 1.4 %collective-permute-start.3 = (bf16[6,16,3072]{2,1,0:T(8,128)(2,1)}, bf16[6,16,3072]{2,1,0:T(8,128)(2,1)}, u32[]{:S(2)}, u32[]{:S(2)}) collective-permute-start(bf16[6,16,3072]{2,1,0:T(8,128)(2,1)} %get-tuple-element.20), channel_id=1, source_target_pairs={{0,4},{4,0},{8,12},{12,8},{1,5},{5,1},{9,13},{13,9},{2,6},{6,2},{1... | collective-permute-start | bytes 1769480 | tf_op jit(solution)/shard_map/ppermute | solution.py:310
  25.9 0.5 collective-permute-start.4
  26.4 0.9 %collective-permute-start.5 = (bf16[6,16,3072]{2,1,0:T(8,128)(2,1)}, bf16[6,16,3072]{2,1,0:T(8,128)(2,1)}, u32[]{:S(2)}, u32[]{:S(2)}) collective-permute-start(bf16[6,16,3072]{2,1,0:T(8,128)(2,1)} %get-tuple-element.22), channel_id=1, source_target_pairs={{0,12},{4,8},{8,4},{12,0},{1,13},{5,9},{9,5},{13,1},{2,14},{6,10},... | collective-permute-start | bytes 1769480 | tf_op jit(solution)/shard_map/ppermute | solution.py:310
  27.3 0.0 collective-permute-done.6.rest_0_
  27.3 4.5 %block_product.10.rest_0_ = bf16[512,512]{1,0:T(8,128)(2,1)} custom-call(s32[1]{0:T(128)} %bitcast.4.first_ref, bf16[512,2048]{1,0:T(8,128)(2,1)S(1)} %copy-done.1, bf16[2048,4096]{1,0:T(8,128)(2,1)} %weight_ref.15, bf16[512,512]{1,0:T(8,128)(2,1)S(1)} %collective-permute-done.6.rest_0_, s32[24]{0:T(128)S(1)} %get-tuple-element.17.rest_1_.start_ref), custom_call_target="tpu_custom_call" | custom-call | flops 1000 | bytes 1000 | tf_op jit(solution)/shard_map/block_product/pallas_call | solution.py:68
  31.9 1.6 %collective-permute-start.7 = (bf16[512,512]{1,0:T(8,128)(2,1)}, bf16[512,512]{1,0:T(8,128)(2,1)}, u32[]{:S(2)}, u32[]{:S(2)}) collective-permute-start(bf16[512,512]{1,0:T(8,128)(2,1)} %block_product.10.rest_0_), channel_id=1, source_target_pairs={{0,1},{1,2},{2,3},{3,0},{4,5},{5,6},{6,7},{7,4},{8,9},{9,10},{10,1... | collective-permute-start | bytes 1572872 | tf_op jit(solution)/shard_map/ppermute | solution.py:323
  33.5 3.7 %block_product.11.rest_1_.rest_4_ = bf16[512,512]{1,0:T(8,128)(2,1)S(1)} custom-call(s32[1]{0:T(128)} %bitcast.7.first_ref, bf16[512,2048]{1,0:T(8,128)(2,1)S(1)} %copy-done.1, bf16[2048,4096]{1,0:T(8,128)(2,1)} %weight_ref.15, bf16[512,512]{1,0:T(8,128)(2,1)} %block_product.10.rest_0_), custom_call_target="tpu_custom_call" | custom-call | flops 1000 | bytes 1000 | tf_op jit(solution)/shard_map/block_product/pallas_call | solution.py:68
  37.2 0.0 collective-permute-done.8.rest_0_
  37.2 5.5 %block_product.12.rest_0_ = bf16[512,512]{1,0:T(8,128)(2,1)} custom-call(s32[1]{0:T(128)} %bitcast.6.first_ref, bf16[512,2048]{1,0:T(8,128)(2,1)S(1)} %copy-done.1, bf16[2048,4096]{1,0:T(8,128)(2,1)} %weight_ref.15, bf16[512,512]{1,0:T(8,128)(2,1)} %collective-permute-done.8.rest_0_, bf16[512,512]{1,0:T(8,128)(2,1)S(1)} %block_product.11.rest_1_.rest_4_), custom_call_target="tpu_custom_call" | custom-call | flops 1000 | bytes 1000 | tf_op jit(solution)/shard_map/block_product/pallas_call | solution.py:68
  42.8 0.3 collective-permute-start.12
  43.0 3.7 %block_product.13.rest_1_.rest_5_ = bf16[512,512]{1,0:T(8,128)(2,1)S(1)} custom-call(s32[1]{0:T(128)} %bitcast.5.first_ref, bf16[512,2048]{1,0:T(8,128)(2,1)S(1)} %copy-done.1, bf16[2048,4096]{1,0:T(8,128)(2,1)} %weight_ref.15, bf16[512,512]{1,0:T(8,128)(2,1)} %block_product.12.rest_0_), custom_call_target="tpu_custom_call" | custom-call | flops 1000 | bytes 1000 | tf_op jit(solution)/shard_map/block_product/pallas_call | solution.py:68
  46.7 2.1 %collective-permute-done.7.rest_0_ = bf16[512,512]{1,0:T(8,128)(2,1)} collective-permute-done((bf16[512,512]{1,0:T(8,128)(2,1)}, bf16[512,512]{1,0:T(8,128)(2,1)}, u32[]{:S(2)}, u32[]{:S(2)}) %collective-permute-start.7) | collective-permute-done | bytes 524320 | tf_op jit(solution)/shard_map/ppermute | solution.py:323
  48.8 4.7 %block_product.14.rest_4_ = bf16[512,512]{1,0:T(8,128)(2,1)S(1)} custom-call(s32[1]{0:T(128)} %bitcast.3.first_ref, bf16[512,2048]{1,0:T(8,128)(2,1)S(1)} %copy-done.1, bf16[2048,4096]{1,0:T(8,128)(2,1)} %weight_ref.15, bf16[512,512]{1,0:T(8,128)(2,1)} %collective-permute-done.7.rest_0_, bf16[512,512]{1,0:T(8,128)(2,1)S(1)} %block_product.13.rest_1_.rest_5_), custom_call_target="tpu_custom_call" | custom-call | flops 1000 | bytes 1000 | tf_op jit(solution)/shard_map/block_product/pallas_call | solution.py:68
  53.6 0.2 collective-permute-start.14
  53.8 0.0 collective-permute-done.3.rest_1_.rest_7_
  53.8 0.0 collective-permute-done.4.rest_2_.rest_8_
  53.8 0.0 collective-permute-done.5.rest_3_.rest_9_
  53.9 3.9 %low_sums.1.rest_1_.rest_0_ = f32[16,512]{1,0:T(8,128)S(1)} custom-call(s32[24]{0:T(128)S(1)} %get-tuple-element.17.rest_1_.start_ref, s32[24]{0:T(128)S(1)} %get-tuple-element.18.end_ref, bf16[512,2048]{1,0:T(8,128)(2,1)S(1)} %copy-done.1, bf16[6,16,3072]{2,1,0:T(8,128)(2,1)S(1)} %get-tuple-element.19.rest_0_.rest_6_, ...), custom_call_target="tpu_custom_call" | custom-call | flops 1000 | bytes 1000 | tf_op jit(solution)/shard_map/low_sums/pallas_call | solution.py:199
  57.8 2.3 %collective-permute-done.12.rest_0_ = bf16[512,512]{1,0:T(8,128)(2,1)} collective-permute-done((bf16[512,512]{1,0:T(8,128)(2,1)}, bf16[512,512]{1,0:T(8,128)(2,1)}, u32[]{:S(2)}, u32[]{:S(2)}) %collective-permute-start.12) | collective-permute-done | bytes 524320 | tf_op jit(solution)/shard_map/ppermute | solution.py:323
  60.1 4.7 %block_product.15.rest_10_ = bf16[512,512]{1,0:T(8,128)(2,1)S(1)} custom-call(s32[1]{0:T(128)} %bitcast.8.first_ref, bf16[512,2048]{1,0:T(8,128)(2,1)S(1)} %copy-done.1, bf16[2048,4096]{1,0:T(8,128)(2,1)} %weight_ref.15, bf16[512,512]{1,0:T(8,128)(2,1)} %collective-permute-done.12.rest_0_, f32[16,512]{1,0:T(8,128)S(1)} %low_sums.1.rest_1_.rest_0_), custom_call_target="tpu_custom_call" | custom-call | flops 1000 | bytes 1000 | tf_op jit(solution)/shard_map/block_product/pallas_call | solution.py:68
  64.8 0.1 collective-permute-start.13
  64.9 3.8 %collective-permute-start.11 = (f32[16,512]{1,0:T(8,128)S(1)}, f32[16,512]{1,0:T(8,128)S(1)}, u32[]{:S(2)}, u32[]{:S(2)}) collective-permute-start(f32[16,512]{1,0:T(8,128)S(1)} %low_sums.1.rest_1_.rest_0_), channel_id=1, source_target_pairs={{0,3},{1,2},{2,1},{3,0},{4,7},{5,6},{6,5},{7,4},{8,11},{9,10},{10,... | collective-permute-start | bytes 98312 | tf_op jit(solution)/shard_map/ppermute | solution.py:320
  68.7 0.0 collective-permute-start.10
  68.7 0.6 collective-permute-start.9
  69.3 13.9 %collective-permute-done.11.rest_3_ = f32[16,512]{1,0:T(8,128)S(1)} collective-permute-done((f32[16,512]{1,0:T(8,128)S(1)}, f32[16,512]{1,0:T(8,128)S(1)}, u32[]{:S(2)}, u32[]{:S(2)}) %collective-permute-start.11) | collective-permute-done | bytes 32800 | tf_op jit(solution)/shard_map/ppermute | solution.py:320
  83.3 1.7 %collective-permute-done.10.rest_2_ = f32[16,512]{1,0:T(8,128)S(1)} collective-permute-done((f32[16,512]{1,0:T(8,128)S(1)}, f32[16,512]{1,0:T(8,128)S(1)}, u32[]{:S(2)}, u32[]{:S(2)}) %collective-permute-start.10) | collective-permute-done | bytes 32800 | tf_op jit(solution)/shard_map/ppermute | solution.py:320
  85.0 0.0 collective-permute-done.9.rest_1_
  85.0 1.9 %adapter_term.1 = (f32[512,512]{1,0:T(8,128)S(1)}, f32[512,512]{1,0:T(8,128)S(1)}) custom-call(s32[24]{0:T(128)S(1)} %get-tuple-element.17.rest_1_.start_ref, s32[24]{0:T(128)S(1)} %get-tuple-element.18.end_ref, f32[16,512]{1,0:T(8,128)S(1)} %low_sums.1.rest_1_.rest_0_, f32[16,512]{1,0:T(8,128)S(1)} %collective-permute-done.9.rest_1_, ...), custom_call_target="tpu_custom_call" | custom-call | flops 1000 | bytes 1000 | tf_op jit(solution)/shard_map/adapter_term/pallas_call | solution.py:245
  86.9 0.0 collective-permute-done.14.rest_0_
  86.9 1.5 %finish.2.rest_1_ = bf16[512,1024]{1,0:T(8,128)(2,1)} custom-call(f32[512,512]{1,0:T(8,128)S(1)} %get-tuple-element.24.term_ref, bf16[512,512]{1,0:T(8,128)(2,1)S(1)} %collective-permute-done.14.rest_0_), custom_call_target="tpu_custom_call" | custom-call | flops 1000 | bytes 1000 | tf_op jit(solution)/shard_map/finish/pallas_call | solution.py:272
  88.3 0.0 collective-permute-done.13.rest_0_
  88.3 1.4 %finish.3 = bf16[512,1024]{1,0:T(8,128)(2,1)} custom-call(f32[512,512]{1,0:T(8,128)S(1)} %get-tuple-element.23.term_ref, bf16[512,512]{1,0:T(8,128)(2,1)S(1)} %collective-permute-done.13.rest_0_, bf16[512,1024]{1,0:T(8,128)(2,1)} %finish.2.rest_1_), custom_call_target="tpu_custom_call", output_to_operand_aliasing={{}: (2, {})} | custom-call | flops 1000 | bytes 1000 | tf_op jit(solution)/shard_map/finish/pallas_call | solution.py:272
Async XLA Ops:
  0.0 1.6 %copy-start = (bf16[512,2048]{1,0:T(8,128)(2,1)S(1)}, bf16[512,2048]{1,0:T(8,128)(2,1)}, u32[]{:S(2)}) copy-start(bf16[512,2048]{1,0:T(8,128)(2,1)} %rows_ref.17) | copy-start | bytes 6291460
  1.6 0.7 copy-start.3
  2.2 8.3 %copy-start.1 = (bf16[512,2048]{1,0:T(8,128)(2,1)S(1)}, bf16[512,2048]{1,0:T(8,128)(2,1)}, u32[]{:S(2)}) copy-start(bf16[512,2048]{1,0:T(8,128)(2,1)} %rows_ref.17) | copy-start | bytes 6291460
  7.5 19.9 %collective-permute-start.6 = (bf16[512,512]{1,0:T(8,128)(2,1)}, bf16[512,512]{1,0:T(8,128)(2,1)S(1)}, u32[]{:S(2)}, u32[]{:S(2)}) collective-permute-start(bf16[512,512]{1,0:T(8,128)(2,1)} %get-tuple-element.16.rest_0_), channel_id=1, source_target_pairs={{0,1},{1,2},{2,3},{3,0},{4,5},{5,6},{6,7},{7,4},{8,9},{9,10},{10,1... | collective-permute-start | bytes 1572872 | tf_op jit(solution)/shard_map/ppermute | solution.py:300
  10.5 10.1 %copy-start.2 = (s32[512]{0:T(512)S(1)}, s32[512]{0:T(512)}, u32[]{:S(2)}) copy-start(s32[512]{0:T(512)} %table_ref.1) | copy-start | bytes 6148
  10.5 10.1 %copy-start.4 = (s32[1,12]{1,0:T(1,128)S(1)}, s32[1,12]{1,0:T(1,128)}, u32[]{:S(2)}) copy-start(s32[1,12]{1,0:T(1,128)} %lens_ref.1) | copy-start | bytes 148
  15.1 22.1 %collective-permute-start.8 = (bf16[512,512]{1,0:T(8,128)(2,1)}, bf16[512,512]{1,0:T(8,128)(2,1)}, u32[]{:S(2)}, u32[]{:S(2)}) collective-permute-start(bf16[512,512]{1,0:T(8,128)(2,1)} %block_product.9.rest_6_), channel_id=1, source_target_pairs={{0,1},{1,2},{2,3},{3,0},{4,5},{5,6},{6,7},{7,4},{8,9},{9,10},{10,1... | collective-permute-start | bytes 1572872 | tf_op jit(solution)/shard_map/ppermute | solution.py:307
  16.7 3.0 %collective-permute-start.2 = (s32[1,12]{1,0:T(1,128)S(1)}, s32[1,12]{1,0:T(1,128)S(1)}, u32[]{:S(2)}, u32[]{:S(2)}) collective-permute-start(s32[1,12]{1,0:T(1,128)S(1)} %get-tuple-element.15.rest_0_), channel_id=1, source_target_pairs={{0,12},{4,8},{8,4},{12,0},{1,13},{5,9},{9,5},{13,1},{2,14},{6,10},... | collective-permute-start | bytes 152 | tf_op jit(solution)/shard_map/ppermute | solution.py:304
  17.1 3.5 %collective-permute-start.1 = (s32[1,12]{1,0:T(1,128)S(1)}, s32[1,12]{1,0:T(1,128)S(1)}, u32[]{:S(2)}, u32[]{:S(2)}) collective-permute-start(s32[1,12]{1,0:T(1,128)S(1)} %get-tuple-element.15.rest_0_), channel_id=1, source_target_pairs={{0,8},{4,12},{8,0},{12,4},{1,9},{5,13},{9,1},{13,5},{2,10},{6,14},... | collective-permute-start | bytes 152 | tf_op jit(solution)/shard_map/ppermute | solution.py:304
  18.3 2.4 %collective-permute-start = (s32[1,12]{1,0:T(1,128)S(1)}, s32[1,12]{1,0:T(1,128)S(1)}, u32[]{:S(2)}, u32[]{:S(2)}) collective-permute-start(s32[1,12]{1,0:T(1,128)S(1)} %get-tuple-element.15.rest_0_), channel_id=1, source_target_pairs={{0,4},{4,0},{8,12},{12,8},{1,5},{5,1},{9,13},{13,9},{2,6},{6,2},{1... | collective-permute-start | bytes 152 | tf_op jit(solution)/shard_map/ppermute | solution.py:304
  24.5 29.3 %collective-permute-start.3 = (bf16[6,16,3072]{2,1,0:T(8,128)(2,1)}, bf16[6,16,3072]{2,1,0:T(8,128)(2,1)}, u32[]{:S(2)}, u32[]{:S(2)}) collective-permute-start(bf16[6,16,3072]{2,1,0:T(8,128)(2,1)} %get-tuple-element.20), channel_id=1, source_target_pairs={{0,4},{4,0},{8,12},{12,8},{1,5},{5,1},{9,13},{13,9},{2,6},{6,2},{1... | collective-permute-start | bytes 1769480 | tf_op jit(solution)/shard_map/ppermute | solution.py:310
  25.9 27.9 %collective-permute-start.4 = (bf16[6,16,3072]{2,1,0:T(8,128)(2,1)}, bf16[6,16,3072]{2,1,0:T(8,128)(2,1)}, u32[]{:S(2)}, u32[]{:S(2)}) collective-permute-start(bf16[6,16,3072]{2,1,0:T(8,128)(2,1)} %get-tuple-element.21), channel_id=1, source_target_pairs={{0,8},{4,12},{8,0},{12,4},{1,9},{5,13},{9,1},{13,5},{2,10},{6,14},... | collective-permute-start | bytes 1769480 | tf_op jit(solution)/shard_map/ppermute | solution.py:310
  26.4 27.5 %collective-permute-start.5 = (bf16[6,16,3072]{2,1,0:T(8,128)(2,1)}, bf16[6,16,3072]{2,1,0:T(8,128)(2,1)}, u32[]{:S(2)}, u32[]{:S(2)}) collective-permute-start(bf16[6,16,3072]{2,1,0:T(8,128)(2,1)} %get-tuple-element.22), channel_id=1, source_target_pairs={{0,12},{4,8},{8,4},{12,0},{1,13},{5,9},{9,5},{13,1},{2,14},{6,10},... | collective-permute-start | bytes 1769480 | tf_op jit(solution)/shard_map/ppermute | solution.py:310
  31.9 17.0 %collective-permute-start.7 = (bf16[512,512]{1,0:T(8,128)(2,1)}, bf16[512,512]{1,0:T(8,128)(2,1)}, u32[]{:S(2)}, u32[]{:S(2)}) collective-permute-start(bf16[512,512]{1,0:T(8,128)(2,1)} %block_product.10.rest_0_), channel_id=1, source_target_pairs={{0,1},{1,2},{2,3},{3,0},{4,5},{5,6},{6,7},{7,4},{8,9},{9,10},{10,1... | collective-permute-start | bytes 1572872 | tf_op jit(solution)/shard_map/ppermute | solution.py:323
  42.8 17.3 %collective-permute-start.12 = (bf16[512,512]{1,0:T(8,128)(2,1)}, bf16[512,512]{1,0:T(8,128)(2,1)}, u32[]{:S(2)}, u32[]{:S(2)}) collective-permute-start(bf16[512,512]{1,0:T(8,128)(2,1)} %block_product.12.rest_0_), channel_id=1, source_target_pairs={{0,1},{1,2},{2,3},{3,0},{4,5},{5,6},{6,7},{7,4},{8,9},{9,10},{10,1... | collective-permute-start | bytes 1572872 | tf_op jit(solution)/shard_map/ppermute | solution.py:323
  53.6 33.3 %collective-permute-start.14 = (bf16[512,512]{1,0:T(8,128)(2,1)S(1)}, bf16[512,512]{1,0:T(8,128)(2,1)S(1)}, u32[]{:S(2)}, u32[]{:S(2)}) collective-permute-start(bf16[512,512]{1,0:T(8,128)(2,1)S(1)} %block_product.14.rest_4_), channel_id=1, source_target_pairs={{0,1},{1,2},{2,3},{3,0},{4,5},{5,6},{6,7},{7,4},{8,9},{9,10},{10,1... | collective-permute-start | bytes 1572872 | tf_op jit(solution)/shard_map/ppermute | solution.py:323
  64.8 23.5 %collective-permute-start.13 = (bf16[512,512]{1,0:T(8,128)(2,1)S(1)}, bf16[512,512]{1,0:T(8,128)(2,1)S(1)}, u32[]{:S(2)}, u32[]{:S(2)}) collective-permute-start(bf16[512,512]{1,0:T(8,128)(2,1)S(1)} %block_product.15.rest_10_), channel_id=1, source_target_pairs={{0,1},{1,2},{2,3},{3,0},{4,5},{5,6},{6,7},{7,4},{8,9},{9,10},{10,1... | collective-permute-start | bytes 1572872 | tf_op jit(solution)/shard_map/ppermute | solution.py:323
  64.9 18.4 %collective-permute-start.11 = (f32[16,512]{1,0:T(8,128)S(1)}, f32[16,512]{1,0:T(8,128)S(1)}, u32[]{:S(2)}, u32[]{:S(2)}) collective-permute-start(f32[16,512]{1,0:T(8,128)S(1)} %low_sums.1.rest_1_.rest_0_), channel_id=1, source_target_pairs={{0,3},{1,2},{2,1},{3,0},{4,7},{5,6},{6,5},{7,4},{8,11},{9,10},{10,... | collective-permute-start | bytes 98312 | tf_op jit(solution)/shard_map/ppermute | solution.py:320
  68.7 16.3 %collective-permute-start.10 = (f32[16,512]{1,0:T(8,128)S(1)}, f32[16,512]{1,0:T(8,128)S(1)}, u32[]{:S(2)}, u32[]{:S(2)}) collective-permute-start(f32[16,512]{1,0:T(8,128)S(1)} %low_sums.1.rest_1_.rest_0_), channel_id=1, source_target_pairs={{0,2},{1,3},{2,0},{3,1},{4,6},{5,7},{6,4},{7,5},{8,10},{9,11},{10,... | collective-permute-start | bytes 98312 | tf_op jit(solution)/shard_map/ppermute | solution.py:320
  68.7 16.3 %collective-permute-start.9 = (f32[16,512]{1,0:T(8,128)S(1)}, f32[16,512]{1,0:T(8,128)S(1)}, u32[]{:S(2)}, u32[]{:S(2)}) collective-permute-start(f32[16,512]{1,0:T(8,128)S(1)} %low_sums.1.rest_1_.rest_0_), channel_id=1, source_target_pairs={{0,1},{1,0},{2,3},{3,2},{4,5},{5,4},{6,7},{7,6},{8,9},{9,8},{10,11... | collective-permute-start | bytes 98312 | tf_op jit(solution)/shard_map/ppermute | solution.py:320

commit v5 on v4

v5 whole, which is shorter than its diff:
```python
import functools

import jax
import jax.numpy as jnp
from jax import lax
from jax.experimental import pallas as pl
from jax.experimental.pallas import tpu as pltpu
from jax.sharding import PartitionSpec as P

CAP = 6
PIECES = 2
VMEM_LIMIT = 48 * 1024 * 1024
F32 = jnp.float32
BF16 = jnp.bfloat16
SMALL = pl.CostEstimate(flops=1000, bytes_accessed=1000, transcendentals=0)


def product_kernel(addends, with_ids, first_ref, rows_ref, weight_ref, *rest):
    out_ref = rest[-1 - with_ids]
    total = jnp.dot(rows_ref[...], weight_ref[...], preferred_element_type=F32)
    for ref in rest[:addends]:
        total = total + ref[...].astype(F32)
    out_ref[...] = total.astype(out_ref.dtype)
    if with_ids:
        ids_ref, ids_out_ref = rest[addends], rest[-1]
        for s in range(ids_ref.shape[1]):
            ids_out_ref[0, s] = ids_ref[0, s]


def block_product(rows, weight, first, width, addends=(), after=(), ids=None):
    row_total, depth = rows.shape
    tile = min(256, width)
    with_ids = ids is not None
    smem = pl.BlockSpec(memory_space=pltpu.SMEM)
    hbm = pl.BlockSpec(memory_space=pl.ANY)
    columns = pl.BlockSpec((row_total, tile), lambda j, t: (0, j))
    out_specs, out_shape = [columns], [jax.ShapeDtypeStruct((row_total, width), BF16)]
    if with_ids:
        out_specs.append(smem)
        out_shape.append(jax.ShapeDtypeStruct(ids.shape, ids.dtype))
    out = pl.pallas_call(
        functools.partial(product_kernel, len(addends), with_ids),
        grid_spec=pltpu.PrefetchScalarGridSpec(
            num_scalar_prefetch=1,
            grid=(width // tile,),
            in_specs=[
                pl.BlockSpec((row_total, depth), lambda j, t: (0, 0)),
                pl.BlockSpec((depth, tile), lambda j, t: (0, t[0] + j)),
            ]
            + [columns] * len(addends)
            + [smem] * with_ids
            + [hbm] * len(after),
            out_specs=out_specs,
        ),
        out_shape=out_shape,
        compiler_params=pltpu.CompilerParams(vmem_limit_bytes=VMEM_LIMIT),
        cost_estimate=SMALL,
        name="block_product",
    )((first // tile).reshape(1), rows, weight, *addends, *([ids] if with_ids else []), *after)
    return out if with_ids else out[0]


def pick_kernel(peers, afters, me_ref, table_ref, lens_ref, *rest):
    ids_refs = rest[:peers]
    down_ref, up_ref = rest[peers : peers + 2]
    rest = rest[peers + 2 + afters :]
    packs, (start_ref, end_ref, pick_ref, sem) = rest[:peers], rest[peers:]
    segs = lens_ref.shape[1]
    share, _, depth = down_ref.shape
    cols = up_ref.shape[2]
    me = me_ref[0]

    def clear(q, carry):
        pick_ref[q] = 0
        start_ref[q] = 0
        end_ref[q] = 0
        return carry

    lax.fori_loop(0, peers * CAP, clear, 0)

    def copies(x, c, source):
        pack = packs[x].at[c]
        return (
            pltpu.make_async_copy(down_ref.at[source], pack.at[:, pl.ds(0, depth)], sem),
            pltpu.make_async_copy(up_ref.at[source], pack.at[:, pl.ds(depth, cols)], sem),
        )

    for x in reversed(range(peers)):

        def choose(s, count):
            local = table_ref[ids_refs[x][0, s]] - me * share
            mine = jnp.logical_and(local >= 0, local < share)

            @pl.when(jnp.logical_and(mine, count < CAP))
            def _():
                pick_ref[x * CAP + count] = local

            return count + mine.astype(jnp.int32)

        lax.fori_loop(0, segs, choose, 0)
        for c in range(CAP):
            for copy in copies(x, c, pick_ref[x * CAP + c]):
                copy.start()

    for x in range(peers):
        owner = lax.bitwise_xor(me, jnp.int32(x))

        def place(s, carry):
            count, first = carry
            local = table_ref[ids_refs[0][0, s]] - owner * share
            theirs = jnp.logical_and(local >= 0, local < share)
            last = first + lens_ref[0, s]

            @pl.when(jnp.logical_and(theirs, count < CAP))
            def _():
                start_ref[x * CAP + count] = first
                end_ref[x * CAP + count] = last

            return count + theirs.astype(jnp.int32), last

        lax.fori_loop(0, segs, place, (0, 0))

    for x in range(peers):
        for c in range(CAP):
            for copy in copies(x, c, 0):
                copy.wait()


def pick_adapters(me, table, all_ids, lens, down, up, after):
    peers = len(all_ids)
    _, rank, depth = down.shape
    cols = up.shape[2]
    smem = pl.BlockSpec(memory_space=pltpu.SMEM)
    vmem = pl.BlockSpec(memory_space=pltpu.VMEM)
    hbm = pl.BlockSpec(memory_space=pl.ANY)
    out = pl.pallas_call(
        functools.partial(pick_kernel, peers, len(after)),
        in_specs=[smem] * (3 + peers) + [hbm] * (2 + len(after)),
        out_specs=[vmem] * peers + [smem, smem],
        out_shape=[jax.ShapeDtypeStruct((CAP, rank, depth + cols), BF16)] * peers
        + [jax.ShapeDtypeStruct((peers * CAP,), jnp.int32)] * 2,
        scratch_shapes=[pltpu.SMEM((peers * CAP,), jnp.int32), pltpu.SemaphoreType.DMA],
        compiler_params=pltpu.CompilerParams(vmem_limit_bytes=VMEM_LIMIT),
        cost_estimate=SMALL,
        name="pick_adapters",
    )(me.reshape(1), table, lens, *all_ids, down, up, *after)
    return list(out[:-2]), out[-2], out[-1]


def pack_spec(pack, first, width):
    return pl.BlockSpec(pack.shape[:2] + (width,), lambda i: (0, 0, first // width))


def low_kernel(peers, start_ref, end_ref, rows_ref, *rest):
    down_refs, out_ref = rest[:peers], rest[-1]
    row_total, depth = rows_ref.shape
    rank = out_ref.shape[0]
    place = lax.broadcasted_iota(jnp.int32, (rank, row_total), 1)
    total = jnp.zeros((rank, row_total), F32)
    for x, down_ref in enumerate(down_refs):
        part = lax.dot_general(
            down_ref[...].reshape(CAP * rank, depth),
            rows_ref[...],
            (((1,), (1,)), ((), ())),
            preferred_element_type=F32,
        )
        for c in range(CAP):
            q = x * CAP + c
            member = jnp.logical_and(place >= start_ref[q], place < end_ref[q])
            total = jnp.where(member, part[c * rank : (c + 1) * rank], total)
    out_ref[...] = total


def low_sums(starts, ends, rows, packs, rank, after):
    row_total, depth = rows.shape
    smem = pl.BlockSpec(memory_space=pltpu.SMEM)
    vmem = pl.BlockSpec(memory_space=pltpu.VMEM)
    return pl.pallas_call(
        functools.partial(low_kernel, len(packs)),
        grid=(1,),
        in_specs=[smem, smem, vmem]
        + [pack_spec(p, 0, depth) for p in packs]
        + [pl.BlockSpec(memory_space=pl.ANY)] * len(after),
        out_specs=vmem,
        out_shape=jax.ShapeDtypeStruct((rank, row_total), F32),
        compiler_params=pltpu.CompilerParams(vmem_limit_bytes=VMEM_LIMIT),
        cost_estimate=SMALL,
        name="low_sums",
    )(starts, ends, rows, *packs, *after)


def finish_kernel(lows, peers, pieces, parts, start_ref, end_ref, *rest):
    low_refs, rest = rest[:lows], rest[lows:]
    up_refs, base_refs, out_ref, spread_ref = rest[:peers], rest[peers:-2], rest[-2], rest[-1]
    rank, row_total = low_refs[0].shape
    tile = out_ref.shape[1]
    step = pl.program_id(0)

    @pl.when(step == 0)
    def _():
        low = low_refs[0][...]
        for ref in low_refs[1:]:
            low = low + ref[...]
        low = low.astype(BF16).astype(F32)
        place = lax.broadcasted_iota(jnp.int32, (rank, row_total), 1)
        spread = []
        for q in range(peers * CAP):
            member = jnp.logical_and(place >= start_ref[q], place < end_ref[q])
            spread.append(jnp.where(member, low, 0.0))
        spread_ref[...] = jnp.concatenate(spread, axis=0).astype(BF16)

    ups = jnp.concatenate([ref[...].reshape(CAP * rank, tile) for ref in up_refs], axis=0)
    total = lax.dot_general(
        spread_ref[...], ups, (((0,), (0,)), ((), ())), preferred_element_type=F32
    )
    steps = pl.num_programs(0) // pieces
    for piece in range(pieces):

        @pl.when(step // steps == piece)
        def _():
            base = base_refs[piece * parts][...].astype(F32)
            for ref in base_refs[piece * parts + 1 : (piece + 1) * parts]:
                base = base + ref[...].astype(F32)
            out_ref[...] = (base + total).astype(out_ref.dtype)


def finish(starts, ends, lows, packs, bases):
    rank, row_total = lows[0].shape
    pieces, parts = len(bases), len(bases[0])
    width = bases[0][0].shape[1]
    cols = width * pieces
    tile = min(256, width)
    steps = width // tile
    skip = (packs[0].shape[2] - cols) // tile
    smem = pl.BlockSpec(memory_space=pltpu.SMEM)
    in_specs = [smem, smem]
    in_specs += [pl.BlockSpec((rank, row_total), lambda j: (0, 0))] * len(lows)
    in_specs += [pl.BlockSpec((CAP, rank, tile), lambda j: (0, 0, skip + j))] * len(packs)
    for piece in range(pieces):

        def place(j, piece=piece):
            return 0, jnp.clip(j - piece * steps, 0, steps - 1)

        in_specs += [pl.BlockSpec((row_total, tile), place)] * parts
    return pl.pallas_call(
        functools.partial(finish_kernel, len(lows), len(packs), pieces, parts),
        grid=(cols // tile,),
        in_specs=in_specs,
        out_specs=pl.BlockSpec((row_total, tile), lambda j: (0, j)),
        out_shape=jax.ShapeDtypeStruct((row_total, cols), BF16),
        scratch_shapes=[pltpu.VMEM((len(packs) * CAP * rank, row_total), BF16)],
        compiler_params=pltpu.CompilerParams(vmem_limit_bytes=VMEM_LIMIT),
        cost_estimate=SMALL,
        name="finish",
    )(starts, ends, *lows, *packs, *[b for piece in bases for b in piece])


def local(req_total, tp_total, rows, weight, down, up, table, ids, lens):
    rank = down.shape[1]
    cols = up.shape[2]
    width = cols // PIECES
    me_req = lax.axis_index("req").astype(jnp.int32)
    me = lax.axis_index("tp").astype(jnp.int32)
    steps = tp_total - 1

    def move(value, piece):
        way = 1 if piece % 2 == 0 else tp_total - 1
        return lax.ppermute(value, "tp", [(i, (i + way) % tp_total) for i in range(tp_total)])

    def partial(back, piece, **options):
        behind = tp_total - back if piece % 2 == 0 else back
        block = lax.rem(me + behind, tp_total)
        return block_product(rows, weight, block * cols + piece * width, width, **options)

    last = partial(1, 0)
    moving, owns = [move(last, 0)], []
    for piece in range(1, PIECES):
        last, ids = partial(1, piece, after=[last], ids=ids)
        moving.append(move(last, piece))

    all_ids = [ids]
    for x in range(1, req_total):
        all_ids.append(lax.ppermute(ids, "req", [(i, i ^ x) for i in range(req_total)]))
    packs, starts, ends = pick_adapters(me_req, table, all_ids, lens, down, up, [last])
    for x in range(1, req_total):
        packs[x] = lax.ppermute(packs[x], "req", [(i, i ^ x) for i in range(req_total)])

    last = starts
    for step in range(1, steps):
        for piece in range(PIECES):
            if step == steps - 1 and piece == PIECES - 1:
                low = low_sums(starts, ends, rows, packs, rank, [last])
                lows = [low]
                for x in range(1, tp_total):
                    pairs = [(i, i ^ x) for i in range(tp_total)]
                    lows.append(lax.ppermute(low, "tp", pairs))
                last = low
            last = partial(1 + step, piece, addends=[moving[piece]], after=[last])
            moving[piece] = move(last, piece)
            if step == 1:
                last = partial(0, piece, after=[last])
                owns.append(last)

    bases = [[owns[piece], moving[piece]] for piece in range(PIECES)]
    return finish(starts, ends, lows, packs, bases)


def solution(mesh):
    return jax.shard_map(
        functools.partial(local, mesh.shape["req"], mesh.shape["tp"]),
        mesh=mesh,
        in_specs=(
            P(("groups", "req"), "tp"),
            P("tp", None),
            P(("groups", "req"), None, "tp"),
            P(("groups", "req"), None, "tp"),
            P("groups"),
            P(("groups", "req"), None),
            P(("groups", "req"), None),
        ),
        out_specs=P(("groups", "req"), "tp"),
        check_vma=False,
    )
```

time: 90 us -> 86.1 us (0.957)
  Pallas kernels: 49.2 us -> 36.1 us
  starting transfers between devices: 16 us -> 25.3 us
    pallas_call x11 -> x9, Pallas kernels: 41.4 us -> 28.3 us  [the longest x8 24.1 us: block_product(): pl.pallas_call(functools.partial(product_kernel, len(addends), with_ids),...]
    ppermute x6, starting transfers between devices: 6.91 us -> 16.6 us  [move(): lax.ppermute(value, 'tp', [(i, (i + way) % tp_total) for i in range(tp_to...]
    ppermute x6, waiting for transfers between devices: 4.4 us -> 10.1 us  [move(): lax.ppermute(value, 'tp', [(i, (i + way) % tp_total) for i in range(tp_to...]
    ppermute x3, waiting for transfers between devices: 15.6 us -> 10.1 us  [local(): lows.append(lax.ppermute(low, 'tp', pairs))]
  transfers between devices with their start and end apart: 15 -> 15, of which waited for: 6 -> 7; matrix products, arithmetic and copies ran while one was open for 0% -> 0% of each run, Pallas kernels for 47% -> 34%
where the time goes in v5:
time: 86.1 us; the launch traced here: 85.6 us
  Pallas kernels  36.1 us (42%)
  starting transfers between devices  25.3 us (29%)
  waiting for transfers between devices  22.5 us (26%)
  local copies, waits for them, and re-layouts  1.61 us (2%)
    pallas_call x8, Pallas kernels, block_product(): pl.pallas_call(functools.partial(product_kernel, len(addends), with_ids),...  24.1 us
    ppermute x6, starting transfers between devices, move(): lax.ppermute(value, 'tp', [(i, (i + way) % tp_total) for i in range(tp_to...  16.6 us
    ppermute x6, waiting for transfers between devices, move(): lax.ppermute(value, 'tp', [(i, (i + way) % tp_total) for i in range(tp_to...  10.1 us
    ppermute x3, waiting for transfers between devices, local(): lows.append(lax.ppermute(low, 'tp', pairs))  10.1 us
    ppermute x3, starting transfers between devices, local(): lows.append(lax.ppermute(low, 'tp', pairs))  4.39 us
    pallas_call x1, Pallas kernels, finish(): pl.pallas_call(functools.partial(finish_kernel, len(lows), len(packs), pi...  4.12 us
    pallas_call x1, Pallas kernels, pick_adapters(): pl.pallas_call(functools.partial(pick_kernel, peers, len(after)), in_spec...  3.91 us
    pallas_call x1, Pallas kernels, low_sums(): pl.pallas_call(functools.partial(low_kernel, len(packs)), grid=(1,), in_s...  3.9 us
  transfers between devices with their start and end apart: 15, of which 7 were waited for; matrix products, arithmetic and copies ran while one was open for 0% of the time, Pallas kernels for 34%

profile of v5, /device:TPU:0, one launch (start us, length us, event | category | flops | bytes accessed | tf_op | source)
XLA Modules:
  0.0 85.6 jit_solution(3626809543996451678)
XLA Ops:
  0.0 0.0 copy-start
  0.0 1.6 %copy-done = bf16[512,2048]{1,0:T(8,128)(2,1)S(1)} copy-done((bf16[512,2048]{1,0:T(8,128)(2,1)S(1)}, bf16[512,2048]{1,0:T(8,128)(2,1)}, u32[]{:S(2)}) %copy-start) | copy-done | bytes 2097176
  1.6 0.0 copy-start.1
  1.6 0.0 copy-start.3
  1.6 2.9 %block_product.8.rest_1_ = bf16[512,512]{1,0:T(8,128)(2,1)S(1)} custom-call(s32[1]{0:T(128)} %bitcast.2.first_ref, bf16[512,2048]{1,0:T(8,128)(2,1)S(1)} %copy-done, bf16[2048,4096]{1,0:T(8,128)(2,1)} %weight_ref.15), custom_call_target="tpu_custom_call" | custom-call | flops 1000 | bytes 1000 | tf_op jit(solution)/shard_map/block_product/pallas_call | solution.py:41
  4.5 3.1 %collective-permute-start.6 = (bf16[512,512]{1,0:T(8,128)(2,1)S(1)}, bf16[512,512]{1,0:T(8,128)(2,1)}, u32[]{:S(2)}, u32[]{:S(2)}) collective-permute-start(bf16[512,512]{1,0:T(8,128)(2,1)S(1)} %block_product.8.rest_1_), channel_id=1, source_target_pairs={{0,1},{1,2},{2,3},{3,0},{4,5},{5,6},{6,7},{7,4},{8,9},{9,10},{10,1... | collective-permute-start | bytes 1572872 | tf_op jit(solution)/shard_map/ppermute | solution.py:268
  7.5 0.0 copy-done.1
  7.5 0.0 copy-done.3
  7.5 0.0 copy-start.2
  7.5 0.0 copy-start.4
  7.5 3.5 %block_product.9 = (bf16[512,512]{1,0:T(8,128)(2,1)}, s32[1,12]{1,0:T(1,128)S(1)}) custom-call(s32[1]{0:T(128)} %bitcast.1.first_ref, bf16[512,2048]{1,0:T(8,128)(2,1)S(1)} %copy-done.1, bf16[2048,4096]{1,0:T(8,128)(2,1)} %weight_ref.15, s32[1,12]{1,0:T(1,128)S(1)} %copy-done.3, bf16[512,512]{1,0:T(8,128)(2,1)S(1)} %block_product.8.rest_1_), custom_call_target="tpu_custom_call" | custom-call | flops 1000 | bytes 1000 | tf_op jit(solution)/shard_map/block_product/pallas_call | solution.py:41
  11.0 2.1 %collective-permute-start.8 = (bf16[512,512]{1,0:T(8,128)(2,1)}, bf16[512,512]{1,0:T(8,128)(2,1)}, u32[]{:S(2)}, u32[]{:S(2)}) collective-permute-start(bf16[512,512]{1,0:T(8,128)(2,1)} %get-tuple-element.14.rest_6_), channel_id=1, source_target_pairs={{0,3},{1,0},{2,1},{3,2},{4,7},{5,4},{6,5},{7,6},{8,11},{9,8},{10,9... | collective-permute-start | bytes 1572872 | tf_op jit(solution)/shard_map/ppermute | solution.py:268
  13.1 0.7 collective-permute-start.2
  13.8 1.0 %collective-permute-start.1 = (s32[1,12]{1,0:T(1,128)S(1)}, s32[1,12]{1,0:T(1,128)S(1)}, u32[]{:S(2)}, u32[]{:S(2)}) collective-permute-start(s32[1,12]{1,0:T(1,128)S(1)} %get-tuple-element.13.rest_0_), channel_id=1, source_target_pairs={{0,8},{4,12},{8,0},{12,4},{1,9},{5,13},{9,1},{13,5},{2,10},{6,14},... | collective-permute-start | bytes 152 | tf_op jit(solution)/shard_map/ppermute | solution.py:283
  14.8 0.2 collective-permute-start
  15.0 1.1 %collective-permute-done.2.rest_3_ = s32[1,12]{1,0:T(1,128)S(1)} collective-permute-done((s32[1,12]{1,0:T(1,128)S(1)}, s32[1,12]{1,0:T(1,128)S(1)}, u32[]{:S(2)}, u32[]{:S(2)}) %collective-permute-start.2) | collective-permute-done | bytes 80 | tf_op jit(solution)/shard_map/ppermute | solution.py:283
  16.1 1.3 %collective-permute-done.1.rest_2_ = s32[1,12]{1,0:T(1,128)S(1)} collective-permute-done((s32[1,12]{1,0:T(1,128)S(1)}, s32[1,12]{1,0:T(1,128)S(1)}, u32[]{:S(2)}, u32[]{:S(2)}) %collective-permute-start.1) | collective-permute-done | bytes 80 | tf_op jit(solution)/shard_map/ppermute | solution.py:283
  17.3 0.0 collective-permute-done.rest_1_
  17.3 0.0 copy-done.2
  17.3 0.0 copy-done.4
  17.3 3.9 %pick_adapters.1 = (bf16[6,16,3072]{2,1,0:T(8,128)(2,1)S(1)}, bf16[6,16,3072]{2,1,0:T(8,128)(2,1)}, bf16[6,16,3072]{2,1,0:T(8,128)(2,1)}, bf16[6,16,3072]{2,1,0:...) custom-call(s32[1]{0:T(128)} %bitcast.me_ref, s32[512]{0:T(512)S(1)} %copy-done.2, s32[1,12]{1,0:T(1,128)S(1)} %copy-done.4, ...), custom_call_target="tpu_custom_call" | custom-call | flops 1000 | bytes 1000 | tf_op jit(solution)/shard_map/pick_adapters/pallas_call | solution.py:136
  21.2 0.7 collective-permute-start.3
  22.0 1.7 %collective-permute-start.4 = (bf16[6,16,3072]{2,1,0:T(8,128)(2,1)}, bf16[6,16,3072]{2,1,0:T(8,128)(2,1)}, u32[]{:S(2)}, u32[]{:S(2)}) collective-permute-start(bf16[6,16,3072]{2,1,0:T(8,128)(2,1)} %get-tuple-element.19), channel_id=1, source_target_pairs={{0,8},{4,12},{8,0},{12,4},{1,9},{5,13},{9,1},{13,5},{2,10},{6,14},... | collective-permute-start | bytes 1769480 | tf_op jit(solution)/shard_map/ppermute | solution.py:286
  23.6 0.1 collective-permute-start.5
  23.7 0.0 collective-permute-done.6.rest_0_
  23.7 3.4 %block_product.10.rest_0_ = bf16[512,512]{1,0:T(8,128)(2,1)} custom-call(s32[1]{0:T(128)} %bitcast.4.first_ref, bf16[512,2048]{1,0:T(8,128)(2,1)S(1)} %copy-done.1, bf16[2048,4096]{1,0:T(8,128)(2,1)} %weight_ref.15, bf16[512,512]{1,0:T(8,128)(2,1)} %collective-permute-done.6.rest_0_, s32[24]{0:T(128)S(1)} %get-tuple-element.15.rest_1_.start_ref), custom_call_target="tpu_custom_call" | custom-call | flops 1000 | bytes 1000 | tf_op jit(solution)/shard_map/block_product/pallas_call | solution.py:41
  27.2 0.0 collective-permute-start.7
  27.2 2.7 %block_product.11.rest_1_.rest_8_ = bf16[512,512]{1,0:T(8,128)(2,1)S(1)} custom-call(s32[1]{0:T(128)} %bitcast.7.first_ref, bf16[512,2048]{1,0:T(8,128)(2,1)S(1)} %copy-done.1, bf16[2048,4096]{1,0:T(8,128)(2,1)} %weight_ref.15, bf16[512,512]{1,0:T(8,128)(2,1)} %block_product.10.rest_0_), custom_call_target="tpu_custom_call" | custom-call | flops 1000 | bytes 1000 | tf_op jit(solution)/shard_map/block_product/pallas_call | solution.py:41
  29.9 3.5 %collective-permute-done.8.rest_0_ = bf16[512,512]{1,0:T(8,128)(2,1)} collective-permute-done((bf16[512,512]{1,0:T(8,128)(2,1)}, bf16[512,512]{1,0:T(8,128)(2,1)}, u32[]{:S(2)}, u32[]{:S(2)}) %collective-permute-start.8) | collective-permute-done | bytes 524320 | tf_op jit(solution)/shard_map/ppermute | solution.py:268
  33.3 3.5 %block_product.12.rest_0_ = bf16[512,512]{1,0:T(8,128)(2,1)} custom-call(s32[1]{0:T(128)} %bitcast.6.first_ref, bf16[512,2048]{1,0:T(8,128)(2,1)S(1)} %copy-done.1, bf16[2048,4096]{1,0:T(8,128)(2,1)} %weight_ref.15, bf16[512,512]{1,0:T(8,128)(2,1)} %collective-permute-done.8.rest_0_, bf16[512,512]{1,0:T(8,128)(2,1)S(1)} %block_product.11.rest_1_.rest_8_), custom_call_target="tpu_custom_call" | custom-call | flops 1000 | bytes 1000 | tf_op jit(solution)/shard_map/block_product/pallas_call | solution.py:41
  36.8 6.5 %collective-permute-start.13 = (bf16[512,512]{1,0:T(8,128)(2,1)}, bf16[512,512]{1,0:T(8,128)(2,1)}, u32[]{:S(2)}, u32[]{:S(2)}) collective-permute-start(bf16[512,512]{1,0:T(8,128)(2,1)} %block_product.12.rest_0_), channel_id=1, source_target_pairs={{0,3},{1,0},{2,1},{3,2},{4,7},{5,4},{6,5},{7,6},{8,11},{9,8},{10,9... | collective-permute-start | bytes 1572872 | tf_op jit(solution)/shard_map/ppermute | solution.py:268
  43.2 2.7 %block_product.13.rest_1_.rest_10_ = bf16[512,512]{1,0:T(8,128)(2,1)S(1)} custom-call(s32[1]{0:T(128)} %bitcast.5.first_ref, bf16[512,2048]{1,0:T(8,128)(2,1)S(1)} %copy-done.1, bf16[2048,4096]{1,0:T(8,128)(2,1)} %weight_ref.15, bf16[512,512]{1,0:T(8,128)(2,1)} %block_product.12.rest_0_), custom_call_target="tpu_custom_call" | custom-call | flops 1000 | bytes 1000 | tf_op jit(solution)/shard_map/block_product/pallas_call | solution.py:41
  45.9 4.3 %collective-permute-done.7.rest_0_ = bf16[512,512]{1,0:T(8,128)(2,1)} collective-permute-done((bf16[512,512]{1,0:T(8,128)(2,1)}, bf16[512,512]{1,0:T(8,128)(2,1)}, u32[]{:S(2)}, u32[]{:S(2)}) %collective-permute-start.7) | collective-permute-done | bytes 524320 | tf_op jit(solution)/shard_map/ppermute | solution.py:268
  50.2 2.8 %block_product.14.rest_4_ = bf16[512,512]{1,0:T(8,128)(2,1)S(1)} custom-call(s32[1]{0:T(128)} %bitcast.3.first_ref, bf16[512,2048]{1,0:T(8,128)(2,1)S(1)} %copy-done.1, bf16[2048,4096]{1,0:T(8,128)(2,1)} %weight_ref.15, bf16[512,512]{1,0:T(8,128)(2,1)} %collective-permute-done.7.rest_0_, bf16[512,512]{1,0:T(8,128)(2,1)S(1)} %block_product.13.rest_1_.rest_10_), custom_call_target="tpu_custom_call" | custom-call | flops 1000 | bytes 1000 | tf_op jit(solution)/shard_map/block_product/pallas_call | solution.py:41
  53.0 2.4 %collective-permute-start.12 = (bf16[512,512]{1,0:T(8,128)(2,1)S(1)}, bf16[512,512]{1,0:T(8,128)(2,1)S(1)}, u32[]{:S(2)}, u32[]{:S(2)}) collective-permute-start(bf16[512,512]{1,0:T(8,128)(2,1)S(1)} %block_product.14.rest_4_), channel_id=1, source_target_pairs={{0,1},{1,2},{2,3},{3,0},{4,5},{5,6},{6,7},{7,4},{8,9},{9,10},{10,1... | collective-permute-start | bytes 1572872 | tf_op jit(solution)/shard_map/ppermute | solution.py:268
  55.4 0.0 collective-permute-done.3.rest_1_.rest_5_
  55.4 0.0 collective-permute-done.4.rest_2_.rest_6_
  55.4 0.0 collective-permute-done.5.rest_3_.rest_7_
  55.4 3.9 %low_sums.1.rest_1_.rest_0_ = f32[16,512]{1,0:T(8,128)S(1)} custom-call(s32[24]{0:T(128)S(1)} %get-tuple-element.15.rest_1_.start_ref, s32[24]{0:T(128)S(1)} %get-tuple-element.16.end_ref, bf16[512,2048]{1,0:T(8,128)(2,1)S(1)} %copy-done.1, bf16[6,16,3072]{2,1,0:T(8,128)(2,1)S(1)} %get-tuple-element.17.rest_0_.rest_4_, ...), custom_call_target="tpu_custom_call" | custom-call | flops 1000 | bytes 1000 | tf_op jit(solution)/shard_map/low_sums/pallas_call | solution.py:178
  59.3 2.4 %collective-permute-done.13.rest_0_ = bf16[512,512]{1,0:T(8,128)(2,1)} collective-permute-done((bf16[512,512]{1,0:T(8,128)(2,1)}, bf16[512,512]{1,0:T(8,128)(2,1)}, u32[]{:S(2)}, u32[]{:S(2)}) %collective-permute-start.13) | collective-permute-done | bytes 524320 | tf_op jit(solution)/shard_map/ppermute | solution.py:268
  61.7 2.8 %block_product.15 = bf16[512,512]{1,0:T(8,128)(2,1)S(1)} custom-call(s32[1]{0:T(128)} %bitcast.8.first_ref, bf16[512,2048]{1,0:T(8,128)(2,1)S(1)} %copy-done.1, bf16[2048,4096]{1,0:T(8,128)(2,1)} %weight_ref.15, bf16[512,512]{1,0:T(8,128)(2,1)} %collective-permute-done.13.rest_0_, f32[16,512]{1,0:T(8,128)S(1)} %low_sums.1.rest_1_.rest_0_), custom_call_target="tpu_custom_call" | custom-call | flops 1000 | bytes 1000 | tf_op jit(solution)/shard_map/block_product/pallas_call | solution.py:41
  64.5 2.5 %collective-permute-start.14 = (bf16[512,512]{1,0:T(8,128)(2,1)S(1)}, bf16[512,512]{1,0:T(8,128)(2,1)S(1)}, u32[]{:S(2)}, u32[]{:S(2)}) collective-permute-start(bf16[512,512]{1,0:T(8,128)(2,1)S(1)} %block_product.15), channel_id=1, source_target_pairs={{0,3},{1,0},{2,1},{3,2},{4,7},{5,4},{6,5},{7,6},{8,11},{9,8},{10,9... | collective-permute-start | bytes 1572872 | tf_op jit(solution)/shard_map/ppermute | solution.py:268
  67.0 2.0 %collective-permute-start.11 = (f32[16,512]{1,0:T(8,128)S(1)}, f32[16,512]{1,0:T(8,128)S(1)}, u32[]{:S(2)}, u32[]{:S(2)}) collective-permute-start(f32[16,512]{1,0:T(8,128)S(1)} %low_sums.1.rest_1_.rest_0_), channel_id=1, source_target_pairs={{0,3},{1,2},{2,1},{3,0},{4,7},{5,6},{6,5},{7,4},{8,11},{9,10},{10,... | collective-permute-start | bytes 98312 | tf_op jit(solution)/shard_map/ppermute | solution.py:296
  69.0 0.0 collective-permute-start.10
  69.0 2.4 %collective-permute-start.9 = (f32[16,512]{1,0:T(8,128)S(1)}, f32[16,512]{1,0:T(8,128)S(1)}, u32[]{:S(2)}, u32[]{:S(2)}) collective-permute-start(f32[16,512]{1,0:T(8,128)S(1)} %low_sums.1.rest_1_.rest_0_), channel_id=1, source_target_pairs={{0,1},{1,0},{2,3},{3,2},{4,5},{5,4},{6,7},{7,6},{8,9},{9,8},{10,11... | collective-permute-start | bytes 98312 | tf_op jit(solution)/shard_map/ppermute | solution.py:296
  71.4 7.9 %collective-permute-done.11.rest_3_ = f32[16,512]{1,0:T(8,128)S(1)} collective-permute-done((f32[16,512]{1,0:T(8,128)S(1)}, f32[16,512]{1,0:T(8,128)S(1)}, u32[]{:S(2)}, u32[]{:S(2)}) %collective-permute-start.11) | collective-permute-done | bytes 32800 | tf_op jit(solution)/shard_map/ppermute | solution.py:296
  79.3 2.1 %collective-permute-done.10.rest_2_ = f32[16,512]{1,0:T(8,128)S(1)} collective-permute-done((f32[16,512]{1,0:T(8,128)S(1)}, f32[16,512]{1,0:T(8,128)S(1)}, u32[]{:S(2)}, u32[]{:S(2)}) %collective-permute-start.10) | collective-permute-done | bytes 32800 | tf_op jit(solution)/shard_map/ppermute | solution.py:296
  81.5 0.0 collective-permute-done.9.rest_1_
  81.5 0.0 collective-permute-done.12.rest_9_
  81.5 0.0 collective-permute-done.14.rest_11_
  81.5 4.1 %finish.1 = bf16[512,1024]{1,0:T(8,128)(2,1)} custom-call(s32[24]{0:T(128)S(1)} %get-tuple-element.15.rest_1_.start_ref, s32[24]{0:T(128)S(1)} %get-tuple-element.16.end_ref, f32[16,512]{1,0:T(8,128)S(1)} %low_sums.1.rest_1_.rest_0_, f32[16,512]{1,0:T(8,128)S(1)} %collective-permute-done.9.rest_1_, f32[16,512]{1,0:T(8,128)S(1)} %collective-permute-done.10.rest_2_, ...), custom_call_target="tpu_custom_call" | custom-call | flops 1000 | bytes 1000 | tf_op jit(solution)/shard_map/finish/pallas_call | solution.py:245
Async XLA Ops:
  0.0 1.6 %copy-start = (bf16[512,2048]{1,0:T(8,128)(2,1)S(1)}, bf16[512,2048]{1,0:T(8,128)(2,1)}, u32[]{:S(2)}) copy-start(bf16[512,2048]{1,0:T(8,128)(2,1)} %rows_ref.17) | copy-start | bytes 6291460
  1.6 5.9 %copy-start.1 = (bf16[512,2048]{1,0:T(8,128)(2,1)S(1)}, bf16[512,2048]{1,0:T(8,128)(2,1)}, u32[]{:S(2)}) copy-start(bf16[512,2048]{1,0:T(8,128)(2,1)} %rows_ref.17) | copy-start | bytes 6291460
  1.6 5.9 %copy-start.3 = (s32[1,12]{1,0:T(1,128)S(1)}, s32[1,12]{1,0:T(1,128)}, u32[]{:S(2)}) copy-start(s32[1,12]{1,0:T(1,128)} %rest_0_.1) | copy-start | bytes 148
  4.5 19.3 %collective-permute-start.6 = (bf16[512,512]{1,0:T(8,128)(2,1)S(1)}, bf16[512,512]{1,0:T(8,128)(2,1)}, u32[]{:S(2)}, u32[]{:S(2)}) collective-permute-start(bf16[512,512]{1,0:T(8,128)(2,1)S(1)} %block_product.8.rest_1_), channel_id=1, source_target_pairs={{0,1},{1,2},{2,3},{3,0},{4,5},{5,6},{6,7},{7,4},{8,9},{9,10},{10,1... | collective-permute-start | bytes 1572872 | tf_op jit(solution)/shard_map/ppermute | solution.py:268
  7.5 9.8 %copy-start.2 = (s32[512]{0:T(512)S(1)}, s32[512]{0:T(512)}, u32[]{:S(2)}) copy-start(s32[512]{0:T(512)} %table_ref.1) | copy-start | bytes 6148
  7.5 9.8 %copy-start.4 = (s32[1,12]{1,0:T(1,128)S(1)}, s32[1,12]{1,0:T(1,128)}, u32[]{:S(2)}) copy-start(s32[1,12]{1,0:T(1,128)} %lens_ref.1) | copy-start | bytes 148
  11.0 22.3 %collective-permute-start.8 = (bf16[512,512]{1,0:T(8,128)(2,1)}, bf16[512,512]{1,0:T(8,128)(2,1)}, u32[]{:S(2)}, u32[]{:S(2)}) collective-permute-start(bf16[512,512]{1,0:T(8,128)(2,1)} %get-tuple-element.14.rest_6_), channel_id=1, source_target_pairs={{0,3},{1,0},{2,1},{3,2},{4,7},{5,4},{6,5},{7,6},{8,11},{9,8},{10,9... | collective-permute-start | bytes 1572872 | tf_op jit(solution)/shard_map/ppermute | solution.py:268
  13.1 3.0 %collective-permute-start.2 = (s32[1,12]{1,0:T(1,128)S(1)}, s32[1,12]{1,0:T(1,128)S(1)}, u32[]{:S(2)}, u32[]{:S(2)}) collective-permute-start(s32[1,12]{1,0:T(1,128)S(1)} %get-tuple-element.13.rest_0_), channel_id=1, source_target_pairs={{0,12},{4,8},{8,4},{12,0},{1,13},{5,9},{9,5},{13,1},{2,14},{6,10},... | collective-permute-start | bytes 152 | tf_op jit(solution)/shard_map/ppermute | solution.py:283
  13.8 3.5 %collective-permute-start.1 = (s32[1,12]{1,0:T(1,128)S(1)}, s32[1,12]{1,0:T(1,128)S(1)}, u32[]{:S(2)}, u32[]{:S(2)}) collective-permute-start(s32[1,12]{1,0:T(1,128)S(1)} %get-tuple-element.13.rest_0_), channel_id=1, source_target_pairs={{0,8},{4,12},{8,0},{12,4},{1,9},{5,13},{9,1},{13,5},{2,10},{6,14},... | collective-permute-start | bytes 152 | tf_op jit(solution)/shard_map/ppermute | solution.py:283
  14.8 2.5 %collective-permute-start = (s32[1,12]{1,0:T(1,128)S(1)}, s32[1,12]{1,0:T(1,128)S(1)}, u32[]{:S(2)}, u32[]{:S(2)}) collective-permute-start(s32[1,12]{1,0:T(1,128)S(1)} %get-tuple-element.13.rest_0_), channel_id=1, source_target_pairs={{0,4},{4,0},{8,12},{12,8},{1,5},{5,1},{9,13},{13,9},{2,6},{6,2},{1... | collective-permute-start | bytes 152 | tf_op jit(solution)/shard_map/ppermute | solution.py:283
  21.2 34.1 %collective-permute-start.3 = (bf16[6,16,3072]{2,1,0:T(8,128)(2,1)}, bf16[6,16,3072]{2,1,0:T(8,128)(2,1)}, u32[]{:S(2)}, u32[]{:S(2)}) collective-permute-start(bf16[6,16,3072]{2,1,0:T(8,128)(2,1)} %get-tuple-element.18), channel_id=1, source_target_pairs={{0,4},{4,0},{8,12},{12,8},{1,5},{5,1},{9,13},{13,9},{2,6},{6,2},{1... | collective-permute-start | bytes 1769480 | tf_op jit(solution)/shard_map/ppermute | solution.py:286
  22.0 33.4 %collective-permute-start.4 = (bf16[6,16,3072]{2,1,0:T(8,128)(2,1)}, bf16[6,16,3072]{2,1,0:T(8,128)(2,1)}, u32[]{:S(2)}, u32[]{:S(2)}) collective-permute-start(bf16[6,16,3072]{2,1,0:T(8,128)(2,1)} %get-tuple-element.19), channel_id=1, source_target_pairs={{0,8},{4,12},{8,0},{12,4},{1,9},{5,13},{9,1},{13,5},{2,10},{6,14},... | collective-permute-start | bytes 1769480 | tf_op jit(solution)/shard_map/ppermute | solution.py:286
  23.6 31.8 %collective-permute-start.5 = (bf16[6,16,3072]{2,1,0:T(8,128)(2,1)}, bf16[6,16,3072]{2,1,0:T(8,128)(2,1)}, u32[]{:S(2)}, u32[]{:S(2)}) collective-permute-start(bf16[6,16,3072]{2,1,0:T(8,128)(2,1)} %get-tuple-element.20), channel_id=1, source_target_pairs={{0,12},{4,8},{8,4},{12,0},{1,13},{5,9},{9,5},{13,1},{2,14},{6,10},... | collective-permute-start | bytes 1769480 | tf_op jit(solution)/shard_map/ppermute | solution.py:286
  27.2 23.0 %collective-permute-start.7 = (bf16[512,512]{1,0:T(8,128)(2,1)}, bf16[512,512]{1,0:T(8,128)(2,1)}, u32[]{:S(2)}, u32[]{:S(2)}) collective-permute-start(bf16[512,512]{1,0:T(8,128)(2,1)} %block_product.10.rest_0_), channel_id=1, source_target_pairs={{0,1},{1,2},{2,3},{3,0},{4,5},{5,6},{6,7},{7,4},{8,9},{9,10},{10,1... | collective-permute-start | bytes 1572872 | tf_op jit(solution)/shard_map/ppermute | solution.py:268
  36.8 24.9 %collective-permute-start.13 = (bf16[512,512]{1,0:T(8,128)(2,1)}, bf16[512,512]{1,0:T(8,128)(2,1)}, u32[]{:S(2)}, u32[]{:S(2)}) collective-permute-start(bf16[512,512]{1,0:T(8,128)(2,1)} %block_product.12.rest_0_), channel_id=1, source_target_pairs={{0,3},{1,0},{2,1},{3,2},{4,7},{5,4},{6,5},{7,6},{8,11},{9,8},{10,9... | collective-permute-start | bytes 1572872 | tf_op jit(solution)/shard_map/ppermute | solution.py:268
  53.0 28.5 %collective-permute-start.12 = (bf16[512,512]{1,0:T(8,128)(2,1)S(1)}, bf16[512,512]{1,0:T(8,128)(2,1)S(1)}, u32[]{:S(2)}, u32[]{:S(2)}) collective-permute-start(bf16[512,512]{1,0:T(8,128)(2,1)S(1)} %block_product.14.rest_4_), channel_id=1, source_target_pairs={{0,1},{1,2},{2,3},{3,0},{4,5},{5,6},{6,7},{7,4},{8,9},{9,10},{10,1... | collective-permute-start | bytes 1572872 | tf_op jit(solution)/shard_map/ppermute | solution.py:268
  64.5 17.0 %collective-permute-start.14 = (bf16[512,512]{1,0:T(8,128)(2,1)S(1)}, bf16[512,512]{1,0:T(8,128)(2,1)S(1)}, u32[]{:S(2)}, u32[]{:S(2)}) collective-permute-start(bf16[512,512]{1,0:T(8,128)(2,1)S(1)} %block_product.15), channel_id=1, source_target_pairs={{0,3},{1,0},{2,1},{3,2},{4,7},{5,4},{6,5},{7,6},{8,11},{9,8},{10,9... | collective-permute-start | bytes 1572872 | tf_op jit(solution)/shard_map/ppermute | solution.py:268
  67.0 12.3 %collective-permute-start.11 = (f32[16,512]{1,0:T(8,128)S(1)}, f32[16,512]{1,0:T(8,128)S(1)}, u32[]{:S(2)}, u32[]{:S(2)}) collective-permute-start(f32[16,512]{1,0:T(8,128)S(1)} %low_sums.1.rest_1_.rest_0_), channel_id=1, source_target_pairs={{0,3},{1,2},{2,1},{3,0},{4,7},{5,6},{6,5},{7,4},{8,11},{9,10},{10,... | collective-permute-start | bytes 98312 | tf_op jit(solution)/shard_map/ppermute | solution.py:296
  69.0 12.5 %collective-permute-start.10 = (f32[16,512]{1,0:T(8,128)S(1)}, f32[16,512]{1,0:T(8,128)S(1)}, u32[]{:S(2)}, u32[]{:S(2)}) collective-permute-start(f32[16,512]{1,0:T(8,128)S(1)} %low_sums.1.rest_1_.rest_0_), channel_id=1, source_target_pairs={{0,2},{1,3},{2,0},{3,1},{4,6},{5,7},{6,4},{7,5},{8,10},{9,11},{10,... | collective-permute-start | bytes 98312 | tf_op jit(solution)/shard_map/ppermute | solution.py:296
  69.0 12.5 %collective-permute-start.9 = (f32[16,512]{1,0:T(8,128)S(1)}, f32[16,512]{1,0:T(8,128)S(1)}, u32[]{:S(2)}, u32[]{:S(2)}) collective-permute-start(f32[16,512]{1,0:T(8,128)S(1)} %low_sums.1.rest_1_.rest_0_), channel_id=1, source_target_pairs={{0,1},{1,0},{2,3},{3,2},{4,5},{5,4},{6,7},{7,6},{8,9},{9,8},{10,11... | collective-permute-start | bytes 98312 | tf_op jit(solution)/shard_map/ppermute | solution.py:296

commit v6 on v5

--- a/solution.py
+++ b/solution.py
@@ -264,11 +264,15 @@
     steps = tp_total - 1
 
     def move(value, piece):
-        way = 1 if piece % 2 == 0 else tp_total - 1
-        return lax.ppermute(value, "tp", [(i, (i + way) % tp_total) for i in range(tp_total)])
+        pairs = []
+        for r in range(req_total):
+            way = 1 if (r + piece) % 2 == 0 else tp_total - 1
+            for i in range(tp_total):
+                pairs.append((r * tp_total + i, r * tp_total + (i + way) % tp_total))
+        return lax.ppermute(value, ("req", "tp"), pairs)
 
     def partial(back, piece, **options):
-        behind = tp_total - back if piece % 2 == 0 else back
+        behind = jnp.where(lax.rem(me_req + piece, 2) == 0, tp_total - back, back)
         block = lax.rem(me + behind, tp_total)
         return block_product(rows, weight, block * cols + piece * width, width, **options)
 

time: 86.1 us -> 87.2 us (1.013)
  starting transfers between devices: 25.3 us -> 28.8 us
  waiting for transfers between devices: 22.5 us -> 19.6 us
    ppermute x6, waiting for transfers between devices: 10.1 us -> 6.05 us  [move(): return lax.ppermute(value, ('req', 'tp'), pairs)]
    ppermute x6, starting transfers between devices: 16.6 us -> 20.4 us  [move(): return lax.ppermute(value, ('req', 'tp'), pairs)]
    ppermute x3, waiting for transfers between devices: 10.1 us -> 11.3 us  [local(): lows.append(lax.ppermute(low, 'tp', pairs))]
  transfers between devices with their start and end apart: 15 -> 15, of which waited for: 7 -> 5; matrix products, arithmetic and copies ran while one was open for 0% -> 0% of each run, Pallas kernels for 34% -> 34%
where the time goes in v6:
time: 87.2 us; the launch traced here: 86.6 us
  Pallas kernels  36.4 us (42%)
  starting transfers between devices  28.8 us (33%)
  waiting for transfers between devices  19.6 us (22%)
  local copies, waits for them, and re-layouts  1.61 us (2%)
    pallas_call x8, Pallas kernels, block_product(): pl.pallas_call(functools.partial(product_kernel, len(addends), with_ids),...  24.2 us
    ppermute x6, starting transfers between devices, move(): return lax.ppermute(value, ('req', 'tp'), pairs)  20.4 us
    ppermute x3, waiting for transfers between devices, local(): lows.append(lax.ppermute(low, 'tp', pairs))  11.3 us
    ppermute x6, waiting for transfers between devices, move(): return lax.ppermute(value, ('req', 'tp'), pairs)  6.05 us
    ppermute x3, starting transfers between devices, local(): lows.append(lax.ppermute(low, 'tp', pairs))  4.45 us
    pallas_call x1, Pallas kernels, pick_adapters(): pl.pallas_call(functools.partial(pick_kernel, peers, len(after)), in_spec...  4.26 us
    pallas_call x1, Pallas kernels, finish(): pl.pallas_call(functools.partial(finish_kernel, len(lows), len(packs), pi...  4.12 us
    pallas_call x1, Pallas kernels, low_sums(): pl.pallas_call(functools.partial(low_kernel, len(packs)), grid=(1,), in_s...  3.9 us
  transfers between devices with their start and end apart: 15, of which 5 were waited for; matrix products, arithmetic and copies ran while one was open for 0% of the time, Pallas kernels for 34%

profile of v6, /device:TPU:0, one launch (start us, length us, event | category | flops | bytes accessed | tf_op | source)
XLA Modules:
  0.0 86.6 jit_solution(3617506032424927321)
XLA Ops:
  0.0 0.0 copy-start
  0.0 1.6 %copy-done = bf16[512,2048]{1,0:T(8,128)(2,1)S(1)} copy-done((bf16[512,2048]{1,0:T(8,128)(2,1)S(1)}, bf16[512,2048]{1,0:T(8,128)(2,1)}, u32[]{:S(2)}) %copy-start) | copy-done | bytes 2097176
  1.6 0.0 copy-start.1
  1.6 0.0 copy-start.3
  1.6 2.9 %block_product.8.rest_1_ = bf16[512,512]{1,0:T(8,128)(2,1)S(1)} custom-call(s32[1]{0:T(128)} %bitcast.2.first_ref, bf16[512,2048]{1,0:T(8,128)(2,1)S(1)} %copy-done, bf16[2048,4096]{1,0:T(8,128)(2,1)} %weight_ref.15), custom_call_target="tpu_custom_call" | custom-call | flops 1000 | bytes 1000 | tf_op jit(solution)/shard_map/block_product/pallas_call | solution.py:41
  4.5 3.1 %collective-permute-start.6 = (bf16[512,512]{1,0:T(8,128)(2,1)S(1)}, bf16[512,512]{1,0:T(8,128)(2,1)}, u32[]{:S(2)}, u32[]{:S(2)}) collective-permute-start(bf16[512,512]{1,0:T(8,128)(2,1)S(1)} %block_product.8.rest_1_), channel_id=1, source_target_pairs={{0,1},{1,2},{2,3},{3,0},{4,7},{5,4},{6,5},{7,6},{8,9},{9,10},{10,1... | collective-permute-start | bytes 1572872 | tf_op jit(solution)/shard_map/ppermute | solution.py:272
  7.5 0.0 copy-done.1
  7.5 0.0 copy-done.3
  7.5 0.0 copy-start.2
  7.5 0.0 copy-start.4
  7.5 3.5 %block_product.9 = (bf16[512,512]{1,0:T(8,128)(2,1)}, s32[1,12]{1,0:T(1,128)S(1)}) custom-call(s32[1]{0:T(128)} %bitcast.1.first_ref, bf16[512,2048]{1,0:T(8,128)(2,1)S(1)} %copy-done.1, bf16[2048,4096]{1,0:T(8,128)(2,1)} %weight_ref.15, s32[1,12]{1,0:T(1,128)S(1)} %copy-done.3, bf16[512,512]{1,0:T(8,128)(2,1)S(1)} %block_product.8.rest_1_), custom_call_target="tpu_custom_call" | custom-call | flops 1000 | bytes 1000 | tf_op jit(solution)/shard_map/block_product/pallas_call | solution.py:41
  11.0 2.1 %collective-permute-start.8 = (bf16[512,512]{1,0:T(8,128)(2,1)}, bf16[512,512]{1,0:T(8,128)(2,1)}, u32[]{:S(2)}, u32[]{:S(2)}) collective-permute-start(bf16[512,512]{1,0:T(8,128)(2,1)} %get-tuple-element.14.rest_6_), channel_id=1, source_target_pairs={{0,3},{1,0},{2,1},{3,2},{4,5},{5,6},{6,7},{7,4},{8,11},{9,8},{10,9... | collective-permute-start | bytes 1572872 | tf_op jit(solution)/shard_map/ppermute | solution.py:272
  13.1 0.6 collective-permute-start.2
  13.7 1.1 %collective-permute-start.1 = (s32[1,12]{1,0:T(1,128)S(1)}, s32[1,12]{1,0:T(1,128)S(1)}, u32[]{:S(2)}, u32[]{:S(2)}) collective-permute-start(s32[1,12]{1,0:T(1,128)S(1)} %get-tuple-element.13.rest_0_), channel_id=1, source_target_pairs={{0,8},{4,12},{8,0},{12,4},{1,9},{5,13},{9,1},{13,5},{2,10},{6,14},... | collective-permute-start | bytes 152 | tf_op jit(solution)/shard_map/ppermute | solution.py:287
  14.8 0.2 collective-permute-start
  15.0 1.1 %collective-permute-done.2.rest_3_ = s32[1,12]{1,0:T(1,128)S(1)} collective-permute-done((s32[1,12]{1,0:T(1,128)S(1)}, s32[1,12]{1,0:T(1,128)S(1)}, u32[]{:S(2)}, u32[]{:S(2)}) %collective-permute-start.2) | collective-permute-done | bytes 80 | tf_op jit(solution)/shard_map/ppermute | solution.py:287
  16.1 1.2 %collective-permute-done.1.rest_2_ = s32[1,12]{1,0:T(1,128)S(1)} collective-permute-done((s32[1,12]{1,0:T(1,128)S(1)}, s32[1,12]{1,0:T(1,128)S(1)}, u32[]{:S(2)}, u32[]{:S(2)}) %collective-permute-start.1) | collective-permute-done | bytes 80 | tf_op jit(solution)/shard_map/ppermute | solution.py:287
  17.2 0.0 collective-permute-done.rest_1_
  17.3 0.0 copy-done.2
  17.3 0.0 copy-done.4
  17.3 4.3 %pick_adapters.1 = (bf16[6,16,3072]{2,1,0:T(8,128)(2,1)S(1)}, bf16[6,16,3072]{2,1,0:T(8,128)(2,1)}, bf16[6,16,3072]{2,1,0:T(8,128)(2,1)}, bf16[6,16,3072]{2,1,0:...) custom-call(s32[1]{0:T(128)} %bitcast.me_ref, s32[512]{0:T(512)S(1)} %copy-done.2, s32[1,12]{1,0:T(1,128)S(1)} %copy-done.4, ...), custom_call_target="tpu_custom_call" | custom-call | flops 1000 | bytes 1000 | tf_op jit(solution)/shard_map/pick_adapters/pallas_call | solution.py:136
  21.5 0.7 collective-permute-start.3
  22.2 0.6 collective-permute-start.4
  22.8 0.8 collective-permute-start.5
  23.6 0.0 collective-permute-done.6.rest_0_
  23.6 3.4 %block_product.10.rest_0_ = bf16[512,512]{1,0:T(8,128)(2,1)} custom-call(s32[1]{0:T(128)} %bitcast.4.first_ref, bf16[512,2048]{1,0:T(8,128)(2,1)S(1)} %copy-done.1, bf16[2048,4096]{1,0:T(8,128)(2,1)} %weight_ref.15, bf16[512,512]{1,0:T(8,128)(2,1)} %collective-permute-done.6.rest_0_, s32[24]{0:T(128)S(1)} %get-tuple-element.15.rest_1_.start_ref), custom_call_target="tpu_custom_call" | custom-call | flops 1000 | bytes 1000 | tf_op jit(solution)/shard_map/block_product/pallas_call | solution.py:41
  27.1 5.9 %collective-permute-start.7 = (bf16[512,512]{1,0:T(8,128)(2,1)}, bf16[512,512]{1,0:T(8,128)(2,1)}, u32[]{:S(2)}, u32[]{:S(2)}) collective-permute-start(bf16[512,512]{1,0:T(8,128)(2,1)} %block_product.10.rest_0_), channel_id=1, source_target_pairs={{0,1},{1,2},{2,3},{3,0},{4,7},{5,4},{6,5},{7,6},{8,9},{9,10},{10,1... | collective-permute-start | bytes 1572872 | tf_op jit(solution)/shard_map/ppermute | solution.py:272
  33.0 2.7 %block_product.11.rest_1_.rest_8_ = bf16[512,512]{1,0:T(8,128)(2,1)S(1)} custom-call(s32[1]{0:T(128)} %bitcast.7.first_ref, bf16[512,2048]{1,0:T(8,128)(2,1)S(1)} %copy-done.1, bf16[2048,4096]{1,0:T(8,128)(2,1)} %weight_ref.15, bf16[512,512]{1,0:T(8,128)(2,1)} %block_product.10.rest_0_), custom_call_target="tpu_custom_call" | custom-call | flops 1000 | bytes 1000 | tf_op jit(solution)/shard_map/block_product/pallas_call | solution.py:41
  35.7 0.0 collective-permute-done.8.rest_0_
  35.7 3.5 %block_product.12.rest_0_ = bf16[512,512]{1,0:T(8,128)(2,1)} custom-call(s32[1]{0:T(128)} %bitcast.6.first_ref, bf16[512,2048]{1,0:T(8,128)(2,1)S(1)} %copy-done.1, bf16[2048,4096]{1,0:T(8,128)(2,1)} %weight_ref.15, bf16[512,512]{1,0:T(8,128)(2,1)} %collective-permute-done.8.rest_0_, bf16[512,512]{1,0:T(8,128)(2,1)S(1)} %block_product.11.rest_1_.rest_8_), custom_call_target="tpu_custom_call" | custom-call | flops 1000 | bytes 1000 | tf_op jit(solution)/shard_map/block_product/pallas_call | solution.py:41
  39.2 3.8 %collective-permute-start.13 = (bf16[512,512]{1,0:T(8,128)(2,1)}, bf16[512,512]{1,0:T(8,128)(2,1)}, u32[]{:S(2)}, u32[]{:S(2)}) collective-permute-start(bf16[512,512]{1,0:T(8,128)(2,1)} %block_product.12.rest_0_), channel_id=1, source_target_pairs={{0,3},{1,0},{2,1},{3,2},{4,5},{5,6},{6,7},{7,4},{8,11},{9,8},{10,9... | collective-permute-start | bytes 1572872 | tf_op jit(solution)/shard_map/ppermute | solution.py:272
  42.9 2.7 %block_product.13.rest_1_.rest_10_ = bf16[512,512]{1,0:T(8,128)(2,1)S(1)} custom-call(s32[1]{0:T(128)} %bitcast.5.first_ref, bf16[512,2048]{1,0:T(8,128)(2,1)S(1)} %copy-done.1, bf16[2048,4096]{1,0:T(8,128)(2,1)} %weight_ref.15, bf16[512,512]{1,0:T(8,128)(2,1)} %block_product.12.rest_0_), custom_call_target="tpu_custom_call" | custom-call | flops 1000 | bytes 1000 | tf_op jit(solution)/shard_map/block_product/pallas_call | solution.py:41
  45.6 0.0 collective-permute-done.7.rest_0_
  45.7 2.8 %block_product.14.rest_4_ = bf16[512,512]{1,0:T(8,128)(2,1)S(1)} custom-call(s32[1]{0:T(128)} %bitcast.3.first_ref, bf16[512,2048]{1,0:T(8,128)(2,1)S(1)} %copy-done.1, bf16[2048,4096]{1,0:T(8,128)(2,1)} %weight_ref.15, bf16[512,512]{1,0:T(8,128)(2,1)} %collective-permute-done.7.rest_0_, bf16[512,512]{1,0:T(8,128)(2,1)S(1)} %block_product.13.rest_1_.rest_10_), custom_call_target="tpu_custom_call" | custom-call | flops 1000 | bytes 1000 | tf_op jit(solution)/shard_map/block_product/pallas_call | solution.py:41
  48.5 5.5 %collective-permute-start.12 = (bf16[512,512]{1,0:T(8,128)(2,1)S(1)}, bf16[512,512]{1,0:T(8,128)(2,1)S(1)}, u32[]{:S(2)}, u32[]{:S(2)}) collective-permute-start(bf16[512,512]{1,0:T(8,128)(2,1)S(1)} %block_product.14.rest_4_), channel_id=1, source_target_pairs={{0,1},{1,2},{2,3},{3,0},{4,7},{5,4},{6,5},{7,6},{8,9},{9,10},{10,1... | collective-permute-start | bytes 1572872 | tf_op jit(solution)/shard_map/ppermute | solution.py:272
  53.9 0.0 collective-permute-done.3.rest_1_.rest_5_
  53.9 0.0 collective-permute-done.4.rest_2_.rest_6_
  53.9 0.0 collective-permute-done.5.rest_3_.rest_7_
  53.9 3.9 %low_sums.1.rest_1_.rest_0_ = f32[16,512]{1,0:T(8,128)S(1)} custom-call(s32[24]{0:T(128)S(1)} %get-tuple-element.15.rest_1_.start_ref, s32[24]{0:T(128)S(1)} %get-tuple-element.16.end_ref, bf16[512,2048]{1,0:T(8,128)(2,1)S(1)} %copy-done.1, bf16[6,16,3072]{2,1,0:T(8,128)(2,1)S(1)} %get-tuple-element.17.rest_0_.rest_4_, ...), custom_call_target="tpu_custom_call" | custom-call | flops 1000 | bytes 1000 | tf_op jit(solution)/shard_map/low_sums/pallas_call | solution.py:178
  57.8 6.0 %collective-permute-done.13.rest_0_ = bf16[512,512]{1,0:T(8,128)(2,1)} collective-permute-done((bf16[512,512]{1,0:T(8,128)(2,1)}, bf16[512,512]{1,0:T(8,128)(2,1)}, u32[]{:S(2)}, u32[]{:S(2)}) %collective-permute-start.13) | collective-permute-done | bytes 524320 | tf_op jit(solution)/shard_map/ppermute | solution.py:272
  63.8 2.8 %block_product.15 = bf16[512,512]{1,0:T(8,128)(2,1)S(1)} custom-call(s32[1]{0:T(128)} %bitcast.8.first_ref, bf16[512,2048]{1,0:T(8,128)(2,1)S(1)} %copy-done.1, bf16[2048,4096]{1,0:T(8,128)(2,1)} %weight_ref.15, bf16[512,512]{1,0:T(8,128)(2,1)} %collective-permute-done.13.rest_0_, f32[16,512]{1,0:T(8,128)S(1)} %low_sums.1.rest_1_.rest_0_), custom_call_target="tpu_custom_call" | custom-call | flops 1000 | bytes 1000 | tf_op jit(solution)/shard_map/block_product/pallas_call | solution.py:41
  66.6 0.1 collective-permute-start.14
  66.7 0.1 collective-permute-start.11
  66.8 3.4 %collective-permute-start.10 = (f32[16,512]{1,0:T(8,128)S(1)}, f32[16,512]{1,0:T(8,128)S(1)}, u32[]{:S(2)}, u32[]{:S(2)}) collective-permute-start(f32[16,512]{1,0:T(8,128)S(1)} %low_sums.1.rest_1_.rest_0_), channel_id=1, source_target_pairs={{0,2},{1,3},{2,0},{3,1},{4,6},{5,7},{6,4},{7,5},{8,10},{9,11},{10,... | collective-permute-start | bytes 98312 | tf_op jit(solution)/shard_map/ppermute | solution.py:300
  70.2 1.0 %collective-permute-start.9 = (f32[16,512]{1,0:T(8,128)S(1)}, f32[16,512]{1,0:T(8,128)S(1)}, u32[]{:S(2)}, u32[]{:S(2)}) collective-permute-start(f32[16,512]{1,0:T(8,128)S(1)} %low_sums.1.rest_1_.rest_0_), channel_id=1, source_target_pairs={{0,1},{1,0},{2,3},{3,2},{4,5},{5,4},{6,7},{7,6},{8,9},{9,8},{10,11... | collective-permute-start | bytes 98312 | tf_op jit(solution)/shard_map/ppermute | solution.py:300
  71.1 6.4 %collective-permute-done.11.rest_3_ = f32[16,512]{1,0:T(8,128)S(1)} collective-permute-done((f32[16,512]{1,0:T(8,128)S(1)}, f32[16,512]{1,0:T(8,128)S(1)}, u32[]{:S(2)}, u32[]{:S(2)}) %collective-permute-start.11) | collective-permute-done | bytes 32800 | tf_op jit(solution)/shard_map/ppermute | solution.py:300
  77.6 4.8 %collective-permute-done.10.rest_2_ = f32[16,512]{1,0:T(8,128)S(1)} collective-permute-done((f32[16,512]{1,0:T(8,128)S(1)}, f32[16,512]{1,0:T(8,128)S(1)}, u32[]{:S(2)}, u32[]{:S(2)}) %collective-permute-start.10) | collective-permute-done | bytes 32800 | tf_op jit(solution)/shard_map/ppermute | solution.py:300
  82.4 0.0 collective-permute-done.9.rest_1_
  82.4 0.0 collective-permute-done.12.rest_9_
  82.4 0.0 collective-permute-done.14.rest_11_
  82.4 4.1 %finish.1 = bf16[512,1024]{1,0:T(8,128)(2,1)} custom-call(s32[24]{0:T(128)S(1)} %get-tuple-element.15.rest_1_.start_ref, s32[24]{0:T(128)S(1)} %get-tuple-element.16.end_ref, f32[16,512]{1,0:T(8,128)S(1)} %low_sums.1.rest_1_.rest_0_, f32[16,512]{1,0:T(8,128)S(1)} %collective-permute-done.9.rest_1_, f32[16,512]{1,0:T(8,128)S(1)} %collective-permute-done.10.rest_2_, ...), custom_call_target="tpu_custom_call" | custom-call | flops 1000 | bytes 1000 | tf_op jit(solution)/shard_map/finish/pallas_call | solution.py:245
Async XLA Ops:
  0.0 1.6 %copy-start = (bf16[512,2048]{1,0:T(8,128)(2,1)S(1)}, bf16[512,2048]{1,0:T(8,128)(2,1)}, u32[]{:S(2)}) copy-start(bf16[512,2048]{1,0:T(8,128)(2,1)} %rows_ref.17) | copy-start | bytes 6291460
  1.6 5.9 %copy-start.1 = (bf16[512,2048]{1,0:T(8,128)(2,1)S(1)}, bf16[512,2048]{1,0:T(8,128)(2,1)}, u32[]{:S(2)}) copy-start(bf16[512,2048]{1,0:T(8,128)(2,1)} %rows_ref.17) | copy-start | bytes 6291460
  1.6 5.9 %copy-start.3 = (s32[1,12]{1,0:T(1,128)S(1)}, s32[1,12]{1,0:T(1,128)}, u32[]{:S(2)}) copy-start(s32[1,12]{1,0:T(1,128)} %rest_0_.1) | copy-start | bytes 148
  4.5 19.2 %collective-permute-start.6 = (bf16[512,512]{1,0:T(8,128)(2,1)S(1)}, bf16[512,512]{1,0:T(8,128)(2,1)}, u32[]{:S(2)}, u32[]{:S(2)}) collective-permute-start(bf16[512,512]{1,0:T(8,128)(2,1)S(1)} %block_product.8.rest_1_), channel_id=1, source_target_pairs={{0,1},{1,2},{2,3},{3,0},{4,7},{5,4},{6,5},{7,6},{8,9},{9,10},{10,1... | collective-permute-start | bytes 1572872 | tf_op jit(solution)/shard_map/ppermute | solution.py:272
  7.5 9.7 %copy-start.2 = (s32[512]{0:T(512)S(1)}, s32[512]{0:T(512)}, u32[]{:S(2)}) copy-start(s32[512]{0:T(512)} %table_ref.1) | copy-start | bytes 6148
  7.5 9.7 %copy-start.4 = (s32[1,12]{1,0:T(1,128)S(1)}, s32[1,12]{1,0:T(1,128)}, u32[]{:S(2)}) copy-start(s32[1,12]{1,0:T(1,128)} %lens_ref.1) | copy-start | bytes 148
  11.0 24.7 %collective-permute-start.8 = (bf16[512,512]{1,0:T(8,128)(2,1)}, bf16[512,512]{1,0:T(8,128)(2,1)}, u32[]{:S(2)}, u32[]{:S(2)}) collective-permute-start(bf16[512,512]{1,0:T(8,128)(2,1)} %get-tuple-element.14.rest_6_), channel_id=1, source_target_pairs={{0,3},{1,0},{2,1},{3,2},{4,5},{5,6},{6,7},{7,4},{8,11},{9,8},{10,9... | collective-permute-start | bytes 1572872 | tf_op jit(solution)/shard_map/ppermute | solution.py:272
  13.1 3.0 %collective-permute-start.2 = (s32[1,12]{1,0:T(1,128)S(1)}, s32[1,12]{1,0:T(1,128)S(1)}, u32[]{:S(2)}, u32[]{:S(2)}) collective-permute-start(s32[1,12]{1,0:T(1,128)S(1)} %get-tuple-element.13.rest_0_), channel_id=1, source_target_pairs={{0,12},{4,8},{8,4},{12,0},{1,13},{5,9},{9,5},{13,1},{2,14},{6,10},... | collective-permute-start | bytes 152 | tf_op jit(solution)/shard_map/ppermute | solution.py:287
  13.7 3.5 %collective-permute-start.1 = (s32[1,12]{1,0:T(1,128)S(1)}, s32[1,12]{1,0:T(1,128)S(1)}, u32[]{:S(2)}, u32[]{:S(2)}) collective-permute-start(s32[1,12]{1,0:T(1,128)S(1)} %get-tuple-element.13.rest_0_), channel_id=1, source_target_pairs={{0,8},{4,12},{8,0},{12,4},{1,9},{5,13},{9,1},{13,5},{2,10},{6,14},... | collective-permute-start | bytes 152 | tf_op jit(solution)/shard_map/ppermute | solution.py:287
  14.8 2.5 %collective-permute-start = (s32[1,12]{1,0:T(1,128)S(1)}, s32[1,12]{1,0:T(1,128)S(1)}, u32[]{:S(2)}, u32[]{:S(2)}) collective-permute-start(s32[1,12]{1,0:T(1,128)S(1)} %get-tuple-element.13.rest_0_), channel_id=1, source_target_pairs={{0,4},{4,0},{8,12},{12,8},{1,5},{5,1},{9,13},{13,9},{2,6},{6,2},{1... | collective-permute-start | bytes 152 | tf_op jit(solution)/shard_map/ppermute | solution.py:287
  21.5 32.4 %collective-permute-start.3 = (bf16[6,16,3072]{2,1,0:T(8,128)(2,1)}, bf16[6,16,3072]{2,1,0:T(8,128)(2,1)}, u32[]{:S(2)}, u32[]{:S(2)}) collective-permute-start(bf16[6,16,3072]{2,1,0:T(8,128)(2,1)} %get-tuple-element.18), channel_id=1, source_target_pairs={{0,4},{4,0},{8,12},{12,8},{1,5},{5,1},{9,13},{13,9},{2,6},{6,2},{1... | collective-permute-start | bytes 1769480 | tf_op jit(solution)/shard_map/ppermute | solution.py:290
  22.2 31.8 %collective-permute-start.4 = (bf16[6,16,3072]{2,1,0:T(8,128)(2,1)}, bf16[6,16,3072]{2,1,0:T(8,128)(2,1)}, u32[]{:S(2)}, u32[]{:S(2)}) collective-permute-start(bf16[6,16,3072]{2,1,0:T(8,128)(2,1)} %get-tuple-element.19), channel_id=1, source_target_pairs={{0,8},{4,12},{8,0},{12,4},{1,9},{5,13},{9,1},{13,5},{2,10},{6,14},... | collective-permute-start | bytes 1769480 | tf_op jit(solution)/shard_map/ppermute | solution.py:290
  22.8 31.2 %collective-permute-start.5 = (bf16[6,16,3072]{2,1,0:T(8,128)(2,1)}, bf16[6,16,3072]{2,1,0:T(8,128)(2,1)}, u32[]{:S(2)}, u32[]{:S(2)}) collective-permute-start(bf16[6,16,3072]{2,1,0:T(8,128)(2,1)} %get-tuple-element.20), channel_id=1, source_target_pairs={{0,12},{4,8},{8,4},{12,0},{1,13},{5,9},{9,5},{13,1},{2,14},{6,10},... | collective-permute-start | bytes 1769480 | tf_op jit(solution)/shard_map/ppermute | solution.py:290
  27.1 18.6 %collective-permute-start.7 = (bf16[512,512]{1,0:T(8,128)(2,1)}, bf16[512,512]{1,0:T(8,128)(2,1)}, u32[]{:S(2)}, u32[]{:S(2)}) collective-permute-start(bf16[512,512]{1,0:T(8,128)(2,1)} %block_product.10.rest_0_), channel_id=1, source_target_pairs={{0,1},{1,2},{2,3},{3,0},{4,7},{5,4},{6,5},{7,6},{8,9},{9,10},{10,1... | collective-permute-start | bytes 1572872 | tf_op jit(solution)/shard_map/ppermute | solution.py:272
  39.2 24.7 %collective-permute-start.13 = (bf16[512,512]{1,0:T(8,128)(2,1)}, bf16[512,512]{1,0:T(8,128)(2,1)}, u32[]{:S(2)}, u32[]{:S(2)}) collective-permute-start(bf16[512,512]{1,0:T(8,128)(2,1)} %block_product.12.rest_0_), channel_id=1, source_target_pairs={{0,3},{1,0},{2,1},{3,2},{4,5},{5,6},{6,7},{7,4},{8,11},{9,8},{10,9... | collective-permute-start | bytes 1572872 | tf_op jit(solution)/shard_map/ppermute | solution.py:272
  48.5 34.0 %collective-permute-start.12 = (bf16[512,512]{1,0:T(8,128)(2,1)S(1)}, bf16[512,512]{1,0:T(8,128)(2,1)S(1)}, u32[]{:S(2)}, u32[]{:S(2)}) collective-permute-start(bf16[512,512]{1,0:T(8,128)(2,1)S(1)} %block_product.14.rest_4_), channel_id=1, source_target_pairs={{0,1},{1,2},{2,3},{3,0},{4,7},{5,4},{6,5},{7,6},{8,9},{9,10},{10,1... | collective-permute-start | bytes 1572872 | tf_op jit(solution)/shard_map/ppermute | solution.py:272
  66.6 15.8 %collective-permute-start.14 = (bf16[512,512]{1,0:T(8,128)(2,1)S(1)}, bf16[512,512]{1,0:T(8,128)(2,1)S(1)}, u32[]{:S(2)}, u32[]{:S(2)}) collective-permute-start(bf16[512,512]{1,0:T(8,128)(2,1)S(1)} %block_product.15), channel_id=1, source_target_pairs={{0,3},{1,0},{2,1},{3,2},{4,5},{5,6},{6,7},{7,4},{8,11},{9,8},{10,9... | collective-permute-start | bytes 1572872 | tf_op jit(solution)/shard_map/ppermute | solution.py:272
  66.7 10.9 %collective-permute-start.11 = (f32[16,512]{1,0:T(8,128)S(1)}, f32[16,512]{1,0:T(8,128)S(1)}, u32[]{:S(2)}, u32[]{:S(2)}) collective-permute-start(f32[16,512]{1,0:T(8,128)S(1)} %low_sums.1.rest_1_.rest_0_), channel_id=1, source_target_pairs={{0,3},{1,2},{2,1},{3,0},{4,7},{5,6},{6,5},{7,4},{8,11},{9,10},{10,... | collective-permute-start | bytes 98312 | tf_op jit(solution)/shard_map/ppermute | solution.py:300
  66.8 15.7 %collective-permute-start.10 = (f32[16,512]{1,0:T(8,128)S(1)}, f32[16,512]{1,0:T(8,128)S(1)}, u32[]{:S(2)}, u32[]{:S(2)}) collective-permute-start(f32[16,512]{1,0:T(8,128)S(1)} %low_sums.1.rest_1_.rest_0_), channel_id=1, source_target_pairs={{0,2},{1,3},{2,0},{3,1},{4,6},{5,7},{6,4},{7,5},{8,10},{9,11},{10,... | collective-permute-start | bytes 98312 | tf_op jit(solution)/shard_map/ppermute | solution.py:300
  70.2 12.3 %collective-permute-start.9 = (f32[16,512]{1,0:T(8,128)S(1)}, f32[16,512]{1,0:T(8,128)S(1)}, u32[]{:S(2)}, u32[]{:S(2)}) collective-permute-start(f32[16,512]{1,0:T(8,128)S(1)} %low_sums.1.rest_1_.rest_0_), channel_id=1, source_target_pairs={{0,1},{1,0},{2,3},{3,2},{4,5},{5,4},{6,7},{7,6},{8,9},{9,8},{10,11... | collective-permute-start | bytes 98312 | tf_op jit(solution)/shard_map/ppermute | solution.py:300

commit v7 on v4

--- a/solution.py
+++ b/solution.py
@@ -13,79 +13,107 @@
 F32 = jnp.float32
 BF16 = jnp.bfloat16
 SMALL = pl.CostEstimate(flops=1000, bytes_accessed=1000, transcendentals=0)
-
-
-def product_kernel(tile, addends, afters, first_call, first_ref, rows_ref, weight_ref, *rest):
-    addend_refs, rest = rest[:addends], rest[addends + afters :]
-    if first_call:
-        ids_ref, out_ref, ids_out_ref, tiles_ref, tile_sems, held_ref, held_sem = rest
-    else:
-        out_ref, tiles_ref, tile_sems = rest
-    tiles = out_ref.shape[1] // tile
-    first = first_ref[0]
-
-    def weight_copy(j):
-        columns = pl.ds(pl.multiple_of(first + j * tile, 128), tile)
-        return pltpu.make_async_copy(
-            weight_ref.at[:, columns], tiles_ref.at[j], tile_sems.at[j]
-        )
-
-    if first_call:
-        rows_copy = pltpu.make_async_copy(rows_ref, held_ref, held_sem)
-        rows_copy.start()
-    for j in range(tiles):
-        weight_copy(j).start()
-    if first_call:
+LARGE = pl.CostEstimate(flops=10**11, bytes_accessed=4 * 10**8, transcendentals=0)
+
+
+def product_kernel(addends, with_ids, first_ref, rows_ref, weight_ref, *rest):
+    out_ref = rest[-1 - with_ids]
+    total = jnp.dot(rows_ref[...], weight_ref[...], preferred_element_type=F32)
+    for ref in rest[:addends]:
+        total = total + ref[...].astype(F32)
+    out_ref[...] = total.astype(out_ref.dtype)
+    if with_ids:
+        ids_ref, ids_out_ref = rest[addends], rest[-1]
         for s in range(ids_ref.shape[1]):
             ids_out_ref[0, s] = ids_ref[0, s]
-        rows_copy.wait()
-        rows_ref = held_ref
-    for j in range(tiles):
-        weight_copy(j).wait()
-        columns = slice(j * tile, (j + 1) * tile)
-        total = jnp.dot(rows_ref[...], tiles_ref[j], preferred_element_type=F32)
-        for ref in addend_refs:
-            total = total + ref[:, columns].astype(F32)
-        out_ref[:, columns] = total.astype(out_ref.dtype)
 
 
 def block_product(rows, weight, first, width, addends=(), after=(), ids=None):
     row_total, depth = rows.shape
     tile = min(256, width)
-    first_call = ids is not None
+    with_ids = ids is not None
     smem = pl.BlockSpec(memory_space=pltpu.SMEM)
-    vmem = pl.BlockSpec(memory_space=pltpu.VMEM)
     hbm = pl.BlockSpec(memory_space=pl.ANY)
-    out_specs, out_shape = [vmem], [jax.ShapeDtypeStruct((row_total, width), BF16)]
-    scratch = [
-        pltpu.VMEM((width // tile, depth, tile), BF16),
-        pltpu.SemaphoreType.DMA((width // tile,)),
-    ]
-    if first_call:
+    columns = pl.BlockSpec((row_total, tile), lambda j, t: (0, j))
+    out_specs, out_shape = [columns], [jax.ShapeDtypeStruct((row_total, width), BF16)]
+    if with_ids:
         out_specs.append(smem)
         out_shape.append(jax.ShapeDtypeStruct(ids.shape, ids.dtype))
-        scratch += [pltpu.VMEM((row_total, depth), BF16), pltpu.SemaphoreType.DMA]
     out = pl.pallas_call(
-        functools.partial(product_kernel, tile, len(addends), len(after), first_call),
-        in_specs=[smem, hbm if first_call else vmem, hbm]
-        + [vmem] * len(addends)
-        + [hbm] * len(after)
-        + [smem] * first_call,
-        out_specs=out_specs,
+        functools.partial(product_kernel, len(addends), with_ids),
+        grid_spec=pltpu.PrefetchScalarGridSpec(
+            num_scalar_prefetch=1,
+            grid=(width // tile,),
+            in_specs=[
+                pl.BlockSpec((row_total, depth), lambda j, t: (0, 0)),
+                pl.BlockSpec((depth, tile), lambda j, t: (0, t[0] + j)),
+            ]
+            + [columns] * len(addends)
+            + [smem] * with_ids
+            + [hbm] * len(after),
+            out_specs=out_specs,
+        ),
         out_shape=out_shape,
-        scratch_shapes=scratch,
         compiler_params=pltpu.CompilerParams(vmem_limit_bytes=VMEM_LIMIT),
         cost_estimate=SMALL,
         name="block_product",
-    )(first.reshape(1), rows, weight, *addends, *after, *([ids] if first_call else []))
-    return out if first_call else out[0]
+    )((first // tile).reshape(1), rows, weight, *addends, *([ids] if with_ids else []), *after)
+    return out if with_ids else out[0]
+
+
+def first_kernel(chunk, first_ref, rows_ref, weight_ref, out_ref, lhs_ref, rhs_ref, acc_ref, sems):
+    columns = pl.ds(pl.multiple_of(first_ref[0], 128), out_ref.shape[1])
+    chunks = lhs_ref.shape[0]
+
+    def copies(k):
+        part = pl.ds(k * chunk, chunk)
+        return (
+            pltpu.make_async_copy(rows_ref.at[:, part], lhs_ref.at[k], sems.at[0, k]),
+            pltpu.make_async_copy(weight_ref.at[part, columns], rhs_ref.at[k], sems.at[1, k]),
+        )
+
+    for k in range(chunks):
+        for copy in copies(k):
+            copy.start()
+    for k in range(chunks):
+        for copy in copies(k):
+            copy.wait()
+        part = jnp.dot(lhs_ref[k], rhs_ref[k], preferred_element_type=F32)
+        if k == 0:
+            acc_ref[...] = part
+        elif k < chunks - 1:
+            acc_ref[...] += part
+        else:
+            out_ref[...] = (acc_ref[...] + part).astype(out_ref.dtype)
+
+
+def first_product(rows, weight, first, width):
+    row_total, depth = rows.shape
+    chunk = min(512, depth // 2)
+    chunks = depth // chunk
+    hbm = pl.BlockSpec(memory_space=pltpu.HBM)
+    return pl.pallas_call(
+        functools.partial(first_kernel, chunk),
+        in_specs=[pl.BlockSpec(memory_space=pltpu.SMEM), hbm, hbm],
+        out_specs=pl.BlockSpec(memory_space=pltpu.VMEM),
+        out_shape=jax.ShapeDtypeStruct((row_total, width), BF16),
+        scratch_shapes=[
+            pltpu.VMEM((chunks, row_total, chunk), BF16),
+            pltpu.VMEM((chunks, chunk, width), BF16),
+            pltpu.VMEM((row_total, width), F32),
+            pltpu.SemaphoreType.DMA((2, chunks)),
+        ],
+        compiler_params=pltpu.CompilerParams(vmem_limit_bytes=VMEM_LIMIT),
+        cost_estimate=SMALL,
+        name="first_product",
+    )(first.reshape(1), rows, weight)
 
 
 def pick_kernel(peers, afters, me_ref, table_ref, lens_ref, *rest):
     ids_refs = rest[:peers]
     down_ref, up_ref = rest[peers : peers + 2]
     rest = rest[peers + 2 + afters :]
-    packs, (start_ref, end_ref, pick_ref, sem) = rest[:peers], rest[peers:]
+    packs, (start_ref, end_ref, pick_ref, count_ref, sem) = rest[:peers], rest[peers:]
     segs = lens_ref.shape[1]
     share, _, depth = down_ref.shape
     cols = up_ref.shape[2]
@@ -97,7 +125,9 @@
         end_ref[q] = 0
         return carry
 
-    lax.fori_loop(0, peers * CAP, clear, 0)
+    lax.fori_loop(0, peers * CAP, clear, 0, unroll=8)
+    for x in range(peers):
+        count_ref[x] = 0
 
     def copies(x, c, source):
         pack = packs[x].at[c]
@@ -118,28 +148,25 @@
 
             return count + mine.astype(jnp.int32)
 
-        lax.fori_loop(0, segs, choose, 0)
+        lax.fori_loop(0, segs, choose, 0, unroll=4)
         for c in range(CAP):
             for copy in copies(x, c, pick_ref[x * CAP + c]):
                 copy.start()
 
-    for x in range(peers):
-        owner = lax.bitwise_xor(me, jnp.int32(x))
-
-        def place(s, carry):
-            count, first = carry
-            local = table_ref[ids_refs[0][0, s]] - owner * share
-            theirs = jnp.logical_and(local >= 0, local < share)
-            last = first + lens_ref[0, s]
-
-            @pl.when(jnp.logical_and(theirs, count < CAP))
-            def _():
-                start_ref[x * CAP + count] = first
-                end_ref[x * CAP + count] = last
-
-            return count + theirs.astype(jnp.int32), last
-
-        lax.fori_loop(0, segs, place, (0, 0))
+    def place(s, first):
+        x = lax.bitwise_xor(table_ref[ids_refs[0][0, s]] // share, me)
+        count = count_ref[x]
+        last = first + lens_ref[0, s]
+
+        @pl.when(count < CAP)
+        def _():
+            start_ref[x * CAP + count] = first
+            end_ref[x * CAP + count] = last
+
+        count_ref[x] = count + 1
+        return last
+
+    lax.fori_loop(0, segs, place, 0, unroll=4)
 
     for x in range(peers):
         for c in range(CAP):
@@ -160,7 +187,11 @@
         out_specs=[vmem] * peers + [smem, smem],
         out_shape=[jax.ShapeDtypeStruct((CAP, rank, depth + cols), BF16)] * peers
         + [jax.ShapeDtypeStruct((peers * CAP,), jnp.int32)] * 2,
-        scratch_shapes=[pltpu.SMEM((peers * CAP,), jnp.int32), pltpu.SemaphoreType.DMA],
+        scratch_shapes=[
+            pltpu.SMEM((peers * CAP,), jnp.int32),
+            pltpu.SMEM((peers,), jnp.int32),
+            pltpu.SemaphoreType.DMA,
+        ],
         compiler_params=pltpu.CompilerParams(vmem_limit_bytes=VMEM_LIMIT),
         cost_estimate=SMALL,
         name="pick_adapters",
@@ -177,18 +208,14 @@
     row_total, depth = rows_ref.shape
     rank = out_ref.shape[0]
     place = lax.broadcasted_iota(jnp.int32, (rank, row_total), 1)
+    downs = jnp.concatenate([ref[...].reshape(CAP * rank, depth) for ref in down_refs], axis=0)
+    part = lax.dot_general(
+        downs, rows_ref[...], (((1,), (1,)), ((), ())), preferred_element_type=F32
+    )
     total = jnp.zeros((rank, row_total), F32)
-    for x, down_ref in enumerate(down_refs):
-        part = lax.dot_general(
-            down_ref[...].reshape(CAP * rank, depth),
-            rows_ref[...],
-            (((1,), (1,)), ((), ())),
-            preferred_element_type=F32,
-        )
-        for c in range(CAP):
-            q = x * CAP + c
-            member = jnp.logical_and(place >= start_ref[q], place < end_ref[q])
-            total = jnp.where(member, part[c * rank : (c + 1) * rank], total)
+    for q in range(peers * CAP):
+        member = jnp.logical_and(place >= start_ref[q], place < end_ref[q])
+        total = jnp.where(member, part[q * rank : (q + 1) * rank], total)
     out_ref[...] = total
 
 
@@ -264,7 +291,7 @@
     rest[-1][...] = total.astype(rest[-1].dtype)
 
 
-def finish(term, arrivals, piece, pieces, result):
+def finish(term, arrivals, piece, pieces, result, cost):
     row_total, width = term.shape
     height = min(row_total, 128)
     block = pl.BlockSpec((height, width), lambda i: (i, 0))
@@ -277,7 +304,7 @@
         out_shape=jax.ShapeDtypeStruct((row_total, width * pieces), BF16),
         input_output_aliases={1 + len(arrivals): 0} if held else {},
         compiler_params=pltpu.CompilerParams(vmem_limit_bytes=VMEM_LIMIT),
-        cost_estimate=SMALL,
+        cost_estimate=cost,
         name="finish",
     )(term, *arrivals, *held)
 
@@ -288,23 +315,33 @@
     width = cols // PIECES
     me_req = lax.axis_index("req").astype(jnp.int32)
     me = lax.axis_index("tp").astype(jnp.int32)
-    right = [(i, (i + 1) % tp_total) for i in range(tp_total)]
     steps = tp_total - 1
 
+    def move(value, piece):
+        pairs = []
+        for r in range(req_total):
+            way = 1 if (r + piece) % 2 == 0 else tp_total - 1
+            for i in range(tp_total):
+                pairs.append((r * tp_total + i, r * tp_total + (i + way) % tp_total))
+        return lax.ppermute(value, ("req", "tp"), pairs)
+
+    def start_of(back, piece):
+        behind = jnp.where(lax.rem(me_req + piece, 2) == 0, tp_total - back, back)
+        block = lax.rem(me + behind, tp_total)
+        return block * cols + piece * width
+
     def partial(back, piece, **options):
-        block = lax.rem(me + (tp_total - back), tp_total)
-        return block_product(rows, weight, block * cols + piece * width, width, **options)
-
-    moving, owns = [None] * PIECES, [None] * PIECES
-    last, ids = partial(1, 0, ids=ids)
-    moving[0] = lax.ppermute(last, "tp", right)
+        return block_product(rows, weight, start_of(back, piece), width, **options)
+
+    last = first_product(rows, weight, start_of(1, 0), width)
+    moving, owns = [move(last, 0)], []
+    for piece in range(1, PIECES):
+        last, ids = partial(1, piece, after=[last], ids=ids)
+        moving.append(move(last, piece))
 
     all_ids = [ids]
     for x in range(1, req_total):
         all_ids.append(lax.ppermute(ids, "req", [(i, i ^ x) for i in range(req_total)]))
-    for piece in range(1, PIECES):
-        last = partial(1, piece, after=[last])
-        moving[piece] = lax.ppermute(last, "tp", right)
     packs, starts, ends = pick_adapters(me_req, table, all_ids, lens, down, up, [last])
     for x in range(1, req_total):
         packs[x] = lax.ppermute(packs[x], "req", [(i, i ^ x) for i in range(req_total)])
@@ -320,14 +357,16 @@
                     lows.append(lax.ppermute(low, "tp", pairs))
                 last = low
             last = partial(1 + step, piece, addends=[moving[piece]], after=[last])
-            moving[piece] = lax.ppermute(last, "tp", right)
+            moving[piece] = move(last, piece)
             if step == 1:
-                last = owns[piece] = partial(0, piece, after=[last])
+                last = partial(0, piece, after=[last])
+                owns.append(last)
 
     terms = adapter_term(starts, ends, lows, owns, packs, [last])
     result = None
     for piece in range(PIECES):
-        result = finish(terms[piece], [moving[piece]], piece, PIECES, result)
+        cost = SMALL if piece == PIECES - 1 else LARGE
+        result = finish(terms[piece], [moving[piece]], piece, PIECES, result, cost)
     return result
 
 

time: 90 us -> 85.8 us (0.953)
  Pallas kernels: 49.2 us -> 37.8 us
  starting transfers between devices: 16 us -> 27.3 us
  waiting for transfers between devices: 22.1 us -> 18.5 us
    ppermute x3, waiting for transfers between devices: 15.6 us -> 0.01 us  [local(): lows.append(lax.ppermute(low, 'tp', pairs))]
    pallas_call x8, Pallas kernels: 36.6 us -> 24.8 us  [the longest x7 22.1 us: block_product(): pl.pallas_call(functools.partial(product_kernel, len(addends), with_ids),...]
    ppermute x6, starting transfers between devices: 6.91 us -> 15.9 us  [move(): return lax.ppermute(value, ('req', 'tp'), pairs)]
    ppermute x3, waiting for transfers between devices: 0.01 us -> 8.84 us  [local(): lax.ppermute(packs[x], 'req', [(i, i ^ x) for i in range(req_total)])]
    ppermute x6, waiting for transfers between devices: 4.4 us -> 7.4 us  [move(): return lax.ppermute(value, ('req', 'tp'), pairs)]
    ppermute x3, starting transfers between devices: 4.45 us -> 6.25 us  [local(): lows.append(lax.ppermute(low, 'tp', pairs))]
    pallas_call x2, Pallas kernels: 2.86 us -> 4.6 us  [finish(): pl.pallas_call(functools.partial(finish_kernel, len(arrivals)), grid=(row...]
    pallas_call x1, Pallas kernels: 3.9 us -> 2.25 us  [low_sums(): pl.pallas_call(functools.partial(low_kernel, len(packs)), grid=(1,), in_s...]
  transfers between devices with their start and end apart: 15 -> 15, of which waited for: 6 -> 4; matrix products, arithmetic and copies ran while one was open for 0% -> 0% of each run, Pallas kernels for 47% -> 39%
where the time goes in v7:
time: 85.8 us; the launch traced here: 85.4 us
  Pallas kernels  37.8 us (44%)
  starting transfers between devices  27.3 us (32%)
  waiting for transfers between devices  18.5 us (22%)
  local copies, waits for them, and re-layouts  1.62 us (2%)
    pallas_call x7, Pallas kernels, block_product(): pl.pallas_call(functools.partial(product_kernel, len(addends), with_ids),...  22.1 us
    ppermute x6, starting transfers between devices, move(): return lax.ppermute(value, ('req', 'tp'), pairs)  15.9 us
    ppermute x3, waiting for transfers between devices, local(): lax.ppermute(packs[x], 'req', [(i, i ^ x) for i in range(req_total)])  8.84 us
    ppermute x6, waiting for transfers between devices, move(): return lax.ppermute(value, ('req', 'tp'), pairs)  7.4 us
    ppermute x3, starting transfers between devices, local(): lows.append(lax.ppermute(low, 'tp', pairs))  6.25 us
    pallas_call x2, Pallas kernels, finish(): pl.pallas_call(functools.partial(finish_kernel, len(arrivals)), grid=(row...  4.6 us
    pallas_call x1, Pallas kernels, pick_adapters(): pl.pallas_call(functools.partial(pick_kernel, peers, len(after)), in_spec...  4.32 us
    ppermute x3, starting transfers between devices, local(): lax.ppermute(ids, 'req', [(i, i ^ x) for i in range(req_total)])  3.28 us
  transfers between devices with their start and end apart: 15, of which 4 were waited for; matrix products, arithmetic and copies ran while one was open for 0% of the time, Pallas kernels for 39%

profile of v7, /device:TPU:0, one launch (start us, length us, event | category | flops | bytes accessed | tf_op | source)
XLA Modules:
  0.0 85.4 jit_solution(15245575670412671727)
XLA Ops:
  0.0 0.0 copy-start
  0.0 1.6 %copy-done = bf16[512,2048]{1,0:T(8,128)(2,1)S(1)} copy-done((bf16[512,2048]{1,0:T(8,128)(2,1)S(1)}, bf16[512,2048]{1,0:T(8,128)(2,1)}, u32[]{:S(2)}) %copy-start) | copy-done | bytes 2097176
  1.6 0.0 copy-start.1
  1.6 0.0 copy-start.6
  1.6 2.7 %first_product.1.rest_1_ = bf16[512,512]{1,0:T(8,128)(2,1)S(1)} custom-call(s32[1]{0:T(128)} %bitcast.2.first_ref, bf16[512,2048]{1,0:T(8,128)(2,1)S(1)} %copy-done, bf16[2048,4096]{1,0:T(8,128)(2,1)} %weight_ref.15), custom_call_target="tpu_custom_call" | custom-call | flops 1000 | bytes 1000 | tf_op jit(solution)/shard_map/first_product/pallas_call | solution.py:95
  4.3 3.1 %collective-permute-start.6 = (bf16[512,512]{1,0:T(8,128)(2,1)S(1)}, bf16[512,512]{1,0:T(8,128)(2,1)}, u32[]{:S(2)}, u32[]{:S(2)}) collective-permute-start(bf16[512,512]{1,0:T(8,128)(2,1)S(1)} %first_product.1.rest_1_), channel_id=1, source_target_pairs={{0,1},{1,2},{2,3},{3,0},{4,7},{5,4},{6,5},{7,6},{8,9},{9,10},{10,1... | collective-permute-start | bytes 1572872 | tf_op jit(solution)/shard_map/ppermute | solution.py:326
  7.4 0.0 copy-done.1
  7.4 0.0 copy-done.6
  7.4 0.0 copy-start.5
  7.4 0.0 copy-start.7
  7.4 3.4 %block_product.7 = (bf16[512,512]{1,0:T(8,128)(2,1)S(1)}, s32[1,12]{1,0:T(1,128)S(1)}) custom-call(s32[1]{0:T(128)} %bitcast.1.first_ref, bf16[512,2048]{1,0:T(8,128)(2,1)S(1)} %copy-done.1, bf16[2048,4096]{1,0:T(8,128)(2,1)} %weight_ref.15, s32[1,12]{1,0:T(1,128)S(1)} %copy-done.6, bf16[512,512]{1,0:T(8,128)(2,1)S(1)} %first_product.1.rest_1_), custom_call_target="tpu_custom_call" | custom-call | flops 1000 | bytes 1000 | tf_op jit(solution)/shard_map/block_product/pallas_call | solution.py:42
  10.8 2.8 %collective-permute-start.2 = (s32[1,12]{1,0:T(1,128)S(1)}, s32[1,12]{1,0:T(1,128)S(1)}, u32[]{:S(2)}, u32[]{:S(2)}) collective-permute-start(s32[1,12]{1,0:T(1,128)S(1)} %get-tuple-element.15.rest_0_), channel_id=1, source_target_pairs={{0,12},{4,8},{8,4},{12,0},{1,13},{5,9},{9,5},{13,1},{2,14},{6,10},... | collective-permute-start | bytes 152 | tf_op jit(solution)/shard_map/ppermute | solution.py:344
  13.6 0.5 collective-permute-start.1
  14.1 0.0 collective-permute-start
  14.1 0.8 collective-permute-start.8
  14.8 0.0 collective-permute-done.2.rest_3_
  14.8 2.2 %collective-permute-done.1.rest_2_ = s32[1,12]{1,0:T(1,128)S(1)} collective-permute-done((s32[1,12]{1,0:T(1,128)S(1)}, s32[1,12]{1,0:T(1,128)S(1)}, u32[]{:S(2)}, u32[]{:S(2)}) %collective-permute-start.1) | collective-permute-done | bytes 80 | tf_op jit(solution)/shard_map/ppermute | solution.py:344
  17.1 0.0 collective-permute-done.rest_1_
  17.1 0.0 copy-done.5
  17.1 0.0 copy-done.7
  17.1 4.3 %pick_adapters.1 = (bf16[6,16,3072]{2,1,0:T(8,128)(2,1)S(1)}, bf16[6,16,3072]{2,1,0:T(8,128)(2,1)}, bf16[6,16,3072]{2,1,0:T(8,128)(2,1)}, bf16[6,16,3072]{2,1,0:...) custom-call(s32[1]{0:T(128)} %bitcast.me_ref, s32[512]{0:T(512)S(1)} %copy-done.5, s32[1,12]{1,0:T(1,128)S(1)} %copy-done.7, ...), custom_call_target="tpu_custom_call" | custom-call | flops 1000 | bytes 1000 | tf_op jit(solution)/shard_map/pick_adapters/pallas_call | solution.py:184
  21.4 0.0 copy-start.2
  21.4 0.9 %collective-permute-done.6.rest_0_ = bf16[512,512]{1,0:T(8,128)(2,1)} collective-permute-done((bf16[512,512]{1,0:T(8,128)(2,1)S(1)}, bf16[512,512]{1,0:T(8,128)(2,1)}, u32[]{:S(2)}, u32[]{:S(2)}) %collective-permute-start.6) | collective-permute-done | bytes 524320 | tf_op jit(solution)/shard_map/ppermute | solution.py:326
  22.4 3.4 %block_product.8.rest_0_ = bf16[512,512]{1,0:T(8,128)(2,1)} custom-call(s32[1]{0:T(128)} %bitcast.4.first_ref, bf16[512,2048]{1,0:T(8,128)(2,1)S(1)} %copy-done.1, bf16[2048,4096]{1,0:T(8,128)(2,1)} %weight_ref.15, bf16[512,512]{1,0:T(8,128)(2,1)} %collective-permute-done.6.rest_0_, s32[24]{0:T(128)S(1)} %get-tuple-element.17.rest_1_.start_ref), custom_call_target="tpu_custom_call" | custom-call | flops 1000 | bytes 1000 | tf_op jit(solution)/shard_map/block_product/pallas_call | solution.py:42
  25.8 0.0 copy-done.2
  25.8 3.6 %collective-permute-start.7 = (bf16[512,512]{1,0:T(8,128)(2,1)}, bf16[512,512]{1,0:T(8,128)(2,1)}, u32[]{:S(2)}, u32[]{:S(2)}) collective-permute-start(bf16[512,512]{1,0:T(8,128)(2,1)} %block_product.8.rest_0_), channel_id=1, source_target_pairs={{0,1},{1,2},{2,3},{3,0},{4,7},{5,4},{6,5},{7,6},{8,9},{9,10},{10,1... | collective-permute-start | bytes 1572872 | tf_op jit(solution)/shard_map/ppermute | solution.py:326
  29.4 0.0 collective-permute-start.3
  29.4 1.8 %collective-permute-start.4 = (bf16[6,16,3072]{2,1,0:T(8,128)(2,1)}, bf16[6,16,3072]{2,1,0:T(8,128)(2,1)}, u32[]{:S(2)}, u32[]{:S(2)}) collective-permute-start(bf16[6,16,3072]{2,1,0:T(8,128)(2,1)} %get-tuple-element.21), channel_id=1, source_target_pairs={{0,8},{4,12},{8,0},{12,4},{1,9},{5,13},{9,1},{13,5},{2,10},{6,14},... | collective-permute-start | bytes 1769480 | tf_op jit(solution)/shard_map/ppermute | solution.py:347
  31.2 0.1 collective-permute-start.5
  31.3 2.7 %block_product.9.rest_1_.rest_4_ = bf16[512,512]{1,0:T(8,128)(2,1)S(1)} custom-call(s32[1]{0:T(128)} %bitcast.7.first_ref, bf16[512,2048]{1,0:T(8,128)(2,1)S(1)} %copy-done.1, bf16[2048,4096]{1,0:T(8,128)(2,1)} %weight_ref.15, bf16[512,512]{1,0:T(8,128)(2,1)} %block_product.8.rest_0_), custom_call_target="tpu_custom_call" | custom-call | flops 1000 | bytes 1000 | tf_op jit(solution)/shard_map/block_product/pallas_call | solution.py:42
  34.0 0.0 collective-permute-done.8.rest_0_
  34.0 3.5 %block_product.10.rest_0_ = bf16[512,512]{1,0:T(8,128)(2,1)} custom-call(s32[1]{0:T(128)} %bitcast.6.first_ref, bf16[512,2048]{1,0:T(8,128)(2,1)S(1)} %copy-done.1, bf16[2048,4096]{1,0:T(8,128)(2,1)} %weight_ref.15, bf16[512,512]{1,0:T(8,128)(2,1)} %collective-permute-done.8.rest_0_, bf16[512,512]{1,0:T(8,128)(2,1)S(1)} %block_product.9.rest_1_.rest_4_), custom_call_target="tpu_custom_call" | custom-call | flops 1000 | bytes 1000 | tf_op jit(solution)/shard_map/block_product/pallas_call | solution.py:42
  37.5 5.1 %collective-permute-start.12 = (bf16[512,512]{1,0:T(8,128)(2,1)}, bf16[512,512]{1,0:T(8,128)(2,1)}, u32[]{:S(2)}, u32[]{:S(2)}) collective-permute-start(bf16[512,512]{1,0:T(8,128)(2,1)} %block_product.10.rest_0_), channel_id=1, source_target_pairs={{0,3},{1,0},{2,1},{3,2},{4,5},{5,6},{6,7},{7,4},{8,11},{9,8},{10,9... | collective-permute-start | bytes 1572872 | tf_op jit(solution)/shard_map/ppermute | solution.py:326
  42.7 2.7 %block_product.11.rest_1_.rest_5_ = bf16[512,512]{1,0:T(8,128)(2,1)S(1)} custom-call(s32[1]{0:T(128)} %bitcast.5.first_ref, bf16[512,2048]{1,0:T(8,128)(2,1)S(1)} %copy-done.1, bf16[2048,4096]{1,0:T(8,128)(2,1)} %weight_ref.15, bf16[512,512]{1,0:T(8,128)(2,1)} %block_product.10.rest_0_), custom_call_target="tpu_custom_call" | custom-call | flops 1000 | bytes 1000 | tf_op jit(solution)/shard_map/block_product/pallas_call | solution.py:42
  45.4 0.0 collective-permute-done.7.rest_0_
  45.4 0.0 copy-start.3
  45.4 3.5 %block_product.12.rest_4_ = bf16[512,512]{1,0:T(8,128)(2,1)} custom-call(s32[1]{0:T(128)} %bitcast.3.first_ref, bf16[512,2048]{1,0:T(8,128)(2,1)S(1)} %copy-done.1, bf16[2048,4096]{1,0:T(8,128)(2,1)} %weight_ref.15, bf16[512,512]{1,0:T(8,128)(2,1)} %collective-permute-done.7.rest_0_, bf16[512,512]{1,0:T(8,128)(2,1)S(1)} %block_product.11.rest_1_.rest_5_), custom_call_target="tpu_custom_call" | custom-call | flops 1000 | bytes 1000 | tf_op jit(solution)/shard_map/block_product/pallas_call | solution.py:42
  48.9 0.0 collective-permute-start.14
  48.9 0.0 collective-permute-done.3.rest_1_.rest_7_
  48.9 0.0 collective-permute-done.4.rest_2_.rest_8_
  48.9 8.8 %collective-permute-done.5.rest_3_.rest_9_ = bf16[6,16,3072]{2,1,0:T(8,128)(2,1)} collective-permute-done((bf16[6,16,3072]{2,1,0:T(8,128)(2,1)}, bf16[6,16,3072]{2,1,0:T(8,128)(2,1)}, u32[]{:S(2)}, u32[]{:S(2)}) %collective-permute-start.5) | collective-permute-done | bytes 589856 | tf_op jit(solution)/shard_map/ppermute | solution.py:347
  57.8 0.0 copy-done.3
  57.8 2.3 %low_sums.1.rest_1_.rest_0_ = f32[16,512]{1,0:T(8,128)S(1)} custom-call(s32[24]{0:T(128)S(1)} %get-tuple-element.17.rest_1_.start_ref, s32[24]{0:T(128)S(1)} %get-tuple-element.18.end_ref, bf16[512,2048]{1,0:T(8,128)(2,1)S(1)} %copy-done.1, bf16[6,16,3072]{2,1,0:T(8,128)(2,1)S(1)} %copy-done.3, bf16[6,16,3072]{2,1,0:T(8,128)(2,1)} %collective-permute-done.3.rest_1_.rest_7_, ...), custom_call_target="tpu_custom_call" | custom-call | flops 1000 | bytes 1000 | tf_op jit(solution)/shard_map/low_sums/pallas_call | solution.py:226
  60.0 5.1 %collective-permute-start.11 = (f32[16,512]{1,0:T(8,128)S(1)}, f32[16,512]{1,0:T(8,128)S(1)}, u32[]{:S(2)}, u32[]{:S(2)}) collective-permute-start(f32[16,512]{1,0:T(8,128)S(1)} %low_sums.1.rest_1_.rest_0_), channel_id=1, source_target_pairs={{0,3},{1,2},{2,1},{3,0},{4,7},{5,6},{6,5},{7,4},{8,11},{9,10},{10,... | collective-permute-start | bytes 98312 | tf_op jit(solution)/shard_map/ppermute | solution.py:357
  65.1 0.7 collective-permute-start.10
  65.8 0.5 collective-permute-start.9
  66.3 0.0 collective-permute-done.12.rest_0_
  66.3 0.0 copy-start.4
  66.3 2.8 %block_product.13.rest_10_ = bf16[512,512]{1,0:T(8,128)(2,1)S(1)} custom-call(s32[1]{0:T(128)} %bitcast.8.first_ref, bf16[512,2048]{1,0:T(8,128)(2,1)S(1)} %copy-done.1, bf16[2048,4096]{1,0:T(8,128)(2,1)} %weight_ref.15, bf16[512,512]{1,0:T(8,128)(2,1)} %collective-permute-done.12.rest_0_, f32[16,512]{1,0:T(8,128)S(1)} %low_sums.1.rest_1_.rest_0_), custom_call_target="tpu_custom_call" | custom-call | flops 1000 | bytes 1000 | tf_op jit(solution)/shard_map/block_product/pallas_call | solution.py:42
  69.1 3.3 %collective-permute-start.13 = (bf16[512,512]{1,0:T(8,128)(2,1)S(1)}, bf16[512,512]{1,0:T(8,128)(2,1)S(1)}, u32[]{:S(2)}, u32[]{:S(2)}) collective-permute-start(bf16[512,512]{1,0:T(8,128)(2,1)S(1)} %block_product.13.rest_10_), channel_id=1, source_target_pairs={{0,3},{1,0},{2,1},{3,2},{4,5},{5,6},{6,7},{7,4},{8,11},{9,8},{10,9... | collective-permute-start | bytes 1572872 | tf_op jit(solution)/shard_map/ppermute | solution.py:326
  72.4 0.0 collective-permute-done.11.rest_3_
  72.4 0.0 collective-permute-done.10.rest_2_
  72.4 0.0 collective-permute-done.9.rest_1_
  72.4 0.0 copy-done.4
  72.4 1.9 %adapter_term.1 = (f32[512,512]{1,0:T(8,128)S(1)}, f32[512,512]{1,0:T(8,128)S(1)}) custom-call(s32[24]{0:T(128)S(1)} %get-tuple-element.17.rest_1_.start_ref, s32[24]{0:T(128)S(1)} %get-tuple-element.18.end_ref, f32[16,512]{1,0:T(8,128)S(1)} %low_sums.1.rest_1_.rest_0_, f32[16,512]{1,0:T(8,128)S(1)} %collective-permute-done.9.rest_1_, ...), custom_call_target="tpu_custom_call" | custom-call | flops 1000 | bytes 1000 | tf_op jit(solution)/shard_map/adapter_term/pallas_call | solution.py:272
  74.3 0.0 collective-permute-done.14.rest_0_
  74.3 3.2 %finish.2.rest_1_ = bf16[512,1024]{1,0:T(8,128)(2,1)} custom-call(f32[512,512]{1,0:T(8,128)S(1)} %get-tuple-element.24.term_ref, bf16[512,512]{1,0:T(8,128)(2,1)} %collective-permute-done.14.rest_0_), custom_call_target="tpu_custom_call" | custom-call | flops 99999997952 | bytes 400000000 | tf_op jit(solution)/shard_map/finish/pallas_call | solution.py:299
  77.5 6.4 %collective-permute-done.13.rest_0_ = bf16[512,512]{1,0:T(8,128)(2,1)S(1)} collective-permute-done((bf16[512,512]{1,0:T(8,128)(2,1)S(1)}, bf16[512,512]{1,0:T(8,128)(2,1)S(1)}, u32[]{:S(2)}, u32[]{:S(2)}) %collective-permute-start.13) | collective-permute-done | bytes 524320 | tf_op jit(solution)/shard_map/ppermute | solution.py:326
  84.0 1.4 %finish.3 = bf16[512,1024]{1,0:T(8,128)(2,1)} custom-call(f32[512,512]{1,0:T(8,128)S(1)} %get-tuple-element.23.term_ref, bf16[512,512]{1,0:T(8,128)(2,1)S(1)} %collective-permute-done.13.rest_0_, bf16[512,1024]{1,0:T(8,128)(2,1)} %finish.2.rest_1_), custom_call_target="tpu_custom_call", output_to_operand_aliasing={{}: (2, {})} | custom-call | flops 1000 | bytes 1000 | tf_op jit(solution)/shard_map/finish/pallas_call | solution.py:299
Async XLA Ops:
  0.0 1.6 %copy-start = (bf16[512,2048]{1,0:T(8,128)(2,1)S(1)}, bf16[512,2048]{1,0:T(8,128)(2,1)}, u32[]{:S(2)}) copy-start(bf16[512,2048]{1,0:T(8,128)(2,1)} %rows_ref.17) | copy-start | bytes 6291460
  1.6 5.8 %copy-start.1 = (bf16[512,2048]{1,0:T(8,128)(2,1)S(1)}, bf16[512,2048]{1,0:T(8,128)(2,1)}, u32[]{:S(2)}) copy-start(bf16[512,2048]{1,0:T(8,128)(2,1)} %rows_ref.17) | copy-start | bytes 6291460
  1.6 5.8 %copy-start.6 = (s32[1,12]{1,0:T(1,128)S(1)}, s32[1,12]{1,0:T(1,128)}, u32[]{:S(2)}) copy-start(s32[1,12]{1,0:T(1,128)} %rest_0_.1) | copy-start | bytes 148
  4.3 18.0 %collective-permute-start.6 = (bf16[512,512]{1,0:T(8,128)(2,1)S(1)}, bf16[512,512]{1,0:T(8,128)(2,1)}, u32[]{:S(2)}, u32[]{:S(2)}) collective-permute-start(bf16[512,512]{1,0:T(8,128)(2,1)S(1)} %first_product.1.rest_1_), channel_id=1, source_target_pairs={{0,1},{1,2},{2,3},{3,0},{4,7},{5,4},{6,5},{7,6},{8,9},{9,10},{10,1... | collective-permute-start | bytes 1572872 | tf_op jit(solution)/shard_map/ppermute | solution.py:326
  7.4 9.7 %copy-start.5 = (s32[512]{0:T(512)S(1)}, s32[512]{0:T(512)}, u32[]{:S(2)}) copy-start(s32[512]{0:T(512)} %table_ref.1) | copy-start | bytes 6148
  7.4 9.7 %copy-start.7 = (s32[1,12]{1,0:T(1,128)S(1)}, s32[1,12]{1,0:T(1,128)}, u32[]{:S(2)}) copy-start(s32[1,12]{1,0:T(1,128)} %lens_ref.1) | copy-start | bytes 148
  10.8 4.1 %collective-permute-start.2 = (s32[1,12]{1,0:T(1,128)S(1)}, s32[1,12]{1,0:T(1,128)S(1)}, u32[]{:S(2)}, u32[]{:S(2)}) collective-permute-start(s32[1,12]{1,0:T(1,128)S(1)} %get-tuple-element.15.rest_0_), channel_id=1, source_target_pairs={{0,12},{4,8},{8,4},{12,0},{1,13},{5,9},{9,5},{13,1},{2,14},{6,10},... | collective-permute-start | bytes 152 | tf_op jit(solution)/shard_map/ppermute | solution.py:344
  13.6 3.5 %collective-permute-start.1 = (s32[1,12]{1,0:T(1,128)S(1)}, s32[1,12]{1,0:T(1,128)S(1)}, u32[]{:S(2)}, u32[]{:S(2)}) collective-permute-start(s32[1,12]{1,0:T(1,128)S(1)} %get-tuple-element.15.rest_0_), channel_id=1, source_target_pairs={{0,8},{4,12},{8,0},{12,4},{1,9},{5,13},{9,1},{13,5},{2,10},{6,14},... | collective-permute-start | bytes 152 | tf_op jit(solution)/shard_map/ppermute | solution.py:344
  14.1 3.0 %collective-permute-start = (s32[1,12]{1,0:T(1,128)S(1)}, s32[1,12]{1,0:T(1,128)S(1)}, u32[]{:S(2)}, u32[]{:S(2)}) collective-permute-start(s32[1,12]{1,0:T(1,128)S(1)} %get-tuple-element.15.rest_0_), channel_id=1, source_target_pairs={{0,4},{4,0},{8,12},{12,8},{1,5},{5,1},{9,13},{13,9},{2,6},{6,2},{1... | collective-permute-start | bytes 152 | tf_op jit(solution)/shard_map/ppermute | solution.py:344
  14.1 20.0 %collective-permute-start.8 = (bf16[512,512]{1,0:T(8,128)(2,1)S(1)}, bf16[512,512]{1,0:T(8,128)(2,1)}, u32[]{:S(2)}, u32[]{:S(2)}) collective-permute-start(bf16[512,512]{1,0:T(8,128)(2,1)S(1)} %get-tuple-element.16.rest_6_), channel_id=1, source_target_pairs={{0,3},{1,0},{2,1},{3,2},{4,5},{5,6},{6,7},{7,4},{8,11},{9,8},{10,9... | collective-permute-start | bytes 1572872 | tf_op jit(solution)/shard_map/ppermute | solution.py:326
  21.4 4.4 %copy-start.2 = (bf16[6,16,3072]{2,1,0:T(8,128)(2,1)}, bf16[6,16,3072]{2,1,0:T(8,128)(2,1)S(1)}, u32[]{:S(2)}) copy-start(bf16[6,16,3072]{2,1,0:T(8,128)(2,1)S(1)} %get-tuple-element.19.rest_0_.rest_6_) | copy-start | bytes 1769476
  25.8 19.5 %collective-permute-start.7 = (bf16[512,512]{1,0:T(8,128)(2,1)}, bf16[512,512]{1,0:T(8,128)(2,1)}, u32[]{:S(2)}, u32[]{:S(2)}) collective-permute-start(bf16[512,512]{1,0:T(8,128)(2,1)} %block_product.8.rest_0_), channel_id=1, source_target_pairs={{0,1},{1,2},{2,3},{3,0},{4,7},{5,4},{6,5},{7,6},{8,9},{9,10},{10,1... | collective-permute-start | bytes 1572872 | tf_op jit(solution)/shard_map/ppermute | solution.py:326
  29.4 19.5 %collective-permute-start.3 = (bf16[6,16,3072]{2,1,0:T(8,128)(2,1)}, bf16[6,16,3072]{2,1,0:T(8,128)(2,1)}, u32[]{:S(2)}, u32[]{:S(2)}) collective-permute-start(bf16[6,16,3072]{2,1,0:T(8,128)(2,1)} %get-tuple-element.20), channel_id=1, source_target_pairs={{0,4},{4,0},{8,12},{12,8},{1,5},{5,1},{9,13},{13,9},{2,6},{6,2},{1... | collective-permute-start | bytes 1769480 | tf_op jit(solution)/shard_map/ppermute | solution.py:347
  29.4 19.5 %collective-permute-start.4 = (bf16[6,16,3072]{2,1,0:T(8,128)(2,1)}, bf16[6,16,3072]{2,1,0:T(8,128)(2,1)}, u32[]{:S(2)}, u32[]{:S(2)}) collective-permute-start(bf16[6,16,3072]{2,1,0:T(8,128)(2,1)} %get-tuple-element.21), channel_id=1, source_target_pairs={{0,8},{4,12},{8,0},{12,4},{1,9},{5,13},{9,1},{13,5},{2,10},{6,14},... | collective-permute-start | bytes 1769480 | tf_op jit(solution)/shard_map/ppermute | solution.py:347
  31.2 26.6 %collective-permute-start.5 = (bf16[6,16,3072]{2,1,0:T(8,128)(2,1)}, bf16[6,16,3072]{2,1,0:T(8,128)(2,1)}, u32[]{:S(2)}, u32[]{:S(2)}) collective-permute-start(bf16[6,16,3072]{2,1,0:T(8,128)(2,1)} %get-tuple-element.22), channel_id=1, source_target_pairs={{0,12},{4,8},{8,4},{12,0},{1,13},{5,9},{9,5},{13,1},{2,14},{6,10},... | collective-permute-start | bytes 1769480 | tf_op jit(solution)/shard_map/ppermute | solution.py:347
  37.5 28.7 %collective-permute-start.12 = (bf16[512,512]{1,0:T(8,128)(2,1)}, bf16[512,512]{1,0:T(8,128)(2,1)}, u32[]{:S(2)}, u32[]{:S(2)}) collective-permute-start(bf16[512,512]{1,0:T(8,128)(2,1)} %block_product.10.rest_0_), channel_id=1, source_target_pairs={{0,3},{1,0},{2,1},{3,2},{4,5},{5,6},{6,7},{7,4},{8,11},{9,8},{10,9... | collective-permute-start | bytes 1572872 | tf_op jit(solution)/shard_map/ppermute | solution.py:326
  45.4 12.4 %copy-start.3 = (bf16[6,16,3072]{2,1,0:T(8,128)(2,1)S(1)}, bf16[6,16,3072]{2,1,0:T(8,128)(2,1)}, u32[]{:S(2)}) copy-start(bf16[6,16,3072]{2,1,0:T(8,128)(2,1)} %copy-done.2) | copy-start | bytes 1769476
  48.9 25.4 %collective-permute-start.14 = (bf16[512,512]{1,0:T(8,128)(2,1)}, bf16[512,512]{1,0:T(8,128)(2,1)}, u32[]{:S(2)}, u32[]{:S(2)}) collective-permute-start(bf16[512,512]{1,0:T(8,128)(2,1)} %block_product.12.rest_4_), channel_id=1, source_target_pairs={{0,1},{1,2},{2,3},{3,0},{4,7},{5,4},{6,5},{7,6},{8,9},{9,10},{10,1... | collective-permute-start | bytes 1572872 | tf_op jit(solution)/shard_map/ppermute | solution.py:326
  60.0 12.4 %collective-permute-start.11 = (f32[16,512]{1,0:T(8,128)S(1)}, f32[16,512]{1,0:T(8,128)S(1)}, u32[]{:S(2)}, u32[]{:S(2)}) collective-permute-start(f32[16,512]{1,0:T(8,128)S(1)} %low_sums.1.rest_1_.rest_0_), channel_id=1, source_target_pairs={{0,3},{1,2},{2,1},{3,0},{4,7},{5,6},{6,5},{7,4},{8,11},{9,10},{10,... | collective-permute-start | bytes 98312 | tf_op jit(solution)/shard_map/ppermute | solution.py:357
  65.1 7.3 %collective-permute-start.10 = (f32[16,512]{1,0:T(8,128)S(1)}, f32[16,512]{1,0:T(8,128)S(1)}, u32[]{:S(2)}, u32[]{:S(2)}) collective-permute-start(f32[16,512]{1,0:T(8,128)S(1)} %low_sums.1.rest_1_.rest_0_), channel_id=1, source_target_pairs={{0,2},{1,3},{2,0},{3,1},{4,6},{5,7},{6,4},{7,5},{8,10},{9,11},{10,... | collective-permute-start | bytes 98312 | tf_op jit(solution)/shard_map/ppermute | solution.py:357
  65.8 6.6 %collective-permute-start.9 = (f32[16,512]{1,0:T(8,128)S(1)}, f32[16,512]{1,0:T(8,128)S(1)}, u32[]{:S(2)}, u32[]{:S(2)}) collective-permute-start(f32[16,512]{1,0:T(8,128)S(1)} %low_sums.1.rest_1_.rest_0_), channel_id=1, source_target_pairs={{0,1},{1,0},{2,3},{3,2},{4,5},{5,4},{6,7},{7,6},{8,9},{9,8},{10,11... | collective-permute-start | bytes 98312 | tf_op jit(solution)/shard_map/ppermute | solution.py:357
  66.3 6.2 %copy-start.4 = (bf16[6,16,3072]{2,1,0:T(8,128)(2,1)S(1)}, bf16[6,16,3072]{2,1,0:T(8,128)(2,1)}, u32[]{:S(2)}) copy-start(bf16[6,16,3072]{2,1,0:T(8,128)(2,1)} %copy-done.2) | copy-start | bytes 1769476
  69.1 14.9 %collective-permute-start.13 = (bf16[512,512]{1,0:T(8,128)(2,1)S(1)}, bf16[512,512]{1,0:T(8,128)(2,1)S(1)}, u32[]{:S(2)}, u32[]{:S(2)}) collective-permute-start(bf16[512,512]{1,0:T(8,128)(2,1)S(1)} %block_product.13.rest_10_), channel_id=1, source_target_pairs={{0,3},{1,0},{2,1},{3,2},{4,5},{5,6},{6,7},{7,4},{8,11},{9,8},{10,9... | collective-permute-start | bytes 1572872 | tf_op jit(solution)/shard_map/ppermute | solution.py:326

commit v8 on v7

--- a/solution.py
+++ b/solution.py
@@ -13,7 +13,7 @@
 F32 = jnp.float32
 BF16 = jnp.bfloat16
 SMALL = pl.CostEstimate(flops=1000, bytes_accessed=1000, transcendentals=0)
-LARGE = pl.CostEstimate(flops=10**11, bytes_accessed=4 * 10**8, transcendentals=0)
+LARGE = pl.CostEstimate(flops=2 * 10**10, bytes_accessed=6 * 10**7, transcendentals=0)
 
 
 def product_kernel(addends, with_ids, first_ref, rows_ref, weight_ref, *rest):
@@ -28,7 +28,7 @@
             ids_out_ref[0, s] = ids_ref[0, s]
 
 
-def block_product(rows, weight, first, width, addends=(), after=(), ids=None):
+def block_product(rows, weight, first, width, addends=(), after=(), ids=None, cost=SMALL):
     row_total, depth = rows.shape
     tile = min(256, width)
     with_ids = ids is not None
@@ -55,7 +55,7 @@
         ),
         out_shape=out_shape,
         compiler_params=pltpu.CompilerParams(vmem_limit_bytes=VMEM_LIMIT),
-        cost_estimate=SMALL,
+        cost_estimate=cost,
         name="block_product",
     )((first // tile).reshape(1), rows, weight, *addends, *([ids] if with_ids else []), *after)
     return out if with_ids else out[0]
@@ -359,7 +359,7 @@
             last = partial(1 + step, piece, addends=[moving[piece]], after=[last])
             moving[piece] = move(last, piece)
             if step == 1:
-                last = partial(0, piece, after=[last])
+                last = partial(0, piece, after=[last], cost=LARGE)
                 owns.append(last)
 
     terms = adapter_term(starts, ends, lows, owns, packs, [last])

time: 85.8 us -> 83.1 us (0.969)
  waiting for transfers between devices: 18.5 us -> 12.1 us
  starting transfers between devices: 27.3 us -> 31.4 us
  Pallas kernels: 37.8 us -> 36.5 us
    ppermute x3, waiting for transfers between devices: 8.84 us -> 0.01 us  [local(): lax.ppermute(packs[x], 'req', [(i, i ^ x) for i in range(req_total)])]
    ppermute x3, waiting for transfers between devices: 0.01 us -> 4.17 us  [local(): lows.append(lax.ppermute(low, 'tp', pairs))]
    ppermute x6, starting transfers between devices: 15.9 us -> 18.5 us  [move(): return lax.ppermute(value, ('req', 'tp'), pairs)]
    ppermute x6, waiting for transfers between devices: 7.4 us -> 5.62 us  [move(): return lax.ppermute(value, ('req', 'tp'), pairs)]
    ppermute x3, starting transfers between devices: 6.25 us -> 7.78 us  [local(): lows.append(lax.ppermute(low, 'tp', pairs))]
    unnamed x16 -> x26, local copies, waits for them, and re-layouts: 1.62 us -> 2.44 us
  transfers between devices with their start and end apart: 15 -> 15, of which waited for: 4 -> 5; matrix products, arithmetic and copies ran while one was open for 0% -> 0% of each run, Pallas kernels for 39% -> 38%
where the time goes in v8:
time: 83.1 us; the launch traced here: 82.6 us
  Pallas kernels  36.5 us (44%)
  starting transfers between devices  31.4 us (38%)
  waiting for transfers between devices  12.1 us (15%)
  local copies, waits for them, and re-layouts  2.44 us (3%)
    pallas_call x7, Pallas kernels, block_product(): pl.pallas_call(functools.partial(product_kernel, len(addends), with_ids),...  21.5 us
    ppermute x6, starting transfers between devices, move(): return lax.ppermute(value, ('req', 'tp'), pairs)  18.5 us
    ppermute x3, starting transfers between devices, local(): lows.append(lax.ppermute(low, 'tp', pairs))  7.78 us
    ppermute x6, waiting for transfers between devices, move(): return lax.ppermute(value, ('req', 'tp'), pairs)  5.62 us
    pallas_call x2, Pallas kernels, finish(): pl.pallas_call(functools.partial(finish_kernel, len(arrivals)), grid=(row...  4.6 us
    ppermute x3, waiting for transfers between devices, local(): lows.append(lax.ppermute(low, 'tp', pairs))  4.17 us
    pallas_call x1, Pallas kernels, pick_adapters(): pl.pallas_call(functools.partial(pick_kernel, peers, len(after)), in_spec...  3.99 us
    pallas_call x1, Pallas kernels, first_product(): pl.pallas_call(functools.partial(first_kernel, chunk), in_specs=[pl.Block...  3.52 us
  transfers between devices with their start and end apart: 15, of which 5 were waited for; matrix products, arithmetic and copies ran while one was open for 0% of the time, Pallas kernels for 38%

profile of v8, /device:TPU:0, one launch (start us, length us, event | category | flops | bytes accessed | tf_op | source)
XLA Modules:
  0.0 82.6 jit_solution(16709463882649532929)
XLA Ops:
  0.0 0.0 copy-start
  0.0 1.6 %copy-done = bf16[512,2048]{1,0:T(8,128)(2,1)S(1)} copy-done((bf16[512,2048]{1,0:T(8,128)(2,1)S(1)}, bf16[512,2048]{1,0:T(8,128)(2,1)}, u32[]{:S(2)}) %copy-start) | copy-done | bytes 2097176
  1.6 0.0 copy-start.1
  1.6 0.0 copy-start.11
  1.6 3.5 %first_product.1.rest_1_ = bf16[512,512]{1,0:T(8,128)(2,1)} custom-call(s32[1]{0:T(128)} %bitcast.2.first_ref, bf16[512,2048]{1,0:T(8,128)(2,1)S(1)} %copy-done, bf16[2048,4096]{1,0:T(8,128)(2,1)} %weight_ref.15), custom_call_target="tpu_custom_call" | custom-call | flops 1000 | bytes 1000 | tf_op jit(solution)/shard_map/first_product/pallas_call | solution.py:95
  5.1 3.1 %collective-permute-start.6 = (bf16[512,512]{1,0:T(8,128)(2,1)}, bf16[512,512]{1,0:T(8,128)(2,1)}, u32[]{:S(2)}, u32[]{:S(2)}) collective-permute-start(bf16[512,512]{1,0:T(8,128)(2,1)} %first_product.1.rest_1_), channel_id=1, source_target_pairs={{0,1},{1,2},{2,3},{3,0},{4,7},{5,4},{6,5},{7,6},{8,9},{9,10},{10,1... | collective-permute-start | bytes 1572872 | tf_op jit(solution)/shard_map/ppermute | solution.py:326
  8.2 0.0 copy-done.1
  8.2 0.0 copy-done.11
  8.2 3.5 %block_product.7 = (bf16[512,512]{1,0:T(8,128)(2,1)}, s32[1,12]{1,0:T(1,128)S(1)}) custom-call(s32[1]{0:T(128)} %bitcast.1.first_ref, bf16[512,2048]{1,0:T(8,128)(2,1)S(1)} %copy-done.1, bf16[2048,4096]{1,0:T(8,128)(2,1)} %weight_ref.15, s32[1,12]{1,0:T(1,128)S(1)} %copy-done.11, bf16[512,512]{1,0:T(8,128)(2,1)} %first_product.1.rest_1_), custom_call_target="tpu_custom_call" | custom-call | flops 1000 | bytes 1000 | tf_op jit(solution)/shard_map/block_product/pallas_call | solution.py:42
  11.7 2.7 %collective-permute-start.2 = (s32[1,12]{1,0:T(1,128)S(1)}, s32[1,12]{1,0:T(1,128)S(1)}, u32[]{:S(2)}, u32[]{:S(2)}) collective-permute-start(s32[1,12]{1,0:T(1,128)S(1)} %get-tuple-element.15.rest_0_), channel_id=1, source_target_pairs={{0,12},{4,8},{8,4},{12,0},{1,13},{5,9},{9,5},{13,1},{2,14},{6,10},... | collective-permute-start | bytes 152 | tf_op jit(solution)/shard_map/ppermute | solution.py:344
  14.4 0.5 collective-permute-start.1
  14.9 0.0 collective-permute-start
  14.9 0.8 collective-permute-start.8
  15.6 0.0 collective-permute-done.2.rest_3_
  15.7 2.2 %collective-permute-done.1.rest_2_ = s32[1,12]{1,0:T(1,128)S(1)} collective-permute-done((s32[1,12]{1,0:T(1,128)S(1)}, s32[1,12]{1,0:T(1,128)S(1)}, u32[]{:S(2)}, u32[]{:S(2)}) %collective-permute-start.1) | collective-permute-done | bytes 80 | tf_op jit(solution)/shard_map/ppermute | solution.py:344
  17.9 0.0 collective-permute-done.rest_1_
  17.9 0.0 copy-done.10
  17.9 0.0 copy-done.12
  17.9 4.0 %pick_adapters.1 = (bf16[6,16,3072]{2,1,0:T(8,128)(2,1)S(1)}, bf16[6,16,3072]{2,1,0:T(8,128)(2,1)S(1)}, bf16[6,16,3072]{2,1,0:T(8,128)(2,1)S(1)}, bf16[6,16,3072...) custom-call(s32[1]{0:T(128)} %bitcast.me_ref, s32[512]{0:T(512)S(1)} %copy-done.10, s32[1,12]{1,0:T(1,128)S(1)} %copy-done.12, ...), custom_call_target="tpu_custom_call" | custom-call | flops 1000 | bytes 1000 | tf_op jit(solution)/shard_map/pick_adapters/pallas_call | solution.py:184
  21.9 0.1 collective-permute-start.3
  22.0 0.1 collective-permute-start.4
  22.1 1.8 %collective-permute-start.5 = (bf16[6,16,3072]{2,1,0:T(8,128)(2,1)S(1)}, bf16[6,16,3072]{2,1,0:T(8,128)(2,1)S(1)}, u32[]{:S(2)}, u32[]{:S(2)}) collective-permute-start(bf16[6,16,3072]{2,1,0:T(8,128)(2,1)S(1)} %get-tuple-element.22), channel_id=1, source_target_pairs={{0,12},{4,8},{8,4},{12,0},{1,13},{5,9},{9,5},{13,1},{2,14},{6,10},... | collective-permute-start | bytes 1769480 | tf_op jit(solution)/shard_map/ppermute | solution.py:347
  23.9 0.0 collective-permute-done.6.rest_0_
  23.9 2.8 %block_product.8.rest_0_ = bf16[512,512]{1,0:T(8,128)(2,1)S(1)} custom-call(s32[1]{0:T(128)} %bitcast.4.first_ref, bf16[512,2048]{1,0:T(8,128)(2,1)S(1)} %copy-done.1, bf16[2048,4096]{1,0:T(8,128)(2,1)} %weight_ref.15, bf16[512,512]{1,0:T(8,128)(2,1)} %collective-permute-done.6.rest_0_, s32[24]{0:T(128)S(1)} %get-tuple-element.17.rest_1_.start_ref), custom_call_target="tpu_custom_call" | custom-call | flops 1000 | bytes 1000 | tf_op jit(solution)/shard_map/block_product/pallas_call | solution.py:42
  26.7 3.2 %collective-permute-start.7 = (bf16[512,512]{1,0:T(8,128)(2,1)S(1)}, bf16[512,512]{1,0:T(8,128)(2,1)S(1)}, u32[]{:S(2)}, u32[]{:S(2)}) collective-permute-start(bf16[512,512]{1,0:T(8,128)(2,1)S(1)} %block_product.8.rest_0_), channel_id=1, source_target_pairs={{0,1},{1,2},{2,3},{3,0},{4,7},{5,4},{6,5},{7,6},{8,9},{9,10},{10,1... | collective-permute-start | bytes 1572872 | tf_op jit(solution)/shard_map/ppermute | solution.py:326
  29.9 2.7 %block_product.9.rest_1_.rest_4_ = bf16[512,512]{1,0:T(8,128)(2,1)S(1)} custom-call(s32[1]{0:T(128)} %bitcast.7.first_ref, bf16[512,2048]{1,0:T(8,128)(2,1)S(1)} %copy-done.1, bf16[2048,4096]{1,0:T(8,128)(2,1)} %weight_ref.15, bf16[512,512]{1,0:T(8,128)(2,1)S(1)} %block_product.8.rest_0_), custom_call_target="tpu_custom_call" | custom-call | flops 20000000000 | bytes 60000000 | tf_op jit(solution)/shard_map/block_product/pallas_call | solution.py:42
  32.6 0.0 copy-start.6
  32.6 0.1 collective-permute-done.8.rest_0_
  32.7 3.6 %block_product.10.rest_0_ = bf16[512,512]{1,0:T(8,128)(2,1)} custom-call(s32[1]{0:T(128)} %bitcast.6.first_ref, bf16[512,2048]{1,0:T(8,128)(2,1)S(1)} %copy-done.1, bf16[2048,4096]{1,0:T(8,128)(2,1)} %weight_ref.15, bf16[512,512]{1,0:T(8,128)(2,1)} %collective-permute-done.8.rest_0_, bf16[512,512]{1,0:T(8,128)(2,1)S(1)} %block_product.9.rest_1_.rest_4_), custom_call_target="tpu_custom_call" | custom-call | flops 1000 | bytes 1000 | tf_op jit(solution)/shard_map/block_product/pallas_call | solution.py:42
  36.3 0.0 copy-done.6
  36.3 5.0 %collective-permute-start.12 = (bf16[512,512]{1,0:T(8,128)(2,1)}, bf16[512,512]{1,0:T(8,128)(2,1)}, u32[]{:S(2)}, u32[]{:S(2)}) collective-permute-start(bf16[512,512]{1,0:T(8,128)(2,1)} %block_product.10.rest_0_), channel_id=1, source_target_pairs={{0,3},{1,0},{2,1},{3,2},{4,5},{5,6},{6,7},{7,4},{8,11},{9,8},{10,9... | collective-permute-start | bytes 1572872 | tf_op jit(solution)/shard_map/ppermute | solution.py:326
  41.3 2.7 %block_product.11.rest_1_.rest_5_ = bf16[512,512]{1,0:T(8,128)(2,1)S(1)} custom-call(s32[1]{0:T(128)} %bitcast.5.first_ref, bf16[512,2048]{1,0:T(8,128)(2,1)S(1)} %copy-done.1, bf16[2048,4096]{1,0:T(8,128)(2,1)} %weight_ref.15, bf16[512,512]{1,0:T(8,128)(2,1)} %block_product.10.rest_0_), custom_call_target="tpu_custom_call" | custom-call | flops 20000000000 | bytes 60000000 | tf_op jit(solution)/shard_map/block_product/pallas_call | solution.py:42
  44.0 0.0 copy-start.8
  44.0 3.9 %collective-permute-done.7.rest_0_ = bf16[512,512]{1,0:T(8,128)(2,1)S(1)} collective-permute-done((bf16[512,512]{1,0:T(8,128)(2,1)S(1)}, bf16[512,512]{1,0:T(8,128)(2,1)S(1)}, u32[]{:S(2)}, u32[]{:S(2)}) %collective-permute-start.7) | collective-permute-done | bytes 524320 | tf_op jit(solution)/shard_map/ppermute | solution.py:326
  47.9 3.4 %block_product.12.rest_4_ = bf16[512,512]{1,0:T(8,128)(2,1)} custom-call(s32[1]{0:T(128)} %bitcast.3.first_ref, bf16[512,2048]{1,0:T(8,128)(2,1)S(1)} %copy-done.1, bf16[2048,4096]{1,0:T(8,128)(2,1)} %weight_ref.15, bf16[512,512]{1,0:T(8,128)(2,1)S(1)} %collective-permute-done.7.rest_0_, bf16[512,512]{1,0:T(8,128)(2,1)S(1)} %block_product.11.rest_1_.rest_5_), custom_call_target="tpu_custom_call" | custom-call | flops 1000 | bytes 1000 | tf_op jit(solution)/shard_map/block_product/pallas_call | solution.py:42
  51.3 0.0 copy-done.8
  51.3 3.1 %collective-permute-start.14 = (bf16[512,512]{1,0:T(8,128)(2,1)}, bf16[512,512]{1,0:T(8,128)(2,1)}, u32[]{:S(2)}, u32[]{:S(2)}) collective-permute-start(bf16[512,512]{1,0:T(8,128)(2,1)} %block_product.12.rest_4_), channel_id=1, source_target_pairs={{0,1},{1,2},{2,3},{3,0},{4,7},{5,4},{6,5},{7,6},{8,9},{9,10},{10,1... | collective-permute-start | bytes 1572872 | tf_op jit(solution)/shard_map/ppermute | solution.py:326
  54.4 0.0 collective-permute-done.3.rest_1_.rest_7_
  54.4 0.0 collective-permute-done.4.rest_2_.rest_8_
  54.4 0.0 collective-permute-done.5.rest_3_.rest_9_
  54.4 0.0 copy-start.4
  54.5 1.6 %low_sums.1.rest_1_.rest_0_ = f32[16,512]{1,0:T(8,128)S(1)} custom-call(s32[24]{0:T(128)S(1)} %get-tuple-element.17.rest_1_.start_ref, s32[24]{0:T(128)S(1)} %get-tuple-element.18.end_ref, bf16[512,2048]{1,0:T(8,128)(2,1)S(1)} %copy-done.1, bf16[6,16,3072]{2,1,0:T(8,128)(2,1)S(1)} %get-tuple-element.19.rest_0_.rest_6_, ...), custom_call_target="tpu_custom_call" | custom-call | flops 1000 | bytes 1000 | tf_op jit(solution)/shard_map/low_sums/pallas_call | solution.py:226
  56.0 0.0 copy-done.4
  56.0 0.0 copy-start.2
  56.0 0.8 copy-done.2
  56.8 6.7 %collective-permute-start.11 = (f32[16,512]{1,0:T(8,128)S(1)}, f32[16,512]{1,0:T(8,128)S(1)}, u32[]{:S(2)}, u32[]{:S(2)}) collective-permute-start(f32[16,512]{1,0:T(8,128)S(1)} %low_sums.1.rest_1_.rest_0_), channel_id=1, source_target_pairs={{0,3},{1,2},{2,1},{3,0},{4,7},{5,6},{6,5},{7,4},{8,11},{9,10},{10,... | collective-permute-start | bytes 98312 | tf_op jit(solution)/shard_map/ppermute | solution.py:357
  63.5 0.6 collective-permute-start.10
  64.1 0.6 collective-permute-start.9
  64.6 0.0 collective-permute-done.12.rest_0_
  64.6 0.0 copy-start.9
  64.6 2.9 %block_product.13.rest_10_ = bf16[512,512]{1,0:T(8,128)(2,1)S(1)} custom-call(s32[1]{0:T(128)} %bitcast.8.first_ref, bf16[512,2048]{1,0:T(8,128)(2,1)S(1)} %copy-done.1, bf16[2048,4096]{1,0:T(8,128)(2,1)} %weight_ref.15, bf16[512,512]{1,0:T(8,128)(2,1)} %collective-permute-done.12.rest_0_, f32[16,512]{1,0:T(8,128)S(1)} %low_sums.1.rest_1_.rest_0_), custom_call_target="tpu_custom_call" | custom-call | flops 1000 | bytes 1000 | tf_op jit(solution)/shard_map/block_product/pallas_call | solution.py:42
  67.6 3.3 %collective-permute-start.13 = (bf16[512,512]{1,0:T(8,128)(2,1)S(1)}, bf16[512,512]{1,0:T(8,128)(2,1)S(1)}, u32[]{:S(2)}, u32[]{:S(2)}) collective-permute-start(bf16[512,512]{1,0:T(8,128)(2,1)S(1)} %block_product.13.rest_10_), channel_id=1, source_target_pairs={{0,3},{1,0},{2,1},{3,2},{4,5},{5,6},{6,7},{7,4},{8,11},{9,8},{10,9... | collective-permute-start | bytes 1572872 | tf_op jit(solution)/shard_map/ppermute | solution.py:326
  70.9 0.0 collective-permute-done.11.rest_3_
  70.9 4.2 %collective-permute-done.10.rest_2_ = f32[16,512]{1,0:T(8,128)S(1)} collective-permute-done((f32[16,512]{1,0:T(8,128)S(1)}, f32[16,512]{1,0:T(8,128)S(1)}, u32[]{:S(2)}, u32[]{:S(2)}) %collective-permute-start.10) | collective-permute-done | bytes 32800 | tf_op jit(solution)/shard_map/ppermute | solution.py:357
  75.1 0.0 collective-permute-done.9.rest_1_
  75.1 0.0 copy-done.3
  75.1 0.0 copy-done.5
  75.1 0.0 copy-done.7
  75.1 0.0 copy-done.9
  75.1 1.3 %adapter_term.1 = (f32[512,512]{1,0:T(8,128)S(1)}, f32[512,512]{1,0:T(8,128)S(1)}) custom-call(s32[24]{0:T(128)S(1)} %get-tuple-element.17.rest_1_.start_ref, s32[24]{0:T(128)S(1)} %get-tuple-element.18.end_ref, f32[16,512]{1,0:T(8,128)S(1)} %low_sums.1.rest_1_.rest_0_, f32[16,512]{1,0:T(8,128)S(1)} %collective-permute-done.9.rest_1_, ...), custom_call_target="tpu_custom_call" | custom-call | flops 1000 | bytes 1000 | tf_op jit(solution)/shard_map/adapter_term/pallas_call | solution.py:272
  76.4 0.0 collective-permute-done.14.rest_0_
  76.4 3.2 %finish.2.rest_1_ = bf16[512,1024]{1,0:T(8,128)(2,1)} custom-call(f32[512,512]{1,0:T(8,128)S(1)} %get-tuple-element.24.term_ref, bf16[512,512]{1,0:T(8,128)(2,1)} %collective-permute-done.14.rest_0_), custom_call_target="tpu_custom_call" | custom-call | flops 20000000000 | bytes 60000000 | tf_op jit(solution)/shard_map/finish/pallas_call | solution.py:299
  79.6 1.6 %collective-permute-done.13.rest_0_ = bf16[512,512]{1,0:T(8,128)(2,1)S(1)} collective-permute-done((bf16[512,512]{1,0:T(8,128)(2,1)S(1)}, bf16[512,512]{1,0:T(8,128)(2,1)S(1)}, u32[]{:S(2)}, u32[]{:S(2)}) %collective-permute-start.13) | collective-permute-done | bytes 524320 | tf_op jit(solution)/shard_map/ppermute | solution.py:326
  81.2 1.4 %finish.3 = bf16[512,1024]{1,0:T(8,128)(2,1)} custom-call(f32[512,512]{1,0:T(8,128)S(1)} %get-tuple-element.23.term_ref, bf16[512,512]{1,0:T(8,128)(2,1)S(1)} %collective-permute-done.13.rest_0_, bf16[512,1024]{1,0:T(8,128)(2,1)} %finish.2.rest_1_), custom_call_target="tpu_custom_call", output_to_operand_aliasing={{}: (2, {})} | custom-call | flops 1000 | bytes 1000 | tf_op jit(solution)/shard_map/finish/pallas_call | solution.py:299
  (5 shorter events, 0.0 us)
Async XLA Ops:
  0.0 1.6 %copy-start = (bf16[512,2048]{1,0:T(8,128)(2,1)S(1)}, bf16[512,2048]{1,0:T(8,128)(2,1)}, u32[]{:S(2)}) copy-start(bf16[512,2048]{1,0:T(8,128)(2,1)} %rows_ref.17) | copy-start | bytes 6291460
  1.6 6.6 %copy-start.1 = (bf16[512,2048]{1,0:T(8,128)(2,1)S(1)}, bf16[512,2048]{1,0:T(8,128)(2,1)}, u32[]{:S(2)}) copy-start(bf16[512,2048]{1,0:T(8,128)(2,1)} %rows_ref.17) | copy-start | bytes 6291460
  1.6 6.6 %copy-start.11 = (s32[1,12]{1,0:T(1,128)S(1)}, s32[1,12]{1,0:T(1,128)}, u32[]{:S(2)}) copy-start(s32[1,12]{1,0:T(1,128)} %rest_0_.1) | copy-start | bytes 148
  5.1 18.8 %collective-permute-start.6 = (bf16[512,512]{1,0:T(8,128)(2,1)}, bf16[512,512]{1,0:T(8,128)(2,1)}, u32[]{:S(2)}, u32[]{:S(2)}) collective-permute-start(bf16[512,512]{1,0:T(8,128)(2,1)} %first_product.1.rest_1_), channel_id=1, source_target_pairs={{0,1},{1,2},{2,3},{3,0},{4,7},{5,4},{6,5},{7,6},{8,9},{9,10},{10,1... | collective-permute-start | bytes 1572872 | tf_op jit(solution)/shard_map/ppermute | solution.py:326
  8.2 9.7 %copy-start.10 = (s32[512]{0:T(512)S(1)}, s32[512]{0:T(512)}, u32[]{:S(2)}) copy-start(s32[512]{0:T(512)} %table_ref.1) | copy-start | bytes 6148
  8.2 9.7 %copy-start.12 = (s32[1,12]{1,0:T(1,128)S(1)}, s32[1,12]{1,0:T(1,128)}, u32[]{:S(2)}) copy-start(s32[1,12]{1,0:T(1,128)} %lens_ref.1) | copy-start | bytes 148
  11.7 4.0 %collective-permute-start.2 = (s32[1,12]{1,0:T(1,128)S(1)}, s32[1,12]{1,0:T(1,128)S(1)}, u32[]{:S(2)}, u32[]{:S(2)}) collective-permute-start(s32[1,12]{1,0:T(1,128)S(1)} %get-tuple-element.15.rest_0_), channel_id=1, source_target_pairs={{0,12},{4,8},{8,4},{12,0},{1,13},{5,9},{9,5},{13,1},{2,14},{6,10},... | collective-permute-start | bytes 152 | tf_op jit(solution)/shard_map/ppermute | solution.py:344
  14.4 3.5 %collective-permute-start.1 = (s32[1,12]{1,0:T(1,128)S(1)}, s32[1,12]{1,0:T(1,128)S(1)}, u32[]{:S(2)}, u32[]{:S(2)}) collective-permute-start(s32[1,12]{1,0:T(1,128)S(1)} %get-tuple-element.15.rest_0_), channel_id=1, source_target_pairs={{0,8},{4,12},{8,0},{12,4},{1,9},{5,13},{9,1},{13,5},{2,10},{6,14},... | collective-permute-start | bytes 152 | tf_op jit(solution)/shard_map/ppermute | solution.py:344
  14.9 3.0 %collective-permute-start = (s32[1,12]{1,0:T(1,128)S(1)}, s32[1,12]{1,0:T(1,128)S(1)}, u32[]{:S(2)}, u32[]{:S(2)}) collective-permute-start(s32[1,12]{1,0:T(1,128)S(1)} %get-tuple-element.15.rest_0_), channel_id=1, source_target_pairs={{0,4},{4,0},{8,12},{12,8},{1,5},{5,1},{9,13},{13,9},{2,6},{6,2},{1... | collective-permute-start | bytes 152 | tf_op jit(solution)/shard_map/ppermute | solution.py:344
  14.9 17.8 %collective-permute-start.8 = (bf16[512,512]{1,0:T(8,128)(2,1)}, bf16[512,512]{1,0:T(8,128)(2,1)}, u32[]{:S(2)}, u32[]{:S(2)}) collective-permute-start(bf16[512,512]{1,0:T(8,128)(2,1)} %get-tuple-element.16.rest_6_), channel_id=1, source_target_pairs={{0,3},{1,0},{2,1},{3,2},{4,5},{5,6},{6,7},{7,4},{8,11},{9,8},{10,9... | collective-permute-start | bytes 1572872 | tf_op jit(solution)/shard_map/ppermute | solution.py:326
  21.9 32.5 %collective-permute-start.3 = (bf16[6,16,3072]{2,1,0:T(8,128)(2,1)S(1)}, bf16[6,16,3072]{2,1,0:T(8,128)(2,1)S(1)}, u32[]{:S(2)}, u32[]{:S(2)}) collective-permute-start(bf16[6,16,3072]{2,1,0:T(8,128)(2,1)S(1)} %get-tuple-element.20), channel_id=1, source_target_pairs={{0,4},{4,0},{8,12},{12,8},{1,5},{5,1},{9,13},{13,9},{2,6},{6,2},{1... | collective-permute-start | bytes 1769480 | tf_op jit(solution)/shard_map/ppermute | solution.py:347
  22.0 32.4 %collective-permute-start.4 = (bf16[6,16,3072]{2,1,0:T(8,128)(2,1)S(1)}, bf16[6,16,3072]{2,1,0:T(8,128)(2,1)S(1)}, u32[]{:S(2)}, u32[]{:S(2)}) collective-permute-start(bf16[6,16,3072]{2,1,0:T(8,128)(2,1)S(1)} %get-tuple-element.21), channel_id=1, source_target_pairs={{0,8},{4,12},{8,0},{12,4},{1,9},{5,13},{9,1},{13,5},{2,10},{6,14},... | collective-permute-start | bytes 1769480 | tf_op jit(solution)/shard_map/ppermute | solution.py:347
  22.1 32.4 %collective-permute-start.5 = (bf16[6,16,3072]{2,1,0:T(8,128)(2,1)S(1)}, bf16[6,16,3072]{2,1,0:T(8,128)(2,1)S(1)}, u32[]{:S(2)}, u32[]{:S(2)}) collective-permute-start(bf16[6,16,3072]{2,1,0:T(8,128)(2,1)S(1)} %get-tuple-element.22), channel_id=1, source_target_pairs={{0,12},{4,8},{8,4},{12,0},{1,13},{5,9},{9,5},{13,1},{2,14},{6,10},... | collective-permute-start | bytes 1769480 | tf_op jit(solution)/shard_map/ppermute | solution.py:347
  26.7 21.2 %collective-permute-start.7 = (bf16[512,512]{1,0:T(8,128)(2,1)S(1)}, bf16[512,512]{1,0:T(8,128)(2,1)S(1)}, u32[]{:S(2)}, u32[]{:S(2)}) collective-permute-start(bf16[512,512]{1,0:T(8,128)(2,1)S(1)} %block_product.8.rest_0_), channel_id=1, source_target_pairs={{0,1},{1,2},{2,3},{3,0},{4,7},{5,4},{6,5},{7,6},{8,9},{9,10},{10,1... | collective-permute-start | bytes 1572872 | tf_op jit(solution)/shard_map/ppermute | solution.py:326
  32.6 3.7 %copy-start.6 = (bf16[512,512]{1,0:T(8,128)(2,1)}, bf16[512,512]{1,0:T(8,128)(2,1)S(1)}, u32[]{:S(2)}) copy-start(bf16[512,512]{1,0:T(8,128)(2,1)S(1)} %block_product.9.rest_1_.rest_4_) | copy-start | bytes 1572868
  36.3 28.3 %collective-permute-start.12 = (bf16[512,512]{1,0:T(8,128)(2,1)}, bf16[512,512]{1,0:T(8,128)(2,1)}, u32[]{:S(2)}, u32[]{:S(2)}) collective-permute-start(bf16[512,512]{1,0:T(8,128)(2,1)} %block_product.10.rest_0_), channel_id=1, source_target_pairs={{0,3},{1,0},{2,1},{3,2},{4,5},{5,6},{6,7},{7,4},{8,11},{9,8},{10,9... | collective-permute-start | bytes 1572872 | tf_op jit(solution)/shard_map/ppermute | solution.py:326
  44.0 7.3 %copy-start.8 = (bf16[512,512]{1,0:T(8,128)(2,1)}, bf16[512,512]{1,0:T(8,128)(2,1)S(1)}, u32[]{:S(2)}) copy-start(bf16[512,512]{1,0:T(8,128)(2,1)S(1)} %block_product.11.rest_1_.rest_5_) | copy-start | bytes 1572868
  51.3 25.1 %collective-permute-start.14 = (bf16[512,512]{1,0:T(8,128)(2,1)}, bf16[512,512]{1,0:T(8,128)(2,1)}, u32[]{:S(2)}, u32[]{:S(2)}) collective-permute-start(bf16[512,512]{1,0:T(8,128)(2,1)} %block_product.12.rest_4_), channel_id=1, source_target_pairs={{0,1},{1,2},{2,3},{3,0},{4,7},{5,4},{6,5},{7,6},{8,9},{9,10},{10,1... | collective-permute-start | bytes 1572872 | tf_op jit(solution)/shard_map/ppermute | solution.py:326
  54.4 1.6 %copy-start.4 = (bf16[6,16,3072]{2,1,0:T(8,128)(2,1)}, bf16[6,16,3072]{2,1,0:T(8,128)(2,1)S(1)}, u32[]{:S(2)}) copy-start(bf16[6,16,3072]{2,1,0:T(8,128)(2,1)S(1)} %collective-permute-done.5.rest_3_.rest_9_) | copy-start | bytes 1769476
  56.0 0.8 copy-start.2
  56.8 14.1 %collective-permute-start.11 = (f32[16,512]{1,0:T(8,128)S(1)}, f32[16,512]{1,0:T(8,128)S(1)}, u32[]{:S(2)}, u32[]{:S(2)}) collective-permute-start(f32[16,512]{1,0:T(8,128)S(1)} %low_sums.1.rest_1_.rest_0_), channel_id=1, source_target_pairs={{0,3},{1,2},{2,1},{3,0},{4,7},{5,6},{6,5},{7,4},{8,11},{9,10},{10,... | collective-permute-start | bytes 98312 | tf_op jit(solution)/shard_map/ppermute | solution.py:357
  63.5 11.6 %collective-permute-start.10 = (f32[16,512]{1,0:T(8,128)S(1)}, f32[16,512]{1,0:T(8,128)S(1)}, u32[]{:S(2)}, u32[]{:S(2)}) collective-permute-start(f32[16,512]{1,0:T(8,128)S(1)} %low_sums.1.rest_1_.rest_0_), channel_id=1, source_target_pairs={{0,2},{1,3},{2,0},{3,1},{4,6},{5,7},{6,4},{7,5},{8,10},{9,11},{10,... | collective-permute-start | bytes 98312 | tf_op jit(solution)/shard_map/ppermute | solution.py:357
  64.1 11.0 %collective-permute-start.9 = (f32[16,512]{1,0:T(8,128)S(1)}, f32[16,512]{1,0:T(8,128)S(1)}, u32[]{:S(2)}, u32[]{:S(2)}) collective-permute-start(f32[16,512]{1,0:T(8,128)S(1)} %low_sums.1.rest_1_.rest_0_), channel_id=1, source_target_pairs={{0,1},{1,0},{2,3},{3,2},{4,5},{5,4},{6,7},{7,6},{8,9},{9,8},{10,11... | collective-permute-start | bytes 98312 | tf_op jit(solution)/shard_map/ppermute | solution.py:357
  64.6 10.5 %copy-start.3 = (bf16[6,16,3072]{2,1,0:T(8,128)(2,1)S(1)}, bf16[6,16,3072]{2,1,0:T(8,128)(2,1)}, u32[]{:S(2)}) copy-start(bf16[6,16,3072]{2,1,0:T(8,128)(2,1)} %copy-done.2) | copy-start | bytes 1769476
  64.6 10.5 %copy-start.5 = (bf16[6,16,3072]{2,1,0:T(8,128)(2,1)S(1)}, bf16[6,16,3072]{2,1,0:T(8,128)(2,1)}, u32[]{:S(2)}) copy-start(bf16[6,16,3072]{2,1,0:T(8,128)(2,1)} %copy-done.4) | copy-start | bytes 1769476
  64.6 10.5 %copy-start.7 = (bf16[512,512]{1,0:T(8,128)(2,1)S(1)}, bf16[512,512]{1,0:T(8,128)(2,1)}, u32[]{:S(2)}) copy-start(bf16[512,512]{1,0:T(8,128)(2,1)} %copy-done.6) | copy-start | bytes 1572868
  64.6 10.5 %copy-start.9 = (bf16[512,512]{1,0:T(8,128)(2,1)S(1)}, bf16[512,512]{1,0:T(8,128)(2,1)}, u32[]{:S(2)}) copy-start(bf16[512,512]{1,0:T(8,128)(2,1)} %copy-done.8) | copy-start | bytes 1572868
  67.6 13.6 %collective-permute-start.13 = (bf16[512,512]{1,0:T(8,128)(2,1)S(1)}, bf16[512,512]{1,0:T(8,128)(2,1)S(1)}, u32[]{:S(2)}, u32[]{:S(2)}) collective-permute-start(bf16[512,512]{1,0:T(8,128)(2,1)S(1)} %block_product.13.rest_10_), channel_id=1, source_target_pairs={{0,3},{1,0},{2,1},{3,2},{4,5},{5,6},{6,7},{7,4},{8,11},{9,8},{10,9... | collective-permute-start | bytes 1572872 | tf_op jit(solution)/shard_map/ppermute | solution.py:326

commit v9 on v8

--- a/solution.py
+++ b/solution.py
@@ -9,11 +9,11 @@
 
 CAP = 6
 PIECES = 2
-VMEM_LIMIT = 48 * 1024 * 1024
+VMEM_LIMIT = 20 * 1024 * 1024
 F32 = jnp.float32
 BF16 = jnp.bfloat16
 SMALL = pl.CostEstimate(flops=1000, bytes_accessed=1000, transcendentals=0)
-LARGE = pl.CostEstimate(flops=2 * 10**10, bytes_accessed=6 * 10**7, transcendentals=0)
+LARGE = pl.CostEstimate(flops=2 * 10**10, bytes_accessed=1000, transcendentals=0)
 
 
 def product_kernel(addends, with_ids, first_ref, rows_ref, weight_ref, *rest):
@@ -106,7 +106,7 @@
         compiler_params=pltpu.CompilerParams(vmem_limit_bytes=VMEM_LIMIT),
         cost_estimate=SMALL,
         name="first_product",
-    )(first.reshape(1), rows, weight)
+    )(first.reshape(1), pltpu.with_memory_space_constraint(rows, pltpu.HBM), weight)
 
 
 def pick_kernel(peers, afters, me_ref, table_ref, lens_ref, *rest):

time: 83.1 us -> 99.1 us (1.19)
  the two profiles are of different devices: /device:TPU:0 before, /device:TPU:1 now
where the time goes in v9:
time: 99.1 us; the launch traced here: 98.7 us
  Pallas kernels  31.8 us (32%)
  local copies, waits for them, and re-layouts  29.5 us (30%)
  waiting for transfers between devices  21.5 us (22%)
  starting transfers between devices  15.6 us (16%)
    unnamed x36, local copies, waits for them, and re-layouts  29.5 us
    ppermute x6, waiting for transfers between devices, move(): return lax.ppermute(value, ('req', 'tp'), pairs)  18 us
    pallas_call x7, Pallas kernels, block_product(): pl.pallas_call(functools.partial(product_kernel, len(addends), with_ids),...  17.7 us
    ppermute x6, starting transfers between devices, move(): return lax.ppermute(value, ('req', 'tp'), pairs)  6.33 us
    pallas_call x2, Pallas kernels, finish(): pl.pallas_call(functools.partial(finish_kernel, len(arrivals)), grid=(row...  4.6 us
    ppermute x3, starting transfers between devices, local(): lax.ppermute(packs[x], 'req', [(i, i ^ x) for i in range(req_total)])  3.58 us
    ppermute x3, starting transfers between devices, local(): lows.append(lax.ppermute(low, 'tp', pairs))  3.55 us
    pallas_call x1, Pallas kernels, first_product(): pl.pallas_call(functools.partial(first_kernel, chunk), in_specs=[pl.Block...  3.46 us
  transfers between devices with their start and end apart: 15, of which 4 were waited for; matrix products, arithmetic and copies ran while one was open for 0% of the time, Pallas kernels for 27%

profile of v9, /device:TPU:1, one launch (start us, length us, event | category | flops | bytes accessed | tf_op | source)
XLA Modules:
  0.0 98.7 jit_solution(15537437035565551669)
XLA Ops:
  0.0 5.8 %copy-done = bf16[2048,4096]{1,0:T(8,128)(2,1)S(1)} copy-done((bf16[2048,4096]{1,0:T(8,128)(2,1)S(1)}, bf16[2048,4096]{1,0:T(8,128)(2,1)}, u32[]{:S(2)}) %copy-start) | copy-done | bytes 16777240
  5.8 3.5 %first_product.1.rest_1_ = bf16[512,512]{1,0:T(8,128)(2,1)} custom-call(s32[1]{0:T(128)} %bitcast.2.first_ref, bf16[512,2048]{1,0:T(8,128)(2,1)} %rows_ref.17, bf16[2048,4096]{1,0:T(8,128)(2,1)S(1)} %copy-done), custom_call_target="tpu_custom_call" | custom-call | flops 1000 | bytes 1000 | tf_op jit(solution)/shard_map/first_product/pallas_call | solution.py:95
  9.2 4.2 %collective-permute-start.6 = (bf16[512,512]{1,0:T(8,128)(2,1)}, bf16[512,512]{1,0:T(8,128)(2,1)}, u32[]{:S(2)}, u32[]{:S(2)}) collective-permute-start(bf16[512,512]{1,0:T(8,128)(2,1)} %first_product.1.rest_1_), channel_id=1, source_target_pairs={{0,1},{1,2},{2,3},{3,0},{4,7},{5,4},{6,5},{7,6},{8,9},{9,10},{10,1... | collective-permute-start | bytes 1572872 | tf_op jit(solution)/shard_map/ppermute | solution.py:326
  13.5 0.0 copy-done.4
  13.5 0.0 copy-done.16
  13.5 5.8 %copy-done.1 = bf16[2048,4096]{1,0:T(8,128)(2,1)S(1)} copy-done((bf16[2048,4096]{1,0:T(8,128)(2,1)S(1)}, bf16[2048,4096]{1,0:T(8,128)(2,1)}, u32[]{:S(2)}) %copy-start.1) | copy-done | bytes 16777240
  19.2 2.9 %block_product.7 = (bf16[512,512]{1,0:T(8,128)(2,1)}, s32[1,12]{1,0:T(1,128)S(1)}) custom-call(s32[1]{0:T(128)} %bitcast.1.first_ref, bf16[512,2048]{1,0:T(8,128)(2,1)S(1)} %copy-done.4, bf16[2048,4096]{1,0:T(8,128)(2,1)S(1)} %copy-done.1, s32[1,12]{1,0:T(1,128)S(1)} %copy-done.16, bf16[512,512]{1,0:T(8,128)(2,1)} %first_product.1.rest_1_), custom_call_target="tpu_custom_call" | custom-call | flops 1000 | bytes 1000 | tf_op jit(solution)/shard_map/block_product/pallas_call | solution.py:42
  22.1 0.1 collective-permute-start.2
  22.2 1.2 %collective-permute-start.1 = (s32[1,12]{1,0:T(1,128)S(1)}, s32[1,12]{1,0:T(1,128)S(1)}, u32[]{:S(2)}, u32[]{:S(2)}) collective-permute-start(s32[1,12]{1,0:T(1,128)S(1)} %get-tuple-element.15.rest_0_), channel_id=1, source_target_pairs={{0,8},{4,12},{8,0},{12,4},{1,9},{5,13},{9,1},{13,5},{2,10},{6,14},... | collective-permute-start | bytes 152 | tf_op jit(solution)/shard_map/ppermute | solution.py:344
  23.4 0.9 collective-permute-start
  24.3 0.0 collective-permute-start.8
  24.3 1.2 %collective-permute-done.2.rest_3_ = s32[1,12]{1,0:T(1,128)S(1)} collective-permute-done((s32[1,12]{1,0:T(1,128)S(1)}, s32[1,12]{1,0:T(1,128)S(1)}, u32[]{:S(2)}, u32[]{:S(2)}) %collective-permute-start.2) | collective-permute-done | bytes 80 | tf_op jit(solution)/shard_map/ppermute | solution.py:344
  25.5 0.0 collective-permute-done.1.rest_2_
  25.5 0.0 collective-permute-done.rest_1_
  25.5 0.0 copy-done.15
  25.5 0.0 copy-done.17
  25.5 0.0 copy-start.5
  25.5 3.4 %copy-done.5 = bf16[128,16,2048]{2,1,0:T(8,128)(2,1)S(1)} copy-done((bf16[128,16,2048]{2,1,0:T(8,128)(2,1)S(1)}, bf16[128,16,2048]{2,1,0:T(8,128)(2,1)}, u32[]{:S(2)}) %copy-start.5) | copy-done | bytes 8388632
  28.9 2.2 %copy-done.6 = bf16[128,16,1024]{2,1,0:T(8,128)(2,1)S(1)} copy-done((bf16[128,16,1024]{2,1,0:T(8,128)(2,1)S(1)}, bf16[128,16,1024]{2,1,0:T(8,128)(2,1)}, u32[]{:S(2)}) %copy-start.6) | copy-done | bytes 4194328
  31.1 3.3 %pick_adapters.1 = (bf16[6,16,3072]{2,1,0:T(8,128)(2,1)S(1)}, bf16[6,16,3072]{2,1,0:T(8,128)(2,1)S(1)}, bf16[6,16,3072]{2,1,0:T(8,128)(2,1)S(1)}, bf16[6,16,3072...) custom-call(s32[1]{0:T(128)} %bitcast.me_ref, s32[512]{0:T(512)S(1)} %copy-done.15, s32[1,12]{1,0:T(1,128)S(1)} %copy-done.17, ...), custom_call_target="tpu_custom_call" | custom-call | flops 1000 | bytes 1000 | tf_op jit(solution)/shard_map/pick_adapters/pallas_call | solution.py:184
  34.4 1.9 %collective-permute-start.3 = (bf16[6,16,3072]{2,1,0:T(8,128)(2,1)S(1)}, bf16[6,16,3072]{2,1,0:T(8,128)(2,1)S(1)}, u32[]{:S(2)}, u32[]{:S(2)}) collective-permute-start(bf16[6,16,3072]{2,1,0:T(8,128)(2,1)S(1)} %get-tuple-element.20), channel_id=1, source_target_pairs={{0,4},{4,0},{8,12},{12,8},{1,5},{5,1},{9,13},{13,9},{2,6},{6,2},{1... | collective-permute-start | bytes 1769480 | tf_op jit(solution)/shard_map/ppermute | solution.py:347
  36.2 0.2 collective-permute-start.4
  36.5 1.5 %collective-permute-start.5 = (bf16[6,16,3072]{2,1,0:T(8,128)(2,1)S(1)}, bf16[6,16,3072]{2,1,0:T(8,128)(2,1)S(1)}, u32[]{:S(2)}, u32[]{:S(2)}) collective-permute-start(bf16[6,16,3072]{2,1,0:T(8,128)(2,1)S(1)} %get-tuple-element.22), channel_id=1, source_target_pairs={{0,12},{4,8},{8,4},{12,0},{1,13},{5,9},{9,5},{13,1},{2,14},{6,10},... | collective-permute-start | bytes 1769480 | tf_op jit(solution)/shard_map/ppermute | solution.py:347
  38.0 0.0 collective-permute-done.6.rest_0_
  38.0 5.8 %copy-done.2 = bf16[2048,4096]{1,0:T(8,128)(2,1)S(1)} copy-done((bf16[2048,4096]{1,0:T(8,128)(2,1)S(1)}, bf16[2048,4096]{1,0:T(8,128)(2,1)}, u32[]{:S(2)}) %copy-start.2) | copy-done | bytes 16777240
  43.7 2.6 %block_product.8.rest_0_ = bf16[512,512]{1,0:T(8,128)(2,1)S(1)} custom-call(s32[1]{0:T(128)} %bitcast.4.first_ref, bf16[512,2048]{1,0:T(8,128)(2,1)S(1)} %copy-done.4, bf16[2048,4096]{1,0:T(8,128)(2,1)S(1)} %copy-done.2, bf16[512,512]{1,0:T(8,128)(2,1)} %collective-permute-done.6.rest_0_, s32[24]{0:T(128)S(1)} %get-tuple-element.17.rest_1_.start_ref), custom_call_target="tpu_custom_call" | custom-call | flops 1000 | bytes 1000 | tf_op jit(solution)/shard_map/block_product/pallas_call | solution.py:42
  46.3 0.7 collective-permute-start.7
  47.0 1.8 %block_product.9.rest_1_.rest_4_ = bf16[512,512]{1,0:T(8,128)(2,1)S(1)} custom-call(s32[1]{0:T(128)} %bitcast.7.first_ref, bf16[512,2048]{1,0:T(8,128)(2,1)S(1)} %copy-done.4, bf16[2048,4096]{1,0:T(8,128)(2,1)S(1)} %copy-done.2, bf16[512,512]{1,0:T(8,128)(2,1)S(1)} %block_product.8.rest_0_), custom_call_target="tpu_custom_call" | custom-call | flops 20000000000 | bytes 1000 | tf_op jit(solution)/shard_map/block_product/pallas_call | solution.py:42
  48.9 0.0 copy-start.11
  48.9 0.0 collective-permute-done.8.rest_0_
  48.9 3.3 %block_product.10.rest_0_ = bf16[512,512]{1,0:T(8,128)(2,1)} custom-call(s32[1]{0:T(128)} %bitcast.6.first_ref, bf16[512,2048]{1,0:T(8,128)(2,1)S(1)} %copy-done.4, bf16[2048,4096]{1,0:T(8,128)(2,1)S(1)} %copy-done.2, bf16[512,512]{1,0:T(8,128)(2,1)} %collective-permute-done.8.rest_0_, bf16[512,512]{1,0:T(8,128)(2,1)S(1)} %block_product.9.rest_1_.rest_4_), custom_call_target="tpu_custom_call" | custom-call | flops 1000 | bytes 1000 | tf_op jit(solution)/shard_map/block_product/pallas_call | solution.py:42
  52.2 0.0 copy-done.11
  52.2 0.8 collective-permute-start.12
  53.0 1.8 %block_product.11.rest_1_.rest_5_ = bf16[512,512]{1,0:T(8,128)(2,1)S(1)} custom-call(s32[1]{0:T(128)} %bitcast.5.first_ref, bf16[512,2048]{1,0:T(8,128)(2,1)S(1)} %copy-done.4, bf16[2048,4096]{1,0:T(8,128)(2,1)S(1)} %copy-done.2, bf16[512,512]{1,0:T(8,128)(2,1)} %block_product.10.rest_0_), custom_call_target="tpu_custom_call" | custom-call | flops 20000000000 | bytes 1000 | tf_op jit(solution)/shard_map/block_product/pallas_call | solution.py:42
  54.8 0.0 copy-start.13
  54.8 10.4 %collective-permute-done.7.rest_0_ = bf16[512,512]{1,0:T(8,128)(2,1)S(1)} collective-permute-done((bf16[512,512]{1,0:T(8,128)(2,1)S(1)}, bf16[512,512]{1,0:T(8,128)(2,1)S(1)}, u32[]{:S(2)}, u32[]{:S(2)}) %collective-permute-start.7) | collective-permute-done | bytes 524320 | tf_op jit(solution)/shard_map/ppermute | solution.py:326
  65.2 2.5 %block_product.12.rest_4_ = bf16[512,512]{1,0:T(8,128)(2,1)} custom-call(s32[1]{0:T(128)} %bitcast.3.first_ref, bf16[512,2048]{1,0:T(8,128)(2,1)S(1)} %copy-done.4, bf16[2048,4096]{1,0:T(8,128)(2,1)S(1)} %copy-done.2, bf16[512,512]{1,0:T(8,128)(2,1)S(1)} %collective-permute-done.7.rest_0_, bf16[512,512]{1,0:T(8,128)(2,1)S(1)} %block_product.11.rest_1_.rest_5_), custom_call_target="tpu_custom_call" | custom-call | flops 1000 | bytes 1000 | tf_op jit(solution)/shard_map/block_product/pallas_call | solution.py:42
  67.7 0.0 copy-done.13
  67.7 0.0 collective-permute-start.14
  67.7 0.0 collective-permute-done.3.rest_1_.rest_7_
  67.7 0.0 collective-permute-done.4.rest_2_.rest_8_
  67.8 0.0 collective-permute-done.5.rest_3_.rest_9_
  67.8 0.0 copy-start.9
  67.8 1.6 %low_sums.1.rest_1_.rest_0_ = f32[16,512]{1,0:T(8,128)S(1)} custom-call(s32[24]{0:T(128)S(1)} %get-tuple-element.17.rest_1_.start_ref, s32[24]{0:T(128)S(1)} %get-tuple-element.18.end_ref, bf16[512,2048]{1,0:T(8,128)(2,1)S(1)} %copy-done.4, bf16[6,16,3072]{2,1,0:T(8,128)(2,1)S(1)} %get-tuple-element.19.rest_0_.rest_6_, ...), custom_call_target="tpu_custom_call" | custom-call | flops 1000 | bytes 1000 | tf_op jit(solution)/shard_map/low_sums/pallas_call | solution.py:226
  69.3 0.0 copy-done.9
  69.3 0.0 copy-start.7
  69.4 0.8 copy-done.7
  70.2 0.0 collective-permute-start.11
  70.2 2.6 %collective-permute-start.10 = (f32[16,512]{1,0:T(8,128)S(1)}, f32[16,512]{1,0:T(8,128)S(1)}, u32[]{:S(2)}, u32[]{:S(2)}) collective-permute-start(f32[16,512]{1,0:T(8,128)S(1)} %low_sums.1.rest_1_.rest_0_), channel_id=1, source_target_pairs={{0,2},{1,3},{2,0},{3,1},{4,6},{5,7},{6,4},{7,5},{8,10},{9,11},{10,... | collective-permute-start | bytes 98312 | tf_op jit(solution)/shard_map/ppermute | solution.py:357
  72.8 0.9 collective-permute-start.9
  73.7 0.0 collective-permute-done.12.rest_0_
  73.7 5.8 %copy-done.3 = bf16[2048,4096]{1,0:T(8,128)(2,1)S(1)} copy-done((bf16[2048,4096]{1,0:T(8,128)(2,1)S(1)}, bf16[2048,4096]{1,0:T(8,128)(2,1)}, u32[]{:S(2)}) %copy-start.3) | copy-done | bytes 16777240
  79.5 2.7 %block_product.13.rest_10_ = bf16[512,512]{1,0:T(8,128)(2,1)S(1)} custom-call(s32[1]{0:T(128)} %bitcast.8.first_ref, bf16[512,2048]{1,0:T(8,128)(2,1)S(1)} %copy-done.4, bf16[2048,4096]{1,0:T(8,128)(2,1)S(1)} %copy-done.3, bf16[512,512]{1,0:T(8,128)(2,1)} %collective-permute-done.12.rest_0_, f32[16,512]{1,0:T(8,128)S(1)} %low_sums.1.rest_1_.rest_0_), custom_call_target="tpu_custom_call" | custom-call | flops 1000 | bytes 1000 | tf_op jit(solution)/shard_map/block_product/pallas_call | solution.py:42
  82.2 0.6 collective-permute-start.13
  82.8 0.0 collective-permute-done.11.rest_3_
  82.8 0.0 collective-permute-done.10.rest_2_
  82.8 2.3 %collective-permute-done.9.rest_1_ = f32[16,512]{1,0:T(8,128)S(1)} collective-permute-done((f32[16,512]{1,0:T(8,128)S(1)}, f32[16,512]{1,0:T(8,128)S(1)}, u32[]{:S(2)}, u32[]{:S(2)}) %collective-permute-start.9) | collective-permute-done | bytes 32800 | tf_op jit(solution)/shard_map/ppermute | solution.py:357
  85.1 0.0 copy-done.8
  85.1 0.0 copy-done.12
  85.1 1.3 %adapter_term.1 = (f32[512,512]{1,0:T(8,128)S(1)}, f32[512,512]{1,0:T(8,128)S(1)}) custom-call(s32[24]{0:T(128)S(1)} %get-tuple-element.17.rest_1_.start_ref, s32[24]{0:T(128)S(1)} %get-tuple-element.18.end_ref, f32[16,512]{1,0:T(8,128)S(1)} %low_sums.1.rest_1_.rest_0_, f32[16,512]{1,0:T(8,128)S(1)} %collective-permute-done.9.rest_1_, ...), custom_call_target="tpu_custom_call" | custom-call | flops 1000 | bytes 1000 | tf_op jit(solution)/shard_map/adapter_term/pallas_call | solution.py:272
  86.4 0.0 collective-permute-done.14.rest_0_
  86.4 3.2 %finish.2.rest_1_ = bf16[512,1024]{1,0:T(8,128)(2,1)} custom-call(f32[512,512]{1,0:T(8,128)S(1)} %get-tuple-element.24.term_ref, bf16[512,512]{1,0:T(8,128)(2,1)} %collective-permute-done.14.rest_0_), custom_call_target="tpu_custom_call" | custom-call | flops 20000000000 | bytes 1000 | tf_op jit(solution)/shard_map/finish/pallas_call | solution.py:299
  89.6 7.6 %collective-permute-done.13.rest_0_ = bf16[512,512]{1,0:T(8,128)(2,1)S(1)} collective-permute-done((bf16[512,512]{1,0:T(8,128)(2,1)S(1)}, bf16[512,512]{1,0:T(8,128)(2,1)S(1)}, u32[]{:S(2)}, u32[]{:S(2)}) %collective-permute-start.13) | collective-permute-done | bytes 524320 | tf_op jit(solution)/shard_map/ppermute | solution.py:326
  97.2 1.4 %finish.3 = bf16[512,1024]{1,0:T(8,128)(2,1)} custom-call(f32[512,512]{1,0:T(8,128)S(1)} %get-tuple-element.23.term_ref, bf16[512,512]{1,0:T(8,128)(2,1)S(1)} %collective-permute-done.13.rest_0_, bf16[512,1024]{1,0:T(8,128)(2,1)} %finish.2.rest_1_), custom_call_target="tpu_custom_call", output_to_operand_aliasing={{}: (2, {})} | custom-call | flops 1000 | bytes 1000 | tf_op jit(solution)/shard_map/finish/pallas_call | solution.py:299
  (15 shorter events, 0.0 us)
Async XLA Ops:
  0.0 5.8 %copy-start = (bf16[2048,4096]{1,0:T(8,128)(2,1)S(1)}, bf16[2048,4096]{1,0:T(8,128)(2,1)}, u32[]{:S(2)}) copy-start(bf16[2048,4096]{1,0:T(8,128)(2,1)} %weight_ref.15) | copy-start | bytes 50331652
  5.8 7.7 %copy-start.4 = (bf16[512,2048]{1,0:T(8,128)(2,1)S(1)}, bf16[512,2048]{1,0:T(8,128)(2,1)}, u32[]{:S(2)}) copy-start(bf16[512,2048]{1,0:T(8,128)(2,1)} %rows_ref.17) | copy-start | bytes 6291460
  5.8 7.7 %copy-start.16 = (s32[1,12]{1,0:T(1,128)S(1)}, s32[1,12]{1,0:T(1,128)}, u32[]{:S(2)}) copy-start(s32[1,12]{1,0:T(1,128)} %rest_0_.1) | copy-start | bytes 148
  9.2 28.7 %collective-permute-start.6 = (bf16[512,512]{1,0:T(8,128)(2,1)}, bf16[512,512]{1,0:T(8,128)(2,1)}, u32[]{:S(2)}, u32[]{:S(2)}) collective-permute-start(bf16[512,512]{1,0:T(8,128)(2,1)} %first_product.1.rest_1_), channel_id=1, source_target_pairs={{0,1},{1,2},{2,3},{3,0},{4,7},{5,4},{6,5},{7,6},{8,9},{9,10},{10,1... | collective-permute-start | bytes 1572872 | tf_op jit(solution)/shard_map/ppermute | solution.py:326
  13.5 5.8 %copy-start.1 = (bf16[2048,4096]{1,0:T(8,128)(2,1)S(1)}, bf16[2048,4096]{1,0:T(8,128)(2,1)}, u32[]{:S(2)}) copy-start(bf16[2048,4096]{1,0:T(8,128)(2,1)} %weight_ref.15) | copy-start | bytes 50331652
  19.2 6.3 %copy-start.15 = (s32[512]{0:T(512)S(1)}, s32[512]{0:T(512)}, u32[]{:S(2)}) copy-start(s32[512]{0:T(512)} %table_ref.1) | copy-start | bytes 6148
  19.2 6.3 %copy-start.17 = (s32[1,12]{1,0:T(1,128)S(1)}, s32[1,12]{1,0:T(1,128)}, u32[]{:S(2)}) copy-start(s32[1,12]{1,0:T(1,128)} %lens_ref.1) | copy-start | bytes 148
  22.1 3.4 %collective-permute-start.2 = (s32[1,12]{1,0:T(1,128)S(1)}, s32[1,12]{1,0:T(1,128)S(1)}, u32[]{:S(2)}, u32[]{:S(2)}) collective-permute-start(s32[1,12]{1,0:T(1,128)S(1)} %get-tuple-element.15.rest_0_), channel_id=1, source_target_pairs={{0,12},{4,8},{8,4},{12,0},{1,13},{5,9},{9,5},{13,1},{2,14},{6,10},... | collective-permute-start | bytes 152 | tf_op jit(solution)/shard_map/ppermute | solution.py:344
  22.2 3.3 %collective-permute-start.1 = (s32[1,12]{1,0:T(1,128)S(1)}, s32[1,12]{1,0:T(1,128)S(1)}, u32[]{:S(2)}, u32[]{:S(2)}) collective-permute-start(s32[1,12]{1,0:T(1,128)S(1)} %get-tuple-element.15.rest_0_), channel_id=1, source_target_pairs={{0,8},{4,12},{8,0},{12,4},{1,9},{5,13},{9,1},{13,5},{2,10},{6,14},... | collective-permute-start | bytes 152 | tf_op jit(solution)/shard_map/ppermute | solution.py:344
  23.4 2.1 %collective-permute-start = (s32[1,12]{1,0:T(1,128)S(1)}, s32[1,12]{1,0:T(1,128)S(1)}, u32[]{:S(2)}, u32[]{:S(2)}) collective-permute-start(s32[1,12]{1,0:T(1,128)S(1)} %get-tuple-element.15.rest_0_), channel_id=1, source_target_pairs={{0,4},{4,0},{8,12},{12,8},{1,5},{5,1},{9,13},{13,9},{2,6},{6,2},{1... | collective-permute-start | bytes 152 | tf_op jit(solution)/shard_map/ppermute | solution.py:344
  24.3 24.6 %collective-permute-start.8 = (bf16[512,512]{1,0:T(8,128)(2,1)}, bf16[512,512]{1,0:T(8,128)(2,1)}, u32[]{:S(2)}, u32[]{:S(2)}) collective-permute-start(bf16[512,512]{1,0:T(8,128)(2,1)} %get-tuple-element.16.rest_6_), channel_id=1, source_target_pairs={{0,3},{1,0},{2,1},{3,2},{4,5},{5,6},{6,7},{7,4},{8,11},{9,8},{10,9... | collective-permute-start | bytes 1572872 | tf_op jit(solution)/shard_map/ppermute | solution.py:326
  25.5 3.4 %copy-start.5 = (bf16[128,16,2048]{2,1,0:T(8,128)(2,1)S(1)}, bf16[128,16,2048]{2,1,0:T(8,128)(2,1)}, u32[]{:S(2)}) copy-start(bf16[128,16,2048]{2,1,0:T(8,128)(2,1)} %rest_4_.1) | copy-start | bytes 25165828
  28.9 2.2 %copy-start.6 = (bf16[128,16,1024]{2,1,0:T(8,128)(2,1)S(1)}, bf16[128,16,1024]{2,1,0:T(8,128)(2,1)}, u32[]{:S(2)}) copy-start(bf16[128,16,1024]{2,1,0:T(8,128)(2,1)} %rest_5_.1) | copy-start | bytes 12582916
  34.4 33.4 %collective-permute-start.3 = (bf16[6,16,3072]{2,1,0:T(8,128)(2,1)S(1)}, bf16[6,16,3072]{2,1,0:T(8,128)(2,1)S(1)}, u32[]{:S(2)}, u32[]{:S(2)}) collective-permute-start(bf16[6,16,3072]{2,1,0:T(8,128)(2,1)S(1)} %get-tuple-element.20), channel_id=1, source_target_pairs={{0,4},{4,0},{8,12},{12,8},{1,5},{5,1},{9,13},{13,9},{2,6},{6,2},{1... | collective-permute-start | bytes 1769480 | tf_op jit(solution)/shard_map/ppermute | solution.py:347
  36.2 31.5 %collective-permute-start.4 = (bf16[6,16,3072]{2,1,0:T(8,128)(2,1)S(1)}, bf16[6,16,3072]{2,1,0:T(8,128)(2,1)S(1)}, u32[]{:S(2)}, u32[]{:S(2)}) collective-permute-start(bf16[6,16,3072]{2,1,0:T(8,128)(2,1)S(1)} %get-tuple-element.21), channel_id=1, source_target_pairs={{0,8},{4,12},{8,0},{12,4},{1,9},{5,13},{9,1},{13,5},{2,10},{6,14},... | collective-permute-start | bytes 1769480 | tf_op jit(solution)/shard_map/ppermute | solution.py:347
  36.5 31.3 %collective-permute-start.5 = (bf16[6,16,3072]{2,1,0:T(8,128)(2,1)S(1)}, bf16[6,16,3072]{2,1,0:T(8,128)(2,1)S(1)}, u32[]{:S(2)}, u32[]{:S(2)}) collective-permute-start(bf16[6,16,3072]{2,1,0:T(8,128)(2,1)S(1)} %get-tuple-element.22), channel_id=1, source_target_pairs={{0,12},{4,8},{8,4},{12,0},{1,13},{5,9},{9,5},{13,1},{2,14},{6,10},... | collective-permute-start | bytes 1769480 | tf_op jit(solution)/shard_map/ppermute | solution.py:347
  38.0 5.8 %copy-start.2 = (bf16[2048,4096]{1,0:T(8,128)(2,1)S(1)}, bf16[2048,4096]{1,0:T(8,128)(2,1)}, u32[]{:S(2)}) copy-start(bf16[2048,4096]{1,0:T(8,128)(2,1)} %weight_ref.15) | copy-start | bytes 50331652
  46.3 18.9 %collective-permute-start.7 = (bf16[512,512]{1,0:T(8,128)(2,1)S(1)}, bf16[512,512]{1,0:T(8,128)(2,1)S(1)}, u32[]{:S(2)}, u32[]{:S(2)}) collective-permute-start(bf16[512,512]{1,0:T(8,128)(2,1)S(1)} %block_product.8.rest_0_), channel_id=1, source_target_pairs={{0,1},{1,2},{2,3},{3,0},{4,7},{5,4},{6,5},{7,6},{8,9},{9,10},{10,1... | collective-permute-start | bytes 1572872 | tf_op jit(solution)/shard_map/ppermute | solution.py:326
  48.9 3.3 %copy-start.11 = (bf16[512,512]{1,0:T(8,128)(2,1)}, bf16[512,512]{1,0:T(8,128)(2,1)S(1)}, u32[]{:S(2)}) copy-start(bf16[512,512]{1,0:T(8,128)(2,1)S(1)} %block_product.9.rest_1_.rest_4_) | copy-start | bytes 1572868
  52.2 21.5 %collective-permute-start.12 = (bf16[512,512]{1,0:T(8,128)(2,1)}, bf16[512,512]{1,0:T(8,128)(2,1)}, u32[]{:S(2)}, u32[]{:S(2)}) collective-permute-start(bf16[512,512]{1,0:T(8,128)(2,1)} %block_product.10.rest_0_), channel_id=1, source_target_pairs={{0,3},{1,0},{2,1},{3,2},{4,5},{5,6},{6,7},{7,4},{8,11},{9,8},{10,9... | collective-permute-start | bytes 1572872 | tf_op jit(solution)/shard_map/ppermute | solution.py:326
  54.8 12.9 %copy-start.13 = (bf16[512,512]{1,0:T(8,128)(2,1)}, bf16[512,512]{1,0:T(8,128)(2,1)S(1)}, u32[]{:S(2)}) copy-start(bf16[512,512]{1,0:T(8,128)(2,1)S(1)} %block_product.11.rest_1_.rest_5_) | copy-start | bytes 1572868
  67.7 18.7 %collective-permute-start.14 = (bf16[512,512]{1,0:T(8,128)(2,1)}, bf16[512,512]{1,0:T(8,128)(2,1)}, u32[]{:S(2)}, u32[]{:S(2)}) collective-permute-start(bf16[512,512]{1,0:T(8,128)(2,1)} %block_product.12.rest_4_), channel_id=1, source_target_pairs={{0,1},{1,2},{2,3},{3,0},{4,7},{5,4},{6,5},{7,6},{8,9},{9,10},{10,1... | collective-permute-start | bytes 1572872 | tf_op jit(solution)/shard_map/ppermute | solution.py:326
  67.8 1.6 %copy-start.9 = (bf16[6,16,3072]{2,1,0:T(8,128)(2,1)}, bf16[6,16,3072]{2,1,0:T(8,128)(2,1)S(1)}, u32[]{:S(2)}) copy-start(bf16[6,16,3072]{2,1,0:T(8,128)(2,1)S(1)} %collective-permute-done.5.rest_3_.rest_9_) | copy-start | bytes 1769476
  69.3 0.8 copy-start.7
  70.2 12.7 %collective-permute-start.11 = (f32[16,512]{1,0:T(8,128)S(1)}, f32[16,512]{1,0:T(8,128)S(1)}, u32[]{:S(2)}, u32[]{:S(2)}) collective-permute-start(f32[16,512]{1,0:T(8,128)S(1)} %low_sums.1.rest_1_.rest_0_), channel_id=1, source_target_pairs={{0,3},{1,2},{2,1},{3,0},{4,7},{5,6},{6,5},{7,4},{8,11},{9,10},{10,... | collective-permute-start | bytes 98312 | tf_op jit(solution)/shard_map/ppermute | solution.py:357
  70.2 12.7 %collective-permute-start.10 = (f32[16,512]{1,0:T(8,128)S(1)}, f32[16,512]{1,0:T(8,128)S(1)}, u32[]{:S(2)}, u32[]{:S(2)}) collective-permute-start(f32[16,512]{1,0:T(8,128)S(1)} %low_sums.1.rest_1_.rest_0_), channel_id=1, source_target_pairs={{0,2},{1,3},{2,0},{3,1},{4,6},{5,7},{6,4},{7,5},{8,10},{9,11},{10,... | collective-permute-start | bytes 98312 | tf_op jit(solution)/shard_map/ppermute | solution.py:357
  72.8 12.3 %collective-permute-start.9 = (f32[16,512]{1,0:T(8,128)S(1)}, f32[16,512]{1,0:T(8,128)S(1)}, u32[]{:S(2)}, u32[]{:S(2)}) collective-permute-start(f32[16,512]{1,0:T(8,128)S(1)} %low_sums.1.rest_1_.rest_0_), channel_id=1, source_target_pairs={{0,1},{1,0},{2,3},{3,2},{4,5},{5,4},{6,7},{7,6},{8,9},{9,8},{10,11... | collective-permute-start | bytes 98312 | tf_op jit(solution)/shard_map/ppermute | solution.py:357
  73.7 5.8 %copy-start.3 = (bf16[2048,4096]{1,0:T(8,128)(2,1)S(1)}, bf16[2048,4096]{1,0:T(8,128)(2,1)}, u32[]{:S(2)}) copy-start(bf16[2048,4096]{1,0:T(8,128)(2,1)} %weight_ref.15) | copy-start | bytes 50331652
  79.5 5.6 %copy-start.8 = (bf16[6,16,3072]{2,1,0:T(8,128)(2,1)S(1)}, bf16[6,16,3072]{2,1,0:T(8,128)(2,1)}, u32[]{:S(2)}) copy-start(bf16[6,16,3072]{2,1,0:T(8,128)(2,1)} %copy-done.7) | copy-start | bytes 1769476
  79.5 5.6 %copy-start.10 = (bf16[6,16,3072]{2,1,0:T(8,128)(2,1)S(1)}, bf16[6,16,3072]{2,1,0:T(8,128)(2,1)}, u32[]{:S(2)}) copy-start(bf16[6,16,3072]{2,1,0:T(8,128)(2,1)} %copy-done.9) | copy-start | bytes 1769476
  79.5 5.6 %copy-start.12 = (bf16[512,512]{1,0:T(8,128)(2,1)S(1)}, bf16[512,512]{1,0:T(8,128)(2,1)}, u32[]{:S(2)}) copy-start(bf16[512,512]{1,0:T(8,128)(2,1)} %copy-done.11) | copy-start | bytes 1572868
  79.5 5.6 %copy-start.14 = (bf16[512,512]{1,0:T(8,128)(2,1)S(1)}, bf16[512,512]{1,0:T(8,128)(2,1)}, u32[]{:S(2)}) copy-start(bf16[512,512]{1,0:T(8,128)(2,1)} %copy-done.13) | copy-start | bytes 1572868
  82.2 15.0 %collective-permute-start.13 = (bf16[512,512]{1,0:T(8,128)(2,1)S(1)}, bf16[512,512]{1,0:T(8,128)(2,1)S(1)}, u32[]{:S(2)}, u32[]{:S(2)}) collective-permute-start(bf16[512,512]{1,0:T(8,128)(2,1)S(1)} %block_product.13.rest_10_), channel_id=1, source_target_pairs={{0,3},{1,0},{2,1},{3,2},{4,5},{5,6},{6,7},{7,4},{8,11},{9,8},{10,9... | collective-permute-start | bytes 1572872 | tf_op jit(solution)/shard_map/ppermute | solution.py:326

commit v10 on v9

--- a/solution.py
+++ b/solution.py
@@ -310,6 +310,9 @@
 
 
 def local(req_total, tp_total, rows, weight, down, up, table, ids, lens):
+    weight = pltpu.with_memory_space_constraint(weight, pltpu.HBM)
+    down = pltpu.with_memory_space_constraint(down, pltpu.HBM)
+    up = pltpu.with_memory_space_constraint(up, pltpu.HBM)
     rank = down.shape[1]
     cols = up.shape[2]
     width = cols // PIECES

time: 99.1 us -> 81.6 us (0.82)
  the two profiles are of different devices: /device:TPU:1 before, /device:TPU:0 now
where the time goes in v10:
time: 81.6 us; the launch traced here: 81.2 us
  Pallas kernels  36.4 us (45%)
  starting transfers between devices  31.5 us (39%)
  waiting for transfers between devices  12.2 us (15%)
  local copies, waits for them, and re-layouts  0.85 us (1%)
    pallas_call x7, Pallas kernels, block_product(): pl.pallas_call(functools.partial(product_kernel, len(addends), with_ids),...  21.5 us
    ppermute x6, starting transfers between devices, move(): return lax.ppermute(value, ('req', 'tp'), pairs)  18.6 us
    ppermute x3, starting transfers between devices, local(): lows.append(lax.ppermute(low, 'tp', pairs))  7.8 us
    ppermute x6, waiting for transfers between devices, move(): return lax.ppermute(value, ('req', 'tp'), pairs)  5.73 us
    pallas_call x2, Pallas kernels, finish(): pl.pallas_call(functools.partial(finish_kernel, len(arrivals)), grid=(row...  4.6 us
    ppermute x3, waiting for transfers between devices, local(): lows.append(lax.ppermute(low, 'tp', pairs))  4.17 us
    pallas_call x1, Pallas kernels, pick_adapters(): pl.pallas_call(functools.partial(pick_kernel, peers, len(after)), in_spec...  3.89 us
    pallas_call x1, Pallas kernels, first_product(): pl.pallas_call(functools.partial(first_kernel, chunk), in_specs=[pl.Block...  3.62 us
  transfers between devices with their start and end apart: 15, of which 5 were waited for; matrix products, arithmetic and copies ran while one was open for 0% of the time, Pallas kernels for 39%

profile of v10, /device:TPU:0, one launch (start us, length us, event | category | flops | bytes accessed | tf_op | source)
XLA Modules:
  0.0 81.2 jit_solution(12344184456477230219)
XLA Ops:
  0.0 0.0 copy-start
  0.0 0.0 copy-start.10
  0.0 3.6 %first_product.1.rest_1_ = bf16[512,512]{1,0:T(8,128)(2,1)} custom-call(s32[1]{0:T(128)} %bitcast.2.first_ref, bf16[512,2048]{1,0:T(8,128)(2,1)} %rows_ref.17, bf16[2048,4096]{1,0:T(8,128)(2,1)} %weight_ref.15), custom_call_target="tpu_custom_call" | custom-call | flops 1000 | bytes 1000 | tf_op jit(solution)/shard_map/first_product/pallas_call | solution.py:95
  3.6 3.1 %collective-permute-start.6 = (bf16[512,512]{1,0:T(8,128)(2,1)}, bf16[512,512]{1,0:T(8,128)(2,1)}, u32[]{:S(2)}, u32[]{:S(2)}) collective-permute-start(bf16[512,512]{1,0:T(8,128)(2,1)} %first_product.1.rest_1_), channel_id=1, source_target_pairs={{0,1},{1,2},{2,3},{3,0},{4,7},{5,4},{6,5},{7,6},{8,9},{9,10},{10,1... | collective-permute-start | bytes 1572872 | tf_op jit(solution)/shard_map/ppermute | solution.py:329
  6.7 0.0 copy-done
  6.7 0.0 copy-done.10
  6.7 0.0 copy-start.9
  6.7 0.0 copy-start.11
  6.7 3.5 %block_product.7 = (bf16[512,512]{1,0:T(8,128)(2,1)}, s32[1,12]{1,0:T(1,128)S(1)}) custom-call(s32[1]{0:T(128)} %bitcast.1.first_ref, bf16[512,2048]{1,0:T(8,128)(2,1)S(1)} %copy-done, bf16[2048,4096]{1,0:T(8,128)(2,1)} %weight_ref.15, s32[1,12]{1,0:T(1,128)S(1)} %copy-done.10, bf16[512,512]{1,0:T(8,128)(2,1)} %first_product.1.rest_1_), custom_call_target="tpu_custom_call" | custom-call | flops 1000 | bytes 1000 | tf_op jit(solution)/shard_map/block_product/pallas_call | solution.py:42
  10.2 2.7 %collective-permute-start.2 = (s32[1,12]{1,0:T(1,128)S(1)}, s32[1,12]{1,0:T(1,128)S(1)}, u32[]{:S(2)}, u32[]{:S(2)}) collective-permute-start(s32[1,12]{1,0:T(1,128)S(1)} %get-tuple-element.15.rest_0_), channel_id=1, source_target_pairs={{0,12},{4,8},{8,4},{12,0},{1,13},{5,9},{9,5},{13,1},{2,14},{6,10},... | collective-permute-start | bytes 152 | tf_op jit(solution)/shard_map/ppermute | solution.py:347
  12.9 0.5 collective-permute-start.1
  13.4 0.0 collective-permute-start
  13.4 0.8 collective-permute-start.8
  14.2 0.0 collective-permute-done.2.rest_3_
  14.2 2.2 %collective-permute-done.1.rest_2_ = s32[1,12]{1,0:T(1,128)S(1)} collective-permute-done((s32[1,12]{1,0:T(1,128)S(1)}, s32[1,12]{1,0:T(1,128)S(1)}, u32[]{:S(2)}, u32[]{:S(2)}) %collective-permute-start.1) | collective-permute-done | bytes 80 | tf_op jit(solution)/shard_map/ppermute | solution.py:347
  16.4 0.0 collective-permute-done.rest_1_
  16.4 0.0 copy-done.9
  16.4 0.0 copy-done.11
  16.5 3.9 %pick_adapters.1 = (bf16[6,16,3072]{2,1,0:T(8,128)(2,1)S(1)}, bf16[6,16,3072]{2,1,0:T(8,128)(2,1)S(1)}, bf16[6,16,3072]{2,1,0:T(8,128)(2,1)S(1)}, bf16[6,16,3072...) custom-call(s32[1]{0:T(128)} %bitcast.me_ref, s32[512]{0:T(512)S(1)} %copy-done.9, s32[1,12]{1,0:T(1,128)S(1)} %copy-done.11, ...), custom_call_target="tpu_custom_call" | custom-call | flops 1000 | bytes 1000 | tf_op jit(solution)/shard_map/pick_adapters/pallas_call | solution.py:184
  20.3 0.1 collective-permute-start.3
  20.4 0.5 collective-permute-start.4
  20.9 1.4 %collective-permute-start.5 = (bf16[6,16,3072]{2,1,0:T(8,128)(2,1)S(1)}, bf16[6,16,3072]{2,1,0:T(8,128)(2,1)S(1)}, u32[]{:S(2)}, u32[]{:S(2)}) collective-permute-start(bf16[6,16,3072]{2,1,0:T(8,128)(2,1)S(1)} %get-tuple-element.22), channel_id=1, source_target_pairs={{0,12},{4,8},{8,4},{12,0},{1,13},{5,9},{9,5},{13,1},{2,14},{6,10},... | collective-permute-start | bytes 1769480 | tf_op jit(solution)/shard_map/ppermute | solution.py:350
  22.3 0.0 collective-permute-done.6.rest_0_
  22.3 2.8 %block_product.8.rest_0_ = bf16[512,512]{1,0:T(8,128)(2,1)S(1)} custom-call(s32[1]{0:T(128)} %bitcast.4.first_ref, bf16[512,2048]{1,0:T(8,128)(2,1)S(1)} %copy-done, bf16[2048,4096]{1,0:T(8,128)(2,1)} %weight_ref.15, bf16[512,512]{1,0:T(8,128)(2,1)} %collective-permute-done.6.rest_0_, s32[24]{0:T(128)S(1)} %get-tuple-element.17.rest_1_.start_ref), custom_call_target="tpu_custom_call" | custom-call | flops 1000 | bytes 1000 | tf_op jit(solution)/shard_map/block_product/pallas_call | solution.py:42
  25.1 3.4 %collective-permute-start.7 = (bf16[512,512]{1,0:T(8,128)(2,1)S(1)}, bf16[512,512]{1,0:T(8,128)(2,1)S(1)}, u32[]{:S(2)}, u32[]{:S(2)}) collective-permute-start(bf16[512,512]{1,0:T(8,128)(2,1)S(1)} %block_product.8.rest_0_), channel_id=1, source_target_pairs={{0,1},{1,2},{2,3},{3,0},{4,7},{5,4},{6,5},{7,6},{8,9},{9,10},{10,1... | collective-permute-start | bytes 1572872 | tf_op jit(solution)/shard_map/ppermute | solution.py:329
  28.4 2.7 %block_product.9.rest_1_.rest_4_ = bf16[512,512]{1,0:T(8,128)(2,1)S(1)} custom-call(s32[1]{0:T(128)} %bitcast.7.first_ref, bf16[512,2048]{1,0:T(8,128)(2,1)S(1)} %copy-done, bf16[2048,4096]{1,0:T(8,128)(2,1)} %weight_ref.15, bf16[512,512]{1,0:T(8,128)(2,1)S(1)} %block_product.8.rest_0_), custom_call_target="tpu_custom_call" | custom-call | flops 20000000000 | bytes 1000 | tf_op jit(solution)/shard_map/block_product/pallas_call | solution.py:42
  31.1 0.0 copy-start.5
  31.1 0.2 collective-permute-done.8.rest_0_
  31.3 3.5 %block_product.10.rest_0_ = bf16[512,512]{1,0:T(8,128)(2,1)} custom-call(s32[1]{0:T(128)} %bitcast.6.first_ref, bf16[512,2048]{1,0:T(8,128)(2,1)S(1)} %copy-done, bf16[2048,4096]{1,0:T(8,128)(2,1)} %weight_ref.15, bf16[512,512]{1,0:T(8,128)(2,1)} %collective-permute-done.8.rest_0_, bf16[512,512]{1,0:T(8,128)(2,1)S(1)} %block_product.9.rest_1_.rest_4_), custom_call_target="tpu_custom_call" | custom-call | flops 1000 | bytes 1000 | tf_op jit(solution)/shard_map/block_product/pallas_call | solution.py:42
  34.8 0.0 copy-done.5
  34.8 5.0 %collective-permute-start.12 = (bf16[512,512]{1,0:T(8,128)(2,1)}, bf16[512,512]{1,0:T(8,128)(2,1)}, u32[]{:S(2)}, u32[]{:S(2)}) collective-permute-start(bf16[512,512]{1,0:T(8,128)(2,1)} %block_product.10.rest_0_), channel_id=1, source_target_pairs={{0,3},{1,0},{2,1},{3,2},{4,5},{5,6},{6,7},{7,4},{8,11},{9,8},{10,9... | collective-permute-start | bytes 1572872 | tf_op jit(solution)/shard_map/ppermute | solution.py:329
  39.8 2.7 %block_product.11.rest_1_.rest_5_ = bf16[512,512]{1,0:T(8,128)(2,1)S(1)} custom-call(s32[1]{0:T(128)} %bitcast.5.first_ref, bf16[512,2048]{1,0:T(8,128)(2,1)S(1)} %copy-done, bf16[2048,4096]{1,0:T(8,128)(2,1)} %weight_ref.15, bf16[512,512]{1,0:T(8,128)(2,1)} %block_product.10.rest_0_), custom_call_target="tpu_custom_call" | custom-call | flops 20000000000 | bytes 1000 | tf_op jit(solution)/shard_map/block_product/pallas_call | solution.py:42
  42.5 0.0 copy-start.7
  42.5 3.9 %collective-permute-done.7.rest_0_ = bf16[512,512]{1,0:T(8,128)(2,1)S(1)} collective-permute-done((bf16[512,512]{1,0:T(8,128)(2,1)S(1)}, bf16[512,512]{1,0:T(8,128)(2,1)S(1)}, u32[]{:S(2)}, u32[]{:S(2)}) %collective-permute-start.7) | collective-permute-done | bytes 524320 | tf_op jit(solution)/shard_map/ppermute | solution.py:329
  46.4 3.4 %block_product.12.rest_4_ = bf16[512,512]{1,0:T(8,128)(2,1)} custom-call(s32[1]{0:T(128)} %bitcast.3.first_ref, bf16[512,2048]{1,0:T(8,128)(2,1)S(1)} %copy-done, bf16[2048,4096]{1,0:T(8,128)(2,1)} %weight_ref.15, bf16[512,512]{1,0:T(8,128)(2,1)S(1)} %collective-permute-done.7.rest_0_, bf16[512,512]{1,0:T(8,128)(2,1)S(1)} %block_product.11.rest_1_.rest_5_), custom_call_target="tpu_custom_call" | custom-call | flops 1000 | bytes 1000 | tf_op jit(solution)/shard_map/block_product/pallas_call | solution.py:42
  49.8 0.0 copy-done.7
  49.8 3.1 %collective-permute-start.14 = (bf16[512,512]{1,0:T(8,128)(2,1)}, bf16[512,512]{1,0:T(8,128)(2,1)}, u32[]{:S(2)}, u32[]{:S(2)}) collective-permute-start(bf16[512,512]{1,0:T(8,128)(2,1)} %block_product.12.rest_4_), channel_id=1, source_target_pairs={{0,1},{1,2},{2,3},{3,0},{4,7},{5,4},{6,5},{7,6},{8,9},{9,10},{10,1... | collective-permute-start | bytes 1572872 | tf_op jit(solution)/shard_map/ppermute | solution.py:329
  52.9 0.0 collective-permute-done.3.rest_1_.rest_7_
  52.9 0.0 collective-permute-done.4.rest_2_.rest_8_
  52.9 0.0 collective-permute-done.5.rest_3_.rest_9_
  52.9 0.0 copy-start.3
  53.0 1.6 %low_sums.1.rest_1_.rest_0_ = f32[16,512]{1,0:T(8,128)S(1)} custom-call(s32[24]{0:T(128)S(1)} %get-tuple-element.17.rest_1_.start_ref, s32[24]{0:T(128)S(1)} %get-tuple-element.18.end_ref, bf16[512,2048]{1,0:T(8,128)(2,1)S(1)} %copy-done, bf16[6,16,3072]{2,1,0:T(8,128)(2,1)S(1)} %get-tuple-element.19.rest_0_.rest_6_, ...), custom_call_target="tpu_custom_call" | custom-call | flops 1000 | bytes 1000 | tf_op jit(solution)/shard_map/low_sums/pallas_call | solution.py:226
  54.5 0.0 copy-done.3
  54.5 0.0 copy-start.1
  54.5 0.8 copy-done.1
  55.3 6.7 %collective-permute-start.11 = (f32[16,512]{1,0:T(8,128)S(1)}, f32[16,512]{1,0:T(8,128)S(1)}, u32[]{:S(2)}, u32[]{:S(2)}) collective-permute-start(f32[16,512]{1,0:T(8,128)S(1)} %low_sums.1.rest_1_.rest_0_), channel_id=1, source_target_pairs={{0,3},{1,2},{2,1},{3,0},{4,7},{5,6},{6,5},{7,4},{8,11},{9,10},{10,... | collective-permute-start | bytes 98312 | tf_op jit(solution)/shard_map/ppermute | solution.py:360
  62.0 0.5 collective-permute-start.10
  62.6 0.6 collective-permute-start.9
  63.1 0.0 collective-permute-done.12.rest_0_
  63.2 0.0 copy-start.8
  63.2 2.9 %block_product.13.rest_10_ = bf16[512,512]{1,0:T(8,128)(2,1)S(1)} custom-call(s32[1]{0:T(128)} %bitcast.8.first_ref, bf16[512,2048]{1,0:T(8,128)(2,1)S(1)} %copy-done, bf16[2048,4096]{1,0:T(8,128)(2,1)} %weight_ref.15, bf16[512,512]{1,0:T(8,128)(2,1)} %collective-permute-done.12.rest_0_, f32[16,512]{1,0:T(8,128)S(1)} %low_sums.1.rest_1_.rest_0_), custom_call_target="tpu_custom_call" | custom-call | flops 1000 | bytes 1000 | tf_op jit(solution)/shard_map/block_product/pallas_call | solution.py:42
  66.1 3.3 %collective-permute-start.13 = (bf16[512,512]{1,0:T(8,128)(2,1)S(1)}, bf16[512,512]{1,0:T(8,128)(2,1)S(1)}, u32[]{:S(2)}, u32[]{:S(2)}) collective-permute-start(bf16[512,512]{1,0:T(8,128)(2,1)S(1)} %block_product.13.rest_10_), channel_id=1, source_target_pairs={{0,3},{1,0},{2,1},{3,2},{4,5},{5,6},{6,7},{7,4},{8,11},{9,8},{10,9... | collective-permute-start | bytes 1572872 | tf_op jit(solution)/shard_map/ppermute | solution.py:329
  69.4 0.0 collective-permute-done.11.rest_3_
  69.4 4.2 %collective-permute-done.10.rest_2_ = f32[16,512]{1,0:T(8,128)S(1)} collective-permute-done((f32[16,512]{1,0:T(8,128)S(1)}, f32[16,512]{1,0:T(8,128)S(1)}, u32[]{:S(2)}, u32[]{:S(2)}) %collective-permute-start.10) | collective-permute-done | bytes 32800 | tf_op jit(solution)/shard_map/ppermute | solution.py:360
  73.6 0.0 collective-permute-done.9.rest_1_
  73.6 0.0 copy-done.2
  73.6 0.0 copy-done.4
  73.6 0.0 copy-done.6
  73.6 0.0 copy-done.8
  73.6 1.3 %adapter_term.1 = (f32[512,512]{1,0:T(8,128)S(1)}, f32[512,512]{1,0:T(8,128)S(1)}) custom-call(s32[24]{0:T(128)S(1)} %get-tuple-element.17.rest_1_.start_ref, s32[24]{0:T(128)S(1)} %get-tuple-element.18.end_ref, f32[16,512]{1,0:T(8,128)S(1)} %low_sums.1.rest_1_.rest_0_, f32[16,512]{1,0:T(8,128)S(1)} %collective-permute-done.9.rest_1_, ...), custom_call_target="tpu_custom_call" | custom-call | flops 1000 | bytes 1000 | tf_op jit(solution)/shard_map/adapter_term/pallas_call | solution.py:272
  74.9 0.0 collective-permute-done.14.rest_0_
  74.9 3.2 %finish.2.rest_1_ = bf16[512,1024]{1,0:T(8,128)(2,1)} custom-call(f32[512,512]{1,0:T(8,128)S(1)} %get-tuple-element.24.term_ref, bf16[512,512]{1,0:T(8,128)(2,1)} %collective-permute-done.14.rest_0_), custom_call_target="tpu_custom_call" | custom-call | flops 20000000000 | bytes 1000 | tf_op jit(solution)/shard_map/finish/pallas_call | solution.py:299
  78.1 1.6 %collective-permute-done.13.rest_0_ = bf16[512,512]{1,0:T(8,128)(2,1)S(1)} collective-permute-done((bf16[512,512]{1,0:T(8,128)(2,1)S(1)}, bf16[512,512]{1,0:T(8,128)(2,1)S(1)}, u32[]{:S(2)}, u32[]{:S(2)}) %collective-permute-start.13) | collective-permute-done | bytes 524320 | tf_op jit(solution)/shard_map/ppermute | solution.py:329
  79.8 1.4 %finish.3 = bf16[512,1024]{1,0:T(8,128)(2,1)} custom-call(f32[512,512]{1,0:T(8,128)S(1)} %get-tuple-element.23.term_ref, bf16[512,512]{1,0:T(8,128)(2,1)S(1)} %collective-permute-done.13.rest_0_, bf16[512,1024]{1,0:T(8,128)(2,1)} %finish.2.rest_1_), custom_call_target="tpu_custom_call", output_to_operand_aliasing={{}: (2, {})} | custom-call | flops 1000 | bytes 1000 | tf_op jit(solution)/shard_map/finish/pallas_call | solution.py:299
  (3 shorter events, 0.0 us)
Async XLA Ops:
  0.0 6.7 %copy-start = (bf16[512,2048]{1,0:T(8,128)(2,1)S(1)}, bf16[512,2048]{1,0:T(8,128)(2,1)}, u32[]{:S(2)}) copy-start(bf16[512,2048]{1,0:T(8,128)(2,1)} %rows_ref.17) | copy-start | bytes 6291460
  0.0 6.7 %copy-start.10 = (s32[1,12]{1,0:T(1,128)S(1)}, s32[1,12]{1,0:T(1,128)}, u32[]{:S(2)}) copy-start(s32[1,12]{1,0:T(1,128)} %rest_0_.1) | copy-start | bytes 148
  3.6 18.7 %collective-permute-start.6 = (bf16[512,512]{1,0:T(8,128)(2,1)}, bf16[512,512]{1,0:T(8,128)(2,1)}, u32[]{:S(2)}, u32[]{:S(2)}) collective-permute-start(bf16[512,512]{1,0:T(8,128)(2,1)} %first_product.1.rest_1_), channel_id=1, source_target_pairs={{0,1},{1,2},{2,3},{3,0},{4,7},{5,4},{6,5},{7,6},{8,9},{9,10},{10,1... | collective-permute-start | bytes 1572872 | tf_op jit(solution)/shard_map/ppermute | solution.py:329
  6.7 9.7 %copy-start.9 = (s32[512]{0:T(512)S(1)}, s32[512]{0:T(512)}, u32[]{:S(2)}) copy-start(s32[512]{0:T(512)} %table_ref.1) | copy-start | bytes 6148
  6.7 9.7 %copy-start.11 = (s32[1,12]{1,0:T(1,128)S(1)}, s32[1,12]{1,0:T(1,128)}, u32[]{:S(2)}) copy-start(s32[1,12]{1,0:T(1,128)} %lens_ref.1) | copy-start | bytes 148
  10.2 4.0 %collective-permute-start.2 = (s32[1,12]{1,0:T(1,128)S(1)}, s32[1,12]{1,0:T(1,128)S(1)}, u32[]{:S(2)}, u32[]{:S(2)}) collective-permute-start(s32[1,12]{1,0:T(1,128)S(1)} %get-tuple-element.15.rest_0_), channel_id=1, source_target_pairs={{0,12},{4,8},{8,4},{12,0},{1,13},{5,9},{9,5},{13,1},{2,14},{6,10},... | collective-permute-start | bytes 152 | tf_op jit(solution)/shard_map/ppermute | solution.py:347
  12.9 3.5 %collective-permute-start.1 = (s32[1,12]{1,0:T(1,128)S(1)}, s32[1,12]{1,0:T(1,128)S(1)}, u32[]{:S(2)}, u32[]{:S(2)}) collective-permute-start(s32[1,12]{1,0:T(1,128)S(1)} %get-tuple-element.15.rest_0_), channel_id=1, source_target_pairs={{0,8},{4,12},{8,0},{12,4},{1,9},{5,13},{9,1},{13,5},{2,10},{6,14},... | collective-permute-start | bytes 152 | tf_op jit(solution)/shard_map/ppermute | solution.py:347
  13.4 3.0 %collective-permute-start = (s32[1,12]{1,0:T(1,128)S(1)}, s32[1,12]{1,0:T(1,128)S(1)}, u32[]{:S(2)}, u32[]{:S(2)}) collective-permute-start(s32[1,12]{1,0:T(1,128)S(1)} %get-tuple-element.15.rest_0_), channel_id=1, source_target_pairs={{0,4},{4,0},{8,12},{12,8},{1,5},{5,1},{9,13},{13,9},{2,6},{6,2},{1... | collective-permute-start | bytes 152 | tf_op jit(solution)/shard_map/ppermute | solution.py:347
  13.4 17.9 %collective-permute-start.8 = (bf16[512,512]{1,0:T(8,128)(2,1)}, bf16[512,512]{1,0:T(8,128)(2,1)}, u32[]{:S(2)}, u32[]{:S(2)}) collective-permute-start(bf16[512,512]{1,0:T(8,128)(2,1)} %get-tuple-element.16.rest_6_), channel_id=1, source_target_pairs={{0,3},{1,0},{2,1},{3,2},{4,5},{5,6},{6,7},{7,4},{8,11},{9,8},{10,9... | collective-permute-start | bytes 1572872 | tf_op jit(solution)/shard_map/ppermute | solution.py:329
  20.3 32.6 %collective-permute-start.3 = (bf16[6,16,3072]{2,1,0:T(8,128)(2,1)S(1)}, bf16[6,16,3072]{2,1,0:T(8,128)(2,1)S(1)}, u32[]{:S(2)}, u32[]{:S(2)}) collective-permute-start(bf16[6,16,3072]{2,1,0:T(8,128)(2,1)S(1)} %get-tuple-element.20), channel_id=1, source_target_pairs={{0,4},{4,0},{8,12},{12,8},{1,5},{5,1},{9,13},{13,9},{2,6},{6,2},{1... | collective-permute-start | bytes 1769480 | tf_op jit(solution)/shard_map/ppermute | solution.py:350
  20.4 32.5 %collective-permute-start.4 = (bf16[6,16,3072]{2,1,0:T(8,128)(2,1)S(1)}, bf16[6,16,3072]{2,1,0:T(8,128)(2,1)S(1)}, u32[]{:S(2)}, u32[]{:S(2)}) collective-permute-start(bf16[6,16,3072]{2,1,0:T(8,128)(2,1)S(1)} %get-tuple-element.21), channel_id=1, source_target_pairs={{0,8},{4,12},{8,0},{12,4},{1,9},{5,13},{9,1},{13,5},{2,10},{6,14},... | collective-permute-start | bytes 1769480 | tf_op jit(solution)/shard_map/ppermute | solution.py:350
  20.9 32.0 %collective-permute-start.5 = (bf16[6,16,3072]{2,1,0:T(8,128)(2,1)S(1)}, bf16[6,16,3072]{2,1,0:T(8,128)(2,1)S(1)}, u32[]{:S(2)}, u32[]{:S(2)}) collective-permute-start(bf16[6,16,3072]{2,1,0:T(8,128)(2,1)S(1)} %get-tuple-element.22), channel_id=1, source_target_pairs={{0,12},{4,8},{8,4},{12,0},{1,13},{5,9},{9,5},{13,1},{2,14},{6,10},... | collective-permute-start | bytes 1769480 | tf_op jit(solution)/shard_map/ppermute | solution.py:350
  25.1 21.3 %collective-permute-start.7 = (bf16[512,512]{1,0:T(8,128)(2,1)S(1)}, bf16[512,512]{1,0:T(8,128)(2,1)S(1)}, u32[]{:S(2)}, u32[]{:S(2)}) collective-permute-start(bf16[512,512]{1,0:T(8,128)(2,1)S(1)} %block_product.8.rest_0_), channel_id=1, source_target_pairs={{0,1},{1,2},{2,3},{3,0},{4,7},{5,4},{6,5},{7,6},{8,9},{9,10},{10,1... | collective-permute-start | bytes 1572872 | tf_op jit(solution)/shard_map/ppermute | solution.py:329
  31.1 3.7 %copy-start.5 = (bf16[512,512]{1,0:T(8,128)(2,1)}, bf16[512,512]{1,0:T(8,128)(2,1)S(1)}, u32[]{:S(2)}) copy-start(bf16[512,512]{1,0:T(8,128)(2,1)S(1)} %block_product.9.rest_1_.rest_4_) | copy-start | bytes 1572868
  34.8 28.3 %collective-permute-start.12 = (bf16[512,512]{1,0:T(8,128)(2,1)}, bf16[512,512]{1,0:T(8,128)(2,1)}, u32[]{:S(2)}, u32[]{:S(2)}) collective-permute-start(bf16[512,512]{1,0:T(8,128)(2,1)} %block_product.10.rest_0_), channel_id=1, source_target_pairs={{0,3},{1,0},{2,1},{3,2},{4,5},{5,6},{6,7},{7,4},{8,11},{9,8},{10,9... | collective-permute-start | bytes 1572872 | tf_op jit(solution)/shard_map/ppermute | solution.py:329
  42.5 7.3 %copy-start.7 = (bf16[512,512]{1,0:T(8,128)(2,1)}, bf16[512,512]{1,0:T(8,128)(2,1)S(1)}, u32[]{:S(2)}) copy-start(bf16[512,512]{1,0:T(8,128)(2,1)S(1)} %block_product.11.rest_1_.rest_5_) | copy-start | bytes 1572868
  49.8 25.1 %collective-permute-start.14 = (bf16[512,512]{1,0:T(8,128)(2,1)}, bf16[512,512]{1,0:T(8,128)(2,1)}, u32[]{:S(2)}, u32[]{:S(2)}) collective-permute-start(bf16[512,512]{1,0:T(8,128)(2,1)} %block_product.12.rest_4_), channel_id=1, source_target_pairs={{0,1},{1,2},{2,3},{3,0},{4,7},{5,4},{6,5},{7,6},{8,9},{9,10},{10,1... | collective-permute-start | bytes 1572872 | tf_op jit(solution)/shard_map/ppermute | solution.py:329
  52.9 1.6 %copy-start.3 = (bf16[6,16,3072]{2,1,0:T(8,128)(2,1)}, bf16[6,16,3072]{2,1,0:T(8,128)(2,1)S(1)}, u32[]{:S(2)}) copy-start(bf16[6,16,3072]{2,1,0:T(8,128)(2,1)S(1)} %collective-permute-done.5.rest_3_.rest_9_) | copy-start | bytes 1769476
  54.5 0.8 %copy-start.1 = (bf16[6,16,3072]{2,1,0:T(8,128)(2,1)}, bf16[6,16,3072]{2,1,0:T(8,128)(2,1)S(1)}, u32[]{:S(2)}) copy-start(bf16[6,16,3072]{2,1,0:T(8,128)(2,1)S(1)} %collective-permute-done.4.rest_2_.rest_8_) | copy-start | bytes 1769476
  55.3 14.1 %collective-permute-start.11 = (f32[16,512]{1,0:T(8,128)S(1)}, f32[16,512]{1,0:T(8,128)S(1)}, u32[]{:S(2)}, u32[]{:S(2)}) collective-permute-start(f32[16,512]{1,0:T(8,128)S(1)} %low_sums.1.rest_1_.rest_0_), channel_id=1, source_target_pairs={{0,3},{1,2},{2,1},{3,0},{4,7},{5,6},{6,5},{7,4},{8,11},{9,10},{10,... | collective-permute-start | bytes 98312 | tf_op jit(solution)/shard_map/ppermute | solution.py:360
  62.0 11.6 %collective-permute-start.10 = (f32[16,512]{1,0:T(8,128)S(1)}, f32[16,512]{1,0:T(8,128)S(1)}, u32[]{:S(2)}, u32[]{:S(2)}) collective-permute-start(f32[16,512]{1,0:T(8,128)S(1)} %low_sums.1.rest_1_.rest_0_), channel_id=1, source_target_pairs={{0,2},{1,3},{2,0},{3,1},{4,6},{5,7},{6,4},{7,5},{8,10},{9,11},{10,... | collective-permute-start | bytes 98312 | tf_op jit(solution)/shard_map/ppermute | solution.py:360
  62.6 11.0 %collective-permute-start.9 = (f32[16,512]{1,0:T(8,128)S(1)}, f32[16,512]{1,0:T(8,128)S(1)}, u32[]{:S(2)}, u32[]{:S(2)}) collective-permute-start(f32[16,512]{1,0:T(8,128)S(1)} %low_sums.1.rest_1_.rest_0_), channel_id=1, source_target_pairs={{0,1},{1,0},{2,3},{3,2},{4,5},{5,4},{6,7},{7,6},{8,9},{9,8},{10,11... | collective-permute-start | bytes 98312 | tf_op jit(solution)/shard_map/ppermute | solution.py:360
  63.1 10.5 %copy-start.2 = (bf16[6,16,3072]{2,1,0:T(8,128)(2,1)S(1)}, bf16[6,16,3072]{2,1,0:T(8,128)(2,1)}, u32[]{:S(2)}) copy-start(bf16[6,16,3072]{2,1,0:T(8,128)(2,1)} %copy-done.1) | copy-start | bytes 1769476
  63.1 10.5 %copy-start.4 = (bf16[6,16,3072]{2,1,0:T(8,128)(2,1)S(1)}, bf16[6,16,3072]{2,1,0:T(8,128)(2,1)}, u32[]{:S(2)}) copy-start(bf16[6,16,3072]{2,1,0:T(8,128)(2,1)} %copy-done.3) | copy-start | bytes 1769476
  63.1 10.5 %copy-start.6 = (bf16[512,512]{1,0:T(8,128)(2,1)S(1)}, bf16[512,512]{1,0:T(8,128)(2,1)}, u32[]{:S(2)}) copy-start(bf16[512,512]{1,0:T(8,128)(2,1)} %copy-done.5) | copy-start | bytes 1572868
  63.2 10.5 %copy-start.8 = (bf16[512,512]{1,0:T(8,128)(2,1)S(1)}, bf16[512,512]{1,0:T(8,128)(2,1)}, u32[]{:S(2)}) copy-start(bf16[512,512]{1,0:T(8,128)(2,1)} %copy-done.7) | copy-start | bytes 1572868
  66.1 13.7 %collective-permute-start.13 = (bf16[512,512]{1,0:T(8,128)(2,1)S(1)}, bf16[512,512]{1,0:T(8,128)(2,1)S(1)}, u32[]{:S(2)}, u32[]{:S(2)}) collective-permute-start(bf16[512,512]{1,0:T(8,128)(2,1)S(1)} %block_product.13.rest_10_), channel_id=1, source_target_pairs={{0,3},{1,0},{2,1},{3,2},{4,5},{5,6},{6,7},{7,4},{8,11},{9,8},{10,9... | collective-permute-start | bytes 1572872 | tf_op jit(solution)/shard_map/ppermute | solution.py:329

commit v11 on v10

--- a/solution.py
+++ b/solution.py
@@ -72,10 +72,12 @@
             pltpu.make_async_copy(weight_ref.at[part, columns], rhs_ref.at[k], sems.at[1, k]),
         )
 
+    for copy in copies(0):
+        copy.start()
     for k in range(chunks):
-        for copy in copies(k):
-            copy.start()
-    for k in range(chunks):
+        if k + 1 < chunks:
+            for copy in copies(k + 1):
+                copy.start()
         for copy in copies(k):
             copy.wait()
         part = jnp.dot(lhs_ref[k], rhs_ref[k], preferred_element_type=F32)
@@ -337,7 +339,7 @@
         return block_product(rows, weight, start_of(back, piece), width, **options)
 
     last = first_product(rows, weight, start_of(1, 0), width)
-    moving, owns = [move(last, 0)], []
+    moving = [move(last, 0)]
     for piece in range(1, PIECES):
         last, ids = partial(1, piece, after=[last], ids=ids)
         moving.append(move(last, piece))
@@ -345,6 +347,8 @@
     all_ids = [ids]
     for x in range(1, req_total):
         all_ids.append(lax.ppermute(ids, "req", [(i, i ^ x) for i in range(req_total)]))
+    last = partial(0, 0, after=[last])
+    owns = [last]
     packs, starts, ends = pick_adapters(me_req, table, all_ids, lens, down, up, [last])
     for x in range(1, req_total):
         packs[x] = lax.ppermute(packs[x], "req", [(i, i ^ x) for i in range(req_total)])
@@ -361,7 +365,7 @@
                 last = low
             last = partial(1 + step, piece, addends=[moving[piece]], after=[last])
             moving[piece] = move(last, piece)
-            if step == 1:
+            if step == 1 and piece > 0:
                 last = partial(0, piece, after=[last], cost=LARGE)
                 owns.append(last)
 

time: 81.6 us -> 82 us (level)
  starting transfers between devices: 31.5 us -> 25.9 us
  waiting for transfers between devices: 12.2 us -> 17.2 us
  Pallas kernels: 36.4 us -> 37.3 us
    ppermute x6, waiting for transfers between devices: 5.73 us -> 12.5 us  [move(): return lax.ppermute(value, ('req', 'tp'), pairs)]
    ppermute x3, starting transfers between devices: 7.8 us -> 4.52 us  [local(): lows.append(lax.ppermute(low, 'tp', pairs))]
    ppermute x3, waiting for transfers between devices: 2.28 us -> 0.01 us  [local(): lax.ppermute(ids, 'req', [(i, i ^ x) for i in range(req_total)])]
    ppermute x3, starting transfers between devices: 3.21 us -> 1.86 us  [local(): lax.ppermute(ids, 'req', [(i, i ^ x) for i in range(req_total)])]
    ppermute x6, starting transfers between devices: 18.6 us -> 17.6 us  [move(): return lax.ppermute(value, ('req', 'tp'), pairs)]
  transfers between devices with their start and end apart: 15 -> 15, of which waited for: 5 -> 6; matrix products, arithmetic and copies ran while one was open for 0% -> 0% of each run, Pallas kernels for 39% -> 39%
where the time goes in v11:
time: 82 us; the launch traced here: 81.5 us
  Pallas kernels  37.3 us (45%)
  starting transfers between devices  25.9 us (32%)
  waiting for transfers between devices  17.2 us (21%)
  local copies, waits for them, and re-layouts  0.85 us (1%)
    pallas_call x7, Pallas kernels, block_product(): pl.pallas_call(functools.partial(product_kernel, len(addends), with_ids),...  21.5 us
    ppermute x6, starting transfers between devices, move(): return lax.ppermute(value, ('req', 'tp'), pairs)  17.6 us
    ppermute x6, waiting for transfers between devices, move(): return lax.ppermute(value, ('req', 'tp'), pairs)  12.5 us
    ppermute x3, waiting for transfers between devices, local(): lows.append(lax.ppermute(low, 'tp', pairs))  4.65 us
    pallas_call x2, Pallas kernels, finish(): pl.pallas_call(functools.partial(finish_kernel, len(arrivals)), grid=(row...  4.6 us
    ppermute x3, starting transfers between devices, local(): lows.append(lax.ppermute(low, 'tp', pairs))  4.52 us
    pallas_call x1, Pallas kernels, first_product(): pl.pallas_call(functools.partial(first_kernel, chunk), in_specs=[pl.Block...  4.44 us
    pallas_call x1, Pallas kernels, pick_adapters(): pl.pallas_call(functools.partial(pick_kernel, peers, len(after)), in_spec...  3.99 us
  transfers between devices with their start and end apart: 15, of which 6 were waited for; matrix products, arithmetic and copies ran while one was open for 0% of the time, Pallas kernels for 39%

profile of v11, /device:TPU:0, one launch (start us, length us, event | category | flops | bytes accessed | tf_op | source)
XLA Modules:
  0.0 81.5 jit_solution(3556796800890076110)
XLA Ops:
  0.0 0.0 copy-start
  0.0 0.0 copy-start.10
  0.0 4.4 %first_product.1.rest_1_ = bf16[512,512]{1,0:T(8,128)(2,1)} custom-call(s32[1]{0:T(128)} %bitcast.2.first_ref, bf16[512,2048]{1,0:T(8,128)(2,1)} %rows_ref.17, bf16[2048,4096]{1,0:T(8,128)(2,1)} %weight_ref.15), custom_call_target="tpu_custom_call" | custom-call | flops 1000 | bytes 1000 | tf_op jit(solution)/shard_map/first_product/pallas_call | solution.py:97
  4.5 3.1 %collective-permute-start.6 = (bf16[512,512]{1,0:T(8,128)(2,1)}, bf16[512,512]{1,0:T(8,128)(2,1)}, u32[]{:S(2)}, u32[]{:S(2)}) collective-permute-start(bf16[512,512]{1,0:T(8,128)(2,1)} %first_product.1.rest_1_), channel_id=1, source_target_pairs={{0,1},{1,2},{2,3},{3,0},{4,7},{5,4},{6,5},{7,6},{8,9},{9,10},{10,1... | collective-permute-start | bytes 1572872 | tf_op jit(solution)/shard_map/ppermute | solution.py:331
  7.5 0.0 copy-done
  7.5 0.0 copy-done.10
  7.5 3.5 %block_product.7 = (bf16[512,512]{1,0:T(8,128)(2,1)}, s32[1,12]{1,0:T(1,128)S(1)}) custom-call(s32[1]{0:T(128)} %bitcast.1.first_ref, bf16[512,2048]{1,0:T(8,128)(2,1)S(1)} %copy-done, bf16[2048,4096]{1,0:T(8,128)(2,1)} %weight_ref.15, s32[1,12]{1,0:T(1,128)S(1)} %copy-done.10, bf16[512,512]{1,0:T(8,128)(2,1)} %first_product.1.rest_1_), custom_call_target="tpu_custom_call" | custom-call | flops 1000 | bytes 1000 | tf_op jit(solution)/shard_map/block_product/pallas_call | solution.py:42
  11.0 2.1 %collective-permute-start.8 = (bf16[512,512]{1,0:T(8,128)(2,1)}, bf16[512,512]{1,0:T(8,128)(2,1)}, u32[]{:S(2)}, u32[]{:S(2)}) collective-permute-start(bf16[512,512]{1,0:T(8,128)(2,1)} %get-tuple-element.16.rest_0_), channel_id=1, source_target_pairs={{0,3},{1,0},{2,1},{3,2},{4,5},{5,6},{6,7},{7,4},{8,11},{9,8},{10,9... | collective-permute-start | bytes 1572872 | tf_op jit(solution)/shard_map/ppermute | solution.py:331
  13.1 0.6 collective-permute-start.2
  13.7 1.1 %collective-permute-start.1 = (s32[1,12]{1,0:T(1,128)S(1)}, s32[1,12]{1,0:T(1,128)S(1)}, u32[]{:S(2)}, u32[]{:S(2)}) collective-permute-start(s32[1,12]{1,0:T(1,128)S(1)} %get-tuple-element.15.rest_0_), channel_id=1, source_target_pairs={{0,8},{4,12},{8,0},{12,4},{1,9},{5,13},{9,1},{13,5},{2,10},{6,14},... | collective-permute-start | bytes 152 | tf_op jit(solution)/shard_map/ppermute | solution.py:349
  14.8 0.2 collective-permute-start
  15.0 0.0 copy-start.9
  15.0 0.0 copy-start.11
  15.0 2.7 %block_product.8.rest_6_.rest_4_ = bf16[512,512]{1,0:T(8,128)(2,1)S(1)} custom-call(s32[1]{0:T(128)} %bitcast.3.first_ref, bf16[512,2048]{1,0:T(8,128)(2,1)S(1)} %copy-done, bf16[2048,4096]{1,0:T(8,128)(2,1)} %weight_ref.15, bf16[512,512]{1,0:T(8,128)(2,1)} %get-tuple-element.16.rest_0_), custom_call_target="tpu_custom_call" | custom-call | flops 1000 | bytes 1000 | tf_op jit(solution)/shard_map/block_product/pallas_call | solution.py:42
  17.8 0.0 collective-permute-done.2.rest_3_
  17.8 0.0 collective-permute-done.1.rest_2_
  17.8 0.0 collective-permute-done.rest_1_
  17.8 0.0 copy-done.9
  17.8 0.0 copy-done.11
  17.9 4.0 %pick_adapters.1 = (bf16[6,16,3072]{2,1,0:T(8,128)(2,1)S(1)}, bf16[6,16,3072]{2,1,0:T(8,128)(2,1)S(1)}, bf16[6,16,3072]{2,1,0:T(8,128)(2,1)S(1)}, bf16[6,16,3072...) custom-call(s32[1]{0:T(128)} %bitcast.me_ref, s32[512]{0:T(512)S(1)} %copy-done.9, s32[1,12]{1,0:T(1,128)S(1)} %copy-done.11, ...), custom_call_target="tpu_custom_call" | custom-call | flops 1000 | bytes 1000 | tf_op jit(solution)/shard_map/pick_adapters/pallas_call | solution.py:186
  21.9 0.1 collective-permute-start.3
  22.0 1.0 %collective-permute-start.4 = (bf16[6,16,3072]{2,1,0:T(8,128)(2,1)S(1)}, bf16[6,16,3072]{2,1,0:T(8,128)(2,1)S(1)}, u32[]{:S(2)}, u32[]{:S(2)}) collective-permute-start(bf16[6,16,3072]{2,1,0:T(8,128)(2,1)S(1)} %get-tuple-element.21), channel_id=1, source_target_pairs={{0,8},{4,12},{8,0},{12,4},{1,9},{5,13},{9,1},{13,5},{2,10},{6,14},... | collective-permute-start | bytes 1769480 | tf_op jit(solution)/shard_map/ppermute | solution.py:354
  22.9 0.9 %collective-permute-start.5 = (bf16[6,16,3072]{2,1,0:T(8,128)(2,1)S(1)}, bf16[6,16,3072]{2,1,0:T(8,128)(2,1)S(1)}, u32[]{:S(2)}, u32[]{:S(2)}) collective-permute-start(bf16[6,16,3072]{2,1,0:T(8,128)(2,1)S(1)} %get-tuple-element.22), channel_id=1, source_target_pairs={{0,12},{4,8},{8,4},{12,0},{1,13},{5,9},{9,5},{13,1},{2,14},{6,10},... | collective-permute-start | bytes 1769480 | tf_op jit(solution)/shard_map/ppermute | solution.py:354
  23.8 0.0 collective-permute-done.6.rest_0_
  23.8 2.8 %block_product.9.rest_1_ = bf16[512,512]{1,0:T(8,128)(2,1)S(1)} custom-call(s32[1]{0:T(128)} %bitcast.5.first_ref, bf16[512,2048]{1,0:T(8,128)(2,1)S(1)} %copy-done, bf16[2048,4096]{1,0:T(8,128)(2,1)} %weight_ref.15, bf16[512,512]{1,0:T(8,128)(2,1)} %collective-permute-done.6.rest_0_, s32[24]{0:T(128)S(1)} %get-tuple-element.17.rest_1_.start_ref), custom_call_target="tpu_custom_call" | custom-call | flops 1000 | bytes 1000 | tf_op jit(solution)/shard_map/block_product/pallas_call | solution.py:42
  26.6 6.3 %collective-permute-start.7 = (bf16[512,512]{1,0:T(8,128)(2,1)S(1)}, bf16[512,512]{1,0:T(8,128)(2,1)S(1)}, u32[]{:S(2)}, u32[]{:S(2)}) collective-permute-start(bf16[512,512]{1,0:T(8,128)(2,1)S(1)} %block_product.9.rest_1_), channel_id=1, source_target_pairs={{0,1},{1,2},{2,3},{3,0},{4,7},{5,4},{6,5},{7,6},{8,9},{9,10},{10,1... | collective-permute-start | bytes 1572872 | tf_op jit(solution)/shard_map/ppermute | solution.py:331
  32.9 0.0 collective-permute-done.8.rest_0_
  32.9 3.5 %block_product.10.rest_0_ = bf16[512,512]{1,0:T(8,128)(2,1)} custom-call(s32[1]{0:T(128)} %bitcast.7.first_ref, bf16[512,2048]{1,0:T(8,128)(2,1)S(1)} %copy-done, bf16[2048,4096]{1,0:T(8,128)(2,1)} %weight_ref.15, bf16[512,512]{1,0:T(8,128)(2,1)} %collective-permute-done.8.rest_0_, bf16[512,512]{1,0:T(8,128)(2,1)S(1)} %block_product.9.rest_1_), custom_call_target="tpu_custom_call" | custom-call | flops 1000 | bytes 1000 | tf_op jit(solution)/shard_map/block_product/pallas_call | solution.py:42
  36.4 3.7 %collective-permute-start.12 = (bf16[512,512]{1,0:T(8,128)(2,1)}, bf16[512,512]{1,0:T(8,128)(2,1)}, u32[]{:S(2)}, u32[]{:S(2)}) collective-permute-start(bf16[512,512]{1,0:T(8,128)(2,1)} %block_product.10.rest_0_), channel_id=1, source_target_pairs={{0,3},{1,0},{2,1},{3,2},{4,5},{5,6},{6,7},{7,4},{8,11},{9,8},{10,9... | collective-permute-start | bytes 1572872 | tf_op jit(solution)/shard_map/ppermute | solution.py:331
  40.1 2.7 %block_product.11.rest_1_.rest_5_ = bf16[512,512]{1,0:T(8,128)(2,1)S(1)} custom-call(s32[1]{0:T(128)} %bitcast.6.first_ref, bf16[512,2048]{1,0:T(8,128)(2,1)S(1)} %copy-done, bf16[2048,4096]{1,0:T(8,128)(2,1)} %weight_ref.15, bf16[512,512]{1,0:T(8,128)(2,1)} %block_product.10.rest_0_), custom_call_target="tpu_custom_call" | custom-call | flops 20000000000 | bytes 1000 | tf_op jit(solution)/shard_map/block_product/pallas_call | solution.py:42
  42.8 0.0 copy-start.7
  42.8 2.6 %collective-permute-done.7.rest_0_ = bf16[512,512]{1,0:T(8,128)(2,1)S(1)} collective-permute-done((bf16[512,512]{1,0:T(8,128)(2,1)S(1)}, bf16[512,512]{1,0:T(8,128)(2,1)S(1)}, u32[]{:S(2)}, u32[]{:S(2)}) %collective-permute-start.7) | collective-permute-done | bytes 524320 | tf_op jit(solution)/shard_map/ppermute | solution.py:331
  45.4 3.4 %block_product.12.rest_4_ = bf16[512,512]{1,0:T(8,128)(2,1)} custom-call(s32[1]{0:T(128)} %bitcast.4.first_ref, bf16[512,2048]{1,0:T(8,128)(2,1)S(1)} %copy-done, bf16[2048,4096]{1,0:T(8,128)(2,1)} %weight_ref.15, bf16[512,512]{1,0:T(8,128)(2,1)S(1)} %collective-permute-done.7.rest_0_, bf16[512,512]{1,0:T(8,128)(2,1)S(1)} %block_product.11.rest_1_.rest_5_), custom_call_target="tpu_custom_call" | custom-call | flops 1000 | bytes 1000 | tf_op jit(solution)/shard_map/block_product/pallas_call | solution.py:42
  48.8 0.0 copy-done.7
  48.8 2.4 %collective-permute-start.14 = (bf16[512,512]{1,0:T(8,128)(2,1)}, bf16[512,512]{1,0:T(8,128)(2,1)}, u32[]{:S(2)}, u32[]{:S(2)}) collective-permute-start(bf16[512,512]{1,0:T(8,128)(2,1)} %block_product.12.rest_4_), channel_id=1, source_target_pairs={{0,1},{1,2},{2,3},{3,0},{4,7},{5,4},{6,5},{7,6},{8,9},{9,10},{10,1... | collective-permute-start | bytes 1572872 | tf_op jit(solution)/shard_map/ppermute | solution.py:331
  51.1 0.0 collective-permute-done.3.rest_1_.rest_7_
  51.1 0.0 collective-permute-done.4.rest_2_.rest_8_
  51.1 0.0 copy-start.3
  51.1 0.0 collective-permute-done.5.rest_3_.rest_9_
  51.1 0.0 copy-start.5
  51.2 1.6 %low_sums.1.rest_1_.rest_0_ = f32[16,512]{1,0:T(8,128)S(1)} custom-call(s32[24]{0:T(128)S(1)} %get-tuple-element.17.rest_1_.start_ref, s32[24]{0:T(128)S(1)} %get-tuple-element.18.end_ref, bf16[512,2048]{1,0:T(8,128)(2,1)S(1)} %copy-done, bf16[6,16,3072]{2,1,0:T(8,128)(2,1)S(1)} %get-tuple-element.19.rest_0_.rest_6_, ...), custom_call_target="tpu_custom_call" | custom-call | flops 1000 | bytes 1000 | tf_op jit(solution)/shard_map/low_sums/pallas_call | solution.py:228
  52.7 0.0 copy-done.3
  52.7 0.0 copy-start.1
  52.7 0.8 copy-done.1
  53.5 3.4 %collective-permute-start.11 = (f32[16,512]{1,0:T(8,128)S(1)}, f32[16,512]{1,0:T(8,128)S(1)}, u32[]{:S(2)}, u32[]{:S(2)}) collective-permute-start(f32[16,512]{1,0:T(8,128)S(1)} %low_sums.1.rest_1_.rest_0_), channel_id=1, source_target_pairs={{0,3},{1,2},{2,1},{3,0},{4,7},{5,6},{6,5},{7,4},{8,11},{9,10},{10,... | collective-permute-start | bytes 98312 | tf_op jit(solution)/shard_map/ppermute | solution.py:364
  57.0 0.0 copy-done.5
  57.0 0.9 %collective-permute-start.10 = (f32[16,512]{1,0:T(8,128)S(1)}, f32[16,512]{1,0:T(8,128)S(1)}, u32[]{:S(2)}, u32[]{:S(2)}) collective-permute-start(f32[16,512]{1,0:T(8,128)S(1)} %low_sums.1.rest_1_.rest_0_), channel_id=1, source_target_pairs={{0,2},{1,3},{2,0},{3,1},{4,6},{5,7},{6,4},{7,5},{8,10},{9,11},{10,... | collective-permute-start | bytes 98312 | tf_op jit(solution)/shard_map/ppermute | solution.py:364
  57.9 0.2 collective-permute-start.9
  58.1 4.1 %collective-permute-done.12.rest_0_ = bf16[512,512]{1,0:T(8,128)(2,1)} collective-permute-done((bf16[512,512]{1,0:T(8,128)(2,1)}, bf16[512,512]{1,0:T(8,128)(2,1)}, u32[]{:S(2)}, u32[]{:S(2)}) %collective-permute-start.12) | collective-permute-done | bytes 524320 | tf_op jit(solution)/shard_map/ppermute | solution.py:331
  62.2 0.0 copy-start.2
  62.2 2.9 %block_product.13.rest_10_ = bf16[512,512]{1,0:T(8,128)(2,1)S(1)} custom-call(s32[1]{0:T(128)} %bitcast.8.first_ref, bf16[512,2048]{1,0:T(8,128)(2,1)S(1)} %copy-done, bf16[2048,4096]{1,0:T(8,128)(2,1)} %weight_ref.15, bf16[512,512]{1,0:T(8,128)(2,1)} %collective-permute-done.12.rest_0_, f32[16,512]{1,0:T(8,128)S(1)} %low_sums.1.rest_1_.rest_0_), custom_call_target="tpu_custom_call" | custom-call | flops 1000 | bytes 1000 | tf_op jit(solution)/shard_map/block_product/pallas_call | solution.py:42
  65.2 0.1 collective-permute-start.13
  65.2 3.3 %collective-permute-done.11.rest_3_ = f32[16,512]{1,0:T(8,128)S(1)} collective-permute-done((f32[16,512]{1,0:T(8,128)S(1)}, f32[16,512]{1,0:T(8,128)S(1)}, u32[]{:S(2)}, u32[]{:S(2)}) %collective-permute-start.11) | collective-permute-done | bytes 32800 | tf_op jit(solution)/shard_map/ppermute | solution.py:364
  68.5 0.6 collective-permute-done.10.rest_2_
  69.2 0.7 collective-permute-done.9.rest_1_
  69.9 0.0 copy-done.2
  69.9 0.0 copy-done.4
  69.9 0.0 copy-done.6
  69.9 0.0 copy-done.8
  69.9 1.3 %adapter_term.1 = (f32[512,512]{1,0:T(8,128)S(1)}, f32[512,512]{1,0:T(8,128)S(1)}) custom-call(s32[24]{0:T(128)S(1)} %get-tuple-element.17.rest_1_.start_ref, s32[24]{0:T(128)S(1)} %get-tuple-element.18.end_ref, f32[16,512]{1,0:T(8,128)S(1)} %low_sums.1.rest_1_.rest_0_, f32[16,512]{1,0:T(8,128)S(1)} %collective-permute-done.9.rest_1_, ...), custom_call_target="tpu_custom_call" | custom-call | flops 1000 | bytes 1000 | tf_op jit(solution)/shard_map/adapter_term/pallas_call | solution.py:274
  71.2 0.0 collective-permute-done.14.rest_0_
  71.2 3.2 %finish.2.rest_1_ = bf16[512,1024]{1,0:T(8,128)(2,1)} custom-call(f32[512,512]{1,0:T(8,128)S(1)} %get-tuple-element.24.term_ref, bf16[512,512]{1,0:T(8,128)(2,1)} %collective-permute-done.14.rest_0_), custom_call_target="tpu_custom_call" | custom-call | flops 20000000000 | bytes 1000 | tf_op jit(solution)/shard_map/finish/pallas_call | solution.py:301
  74.4 5.7 %collective-permute-done.13.rest_0_ = bf16[512,512]{1,0:T(8,128)(2,1)S(1)} collective-permute-done((bf16[512,512]{1,0:T(8,128)(2,1)S(1)}, bf16[512,512]{1,0:T(8,128)(2,1)S(1)}, u32[]{:S(2)}, u32[]{:S(2)}) %collective-permute-start.13) | collective-permute-done | bytes 524320 | tf_op jit(solution)/shard_map/ppermute | solution.py:331
  80.1 1.4 %finish.3 = bf16[512,1024]{1,0:T(8,128)(2,1)} custom-call(f32[512,512]{1,0:T(8,128)S(1)} %get-tuple-element.23.term_ref, bf16[512,512]{1,0:T(8,128)(2,1)S(1)} %collective-permute-done.13.rest_0_, bf16[512,1024]{1,0:T(8,128)(2,1)} %finish.2.rest_1_), custom_call_target="tpu_custom_call", output_to_operand_aliasing={{}: (2, {})} | custom-call | flops 1000 | bytes 1000 | tf_op jit(solution)/shard_map/finish/pallas_call | solution.py:301
  (3 shorter events, 0.0 us)
Async XLA Ops:
  0.0 7.5 %copy-start = (bf16[512,2048]{1,0:T(8,128)(2,1)S(1)}, bf16[512,2048]{1,0:T(8,128)(2,1)}, u32[]{:S(2)}) copy-start(bf16[512,2048]{1,0:T(8,128)(2,1)} %rows_ref.17) | copy-start | bytes 6291460
  0.0 7.5 %copy-start.10 = (s32[1,12]{1,0:T(1,128)S(1)}, s32[1,12]{1,0:T(1,128)}, u32[]{:S(2)}) copy-start(s32[1,12]{1,0:T(1,128)} %rest_0_.1) | copy-start | bytes 148
  4.5 19.3 %collective-permute-start.6 = (bf16[512,512]{1,0:T(8,128)(2,1)}, bf16[512,512]{1,0:T(8,128)(2,1)}, u32[]{:S(2)}, u32[]{:S(2)}) collective-permute-start(bf16[512,512]{1,0:T(8,128)(2,1)} %first_product.1.rest_1_), channel_id=1, source_target_pairs={{0,1},{1,2},{2,3},{3,0},{4,7},{5,4},{6,5},{7,6},{8,9},{9,10},{10,1... | collective-permute-start | bytes 1572872 | tf_op jit(solution)/shard_map/ppermute | solution.py:331
  11.0 21.9 %collective-permute-start.8 = (bf16[512,512]{1,0:T(8,128)(2,1)}, bf16[512,512]{1,0:T(8,128)(2,1)}, u32[]{:S(2)}, u32[]{:S(2)}) collective-permute-start(bf16[512,512]{1,0:T(8,128)(2,1)} %get-tuple-element.16.rest_0_), channel_id=1, source_target_pairs={{0,3},{1,0},{2,1},{3,2},{4,5},{5,6},{6,7},{7,4},{8,11},{9,8},{10,9... | collective-permute-start | bytes 1572872 | tf_op jit(solution)/shard_map/ppermute | solution.py:331
  13.1 4.7 %collective-permute-start.2 = (s32[1,12]{1,0:T(1,128)S(1)}, s32[1,12]{1,0:T(1,128)S(1)}, u32[]{:S(2)}, u32[]{:S(2)}) collective-permute-start(s32[1,12]{1,0:T(1,128)S(1)} %get-tuple-element.15.rest_0_), channel_id=1, source_target_pairs={{0,12},{4,8},{8,4},{12,0},{1,13},{5,9},{9,5},{13,1},{2,14},{6,10},... | collective-permute-start | bytes 152 | tf_op jit(solution)/shard_map/ppermute | solution.py:349
  13.7 4.1 %collective-permute-start.1 = (s32[1,12]{1,0:T(1,128)S(1)}, s32[1,12]{1,0:T(1,128)S(1)}, u32[]{:S(2)}, u32[]{:S(2)}) collective-permute-start(s32[1,12]{1,0:T(1,128)S(1)} %get-tuple-element.15.rest_0_), channel_id=1, source_target_pairs={{0,8},{4,12},{8,0},{12,4},{1,9},{5,13},{9,1},{13,5},{2,10},{6,14},... | collective-permute-start | bytes 152 | tf_op jit(solution)/shard_map/ppermute | solution.py:349
  14.8 3.0 %collective-permute-start = (s32[1,12]{1,0:T(1,128)S(1)}, s32[1,12]{1,0:T(1,128)S(1)}, u32[]{:S(2)}, u32[]{:S(2)}) collective-permute-start(s32[1,12]{1,0:T(1,128)S(1)} %get-tuple-element.15.rest_0_), channel_id=1, source_target_pairs={{0,4},{4,0},{8,12},{12,8},{1,5},{5,1},{9,13},{13,9},{2,6},{6,2},{1... | collective-permute-start | bytes 152 | tf_op jit(solution)/shard_map/ppermute | solution.py:349
  15.0 2.9 %copy-start.9 = (s32[512]{0:T(512)S(1)}, s32[512]{0:T(512)}, u32[]{:S(2)}) copy-start(s32[512]{0:T(512)} %table_ref.1) | copy-start | bytes 6148
  15.0 2.9 %copy-start.11 = (s32[1,12]{1,0:T(1,128)S(1)}, s32[1,12]{1,0:T(1,128)}, u32[]{:S(2)}) copy-start(s32[1,12]{1,0:T(1,128)} %lens_ref.1) | copy-start | bytes 148
  21.9 29.3 %collective-permute-start.3 = (bf16[6,16,3072]{2,1,0:T(8,128)(2,1)S(1)}, bf16[6,16,3072]{2,1,0:T(8,128)(2,1)S(1)}, u32[]{:S(2)}, u32[]{:S(2)}) collective-permute-start(bf16[6,16,3072]{2,1,0:T(8,128)(2,1)S(1)} %get-tuple-element.20), channel_id=1, source_target_pairs={{0,4},{4,0},{8,12},{12,8},{1,5},{5,1},{9,13},{13,9},{2,6},{6,2},{1... | collective-permute-start | bytes 1769480 | tf_op jit(solution)/shard_map/ppermute | solution.py:354
  22.0 29.2 %collective-permute-start.4 = (bf16[6,16,3072]{2,1,0:T(8,128)(2,1)S(1)}, bf16[6,16,3072]{2,1,0:T(8,128)(2,1)S(1)}, u32[]{:S(2)}, u32[]{:S(2)}) collective-permute-start(bf16[6,16,3072]{2,1,0:T(8,128)(2,1)S(1)} %get-tuple-element.21), channel_id=1, source_target_pairs={{0,8},{4,12},{8,0},{12,4},{1,9},{5,13},{9,1},{13,5},{2,10},{6,14},... | collective-permute-start | bytes 1769480 | tf_op jit(solution)/shard_map/ppermute | solution.py:354
  22.9 28.2 %collective-permute-start.5 = (bf16[6,16,3072]{2,1,0:T(8,128)(2,1)S(1)}, bf16[6,16,3072]{2,1,0:T(8,128)(2,1)S(1)}, u32[]{:S(2)}, u32[]{:S(2)}) collective-permute-start(bf16[6,16,3072]{2,1,0:T(8,128)(2,1)S(1)} %get-tuple-element.22), channel_id=1, source_target_pairs={{0,12},{4,8},{8,4},{12,0},{1,13},{5,9},{9,5},{13,1},{2,14},{6,10},... | collective-permute-start | bytes 1769480 | tf_op jit(solution)/shard_map/ppermute | solution.py:354
  26.6 18.8 %collective-permute-start.7 = (bf16[512,512]{1,0:T(8,128)(2,1)S(1)}, bf16[512,512]{1,0:T(8,128)(2,1)S(1)}, u32[]{:S(2)}, u32[]{:S(2)}) collective-permute-start(bf16[512,512]{1,0:T(8,128)(2,1)S(1)} %block_product.9.rest_1_), channel_id=1, source_target_pairs={{0,1},{1,2},{2,3},{3,0},{4,7},{5,4},{6,5},{7,6},{8,9},{9,10},{10,1... | collective-permute-start | bytes 1572872 | tf_op jit(solution)/shard_map/ppermute | solution.py:331
  36.4 25.8 %collective-permute-start.12 = (bf16[512,512]{1,0:T(8,128)(2,1)}, bf16[512,512]{1,0:T(8,128)(2,1)}, u32[]{:S(2)}, u32[]{:S(2)}) collective-permute-start(bf16[512,512]{1,0:T(8,128)(2,1)} %block_product.10.rest_0_), channel_id=1, source_target_pairs={{0,3},{1,0},{2,1},{3,2},{4,5},{5,6},{6,7},{7,4},{8,11},{9,8},{10,9... | collective-permute-start | bytes 1572872 | tf_op jit(solution)/shard_map/ppermute | solution.py:331
  42.8 6.0 %copy-start.7 = (bf16[512,512]{1,0:T(8,128)(2,1)}, bf16[512,512]{1,0:T(8,128)(2,1)S(1)}, u32[]{:S(2)}) copy-start(bf16[512,512]{1,0:T(8,128)(2,1)S(1)} %block_product.11.rest_1_.rest_5_) | copy-start | bytes 1572868
  48.8 22.4 %collective-permute-start.14 = (bf16[512,512]{1,0:T(8,128)(2,1)}, bf16[512,512]{1,0:T(8,128)(2,1)}, u32[]{:S(2)}, u32[]{:S(2)}) collective-permute-start(bf16[512,512]{1,0:T(8,128)(2,1)} %block_product.12.rest_4_), channel_id=1, source_target_pairs={{0,1},{1,2},{2,3},{3,0},{4,7},{5,4},{6,5},{7,6},{8,9},{9,10},{10,1... | collective-permute-start | bytes 1572872 | tf_op jit(solution)/shard_map/ppermute | solution.py:331
  51.1 1.6 %copy-start.3 = (bf16[6,16,3072]{2,1,0:T(8,128)(2,1)}, bf16[6,16,3072]{2,1,0:T(8,128)(2,1)S(1)}, u32[]{:S(2)}) copy-start(bf16[6,16,3072]{2,1,0:T(8,128)(2,1)S(1)} %collective-permute-done.4.rest_2_.rest_8_) | copy-start | bytes 1769476
  51.1 5.8 %copy-start.5 = (bf16[6,16,3072]{2,1,0:T(8,128)(2,1)}, bf16[6,16,3072]{2,1,0:T(8,128)(2,1)S(1)}, u32[]{:S(2)}) copy-start(bf16[6,16,3072]{2,1,0:T(8,128)(2,1)S(1)} %collective-permute-done.5.rest_3_.rest_9_) | copy-start | bytes 1769476
  52.7 0.8 %copy-start.1 = (bf16[6,16,3072]{2,1,0:T(8,128)(2,1)}, bf16[6,16,3072]{2,1,0:T(8,128)(2,1)S(1)}, u32[]{:S(2)}) copy-start(bf16[6,16,3072]{2,1,0:T(8,128)(2,1)S(1)} %collective-permute-done.3.rest_1_.rest_7_) | copy-start | bytes 1769476
  53.5 15.0 %collective-permute-start.11 = (f32[16,512]{1,0:T(8,128)S(1)}, f32[16,512]{1,0:T(8,128)S(1)}, u32[]{:S(2)}, u32[]{:S(2)}) collective-permute-start(f32[16,512]{1,0:T(8,128)S(1)} %low_sums.1.rest_1_.rest_0_), channel_id=1, source_target_pairs={{0,3},{1,2},{2,1},{3,0},{4,7},{5,6},{6,5},{7,4},{8,11},{9,10},{10,... | collective-permute-start | bytes 98312 | tf_op jit(solution)/shard_map/ppermute | solution.py:364
  57.0 12.2 %collective-permute-start.10 = (f32[16,512]{1,0:T(8,128)S(1)}, f32[16,512]{1,0:T(8,128)S(1)}, u32[]{:S(2)}, u32[]{:S(2)}) collective-permute-start(f32[16,512]{1,0:T(8,128)S(1)} %low_sums.1.rest_1_.rest_0_), channel_id=1, source_target_pairs={{0,2},{1,3},{2,0},{3,1},{4,6},{5,7},{6,4},{7,5},{8,10},{9,11},{10,... | collective-permute-start | bytes 98312 | tf_op jit(solution)/shard_map/ppermute | solution.py:364
  57.9 12.0 %collective-permute-start.9 = (f32[16,512]{1,0:T(8,128)S(1)}, f32[16,512]{1,0:T(8,128)S(1)}, u32[]{:S(2)}, u32[]{:S(2)}) collective-permute-start(f32[16,512]{1,0:T(8,128)S(1)} %low_sums.1.rest_1_.rest_0_), channel_id=1, source_target_pairs={{0,1},{1,0},{2,3},{3,2},{4,5},{5,4},{6,7},{7,6},{8,9},{9,8},{10,11... | collective-permute-start | bytes 98312 | tf_op jit(solution)/shard_map/ppermute | solution.py:364
  62.2 7.7 %copy-start.2 = (bf16[6,16,3072]{2,1,0:T(8,128)(2,1)S(1)}, bf16[6,16,3072]{2,1,0:T(8,128)(2,1)}, u32[]{:S(2)}) copy-start(bf16[6,16,3072]{2,1,0:T(8,128)(2,1)} %copy-done.1) | copy-start | bytes 1769476
  62.2 7.7 %copy-start.4 = (bf16[6,16,3072]{2,1,0:T(8,128)(2,1)S(1)}, bf16[6,16,3072]{2,1,0:T(8,128)(2,1)}, u32[]{:S(2)}) copy-start(bf16[6,16,3072]{2,1,0:T(8,128)(2,1)} %copy-done.3) | copy-start | bytes 1769476
  62.2 7.7 %copy-start.6 = (bf16[6,16,3072]{2,1,0:T(8,128)(2,1)S(1)}, bf16[6,16,3072]{2,1,0:T(8,128)(2,1)}, u32[]{:S(2)}) copy-start(bf16[6,16,3072]{2,1,0:T(8,128)(2,1)} %copy-done.5) | copy-start | bytes 1769476
  62.2 7.7 %copy-start.8 = (bf16[512,512]{1,0:T(8,128)(2,1)S(1)}, bf16[512,512]{1,0:T(8,128)(2,1)}, u32[]{:S(2)}) copy-start(bf16[512,512]{1,0:T(8,128)(2,1)} %copy-done.7) | copy-start | bytes 1572868
  65.2 15.0 %collective-permute-start.13 = (bf16[512,512]{1,0:T(8,128)(2,1)S(1)}, bf16[512,512]{1,0:T(8,128)(2,1)S(1)}, u32[]{:S(2)}, u32[]{:S(2)}) collective-permute-start(bf16[512,512]{1,0:T(8,128)(2,1)S(1)} %block_product.13.rest_10_), channel_id=1, source_target_pairs={{0,3},{1,0},{2,1},{3,2},{4,5},{5,6},{6,7},{7,4},{8,11},{9,8},{10,9... | collective-permute-start | bytes 1572872 | tf_op jit(solution)/shard_map/ppermute | solution.py:331

commit v12 on v10

--- a/solution.py
+++ b/solution.py
@@ -320,24 +320,36 @@
     me = lax.axis_index("tp").astype(jnp.int32)
     steps = tp_total - 1
 
+    ring = list(range(0, tp_total, 2))[:1] + list(range(1, tp_total, 2))
+    ring += list(range(2, tp_total, 2))[::-1]
+
     def move(value, piece):
         pairs = []
         for r in range(req_total):
             way = 1 if (r + piece) % 2 == 0 else tp_total - 1
-            for i in range(tp_total):
-                pairs.append((r * tp_total + i, r * tp_total + (i + way) % tp_total))
+            for q in range(tp_total):
+                target = ring[(q + way) % tp_total]
+                pairs.append((r * tp_total + ring[q], r * tp_total + target))
         return lax.ppermute(value, ("req", "tp"), pairs)
+
+    def lookup(table, index):
+        result = jnp.int32(table[0])
+        for i in range(1, tp_total):
+            result = jnp.where(index == i, jnp.int32(table[i]), result)
+        return result
+
+    place = lookup([ring.index(i) for i in range(tp_total)], me)
 
     def start_of(back, piece):
         behind = jnp.where(lax.rem(me_req + piece, 2) == 0, tp_total - back, back)
-        block = lax.rem(me + behind, tp_total)
+        block = lookup(ring, lax.rem(place + behind, tp_total))
         return block * cols + piece * width
 
     def partial(back, piece, **options):
         return block_product(rows, weight, start_of(back, piece), width, **options)
 
     last = first_product(rows, weight, start_of(1, 0), width)
-    moving, owns = [move(last, 0)], []
+    moving = [move(last, 0)]
     for piece in range(1, PIECES):
         last, ids = partial(1, piece, after=[last], ids=ids)
         moving.append(move(last, piece))
@@ -345,6 +357,8 @@
     all_ids = [ids]
     for x in range(1, req_total):
         all_ids.append(lax.ppermute(ids, "req", [(i, i ^ x) for i in range(req_total)]))
+    last = partial(0, 0, after=[last])
+    owns = [last]
     packs, starts, ends = pick_adapters(me_req, table, all_ids, lens, down, up, [last])
     for x in range(1, req_total):
         packs[x] = lax.ppermute(packs[x], "req", [(i, i ^ x) for i in range(req_total)])
@@ -361,7 +375,7 @@
                 last = low
             last = partial(1 + step, piece, addends=[moving[piece]], after=[last])
             moving[piece] = move(last, piece)
-            if step == 1:
+            if step == 1 and piece > 0:
                 last = partial(0, piece, after=[last], cost=LARGE)
                 owns.append(last)
 

time: 81.6 us -> 83.9 us (1.028)
  waiting for transfers between devices: 12.2 us -> 27 us
  starting transfers between devices: 31.5 us -> 19.3 us
    ppermute x6, waiting for transfers between devices: 5.73 us -> 18.5 us  [move(): return lax.ppermute(value, ('req', 'tp'), pairs)]
    ppermute x6, starting transfers between devices: 18.6 us -> 11 us  [move(): return lax.ppermute(value, ('req', 'tp'), pairs)]
    ppermute x3, waiting for transfers between devices: 4.17 us -> 8.44 us  [local(): lows.append(lax.ppermute(low, 'tp', pairs))]
    ppermute x3, starting transfers between devices: 7.8 us -> 4.39 us  [local(): lows.append(lax.ppermute(low, 'tp', pairs))]
    ppermute x3, waiting for transfers between devices: 2.28 us -> 0.01 us  [local(): lax.ppermute(ids, 'req', [(i, i ^ x) for i in range(req_total)])]
    ppermute x3, starting transfers between devices: 3.21 us -> 1.91 us  [local(): lax.ppermute(ids, 'req', [(i, i ^ x) for i in range(req_total)])]
  transfers between devices with their start and end apart: 15 -> 15, of which waited for: 5 -> 3; matrix products, arithmetic and copies ran while one was open for 0% -> 0% of each run, Pallas kernels for 39% -> 37%
where the time goes in v12:
time: 83.9 us; the launch traced here: 83.5 us
  Pallas kernels  36.1 us (43%)
  waiting for transfers between devices  27 us (32%)
  starting transfers between devices  19.3 us (23%)
  local copies, waits for them, and re-layouts  0.85 us (1%)
    pallas_call x7, Pallas kernels, block_product(): pl.pallas_call(functools.partial(product_kernel, len(addends), with_ids),...  21.5 us
    ppermute x6, waiting for transfers between devices, move(): return lax.ppermute(value, ('req', 'tp'), pairs)  18.5 us
    ppermute x6, starting transfers between devices, move(): return lax.ppermute(value, ('req', 'tp'), pairs)  11 us
    ppermute x3, waiting for transfers between devices, local(): lows.append(lax.ppermute(low, 'tp', pairs))  8.44 us
    pallas_call x2, Pallas kernels, finish(): pl.pallas_call(functools.partial(finish_kernel, len(arrivals)), grid=(row...  4.6 us
    ppermute x3, starting transfers between devices, local(): lows.append(lax.ppermute(low, 'tp', pairs))  4.39 us
    pallas_call x1, Pallas kernels, first_product(): pl.pallas_call(functools.partial(first_kernel, chunk), in_specs=[pl.Block...  3.62 us
    pallas_call x1, Pallas kernels, pick_adapters(): pl.pallas_call(functools.partial(pick_kernel, peers, len(after)), in_spec...  3.57 us
  transfers between devices with their start and end apart: 15, of which 3 were waited for; matrix products, arithmetic and copies ran while one was open for 0% of the time, Pallas kernels for 37%

profile of v12, /device:TPU:0, one launch (start us, length us, event | category | flops | bytes accessed | tf_op | source)
XLA Modules:
  0.0 83.5 jit_solution(9711585706119090730)
XLA Ops:
  0.0 0.0 copy-start
  0.0 0.0 copy-start.10
  0.0 3.6 %first_product.1.rest_1_ = bf16[512,512]{1,0:T(8,128)(2,1)} custom-call(s32[1]{0:T(128)} %bitcast.2.first_ref, bf16[512,2048]{1,0:T(8,128)(2,1)} %rows_ref.17, bf16[2048,4096]{1,0:T(8,128)(2,1)} %weight_ref.15), custom_call_target="tpu_custom_call" | custom-call | flops 1000 | bytes 1000 | tf_op jit(solution)/shard_map/first_product/pallas_call | solution.py:95
  3.6 3.1 %collective-permute-start.6 = (bf16[512,512]{1,0:T(8,128)(2,1)}, bf16[512,512]{1,0:T(8,128)(2,1)}, u32[]{:S(2)}, u32[]{:S(2)}) collective-permute-start(bf16[512,512]{1,0:T(8,128)(2,1)} %first_product.1.rest_1_), channel_id=1, source_target_pairs={{0,1},{1,3},{3,2},{2,0},{4,6},{5,4},{7,5},{6,7},{8,9},{9,11},{11,1... | collective-permute-start | bytes 1572872 | tf_op jit(solution)/shard_map/ppermute | solution.py:333
  6.7 0.0 copy-done
  6.7 0.0 copy-done.10
  6.7 3.5 %block_product.7 = (bf16[512,512]{1,0:T(8,128)(2,1)}, s32[1,12]{1,0:T(1,128)S(1)}) custom-call(s32[1]{0:T(128)} %bitcast.1.first_ref, bf16[512,2048]{1,0:T(8,128)(2,1)S(1)} %copy-done, bf16[2048,4096]{1,0:T(8,128)(2,1)} %weight_ref.15, s32[1,12]{1,0:T(1,128)S(1)} %copy-done.10, bf16[512,512]{1,0:T(8,128)(2,1)} %first_product.1.rest_1_), custom_call_target="tpu_custom_call" | custom-call | flops 1000 | bytes 1000 | tf_op jit(solution)/shard_map/block_product/pallas_call | solution.py:42
  10.2 1.1 %collective-permute-start.8 = (bf16[512,512]{1,0:T(8,128)(2,1)}, bf16[512,512]{1,0:T(8,128)(2,1)}, u32[]{:S(2)}, u32[]{:S(2)}) collective-permute-start(bf16[512,512]{1,0:T(8,128)(2,1)} %get-tuple-element.16.rest_0_), channel_id=1, source_target_pairs={{0,2},{1,0},{3,1},{2,3},{4,5},{5,7},{7,6},{6,4},{8,10},{9,8},{11,9... | collective-permute-start | bytes 1572872 | tf_op jit(solution)/shard_map/ppermute | solution.py:333
  11.3 0.6 collective-permute-start.2
  11.9 1.2 %collective-permute-start.1 = (s32[1,12]{1,0:T(1,128)S(1)}, s32[1,12]{1,0:T(1,128)S(1)}, u32[]{:S(2)}, u32[]{:S(2)}) collective-permute-start(s32[1,12]{1,0:T(1,128)S(1)} %get-tuple-element.15.rest_0_), channel_id=1, source_target_pairs={{0,8},{4,12},{8,0},{12,4},{1,9},{5,13},{9,1},{13,5},{2,10},{6,14},... | collective-permute-start | bytes 152 | tf_op jit(solution)/shard_map/ppermute | solution.py:359
  13.1 0.1 collective-permute-start
  13.2 0.0 copy-start.9
  13.2 2.7 %block_product.8.rest_6_.rest_4_ = bf16[512,512]{1,0:T(8,128)(2,1)S(1)} custom-call(s32[1]{0:T(128)} %bitcast.3.first_ref, bf16[512,2048]{1,0:T(8,128)(2,1)S(1)} %copy-done, bf16[2048,4096]{1,0:T(8,128)(2,1)} %weight_ref.15, bf16[512,512]{1,0:T(8,128)(2,1)} %get-tuple-element.16.rest_0_), custom_call_target="tpu_custom_call" | custom-call | flops 1000 | bytes 1000 | tf_op jit(solution)/shard_map/block_product/pallas_call | solution.py:42
  16.0 0.0 collective-permute-done.2.rest_3_
  16.0 0.0 collective-permute-done.1.rest_2_
  16.0 0.0 collective-permute-done.rest_1_
  16.0 0.0 copy-done.9
  16.0 0.0 copy-done.11
  16.0 3.6 %pick_adapters.1 = (bf16[6,16,3072]{2,1,0:T(8,128)(2,1)S(1)}, bf16[6,16,3072]{2,1,0:T(8,128)(2,1)S(1)}, bf16[6,16,3072]{2,1,0:T(8,128)(2,1)S(1)}, bf16[6,16,3072...) custom-call(s32[1]{0:T(128)} %bitcast.me_ref, s32[512]{0:T(512)S(1)} %copy-done.9, s32[1,12]{1,0:T(1,128)S(1)} %copy-done.11, ...), custom_call_target="tpu_custom_call" | custom-call | flops 1000 | bytes 1000 | tf_op jit(solution)/shard_map/pick_adapters/pallas_call | solution.py:184
  19.6 0.2 collective-permute-start.3
  19.8 1.8 %collective-permute-start.4 = (bf16[6,16,3072]{2,1,0:T(8,128)(2,1)S(1)}, bf16[6,16,3072]{2,1,0:T(8,128)(2,1)S(1)}, u32[]{:S(2)}, u32[]{:S(2)}) collective-permute-start(bf16[6,16,3072]{2,1,0:T(8,128)(2,1)S(1)} %get-tuple-element.21), channel_id=1, source_target_pairs={{0,8},{4,12},{8,0},{12,4},{1,9},{5,13},{9,1},{13,5},{2,10},{6,14},... | collective-permute-start | bytes 1769480 | tf_op jit(solution)/shard_map/ppermute | solution.py:364
  21.5 0.1 collective-permute-start.5
  21.6 4.9 %collective-permute-done.6.rest_0_ = bf16[512,512]{1,0:T(8,128)(2,1)} collective-permute-done((bf16[512,512]{1,0:T(8,128)(2,1)}, bf16[512,512]{1,0:T(8,128)(2,1)}, u32[]{:S(2)}, u32[]{:S(2)}) %collective-permute-start.6) | collective-permute-done | bytes 524320 | tf_op jit(solution)/shard_map/ppermute | solution.py:333
  26.5 2.8 %block_product.9.rest_1_ = bf16[512,512]{1,0:T(8,128)(2,1)S(1)} custom-call(s32[1]{0:T(128)} %bitcast.5.first_ref, bf16[512,2048]{1,0:T(8,128)(2,1)S(1)} %copy-done, bf16[2048,4096]{1,0:T(8,128)(2,1)} %weight_ref.15, bf16[512,512]{1,0:T(8,128)(2,1)} %collective-permute-done.6.rest_0_, s32[24]{0:T(128)S(1)} %get-tuple-element.17.rest_1_.start_ref), custom_call_target="tpu_custom_call" | custom-call | flops 1000 | bytes 1000 | tf_op jit(solution)/shard_map/block_product/pallas_call | solution.py:42
  29.3 3.4 %collective-permute-start.7 = (bf16[512,512]{1,0:T(8,128)(2,1)S(1)}, bf16[512,512]{1,0:T(8,128)(2,1)S(1)}, u32[]{:S(2)}, u32[]{:S(2)}) collective-permute-start(bf16[512,512]{1,0:T(8,128)(2,1)S(1)} %block_product.9.rest_1_), channel_id=1, source_target_pairs={{0,1},{1,3},{3,2},{2,0},{4,6},{5,4},{7,5},{6,7},{8,9},{9,11},{11,1... | collective-permute-start | bytes 1572872 | tf_op jit(solution)/shard_map/ppermute | solution.py:333
  32.7 0.0 collective-permute-done.8.rest_0_
  32.7 3.5 %block_product.10.rest_0_ = bf16[512,512]{1,0:T(8,128)(2,1)} custom-call(s32[1]{0:T(128)} %bitcast.7.first_ref, bf16[512,2048]{1,0:T(8,128)(2,1)S(1)} %copy-done, bf16[2048,4096]{1,0:T(8,128)(2,1)} %weight_ref.15, bf16[512,512]{1,0:T(8,128)(2,1)} %collective-permute-done.8.rest_0_, bf16[512,512]{1,0:T(8,128)(2,1)S(1)} %block_product.9.rest_1_), custom_call_target="tpu_custom_call" | custom-call | flops 1000 | bytes 1000 | tf_op jit(solution)/shard_map/block_product/pallas_call | solution.py:42
  36.2 1.4 %collective-permute-start.12 = (bf16[512,512]{1,0:T(8,128)(2,1)}, bf16[512,512]{1,0:T(8,128)(2,1)}, u32[]{:S(2)}, u32[]{:S(2)}) collective-permute-start(bf16[512,512]{1,0:T(8,128)(2,1)} %block_product.10.rest_0_), channel_id=1, source_target_pairs={{0,2},{1,0},{3,1},{2,3},{4,5},{5,7},{7,6},{6,4},{8,10},{9,8},{11,9... | collective-permute-start | bytes 1572872 | tf_op jit(solution)/shard_map/ppermute | solution.py:333
  37.6 2.7 %block_product.11.rest_1_.rest_5_ = bf16[512,512]{1,0:T(8,128)(2,1)S(1)} custom-call(s32[1]{0:T(128)} %bitcast.6.first_ref, bf16[512,2048]{1,0:T(8,128)(2,1)S(1)} %copy-done, bf16[2048,4096]{1,0:T(8,128)(2,1)} %weight_ref.15, bf16[512,512]{1,0:T(8,128)(2,1)} %block_product.10.rest_0_), custom_call_target="tpu_custom_call" | custom-call | flops 20000000000 | bytes 1000 | tf_op jit(solution)/shard_map/block_product/pallas_call | solution.py:42
  40.3 0.0 copy-start.7
  40.3 13.6 %collective-permute-done.7.rest_0_ = bf16[512,512]{1,0:T(8,128)(2,1)S(1)} collective-permute-done((bf16[512,512]{1,0:T(8,128)(2,1)S(1)}, bf16[512,512]{1,0:T(8,128)(2,1)S(1)}, u32[]{:S(2)}, u32[]{:S(2)}) %collective-permute-start.7) | collective-permute-done | bytes 524320 | tf_op jit(solution)/shard_map/ppermute | solution.py:333
  53.9 3.4 %block_product.12.rest_4_ = bf16[512,512]{1,0:T(8,128)(2,1)} custom-call(s32[1]{0:T(128)} %bitcast.4.first_ref, bf16[512,2048]{1,0:T(8,128)(2,1)S(1)} %copy-done, bf16[2048,4096]{1,0:T(8,128)(2,1)} %weight_ref.15, bf16[512,512]{1,0:T(8,128)(2,1)S(1)} %collective-permute-done.7.rest_0_, bf16[512,512]{1,0:T(8,128)(2,1)S(1)} %block_product.11.rest_1_.rest_5_), custom_call_target="tpu_custom_call" | custom-call | flops 1000 | bytes 1000 | tf_op jit(solution)/shard_map/block_product/pallas_call | solution.py:42
  57.2 0.0 copy-done.7
  57.2 0.0 collective-permute-start.14
  57.3 0.0 collective-permute-done.3.rest_1_.rest_7_
  57.3 0.0 collective-permute-done.4.rest_2_.rest_8_
  57.3 0.0 copy-start.3
  57.3 0.0 collective-permute-done.5.rest_3_.rest_9_
  57.3 0.0 copy-start.5
  57.3 1.6 %low_sums.1.rest_1_.rest_0_ = f32[16,512]{1,0:T(8,128)S(1)} custom-call(s32[24]{0:T(128)S(1)} %get-tuple-element.17.rest_1_.start_ref, s32[24]{0:T(128)S(1)} %get-tuple-element.18.end_ref, bf16[512,2048]{1,0:T(8,128)(2,1)S(1)} %copy-done, bf16[6,16,3072]{2,1,0:T(8,128)(2,1)S(1)} %get-tuple-element.19.rest_0_.rest_6_, ...), custom_call_target="tpu_custom_call" | custom-call | flops 1000 | bytes 1000 | tf_op jit(solution)/shard_map/low_sums/pallas_call | solution.py:226
  58.9 0.0 copy-done.3
  58.9 0.0 copy-start.1
  58.9 0.8 copy-done.1
  59.7 0.5 collective-permute-start.11
  60.2 0.0 copy-done.5
  60.2 2.4 %collective-permute-start.10 = (f32[16,512]{1,0:T(8,128)S(1)}, f32[16,512]{1,0:T(8,128)S(1)}, u32[]{:S(2)}, u32[]{:S(2)}) collective-permute-start(f32[16,512]{1,0:T(8,128)S(1)} %low_sums.1.rest_1_.rest_0_), channel_id=1, source_target_pairs={{0,2},{1,3},{2,0},{3,1},{4,6},{5,7},{6,4},{7,5},{8,10},{9,11},{10,... | collective-permute-start | bytes 98312 | tf_op jit(solution)/shard_map/ppermute | solution.py:374
  62.6 1.5 %collective-permute-start.9 = (f32[16,512]{1,0:T(8,128)S(1)}, f32[16,512]{1,0:T(8,128)S(1)}, u32[]{:S(2)}, u32[]{:S(2)}) collective-permute-start(f32[16,512]{1,0:T(8,128)S(1)} %low_sums.1.rest_1_.rest_0_), channel_id=1, source_target_pairs={{0,1},{1,0},{2,3},{3,2},{4,5},{5,4},{6,7},{7,6},{8,9},{9,8},{10,11... | collective-permute-start | bytes 98312 | tf_op jit(solution)/shard_map/ppermute | solution.py:374
  64.1 0.0 collective-permute-done.12.rest_0_
  64.1 0.0 copy-start.2
  64.1 0.0 copy-start.8
  64.1 2.9 %block_product.13.rest_10_ = bf16[512,512]{1,0:T(8,128)(2,1)S(1)} custom-call(s32[1]{0:T(128)} %bitcast.8.first_ref, bf16[512,2048]{1,0:T(8,128)(2,1)S(1)} %copy-done, bf16[2048,4096]{1,0:T(8,128)(2,1)} %weight_ref.15, bf16[512,512]{1,0:T(8,128)(2,1)} %collective-permute-done.12.rest_0_, f32[16,512]{1,0:T(8,128)S(1)} %low_sums.1.rest_1_.rest_0_), custom_call_target="tpu_custom_call" | custom-call | flops 1000 | bytes 1000 | tf_op jit(solution)/shard_map/block_product/pallas_call | solution.py:42
  67.0 2.1 %collective-permute-start.13 = (bf16[512,512]{1,0:T(8,128)(2,1)S(1)}, bf16[512,512]{1,0:T(8,128)(2,1)S(1)}, u32[]{:S(2)}, u32[]{:S(2)}) collective-permute-start(bf16[512,512]{1,0:T(8,128)(2,1)S(1)} %block_product.13.rest_10_), channel_id=1, source_target_pairs={{0,2},{1,0},{3,1},{2,3},{4,5},{5,7},{7,6},{6,4},{8,10},{9,8},{11,9... | collective-permute-start | bytes 1572872 | tf_op jit(solution)/shard_map/ppermute | solution.py:333
  69.1 0.0 collective-permute-done.11.rest_3_
  69.1 8.4 %collective-permute-done.10.rest_2_ = f32[16,512]{1,0:T(8,128)S(1)} collective-permute-done((f32[16,512]{1,0:T(8,128)S(1)}, f32[16,512]{1,0:T(8,128)S(1)}, u32[]{:S(2)}, u32[]{:S(2)}) %collective-permute-start.10) | collective-permute-done | bytes 32800 | tf_op jit(solution)/shard_map/ppermute | solution.py:374
  77.5 0.0 collective-permute-done.9.rest_1_
  77.5 0.0 copy-done.2
  77.6 0.0 copy-done.4
  77.6 0.0 copy-done.6
  77.6 0.0 copy-done.8
  77.6 1.3 %adapter_term.1 = (f32[512,512]{1,0:T(8,128)S(1)}, f32[512,512]{1,0:T(8,128)S(1)}) custom-call(s32[24]{0:T(128)S(1)} %get-tuple-element.17.rest_1_.start_ref, s32[24]{0:T(128)S(1)} %get-tuple-element.18.end_ref, f32[16,512]{1,0:T(8,128)S(1)} %low_sums.1.rest_1_.rest_0_, f32[16,512]{1,0:T(8,128)S(1)} %collective-permute-done.9.rest_1_, ...), custom_call_target="tpu_custom_call" | custom-call | flops 1000 | bytes 1000 | tf_op jit(solution)/shard_map/adapter_term/pallas_call | solution.py:272
  78.9 0.0 collective-permute-done.14.rest_0_
  78.9 3.2 %finish.2.rest_1_ = bf16[512,1024]{1,0:T(8,128)(2,1)} custom-call(f32[512,512]{1,0:T(8,128)S(1)} %get-tuple-element.24.term_ref, bf16[512,512]{1,0:T(8,128)(2,1)} %collective-permute-done.14.rest_0_), custom_call_target="tpu_custom_call" | custom-call | flops 20000000000 | bytes 1000 | tf_op jit(solution)/shard_map/finish/pallas_call | solution.py:299
  82.1 0.0 collective-permute-done.13.rest_0_
  82.1 1.4 %finish.3 = bf16[512,1024]{1,0:T(8,128)(2,1)} custom-call(f32[512,512]{1,0:T(8,128)S(1)} %get-tuple-element.23.term_ref, bf16[512,512]{1,0:T(8,128)(2,1)S(1)} %collective-permute-done.13.rest_0_, bf16[512,1024]{1,0:T(8,128)(2,1)} %finish.2.rest_1_), custom_call_target="tpu_custom_call", output_to_operand_aliasing={{}: (2, {})} | custom-call | flops 1000 | bytes 1000 | tf_op jit(solution)/shard_map/finish/pallas_call | solution.py:299
  (3 shorter events, 0.0 us)
Async XLA Ops:
  0.0 6.7 %copy-start = (bf16[512,2048]{1,0:T(8,128)(2,1)S(1)}, bf16[512,2048]{1,0:T(8,128)(2,1)}, u32[]{:S(2)}) copy-start(bf16[512,2048]{1,0:T(8,128)(2,1)} %rows_ref.17) | copy-start | bytes 6291460
  0.0 6.7 %copy-start.10 = (s32[1,12]{1,0:T(1,128)S(1)}, s32[1,12]{1,0:T(1,128)}, u32[]{:S(2)}) copy-start(s32[1,12]{1,0:T(1,128)} %rest_0_.1) | copy-start | bytes 148
  3.6 22.9 %collective-permute-start.6 = (bf16[512,512]{1,0:T(8,128)(2,1)}, bf16[512,512]{1,0:T(8,128)(2,1)}, u32[]{:S(2)}, u32[]{:S(2)}) collective-permute-start(bf16[512,512]{1,0:T(8,128)(2,1)} %first_product.1.rest_1_), channel_id=1, source_target_pairs={{0,1},{1,3},{3,2},{2,0},{4,6},{5,4},{7,5},{6,7},{8,9},{9,11},{11,1... | collective-permute-start | bytes 1572872 | tf_op jit(solution)/shard_map/ppermute | solution.py:333
  10.2 22.5 %collective-permute-start.8 = (bf16[512,512]{1,0:T(8,128)(2,1)}, bf16[512,512]{1,0:T(8,128)(2,1)}, u32[]{:S(2)}, u32[]{:S(2)}) collective-permute-start(bf16[512,512]{1,0:T(8,128)(2,1)} %get-tuple-element.16.rest_0_), channel_id=1, source_target_pairs={{0,2},{1,0},{3,1},{2,3},{4,5},{5,7},{7,6},{6,4},{8,10},{9,8},{11,9... | collective-permute-start | bytes 1572872 | tf_op jit(solution)/shard_map/ppermute | solution.py:333
  11.3 4.7 %collective-permute-start.2 = (s32[1,12]{1,0:T(1,128)S(1)}, s32[1,12]{1,0:T(1,128)S(1)}, u32[]{:S(2)}, u32[]{:S(2)}) collective-permute-start(s32[1,12]{1,0:T(1,128)S(1)} %get-tuple-element.15.rest_0_), channel_id=1, source_target_pairs={{0,12},{4,8},{8,4},{12,0},{1,13},{5,9},{9,5},{13,1},{2,14},{6,10},... | collective-permute-start | bytes 152 | tf_op jit(solution)/shard_map/ppermute | solution.py:359
  11.9 4.1 %collective-permute-start.1 = (s32[1,12]{1,0:T(1,128)S(1)}, s32[1,12]{1,0:T(1,128)S(1)}, u32[]{:S(2)}, u32[]{:S(2)}) collective-permute-start(s32[1,12]{1,0:T(1,128)S(1)} %get-tuple-element.15.rest_0_), channel_id=1, source_target_pairs={{0,8},{4,12},{8,0},{12,4},{1,9},{5,13},{9,1},{13,5},{2,10},{6,14},... | collective-permute-start | bytes 152 | tf_op jit(solution)/shard_map/ppermute | solution.py:359
  13.1 2.9 %collective-permute-start = (s32[1,12]{1,0:T(1,128)S(1)}, s32[1,12]{1,0:T(1,128)S(1)}, u32[]{:S(2)}, u32[]{:S(2)}) collective-permute-start(s32[1,12]{1,0:T(1,128)S(1)} %get-tuple-element.15.rest_0_), channel_id=1, source_target_pairs={{0,4},{4,0},{8,12},{12,8},{1,5},{5,1},{9,13},{13,9},{2,6},{6,2},{1... | collective-permute-start | bytes 152 | tf_op jit(solution)/shard_map/ppermute | solution.py:359
  13.2 2.8 %copy-start.9 = (s32[512]{0:T(512)S(1)}, s32[512]{0:T(512)}, u32[]{:S(2)}) copy-start(s32[512]{0:T(512)} %table_ref.1) | copy-start | bytes 6148
  13.2 2.9 %copy-start.11 = (s32[1,12]{1,0:T(1,128)S(1)}, s32[1,12]{1,0:T(1,128)}, u32[]{:S(2)}) copy-start(s32[1,12]{1,0:T(1,128)} %lens_ref.1) | copy-start | bytes 148
  19.6 37.6 %collective-permute-start.3 = (bf16[6,16,3072]{2,1,0:T(8,128)(2,1)S(1)}, bf16[6,16,3072]{2,1,0:T(8,128)(2,1)S(1)}, u32[]{:S(2)}, u32[]{:S(2)}) collective-permute-start(bf16[6,16,3072]{2,1,0:T(8,128)(2,1)S(1)} %get-tuple-element.20), channel_id=1, source_target_pairs={{0,4},{4,0},{8,12},{12,8},{1,5},{5,1},{9,13},{13,9},{2,6},{6,2},{1... | collective-permute-start | bytes 1769480 | tf_op jit(solution)/shard_map/ppermute | solution.py:364
  19.8 37.5 %collective-permute-start.4 = (bf16[6,16,3072]{2,1,0:T(8,128)(2,1)S(1)}, bf16[6,16,3072]{2,1,0:T(8,128)(2,1)S(1)}, u32[]{:S(2)}, u32[]{:S(2)}) collective-permute-start(bf16[6,16,3072]{2,1,0:T(8,128)(2,1)S(1)} %get-tuple-element.21), channel_id=1, source_target_pairs={{0,8},{4,12},{8,0},{12,4},{1,9},{5,13},{9,1},{13,5},{2,10},{6,14},... | collective-permute-start | bytes 1769480 | tf_op jit(solution)/shard_map/ppermute | solution.py:364
  21.5 35.8 %collective-permute-start.5 = (bf16[6,16,3072]{2,1,0:T(8,128)(2,1)S(1)}, bf16[6,16,3072]{2,1,0:T(8,128)(2,1)S(1)}, u32[]{:S(2)}, u32[]{:S(2)}) collective-permute-start(bf16[6,16,3072]{2,1,0:T(8,128)(2,1)S(1)} %get-tuple-element.22), channel_id=1, source_target_pairs={{0,12},{4,8},{8,4},{12,0},{1,13},{5,9},{9,5},{13,1},{2,14},{6,10},... | collective-permute-start | bytes 1769480 | tf_op jit(solution)/shard_map/ppermute | solution.py:364
  29.3 24.6 %collective-permute-start.7 = (bf16[512,512]{1,0:T(8,128)(2,1)S(1)}, bf16[512,512]{1,0:T(8,128)(2,1)S(1)}, u32[]{:S(2)}, u32[]{:S(2)}) collective-permute-start(bf16[512,512]{1,0:T(8,128)(2,1)S(1)} %block_product.9.rest_1_), channel_id=1, source_target_pairs={{0,1},{1,3},{3,2},{2,0},{4,6},{5,4},{7,5},{6,7},{8,9},{9,11},{11,1... | collective-permute-start | bytes 1572872 | tf_op jit(solution)/shard_map/ppermute | solution.py:333
  36.2 27.9 %collective-permute-start.12 = (bf16[512,512]{1,0:T(8,128)(2,1)}, bf16[512,512]{1,0:T(8,128)(2,1)}, u32[]{:S(2)}, u32[]{:S(2)}) collective-permute-start(bf16[512,512]{1,0:T(8,128)(2,1)} %block_product.10.rest_0_), channel_id=1, source_target_pairs={{0,2},{1,0},{3,1},{2,3},{4,5},{5,7},{7,6},{6,4},{8,10},{9,8},{11,9... | collective-permute-start | bytes 1572872 | tf_op jit(solution)/shard_map/ppermute | solution.py:333
  40.3 17.0 %copy-start.7 = (bf16[512,512]{1,0:T(8,128)(2,1)}, bf16[512,512]{1,0:T(8,128)(2,1)S(1)}, u32[]{:S(2)}) copy-start(bf16[512,512]{1,0:T(8,128)(2,1)S(1)} %block_product.11.rest_1_.rest_5_) | copy-start | bytes 1572868
  57.2 21.6 %collective-permute-start.14 = (bf16[512,512]{1,0:T(8,128)(2,1)}, bf16[512,512]{1,0:T(8,128)(2,1)}, u32[]{:S(2)}, u32[]{:S(2)}) collective-permute-start(bf16[512,512]{1,0:T(8,128)(2,1)} %block_product.12.rest_4_), channel_id=1, source_target_pairs={{0,1},{1,3},{3,2},{2,0},{4,6},{5,4},{7,5},{6,7},{8,9},{9,11},{11,1... | collective-permute-start | bytes 1572872 | tf_op jit(solution)/shard_map/ppermute | solution.py:333
  57.3 1.6 %copy-start.3 = (bf16[6,16,3072]{2,1,0:T(8,128)(2,1)}, bf16[6,16,3072]{2,1,0:T(8,128)(2,1)S(1)}, u32[]{:S(2)}) copy-start(bf16[6,16,3072]{2,1,0:T(8,128)(2,1)S(1)} %collective-permute-done.4.rest_2_.rest_8_) | copy-start | bytes 1769476
  57.3 2.9 %copy-start.5 = (bf16[6,16,3072]{2,1,0:T(8,128)(2,1)}, bf16[6,16,3072]{2,1,0:T(8,128)(2,1)S(1)}, u32[]{:S(2)}) copy-start(bf16[6,16,3072]{2,1,0:T(8,128)(2,1)S(1)} %collective-permute-done.5.rest_3_.rest_9_) | copy-start | bytes 1769476
  58.9 0.8 copy-start.1
  59.7 9.4 %collective-permute-start.11 = (f32[16,512]{1,0:T(8,128)S(1)}, f32[16,512]{1,0:T(8,128)S(1)}, u32[]{:S(2)}, u32[]{:S(2)}) collective-permute-start(f32[16,512]{1,0:T(8,128)S(1)} %low_sums.1.rest_1_.rest_0_), channel_id=1, source_target_pairs={{0,3},{1,2},{2,1},{3,0},{4,7},{5,6},{6,5},{7,4},{8,11},{9,10},{10,... | collective-permute-start | bytes 98312 | tf_op jit(solution)/shard_map/ppermute | solution.py:374
  60.2 17.4 %collective-permute-start.10 = (f32[16,512]{1,0:T(8,128)S(1)}, f32[16,512]{1,0:T(8,128)S(1)}, u32[]{:S(2)}, u32[]{:S(2)}) collective-permute-start(f32[16,512]{1,0:T(8,128)S(1)} %low_sums.1.rest_1_.rest_0_), channel_id=1, source_target_pairs={{0,2},{1,3},{2,0},{3,1},{4,6},{5,7},{6,4},{7,5},{8,10},{9,11},{10,... | collective-permute-start | bytes 98312 | tf_op jit(solution)/shard_map/ppermute | solution.py:374
  62.6 14.9 %collective-permute-start.9 = (f32[16,512]{1,0:T(8,128)S(1)}, f32[16,512]{1,0:T(8,128)S(1)}, u32[]{:S(2)}, u32[]{:S(2)}) collective-permute-start(f32[16,512]{1,0:T(8,128)S(1)} %low_sums.1.rest_1_.rest_0_), channel_id=1, source_target_pairs={{0,1},{1,0},{2,3},{3,2},{4,5},{5,4},{6,7},{7,6},{8,9},{9,8},{10,11... | collective-permute-start | bytes 98312 | tf_op jit(solution)/shard_map/ppermute | solution.py:374
  64.1 13.5 %copy-start.2 = (bf16[6,16,3072]{2,1,0:T(8,128)(2,1)S(1)}, bf16[6,16,3072]{2,1,0:T(8,128)(2,1)}, u32[]{:S(2)}) copy-start(bf16[6,16,3072]{2,1,0:T(8,128)(2,1)} %copy-done.1) | copy-start | bytes 1769476
  64.1 13.5 %copy-start.4 = (bf16[6,16,3072]{2,1,0:T(8,128)(2,1)S(1)}, bf16[6,16,3072]{2,1,0:T(8,128)(2,1)}, u32[]{:S(2)}) copy-start(bf16[6,16,3072]{2,1,0:T(8,128)(2,1)} %copy-done.3) | copy-start | bytes 1769476
  64.1 13.5 %copy-start.6 = (bf16[6,16,3072]{2,1,0:T(8,128)(2,1)S(1)}, bf16[6,16,3072]{2,1,0:T(8,128)(2,1)}, u32[]{:S(2)}) copy-start(bf16[6,16,3072]{2,1,0:T(8,128)(2,1)} %copy-done.5) | copy-start | bytes 1769476
  64.1 13.5 %copy-start.8 = (bf16[512,512]{1,0:T(8,128)(2,1)S(1)}, bf16[512,512]{1,0:T(8,128)(2,1)}, u32[]{:S(2)}) copy-start(bf16[512,512]{1,0:T(8,128)(2,1)} %copy-done.7) | copy-start | bytes 1572868
  67.0 15.0 %collective-permute-start.13 = (bf16[512,512]{1,0:T(8,128)(2,1)S(1)}, bf16[512,512]{1,0:T(8,128)(2,1)S(1)}, u32[]{:S(2)}, u32[]{:S(2)}) collective-permute-start(bf16[512,512]{1,0:T(8,128)(2,1)S(1)} %block_product.13.rest_10_), channel_id=1, source_target_pairs={{0,2},{1,0},{3,1},{2,3},{4,5},{5,7},{7,6},{6,4},{8,10},{9,8},{11,9... | collective-permute-start | bytes 1572872 | tf_op jit(solution)/shard_map/ppermute | solution.py:333

commit v13 on v10

--- a/solution.py
+++ b/solution.py
@@ -337,7 +337,7 @@
         return block_product(rows, weight, start_of(back, piece), width, **options)
 
     last = first_product(rows, weight, start_of(1, 0), width)
-    moving, owns = [move(last, 0)], []
+    moving = [move(last, 0)]
     for piece in range(1, PIECES):
         last, ids = partial(1, piece, after=[last], ids=ids)
         moving.append(move(last, piece))
@@ -345,6 +345,8 @@
     all_ids = [ids]
     for x in range(1, req_total):
         all_ids.append(lax.ppermute(ids, "req", [(i, i ^ x) for i in range(req_total)]))
+    last = partial(0, 0, after=[last])
+    owns = [last]
     packs, starts, ends = pick_adapters(me_req, table, all_ids, lens, down, up, [last])
     for x in range(1, req_total):
         packs[x] = lax.ppermute(packs[x], "req", [(i, i ^ x) for i in range(req_total)])
@@ -361,7 +363,7 @@
                 last = low
             last = partial(1 + step, piece, addends=[moving[piece]], after=[last])
             moving[piece] = move(last, piece)
-            if step == 1:
+            if step == 1 and piece > 0:
                 last = partial(0, piece, after=[last], cost=LARGE)
                 owns.append(last)
 

time: 81.6 us -> 81.1 us (level)
  waiting for transfers between devices: 12.2 us -> 17.2 us
  starting transfers between devices: 31.5 us -> 26.7 us
    ppermute x6, waiting for transfers between devices: 5.73 us -> 12.5 us  [move(): return lax.ppermute(value, ('req', 'tp'), pairs)]
    ppermute x3, starting transfers between devices: 7.8 us -> 4.51 us  [local(): lows.append(lax.ppermute(low, 'tp', pairs))]
    ppermute x3, waiting for transfers between devices: 2.28 us -> 0.01 us  [local(): lax.ppermute(ids, 'req', [(i, i ^ x) for i in range(req_total)])]
    ppermute x3, starting transfers between devices: 3.21 us -> 1.86 us  [local(): lax.ppermute(ids, 'req', [(i, i ^ x) for i in range(req_total)])]
  transfers between devices with their start and end apart: 15 -> 15, of which waited for: 5 -> 6; matrix products, arithmetic and copies ran while one was open for 0% -> 0% of each run, Pallas kernels for 39% -> 38%
where the time goes in v13:
time: 81.1 us; the launch traced here: 80.7 us
  Pallas kernels  35.7 us (44%)
  starting transfers between devices  26.7 us (33%)
  waiting for transfers between devices  17.2 us (21%)
  local copies, waits for them, and re-layouts  0.85 us (1%)
    pallas_call x7, Pallas kernels, block_product(): pl.pallas_call(functools.partial(product_kernel, len(addends), with_ids),...  21.5 us
    ppermute x6, starting transfers between devices, move(): return lax.ppermute(value, ('req', 'tp'), pairs)  17.9 us
    ppermute x6, waiting for transfers between devices, move(): return lax.ppermute(value, ('req', 'tp'), pairs)  12.5 us
    ppermute x3, waiting for transfers between devices, local(): lows.append(lax.ppermute(low, 'tp', pairs))  4.65 us
    pallas_call x2, Pallas kernels, finish(): pl.pallas_call(functools.partial(finish_kernel, len(arrivals)), grid=(row...  4.6 us
    ppermute x3, starting transfers between devices, local(): lows.append(lax.ppermute(low, 'tp', pairs))  4.51 us
    pallas_call x1, Pallas kernels, first_product(): pl.pallas_call(functools.partial(first_kernel, chunk), in_specs=[pl.Block...  3.62 us
    pallas_call x1, Pallas kernels, pick_adapters(): pl.pallas_call(functools.partial(pick_kernel, peers, len(after)), in_spec...  3.15 us
  transfers between devices with their start and end apart: 15, of which 6 were waited for; matrix products, arithmetic and copies ran while one was open for 0% of the time, Pallas kernels for 38%

profile of v13, /device:TPU:0, one launch (start us, length us, event | category | flops | bytes accessed | tf_op | source)
XLA Modules:
  0.0 80.7 jit_solution(1029515878145299201)
XLA Ops:
  0.0 0.0 copy-start
  0.0 0.0 copy-start.10
  0.0 3.6 %first_product.1.rest_1_ = bf16[512,512]{1,0:T(8,128)(2,1)} custom-call(s32[1]{0:T(128)} %bitcast.2.first_ref, bf16[512,2048]{1,0:T(8,128)(2,1)} %rows_ref.17, bf16[2048,4096]{1,0:T(8,128)(2,1)} %weight_ref.15), custom_call_target="tpu_custom_call" | custom-call | flops 1000 | bytes 1000 | tf_op jit(solution)/shard_map/first_product/pallas_call | solution.py:95
  3.6 3.1 %collective-permute-start.6 = (bf16[512,512]{1,0:T(8,128)(2,1)}, bf16[512,512]{1,0:T(8,128)(2,1)}, u32[]{:S(2)}, u32[]{:S(2)}) collective-permute-start(bf16[512,512]{1,0:T(8,128)(2,1)} %first_product.1.rest_1_), channel_id=1, source_target_pairs={{0,1},{1,2},{2,3},{3,0},{4,7},{5,4},{6,5},{7,6},{8,9},{9,10},{10,1... | collective-permute-start | bytes 1572872 | tf_op jit(solution)/shard_map/ppermute | solution.py:329
  6.7 0.0 copy-done
  6.7 0.0 copy-done.10
  6.7 3.5 %block_product.7 = (bf16[512,512]{1,0:T(8,128)(2,1)}, s32[1,12]{1,0:T(1,128)S(1)}) custom-call(s32[1]{0:T(128)} %bitcast.1.first_ref, bf16[512,2048]{1,0:T(8,128)(2,1)S(1)} %copy-done, bf16[2048,4096]{1,0:T(8,128)(2,1)} %weight_ref.15, s32[1,12]{1,0:T(1,128)S(1)} %copy-done.10, bf16[512,512]{1,0:T(8,128)(2,1)} %first_product.1.rest_1_), custom_call_target="tpu_custom_call" | custom-call | flops 1000 | bytes 1000 | tf_op jit(solution)/shard_map/block_product/pallas_call | solution.py:42
  10.2 2.1 %collective-permute-start.8 = (bf16[512,512]{1,0:T(8,128)(2,1)}, bf16[512,512]{1,0:T(8,128)(2,1)}, u32[]{:S(2)}, u32[]{:S(2)}) collective-permute-start(bf16[512,512]{1,0:T(8,128)(2,1)} %get-tuple-element.16.rest_0_), channel_id=1, source_target_pairs={{0,3},{1,0},{2,1},{3,2},{4,5},{5,6},{6,7},{7,4},{8,11},{9,8},{10,9... | collective-permute-start | bytes 1572872 | tf_op jit(solution)/shard_map/ppermute | solution.py:329
  12.3 0.6 collective-permute-start.2
  12.9 1.1 %collective-permute-start.1 = (s32[1,12]{1,0:T(1,128)S(1)}, s32[1,12]{1,0:T(1,128)S(1)}, u32[]{:S(2)}, u32[]{:S(2)}) collective-permute-start(s32[1,12]{1,0:T(1,128)S(1)} %get-tuple-element.15.rest_0_), channel_id=1, source_target_pairs={{0,8},{4,12},{8,0},{12,4},{1,9},{5,13},{9,1},{13,5},{2,10},{6,14},... | collective-permute-start | bytes 152 | tf_op jit(solution)/shard_map/ppermute | solution.py:347
  14.0 0.2 collective-permute-start
  14.2 0.0 copy-start.9
  14.2 0.0 copy-start.11
  14.2 2.7 %block_product.8.rest_6_.rest_4_ = bf16[512,512]{1,0:T(8,128)(2,1)S(1)} custom-call(s32[1]{0:T(128)} %bitcast.3.first_ref, bf16[512,2048]{1,0:T(8,128)(2,1)S(1)} %copy-done, bf16[2048,4096]{1,0:T(8,128)(2,1)} %weight_ref.15, bf16[512,512]{1,0:T(8,128)(2,1)} %get-tuple-element.16.rest_0_), custom_call_target="tpu_custom_call" | custom-call | flops 1000 | bytes 1000 | tf_op jit(solution)/shard_map/block_product/pallas_call | solution.py:42
  17.0 0.0 collective-permute-done.2.rest_3_
  17.0 0.0 collective-permute-done.1.rest_2_
  17.0 0.0 collective-permute-done.rest_1_
  17.0 0.0 copy-done.9
  17.0 0.0 copy-done.11
  17.0 3.2 %pick_adapters.1 = (bf16[6,16,3072]{2,1,0:T(8,128)(2,1)S(1)}, bf16[6,16,3072]{2,1,0:T(8,128)(2,1)S(1)}, bf16[6,16,3072]{2,1,0:T(8,128)(2,1)S(1)}, bf16[6,16,3072...) custom-call(s32[1]{0:T(128)} %bitcast.me_ref, s32[512]{0:T(512)S(1)} %copy-done.9, s32[1,12]{1,0:T(1,128)S(1)} %copy-done.11, ...), custom_call_target="tpu_custom_call" | custom-call | flops 1000 | bytes 1000 | tf_op jit(solution)/shard_map/pick_adapters/pallas_call | solution.py:184
  20.2 0.7 collective-permute-start.3
  20.9 1.7 %collective-permute-start.4 = (bf16[6,16,3072]{2,1,0:T(8,128)(2,1)S(1)}, bf16[6,16,3072]{2,1,0:T(8,128)(2,1)S(1)}, u32[]{:S(2)}, u32[]{:S(2)}) collective-permute-start(bf16[6,16,3072]{2,1,0:T(8,128)(2,1)S(1)} %get-tuple-element.21), channel_id=1, source_target_pairs={{0,8},{4,12},{8,0},{12,4},{1,9},{5,13},{9,1},{13,5},{2,10},{6,14},... | collective-permute-start | bytes 1769480 | tf_op jit(solution)/shard_map/ppermute | solution.py:352
  22.6 0.1 collective-permute-start.5
  22.7 0.0 collective-permute-done.6.rest_0_
  22.7 2.8 %block_product.9.rest_1_ = bf16[512,512]{1,0:T(8,128)(2,1)S(1)} custom-call(s32[1]{0:T(128)} %bitcast.5.first_ref, bf16[512,2048]{1,0:T(8,128)(2,1)S(1)} %copy-done, bf16[2048,4096]{1,0:T(8,128)(2,1)} %weight_ref.15, bf16[512,512]{1,0:T(8,128)(2,1)} %collective-permute-done.6.rest_0_, s32[24]{0:T(128)S(1)} %get-tuple-element.17.rest_1_.start_ref), custom_call_target="tpu_custom_call" | custom-call | flops 1000 | bytes 1000 | tf_op jit(solution)/shard_map/block_product/pallas_call | solution.py:42
  25.5 6.6 %collective-permute-start.7 = (bf16[512,512]{1,0:T(8,128)(2,1)S(1)}, bf16[512,512]{1,0:T(8,128)(2,1)S(1)}, u32[]{:S(2)}, u32[]{:S(2)}) collective-permute-start(bf16[512,512]{1,0:T(8,128)(2,1)S(1)} %block_product.9.rest_1_), channel_id=1, source_target_pairs={{0,1},{1,2},{2,3},{3,0},{4,7},{5,4},{6,5},{7,6},{8,9},{9,10},{10,1... | collective-permute-start | bytes 1572872 | tf_op jit(solution)/shard_map/ppermute | solution.py:329
  32.1 0.0 collective-permute-done.8.rest_0_
  32.1 3.5 %block_product.10.rest_0_ = bf16[512,512]{1,0:T(8,128)(2,1)} custom-call(s32[1]{0:T(128)} %bitcast.7.first_ref, bf16[512,2048]{1,0:T(8,128)(2,1)S(1)} %copy-done, bf16[2048,4096]{1,0:T(8,128)(2,1)} %weight_ref.15, bf16[512,512]{1,0:T(8,128)(2,1)} %collective-permute-done.8.rest_0_, bf16[512,512]{1,0:T(8,128)(2,1)S(1)} %block_product.9.rest_1_), custom_call_target="tpu_custom_call" | custom-call | flops 1000 | bytes 1000 | tf_op jit(solution)/shard_map/block_product/pallas_call | solution.py:42
  35.6 3.7 %collective-permute-start.12 = (bf16[512,512]{1,0:T(8,128)(2,1)}, bf16[512,512]{1,0:T(8,128)(2,1)}, u32[]{:S(2)}, u32[]{:S(2)}) collective-permute-start(bf16[512,512]{1,0:T(8,128)(2,1)} %block_product.10.rest_0_), channel_id=1, source_target_pairs={{0,3},{1,0},{2,1},{3,2},{4,5},{5,6},{6,7},{7,4},{8,11},{9,8},{10,9... | collective-permute-start | bytes 1572872 | tf_op jit(solution)/shard_map/ppermute | solution.py:329
  39.2 2.7 %block_product.11.rest_1_.rest_5_ = bf16[512,512]{1,0:T(8,128)(2,1)S(1)} custom-call(s32[1]{0:T(128)} %bitcast.6.first_ref, bf16[512,2048]{1,0:T(8,128)(2,1)S(1)} %copy-done, bf16[2048,4096]{1,0:T(8,128)(2,1)} %weight_ref.15, bf16[512,512]{1,0:T(8,128)(2,1)} %block_product.10.rest_0_), custom_call_target="tpu_custom_call" | custom-call | flops 20000000000 | bytes 1000 | tf_op jit(solution)/shard_map/block_product/pallas_call | solution.py:42
  41.9 0.0 copy-start.7
  42.0 2.6 %collective-permute-done.7.rest_0_ = bf16[512,512]{1,0:T(8,128)(2,1)S(1)} collective-permute-done((bf16[512,512]{1,0:T(8,128)(2,1)S(1)}, bf16[512,512]{1,0:T(8,128)(2,1)S(1)}, u32[]{:S(2)}, u32[]{:S(2)}) %collective-permute-start.7) | collective-permute-done | bytes 524320 | tf_op jit(solution)/shard_map/ppermute | solution.py:329
  44.6 3.4 %block_product.12.rest_4_ = bf16[512,512]{1,0:T(8,128)(2,1)} custom-call(s32[1]{0:T(128)} %bitcast.4.first_ref, bf16[512,2048]{1,0:T(8,128)(2,1)S(1)} %copy-done, bf16[2048,4096]{1,0:T(8,128)(2,1)} %weight_ref.15, bf16[512,512]{1,0:T(8,128)(2,1)S(1)} %collective-permute-done.7.rest_0_, bf16[512,512]{1,0:T(8,128)(2,1)S(1)} %block_product.11.rest_1_.rest_5_), custom_call_target="tpu_custom_call" | custom-call | flops 1000 | bytes 1000 | tf_op jit(solution)/shard_map/block_product/pallas_call | solution.py:42
  48.0 0.0 copy-done.7
  48.0 2.4 %collective-permute-start.14 = (bf16[512,512]{1,0:T(8,128)(2,1)}, bf16[512,512]{1,0:T(8,128)(2,1)}, u32[]{:S(2)}, u32[]{:S(2)}) collective-permute-start(bf16[512,512]{1,0:T(8,128)(2,1)} %block_product.12.rest_4_), channel_id=1, source_target_pairs={{0,1},{1,2},{2,3},{3,0},{4,7},{5,4},{6,5},{7,6},{8,9},{9,10},{10,1... | collective-permute-start | bytes 1572872 | tf_op jit(solution)/shard_map/ppermute | solution.py:329
  50.3 0.0 collective-permute-done.3.rest_1_.rest_7_
  50.3 0.0 collective-permute-done.4.rest_2_.rest_8_
  50.3 0.0 copy-start.3
  50.3 0.0 collective-permute-done.5.rest_3_.rest_9_
  50.3 0.0 copy-start.5
  50.3 1.5 %low_sums.1.rest_1_.rest_0_ = f32[16,512]{1,0:T(8,128)S(1)} custom-call(s32[24]{0:T(128)S(1)} %get-tuple-element.17.rest_1_.start_ref, s32[24]{0:T(128)S(1)} %get-tuple-element.18.end_ref, bf16[512,2048]{1,0:T(8,128)(2,1)S(1)} %copy-done, bf16[6,16,3072]{2,1,0:T(8,128)(2,1)S(1)} %get-tuple-element.19.rest_0_.rest_6_, ...), custom_call_target="tpu_custom_call" | custom-call | flops 1000 | bytes 1000 | tf_op jit(solution)/shard_map/low_sums/pallas_call | solution.py:226
  51.9 0.0 copy-done.3
  51.9 0.0 copy-start.1
  51.9 0.8 copy-done.1
  52.7 3.4 %collective-permute-start.11 = (f32[16,512]{1,0:T(8,128)S(1)}, f32[16,512]{1,0:T(8,128)S(1)}, u32[]{:S(2)}, u32[]{:S(2)}) collective-permute-start(f32[16,512]{1,0:T(8,128)S(1)} %low_sums.1.rest_1_.rest_0_), channel_id=1, source_target_pairs={{0,3},{1,2},{2,1},{3,0},{4,7},{5,6},{6,5},{7,4},{8,11},{9,10},{10,... | collective-permute-start | bytes 98312 | tf_op jit(solution)/shard_map/ppermute | solution.py:362
  56.1 0.0 copy-done.5
  56.1 0.9 %collective-permute-start.10 = (f32[16,512]{1,0:T(8,128)S(1)}, f32[16,512]{1,0:T(8,128)S(1)}, u32[]{:S(2)}, u32[]{:S(2)}) collective-permute-start(f32[16,512]{1,0:T(8,128)S(1)} %low_sums.1.rest_1_.rest_0_), channel_id=1, source_target_pairs={{0,2},{1,3},{2,0},{3,1},{4,6},{5,7},{6,4},{7,5},{8,10},{9,11},{10,... | collective-permute-start | bytes 98312 | tf_op jit(solution)/shard_map/ppermute | solution.py:362
  57.1 0.2 collective-permute-start.9
  57.2 4.1 %collective-permute-done.12.rest_0_ = bf16[512,512]{1,0:T(8,128)(2,1)} collective-permute-done((bf16[512,512]{1,0:T(8,128)(2,1)}, bf16[512,512]{1,0:T(8,128)(2,1)}, u32[]{:S(2)}, u32[]{:S(2)}) %collective-permute-start.12) | collective-permute-done | bytes 524320 | tf_op jit(solution)/shard_map/ppermute | solution.py:329
  61.4 0.0 copy-start.2
  61.4 2.9 %block_product.13.rest_10_ = bf16[512,512]{1,0:T(8,128)(2,1)S(1)} custom-call(s32[1]{0:T(128)} %bitcast.8.first_ref, bf16[512,2048]{1,0:T(8,128)(2,1)S(1)} %copy-done, bf16[2048,4096]{1,0:T(8,128)(2,1)} %weight_ref.15, bf16[512,512]{1,0:T(8,128)(2,1)} %collective-permute-done.12.rest_0_, f32[16,512]{1,0:T(8,128)S(1)} %low_sums.1.rest_1_.rest_0_), custom_call_target="tpu_custom_call" | custom-call | flops 1000 | bytes 1000 | tf_op jit(solution)/shard_map/block_product/pallas_call | solution.py:42
  64.4 0.1 collective-permute-start.13
  64.4 3.3 %collective-permute-done.11.rest_3_ = f32[16,512]{1,0:T(8,128)S(1)} collective-permute-done((f32[16,512]{1,0:T(8,128)S(1)}, f32[16,512]{1,0:T(8,128)S(1)}, u32[]{:S(2)}, u32[]{:S(2)}) %collective-permute-start.11) | collective-permute-done | bytes 32800 | tf_op jit(solution)/shard_map/ppermute | solution.py:362
  67.7 0.6 collective-permute-done.10.rest_2_
  68.4 0.7 collective-permute-done.9.rest_1_
  69.1 0.0 copy-done.2
  69.1 0.0 copy-done.4
  69.1 0.0 copy-done.6
  69.1 0.0 copy-done.8
  69.1 1.3 %adapter_term.1 = (f32[512,512]{1,0:T(8,128)S(1)}, f32[512,512]{1,0:T(8,128)S(1)}) custom-call(s32[24]{0:T(128)S(1)} %get-tuple-element.17.rest_1_.start_ref, s32[24]{0:T(128)S(1)} %get-tuple-element.18.end_ref, f32[16,512]{1,0:T(8,128)S(1)} %low_sums.1.rest_1_.rest_0_, f32[16,512]{1,0:T(8,128)S(1)} %collective-permute-done.9.rest_1_, ...), custom_call_target="tpu_custom_call" | custom-call | flops 1000 | bytes 1000 | tf_op jit(solution)/shard_map/adapter_term/pallas_call | solution.py:272
  70.4 0.0 collective-permute-done.14.rest_0_
  70.4 3.2 %finish.2.rest_1_ = bf16[512,1024]{1,0:T(8,128)(2,1)} custom-call(f32[512,512]{1,0:T(8,128)S(1)} %get-tuple-element.24.term_ref, bf16[512,512]{1,0:T(8,128)(2,1)} %collective-permute-done.14.rest_0_), custom_call_target="tpu_custom_call" | custom-call | flops 20000000000 | bytes 1000 | tf_op jit(solution)/shard_map/finish/pallas_call | solution.py:299
  73.6 5.7 %collective-permute-done.13.rest_0_ = bf16[512,512]{1,0:T(8,128)(2,1)S(1)} collective-permute-done((bf16[512,512]{1,0:T(8,128)(2,1)S(1)}, bf16[512,512]{1,0:T(8,128)(2,1)S(1)}, u32[]{:S(2)}, u32[]{:S(2)}) %collective-permute-start.13) | collective-permute-done | bytes 524320 | tf_op jit(solution)/shard_map/ppermute | solution.py:329
  79.3 1.4 %finish.3 = bf16[512,1024]{1,0:T(8,128)(2,1)} custom-call(f32[512,512]{1,0:T(8,128)S(1)} %get-tuple-element.23.term_ref, bf16[512,512]{1,0:T(8,128)(2,1)S(1)} %collective-permute-done.13.rest_0_, bf16[512,1024]{1,0:T(8,128)(2,1)} %finish.2.rest_1_), custom_call_target="tpu_custom_call", output_to_operand_aliasing={{}: (2, {})} | custom-call | flops 1000 | bytes 1000 | tf_op jit(solution)/shard_map/finish/pallas_call | solution.py:299
  (3 shorter events, 0.0 us)
Async XLA Ops:
  0.0 6.7 %copy-start = (bf16[512,2048]{1,0:T(8,128)(2,1)S(1)}, bf16[512,2048]{1,0:T(8,128)(2,1)}, u32[]{:S(2)}) copy-start(bf16[512,2048]{1,0:T(8,128)(2,1)} %rows_ref.17) | copy-start | bytes 6291460
  0.0 6.7 %copy-start.10 = (s32[1,12]{1,0:T(1,128)S(1)}, s32[1,12]{1,0:T(1,128)}, u32[]{:S(2)}) copy-start(s32[1,12]{1,0:T(1,128)} %rest_0_.1) | copy-start | bytes 148
  3.6 19.1 %collective-permute-start.6 = (bf16[512,512]{1,0:T(8,128)(2,1)}, bf16[512,512]{1,0:T(8,128)(2,1)}, u32[]{:S(2)}, u32[]{:S(2)}) collective-permute-start(bf16[512,512]{1,0:T(8,128)(2,1)} %first_product.1.rest_1_), channel_id=1, source_target_pairs={{0,1},{1,2},{2,3},{3,0},{4,7},{5,4},{6,5},{7,6},{8,9},{9,10},{10,1... | collective-permute-start | bytes 1572872 | tf_op jit(solution)/shard_map/ppermute | solution.py:329
  10.2 21.9 %collective-permute-start.8 = (bf16[512,512]{1,0:T(8,128)(2,1)}, bf16[512,512]{1,0:T(8,128)(2,1)}, u32[]{:S(2)}, u32[]{:S(2)}) collective-permute-start(bf16[512,512]{1,0:T(8,128)(2,1)} %get-tuple-element.16.rest_0_), channel_id=1, source_target_pairs={{0,3},{1,0},{2,1},{3,2},{4,5},{5,6},{6,7},{7,4},{8,11},{9,8},{10,9... | collective-permute-start | bytes 1572872 | tf_op jit(solution)/shard_map/ppermute | solution.py:329
  12.3 4.7 %collective-permute-start.2 = (s32[1,12]{1,0:T(1,128)S(1)}, s32[1,12]{1,0:T(1,128)S(1)}, u32[]{:S(2)}, u32[]{:S(2)}) collective-permute-start(s32[1,12]{1,0:T(1,128)S(1)} %get-tuple-element.15.rest_0_), channel_id=1, source_target_pairs={{0,12},{4,8},{8,4},{12,0},{1,13},{5,9},{9,5},{13,1},{2,14},{6,10},... | collective-permute-start | bytes 152 | tf_op jit(solution)/shard_map/ppermute | solution.py:347
  12.9 4.1 %collective-permute-start.1 = (s32[1,12]{1,0:T(1,128)S(1)}, s32[1,12]{1,0:T(1,128)S(1)}, u32[]{:S(2)}, u32[]{:S(2)}) collective-permute-start(s32[1,12]{1,0:T(1,128)S(1)} %get-tuple-element.15.rest_0_), channel_id=1, source_target_pairs={{0,8},{4,12},{8,0},{12,4},{1,9},{5,13},{9,1},{13,5},{2,10},{6,14},... | collective-permute-start | bytes 152 | tf_op jit(solution)/shard_map/ppermute | solution.py:347
  14.0 3.0 %collective-permute-start = (s32[1,12]{1,0:T(1,128)S(1)}, s32[1,12]{1,0:T(1,128)S(1)}, u32[]{:S(2)}, u32[]{:S(2)}) collective-permute-start(s32[1,12]{1,0:T(1,128)S(1)} %get-tuple-element.15.rest_0_), channel_id=1, source_target_pairs={{0,4},{4,0},{8,12},{12,8},{1,5},{5,1},{9,13},{13,9},{2,6},{6,2},{1... | collective-permute-start | bytes 152 | tf_op jit(solution)/shard_map/ppermute | solution.py:347
  14.2 2.9 %copy-start.9 = (s32[512]{0:T(512)S(1)}, s32[512]{0:T(512)}, u32[]{:S(2)}) copy-start(s32[512]{0:T(512)} %table_ref.1) | copy-start | bytes 6148
  14.2 2.9 %copy-start.11 = (s32[1,12]{1,0:T(1,128)S(1)}, s32[1,12]{1,0:T(1,128)}, u32[]{:S(2)}) copy-start(s32[1,12]{1,0:T(1,128)} %lens_ref.1) | copy-start | bytes 148
  20.2 30.1 %collective-permute-start.3 = (bf16[6,16,3072]{2,1,0:T(8,128)(2,1)S(1)}, bf16[6,16,3072]{2,1,0:T(8,128)(2,1)S(1)}, u32[]{:S(2)}, u32[]{:S(2)}) collective-permute-start(bf16[6,16,3072]{2,1,0:T(8,128)(2,1)S(1)} %get-tuple-element.20), channel_id=1, source_target_pairs={{0,4},{4,0},{8,12},{12,8},{1,5},{5,1},{9,13},{13,9},{2,6},{6,2},{1... | collective-permute-start | bytes 1769480 | tf_op jit(solution)/shard_map/ppermute | solution.py:352
  20.9 29.4 %collective-permute-start.4 = (bf16[6,16,3072]{2,1,0:T(8,128)(2,1)S(1)}, bf16[6,16,3072]{2,1,0:T(8,128)(2,1)S(1)}, u32[]{:S(2)}, u32[]{:S(2)}) collective-permute-start(bf16[6,16,3072]{2,1,0:T(8,128)(2,1)S(1)} %get-tuple-element.21), channel_id=1, source_target_pairs={{0,8},{4,12},{8,0},{12,4},{1,9},{5,13},{9,1},{13,5},{2,10},{6,14},... | collective-permute-start | bytes 1769480 | tf_op jit(solution)/shard_map/ppermute | solution.py:352
  22.6 27.7 %collective-permute-start.5 = (bf16[6,16,3072]{2,1,0:T(8,128)(2,1)S(1)}, bf16[6,16,3072]{2,1,0:T(8,128)(2,1)S(1)}, u32[]{:S(2)}, u32[]{:S(2)}) collective-permute-start(bf16[6,16,3072]{2,1,0:T(8,128)(2,1)S(1)} %get-tuple-element.22), channel_id=1, source_target_pairs={{0,12},{4,8},{8,4},{12,0},{1,13},{5,9},{9,5},{13,1},{2,14},{6,10},... | collective-permute-start | bytes 1769480 | tf_op jit(solution)/shard_map/ppermute | solution.py:352
  25.5 19.1 %collective-permute-start.7 = (bf16[512,512]{1,0:T(8,128)(2,1)S(1)}, bf16[512,512]{1,0:T(8,128)(2,1)S(1)}, u32[]{:S(2)}, u32[]{:S(2)}) collective-permute-start(bf16[512,512]{1,0:T(8,128)(2,1)S(1)} %block_product.9.rest_1_), channel_id=1, source_target_pairs={{0,1},{1,2},{2,3},{3,0},{4,7},{5,4},{6,5},{7,6},{8,9},{9,10},{10,1... | collective-permute-start | bytes 1572872 | tf_op jit(solution)/shard_map/ppermute | solution.py:329
  35.6 25.8 %collective-permute-start.12 = (bf16[512,512]{1,0:T(8,128)(2,1)}, bf16[512,512]{1,0:T(8,128)(2,1)}, u32[]{:S(2)}, u32[]{:S(2)}) collective-permute-start(bf16[512,512]{1,0:T(8,128)(2,1)} %block_product.10.rest_0_), channel_id=1, source_target_pairs={{0,3},{1,0},{2,1},{3,2},{4,5},{5,6},{6,7},{7,4},{8,11},{9,8},{10,9... | collective-permute-start | bytes 1572872 | tf_op jit(solution)/shard_map/ppermute | solution.py:329
  41.9 6.0 %copy-start.7 = (bf16[512,512]{1,0:T(8,128)(2,1)}, bf16[512,512]{1,0:T(8,128)(2,1)S(1)}, u32[]{:S(2)}) copy-start(bf16[512,512]{1,0:T(8,128)(2,1)S(1)} %block_product.11.rest_1_.rest_5_) | copy-start | bytes 1572868
  48.0 22.4 %collective-permute-start.14 = (bf16[512,512]{1,0:T(8,128)(2,1)}, bf16[512,512]{1,0:T(8,128)(2,1)}, u32[]{:S(2)}, u32[]{:S(2)}) collective-permute-start(bf16[512,512]{1,0:T(8,128)(2,1)} %block_product.12.rest_4_), channel_id=1, source_target_pairs={{0,1},{1,2},{2,3},{3,0},{4,7},{5,4},{6,5},{7,6},{8,9},{9,10},{10,1... | collective-permute-start | bytes 1572872 | tf_op jit(solution)/shard_map/ppermute | solution.py:329
  50.3 1.6 %copy-start.3 = (bf16[6,16,3072]{2,1,0:T(8,128)(2,1)}, bf16[6,16,3072]{2,1,0:T(8,128)(2,1)S(1)}, u32[]{:S(2)}) copy-start(bf16[6,16,3072]{2,1,0:T(8,128)(2,1)S(1)} %collective-permute-done.4.rest_2_.rest_8_) | copy-start | bytes 1769476
  50.3 5.8 %copy-start.5 = (bf16[6,16,3072]{2,1,0:T(8,128)(2,1)}, bf16[6,16,3072]{2,1,0:T(8,128)(2,1)S(1)}, u32[]{:S(2)}) copy-start(bf16[6,16,3072]{2,1,0:T(8,128)(2,1)S(1)} %collective-permute-done.5.rest_3_.rest_9_) | copy-start | bytes 1769476
  51.9 0.8 %copy-start.1 = (bf16[6,16,3072]{2,1,0:T(8,128)(2,1)}, bf16[6,16,3072]{2,1,0:T(8,128)(2,1)S(1)}, u32[]{:S(2)}) copy-start(bf16[6,16,3072]{2,1,0:T(8,128)(2,1)S(1)} %collective-permute-done.3.rest_1_.rest_7_) | copy-start | bytes 1769476
  52.7 15.0 %collective-permute-start.11 = (f32[16,512]{1,0:T(8,128)S(1)}, f32[16,512]{1,0:T(8,128)S(1)}, u32[]{:S(2)}, u32[]{:S(2)}) collective-permute-start(f32[16,512]{1,0:T(8,128)S(1)} %low_sums.1.rest_1_.rest_0_), channel_id=1, source_target_pairs={{0,3},{1,2},{2,1},{3,0},{4,7},{5,6},{6,5},{7,4},{8,11},{9,10},{10,... | collective-permute-start | bytes 98312 | tf_op jit(solution)/shard_map/ppermute | solution.py:362
  56.1 12.2 %collective-permute-start.10 = (f32[16,512]{1,0:T(8,128)S(1)}, f32[16,512]{1,0:T(8,128)S(1)}, u32[]{:S(2)}, u32[]{:S(2)}) collective-permute-start(f32[16,512]{1,0:T(8,128)S(1)} %low_sums.1.rest_1_.rest_0_), channel_id=1, source_target_pairs={{0,2},{1,3},{2,0},{3,1},{4,6},{5,7},{6,4},{7,5},{8,10},{9,11},{10,... | collective-permute-start | bytes 98312 | tf_op jit(solution)/shard_map/ppermute | solution.py:362
  57.1 12.0 %collective-permute-start.9 = (f32[16,512]{1,0:T(8,128)S(1)}, f32[16,512]{1,0:T(8,128)S(1)}, u32[]{:S(2)}, u32[]{:S(2)}) collective-permute-start(f32[16,512]{1,0:T(8,128)S(1)} %low_sums.1.rest_1_.rest_0_), channel_id=1, source_target_pairs={{0,1},{1,0},{2,3},{3,2},{4,5},{5,4},{6,7},{7,6},{8,9},{9,8},{10,11... | collective-permute-start | bytes 98312 | tf_op jit(solution)/shard_map/ppermute | solution.py:362
  61.4 7.7 %copy-start.2 = (bf16[6,16,3072]{2,1,0:T(8,128)(2,1)S(1)}, bf16[6,16,3072]{2,1,0:T(8,128)(2,1)}, u32[]{:S(2)}) copy-start(bf16[6,16,3072]{2,1,0:T(8,128)(2,1)} %copy-done.1) | copy-start | bytes 1769476
  61.4 7.7 %copy-start.4 = (bf16[6,16,3072]{2,1,0:T(8,128)(2,1)S(1)}, bf16[6,16,3072]{2,1,0:T(8,128)(2,1)}, u32[]{:S(2)}) copy-start(bf16[6,16,3072]{2,1,0:T(8,128)(2,1)} %copy-done.3) | copy-start | bytes 1769476
  61.4 7.7 %copy-start.6 = (bf16[6,16,3072]{2,1,0:T(8,128)(2,1)S(1)}, bf16[6,16,3072]{2,1,0:T(8,128)(2,1)}, u32[]{:S(2)}) copy-start(bf16[6,16,3072]{2,1,0:T(8,128)(2,1)} %copy-done.5) | copy-start | bytes 1769476
  61.4 7.7 %copy-start.8 = (bf16[512,512]{1,0:T(8,128)(2,1)S(1)}, bf16[512,512]{1,0:T(8,128)(2,1)}, u32[]{:S(2)}) copy-start(bf16[512,512]{1,0:T(8,128)(2,1)} %copy-done.7) | copy-start | bytes 1572868
  64.4 15.0 %collective-permute-start.13 = (bf16[512,512]{1,0:T(8,128)(2,1)S(1)}, bf16[512,512]{1,0:T(8,128)(2,1)S(1)}, u32[]{:S(2)}, u32[]{:S(2)}) collective-permute-start(bf16[512,512]{1,0:T(8,128)(2,1)S(1)} %block_product.13.rest_10_), channel_id=1, source_target_pairs={{0,3},{1,0},{2,1},{3,2},{4,5},{5,6},{6,7},{7,4},{8,11},{9,8},{10,9... | collective-permute-start | bytes 1572872 | tf_op jit(solution)/shard_map/ppermute | solution.py:329

commit v14 on v13

--- a/solution.py
+++ b/solution.py
@@ -323,13 +323,13 @@
     def move(value, piece):
         pairs = []
         for r in range(req_total):
-            way = 1 if (r + piece) % 2 == 0 else tp_total - 1
+            way = 1 if (r + piece) % 2 == 1 else tp_total - 1
             for i in range(tp_total):
                 pairs.append((r * tp_total + i, r * tp_total + (i + way) % tp_total))
         return lax.ppermute(value, ("req", "tp"), pairs)
 
     def start_of(back, piece):
-        behind = jnp.where(lax.rem(me_req + piece, 2) == 0, tp_total - back, back)
+        behind = jnp.where(lax.rem(me_req + piece, 2) == 1, tp_total - back, back)
         block = lax.rem(me + behind, tp_total)
         return block * cols + piece * width
 

time: 81.1 us -> 85.9 us (1.059)
  waiting for transfers between devices: 17.2 us -> 30.4 us
  starting transfers between devices: 26.7 us -> 17.2 us
    ppermute x6, starting transfers between devices: 17.9 us -> 9.02 us  [move(): return lax.ppermute(value, ('req', 'tp'), pairs)]
    ppermute x3, waiting for transfers between devices: 4.65 us -> 12.1 us  [local(): lows.append(lax.ppermute(low, 'tp', pairs))]
    ppermute x6, waiting for transfers between devices: 12.5 us -> 18.2 us  [move(): return lax.ppermute(value, ('req', 'tp'), pairs)]
  transfers between devices with their start and end apart: 15 -> 15, of which waited for: 6 -> 5; matrix products, arithmetic and copies ran while one was open for 0% -> 0% of each run, Pallas kernels for 38% -> 37%
where the time goes in v14:
time: 85.9 us; the launch traced here: 84.9 us
  Pallas kernels  36.2 us (42%)
  waiting for transfers between devices  30.4 us (35%)
  starting transfers between devices  17.2 us (20%)
    pallas_call x7, Pallas kernels, block_product(): pl.pallas_call(functools.partial(product_kernel, len(addends), with_ids),...  21.5 us
    ppermute x6, waiting for transfers between devices, move(): return lax.ppermute(value, ('req', 'tp'), pairs)  18.2 us
    ppermute x3, waiting for transfers between devices, local(): lows.append(lax.ppermute(low, 'tp', pairs))  12.1 us
    ppermute x6, starting transfers between devices, move(): return lax.ppermute(value, ('req', 'tp'), pairs)  9.02 us
    pallas_call x2, Pallas kernels, finish(): pl.pallas_call(functools.partial(finish_kernel, len(arrivals)), grid=(row...  4.6 us
    ppermute x3, starting transfers between devices, local(): lows.append(lax.ppermute(low, 'tp', pairs))  4.39 us
    pallas_call x1, Pallas kernels, pick_adapters(): pl.pallas_call(functools.partial(pick_kernel, peers, len(after)), in_spec...  3.63 us
    pallas_call x1, Pallas kernels, first_product(): pl.pallas_call(functools.partial(first_kernel, chunk), in_specs=[pl.Block...  3.62 us
  transfers between devices with their start and end apart: 15, of which 5 were waited for; matrix products, arithmetic and copies ran while one was open for 0% of the time, Pallas kernels for 37%

profile of v14, /device:TPU:0, one launch (start us, length us, event | category | flops | bytes accessed | tf_op | source)
XLA Modules:
  0.0 84.9 jit_solution(9702915451011480877)
XLA Ops:
  0.0 0.0 copy-start
  0.0 0.0 copy-start.10
  0.0 3.6 %first_product.1.rest_1_ = bf16[512,512]{1,0:T(8,128)(2,1)} custom-call(s32[1]{0:T(128)} %bitcast.2.first_ref, bf16[512,2048]{1,0:T(8,128)(2,1)} %rows_ref.17, bf16[2048,4096]{1,0:T(8,128)(2,1)} %weight_ref.15), custom_call_target="tpu_custom_call" | custom-call | flops 1000 | bytes 1000 | tf_op jit(solution)/shard_map/first_product/pallas_call | solution.py:95
  3.6 5.1 %collective-permute-start.6 = (bf16[512,512]{1,0:T(8,128)(2,1)}, bf16[512,512]{1,0:T(8,128)(2,1)}, u32[]{:S(2)}, u32[]{:S(2)}) collective-permute-start(bf16[512,512]{1,0:T(8,128)(2,1)} %first_product.1.rest_1_), channel_id=1, source_target_pairs={{0,3},{1,0},{2,1},{3,2},{4,5},{5,6},{6,7},{7,4},{8,11},{9,8},{10,9... | collective-permute-start | bytes 1572872 | tf_op jit(solution)/shard_map/ppermute | solution.py:329
  8.7 0.0 copy-done
  8.7 0.0 copy-done.10
  8.7 3.5 %block_product.7 = (bf16[512,512]{1,0:T(8,128)(2,1)}, s32[1,12]{1,0:T(1,128)S(1)}) custom-call(s32[1]{0:T(128)} %bitcast.1.first_ref, bf16[512,2048]{1,0:T(8,128)(2,1)S(1)} %copy-done, bf16[2048,4096]{1,0:T(8,128)(2,1)} %weight_ref.15, s32[1,12]{1,0:T(1,128)S(1)} %copy-done.10, bf16[512,512]{1,0:T(8,128)(2,1)} %first_product.1.rest_1_), custom_call_target="tpu_custom_call" | custom-call | flops 1000 | bytes 1000 | tf_op jit(solution)/shard_map/block_product/pallas_call | solution.py:42
  12.2 0.0 collective-permute-start.8
  12.2 0.7 collective-permute-start.2
  13.0 0.8 collective-permute-start.1
  13.8 0.3 collective-permute-start
  14.1 0.0 copy-start.9
  14.1 0.0 copy-start.11
  14.1 2.7 %block_product.8.rest_6_.rest_4_ = bf16[512,512]{1,0:T(8,128)(2,1)S(1)} custom-call(s32[1]{0:T(128)} %bitcast.3.first_ref, bf16[512,2048]{1,0:T(8,128)(2,1)S(1)} %copy-done, bf16[2048,4096]{1,0:T(8,128)(2,1)} %weight_ref.15, bf16[512,512]{1,0:T(8,128)(2,1)} %get-tuple-element.16.rest_0_), custom_call_target="tpu_custom_call" | custom-call | flops 1000 | bytes 1000 | tf_op jit(solution)/shard_map/block_product/pallas_call | solution.py:42
  16.9 0.0 collective-permute-done.2.rest_3_
  16.9 0.0 collective-permute-done.1.rest_2_
  16.9 0.0 collective-permute-done.rest_1_
  16.9 0.0 copy-done.9
  17.0 0.0 copy-done.11
  17.0 3.6 %pick_adapters.1 = (bf16[6,16,3072]{2,1,0:T(8,128)(2,1)S(1)}, bf16[6,16,3072]{2,1,0:T(8,128)(2,1)S(1)}, bf16[6,16,3072]{2,1,0:T(8,128)(2,1)S(1)}, bf16[6,16,3072...) custom-call(s32[1]{0:T(128)} %bitcast.me_ref, s32[512]{0:T(512)S(1)} %copy-done.9, s32[1,12]{1,0:T(1,128)S(1)} %copy-done.11, ...), custom_call_target="tpu_custom_call" | custom-call | flops 1000 | bytes 1000 | tf_op jit(solution)/shard_map/pick_adapters/pallas_call | solution.py:184
  20.6 0.4 collective-permute-start.3
  21.0 1.3 %collective-permute-start.4 = (bf16[6,16,3072]{2,1,0:T(8,128)(2,1)S(1)}, bf16[6,16,3072]{2,1,0:T(8,128)(2,1)S(1)}, u32[]{:S(2)}, u32[]{:S(2)}) collective-permute-start(bf16[6,16,3072]{2,1,0:T(8,128)(2,1)S(1)} %get-tuple-element.21), channel_id=1, source_target_pairs={{0,8},{4,12},{8,0},{12,4},{1,9},{5,13},{9,1},{13,5},{2,10},{6,14},... | collective-permute-start | bytes 1769480 | tf_op jit(solution)/shard_map/ppermute | solution.py:352
  22.3 0.3 collective-permute-start.5
  22.5 1.9 %collective-permute-done.6.rest_0_ = bf16[512,512]{1,0:T(8,128)(2,1)} collective-permute-done((bf16[512,512]{1,0:T(8,128)(2,1)}, bf16[512,512]{1,0:T(8,128)(2,1)}, u32[]{:S(2)}, u32[]{:S(2)}) %collective-permute-start.6) | collective-permute-done | bytes 524320 | tf_op jit(solution)/shard_map/ppermute | solution.py:329
  24.5 2.8 %block_product.9.rest_1_ = bf16[512,512]{1,0:T(8,128)(2,1)S(1)} custom-call(s32[1]{0:T(128)} %bitcast.5.first_ref, bf16[512,2048]{1,0:T(8,128)(2,1)S(1)} %copy-done, bf16[2048,4096]{1,0:T(8,128)(2,1)} %weight_ref.15, bf16[512,512]{1,0:T(8,128)(2,1)} %collective-permute-done.6.rest_0_, s32[24]{0:T(128)S(1)} %get-tuple-element.17.rest_1_.start_ref), custom_call_target="tpu_custom_call" | custom-call | flops 1000 | bytes 1000 | tf_op jit(solution)/shard_map/block_product/pallas_call | solution.py:42
  27.2 1.9 %collective-permute-start.7 = (bf16[512,512]{1,0:T(8,128)(2,1)S(1)}, bf16[512,512]{1,0:T(8,128)(2,1)S(1)}, u32[]{:S(2)}, u32[]{:S(2)}) collective-permute-start(bf16[512,512]{1,0:T(8,128)(2,1)S(1)} %block_product.9.rest_1_), channel_id=1, source_target_pairs={{0,3},{1,0},{2,1},{3,2},{4,5},{5,6},{6,7},{7,4},{8,11},{9,8},{10,9... | collective-permute-start | bytes 1572872 | tf_op jit(solution)/shard_map/ppermute | solution.py:329
  29.2 3.0 %collective-permute-done.8.rest_0_ = bf16[512,512]{1,0:T(8,128)(2,1)} collective-permute-done((bf16[512,512]{1,0:T(8,128)(2,1)}, bf16[512,512]{1,0:T(8,128)(2,1)}, u32[]{:S(2)}, u32[]{:S(2)}) %collective-permute-start.8) | collective-permute-done | bytes 524320 | tf_op jit(solution)/shard_map/ppermute | solution.py:329
  32.2 3.5 %block_product.10.rest_0_ = bf16[512,512]{1,0:T(8,128)(2,1)} custom-call(s32[1]{0:T(128)} %bitcast.7.first_ref, bf16[512,2048]{1,0:T(8,128)(2,1)S(1)} %copy-done, bf16[2048,4096]{1,0:T(8,128)(2,1)} %weight_ref.15, bf16[512,512]{1,0:T(8,128)(2,1)} %collective-permute-done.8.rest_0_, bf16[512,512]{1,0:T(8,128)(2,1)S(1)} %block_product.9.rest_1_), custom_call_target="tpu_custom_call" | custom-call | flops 1000 | bytes 1000 | tf_op jit(solution)/shard_map/block_product/pallas_call | solution.py:42
  35.7 0.5 collective-permute-start.12
  36.2 2.7 %block_product.11.rest_1_.rest_5_ = bf16[512,512]{1,0:T(8,128)(2,1)S(1)} custom-call(s32[1]{0:T(128)} %bitcast.6.first_ref, bf16[512,2048]{1,0:T(8,128)(2,1)S(1)} %copy-done, bf16[2048,4096]{1,0:T(8,128)(2,1)} %weight_ref.15, bf16[512,512]{1,0:T(8,128)(2,1)} %block_product.10.rest_0_), custom_call_target="tpu_custom_call" | custom-call | flops 20000000000 | bytes 1000 | tf_op jit(solution)/shard_map/block_product/pallas_call | solution.py:42
  38.9 0.0 copy-start.7
  38.9 13.3 %collective-permute-done.7.rest_0_ = bf16[512,512]{1,0:T(8,128)(2,1)S(1)} collective-permute-done((bf16[512,512]{1,0:T(8,128)(2,1)S(1)}, bf16[512,512]{1,0:T(8,128)(2,1)S(1)}, u32[]{:S(2)}, u32[]{:S(2)}) %collective-permute-start.7) | collective-permute-done | bytes 524320 | tf_op jit(solution)/shard_map/ppermute | solution.py:329
  52.2 3.4 %block_product.12.rest_4_ = bf16[512,512]{1,0:T(8,128)(2,1)} custom-call(s32[1]{0:T(128)} %bitcast.4.first_ref, bf16[512,2048]{1,0:T(8,128)(2,1)S(1)} %copy-done, bf16[2048,4096]{1,0:T(8,128)(2,1)} %weight_ref.15, bf16[512,512]{1,0:T(8,128)(2,1)S(1)} %collective-permute-done.7.rest_0_, bf16[512,512]{1,0:T(8,128)(2,1)S(1)} %block_product.11.rest_1_.rest_5_), custom_call_target="tpu_custom_call" | custom-call | flops 1000 | bytes 1000 | tf_op jit(solution)/shard_map/block_product/pallas_call | solution.py:42
  55.6 0.0 copy-done.7
  55.6 0.0 collective-permute-start.14
  55.6 0.0 collective-permute-done.3.rest_1_.rest_7_
  55.6 0.0 collective-permute-done.4.rest_2_.rest_8_
  55.6 0.0 copy-start.3
  55.6 0.0 collective-permute-done.5.rest_3_.rest_9_
  55.7 0.0 copy-start.5
  55.7 1.6 %low_sums.1.rest_1_.rest_0_ = f32[16,512]{1,0:T(8,128)S(1)} custom-call(s32[24]{0:T(128)S(1)} %get-tuple-element.17.rest_1_.start_ref, s32[24]{0:T(128)S(1)} %get-tuple-element.18.end_ref, bf16[512,2048]{1,0:T(8,128)(2,1)S(1)} %copy-done, bf16[6,16,3072]{2,1,0:T(8,128)(2,1)S(1)} %get-tuple-element.19.rest_0_.rest_6_, ...), custom_call_target="tpu_custom_call" | custom-call | flops 1000 | bytes 1000 | tf_op jit(solution)/shard_map/low_sums/pallas_call | solution.py:226
  57.2 0.0 copy-done.3
  57.2 0.0 copy-start.1
  57.2 0.8 copy-done.1
  58.1 2.2 %collective-permute-start.11 = (f32[16,512]{1,0:T(8,128)S(1)}, f32[16,512]{1,0:T(8,128)S(1)}, u32[]{:S(2)}, u32[]{:S(2)}) collective-permute-start(f32[16,512]{1,0:T(8,128)S(1)} %low_sums.1.rest_1_.rest_0_), channel_id=1, source_target_pairs={{0,3},{1,2},{2,1},{3,0},{4,7},{5,6},{6,5},{7,4},{8,11},{9,10},{10,... | collective-permute-start | bytes 98312 | tf_op jit(solution)/shard_map/ppermute | solution.py:362
  60.3 0.0 copy-done.5
  60.3 1.5 %collective-permute-start.10 = (f32[16,512]{1,0:T(8,128)S(1)}, f32[16,512]{1,0:T(8,128)S(1)}, u32[]{:S(2)}, u32[]{:S(2)}) collective-permute-start(f32[16,512]{1,0:T(8,128)S(1)} %low_sums.1.rest_1_.rest_0_), channel_id=1, source_target_pairs={{0,2},{1,3},{2,0},{3,1},{4,6},{5,7},{6,4},{7,5},{8,10},{9,11},{10,... | collective-permute-start | bytes 98312 | tf_op jit(solution)/shard_map/ppermute | solution.py:362
  61.8 0.6 collective-permute-start.9
  62.4 0.0 collective-permute-done.12.rest_0_
  62.5 0.0 copy-start.8
  62.5 2.9 %block_product.13.rest_10_ = bf16[512,512]{1,0:T(8,128)(2,1)S(1)} custom-call(s32[1]{0:T(128)} %bitcast.8.first_ref, bf16[512,2048]{1,0:T(8,128)(2,1)S(1)} %copy-done, bf16[2048,4096]{1,0:T(8,128)(2,1)} %weight_ref.15, bf16[512,512]{1,0:T(8,128)(2,1)} %collective-permute-done.12.rest_0_, f32[16,512]{1,0:T(8,128)S(1)} %low_sums.1.rest_1_.rest_0_), custom_call_target="tpu_custom_call" | custom-call | flops 1000 | bytes 1000 | tf_op jit(solution)/shard_map/block_product/pallas_call | solution.py:42
  65.4 1.5 %collective-permute-start.13 = (bf16[512,512]{1,0:T(8,128)(2,1)S(1)}, bf16[512,512]{1,0:T(8,128)(2,1)S(1)}, u32[]{:S(2)}, u32[]{:S(2)}) collective-permute-start(bf16[512,512]{1,0:T(8,128)(2,1)S(1)} %block_product.13.rest_10_), channel_id=1, source_target_pairs={{0,1},{1,2},{2,3},{3,0},{4,7},{5,4},{6,5},{7,6},{8,9},{9,10},{10,1... | collective-permute-start | bytes 1572872 | tf_op jit(solution)/shard_map/ppermute | solution.py:329
  66.9 4.8 %collective-permute-done.11.rest_3_ = f32[16,512]{1,0:T(8,128)S(1)} collective-permute-done((f32[16,512]{1,0:T(8,128)S(1)}, f32[16,512]{1,0:T(8,128)S(1)}, u32[]{:S(2)}, u32[]{:S(2)}) %collective-permute-start.11) | collective-permute-done | bytes 32800 | tf_op jit(solution)/shard_map/ppermute | solution.py:362
  71.6 7.3 %collective-permute-done.10.rest_2_ = f32[16,512]{1,0:T(8,128)S(1)} collective-permute-done((f32[16,512]{1,0:T(8,128)S(1)}, f32[16,512]{1,0:T(8,128)S(1)}, u32[]{:S(2)}, u32[]{:S(2)}) %collective-permute-start.10) | collective-permute-done | bytes 32800 | tf_op jit(solution)/shard_map/ppermute | solution.py:362
  79.0 0.0 collective-permute-done.9.rest_1_
  79.0 0.0 copy-done.2
  79.0 0.0 copy-done.4
  79.0 0.0 copy-done.6
  79.0 0.0 copy-done.8
  79.0 1.3 %adapter_term.1 = (f32[512,512]{1,0:T(8,128)S(1)}, f32[512,512]{1,0:T(8,128)S(1)}) custom-call(s32[24]{0:T(128)S(1)} %get-tuple-element.17.rest_1_.start_ref, s32[24]{0:T(128)S(1)} %get-tuple-element.18.end_ref, f32[16,512]{1,0:T(8,128)S(1)} %low_sums.1.rest_1_.rest_0_, f32[16,512]{1,0:T(8,128)S(1)} %collective-permute-done.9.rest_1_, ...), custom_call_target="tpu_custom_call" | custom-call | flops 1000 | bytes 1000 | tf_op jit(solution)/shard_map/adapter_term/pallas_call | solution.py:272
  80.3 0.0 collective-permute-done.14.rest_0_
  80.3 3.2 %finish.2.rest_1_ = bf16[512,1024]{1,0:T(8,128)(2,1)} custom-call(f32[512,512]{1,0:T(8,128)S(1)} %get-tuple-element.24.term_ref, bf16[512,512]{1,0:T(8,128)(2,1)} %collective-permute-done.14.rest_0_), custom_call_target="tpu_custom_call" | custom-call | flops 20000000000 | bytes 1000 | tf_op jit(solution)/shard_map/finish/pallas_call | solution.py:299
  83.5 0.0 collective-permute-done.13.rest_0_
  83.5 1.4 %finish.3 = bf16[512,1024]{1,0:T(8,128)(2,1)} custom-call(f32[512,512]{1,0:T(8,128)S(1)} %get-tuple-element.23.term_ref, bf16[512,512]{1,0:T(8,128)(2,1)S(1)} %collective-permute-done.13.rest_0_, bf16[512,1024]{1,0:T(8,128)(2,1)} %finish.2.rest_1_), custom_call_target="tpu_custom_call", output_to_operand_aliasing={{}: (2, {})} | custom-call | flops 1000 | bytes 1000 | tf_op jit(solution)/shard_map/finish/pallas_call | solution.py:299
  (3 shorter events, 0.0 us)
Async XLA Ops:
  0.0 8.7 %copy-start = (bf16[512,2048]{1,0:T(8,128)(2,1)S(1)}, bf16[512,2048]{1,0:T(8,128)(2,1)}, u32[]{:S(2)}) copy-start(bf16[512,2048]{1,0:T(8,128)(2,1)} %rows_ref.17) | copy-start | bytes 6291460
  0.0 8.7 %copy-start.10 = (s32[1,12]{1,0:T(1,128)S(1)}, s32[1,12]{1,0:T(1,128)}, u32[]{:S(2)}) copy-start(s32[1,12]{1,0:T(1,128)} %rest_0_.1) | copy-start | bytes 148
  3.6 20.8 %collective-permute-start.6 = (bf16[512,512]{1,0:T(8,128)(2,1)}, bf16[512,512]{1,0:T(8,128)(2,1)}, u32[]{:S(2)}, u32[]{:S(2)}) collective-permute-start(bf16[512,512]{1,0:T(8,128)(2,1)} %first_product.1.rest_1_), channel_id=1, source_target_pairs={{0,3},{1,0},{2,1},{3,2},{4,5},{5,6},{6,7},{7,4},{8,11},{9,8},{10,9... | collective-permute-start | bytes 1572872 | tf_op jit(solution)/shard_map/ppermute | solution.py:329
  12.2 20.0 %collective-permute-start.8 = (bf16[512,512]{1,0:T(8,128)(2,1)}, bf16[512,512]{1,0:T(8,128)(2,1)}, u32[]{:S(2)}, u32[]{:S(2)}) collective-permute-start(bf16[512,512]{1,0:T(8,128)(2,1)} %get-tuple-element.16.rest_0_), channel_id=1, source_target_pairs={{0,1},{1,2},{2,3},{3,0},{4,7},{5,4},{6,5},{7,6},{8,9},{9,10},{10,1... | collective-permute-start | bytes 1572872 | tf_op jit(solution)/shard_map/ppermute | solution.py:329
  12.2 4.7 %collective-permute-start.2 = (s32[1,12]{1,0:T(1,128)S(1)}, s32[1,12]{1,0:T(1,128)S(1)}, u32[]{:S(2)}, u32[]{:S(2)}) collective-permute-start(s32[1,12]{1,0:T(1,128)S(1)} %get-tuple-element.15.rest_0_), channel_id=1, source_target_pairs={{0,12},{4,8},{8,4},{12,0},{1,13},{5,9},{9,5},{13,1},{2,14},{6,10},... | collective-permute-start | bytes 152 | tf_op jit(solution)/shard_map/ppermute | solution.py:347
  13.0 4.0 %collective-permute-start.1 = (s32[1,12]{1,0:T(1,128)S(1)}, s32[1,12]{1,0:T(1,128)S(1)}, u32[]{:S(2)}, u32[]{:S(2)}) collective-permute-start(s32[1,12]{1,0:T(1,128)S(1)} %get-tuple-element.15.rest_0_), channel_id=1, source_target_pairs={{0,8},{4,12},{8,0},{12,4},{1,9},{5,13},{9,1},{13,5},{2,10},{6,14},... | collective-permute-start | bytes 152 | tf_op jit(solution)/shard_map/ppermute | solution.py:347
  13.8 3.1 %collective-permute-start = (s32[1,12]{1,0:T(1,128)S(1)}, s32[1,12]{1,0:T(1,128)S(1)}, u32[]{:S(2)}, u32[]{:S(2)}) collective-permute-start(s32[1,12]{1,0:T(1,128)S(1)} %get-tuple-element.15.rest_0_), channel_id=1, source_target_pairs={{0,4},{4,0},{8,12},{12,8},{1,5},{5,1},{9,13},{13,9},{2,6},{6,2},{1... | collective-permute-start | bytes 152 | tf_op jit(solution)/shard_map/ppermute | solution.py:347
  14.1 2.9 %copy-start.9 = (s32[512]{0:T(512)S(1)}, s32[512]{0:T(512)}, u32[]{:S(2)}) copy-start(s32[512]{0:T(512)} %table_ref.1) | copy-start | bytes 6148
  14.1 2.9 %copy-start.11 = (s32[1,12]{1,0:T(1,128)S(1)}, s32[1,12]{1,0:T(1,128)}, u32[]{:S(2)}) copy-start(s32[1,12]{1,0:T(1,128)} %lens_ref.1) | copy-start | bytes 148
  20.6 35.0 %collective-permute-start.3 = (bf16[6,16,3072]{2,1,0:T(8,128)(2,1)S(1)}, bf16[6,16,3072]{2,1,0:T(8,128)(2,1)S(1)}, u32[]{:S(2)}, u32[]{:S(2)}) collective-permute-start(bf16[6,16,3072]{2,1,0:T(8,128)(2,1)S(1)} %get-tuple-element.20), channel_id=1, source_target_pairs={{0,4},{4,0},{8,12},{12,8},{1,5},{5,1},{9,13},{13,9},{2,6},{6,2},{1... | collective-permute-start | bytes 1769480 | tf_op jit(solution)/shard_map/ppermute | solution.py:352
  21.0 34.7 %collective-permute-start.4 = (bf16[6,16,3072]{2,1,0:T(8,128)(2,1)S(1)}, bf16[6,16,3072]{2,1,0:T(8,128)(2,1)S(1)}, u32[]{:S(2)}, u32[]{:S(2)}) collective-permute-start(bf16[6,16,3072]{2,1,0:T(8,128)(2,1)S(1)} %get-tuple-element.21), channel_id=1, source_target_pairs={{0,8},{4,12},{8,0},{12,4},{1,9},{5,13},{9,1},{13,5},{2,10},{6,14},... | collective-permute-start | bytes 1769480 | tf_op jit(solution)/shard_map/ppermute | solution.py:352
  22.3 33.4 %collective-permute-start.5 = (bf16[6,16,3072]{2,1,0:T(8,128)(2,1)S(1)}, bf16[6,16,3072]{2,1,0:T(8,128)(2,1)S(1)}, u32[]{:S(2)}, u32[]{:S(2)}) collective-permute-start(bf16[6,16,3072]{2,1,0:T(8,128)(2,1)S(1)} %get-tuple-element.22), channel_id=1, source_target_pairs={{0,12},{4,8},{8,4},{12,0},{1,13},{5,9},{9,5},{13,1},{2,14},{6,10},... | collective-permute-start | bytes 1769480 | tf_op jit(solution)/shard_map/ppermute | solution.py:352
  27.2 25.0 %collective-permute-start.7 = (bf16[512,512]{1,0:T(8,128)(2,1)S(1)}, bf16[512,512]{1,0:T(8,128)(2,1)S(1)}, u32[]{:S(2)}, u32[]{:S(2)}) collective-permute-start(bf16[512,512]{1,0:T(8,128)(2,1)S(1)} %block_product.9.rest_1_), channel_id=1, source_target_pairs={{0,3},{1,0},{2,1},{3,2},{4,5},{5,6},{6,7},{7,4},{8,11},{9,8},{10,9... | collective-permute-start | bytes 1572872 | tf_op jit(solution)/shard_map/ppermute | solution.py:329
  35.7 26.7 %collective-permute-start.12 = (bf16[512,512]{1,0:T(8,128)(2,1)}, bf16[512,512]{1,0:T(8,128)(2,1)}, u32[]{:S(2)}, u32[]{:S(2)}) collective-permute-start(bf16[512,512]{1,0:T(8,128)(2,1)} %block_product.10.rest_0_), channel_id=1, source_target_pairs={{0,1},{1,2},{2,3},{3,0},{4,7},{5,4},{6,5},{7,6},{8,9},{9,10},{10,1... | collective-permute-start | bytes 1572872 | tf_op jit(solution)/shard_map/ppermute | solution.py:329
  38.9 16.7 %copy-start.7 = (bf16[512,512]{1,0:T(8,128)(2,1)}, bf16[512,512]{1,0:T(8,128)(2,1)S(1)}, u32[]{:S(2)}) copy-start(bf16[512,512]{1,0:T(8,128)(2,1)S(1)} %block_product.11.rest_1_.rest_5_) | copy-start | bytes 1572868
  55.6 24.7 %collective-permute-start.14 = (bf16[512,512]{1,0:T(8,128)(2,1)}, bf16[512,512]{1,0:T(8,128)(2,1)}, u32[]{:S(2)}, u32[]{:S(2)}) collective-permute-start(bf16[512,512]{1,0:T(8,128)(2,1)} %block_product.12.rest_4_), channel_id=1, source_target_pairs={{0,3},{1,0},{2,1},{3,2},{4,5},{5,6},{6,7},{7,4},{8,11},{9,8},{10,9... | collective-permute-start | bytes 1572872 | tf_op jit(solution)/shard_map/ppermute | solution.py:329
  55.6 1.6 %copy-start.3 = (bf16[6,16,3072]{2,1,0:T(8,128)(2,1)}, bf16[6,16,3072]{2,1,0:T(8,128)(2,1)S(1)}, u32[]{:S(2)}) copy-start(bf16[6,16,3072]{2,1,0:T(8,128)(2,1)S(1)} %collective-permute-done.4.rest_2_.rest_8_) | copy-start | bytes 1769476
  55.7 4.6 %copy-start.5 = (bf16[6,16,3072]{2,1,0:T(8,128)(2,1)}, bf16[6,16,3072]{2,1,0:T(8,128)(2,1)S(1)}, u32[]{:S(2)}) copy-start(bf16[6,16,3072]{2,1,0:T(8,128)(2,1)S(1)} %collective-permute-done.5.rest_3_.rest_9_) | copy-start | bytes 1769476
  57.2 0.8 copy-start.1
  58.1 13.6 %collective-permute-start.11 = (f32[16,512]{1,0:T(8,128)S(1)}, f32[16,512]{1,0:T(8,128)S(1)}, u32[]{:S(2)}, u32[]{:S(2)}) collective-permute-start(f32[16,512]{1,0:T(8,128)S(1)} %low_sums.1.rest_1_.rest_0_), channel_id=1, source_target_pairs={{0,3},{1,2},{2,1},{3,0},{4,7},{5,6},{6,5},{7,4},{8,11},{9,10},{10,... | collective-permute-start | bytes 98312 | tf_op jit(solution)/shard_map/ppermute | solution.py:362
  60.3 18.7 %collective-permute-start.10 = (f32[16,512]{1,0:T(8,128)S(1)}, f32[16,512]{1,0:T(8,128)S(1)}, u32[]{:S(2)}, u32[]{:S(2)}) collective-permute-start(f32[16,512]{1,0:T(8,128)S(1)} %low_sums.1.rest_1_.rest_0_), channel_id=1, source_target_pairs={{0,2},{1,3},{2,0},{3,1},{4,6},{5,7},{6,4},{7,5},{8,10},{9,11},{10,... | collective-permute-start | bytes 98312 | tf_op jit(solution)/shard_map/ppermute | solution.py:362
  61.8 17.1 %collective-permute-start.9 = (f32[16,512]{1,0:T(8,128)S(1)}, f32[16,512]{1,0:T(8,128)S(1)}, u32[]{:S(2)}, u32[]{:S(2)}) collective-permute-start(f32[16,512]{1,0:T(8,128)S(1)} %low_sums.1.rest_1_.rest_0_), channel_id=1, source_target_pairs={{0,1},{1,0},{2,3},{3,2},{4,5},{5,4},{6,7},{7,6},{8,9},{9,8},{10,11... | collective-permute-start | bytes 98312 | tf_op jit(solution)/shard_map/ppermute | solution.py:362
  62.4 16.5 %copy-start.2 = (bf16[6,16,3072]{2,1,0:T(8,128)(2,1)S(1)}, bf16[6,16,3072]{2,1,0:T(8,128)(2,1)}, u32[]{:S(2)}) copy-start(bf16[6,16,3072]{2,1,0:T(8,128)(2,1)} %copy-done.1) | copy-start | bytes 1769476
  62.5 16.5 %copy-start.4 = (bf16[6,16,3072]{2,1,0:T(8,128)(2,1)S(1)}, bf16[6,16,3072]{2,1,0:T(8,128)(2,1)}, u32[]{:S(2)}) copy-start(bf16[6,16,3072]{2,1,0:T(8,128)(2,1)} %copy-done.3) | copy-start | bytes 1769476
  62.5 16.5 %copy-start.6 = (bf16[6,16,3072]{2,1,0:T(8,128)(2,1)S(1)}, bf16[6,16,3072]{2,1,0:T(8,128)(2,1)}, u32[]{:S(2)}) copy-start(bf16[6,16,3072]{2,1,0:T(8,128)(2,1)} %copy-done.5) | copy-start | bytes 1769476
  62.5 16.5 %copy-start.8 = (bf16[512,512]{1,0:T(8,128)(2,1)S(1)}, bf16[512,512]{1,0:T(8,128)(2,1)}, u32[]{:S(2)}) copy-start(bf16[512,512]{1,0:T(8,128)(2,1)} %copy-done.7) | copy-start | bytes 1572868
  65.4 18.1 %collective-permute-start.13 = (bf16[512,512]{1,0:T(8,128)(2,1)S(1)}, bf16[512,512]{1,0:T(8,128)(2,1)S(1)}, u32[]{:S(2)}, u32[]{:S(2)}) collective-permute-start(bf16[512,512]{1,0:T(8,128)(2,1)S(1)} %block_product.13.rest_10_), channel_id=1, source_target_pairs={{0,1},{1,2},{2,3},{3,0},{4,7},{5,4},{6,5},{7,6},{8,9},{9,10},{10,1... | collective-permute-start | bytes 1572872 | tf_op jit(solution)/shard_map/ppermute | solution.py:329

commit v15 on v13

--- a/solution.py
+++ b/solution.py
@@ -16,19 +16,17 @@
 LARGE = pl.CostEstimate(flops=2 * 10**10, bytes_accessed=1000, transcendentals=0)
 
 
-def product_kernel(addends, with_ids, first_ref, rows_ref, weight_ref, *rest):
+def product_kernel(with_ids, first_ref, rows_ref, weight_ref, *rest):
     out_ref = rest[-1 - with_ids]
     total = jnp.dot(rows_ref[...], weight_ref[...], preferred_element_type=F32)
-    for ref in rest[:addends]:
-        total = total + ref[...].astype(F32)
     out_ref[...] = total.astype(out_ref.dtype)
     if with_ids:
-        ids_ref, ids_out_ref = rest[addends], rest[-1]
+        ids_ref, ids_out_ref = rest[0], rest[-1]
         for s in range(ids_ref.shape[1]):
             ids_out_ref[0, s] = ids_ref[0, s]
 
 
-def block_product(rows, weight, first, width, addends=(), after=(), ids=None, cost=SMALL):
+def block_product(rows, weight, first, width, after=(), ids=None, cost=SMALL):
     row_total, depth = rows.shape
     tile = min(256, width)
     with_ids = ids is not None
@@ -40,7 +38,7 @@
         out_specs.append(smem)
         out_shape.append(jax.ShapeDtypeStruct(ids.shape, ids.dtype))
     out = pl.pallas_call(
-        functools.partial(product_kernel, len(addends), with_ids),
+        functools.partial(product_kernel, with_ids),
         grid_spec=pltpu.PrefetchScalarGridSpec(
             num_scalar_prefetch=1,
             grid=(width // tile,),
@@ -48,7 +46,6 @@
                 pl.BlockSpec((row_total, depth), lambda j, t: (0, 0)),
                 pl.BlockSpec((depth, tile), lambda j, t: (0, t[0] + j)),
             ]
-            + [columns] * len(addends)
             + [smem] * with_ids
             + [hbm] * len(after),
             out_specs=out_specs,
@@ -57,7 +54,7 @@
         compiler_params=pltpu.CompilerParams(vmem_limit_bytes=VMEM_LIMIT),
         cost_estimate=cost,
         name="block_product",
-    )((first // tile).reshape(1), rows, weight, *addends, *([ids] if with_ids else []), *after)
+    )((first // tile).reshape(1), rows, weight, *([ids] if with_ids else []), *after)
     return out if with_ids else out[0]
 
 
@@ -361,7 +358,8 @@
                     pairs = [(i, i ^ x) for i in range(tp_total)]
                     lows.append(lax.ppermute(low, "tp", pairs))
                 last = low
-            last = partial(1 + step, piece, addends=[moving[piece]], after=[last])
+            product = partial(1 + step, piece, after=[last])
+            last = (product.astype(F32) + moving[piece].astype(F32)).astype(BF16)
             moving[piece] = move(last, piece)
             if step == 1 and piece > 0:
                 last = partial(0, piece, after=[last], cost=LARGE)

time: 81.1 us -> 85 us (1.048)
  the two profiles are of different devices: /device:TPU:0 before, /device:TPU:30 now
where the time goes in v15:
time: 85 us; the launch traced here: 84.7 us
  Pallas kernels  36.2 us (43%)
  waiting for transfers between devices  27.6 us (32%)
  starting transfers between devices  15.2 us (18%)
  other arithmetic  5.28 us (6%)
    pallas_call x7, Pallas kernels, block_product(): pl.pallas_call(functools.partial(product_kernel, with_ids), grid_spec=plt...  19.9 us
    ppermute x6, waiting for transfers between devices, move(): return lax.ppermute(value, ('req', 'tp'), pairs)  14.4 us
    ppermute x3, waiting for transfers between devices, local(): lows.append(lax.ppermute(low, 'tp', pairs))  13.3 us
    ppermute x6, starting transfers between devices, move(): return lax.ppermute(value, ('req', 'tp'), pairs)  5.3 us
    convert_element_type x4, other arithmetic, local(): last = (product.astype(F32) + moving[piece].astype(F32)).astype(BF16)  5.28 us
    pallas_call x2, Pallas kernels, finish(): pl.pallas_call(functools.partial(finish_kernel, len(arrivals)), grid=(row...  4.6 us
    ppermute x3, starting transfers between devices, local(): lows.append(lax.ppermute(low, 'tp', pairs))  4.44 us
    pallas_call x1, Pallas kernels, pick_adapters(): pl.pallas_call(functools.partial(pick_kernel, peers, len(after)), in_spec...  3.98 us
  transfers between devices with their start and end apart: 15, of which 4 were waited for; matrix products, arithmetic and copies ran while one was open for 6% of the time, Pallas kernels for 37%

profile of v15, /device:TPU:30, one launch (start us, length us, event | category | flops | bytes accessed | tf_op | source)
XLA Modules:
  0.0 84.7 jit_solution(7046616422050814551)
XLA Ops:
  0.0 0.0 copy-start
  0.0 0.0 copy-start.4
  0.0 3.6 %first_product.1.rest_1_ = bf16[512,512]{1,0:T(8,128)(2,1)} custom-call(s32[1]{0:T(128)} %bitcast.2.first_ref, bf16[512,2048]{1,0:T(8,128)(2,1)} %rows_ref.17, bf16[2048,4096]{1,0:T(8,128)(2,1)} %weight_ref.15), custom_call_target="tpu_custom_call" | custom-call | flops 1000 | bytes 1000 | tf_op jit(solution)/shard_map/first_product/pallas_call | solution.py:92
  3.6 0.3 collective-permute-start.6
  3.9 0.0 copy-done
  3.9 0.0 copy-done.4
  3.9 3.4 %block_product.7 = (bf16[512,512]{1,0:T(8,128)(2,1)}, s32[1,12]{1,0:T(1,128)S(1)}) custom-call(s32[1]{0:T(128)} %bitcast.1.first_ref, bf16[512,2048]{1,0:T(8,128)(2,1)S(1)} %copy-done, bf16[2048,4096]{1,0:T(8,128)(2,1)} %weight_ref.15, s32[1,12]{1,0:T(1,128)S(1)} %copy-done.4, bf16[512,512]{1,0:T(8,128)(2,1)} %first_product.1.rest_1_), custom_call_target="tpu_custom_call" | custom-call | flops 1000 | bytes 1000 | tf_op jit(solution)/shard_map/block_product/pallas_call | solution.py:40
  7.4 1.8 %collective-permute-start.7 = (bf16[512,512]{1,0:T(8,128)(2,1)}, bf16[512,512]{1,0:T(8,128)(2,1)}, u32[]{:S(2)}, u32[]{:S(2)}) collective-permute-start(bf16[512,512]{1,0:T(8,128)(2,1)} %get-tuple-element.16.rest_0_), channel_id=1, source_target_pairs={{0,3},{1,0},{2,1},{3,2},{4,5},{5,6},{6,7},{7,4},{8,11},{9,8},{10,9... | collective-permute-start | bytes 1572872 | tf_op jit(solution)/shard_map/ppermute | solution.py:326
  9.2 1.2 %collective-permute-start.2 = (s32[1,12]{1,0:T(1,128)S(1)}, s32[1,12]{1,0:T(1,128)S(1)}, u32[]{:S(2)}, u32[]{:S(2)}) collective-permute-start(s32[1,12]{1,0:T(1,128)S(1)} %get-tuple-element.15.rest_0_), channel_id=1, source_target_pairs={{0,12},{4,8},{8,4},{12,0},{1,13},{5,9},{9,5},{13,1},{2,14},{6,10},... | collective-permute-start | bytes 152 | tf_op jit(solution)/shard_map/ppermute | solution.py:344
  10.3 1.5 %collective-permute-start.1 = (s32[1,12]{1,0:T(1,128)S(1)}, s32[1,12]{1,0:T(1,128)S(1)}, u32[]{:S(2)}, u32[]{:S(2)}) collective-permute-start(s32[1,12]{1,0:T(1,128)S(1)} %get-tuple-element.15.rest_0_), channel_id=1, source_target_pairs={{0,8},{4,12},{8,0},{12,4},{1,9},{5,13},{9,1},{13,5},{2,10},{6,14},... | collective-permute-start | bytes 152 | tf_op jit(solution)/shard_map/ppermute | solution.py:344
  11.9 0.0 collective-permute-start
  11.9 0.0 copy-start.3
  11.9 0.0 copy-start.5
  11.9 2.7 %block_product.8.rest_6_.rest_4_ = bf16[512,512]{1,0:T(8,128)(2,1)S(1)} custom-call(s32[1]{0:T(128)} %bitcast.3.first_ref, bf16[512,2048]{1,0:T(8,128)(2,1)S(1)} %copy-done, bf16[2048,4096]{1,0:T(8,128)(2,1)} %weight_ref.15, bf16[512,512]{1,0:T(8,128)(2,1)} %get-tuple-element.16.rest_0_), custom_call_target="tpu_custom_call" | custom-call | flops 1000 | bytes 1000 | tf_op jit(solution)/shard_map/block_product/pallas_call | solution.py:40
  14.7 0.0 collective-permute-done.2.rest_3_
  14.7 0.0 collective-permute-done.1.rest_2_
  14.7 0.0 collective-permute-done.rest_1_
  14.7 0.0 copy-done.3
  14.7 0.0 copy-done.5
  14.8 4.0 %pick_adapters.1 = (bf16[6,16,3072]{2,1,0:T(8,128)(2,1)S(1)}, bf16[6,16,3072]{2,1,0:T(8,128)(2,1)}, bf16[6,16,3072]{2,1,0:T(8,128)(2,1)}, bf16[6,16,3072]{2,1,0:...) custom-call(s32[1]{0:T(128)} %bitcast.me_ref, s32[512]{0:T(512)S(1)} %copy-done.3, s32[1,12]{1,0:T(1,128)S(1)} %copy-done.5, ...), custom_call_target="tpu_custom_call" | custom-call | flops 1000 | bytes 1000 | tf_op jit(solution)/shard_map/pick_adapters/pallas_call | solution.py:181
  18.7 1.3 %collective-permute-start.3 = (bf16[6,16,3072]{2,1,0:T(8,128)(2,1)}, bf16[6,16,3072]{2,1,0:T(8,128)(2,1)}, u32[]{:S(2)}, u32[]{:S(2)}) collective-permute-start(bf16[6,16,3072]{2,1,0:T(8,128)(2,1)} %get-tuple-element.20), channel_id=1, source_target_pairs={{0,4},{4,0},{8,12},{12,8},{1,5},{5,1},{9,13},{13,9},{2,6},{6,2},{1... | collective-permute-start | bytes 1769480 | tf_op jit(solution)/shard_map/ppermute | solution.py:349
  20.0 0.1 collective-permute-start.4
  20.2 1.3 %collective-permute-start.5 = (bf16[6,16,3072]{2,1,0:T(8,128)(2,1)}, bf16[6,16,3072]{2,1,0:T(8,128)(2,1)}, u32[]{:S(2)}, u32[]{:S(2)}) collective-permute-start(bf16[6,16,3072]{2,1,0:T(8,128)(2,1)} %get-tuple-element.22), channel_id=1, source_target_pairs={{0,12},{4,8},{8,4},{12,0},{1,13},{5,9},{9,5},{13,1},{2,14},{6,10},... | collective-permute-start | bytes 1769480 | tf_op jit(solution)/shard_map/ppermute | solution.py:349
  21.5 2.7 %block_product.9 = bf16[512,512]{1,0:T(8,128)(2,1)S(1)} custom-call(s32[1]{0:T(128)} %bitcast.7.first_ref, bf16[512,2048]{1,0:T(8,128)(2,1)S(1)} %copy-done, bf16[2048,4096]{1,0:T(8,128)(2,1)} %weight_ref.15, s32[24]{0:T(128)S(1)} %get-tuple-element.17.rest_0_.start_ref), custom_call_target="tpu_custom_call" | custom-call | flops 1000 | bytes 1000 | tf_op jit(solution)/shard_map/block_product/pallas_call | solution.py:40
  24.2 3.7 %collective-permute-done.6 = bf16[512,512]{1,0:T(8,128)(2,1)} collective-permute-done((bf16[512,512]{1,0:T(8,128)(2,1)}, bf16[512,512]{1,0:T(8,128)(2,1)}, u32[]{:S(2)}, u32[]{:S(2)}) %collective-permute-start.6) | collective-permute-done | bytes 524320 | tf_op jit(solution)/shard_map/ppermute | solution.py:326
  27.9 1.2 %add_convert_fusion.3.rest_0_ = bf16[512,512]{1,0:T(8,128)(2,1)S(1)} fusion(bf16[512,512]{1,0:T(8,128)(2,1)} %collective-permute-done.6, bf16[512,512]{1,0:T(8,128)(2,1)S(1)} %block_product.9), kind=kLoop, calls=%fused_computation.3 | loop fusion | flops 1048576 | bytes 1572864 | tf_op jit(solution)/shard_map/convert_element_type | solution.py:362
  29.0 0.1 collective-permute-start.8
  29.1 2.7 %block_product.10 = bf16[512,512]{1,0:T(8,128)(2,1)S(1)} custom-call(s32[1]{0:T(128)} %bitcast.6.first_ref, bf16[512,2048]{1,0:T(8,128)(2,1)S(1)} %copy-done, bf16[2048,4096]{1,0:T(8,128)(2,1)} %weight_ref.15, bf16[512,512]{1,0:T(8,128)(2,1)S(1)} %add_convert_fusion.3.rest_0_), custom_call_target="tpu_custom_call" | custom-call | flops 1000 | bytes 1000 | tf_op jit(solution)/shard_map/block_product/pallas_call | solution.py:40
  31.8 0.0 collective-permute-done.7
  31.8 2.0 %add_convert_fusion.2.rest_0_ = bf16[512,512]{1,0:T(8,128)(2,1)} fusion(bf16[512,512]{1,0:T(8,128)(2,1)} %collective-permute-done.7, bf16[512,512]{1,0:T(8,128)(2,1)S(1)} %block_product.10), kind=kLoop, calls=%fused_computation.2 | loop fusion | flops 1048576 | bytes 1572864 | tf_op jit(solution)/shard_map/convert_element_type | solution.py:362
  33.8 2.0 %collective-permute-start.12 = (bf16[512,512]{1,0:T(8,128)(2,1)}, bf16[512,512]{1,0:T(8,128)(2,1)}, u32[]{:S(2)}, u32[]{:S(2)}) collective-permute-start(bf16[512,512]{1,0:T(8,128)(2,1)} %add_convert_fusion.2.rest_0_), channel_id=1, source_target_pairs={{0,3},{1,0},{2,1},{3,2},{4,5},{5,6},{6,7},{7,4},{8,11},{9,8},{10,9... | collective-permute-start | bytes 1572872 | tf_op jit(solution)/shard_map/ppermute | solution.py:326
  35.8 2.7 %block_product.11.rest_0_.rest_5_ = bf16[512,512]{1,0:T(8,128)(2,1)S(1)} custom-call(s32[1]{0:T(128)} %bitcast.5.first_ref, bf16[512,2048]{1,0:T(8,128)(2,1)S(1)} %copy-done, bf16[2048,4096]{1,0:T(8,128)(2,1)} %weight_ref.15, bf16[512,512]{1,0:T(8,128)(2,1)} %add_convert_fusion.2.rest_0_), custom_call_target="tpu_custom_call" | custom-call | flops 20000000000 | bytes 1000 | tf_op jit(solution)/shard_map/block_product/pallas_call | solution.py:40
  38.5 0.0 copy-start.1
  38.5 2.9 %block_product.12 = bf16[512,512]{1,0:T(8,128)(2,1)S(1)} custom-call(s32[1]{0:T(128)} %bitcast.4.first_ref, bf16[512,2048]{1,0:T(8,128)(2,1)S(1)} %copy-done, bf16[2048,4096]{1,0:T(8,128)(2,1)} %weight_ref.15, bf16[512,512]{1,0:T(8,128)(2,1)S(1)} %block_product.11.rest_0_.rest_5_), custom_call_target="tpu_custom_call" | custom-call | flops 1000 | bytes 1000 | tf_op jit(solution)/shard_map/block_product/pallas_call | solution.py:40
  41.4 0.0 copy-done.1
  41.4 10.6 %collective-permute-done.8 = bf16[512,512]{1,0:T(8,128)(2,1)S(1)} collective-permute-done((bf16[512,512]{1,0:T(8,128)(2,1)S(1)}, bf16[512,512]{1,0:T(8,128)(2,1)S(1)}, u32[]{:S(2)}, u32[]{:S(2)}) %collective-permute-start.8) | collective-permute-done | bytes 524320 | tf_op jit(solution)/shard_map/ppermute | solution.py:326
  52.1 1.0 %add_convert_fusion.1.rest_4_ = bf16[512,512]{1,0:T(8,128)(2,1)} fusion(bf16[512,512]{1,0:T(8,128)(2,1)S(1)} %collective-permute-done.8, bf16[512,512]{1,0:T(8,128)(2,1)S(1)} %block_product.12), kind=kLoop, calls=%fused_computation.1 | loop fusion | flops 1048576 | bytes 1572864 | tf_op jit(solution)/shard_map/convert_element_type | solution.py:362
  53.0 0.0 collective-permute-start.14
  53.0 0.0 collective-permute-done.3.rest_1_.rest_7_
  53.0 0.0 collective-permute-done.4.rest_2_.rest_8_
  53.0 0.0 collective-permute-done.5.rest_3_.rest_9_
  53.1 2.3 %low_sums.1.rest_0_ = f32[16,512]{1,0:T(8,128)S(1)} custom-call(s32[24]{0:T(128)S(1)} %get-tuple-element.17.rest_0_.start_ref, s32[24]{0:T(128)S(1)} %get-tuple-element.18.end_ref, bf16[512,2048]{1,0:T(8,128)(2,1)S(1)} %copy-done, bf16[6,16,3072]{2,1,0:T(8,128)(2,1)S(1)} %get-tuple-element.19.rest_0_.rest_6_, ...), custom_call_target="tpu_custom_call" | custom-call | flops 1000 | bytes 1000 | tf_op jit(solution)/shard_map/low_sums/pallas_call | solution.py:223
  55.3 0.1 collective-permute-start.11
  55.4 3.5 %collective-permute-start.10 = (f32[16,512]{1,0:T(8,128)S(1)}, f32[16,512]{1,0:T(8,128)S(1)}, u32[]{:S(2)}, u32[]{:S(2)}) collective-permute-start(f32[16,512]{1,0:T(8,128)S(1)} %low_sums.1.rest_0_), channel_id=1, source_target_pairs={{0,2},{1,3},{2,0},{3,1},{4,6},{5,7},{6,4},{7,5},{8,10},{9,11},{10,... | collective-permute-start | bytes 98312 | tf_op jit(solution)/shard_map/ppermute | solution.py:359
  58.9 0.9 %collective-permute-start.9 = (f32[16,512]{1,0:T(8,128)S(1)}, f32[16,512]{1,0:T(8,128)S(1)}, u32[]{:S(2)}, u32[]{:S(2)}) collective-permute-start(f32[16,512]{1,0:T(8,128)S(1)} %low_sums.1.rest_0_), channel_id=1, source_target_pairs={{0,1},{1,0},{2,3},{3,2},{4,5},{5,4},{6,7},{7,6},{8,9},{9,8},{10,11... | collective-permute-start | bytes 98312 | tf_op jit(solution)/shard_map/ppermute | solution.py:359
  59.8 0.0 copy-start.2
  59.8 2.8 %block_product.13 = bf16[512,512]{1,0:T(8,128)(2,1)S(1)} custom-call(s32[1]{0:T(128)} %bitcast.8.first_ref, bf16[512,2048]{1,0:T(8,128)(2,1)S(1)} %copy-done, bf16[2048,4096]{1,0:T(8,128)(2,1)} %weight_ref.15, f32[16,512]{1,0:T(8,128)S(1)} %low_sums.1.rest_0_), custom_call_target="tpu_custom_call" | custom-call | flops 1000 | bytes 1000 | tf_op jit(solution)/shard_map/block_product/pallas_call | solution.py:40
  62.5 0.0 collective-permute-done.12
  62.5 1.2 %add_convert_fusion.rest_10_ = bf16[512,512]{1,0:T(8,128)(2,1)S(1)} fusion(bf16[512,512]{1,0:T(8,128)(2,1)} %collective-permute-done.12, bf16[512,512]{1,0:T(8,128)(2,1)S(1)} %block_product.13), kind=kLoop, calls=%fused_computation | loop fusion | flops 1048576 | bytes 1572864 | tf_op jit(solution)/shard_map/convert_element_type | solution.py:362
  63.7 1.2 %collective-permute-start.13 = (bf16[512,512]{1,0:T(8,128)(2,1)S(1)}, bf16[512,512]{1,0:T(8,128)(2,1)S(1)}, u32[]{:S(2)}, u32[]{:S(2)}) collective-permute-start(bf16[512,512]{1,0:T(8,128)(2,1)S(1)} %add_convert_fusion.rest_10_), channel_id=1, source_target_pairs={{0,3},{1,0},{2,1},{3,2},{4,5},{5,6},{6,7},{7,4},{8,11},{9,8},{10,9... | collective-permute-start | bytes 1572872 | tf_op jit(solution)/shard_map/ppermute | solution.py:326
  64.9 1.9 %collective-permute-done.11.rest_3_ = f32[16,512]{1,0:T(8,128)S(1)} collective-permute-done((f32[16,512]{1,0:T(8,128)S(1)}, f32[16,512]{1,0:T(8,128)S(1)}, u32[]{:S(2)}, u32[]{:S(2)}) %collective-permute-start.11) | collective-permute-done | bytes 32800 | tf_op jit(solution)/shard_map/ppermute | solution.py:359
  66.8 11.4 %collective-permute-done.10.rest_2_ = f32[16,512]{1,0:T(8,128)S(1)} collective-permute-done((f32[16,512]{1,0:T(8,128)S(1)}, f32[16,512]{1,0:T(8,128)S(1)}, u32[]{:S(2)}, u32[]{:S(2)}) %collective-permute-start.10) | collective-permute-done | bytes 32800 | tf_op jit(solution)/shard_map/ppermute | solution.py:359
  78.2 0.0 collective-permute-done.9.rest_1_
  78.2 0.0 copy-done.2
  78.2 1.9 %adapter_term.1 = (f32[512,512]{1,0:T(8,128)S(1)}, f32[512,512]{1,0:T(8,128)S(1)}) custom-call(s32[24]{0:T(128)S(1)} %get-tuple-element.17.rest_0_.start_ref, s32[24]{0:T(128)S(1)} %get-tuple-element.18.end_ref, f32[16,512]{1,0:T(8,128)S(1)} %low_sums.1.rest_0_, f32[16,512]{1,0:T(8,128)S(1)} %collective-permute-done.9.rest_1_, ...), custom_call_target="tpu_custom_call" | custom-call | flops 1000 | bytes 1000 | tf_op jit(solution)/shard_map/adapter_term/pallas_call | solution.py:269
  80.0 0.0 collective-permute-done.14.rest_0_
  80.1 3.2 %finish.2.rest_1_ = bf16[512,1024]{1,0:T(8,128)(2,1)} custom-call(f32[512,512]{1,0:T(8,128)S(1)} %get-tuple-element.24.term_ref, bf16[512,512]{1,0:T(8,128)(2,1)} %collective-permute-done.14.rest_0_), custom_call_target="tpu_custom_call" | custom-call | flops 20000000000 | bytes 1000 | tf_op jit(solution)/shard_map/finish/pallas_call | solution.py:296
  83.3 0.0 collective-permute-done.13.rest_0_
  83.3 1.4 %finish.3 = bf16[512,1024]{1,0:T(8,128)(2,1)} custom-call(f32[512,512]{1,0:T(8,128)S(1)} %get-tuple-element.23.term_ref, bf16[512,512]{1,0:T(8,128)(2,1)S(1)} %collective-permute-done.13.rest_0_, bf16[512,1024]{1,0:T(8,128)(2,1)} %finish.2.rest_1_), custom_call_target="tpu_custom_call", output_to_operand_aliasing={{}: (2, {})} | custom-call | flops 1000 | bytes 1000 | tf_op jit(solution)/shard_map/finish/pallas_call | solution.py:296
Async XLA Ops:
  0.0 3.9 %copy-start = (bf16[512,2048]{1,0:T(8,128)(2,1)S(1)}, bf16[512,2048]{1,0:T(8,128)(2,1)}, u32[]{:S(2)}) copy-start(bf16[512,2048]{1,0:T(8,128)(2,1)} %rows_ref.17) | copy-start | bytes 6291460
  0.0 3.9 %copy-start.4 = (s32[1,12]{1,0:T(1,128)S(1)}, s32[1,12]{1,0:T(1,128)}, u32[]{:S(2)}) copy-start(s32[1,12]{1,0:T(1,128)} %rest_0_.1) | copy-start | bytes 148
  3.6 24.2 %collective-permute-start.6 = (bf16[512,512]{1,0:T(8,128)(2,1)}, bf16[512,512]{1,0:T(8,128)(2,1)}, u32[]{:S(2)}, u32[]{:S(2)}) collective-permute-start(bf16[512,512]{1,0:T(8,128)(2,1)} %first_product.1.rest_1_), channel_id=1, source_target_pairs={{0,1},{1,2},{2,3},{3,0},{4,7},{5,4},{6,5},{7,6},{8,9},{9,10},{10,1... | collective-permute-start | bytes 1572872 | tf_op jit(solution)/shard_map/ppermute | solution.py:326
  7.4 24.5 %collective-permute-start.7 = (bf16[512,512]{1,0:T(8,128)(2,1)}, bf16[512,512]{1,0:T(8,128)(2,1)}, u32[]{:S(2)}, u32[]{:S(2)}) collective-permute-start(bf16[512,512]{1,0:T(8,128)(2,1)} %get-tuple-element.16.rest_0_), channel_id=1, source_target_pairs={{0,3},{1,0},{2,1},{3,2},{4,5},{5,6},{6,7},{7,4},{8,11},{9,8},{10,9... | collective-permute-start | bytes 1572872 | tf_op jit(solution)/shard_map/ppermute | solution.py:326
  9.2 5.5 %collective-permute-start.2 = (s32[1,12]{1,0:T(1,128)S(1)}, s32[1,12]{1,0:T(1,128)S(1)}, u32[]{:S(2)}, u32[]{:S(2)}) collective-permute-start(s32[1,12]{1,0:T(1,128)S(1)} %get-tuple-element.15.rest_0_), channel_id=1, source_target_pairs={{0,12},{4,8},{8,4},{12,0},{1,13},{5,9},{9,5},{13,1},{2,14},{6,10},... | collective-permute-start | bytes 152 | tf_op jit(solution)/shard_map/ppermute | solution.py:344
  10.3 4.4 %collective-permute-start.1 = (s32[1,12]{1,0:T(1,128)S(1)}, s32[1,12]{1,0:T(1,128)S(1)}, u32[]{:S(2)}, u32[]{:S(2)}) collective-permute-start(s32[1,12]{1,0:T(1,128)S(1)} %get-tuple-element.15.rest_0_), channel_id=1, source_target_pairs={{0,8},{4,12},{8,0},{12,4},{1,9},{5,13},{9,1},{13,5},{2,10},{6,14},... | collective-permute-start | bytes 152 | tf_op jit(solution)/shard_map/ppermute | solution.py:344
  11.9 2.9 %collective-permute-start = (s32[1,12]{1,0:T(1,128)S(1)}, s32[1,12]{1,0:T(1,128)S(1)}, u32[]{:S(2)}, u32[]{:S(2)}) collective-permute-start(s32[1,12]{1,0:T(1,128)S(1)} %get-tuple-element.15.rest_0_), channel_id=1, source_target_pairs={{0,4},{4,0},{8,12},{12,8},{1,5},{5,1},{9,13},{13,9},{2,6},{6,2},{1... | collective-permute-start | bytes 152 | tf_op jit(solution)/shard_map/ppermute | solution.py:344
  11.9 2.9 %copy-start.3 = (s32[512]{0:T(512)S(1)}, s32[512]{0:T(512)}, u32[]{:S(2)}) copy-start(s32[512]{0:T(512)} %table_ref.1) | copy-start | bytes 6148
  11.9 2.9 %copy-start.5 = (s32[1,12]{1,0:T(1,128)S(1)}, s32[1,12]{1,0:T(1,128)}, u32[]{:S(2)}) copy-start(s32[1,12]{1,0:T(1,128)} %lens_ref.1) | copy-start | bytes 148
  18.7 34.3 %collective-permute-start.3 = (bf16[6,16,3072]{2,1,0:T(8,128)(2,1)}, bf16[6,16,3072]{2,1,0:T(8,128)(2,1)}, u32[]{:S(2)}, u32[]{:S(2)}) collective-permute-start(bf16[6,16,3072]{2,1,0:T(8,128)(2,1)} %get-tuple-element.20), channel_id=1, source_target_pairs={{0,4},{4,0},{8,12},{12,8},{1,5},{5,1},{9,13},{13,9},{2,6},{6,2},{1... | collective-permute-start | bytes 1769480 | tf_op jit(solution)/shard_map/ppermute | solution.py:349
  20.0 33.0 %collective-permute-start.4 = (bf16[6,16,3072]{2,1,0:T(8,128)(2,1)}, bf16[6,16,3072]{2,1,0:T(8,128)(2,1)}, u32[]{:S(2)}, u32[]{:S(2)}) collective-permute-start(bf16[6,16,3072]{2,1,0:T(8,128)(2,1)} %get-tuple-element.21), channel_id=1, source_target_pairs={{0,8},{4,12},{8,0},{12,4},{1,9},{5,13},{9,1},{13,5},{2,10},{6,14},... | collective-permute-start | bytes 1769480 | tf_op jit(solution)/shard_map/ppermute | solution.py:349
  20.2 32.9 %collective-permute-start.5 = (bf16[6,16,3072]{2,1,0:T(8,128)(2,1)}, bf16[6,16,3072]{2,1,0:T(8,128)(2,1)}, u32[]{:S(2)}, u32[]{:S(2)}) collective-permute-start(bf16[6,16,3072]{2,1,0:T(8,128)(2,1)} %get-tuple-element.22), channel_id=1, source_target_pairs={{0,12},{4,8},{8,4},{12,0},{1,13},{5,9},{9,5},{13,1},{2,14},{6,10},... | collective-permute-start | bytes 1769480 | tf_op jit(solution)/shard_map/ppermute | solution.py:349
  29.0 23.0 %collective-permute-start.8 = (bf16[512,512]{1,0:T(8,128)(2,1)S(1)}, bf16[512,512]{1,0:T(8,128)(2,1)S(1)}, u32[]{:S(2)}, u32[]{:S(2)}) collective-permute-start(bf16[512,512]{1,0:T(8,128)(2,1)S(1)} %add_convert_fusion.3.rest_0_), channel_id=1, source_target_pairs={{0,1},{1,2},{2,3},{3,0},{4,7},{5,4},{6,5},{7,6},{8,9},{9,10},{10,1... | collective-permute-start | bytes 1572872 | tf_op jit(solution)/shard_map/ppermute | solution.py:326
  33.8 28.7 %collective-permute-start.12 = (bf16[512,512]{1,0:T(8,128)(2,1)}, bf16[512,512]{1,0:T(8,128)(2,1)}, u32[]{:S(2)}, u32[]{:S(2)}) collective-permute-start(bf16[512,512]{1,0:T(8,128)(2,1)} %add_convert_fusion.2.rest_0_), channel_id=1, source_target_pairs={{0,3},{1,0},{2,1},{3,2},{4,5},{5,6},{6,7},{7,4},{8,11},{9,8},{10,9... | collective-permute-start | bytes 1572872 | tf_op jit(solution)/shard_map/ppermute | solution.py:326
  38.5 2.9 %copy-start.1 = (bf16[512,512]{1,0:T(8,128)(2,1)}, bf16[512,512]{1,0:T(8,128)(2,1)S(1)}, u32[]{:S(2)}) copy-start(bf16[512,512]{1,0:T(8,128)(2,1)S(1)} %block_product.11.rest_0_.rest_5_) | copy-start | bytes 1572868
  53.0 27.0 %collective-permute-start.14 = (bf16[512,512]{1,0:T(8,128)(2,1)}, bf16[512,512]{1,0:T(8,128)(2,1)}, u32[]{:S(2)}, u32[]{:S(2)}) collective-permute-start(bf16[512,512]{1,0:T(8,128)(2,1)} %add_convert_fusion.1.rest_4_), channel_id=1, source_target_pairs={{0,1},{1,2},{2,3},{3,0},{4,7},{5,4},{6,5},{7,6},{8,9},{9,10},{10,1... | collective-permute-start | bytes 1572872 | tf_op jit(solution)/shard_map/ppermute | solution.py:326
  55.3 11.4 %collective-permute-start.11 = (f32[16,512]{1,0:T(8,128)S(1)}, f32[16,512]{1,0:T(8,128)S(1)}, u32[]{:S(2)}, u32[]{:S(2)}) collective-permute-start(f32[16,512]{1,0:T(8,128)S(1)} %low_sums.1.rest_0_), channel_id=1, source_target_pairs={{0,3},{1,2},{2,1},{3,0},{4,7},{5,6},{6,5},{7,4},{8,11},{9,10},{10,... | collective-permute-start | bytes 98312 | tf_op jit(solution)/shard_map/ppermute | solution.py:359
  55.4 22.8 %collective-permute-start.10 = (f32[16,512]{1,0:T(8,128)S(1)}, f32[16,512]{1,0:T(8,128)S(1)}, u32[]{:S(2)}, u32[]{:S(2)}) collective-permute-start(f32[16,512]{1,0:T(8,128)S(1)} %low_sums.1.rest_0_), channel_id=1, source_target_pairs={{0,2},{1,3},{2,0},{3,1},{4,6},{5,7},{6,4},{7,5},{8,10},{9,11},{10,... | collective-permute-start | bytes 98312 | tf_op jit(solution)/shard_map/ppermute | solution.py:359
  58.9 19.3 %collective-permute-start.9 = (f32[16,512]{1,0:T(8,128)S(1)}, f32[16,512]{1,0:T(8,128)S(1)}, u32[]{:S(2)}, u32[]{:S(2)}) collective-permute-start(f32[16,512]{1,0:T(8,128)S(1)} %low_sums.1.rest_0_), channel_id=1, source_target_pairs={{0,1},{1,0},{2,3},{3,2},{4,5},{5,4},{6,7},{7,6},{8,9},{9,8},{10,11... | collective-permute-start | bytes 98312 | tf_op jit(solution)/shard_map/ppermute | solution.py:359
  59.8 18.4 %copy-start.2 = (bf16[512,512]{1,0:T(8,128)(2,1)S(1)}, bf16[512,512]{1,0:T(8,128)(2,1)}, u32[]{:S(2)}) copy-start(bf16[512,512]{1,0:T(8,128)(2,1)} %copy-done.1) | copy-start | bytes 1572868
  63.7 19.5 %collective-permute-start.13 = (bf16[512,512]{1,0:T(8,128)(2,1)S(1)}, bf16[512,512]{1,0:T(8,128)(2,1)S(1)}, u32[]{:S(2)}, u32[]{:S(2)}) collective-permute-start(bf16[512,512]{1,0:T(8,128)(2,1)S(1)} %add_convert_fusion.rest_10_), channel_id=1, source_target_pairs={{0,3},{1,0},{2,1},{3,2},{4,5},{5,6},{6,7},{7,4},{8,11},{9,8},{10,9... | collective-permute-start | bytes 1572872 | tf_op jit(solution)/shard_map/ppermute | solution.py:326

commit v16 on v13

--- a/solution.py
+++ b/solution.py
@@ -63,12 +63,12 @@
 
 def first_kernel(chunk, first_ref, rows_ref, weight_ref, out_ref, lhs_ref, rhs_ref, acc_ref, sems):
     columns = pl.ds(pl.multiple_of(first_ref[0], 128), out_ref.shape[1])
-    chunks = lhs_ref.shape[0]
+    chunks = rhs_ref.shape[0]
 
     def copies(k):
         part = pl.ds(k * chunk, chunk)
         return (
-            pltpu.make_async_copy(rows_ref.at[:, part], lhs_ref.at[k], sems.at[0, k]),
+            pltpu.make_async_copy(rows_ref.at[:, part], lhs_ref.at[:, part], sems.at[0, k]),
             pltpu.make_async_copy(weight_ref.at[part, columns], rhs_ref.at[k], sems.at[1, k]),
         )
 
@@ -78,7 +78,8 @@
     for k in range(chunks):
         for copy in copies(k):
             copy.wait()
-        part = jnp.dot(lhs_ref[k], rhs_ref[k], preferred_element_type=F32)
+        lhs = lhs_ref[:, k * chunk : (k + 1) * chunk]
+        part = jnp.dot(lhs, rhs_ref[k], preferred_element_type=F32)
         if k == 0:
             acc_ref[...] = part
         elif k < chunks - 1:
@@ -95,10 +96,12 @@
     return pl.pallas_call(
         functools.partial(first_kernel, chunk),
         in_specs=[pl.BlockSpec(memory_space=pltpu.SMEM), hbm, hbm],
-        out_specs=pl.BlockSpec(memory_space=pltpu.VMEM),
-        out_shape=jax.ShapeDtypeStruct((row_total, width), BF16),
+        out_specs=[pl.BlockSpec(memory_space=pltpu.VMEM)] * 2,
+        out_shape=[
+            jax.ShapeDtypeStruct((row_total, width), BF16),
+            jax.ShapeDtypeStruct((row_total, depth), BF16),
+        ],
         scratch_shapes=[
-            pltpu.VMEM((chunks, row_total, chunk), BF16),
             pltpu.VMEM((chunks, chunk, width), BF16),
             pltpu.VMEM((row_total, width), F32),
             pltpu.SemaphoreType.DMA((2, chunks)),
@@ -216,7 +219,7 @@
     for q in range(peers * CAP):
         member = jnp.logical_and(place >= start_ref[q], place < end_ref[q])
         total = jnp.where(member, part[q * rank : (q + 1) * rank], total)
-    out_ref[...] = total
+    out_ref[...] = total.astype(BF16)
 
 
 def low_sums(starts, ends, rows, packs, rank, after):
@@ -230,7 +233,7 @@
         + [pack_spec(p, 0, depth) for p in packs]
         + [pl.BlockSpec(memory_space=pl.ANY)] * len(after),
         out_specs=vmem,
-        out_shape=jax.ShapeDtypeStruct((rank, row_total), F32),
+        out_shape=jax.ShapeDtypeStruct((rank, row_total), BF16),
         compiler_params=pltpu.CompilerParams(vmem_limit_bytes=VMEM_LIMIT),
         cost_estimate=SMALL,
         name="low_sums",
@@ -244,9 +247,9 @@
     rank, row_total = low_refs[0].shape
     width = out_refs[0].shape[1]
     cols = width * pieces
-    low = low_refs[0][...]
+    low = low_refs[0][...].astype(F32)
     for ref in low_refs[1:]:
-        low = low + ref[...]
+        low = low + ref[...].astype(F32)
     low = low.astype(BF16).astype(F32)
     place = lax.broadcasted_iota(jnp.int32, (rank, row_total), 1)
     spread = []
@@ -336,7 +339,8 @@
     def partial(back, piece, **options):
         return block_product(rows, weight, start_of(back, piece), width, **options)
 
-    last = first_product(rows, weight, start_of(1, 0), width)
+    last, rows = first_product(rows, weight, start_of(1, 0), width)
+    rows = pltpu.with_memory_space_constraint(rows, pltpu.VMEM)
     moving = [move(last, 0)]
     for piece in range(1, PIECES):
         last, ids = partial(1, piece, after=[last], ids=ids)
@@ -371,7 +375,8 @@
     result = None
     for piece in range(PIECES):
         cost = SMALL if piece == PIECES - 1 else LARGE
-        result = finish(terms[piece], [moving[piece]], piece, PIECES, result, cost)
+        arrived = pltpu.with_memory_space_constraint(moving[piece], pltpu.VMEM)
+        result = finish(terms[piece], [arrived], piece, PIECES, result, cost)
     return result
 
 

time: 81.1 us -> 80.9 us (level)
  waiting for transfers between devices: 17.2 us -> 16.1 us
    ppermute x3, waiting for transfers between devices: 4.65 us -> 3.23 us  [local(): lows.append(lax.ppermute(low, 'tp', pairs))]
    ppermute x3, starting transfers between devices: 4.51 us -> 5.44 us  [local(): lows.append(lax.ppermute(low, 'tp', pairs))]
  transfers between devices with their start and end apart: 15 -> 15, of which waited for: 6 -> 6; matrix products, arithmetic and copies ran while one was open for 0% -> 0% of each run, Pallas kernels for 38% -> 39%
where the time goes in v16:
time: 80.9 us; the launch traced here: 80.5 us
  Pallas kernels  36.1 us (45%)
  starting transfers between devices  27 us (33%)
  waiting for transfers between devices  16.1 us (20%)
  local copies, waits for them, and re-layouts  0.85 us (1%)
    pallas_call x7, Pallas kernels, block_product(): pl.pallas_call(functools.partial(product_kernel, len(addends), with_ids),...  21.5 us
    ppermute x6, starting transfers between devices, move(): return lax.ppermute(value, ('req', 'tp'), pairs)  17.8 us
    ppermute x6, waiting for transfers between devices, move(): return lax.ppermute(value, ('req', 'tp'), pairs)  12.9 us
    ppermute x3, starting transfers between devices, local(): lows.append(lax.ppermute(low, 'tp', pairs))  5.44 us
    pallas_call x2, Pallas kernels, finish(): pl.pallas_call(functools.partial(finish_kernel, len(arrivals)), grid=(row...  4.6 us
    pallas_call x1, Pallas kernels, pick_adapters(): pl.pallas_call(functools.partial(pick_kernel, peers, len(after)), in_spec...  3.76 us
    pallas_call x1, Pallas kernels, first_product(): pl.pallas_call(functools.partial(first_kernel, chunk), in_specs=[pl.Block...  3.49 us
    ppermute x3, waiting for transfers between devices, local(): lows.append(lax.ppermute(low, 'tp', pairs))  3.23 us
  transfers between devices with their start and end apart: 15, of which 6 were waited for; matrix products, arithmetic and copies ran while one was open for 0% of the time, Pallas kernels for 39%

profile of v16, /device:TPU:0, one launch (start us, length us, event | category | flops | bytes accessed | tf_op | source)
XLA Modules:
  0.0 80.5 jit_solution(15457518562855821580)
XLA Ops:
  0.0 0.0 copy-start.9
  0.0 3.5 %first_product.1 = (bf16[512,512]{1,0:T(8,128)(2,1)}, bf16[512,2048]{1,0:T(8,128)(2,1)S(1)}) custom-call(s32[1]{0:T(128)} %bitcast.2.first_ref, bf16[512,2048]{1,0:T(8,128)(2,1)} %rows_ref.1, bf16[2048,4096]{1,0:T(8,128)(2,1)} %weight_ref.15), custom_call_target="tpu_custom_call" | custom-call | flops 1000 | bytes 1000 | tf_op jit(solution)/shard_map/first_product/pallas_call | solution.py:96
  3.5 3.1 %collective-permute-start.6 = (bf16[512,512]{1,0:T(8,128)(2,1)}, bf16[512,512]{1,0:T(8,128)(2,1)}, u32[]{:S(2)}, u32[]{:S(2)}) collective-permute-start(bf16[512,512]{1,0:T(8,128)(2,1)} %get-tuple-element.18.rest_1_), channel_id=1, source_target_pairs={{0,1},{1,2},{2,3},{3,0},{4,7},{5,4},{6,5},{7,6},{8,9},{9,10},{10,1... | collective-permute-start | bytes 1572872 | tf_op jit(solution)/shard_map/ppermute | solution.py:332
  6.6 0.0 copy-done.9
  6.6 3.5 %block_product.7 = (bf16[512,512]{1,0:T(8,128)(2,1)}, s32[1,12]{1,0:T(1,128)S(1)}) custom-call(s32[1]{0:T(128)} %bitcast.1.first_ref, bf16[512,2048]{1,0:T(8,128)(2,1)S(1)} %get-tuple-element.17.rows_ref, bf16[2048,4096]{1,0:T(8,128)(2,1)} %weight_ref.15, s32[1,12]{1,0:T(1,128)S(1)} %copy-done.9, bf16[512,512]{1,0:T(8,128)(2,1)} %get-tuple-element.18.rest_1_), custom_call_target="tpu_custom_call" | custom-call | flops 1000 | bytes 1000 | tf_op jit(solution)/shard_map/block_product/pallas_call | solution.py:42
  10.0 2.1 %collective-permute-start.8 = (bf16[512,512]{1,0:T(8,128)(2,1)}, bf16[512,512]{1,0:T(8,128)(2,1)}, u32[]{:S(2)}, u32[]{:S(2)}) collective-permute-start(bf16[512,512]{1,0:T(8,128)(2,1)} %get-tuple-element.20.rest_0_), channel_id=1, source_target_pairs={{0,3},{1,0},{2,1},{3,2},{4,5},{5,6},{6,7},{7,4},{8,11},{9,8},{10,9... | collective-permute-start | bytes 1572872 | tf_op jit(solution)/shard_map/ppermute | solution.py:332
  12.1 0.0 collective-permute-start
  12.1 1.7 %collective-permute-start.1 = (s32[1,12]{1,0:T(1,128)S(1)}, s32[1,12]{1,0:T(1,128)S(1)}, u32[]{:S(2)}, u32[]{:S(2)}) collective-permute-start(s32[1,12]{1,0:T(1,128)S(1)} %get-tuple-element.19.rest_0_), channel_id=1, source_target_pairs={{0,8},{4,12},{8,0},{12,4},{1,9},{5,13},{9,1},{13,5},{2,10},{6,14},... | collective-permute-start | bytes 152 | tf_op jit(solution)/shard_map/ppermute | solution.py:351
  13.8 0.2 collective-permute-start.2
  14.0 0.0 copy-start.8
  14.0 0.0 copy-start.10
  14.0 2.7 %block_product.8.rest_6_.rest_4_ = bf16[512,512]{1,0:T(8,128)(2,1)S(1)} custom-call(s32[1]{0:T(128)} %bitcast.3.first_ref, bf16[512,2048]{1,0:T(8,128)(2,1)S(1)} %get-tuple-element.17.rows_ref, bf16[2048,4096]{1,0:T(8,128)(2,1)} %weight_ref.15, bf16[512,512]{1,0:T(8,128)(2,1)} %get-tuple-element.20.rest_0_), custom_call_target="tpu_custom_call" | custom-call | flops 1000 | bytes 1000 | tf_op jit(solution)/shard_map/block_product/pallas_call | solution.py:42
  16.8 0.0 collective-permute-done.rest_1_
  16.9 0.0 collective-permute-done.1.rest_2_
  16.9 0.0 collective-permute-done.2.rest_3_
  16.9 0.0 copy-done.8
  16.9 0.0 copy-done.10
  16.9 3.8 %pick_adapters.1 = (bf16[6,16,3072]{2,1,0:T(8,128)(2,1)S(1)}, bf16[6,16,3072]{2,1,0:T(8,128)(2,1)S(1)}, bf16[6,16,3072]{2,1,0:T(8,128)(2,1)S(1)}, bf16[6,16,3072...) custom-call(s32[1]{0:T(128)} %bitcast.me_ref, s32[512]{0:T(512)S(1)} %copy-done.8, s32[1,12]{1,0:T(1,128)S(1)} %copy-done.10, ...), custom_call_target="tpu_custom_call" | custom-call | flops 1000 | bytes 1000 | tf_op jit(solution)/shard_map/pick_adapters/pallas_call | solution.py:187
  20.7 0.5 collective-permute-start.3
  21.2 1.2 %collective-permute-start.4 = (bf16[6,16,3072]{2,1,0:T(8,128)(2,1)S(1)}, bf16[6,16,3072]{2,1,0:T(8,128)(2,1)S(1)}, u32[]{:S(2)}, u32[]{:S(2)}) collective-permute-start(bf16[6,16,3072]{2,1,0:T(8,128)(2,1)S(1)} %get-tuple-element.25), channel_id=1, source_target_pairs={{0,8},{4,12},{8,0},{12,4},{1,9},{5,13},{9,1},{13,5},{2,10},{6,14},... | collective-permute-start | bytes 1769480 | tf_op jit(solution)/shard_map/ppermute | solution.py:356
  22.4 0.2 collective-permute-start.5
  22.6 0.0 collective-permute-done.6.rest_0_
  22.6 2.8 %block_product.9.rest_1_ = bf16[512,512]{1,0:T(8,128)(2,1)S(1)} custom-call(s32[1]{0:T(128)} %bitcast.5.first_ref, bf16[512,2048]{1,0:T(8,128)(2,1)S(1)} %get-tuple-element.17.rows_ref, bf16[2048,4096]{1,0:T(8,128)(2,1)} %weight_ref.15, bf16[512,512]{1,0:T(8,128)(2,1)} %collective-permute-done.6.rest_0_, s32[24]{0:T(128)S(1)} %get-tuple-element.21.rest_1_.start_ref), custom_call_target="tpu_custom_call" | custom-call | flops 1000 | bytes 1000 | tf_op jit(solution)/shard_map/block_product/pallas_call | solution.py:42
  25.4 6.5 %collective-permute-start.7 = (bf16[512,512]{1,0:T(8,128)(2,1)S(1)}, bf16[512,512]{1,0:T(8,128)(2,1)S(1)}, u32[]{:S(2)}, u32[]{:S(2)}) collective-permute-start(bf16[512,512]{1,0:T(8,128)(2,1)S(1)} %block_product.9.rest_1_), channel_id=1, source_target_pairs={{0,1},{1,2},{2,3},{3,0},{4,7},{5,4},{6,5},{7,6},{8,9},{9,10},{10,1... | collective-permute-start | bytes 1572872 | tf_op jit(solution)/shard_map/ppermute | solution.py:332
  31.9 0.0 collective-permute-done.8.rest_0_
  31.9 3.5 %block_product.10.rest_0_ = bf16[512,512]{1,0:T(8,128)(2,1)} custom-call(s32[1]{0:T(128)} %bitcast.7.first_ref, bf16[512,2048]{1,0:T(8,128)(2,1)S(1)} %get-tuple-element.17.rows_ref, bf16[2048,4096]{1,0:T(8,128)(2,1)} %weight_ref.15, bf16[512,512]{1,0:T(8,128)(2,1)} %collective-permute-done.8.rest_0_, bf16[512,512]{1,0:T(8,128)(2,1)S(1)} %block_product.9.rest_1_), custom_call_target="tpu_custom_call" | custom-call | flops 1000 | bytes 1000 | tf_op jit(solution)/shard_map/block_product/pallas_call | solution.py:42
  35.4 3.7 %collective-permute-start.12 = (bf16[512,512]{1,0:T(8,128)(2,1)}, bf16[512,512]{1,0:T(8,128)(2,1)}, u32[]{:S(2)}, u32[]{:S(2)}) collective-permute-start(bf16[512,512]{1,0:T(8,128)(2,1)} %block_product.10.rest_0_), channel_id=1, source_target_pairs={{0,3},{1,0},{2,1},{3,2},{4,5},{5,6},{6,7},{7,4},{8,11},{9,8},{10,9... | collective-permute-start | bytes 1572872 | tf_op jit(solution)/shard_map/ppermute | solution.py:332
  39.1 2.7 %block_product.11.rest_1_.rest_5_ = bf16[512,512]{1,0:T(8,128)(2,1)S(1)} custom-call(s32[1]{0:T(128)} %bitcast.6.first_ref, bf16[512,2048]{1,0:T(8,128)(2,1)S(1)} %get-tuple-element.17.rows_ref, bf16[2048,4096]{1,0:T(8,128)(2,1)} %weight_ref.15, bf16[512,512]{1,0:T(8,128)(2,1)} %block_product.10.rest_0_), custom_call_target="tpu_custom_call" | custom-call | flops 20000000000 | bytes 1000 | tf_op jit(solution)/shard_map/block_product/pallas_call | solution.py:42
  41.8 0.0 copy-start.6
  41.8 2.6 %collective-permute-done.7.rest_0_ = bf16[512,512]{1,0:T(8,128)(2,1)S(1)} collective-permute-done((bf16[512,512]{1,0:T(8,128)(2,1)S(1)}, bf16[512,512]{1,0:T(8,128)(2,1)S(1)}, u32[]{:S(2)}, u32[]{:S(2)}) %collective-permute-start.7) | collective-permute-done | bytes 524320 | tf_op jit(solution)/shard_map/ppermute | solution.py:332
  44.5 3.4 %block_product.12.rest_4_ = bf16[512,512]{1,0:T(8,128)(2,1)} custom-call(s32[1]{0:T(128)} %bitcast.4.first_ref, bf16[512,2048]{1,0:T(8,128)(2,1)S(1)} %get-tuple-element.17.rows_ref, bf16[2048,4096]{1,0:T(8,128)(2,1)} %weight_ref.15, bf16[512,512]{1,0:T(8,128)(2,1)S(1)} %collective-permute-done.7.rest_0_, bf16[512,512]{1,0:T(8,128)(2,1)S(1)} %block_product.11.rest_1_.rest_5_), custom_call_target="tpu_custom_call" | custom-call | flops 1000 | bytes 1000 | tf_op jit(solution)/shard_map/block_product/pallas_call | solution.py:42
  47.8 0.0 copy-done.6
  47.8 2.3 %collective-permute-start.14 = (bf16[512,512]{1,0:T(8,128)(2,1)}, bf16[512,512]{1,0:T(8,128)(2,1)}, u32[]{:S(2)}, u32[]{:S(2)}) collective-permute-start(bf16[512,512]{1,0:T(8,128)(2,1)} %block_product.12.rest_4_), channel_id=1, source_target_pairs={{0,1},{1,2},{2,3},{3,0},{4,7},{5,4},{6,5},{7,6},{8,9},{9,10},{10,1... | collective-permute-start | bytes 1572872 | tf_op jit(solution)/shard_map/ppermute | solution.py:332
  50.2 0.0 collective-permute-done.3.rest_1_.rest_7_
  50.2 0.0 collective-permute-done.4.rest_2_.rest_8_
  50.2 0.0 copy-start.2
  50.2 0.0 collective-permute-done.5.rest_3_.rest_9_
  50.2 0.0 copy-start.4
  50.2 1.6 %low_sums.1.rest_1_.rest_0_ = bf16[16,512]{1,0:T(8,128)(2,1)S(1)} custom-call(s32[24]{0:T(128)S(1)} %get-tuple-element.21.rest_1_.start_ref, s32[24]{0:T(128)S(1)} %get-tuple-element.22.end_ref, bf16[512,2048]{1,0:T(8,128)(2,1)S(1)} %get-tuple-element.17.rows_ref, bf16[6,16,3072]{2,1,0:T(8,128)(2,1)S(1)} %get-tuple-element.23.rest_0_.rest_6_, ...), custom_call_target="tpu_custom_call" | custom-call | flops 1000 | bytes 1000 | tf_op jit(solution)/shard_map/low_sums/pallas_call | solution.py:229
  51.8 0.0 copy-done.2
  51.8 0.0 copy-start
  51.8 0.8 %copy-done = bf16[6,16,3072]{2,1,0:T(8,128)(2,1)} copy-done((bf16[6,16,3072]{2,1,0:T(8,128)(2,1)}, bf16[6,16,3072]{2,1,0:T(8,128)(2,1)S(1)}, u32[]{:S(2)}) %copy-start) | copy-done | bytes 589848
  52.6 2.9 %collective-permute-start.9 = (bf16[16,512]{1,0:T(8,128)(2,1)S(1)}, bf16[16,512]{1,0:T(8,128)(2,1)S(1)}, u32[]{:S(2)}, u32[]{:S(2)}) collective-permute-start(bf16[16,512]{1,0:T(8,128)(2,1)S(1)} %low_sums.1.rest_1_.rest_0_), channel_id=1, source_target_pairs={{0,1},{1,0},{2,3},{3,2},{4,5},{5,4},{6,7},{7,6},{8,9},{9,8},{10,11... | collective-permute-start | bytes 49160 | tf_op jit(solution)/shard_map/ppermute | solution.py:366
  55.5 0.0 copy-done.4
  55.5 1.1 %collective-permute-start.10 = (bf16[16,512]{1,0:T(8,128)(2,1)S(1)}, bf16[16,512]{1,0:T(8,128)(2,1)S(1)}, u32[]{:S(2)}, u32[]{:S(2)}) collective-permute-start(bf16[16,512]{1,0:T(8,128)(2,1)S(1)} %low_sums.1.rest_1_.rest_0_), channel_id=1, source_target_pairs={{0,2},{1,3},{2,0},{3,1},{4,6},{5,7},{6,4},{7,5},{8,10},{9,11},{10,... | collective-permute-start | bytes 49160 | tf_op jit(solution)/shard_map/ppermute | solution.py:366
  56.6 1.4 %collective-permute-start.11 = (bf16[16,512]{1,0:T(8,128)(2,1)S(1)}, bf16[16,512]{1,0:T(8,128)(2,1)S(1)}, u32[]{:S(2)}, u32[]{:S(2)}) collective-permute-start(bf16[16,512]{1,0:T(8,128)(2,1)S(1)} %low_sums.1.rest_1_.rest_0_), channel_id=1, source_target_pairs={{0,3},{1,2},{2,1},{3,0},{4,7},{5,6},{6,5},{7,4},{8,11},{9,10},{10,... | collective-permute-start | bytes 49160 | tf_op jit(solution)/shard_map/ppermute | solution.py:366
  58.0 3.6 %collective-permute-done.12.rest_0_ = bf16[512,512]{1,0:T(8,128)(2,1)} collective-permute-done((bf16[512,512]{1,0:T(8,128)(2,1)}, bf16[512,512]{1,0:T(8,128)(2,1)}, u32[]{:S(2)}, u32[]{:S(2)}) %collective-permute-start.12) | collective-permute-done | bytes 524320 | tf_op jit(solution)/shard_map/ppermute | solution.py:332
  61.6 0.0 copy-start.1
  61.6 0.0 copy-start.3
  61.6 0.0 copy-start.7
  61.6 2.9 %block_product.13.rest_10_ = bf16[512,512]{1,0:T(8,128)(2,1)S(1)} custom-call(s32[1]{0:T(128)} %bitcast.8.first_ref, bf16[512,2048]{1,0:T(8,128)(2,1)S(1)} %get-tuple-element.17.rows_ref, bf16[2048,4096]{1,0:T(8,128)(2,1)} %weight_ref.15, bf16[512,512]{1,0:T(8,128)(2,1)} %collective-permute-done.12.rest_0_, bf16[16,512]{1,0:T(8,128)(2,1)S(1)} %low_sums.1.rest_1_.rest_0_), custom_call_target="tpu_custom_call" | custom-call | flops 1000 | bytes 1000 | tf_op jit(solution)/shard_map/block_product/pallas_call | solution.py:42
  64.6 0.1 collective-permute-start.13
  64.7 2.5 %collective-permute-done.9.rest_1_ = bf16[16,512]{1,0:T(8,128)(2,1)S(1)} collective-permute-done((bf16[16,512]{1,0:T(8,128)(2,1)S(1)}, bf16[16,512]{1,0:T(8,128)(2,1)S(1)}, u32[]{:S(2)}, u32[]{:S(2)}) %collective-permute-start.9) | collective-permute-done | bytes 16416 | tf_op jit(solution)/shard_map/ppermute | solution.py:366
  67.2 0.4 collective-permute-done.10.rest_2_
  67.5 0.4 collective-permute-done.11.rest_3_
  67.9 0.0 copy-done.1
  67.9 0.0 copy-done.3
  67.9 0.0 copy-done.5
  67.9 0.0 copy-done.7
  67.9 1.3 %adapter_term.1 = (f32[512,512]{1,0:T(8,128)S(1)}, f32[512,512]{1,0:T(8,128)S(1)}) custom-call(s32[24]{0:T(128)S(1)} %get-tuple-element.21.rest_1_.start_ref, s32[24]{0:T(128)S(1)} %get-tuple-element.22.end_ref, bf16[16,512]{1,0:T(8,128)(2,1)S(1)} %low_sums.1.rest_1_.rest_0_, bf16[16,512]{1,0:T(8,128)(2,1)S(1)} %collective-permute-done.9.rest_1_, ...), custom_call_target="tpu_custom_call" | custom-call | flops 1000 | bytes 1000 | tf_op jit(solution)/shard_map/adapter_term/pallas_call | solution.py:275
  69.2 0.0 collective-permute-done.14.rest_0_
  69.2 3.2 %finish.2.rest_1_ = bf16[512,1024]{1,0:T(8,128)(2,1)} custom-call(f32[512,512]{1,0:T(8,128)S(1)} %get-tuple-element.28.term_ref, bf16[512,512]{1,0:T(8,128)(2,1)} %collective-permute-done.14.rest_0_), custom_call_target="tpu_custom_call" | custom-call | flops 20000000000 | bytes 1000 | tf_op jit(solution)/shard_map/finish/pallas_call | solution.py:302
  72.4 6.6 %collective-permute-done.13.rest_0_ = bf16[512,512]{1,0:T(8,128)(2,1)S(1)} collective-permute-done((bf16[512,512]{1,0:T(8,128)(2,1)S(1)}, bf16[512,512]{1,0:T(8,128)(2,1)S(1)}, u32[]{:S(2)}, u32[]{:S(2)}) %collective-permute-start.13) | collective-permute-done | bytes 524320 | tf_op jit(solution)/shard_map/ppermute | solution.py:332
  79.0 1.4 %finish.3 = bf16[512,1024]{1,0:T(8,128)(2,1)} custom-call(f32[512,512]{1,0:T(8,128)S(1)} %get-tuple-element.27.term_ref, bf16[512,512]{1,0:T(8,128)(2,1)S(1)} %collective-permute-done.13.rest_0_, bf16[512,1024]{1,0:T(8,128)(2,1)} %finish.2.rest_1_), custom_call_target="tpu_custom_call", output_to_operand_aliasing={{}: (2, {})} | custom-call | flops 1000 | bytes 1000 | tf_op jit(solution)/shard_map/finish/pallas_call | solution.py:302
  (1 shorter events, 0.0 us)
Async XLA Ops:
  0.0 6.6 %copy-start.9 = (s32[1,12]{1,0:T(1,128)S(1)}, s32[1,12]{1,0:T(1,128)}, u32[]{:S(2)}) copy-start(s32[1,12]{1,0:T(1,128)} %rest_0_.1) | copy-start | bytes 148
  3.5 19.1 %collective-permute-start.6 = (bf16[512,512]{1,0:T(8,128)(2,1)}, bf16[512,512]{1,0:T(8,128)(2,1)}, u32[]{:S(2)}, u32[]{:S(2)}) collective-permute-start(bf16[512,512]{1,0:T(8,128)(2,1)} %get-tuple-element.18.rest_1_), channel_id=1, source_target_pairs={{0,1},{1,2},{2,3},{3,0},{4,7},{5,4},{6,5},{7,6},{8,9},{9,10},{10,1... | collective-permute-start | bytes 1572872 | tf_op jit(solution)/shard_map/ppermute | solution.py:332
  10.0 21.9 %collective-permute-start.8 = (bf16[512,512]{1,0:T(8,128)(2,1)}, bf16[512,512]{1,0:T(8,128)(2,1)}, u32[]{:S(2)}, u32[]{:S(2)}) collective-permute-start(bf16[512,512]{1,0:T(8,128)(2,1)} %get-tuple-element.20.rest_0_), channel_id=1, source_target_pairs={{0,3},{1,0},{2,1},{3,2},{4,5},{5,6},{6,7},{7,4},{8,11},{9,8},{10,9... | collective-permute-start | bytes 1572872 | tf_op jit(solution)/shard_map/ppermute | solution.py:332
  12.1 4.7 %collective-permute-start = (s32[1,12]{1,0:T(1,128)S(1)}, s32[1,12]{1,0:T(1,128)S(1)}, u32[]{:S(2)}, u32[]{:S(2)}) collective-permute-start(s32[1,12]{1,0:T(1,128)S(1)} %get-tuple-element.19.rest_0_), channel_id=1, source_target_pairs={{0,4},{4,0},{8,12},{12,8},{1,5},{5,1},{9,13},{13,9},{2,6},{6,2},{1... | collective-permute-start | bytes 152 | tf_op jit(solution)/shard_map/ppermute | solution.py:351
  12.1 4.7 %collective-permute-start.1 = (s32[1,12]{1,0:T(1,128)S(1)}, s32[1,12]{1,0:T(1,128)S(1)}, u32[]{:S(2)}, u32[]{:S(2)}) collective-permute-start(s32[1,12]{1,0:T(1,128)S(1)} %get-tuple-element.19.rest_0_), channel_id=1, source_target_pairs={{0,8},{4,12},{8,0},{12,4},{1,9},{5,13},{9,1},{13,5},{2,10},{6,14},... | collective-permute-start | bytes 152 | tf_op jit(solution)/shard_map/ppermute | solution.py:351
  13.8 3.1 %collective-permute-start.2 = (s32[1,12]{1,0:T(1,128)S(1)}, s32[1,12]{1,0:T(1,128)S(1)}, u32[]{:S(2)}, u32[]{:S(2)}) collective-permute-start(s32[1,12]{1,0:T(1,128)S(1)} %get-tuple-element.19.rest_0_), channel_id=1, source_target_pairs={{0,12},{4,8},{8,4},{12,0},{1,13},{5,9},{9,5},{13,1},{2,14},{6,10},... | collective-permute-start | bytes 152 | tf_op jit(solution)/shard_map/ppermute | solution.py:351
  14.0 2.9 %copy-start.8 = (s32[512]{0:T(512)S(1)}, s32[512]{0:T(512)}, u32[]{:S(2)}) copy-start(s32[512]{0:T(512)} %table_ref.1) | copy-start | bytes 6148
  14.0 2.9 %copy-start.10 = (s32[1,12]{1,0:T(1,128)S(1)}, s32[1,12]{1,0:T(1,128)}, u32[]{:S(2)}) copy-start(s32[1,12]{1,0:T(1,128)} %lens_ref.1) | copy-start | bytes 148
  20.7 29.5 %collective-permute-start.3 = (bf16[6,16,3072]{2,1,0:T(8,128)(2,1)S(1)}, bf16[6,16,3072]{2,1,0:T(8,128)(2,1)S(1)}, u32[]{:S(2)}, u32[]{:S(2)}) collective-permute-start(bf16[6,16,3072]{2,1,0:T(8,128)(2,1)S(1)} %get-tuple-element.24), channel_id=1, source_target_pairs={{0,4},{4,0},{8,12},{12,8},{1,5},{5,1},{9,13},{13,9},{2,6},{6,2},{1... | collective-permute-start | bytes 1769480 | tf_op jit(solution)/shard_map/ppermute | solution.py:356
  21.2 29.0 %collective-permute-start.4 = (bf16[6,16,3072]{2,1,0:T(8,128)(2,1)S(1)}, bf16[6,16,3072]{2,1,0:T(8,128)(2,1)S(1)}, u32[]{:S(2)}, u32[]{:S(2)}) collective-permute-start(bf16[6,16,3072]{2,1,0:T(8,128)(2,1)S(1)} %get-tuple-element.25), channel_id=1, source_target_pairs={{0,8},{4,12},{8,0},{12,4},{1,9},{5,13},{9,1},{13,5},{2,10},{6,14},... | collective-permute-start | bytes 1769480 | tf_op jit(solution)/shard_map/ppermute | solution.py:356
  22.4 27.8 %collective-permute-start.5 = (bf16[6,16,3072]{2,1,0:T(8,128)(2,1)S(1)}, bf16[6,16,3072]{2,1,0:T(8,128)(2,1)S(1)}, u32[]{:S(2)}, u32[]{:S(2)}) collective-permute-start(bf16[6,16,3072]{2,1,0:T(8,128)(2,1)S(1)} %get-tuple-element.26), channel_id=1, source_target_pairs={{0,12},{4,8},{8,4},{12,0},{1,13},{5,9},{9,5},{13,1},{2,14},{6,10},... | collective-permute-start | bytes 1769480 | tf_op jit(solution)/shard_map/ppermute | solution.py:356
  25.4 19.1 %collective-permute-start.7 = (bf16[512,512]{1,0:T(8,128)(2,1)S(1)}, bf16[512,512]{1,0:T(8,128)(2,1)S(1)}, u32[]{:S(2)}, u32[]{:S(2)}) collective-permute-start(bf16[512,512]{1,0:T(8,128)(2,1)S(1)} %block_product.9.rest_1_), channel_id=1, source_target_pairs={{0,1},{1,2},{2,3},{3,0},{4,7},{5,4},{6,5},{7,6},{8,9},{9,10},{10,1... | collective-permute-start | bytes 1572872 | tf_op jit(solution)/shard_map/ppermute | solution.py:332
  35.4 26.2 %collective-permute-start.12 = (bf16[512,512]{1,0:T(8,128)(2,1)}, bf16[512,512]{1,0:T(8,128)(2,1)}, u32[]{:S(2)}, u32[]{:S(2)}) collective-permute-start(bf16[512,512]{1,0:T(8,128)(2,1)} %block_product.10.rest_0_), channel_id=1, source_target_pairs={{0,3},{1,0},{2,1},{3,2},{4,5},{5,6},{6,7},{7,4},{8,11},{9,8},{10,9... | collective-permute-start | bytes 1572872 | tf_op jit(solution)/shard_map/ppermute | solution.py:332
  41.8 6.0 %copy-start.6 = (bf16[512,512]{1,0:T(8,128)(2,1)}, bf16[512,512]{1,0:T(8,128)(2,1)S(1)}, u32[]{:S(2)}) copy-start(bf16[512,512]{1,0:T(8,128)(2,1)S(1)} %block_product.11.rest_1_.rest_5_) | copy-start | bytes 1572868
  47.8 21.3 %collective-permute-start.14 = (bf16[512,512]{1,0:T(8,128)(2,1)}, bf16[512,512]{1,0:T(8,128)(2,1)}, u32[]{:S(2)}, u32[]{:S(2)}) collective-permute-start(bf16[512,512]{1,0:T(8,128)(2,1)} %block_product.12.rest_4_), channel_id=1, source_target_pairs={{0,1},{1,2},{2,3},{3,0},{4,7},{5,4},{6,5},{7,6},{8,9},{9,10},{10,1... | collective-permute-start | bytes 1572872 | tf_op jit(solution)/shard_map/ppermute | solution.py:332
  50.2 1.6 %copy-start.2 = (bf16[6,16,3072]{2,1,0:T(8,128)(2,1)}, bf16[6,16,3072]{2,1,0:T(8,128)(2,1)S(1)}, u32[]{:S(2)}) copy-start(bf16[6,16,3072]{2,1,0:T(8,128)(2,1)S(1)} %collective-permute-done.4.rest_2_.rest_8_) | copy-start | bytes 1769476
  50.2 5.3 %copy-start.4 = (bf16[6,16,3072]{2,1,0:T(8,128)(2,1)}, bf16[6,16,3072]{2,1,0:T(8,128)(2,1)S(1)}, u32[]{:S(2)}) copy-start(bf16[6,16,3072]{2,1,0:T(8,128)(2,1)S(1)} %collective-permute-done.5.rest_3_.rest_9_) | copy-start | bytes 1769476
  51.8 0.8 %copy-start = (bf16[6,16,3072]{2,1,0:T(8,128)(2,1)}, bf16[6,16,3072]{2,1,0:T(8,128)(2,1)S(1)}, u32[]{:S(2)}) copy-start(bf16[6,16,3072]{2,1,0:T(8,128)(2,1)S(1)} %collective-permute-done.3.rest_1_.rest_7_) | copy-start | bytes 1769476
  52.6 14.6 %collective-permute-start.9 = (bf16[16,512]{1,0:T(8,128)(2,1)S(1)}, bf16[16,512]{1,0:T(8,128)(2,1)S(1)}, u32[]{:S(2)}, u32[]{:S(2)}) collective-permute-start(bf16[16,512]{1,0:T(8,128)(2,1)S(1)} %low_sums.1.rest_1_.rest_0_), channel_id=1, source_target_pairs={{0,1},{1,0},{2,3},{3,2},{4,5},{5,4},{6,7},{7,6},{8,9},{9,8},{10,11... | collective-permute-start | bytes 49160 | tf_op jit(solution)/shard_map/ppermute | solution.py:366
  55.5 12.1 %collective-permute-start.10 = (bf16[16,512]{1,0:T(8,128)(2,1)S(1)}, bf16[16,512]{1,0:T(8,128)(2,1)S(1)}, u32[]{:S(2)}, u32[]{:S(2)}) collective-permute-start(bf16[16,512]{1,0:T(8,128)(2,1)S(1)} %low_sums.1.rest_1_.rest_0_), channel_id=1, source_target_pairs={{0,2},{1,3},{2,0},{3,1},{4,6},{5,7},{6,4},{7,5},{8,10},{9,11},{10,... | collective-permute-start | bytes 49160 | tf_op jit(solution)/shard_map/ppermute | solution.py:366
  56.6 11.3 %collective-permute-start.11 = (bf16[16,512]{1,0:T(8,128)(2,1)S(1)}, bf16[16,512]{1,0:T(8,128)(2,1)S(1)}, u32[]{:S(2)}, u32[]{:S(2)}) collective-permute-start(bf16[16,512]{1,0:T(8,128)(2,1)S(1)} %low_sums.1.rest_1_.rest_0_), channel_id=1, source_target_pairs={{0,3},{1,2},{2,1},{3,0},{4,7},{5,6},{6,5},{7,4},{8,11},{9,10},{10,... | collective-permute-start | bytes 49160 | tf_op jit(solution)/shard_map/ppermute | solution.py:366
  61.6 6.3 %copy-start.1 = (bf16[6,16,3072]{2,1,0:T(8,128)(2,1)S(1)}, bf16[6,16,3072]{2,1,0:T(8,128)(2,1)}, u32[]{:S(2)}) copy-start(bf16[6,16,3072]{2,1,0:T(8,128)(2,1)} %copy-done) | copy-start | bytes 1769476
  61.6 6.3 %copy-start.3 = (bf16[6,16,3072]{2,1,0:T(8,128)(2,1)S(1)}, bf16[6,16,3072]{2,1,0:T(8,128)(2,1)}, u32[]{:S(2)}) copy-start(bf16[6,16,3072]{2,1,0:T(8,128)(2,1)} %copy-done.2) | copy-start | bytes 1769476
  61.6 6.3 %copy-start.5 = (bf16[6,16,3072]{2,1,0:T(8,128)(2,1)S(1)}, bf16[6,16,3072]{2,1,0:T(8,128)(2,1)}, u32[]{:S(2)}) copy-start(bf16[6,16,3072]{2,1,0:T(8,128)(2,1)} %copy-done.4) | copy-start | bytes 1769476
  61.6 6.3 %copy-start.7 = (bf16[512,512]{1,0:T(8,128)(2,1)S(1)}, bf16[512,512]{1,0:T(8,128)(2,1)}, u32[]{:S(2)}) copy-start(bf16[512,512]{1,0:T(8,128)(2,1)} %copy-done.6) | copy-start | bytes 1572868
  64.6 14.5 %collective-permute-start.13 = (bf16[512,512]{1,0:T(8,128)(2,1)S(1)}, bf16[512,512]{1,0:T(8,128)(2,1)S(1)}, u32[]{:S(2)}, u32[]{:S(2)}) collective-permute-start(bf16[512,512]{1,0:T(8,128)(2,1)S(1)} %block_product.13.rest_10_), channel_id=1, source_target_pairs={{0,3},{1,0},{2,1},{3,2},{4,5},{5,6},{6,7},{7,4},{8,11},{9,8},{10,9... | collective-permute-start | bytes 1572872 | tf_op jit(solution)/shard_map/ppermute | solution.py:332

commit v17 on v10

--- a/solution.py
+++ b/solution.py
@@ -8,7 +8,6 @@
 from jax.sharding import PartitionSpec as P
 
 CAP = 6
-PIECES = 2
 VMEM_LIMIT = 20 * 1024 * 1024
 F32 = jnp.float32
 BF16 = jnp.bfloat16
@@ -113,7 +112,7 @@
     ids_refs = rest[:peers]
     down_ref, up_ref = rest[peers : peers + 2]
     rest = rest[peers + 2 + afters :]
-    packs, (start_ref, end_ref, pick_ref, count_ref, sem) = rest[:peers], rest[peers:]
+    pairs, (start_ref, end_ref, pick_ref, count_ref, sem) = rest[: peers // 2], rest[peers // 2 :]
     segs = lens_ref.shape[1]
     share, _, depth = down_ref.shape
     cols = up_ref.shape[2]
@@ -130,7 +129,7 @@
         count_ref[x] = 0
 
     def copies(x, c, source):
-        pack = packs[x].at[c]
+        pack = pairs[x // 2].at[x % 2, c]
         return (
             pltpu.make_async_copy(down_ref.at[source], pack.at[:, pl.ds(0, depth)], sem),
             pltpu.make_async_copy(up_ref.at[source], pack.at[:, pl.ds(depth, cols)], sem),
@@ -184,8 +183,8 @@
     out = pl.pallas_call(
         functools.partial(pick_kernel, peers, len(after)),
         in_specs=[smem] * (3 + peers) + [hbm] * (2 + len(after)),
-        out_specs=[vmem] * peers + [smem, smem],
-        out_shape=[jax.ShapeDtypeStruct((CAP, rank, depth + cols), BF16)] * peers
+        out_specs=[vmem] * (peers // 2) + [smem, smem],
+        out_shape=[jax.ShapeDtypeStruct((2, CAP, rank, depth + cols), BF16)] * (peers // 2)
         + [jax.ShapeDtypeStruct((peers * CAP,), jnp.int32)] * 2,
         scratch_shapes=[
             pltpu.SMEM((peers * CAP,), jnp.int32),
@@ -199,8 +198,19 @@
     return list(out[:-2]), out[-2], out[-1]
 
 
+def exchange(pairs, peers):
+    packs = []
+    for y, pair in enumerate(pairs):
+        if y > 0:
+            pair = lax.ppermute(pair, "req", [(i, i ^ (2 * y)) for i in range(peers)])
+        other = lax.ppermute(pair, "req", [(i, i ^ 1) for i in range(peers)])
+        packs += [(pair, 0), (other, 1)]
+    return packs
+
+
 def pack_spec(pack, first, width):
-    return pl.BlockSpec(pack.shape[:2] + (width,), lambda i: (0, 0, first // width))
+    array, place = pack
+    return pl.BlockSpec((1,) + array.shape[1:3] + (width,), lambda i: (place, 0, 0, first // width))
 
 
 def low_kernel(peers, start_ref, end_ref, rows_ref, *rest):
@@ -234,19 +244,16 @@
         compiler_params=pltpu.CompilerParams(vmem_limit_bytes=VMEM_LIMIT),
         cost_estimate=SMALL,
         name="low_sums",
-    )(starts, ends, rows, *packs, *after)
-
-
-def term_kernel(lows, pieces, peers, start_ref, end_ref, *rest):
-    low_refs, rest = rest[:lows], rest[lows:]
+    )(starts, ends, rows, *[array for array, _ in packs], *after)
+
+
+def term_kernel(offsets, peers, start_ref, end_ref, low_ref, came_ref, *rest):
+    pieces = len(offsets)
     own_refs, rest = rest[:pieces], rest[pieces:]
     up_refs, out_refs = rest[:peers], rest[-pieces:]
-    rank, row_total = low_refs[0].shape
-    width = out_refs[0].shape[1]
-    cols = width * pieces
-    low = low_refs[0][...]
-    for ref in low_refs[1:]:
-        low = low + ref[...]
+    rank, row_total = low_ref.shape
+    cols = sum(ref.shape[1] for ref in out_refs)
+    low = low_ref[...] + came_ref[...]
     low = low.astype(BF16).astype(F32)
     place = lax.broadcasted_iota(jnp.int32, (rank, row_total), 1)
     spread = []
@@ -256,32 +263,49 @@
     spread = jnp.concatenate(spread, axis=0).astype(BF16)
     ups = jnp.concatenate([ref[...].reshape(CAP * rank, cols) for ref in up_refs], axis=0)
     for piece in range(pieces):
-        columns = slice(piece * width, (piece + 1) * width)
+        columns = slice(offsets[piece], offsets[piece] + out_refs[piece].shape[1])
         term = lax.dot_general(
             spread, ups[:, columns], (((0,), (0,)), ((), ())), preferred_element_type=F32
         )
         out_refs[piece][...] = own_refs[piece][...].astype(F32) + term
 
 
-def adapter_term(starts, ends, lows, owns, packs, after):
-    row_total, width = owns[0].shape
-    cols = width * len(owns)
+def adapter_term(starts, ends, low, came, owns, packs, offsets, after):
+    row_total = owns[0].shape[0]
+    cols = sum(own.shape[1] for own in owns)
     smem = pl.BlockSpec(memory_space=pltpu.SMEM)
     vmem = pl.BlockSpec(memory_space=pltpu.VMEM)
-    depth = packs[0].shape[2] - cols
+    depth = packs[0][0].shape[3] - cols
     return pl.pallas_call(
-        functools.partial(term_kernel, len(lows), len(owns), len(packs)),
+        functools.partial(term_kernel, offsets, len(packs)),
         grid=(1,),
         in_specs=[smem, smem]
-        + [vmem] * (len(lows) + len(owns))
+        + [vmem] * (2 + len(owns))
         + [pack_spec(p, depth, cols) for p in packs]
         + [pl.BlockSpec(memory_space=pl.ANY)] * len(after),
         out_specs=[vmem] * len(owns),
-        out_shape=[jax.ShapeDtypeStruct((row_total, width), F32)] * len(owns),
+        out_shape=[jax.ShapeDtypeStruct(own.shape, F32) for own in owns],
         compiler_params=pltpu.CompilerParams(vmem_limit_bytes=VMEM_LIMIT),
         cost_estimate=SMALL,
         name="adapter_term",
-    )(starts, ends, *lows, *owns, *packs, *after)
+    )(starts, ends, low, came, *owns, *[array for array, _ in packs], *after)
+
+
+def sum_kernel(a_ref, b_ref, *rest):
+    rest[-1][...] = a_ref[...] + b_ref[...]
+
+
+def sum_after(a, b, after):
+    vmem = pl.BlockSpec(memory_space=pltpu.VMEM)
+    return pl.pallas_call(
+        sum_kernel,
+        in_specs=[vmem, vmem] + [pl.BlockSpec(memory_space=pl.ANY)] * len(after),
+        out_specs=vmem,
+        out_shape=jax.ShapeDtypeStruct(a.shape, a.dtype),
+        compiler_params=pltpu.CompilerParams(vmem_limit_bytes=VMEM_LIMIT),
+        cost_estimate=SMALL,
+        name="sum_after",
+    )(a, b, *after)
 
 
 def finish_kernel(addends, term_ref, *rest):
@@ -291,7 +315,7 @@
     rest[-1][...] = total.astype(rest[-1].dtype)
 
 
-def finish(term, arrivals, piece, pieces, result, cost):
+def finish(term, arrivals, offset, cols, result, cost):
     row_total, width = term.shape
     height = min(row_total, 128)
     block = pl.BlockSpec((height, width), lambda i: (i, 0))
@@ -300,8 +324,8 @@
         functools.partial(finish_kernel, len(arrivals)),
         grid=(row_total // height,),
         in_specs=[block] * (1 + len(arrivals)) + [pl.BlockSpec(memory_space=pl.ANY)] * len(held),
-        out_specs=pl.BlockSpec((height, width), lambda i: (i, piece)),
-        out_shape=jax.ShapeDtypeStruct((row_total, width * pieces), BF16),
+        out_specs=pl.BlockSpec((height, width), lambda i: (i, offset // width)),
+        out_shape=jax.ShapeDtypeStruct((row_total, cols), BF16),
         input_output_aliases={1 + len(arrivals): 0} if held else {},
         compiler_params=pltpu.CompilerParams(vmem_limit_bytes=VMEM_LIMIT),
         cost_estimate=cost,
@@ -315,7 +339,9 @@
     up = pltpu.with_memory_space_constraint(up, pltpu.HBM)
     rank = down.shape[1]
     cols = up.shape[2]
-    width = cols // PIECES
+    widths = (cols // 4, cols // 2, cols // 4)
+    offsets = (cols // 2, 0, 3 * cols // 4)
+    pieces = range(len(widths))
     me_req = lax.axis_index("req").astype(jnp.int32)
     me = lax.axis_index("tp").astype(jnp.int32)
     steps = tp_total - 1
@@ -331,45 +357,47 @@
     def start_of(back, piece):
         behind = jnp.where(lax.rem(me_req + piece, 2) == 0, tp_total - back, back)
         block = lax.rem(me + behind, tp_total)
-        return block * cols + piece * width
+        return block * cols + offsets[piece]
 
     def partial(back, piece, **options):
-        return block_product(rows, weight, start_of(back, piece), width, **options)
-
-    last = first_product(rows, weight, start_of(1, 0), width)
-    moving, owns = [move(last, 0)], []
-    for piece in range(1, PIECES):
-        last, ids = partial(1, piece, after=[last], ids=ids)
-        moving.append(move(last, piece))
+        return block_product(rows, weight, start_of(back, piece), widths[piece], **options)
+
+    last = first_product(rows, weight, start_of(1, 0), widths[0])
+    moving, owns = [move(last, 0)], [None for _ in pieces]
+    last, ids = partial(1, 1, after=[last], ids=ids)
+    moving.append(move(last, 1))
 
     all_ids = [ids]
     for x in range(1, req_total):
         all_ids.append(lax.ppermute(ids, "req", [(i, i ^ x) for i in range(req_total)]))
-    packs, starts, ends = pick_adapters(me_req, table, all_ids, lens, down, up, [last])
-    for x in range(1, req_total):
-        packs[x] = lax.ppermute(packs[x], "req", [(i, i ^ x) for i in range(req_total)])
-
-    last = starts
+    last = owns[0] = partial(0, 0, after=[last])
+    pairs, starts, ends = pick_adapters(me_req, table, all_ids, lens, down, up, [last])
+    packs = exchange(pairs, req_total)
+    last = partial(1, 2, after=[starts, moving[0]])
+    moving.append(move(last, 2))
+
     for step in range(1, steps):
-        for piece in range(PIECES):
-            if step == steps - 1 and piece == PIECES - 1:
-                low = low_sums(starts, ends, rows, packs, rank, [last])
-                lows = [low]
-                for x in range(1, tp_total):
-                    pairs = [(i, i ^ x) for i in range(tp_total)]
-                    lows.append(lax.ppermute(low, "tp", pairs))
-                last = low
-            last = partial(1 + step, piece, addends=[moving[piece]], after=[last])
+        for piece in pieces:
+            cost = LARGE if step == steps - 1 else SMALL
+            last = partial(1 + step, piece, addends=[moving[piece]], after=[last], cost=cost)
             moving[piece] = move(last, piece)
-            if step == 1:
-                last = partial(0, piece, after=[last], cost=LARGE)
-                owns.append(last)
-
-    terms = adapter_term(starts, ends, lows, owns, packs, [last])
+            if step == 1 and piece < 2:
+                last = owns[2 - piece] = partial(0, 2 - piece, after=[last], cost=LARGE if piece == 0 else SMALL)
+            if step == steps - 1 and piece == 0:
+                last = low = low_sums(starts, ends, rows, packs, rank, [last])
+                bit = 1
+                came = lax.ppermute(low, "tp", [(i, i ^ bit) for i in range(tp_total)])
+            if step == steps - 1 and piece == 1:
+                while 2 * bit < tp_total:
+                    last = low = sum_after(low, came, [last])
+                    bit *= 2
+                    came = lax.ppermute(low, "tp", [(i, i ^ bit) for i in range(tp_total)])
+
+    terms = adapter_term(starts, ends, low, came, owns, packs, offsets, [last])
     result = None
-    for piece in range(PIECES):
-        cost = SMALL if piece == PIECES - 1 else LARGE
-        result = finish(terms[piece], [moving[piece]], piece, PIECES, result, cost)
+    for piece in pieces:
+        cost = LARGE if piece == 0 else SMALL
+        result = finish(terms[piece], [moving[piece]], offsets[piece], cols, result, cost)
     return result
 
 

time: 81.6 us -> 86.9 us (1.065)
  waiting for transfers between devices: 12.2 us -> 26.6 us
  starting transfers between devices: 31.5 us -> 20.7 us
  Pallas kernels: 36.4 us -> 38.7 us
    ppermute x6 -> x5, waiting for transfers between devices: 4.17 us -> 22.3 us  [the longest x2 14.6 us: local(): came = lax.ppermute(low, 'tp', [(i, i ^ bit) for i in range(tp_total)])]
    ppermute x6 -> x9, starting transfers between devices: 18.6 us -> 11.7 us  [move(): return lax.ppermute(value, ('req', 'tp'), pairs)]
    ppermute x6 -> x5, starting transfers between devices: 9.73 us -> 5.75 us  [the longest x2 4.4 us: local(): came = lax.ppermute(low, 'tp', [(i, i ^ bit) for i in range(tp_total)])]
    pallas_call x7 -> x11, Pallas kernels: 21.5 us -> 25.1 us  [block_product(): pl.pallas_call(functools.partial(product_kernel, len(addends), with_ids),...]
    ppermute x3, waiting for transfers between devices: 2.28 us -> 0.02 us  [local(): lax.ppermute(ids, 'req', [(i, i ^ x) for i in range(req_total)])]
    ppermute x6 -> x9, waiting for transfers between devices: 5.73 us -> 4.26 us  [move(): return lax.ppermute(value, ('req', 'tp'), pairs)]
    pallas_call x2 -> x3, Pallas kernels: 4.6 us -> 4.08 us  [finish(): pl.pallas_call(functools.partial(finish_kernel, len(arrivals)), grid=(row...]
  transfers between devices with their start and end apart: 15 -> 17, of which waited for: 5 -> 3; matrix products, arithmetic and copies ran while one was open for 0% -> 0% of each run, Pallas kernels for 39% -> 40%
where the time goes in v17:
time: 86.9 us; the launch traced here: 86.4 us
  Pallas kernels  38.7 us (45%)
  waiting for transfers between devices  26.6 us (31%)
  starting transfers between devices  20.7 us (24%)
    pallas_call x11, Pallas kernels, block_product(): pl.pallas_call(functools.partial(product_kernel, len(addends), with_ids),...  25.1 us
    ppermute x2, waiting for transfers between devices, local(): came = lax.ppermute(low, 'tp', [(i, i ^ bit) for i in range(tp_total)])  14.6 us
    ppermute x9, starting transfers between devices, move(): return lax.ppermute(value, ('req', 'tp'), pairs)  11.7 us
    ppermute x1, waiting for transfers between devices, exchange(): pair = lax.ppermute(pair, 'req', [(i, i ^ 2 * y) for i in range(peers)])  7.67 us
    ppermute x2, starting transfers between devices, local(): came = lax.ppermute(low, 'tp', [(i, i ^ bit) for i in range(tp_total)])  4.4 us
    ppermute x9, waiting for transfers between devices, move(): return lax.ppermute(value, ('req', 'tp'), pairs)  4.26 us
    pallas_call x3, Pallas kernels, finish(): pl.pallas_call(functools.partial(finish_kernel, len(arrivals)), grid=(row...  4.08 us
    pallas_call x1, Pallas kernels, pick_adapters(): pl.pallas_call(functools.partial(pick_kernel, peers, len(after)), in_spec...  3.86 us
  transfers between devices with their start and end apart: 17, of which 3 were waited for; matrix products, arithmetic and copies ran while one was open for 0% of the time, Pallas kernels for 40%

profile of v17, /device:TPU:0, one launch (start us, length us, event | category | flops | bytes accessed | tf_op | source)
XLA Modules:
  0.0 86.4 jit_solution(7963123386900421269)
XLA Ops:
  0.0 0.0 copy-start
  0.0 0.0 copy-start.2
  0.0 2.8 %first_product.1.rest_1_ = bf16[512,256]{1,0:T(8,128)(2,1)S(1)} custom-call(s32[1]{0:T(128)} %bitcast.2.first_ref, bf16[512,2048]{1,0:T(8,128)(2,1)} %rows_ref.25, bf16[2048,4096]{1,0:T(8,128)(2,1)} %weight_ref.23), custom_call_target="tpu_custom_call" | custom-call | flops 1000 | bytes 1000 | tf_op jit(solution)/shard_map/first_product/pallas_call | solution.py:94
  2.8 3.1 %collective-permute-start.6 = (bf16[512,256]{1,0:T(8,128)(2,1)S(1)}, bf16[512,256]{1,0:T(8,128)(2,1)S(1)}, u32[]{:S(2)}, u32[]{:S(2)}) collective-permute-start(bf16[512,256]{1,0:T(8,128)(2,1)S(1)} %first_product.1.rest_1_), channel_id=1, source_target_pairs={{0,1},{1,2},{2,3},{3,0},{4,7},{5,4},{6,5},{7,6},{8,9},{9,10},{10,1... | collective-permute-start | bytes 786440 | tf_op jit(solution)/shard_map/ppermute | solution.py:355
  5.9 0.0 copy-done
  5.9 0.0 copy-done.2
  5.9 3.3 %block_product.11 = (bf16[512,512]{1,0:T(8,128)(2,1)S(1)}, s32[1,12]{1,0:T(1,128)S(1)}) custom-call(s32[1]{0:T(128)} %bitcast.1.first_ref, bf16[512,2048]{1,0:T(8,128)(2,1)S(1)} %copy-done, bf16[2048,4096]{1,0:T(8,128)(2,1)} %weight_ref.23, s32[1,12]{1,0:T(1,128)S(1)} %copy-done.2, bf16[512,256]{1,0:T(8,128)(2,1)S(1)} %first_product.1.rest_1_), custom_call_target="tpu_custom_call" | custom-call | flops 1000 | bytes 1000 | tf_op jit(solution)/shard_map/block_product/pallas_call | solution.py:41
  9.2 2.8 %collective-permute-start.2 = (s32[1,12]{1,0:T(1,128)S(1)}, s32[1,12]{1,0:T(1,128)S(1)}, u32[]{:S(2)}, u32[]{:S(2)}) collective-permute-start(s32[1,12]{1,0:T(1,128)S(1)} %get-tuple-element.14.rest_0_), channel_id=1, source_target_pairs={{0,12},{4,8},{8,4},{12,0},{1,13},{5,9},{9,5},{13,1},{2,14},{6,10},... | collective-permute-start | bytes 152 | tf_op jit(solution)/shard_map/ppermute | solution.py:372
  12.0 0.5 collective-permute-start.1
  12.5 0.0 collective-permute-start
  12.5 0.8 collective-permute-start.9
  13.3 0.0 copy-start.1
  13.3 0.0 copy-start.3
  13.3 2.0 %block_product.12.rest_6_.rest_0_ = bf16[512,256]{1,0:T(8,128)(2,1)S(1)} custom-call(s32[1]{0:T(128)} %bitcast.3.first_ref, bf16[512,2048]{1,0:T(8,128)(2,1)S(1)} %copy-done, bf16[2048,4096]{1,0:T(8,128)(2,1)} %weight_ref.23, bf16[512,512]{1,0:T(8,128)(2,1)S(1)} %get-tuple-element.15.rest_0_), custom_call_target="tpu_custom_call" | custom-call | flops 1000 | bytes 1000 | tf_op jit(solution)/shard_map/block_product/pallas_call | solution.py:41
  15.5 0.0 collective-permute-done.2.rest_3_
  15.5 0.0 collective-permute-done.1.rest_2_
  15.5 0.0 collective-permute-done.rest_1_
  15.5 0.0 copy-done.1
  15.5 0.0 copy-done.3
  15.6 3.9 %pick_adapters.1 = (bf16[2,6,16,3072]{3,2,1,0:T(8,128)(2,1)S(1)}, bf16[2,6,16,3072]{3,2,1,0:T(8,128)(2,1)S(1)}, s32[24]{0:T(128)S(1)}, s32[24]{0:T(128)S(1)}) custom-call(s32[1]{0:T(128)} %bitcast.me_ref, s32[512]{0:T(512)S(1)} %copy-done.1, s32[1,12]{1,0:T(1,128)S(1)} %copy-done.3, s32[1,12]{1,0:T(1,128)S(1)} %get-tuple-element.14.rest_0_, ...), custom_call_target="tpu_custom_call" | custom-call | flops 1000 | bytes 1000 | tf_op jit(solution)/shard_map/pick_adapters/pallas_call | solution.py:183
  19.4 1.3 %collective-permute-start.4 = (bf16[2,6,16,3072]{3,2,1,0:T(8,128)(2,1)S(1)}, bf16[2,6,16,3072]{3,2,1,0:T(8,128)(2,1)S(1)}, u32[]{:S(2)}, u32[]{:S(2)}) collective-permute-start(bf16[2,6,16,3072]{3,2,1,0:T(8,128)(2,1)S(1)} %get-tuple-element.19), channel_id=1, source_target_pairs={{0,8},{4,12},{8,0},{12,4},{1,9},{5,13},{9,1},{13,5},{2,10},{6,14},... | collective-permute-start | bytes 3538952 | tf_op jit(solution)/shard_map/ppermute | solution.py:205
  20.8 0.0 collective-permute-start.3
  20.8 0.0 collective-permute-done.6.rest_1_.rest_0_
  20.8 1.9 %block_product.13.rest_1_ = bf16[512,256]{1,0:T(8,128)(2,1)S(1)} custom-call(s32[1]{0:T(128)} %bitcast.6.first_ref, bf16[512,2048]{1,0:T(8,128)(2,1)S(1)} %copy-done, bf16[2048,4096]{1,0:T(8,128)(2,1)} %weight_ref.23, s32[24]{0:T(128)S(1)} %get-tuple-element.16.rest_0_.start_ref, bf16[512,256]{1,0:T(8,128)(2,1)S(1)} %collective-permute-done.6.rest_1_.rest_0_), custom_call_target="tpu_custom_call" | custom-call | flops 1000 | bytes 1000 | tf_op jit(solution)/shard_map/block_product/pallas_call | solution.py:41
  22.7 1.2 %collective-permute-start.8 = (bf16[512,256]{1,0:T(8,128)(2,1)S(1)}, bf16[512,256]{1,0:T(8,128)(2,1)S(1)}, u32[]{:S(2)}, u32[]{:S(2)}) collective-permute-start(bf16[512,256]{1,0:T(8,128)(2,1)S(1)} %block_product.13.rest_1_), channel_id=1, source_target_pairs={{0,1},{1,2},{2,3},{3,0},{4,7},{5,4},{6,5},{7,6},{8,9},{9,10},{10,1... | collective-permute-start | bytes 786440 | tf_op jit(solution)/shard_map/ppermute | solution.py:355
  23.9 1.9 %block_product.14.rest_0_ = bf16[512,256]{1,0:T(8,128)(2,1)S(1)} custom-call(s32[1]{0:T(128)} %bitcast.5.first_ref, bf16[512,2048]{1,0:T(8,128)(2,1)S(1)} %copy-done, bf16[2048,4096]{1,0:T(8,128)(2,1)} %weight_ref.23, bf16[512,256]{1,0:T(8,128)(2,1)S(1)} %collective-permute-done.6.rest_1_.rest_0_, bf16[512,256]{1,0:T(8,128)(2,1)S(1)} %block_product.13.rest_1_), custom_call_target="tpu_custom_call" | custom-call | flops 1000 | bytes 1000 | tf_op jit(solution)/shard_map/block_product/pallas_call | solution.py:41
  25.8 0.3 collective-permute-start.7
  26.1 1.9 %block_product.15.rest_1_.rest_2_ = bf16[512,256]{1,0:T(8,128)(2,1)S(1)} custom-call(s32[1]{0:T(128)} %bitcast.10.first_ref, bf16[512,2048]{1,0:T(8,128)(2,1)S(1)} %copy-done, bf16[2048,4096]{1,0:T(8,128)(2,1)} %weight_ref.23, bf16[512,256]{1,0:T(8,128)(2,1)S(1)} %block_product.14.rest_0_), custom_call_target="tpu_custom_call" | custom-call | flops 20000000000 | bytes 1000 | tf_op jit(solution)/shard_map/block_product/pallas_call | solution.py:41
  28.1 0.0 collective-permute-done.9.rest_0_
  28.1 2.8 %block_product.16.rest_0_ = bf16[512,512]{1,0:T(8,128)(2,1)S(1)} custom-call(s32[1]{0:T(128)} %bitcast.9.first_ref, bf16[512,2048]{1,0:T(8,128)(2,1)S(1)} %copy-done, bf16[2048,4096]{1,0:T(8,128)(2,1)} %weight_ref.23, bf16[512,512]{1,0:T(8,128)(2,1)} %collective-permute-done.9.rest_0_, bf16[512,256]{1,0:T(8,128)(2,1)S(1)} %block_product.15.rest_1_.rest_2_), custom_call_target="tpu_custom_call" | custom-call | flops 1000 | bytes 1000 | tf_op jit(solution)/shard_map/block_product/pallas_call | solution.py:41
  30.9 3.6 %collective-permute-start.11 = (bf16[512,512]{1,0:T(8,128)(2,1)S(1)}, bf16[512,512]{1,0:T(8,128)(2,1)S(1)}, u32[]{:S(2)}, u32[]{:S(2)}) collective-permute-start(bf16[512,512]{1,0:T(8,128)(2,1)S(1)} %block_product.16.rest_0_), channel_id=1, source_target_pairs={{0,3},{1,0},{2,1},{3,2},{4,5},{5,6},{6,7},{7,4},{8,11},{9,8},{10,9... | collective-permute-start | bytes 1572872 | tf_op jit(solution)/shard_map/ppermute | solution.py:355
  34.5 2.7 %block_product.17.rest_1_ = bf16[512,512]{1,0:T(8,128)(2,1)S(1)} custom-call(s32[1]{0:T(128)} %bitcast.8.first_ref, bf16[512,2048]{1,0:T(8,128)(2,1)S(1)} %copy-done, bf16[2048,4096]{1,0:T(8,128)(2,1)} %weight_ref.23, bf16[512,512]{1,0:T(8,128)(2,1)S(1)} %block_product.16.rest_0_), custom_call_target="tpu_custom_call" | custom-call | flops 1000 | bytes 1000 | tf_op jit(solution)/shard_map/block_product/pallas_call | solution.py:41
  37.2 0.0 collective-permute-done.8.rest_0_
  37.2 1.9 %block_product.18.rest_1_ = bf16[512,256]{1,0:T(8,128)(2,1)S(1)} custom-call(s32[1]{0:T(128)} %bitcast.7.first_ref, bf16[512,2048]{1,0:T(8,128)(2,1)S(1)} %copy-done, bf16[2048,4096]{1,0:T(8,128)(2,1)} %weight_ref.23, bf16[512,256]{1,0:T(8,128)(2,1)S(1)} %collective-permute-done.8.rest_0_, bf16[512,512]{1,0:T(8,128)(2,1)S(1)} %block_product.17.rest_1_), custom_call_target="tpu_custom_call" | custom-call | flops 1000 | bytes 1000 | tf_op jit(solution)/shard_map/block_product/pallas_call | solution.py:41
  39.2 0.1 collective-permute-start.13
  39.2 7.7 %collective-permute-done.4.rest_2_.rest_5_ = bf16[2,6,16,3072]{3,2,1,0:T(8,128)(2,1)S(1)} collective-permute-done((bf16[2,6,16,3072]{3,2,1,0:T(8,128)(2,1)S(1)}, bf16[2,6,16,3072]{3,2,1,0:T(8,128)(2,1)S(1)}, u32[]{:S(2)}, u32[]{:S(2)}) %collective-permute-start.4) | collective-permute-done | bytes 1179680 | tf_op jit(solution)/shard_map/ppermute | solution.py:205
  46.9 0.0 collective-permute-start.5
  46.9 0.0 collective-permute-done.7.rest_0_
  46.9 1.9 %block_product.19.rest_4_ = bf16[512,256]{1,0:T(8,128)(2,1)S(1)} custom-call(s32[1]{0:T(128)} %bitcast.4.first_ref, bf16[512,2048]{1,0:T(8,128)(2,1)S(1)} %copy-done, bf16[2048,4096]{1,0:T(8,128)(2,1)} %weight_ref.23, bf16[512,256]{1,0:T(8,128)(2,1)S(1)} %collective-permute-done.7.rest_0_, bf16[512,256]{1,0:T(8,128)(2,1)S(1)} %block_product.18.rest_1_), custom_call_target="tpu_custom_call" | custom-call | flops 20000000000 | bytes 1000 | tf_op jit(solution)/shard_map/block_product/pallas_call | solution.py:41
  48.8 1.3 %collective-permute-start.16 = (bf16[512,256]{1,0:T(8,128)(2,1)S(1)}, bf16[512,256]{1,0:T(8,128)(2,1)S(1)}, u32[]{:S(2)}, u32[]{:S(2)}) collective-permute-start(bf16[512,256]{1,0:T(8,128)(2,1)S(1)} %block_product.19.rest_4_), channel_id=1, source_target_pairs={{0,1},{1,2},{2,3},{3,0},{4,7},{5,4},{6,5},{7,6},{8,9},{9,10},{10,1... | collective-permute-start | bytes 786440 | tf_op jit(solution)/shard_map/ppermute | solution.py:355
  50.2 0.0 collective-permute-done.3.rest_1_.rest_4_
  50.2 0.0 collective-permute-done.5.rest_3_.rest_6_
  50.2 1.6 %low_sums.1.rest_1_.a_ref = f32[16,512]{1,0:T(8,128)S(1)} custom-call(s32[24]{0:T(128)S(1)} %get-tuple-element.16.rest_0_.start_ref, s32[24]{0:T(128)S(1)} %get-tuple-element.17.end_ref, bf16[512,2048]{1,0:T(8,128)(2,1)S(1)} %copy-done, bf16[2,6,16,3072]{3,2,1,0:T(8,128)(2,1)S(1)} %get-tuple-element.18.rest_0_.rest_3_, ...), custom_call_target="tpu_custom_call" | custom-call | flops 1000 | bytes 1000 | tf_op jit(solution)/shard_map/low_sums/pallas_call | solution.py:236
  51.7 0.9 %collective-permute-start.10 = (f32[16,512]{1,0:T(8,128)S(1)}, f32[16,512]{1,0:T(8,128)S(1)}, u32[]{:S(2)}, u32[]{:S(2)}) collective-permute-start(f32[16,512]{1,0:T(8,128)S(1)} %low_sums.1.rest_1_.a_ref), channel_id=1, source_target_pairs={{0,1},{1,0},{2,3},{3,2},{4,5},{5,4},{6,7},{7,6},{8,9},{9,8},{10,11... | collective-permute-start | bytes 98312 | tf_op jit(solution)/shard_map/ppermute | solution.py:389
  52.6 4.2 %collective-permute-done.11.rest_0_ = bf16[512,512]{1,0:T(8,128)(2,1)S(1)} collective-permute-done((bf16[512,512]{1,0:T(8,128)(2,1)S(1)}, bf16[512,512]{1,0:T(8,128)(2,1)S(1)}, u32[]{:S(2)}, u32[]{:S(2)}) %collective-permute-start.11) | collective-permute-done | bytes 524320 | tf_op jit(solution)/shard_map/ppermute | solution.py:355
  56.9 2.7 %block_product.20.rest_0_ = bf16[512,512]{1,0:T(8,128)(2,1)S(1)} custom-call(s32[1]{0:T(128)} %bitcast.11.first_ref, bf16[512,2048]{1,0:T(8,128)(2,1)S(1)} %copy-done, bf16[2048,4096]{1,0:T(8,128)(2,1)} %weight_ref.23, bf16[512,512]{1,0:T(8,128)(2,1)S(1)} %collective-permute-done.11.rest_0_, f32[16,512]{1,0:T(8,128)S(1)} %low_sums.1.rest_1_.a_ref), custom_call_target="tpu_custom_call" | custom-call | flops 20000000000 | bytes 1000 | tf_op jit(solution)/shard_map/block_product/pallas_call | solution.py:41
  59.6 0.1 collective-permute-start.15
  59.6 0.0 collective-permute-done.10.b_ref
  59.7 3.5 %collective-permute-start.12 = (f32[16,512]{1,0:T(8,128)S(1)}, f32[16,512]{1,0:T(8,128)S(1)}, u32[]{:S(2)}, u32[]{:S(2)}) collective-permute-start(f32[16,512]{1,0:T(8,128)S(1)} %sum_after.1.rest_1_.low_ref), channel_id=1, source_target_pairs={{0,2},{1,3},{2,0},{3,1},{4,6},{5,7},{6,4},{7,5},{8,10},{9,11},{10,... | collective-permute-start | bytes 98312 | tf_op jit(solution)/shard_map/ppermute | solution.py:394
  63.2 0.0 collective-permute-done.13.rest_0_
  63.2 1.9 %block_product.21.rest_7_ = bf16[512,256]{1,0:T(8,128)(2,1)S(1)} custom-call(s32[1]{0:T(128)} %bitcast.12.first_ref, bf16[512,2048]{1,0:T(8,128)(2,1)S(1)} %copy-done, bf16[2048,4096]{1,0:T(8,128)(2,1)} %weight_ref.23, bf16[512,256]{1,0:T(8,128)(2,1)S(1)} %collective-permute-done.13.rest_0_, f32[16,512]{1,0:T(8,128)S(1)} %sum_after.1.rest_1_.low_ref), custom_call_target="tpu_custom_call" | custom-call | flops 20000000000 | bytes 1000 | tf_op jit(solution)/shard_map/block_product/pallas_call | solution.py:41
  65.1 1.3 %collective-permute-start.14 = (bf16[512,256]{1,0:T(8,128)(2,1)S(1)}, bf16[512,256]{1,0:T(8,128)(2,1)S(1)}, u32[]{:S(2)}, u32[]{:S(2)}) collective-permute-start(bf16[512,256]{1,0:T(8,128)(2,1)S(1)} %block_product.21.rest_7_), channel_id=1, source_target_pairs={{0,1},{1,2},{2,3},{3,0},{4,7},{5,4},{6,5},{7,6},{8,9},{9,10},{10,1... | collective-permute-start | bytes 786440 | tf_op jit(solution)/shard_map/ppermute | solution.py:355
  66.4 14.6 %collective-permute-done.12.came_ref = f32[16,512]{1,0:T(8,128)S(1)} collective-permute-done((f32[16,512]{1,0:T(8,128)S(1)}, f32[16,512]{1,0:T(8,128)S(1)}, u32[]{:S(2)}, u32[]{:S(2)}) %collective-permute-start.12) | collective-permute-done | bytes 32800 | tf_op jit(solution)/shard_map/ppermute | solution.py:394
  81.0 1.3 %adapter_term.1 = (f32[512,256]{1,0:T(8,128)S(1)}, f32[512,512]{1,0:T(8,128)S(1)}, f32[512,256]{1,0:T(8,128)S(1)}) custom-call(s32[24]{0:T(128)S(1)} %get-tuple-element.16.rest_0_.start_ref, s32[24]{0:T(128)S(1)} %get-tuple-element.17.end_ref, f32[16,512]{1,0:T(8,128)S(1)} %sum_after.1.rest_1_.low_ref, f32[16,512]{1,0:T(8,128)S(1)} %collective-permute-done.12.came_ref, ...), custom_call_target="tpu_custom_call" | custom-call | flops 1000 | bytes 1000 | tf_op jit(solution)/shard_map/adapter_term/pallas_call | solution.py:279
  82.3 0.0 collective-permute-done.16.rest_0_
  82.3 1.4 %finish.3.rest_1_ = bf16[512,1024]{1,0:T(8,128)(2,1)} custom-call(f32[512,256]{1,0:T(8,128)S(1)} %get-tuple-element.22.term_ref, bf16[512,256]{1,0:T(8,128)(2,1)S(1)} %collective-permute-done.16.rest_0_), custom_call_target="tpu_custom_call" | custom-call | flops 20000000000 | bytes 1000 | tf_op jit(solution)/shard_map/finish/pallas_call | solution.py:323
  83.7 0.0 collective-permute-done.15.rest_0_
  83.7 1.4 %finish.4.rest_1_ = bf16[512,1024]{1,0:T(8,128)(2,1)} custom-call(f32[512,512]{1,0:T(8,128)S(1)} %get-tuple-element.21.term_ref, bf16[512,512]{1,0:T(8,128)(2,1)S(1)} %collective-permute-done.15.rest_0_, bf16[512,1024]{1,0:T(8,128)(2,1)} %finish.3.rest_1_), custom_call_target="tpu_custom_call", output_to_operand_aliasing={{}: (2, {})} | custom-call | flops 1000 | bytes 1000 | tf_op jit(solution)/shard_map/finish/pallas_call | solution.py:323
  85.1 0.0 collective-permute-done.14.rest_0_
  85.1 1.3 %finish.5 = bf16[512,1024]{1,0:T(8,128)(2,1)} custom-call(f32[512,256]{1,0:T(8,128)S(1)} %get-tuple-element.20.term_ref, bf16[512,256]{1,0:T(8,128)(2,1)S(1)} %collective-permute-done.14.rest_0_, bf16[512,1024]{1,0:T(8,128)(2,1)} %finish.4.rest_1_), custom_call_target="tpu_custom_call", output_to_operand_aliasing={{}: (2, {})} | custom-call | flops 1000 | bytes 1000 | tf_op jit(solution)/shard_map/finish/pallas_call | solution.py:323
  (1 shorter events, 0.0 us)
Async XLA Ops:
  0.0 5.9 %copy-start = (bf16[512,2048]{1,0:T(8,128)(2,1)S(1)}, bf16[512,2048]{1,0:T(8,128)(2,1)}, u32[]{:S(2)}) copy-start(bf16[512,2048]{1,0:T(8,128)(2,1)} %rows_ref.25) | copy-start | bytes 6291460
  0.0 5.9 %copy-start.2 = (s32[1,12]{1,0:T(1,128)S(1)}, s32[1,12]{1,0:T(1,128)}, u32[]{:S(2)}) copy-start(s32[1,12]{1,0:T(1,128)} %rest_0_.1) | copy-start | bytes 148
  2.8 18.0 %collective-permute-start.6 = (bf16[512,256]{1,0:T(8,128)(2,1)S(1)}, bf16[512,256]{1,0:T(8,128)(2,1)S(1)}, u32[]{:S(2)}, u32[]{:S(2)}) collective-permute-start(bf16[512,256]{1,0:T(8,128)(2,1)S(1)} %first_product.1.rest_1_), channel_id=1, source_target_pairs={{0,1},{1,2},{2,3},{3,0},{4,7},{5,4},{6,5},{7,6},{8,9},{9,10},{10,1... | collective-permute-start | bytes 786440 | tf_op jit(solution)/shard_map/ppermute | solution.py:355
  9.2 6.3 %collective-permute-start.2 = (s32[1,12]{1,0:T(1,128)S(1)}, s32[1,12]{1,0:T(1,128)S(1)}, u32[]{:S(2)}, u32[]{:S(2)}) collective-permute-start(s32[1,12]{1,0:T(1,128)S(1)} %get-tuple-element.14.rest_0_), channel_id=1, source_target_pairs={{0,12},{4,8},{8,4},{12,0},{1,13},{5,9},{9,5},{13,1},{2,14},{6,10},... | collective-permute-start | bytes 152 | tf_op jit(solution)/shard_map/ppermute | solution.py:372
  12.0 3.5 %collective-permute-start.1 = (s32[1,12]{1,0:T(1,128)S(1)}, s32[1,12]{1,0:T(1,128)S(1)}, u32[]{:S(2)}, u32[]{:S(2)}) collective-permute-start(s32[1,12]{1,0:T(1,128)S(1)} %get-tuple-element.14.rest_0_), channel_id=1, source_target_pairs={{0,8},{4,12},{8,0},{12,4},{1,9},{5,13},{9,1},{13,5},{2,10},{6,14},... | collective-permute-start | bytes 152 | tf_op jit(solution)/shard_map/ppermute | solution.py:372
  12.5 3.0 %collective-permute-start = (s32[1,12]{1,0:T(1,128)S(1)}, s32[1,12]{1,0:T(1,128)S(1)}, u32[]{:S(2)}, u32[]{:S(2)}) collective-permute-start(s32[1,12]{1,0:T(1,128)S(1)} %get-tuple-element.14.rest_0_), channel_id=1, source_target_pairs={{0,4},{4,0},{8,12},{12,8},{1,5},{5,1},{9,13},{13,9},{2,6},{6,2},{1... | collective-permute-start | bytes 152 | tf_op jit(solution)/shard_map/ppermute | solution.py:372
  12.5 15.6 %collective-permute-start.9 = (bf16[512,512]{1,0:T(8,128)(2,1)S(1)}, bf16[512,512]{1,0:T(8,128)(2,1)}, u32[]{:S(2)}, u32[]{:S(2)}) collective-permute-start(bf16[512,512]{1,0:T(8,128)(2,1)S(1)} %get-tuple-element.15.rest_0_), channel_id=1, source_target_pairs={{0,3},{1,0},{2,1},{3,2},{4,5},{5,6},{6,7},{7,4},{8,11},{9,8},{10,9... | collective-permute-start | bytes 1572872 | tf_op jit(solution)/shard_map/ppermute | solution.py:355
  13.3 2.3 %copy-start.1 = (s32[512]{0:T(512)S(1)}, s32[512]{0:T(512)}, u32[]{:S(2)}) copy-start(s32[512]{0:T(512)} %table_ref.1) | copy-start | bytes 6148
  13.3 2.3 %copy-start.3 = (s32[1,12]{1,0:T(1,128)S(1)}, s32[1,12]{1,0:T(1,128)}, u32[]{:S(2)}) copy-start(s32[1,12]{1,0:T(1,128)} %lens_ref.1) | copy-start | bytes 148
  19.4 27.5 %collective-permute-start.4 = (bf16[2,6,16,3072]{3,2,1,0:T(8,128)(2,1)S(1)}, bf16[2,6,16,3072]{3,2,1,0:T(8,128)(2,1)S(1)}, u32[]{:S(2)}, u32[]{:S(2)}) collective-permute-start(bf16[2,6,16,3072]{3,2,1,0:T(8,128)(2,1)S(1)} %get-tuple-element.19), channel_id=1, source_target_pairs={{0,8},{4,12},{8,0},{12,4},{1,9},{5,13},{9,1},{13,5},{2,10},{6,14},... | collective-permute-start | bytes 3538952 | tf_op jit(solution)/shard_map/ppermute | solution.py:205
  20.8 29.4 %collective-permute-start.3 = (bf16[2,6,16,3072]{3,2,1,0:T(8,128)(2,1)S(1)}, bf16[2,6,16,3072]{3,2,1,0:T(8,128)(2,1)S(1)}, u32[]{:S(2)}, u32[]{:S(2)}) collective-permute-start(bf16[2,6,16,3072]{3,2,1,0:T(8,128)(2,1)S(1)} %get-tuple-element.18.rest_0_.rest_3_), channel_id=1, source_target_pairs={{0,4},{4,0},{8,12},{12,8},{1,5},{5,1},{9,13},{13,9},{2,6},{6,2},{1... | collective-permute-start | bytes 3538952 | tf_op jit(solution)/shard_map/ppermute | solution.py:206
  22.7 14.5 %collective-permute-start.8 = (bf16[512,256]{1,0:T(8,128)(2,1)S(1)}, bf16[512,256]{1,0:T(8,128)(2,1)S(1)}, u32[]{:S(2)}, u32[]{:S(2)}) collective-permute-start(bf16[512,256]{1,0:T(8,128)(2,1)S(1)} %block_product.13.rest_1_), channel_id=1, source_target_pairs={{0,1},{1,2},{2,3},{3,0},{4,7},{5,4},{6,5},{7,6},{8,9},{9,10},{10,1... | collective-permute-start | bytes 786440 | tf_op jit(solution)/shard_map/ppermute | solution.py:355
  25.8 21.1 %collective-permute-start.7 = (bf16[512,256]{1,0:T(8,128)(2,1)S(1)}, bf16[512,256]{1,0:T(8,128)(2,1)S(1)}, u32[]{:S(2)}, u32[]{:S(2)}) collective-permute-start(bf16[512,256]{1,0:T(8,128)(2,1)S(1)} %block_product.14.rest_0_), channel_id=1, source_target_pairs={{0,1},{1,2},{2,3},{3,0},{4,7},{5,4},{6,5},{7,6},{8,9},{9,10},{10,1... | collective-permute-start | bytes 786440 | tf_op jit(solution)/shard_map/ppermute | solution.py:355
  30.9 26.0 %collective-permute-start.11 = (bf16[512,512]{1,0:T(8,128)(2,1)S(1)}, bf16[512,512]{1,0:T(8,128)(2,1)S(1)}, u32[]{:S(2)}, u32[]{:S(2)}) collective-permute-start(bf16[512,512]{1,0:T(8,128)(2,1)S(1)} %block_product.16.rest_0_), channel_id=1, source_target_pairs={{0,3},{1,0},{2,1},{3,2},{4,5},{5,6},{6,7},{7,4},{8,11},{9,8},{10,9... | collective-permute-start | bytes 1572872 | tf_op jit(solution)/shard_map/ppermute | solution.py:355
  39.2 24.0 %collective-permute-start.13 = (bf16[512,256]{1,0:T(8,128)(2,1)S(1)}, bf16[512,256]{1,0:T(8,128)(2,1)S(1)}, u32[]{:S(2)}, u32[]{:S(2)}) collective-permute-start(bf16[512,256]{1,0:T(8,128)(2,1)S(1)} %block_product.18.rest_1_), channel_id=1, source_target_pairs={{0,1},{1,2},{2,3},{3,0},{4,7},{5,4},{6,5},{7,6},{8,9},{9,10},{10,1... | collective-permute-start | bytes 786440 | tf_op jit(solution)/shard_map/ppermute | solution.py:355
  46.9 3.3 %collective-permute-start.5 = (bf16[2,6,16,3072]{3,2,1,0:T(8,128)(2,1)S(1)}, bf16[2,6,16,3072]{3,2,1,0:T(8,128)(2,1)S(1)}, u32[]{:S(2)}, u32[]{:S(2)}) collective-permute-start(bf16[2,6,16,3072]{3,2,1,0:T(8,128)(2,1)S(1)} %collective-permute-done.4.rest_2_.rest_5_), channel_id=1, source_target_pairs={{0,4},{4,0},{8,12},{12,8},{1,5},{5,1},{9,13},{13,9},{2,6},{6,2},{1... | collective-permute-start | bytes 3538952 | tf_op jit(solution)/shard_map/ppermute | solution.py:206
  48.8 33.4 %collective-permute-start.16 = (bf16[512,256]{1,0:T(8,128)(2,1)S(1)}, bf16[512,256]{1,0:T(8,128)(2,1)S(1)}, u32[]{:S(2)}, u32[]{:S(2)}) collective-permute-start(bf16[512,256]{1,0:T(8,128)(2,1)S(1)} %block_product.19.rest_4_), channel_id=1, source_target_pairs={{0,1},{1,2},{2,3},{3,0},{4,7},{5,4},{6,5},{7,6},{8,9},{9,10},{10,1... | collective-permute-start | bytes 786440 | tf_op jit(solution)/shard_map/ppermute | solution.py:355
  51.7 7.9 %collective-permute-start.10 = (f32[16,512]{1,0:T(8,128)S(1)}, f32[16,512]{1,0:T(8,128)S(1)}, u32[]{:S(2)}, u32[]{:S(2)}) collective-permute-start(f32[16,512]{1,0:T(8,128)S(1)} %low_sums.1.rest_1_.a_ref), channel_id=1, source_target_pairs={{0,1},{1,0},{2,3},{3,2},{4,5},{5,4},{6,7},{7,6},{8,9},{9,8},{10,11... | collective-permute-start | bytes 98312 | tf_op jit(solution)/shard_map/ppermute | solution.py:389
  59.6 24.1 %collective-permute-start.15 = (bf16[512,512]{1,0:T(8,128)(2,1)S(1)}, bf16[512,512]{1,0:T(8,128)(2,1)S(1)}, u32[]{:S(2)}, u32[]{:S(2)}) collective-permute-start(bf16[512,512]{1,0:T(8,128)(2,1)S(1)} %block_product.20.rest_0_), channel_id=1, source_target_pairs={{0,3},{1,0},{2,1},{3,2},{4,5},{5,6},{6,7},{7,4},{8,11},{9,8},{10,9... | collective-permute-start | bytes 1572872 | tf_op jit(solution)/shard_map/ppermute | solution.py:355
  59.7 21.3 %collective-permute-start.12 = (f32[16,512]{1,0:T(8,128)S(1)}, f32[16,512]{1,0:T(8,128)S(1)}, u32[]{:S(2)}, u32[]{:S(2)}) collective-permute-start(f32[16,512]{1,0:T(8,128)S(1)} %sum_after.1.rest_1_.low_ref), channel_id=1, source_target_pairs={{0,2},{1,3},{2,0},{3,1},{4,6},{5,7},{6,4},{7,5},{8,10},{9,11},{10,... | collective-permute-start | bytes 98312 | tf_op jit(solution)/shard_map/ppermute | solution.py:394
  65.1 20.0 %collective-permute-start.14 = (bf16[512,256]{1,0:T(8,128)(2,1)S(1)}, bf16[512,256]{1,0:T(8,128)(2,1)S(1)}, u32[]{:S(2)}, u32[]{:S(2)}) collective-permute-start(bf16[512,256]{1,0:T(8,128)(2,1)S(1)} %block_product.21.rest_7_), channel_id=1, source_target_pairs={{0,1},{1,2},{2,3},{3,0},{4,7},{5,4},{6,5},{7,6},{8,9},{9,10},{10,1... | collective-permute-start | bytes 786440 | tf_op jit(solution)/shard_map/ppermute | solution.py:355

commit v18 on v17

--- a/solution.py
+++ b/solution.py
@@ -226,7 +226,7 @@
     for q in range(peers * CAP):
         member = jnp.logical_and(place >= start_ref[q], place < end_ref[q])
         total = jnp.where(member, part[q * rank : (q + 1) * rank], total)
-    out_ref[...] = total
+    out_ref[...] = total.astype(BF16)
 
 
 def low_sums(starts, ends, rows, packs, rank, after):
@@ -240,20 +240,23 @@
         + [pack_spec(p, 0, depth) for p in packs]
         + [pl.BlockSpec(memory_space=pl.ANY)] * len(after),
         out_specs=vmem,
-        out_shape=jax.ShapeDtypeStruct((rank, row_total), F32),
+        out_shape=jax.ShapeDtypeStruct((rank, row_total), BF16),
         compiler_params=pltpu.CompilerParams(vmem_limit_bytes=VMEM_LIMIT),
         cost_estimate=SMALL,
         name="low_sums",
     )(starts, ends, rows, *[array for array, _ in packs], *after)
 
 
-def term_kernel(offsets, peers, start_ref, end_ref, low_ref, came_ref, *rest):
+def term_kernel(offsets, lows, peers, start_ref, end_ref, *rest):
     pieces = len(offsets)
+    low_refs, rest = rest[:lows], rest[lows:]
     own_refs, rest = rest[:pieces], rest[pieces:]
     up_refs, out_refs = rest[:peers], rest[-pieces:]
-    rank, row_total = low_ref.shape
+    rank, row_total = low_refs[0].shape
     cols = sum(ref.shape[1] for ref in out_refs)
-    low = low_ref[...] + came_ref[...]
+    low = low_refs[0][...].astype(F32)
+    for ref in low_refs[1:]:
+        low = low + ref[...].astype(F32)
     low = low.astype(BF16).astype(F32)
     place = lax.broadcasted_iota(jnp.int32, (rank, row_total), 1)
     spread = []
@@ -270,17 +273,17 @@
         out_refs[piece][...] = own_refs[piece][...].astype(F32) + term
 
 
-def adapter_term(starts, ends, low, came, owns, packs, offsets, after):
+def adapter_term(starts, ends, lows, owns, packs, offsets, after):
     row_total = owns[0].shape[0]
     cols = sum(own.shape[1] for own in owns)
     smem = pl.BlockSpec(memory_space=pltpu.SMEM)
     vmem = pl.BlockSpec(memory_space=pltpu.VMEM)
     depth = packs[0][0].shape[3] - cols
     return pl.pallas_call(
-        functools.partial(term_kernel, offsets, len(packs)),
+        functools.partial(term_kernel, offsets, len(lows), len(packs)),
         grid=(1,),
         in_specs=[smem, smem]
-        + [vmem] * (2 + len(owns))
+        + [vmem] * (len(lows) + len(owns))
         + [pack_spec(p, depth, cols) for p in packs]
         + [pl.BlockSpec(memory_space=pl.ANY)] * len(after),
         out_specs=[vmem] * len(owns),
@@ -288,24 +291,7 @@
         compiler_params=pltpu.CompilerParams(vmem_limit_bytes=VMEM_LIMIT),
         cost_estimate=SMALL,
         name="adapter_term",
-    )(starts, ends, low, came, *owns, *[array for array, _ in packs], *after)
-
-
-def sum_kernel(a_ref, b_ref, *rest):
-    rest[-1][...] = a_ref[...] + b_ref[...]
-
-
-def sum_after(a, b, after):
-    vmem = pl.BlockSpec(memory_space=pltpu.VMEM)
-    return pl.pallas_call(
-        sum_kernel,
-        in_specs=[vmem, vmem] + [pl.BlockSpec(memory_space=pl.ANY)] * len(after),
-        out_specs=vmem,
-        out_shape=jax.ShapeDtypeStruct(a.shape, a.dtype),
-        compiler_params=pltpu.CompilerParams(vmem_limit_bytes=VMEM_LIMIT),
-        cost_estimate=SMALL,
-        name="sum_after",
-    )(a, b, *after)
+    )(starts, ends, *lows, *owns, *[array for array, _ in packs], *after)
 
 
 def finish_kernel(addends, term_ref, *rest):
@@ -385,15 +371,12 @@
                 last = owns[2 - piece] = partial(0, 2 - piece, after=[last], cost=LARGE if piece == 0 else SMALL)
             if step == steps - 1 and piece == 0:
                 last = low = low_sums(starts, ends, rows, packs, rank, [last])
-                bit = 1
-                came = lax.ppermute(low, "tp", [(i, i ^ bit) for i in range(tp_total)])
-            if step == steps - 1 and piece == 1:
-                while 2 * bit < tp_total:
-                    last = low = sum_after(low, came, [last])
-                    bit *= 2
-                    came = lax.ppermute(low, "tp", [(i, i ^ bit) for i in range(tp_total)])
-
-    terms = adapter_term(starts, ends, low, came, owns, packs, offsets, [last])
+                lows = [low]
+                for x in range(1, tp_total):
+                    pairs = [(i, i ^ x) for i in range(tp_total)]
+                    lows.append(lax.ppermute(low, "tp", pairs))
+
+    terms = adapter_term(starts, ends, lows, owns, packs, offsets, [last])
     result = None
     for piece in pieces:
         cost = LARGE if piece == 0 else SMALL

time: 86.9 us -> 84 us (0.967)
  waiting for transfers between devices: 26.6 us -> 24.5 us
    ppermute x2 -> x3, waiting for transfers between devices: 14.6 us -> 0.01 us  [local(): lows.append(lax.ppermute(low, 'tp', pairs))]
    ppermute x9, waiting for transfers between devices: 4.26 us -> 16.1 us  [move(): return lax.ppermute(value, ('req', 'tp'), pairs)]
    ppermute x2 -> x3, starting transfers between devices: 4.4 us -> 3.08 us  [local(): lows.append(lax.ppermute(low, 'tp', pairs))]
  transfers between devices with their start and end apart: 17 -> 18, of which waited for: 3 -> 3; matrix products, arithmetic and copies ran while one was open for 0% -> 0% of each run, Pallas kernels for 40% -> 41%
where the time goes in v18:
time: 84 us; the launch traced here: 83.3 us
  Pallas kernels  38.3 us (46%)
  waiting for transfers between devices  24.5 us (29%)
  starting transfers between devices  20.1 us (24%)
    pallas_call x11, Pallas kernels, block_product(): pl.pallas_call(functools.partial(product_kernel, len(addends), with_ids),...  25.1 us
    ppermute x9, waiting for transfers between devices, move(): return lax.ppermute(value, ('req', 'tp'), pairs)  16.1 us
    ppermute x9, starting transfers between devices, move(): return lax.ppermute(value, ('req', 'tp'), pairs)  12.5 us
    ppermute x1, waiting for transfers between devices, exchange(): pair = lax.ppermute(pair, 'req', [(i, i ^ 2 * y) for i in range(peers)])  8.3 us
    pallas_call x3, Pallas kernels, finish(): pl.pallas_call(functools.partial(finish_kernel, len(arrivals)), grid=(row...  4.1 us
    pallas_call x1, Pallas kernels, pick_adapters(): pl.pallas_call(functools.partial(pick_kernel, peers, len(after)), in_spec...  3.48 us
    ppermute x3, starting transfers between devices, local(): lax.ppermute(ids, 'req', [(i, i ^ x) for i in range(req_total)])  3.28 us
    ppermute x3, starting transfers between devices, local(): lows.append(lax.ppermute(low, 'tp', pairs))  3.08 us
  transfers between devices with their start and end apart: 18, of which 3 were waited for; matrix products, arithmetic and copies ran while one was open for 0% of the time, Pallas kernels for 41%

profile of v18, /device:TPU:0, one launch (start us, length us, event | category | flops | bytes accessed | tf_op | source)
XLA Modules:
  0.0 83.3 jit_solution(12460050582024071008)
XLA Ops:
  0.0 0.0 copy-start
  0.0 0.0 copy-start.2
  0.0 2.8 %first_product.1.rest_1_ = bf16[512,256]{1,0:T(8,128)(2,1)S(1)} custom-call(s32[1]{0:T(128)} %bitcast.2.first_ref, bf16[512,2048]{1,0:T(8,128)(2,1)} %rows_ref.25, bf16[2048,4096]{1,0:T(8,128)(2,1)} %weight_ref.23), custom_call_target="tpu_custom_call" | custom-call | flops 1000 | bytes 1000 | tf_op jit(solution)/shard_map/first_product/pallas_call | solution.py:94
  2.8 3.1 %collective-permute-start.6 = (bf16[512,256]{1,0:T(8,128)(2,1)S(1)}, bf16[512,256]{1,0:T(8,128)(2,1)S(1)}, u32[]{:S(2)}, u32[]{:S(2)}) collective-permute-start(bf16[512,256]{1,0:T(8,128)(2,1)S(1)} %first_product.1.rest_1_), channel_id=1, source_target_pairs={{0,1},{1,2},{2,3},{3,0},{4,7},{5,4},{6,5},{7,6},{8,9},{9,10},{10,1... | collective-permute-start | bytes 786440 | tf_op jit(solution)/shard_map/ppermute | solution.py:341
  5.9 0.0 copy-done
  5.9 0.0 copy-done.2
  5.9 3.3 %block_product.11 = (bf16[512,512]{1,0:T(8,128)(2,1)S(1)}, s32[1,12]{1,0:T(1,128)S(1)}) custom-call(s32[1]{0:T(128)} %bitcast.1.first_ref, bf16[512,2048]{1,0:T(8,128)(2,1)S(1)} %copy-done, bf16[2048,4096]{1,0:T(8,128)(2,1)} %weight_ref.23, s32[1,12]{1,0:T(1,128)S(1)} %copy-done.2, bf16[512,256]{1,0:T(8,128)(2,1)S(1)} %first_product.1.rest_1_), custom_call_target="tpu_custom_call" | custom-call | flops 1000 | bytes 1000 | tf_op jit(solution)/shard_map/block_product/pallas_call | solution.py:41
  9.2 2.8 %collective-permute-start.2 = (s32[1,12]{1,0:T(1,128)S(1)}, s32[1,12]{1,0:T(1,128)S(1)}, u32[]{:S(2)}, u32[]{:S(2)}) collective-permute-start(s32[1,12]{1,0:T(1,128)S(1)} %get-tuple-element.14.rest_0_), channel_id=1, source_target_pairs={{0,12},{4,8},{8,4},{12,0},{1,13},{5,9},{9,5},{13,1},{2,14},{6,10},... | collective-permute-start | bytes 152 | tf_op jit(solution)/shard_map/ppermute | solution.py:358
  12.0 0.5 collective-permute-start.1
  12.5 0.0 collective-permute-start
  12.5 0.8 collective-permute-start.9
  13.3 0.0 copy-start.1
  13.3 0.0 copy-start.3
  13.3 2.0 %block_product.12.rest_6_.rest_4_ = bf16[512,256]{1,0:T(8,128)(2,1)S(1)} custom-call(s32[1]{0:T(128)} %bitcast.3.first_ref, bf16[512,2048]{1,0:T(8,128)(2,1)S(1)} %copy-done, bf16[2048,4096]{1,0:T(8,128)(2,1)} %weight_ref.23, bf16[512,512]{1,0:T(8,128)(2,1)S(1)} %get-tuple-element.15.rest_0_), custom_call_target="tpu_custom_call" | custom-call | flops 1000 | bytes 1000 | tf_op jit(solution)/shard_map/block_product/pallas_call | solution.py:41
  15.5 0.0 collective-permute-done.2.rest_3_
  15.5 0.0 collective-permute-done.1.rest_2_
  15.5 0.0 collective-permute-done.rest_1_
  15.5 0.0 copy-done.1
  15.5 0.0 copy-done.3
  15.6 3.5 %pick_adapters.1 = (bf16[2,6,16,3072]{3,2,1,0:T(8,128)(2,1)S(1)}, bf16[2,6,16,3072]{3,2,1,0:T(8,128)(2,1)S(1)}, s32[24]{0:T(128)S(1)}, s32[24]{0:T(128)S(1)}) custom-call(s32[1]{0:T(128)} %bitcast.me_ref, s32[512]{0:T(512)S(1)} %copy-done.1, s32[1,12]{1,0:T(1,128)S(1)} %copy-done.3, s32[1,12]{1,0:T(1,128)S(1)} %get-tuple-element.14.rest_0_, ...), custom_call_target="tpu_custom_call" | custom-call | flops 1000 | bytes 1000 | tf_op jit(solution)/shard_map/pick_adapters/pallas_call | solution.py:183
  19.0 1.3 %collective-permute-start.4 = (bf16[2,6,16,3072]{3,2,1,0:T(8,128)(2,1)S(1)}, bf16[2,6,16,3072]{3,2,1,0:T(8,128)(2,1)S(1)}, u32[]{:S(2)}, u32[]{:S(2)}) collective-permute-start(bf16[2,6,16,3072]{3,2,1,0:T(8,128)(2,1)S(1)} %get-tuple-element.19), channel_id=1, source_target_pairs={{0,8},{4,12},{8,0},{12,4},{1,9},{5,13},{9,1},{13,5},{2,10},{6,14},... | collective-permute-start | bytes 3538952 | tf_op jit(solution)/shard_map/ppermute | solution.py:205
  20.3 0.0 collective-permute-start.3
  20.3 0.0 collective-permute-done.6.rest_1_.rest_0_
  20.3 1.9 %block_product.13.rest_1_ = bf16[512,256]{1,0:T(8,128)(2,1)S(1)} custom-call(s32[1]{0:T(128)} %bitcast.6.first_ref, bf16[512,2048]{1,0:T(8,128)(2,1)S(1)} %copy-done, bf16[2048,4096]{1,0:T(8,128)(2,1)} %weight_ref.23, s32[24]{0:T(128)S(1)} %get-tuple-element.16.rest_0_.start_ref, bf16[512,256]{1,0:T(8,128)(2,1)S(1)} %collective-permute-done.6.rest_1_.rest_0_), custom_call_target="tpu_custom_call" | custom-call | flops 1000 | bytes 1000 | tf_op jit(solution)/shard_map/block_product/pallas_call | solution.py:41
  22.3 1.2 %collective-permute-start.8 = (bf16[512,256]{1,0:T(8,128)(2,1)S(1)}, bf16[512,256]{1,0:T(8,128)(2,1)S(1)}, u32[]{:S(2)}, u32[]{:S(2)}) collective-permute-start(bf16[512,256]{1,0:T(8,128)(2,1)S(1)} %block_product.13.rest_1_), channel_id=1, source_target_pairs={{0,1},{1,2},{2,3},{3,0},{4,7},{5,4},{6,5},{7,6},{8,9},{9,10},{10,1... | collective-permute-start | bytes 786440 | tf_op jit(solution)/shard_map/ppermute | solution.py:341
  23.4 1.9 %block_product.14.rest_0_ = bf16[512,256]{1,0:T(8,128)(2,1)S(1)} custom-call(s32[1]{0:T(128)} %bitcast.5.first_ref, bf16[512,2048]{1,0:T(8,128)(2,1)S(1)} %copy-done, bf16[2048,4096]{1,0:T(8,128)(2,1)} %weight_ref.23, bf16[512,256]{1,0:T(8,128)(2,1)S(1)} %collective-permute-done.6.rest_1_.rest_0_, bf16[512,256]{1,0:T(8,128)(2,1)S(1)} %block_product.13.rest_1_), custom_call_target="tpu_custom_call" | custom-call | flops 1000 | bytes 1000 | tf_op jit(solution)/shard_map/block_product/pallas_call | solution.py:41
  25.4 0.3 collective-permute-start.7
  25.7 1.9 %block_product.15.rest_1_.rest_6_ = bf16[512,256]{1,0:T(8,128)(2,1)S(1)} custom-call(s32[1]{0:T(128)} %bitcast.10.first_ref, bf16[512,2048]{1,0:T(8,128)(2,1)S(1)} %copy-done, bf16[2048,4096]{1,0:T(8,128)(2,1)} %weight_ref.23, bf16[512,256]{1,0:T(8,128)(2,1)S(1)} %block_product.14.rest_0_), custom_call_target="tpu_custom_call" | custom-call | flops 20000000000 | bytes 1000 | tf_op jit(solution)/shard_map/block_product/pallas_call | solution.py:41
  27.6 0.0 collective-permute-done.9.rest_0_
  27.6 2.8 %block_product.16.rest_0_ = bf16[512,512]{1,0:T(8,128)(2,1)S(1)} custom-call(s32[1]{0:T(128)} %bitcast.9.first_ref, bf16[512,2048]{1,0:T(8,128)(2,1)S(1)} %copy-done, bf16[2048,4096]{1,0:T(8,128)(2,1)} %weight_ref.23, bf16[512,512]{1,0:T(8,128)(2,1)} %collective-permute-done.9.rest_0_, bf16[512,256]{1,0:T(8,128)(2,1)S(1)} %block_product.15.rest_1_.rest_6_), custom_call_target="tpu_custom_call" | custom-call | flops 1000 | bytes 1000 | tf_op jit(solution)/shard_map/block_product/pallas_call | solution.py:41
  30.4 3.6 %collective-permute-start.14 = (bf16[512,512]{1,0:T(8,128)(2,1)S(1)}, bf16[512,512]{1,0:T(8,128)(2,1)S(1)}, u32[]{:S(2)}, u32[]{:S(2)}) collective-permute-start(bf16[512,512]{1,0:T(8,128)(2,1)S(1)} %block_product.16.rest_0_), channel_id=1, source_target_pairs={{0,3},{1,0},{2,1},{3,2},{4,5},{5,6},{6,7},{7,4},{8,11},{9,8},{10,9... | collective-permute-start | bytes 1572872 | tf_op jit(solution)/shard_map/ppermute | solution.py:341
  34.1 2.7 %block_product.17.rest_1_.rest_5_ = bf16[512,512]{1,0:T(8,128)(2,1)S(1)} custom-call(s32[1]{0:T(128)} %bitcast.8.first_ref, bf16[512,2048]{1,0:T(8,128)(2,1)S(1)} %copy-done, bf16[2048,4096]{1,0:T(8,128)(2,1)} %weight_ref.23, bf16[512,512]{1,0:T(8,128)(2,1)S(1)} %block_product.16.rest_0_), custom_call_target="tpu_custom_call" | custom-call | flops 1000 | bytes 1000 | tf_op jit(solution)/shard_map/block_product/pallas_call | solution.py:41
  36.8 0.0 collective-permute-done.8.rest_0_
  36.8 1.9 %block_product.18.rest_1_ = bf16[512,256]{1,0:T(8,128)(2,1)S(1)} custom-call(s32[1]{0:T(128)} %bitcast.7.first_ref, bf16[512,2048]{1,0:T(8,128)(2,1)S(1)} %copy-done, bf16[2048,4096]{1,0:T(8,128)(2,1)} %weight_ref.23, bf16[512,256]{1,0:T(8,128)(2,1)S(1)} %collective-permute-done.8.rest_0_, bf16[512,512]{1,0:T(8,128)(2,1)S(1)} %block_product.17.rest_1_.rest_5_), custom_call_target="tpu_custom_call" | custom-call | flops 1000 | bytes 1000 | tf_op jit(solution)/shard_map/block_product/pallas_call | solution.py:41
  38.7 0.1 collective-permute-start.13
  38.8 8.3 %collective-permute-done.4.rest_2_.rest_9_ = bf16[2,6,16,3072]{3,2,1,0:T(8,128)(2,1)S(1)} collective-permute-done((bf16[2,6,16,3072]{3,2,1,0:T(8,128)(2,1)S(1)}, bf16[2,6,16,3072]{3,2,1,0:T(8,128)(2,1)S(1)}, u32[]{:S(2)}, u32[]{:S(2)}) %collective-permute-start.4) | collective-permute-done | bytes 1179680 | tf_op jit(solution)/shard_map/ppermute | solution.py:205
  47.1 0.0 collective-permute-start.5
  47.1 0.0 collective-permute-done.7.rest_0_
  47.1 1.9 %block_product.19.rest_4_ = bf16[512,256]{1,0:T(8,128)(2,1)S(1)} custom-call(s32[1]{0:T(128)} %bitcast.4.first_ref, bf16[512,2048]{1,0:T(8,128)(2,1)S(1)} %copy-done, bf16[2048,4096]{1,0:T(8,128)(2,1)} %weight_ref.23, bf16[512,256]{1,0:T(8,128)(2,1)S(1)} %collective-permute-done.7.rest_0_, bf16[512,256]{1,0:T(8,128)(2,1)S(1)} %block_product.18.rest_1_), custom_call_target="tpu_custom_call" | custom-call | flops 20000000000 | bytes 1000 | tf_op jit(solution)/shard_map/block_product/pallas_call | solution.py:41
  49.0 1.3 %collective-permute-start.17 = (bf16[512,256]{1,0:T(8,128)(2,1)S(1)}, bf16[512,256]{1,0:T(8,128)(2,1)S(1)}, u32[]{:S(2)}, u32[]{:S(2)}) collective-permute-start(bf16[512,256]{1,0:T(8,128)(2,1)S(1)} %block_product.19.rest_4_), channel_id=1, source_target_pairs={{0,1},{1,2},{2,3},{3,0},{4,7},{5,4},{6,5},{7,6},{8,9},{9,10},{10,1... | collective-permute-start | bytes 786440 | tf_op jit(solution)/shard_map/ppermute | solution.py:341
  50.3 0.0 collective-permute-done.3.rest_1_.rest_8_
  50.3 0.0 collective-permute-done.5.rest_3_.rest_10_
  50.4 1.6 %low_sums.1.rest_1_.rest_0_ = bf16[16,512]{1,0:T(8,128)(2,1)S(1)} custom-call(s32[24]{0:T(128)S(1)} %get-tuple-element.16.rest_0_.start_ref, s32[24]{0:T(128)S(1)} %get-tuple-element.17.end_ref, bf16[512,2048]{1,0:T(8,128)(2,1)S(1)} %copy-done, bf16[2,6,16,3072]{3,2,1,0:T(8,128)(2,1)S(1)} %get-tuple-element.18.rest_0_.rest_7_, ...), custom_call_target="tpu_custom_call" | custom-call | flops 1000 | bytes 1000 | tf_op jit(solution)/shard_map/low_sums/pallas_call | solution.py:236
  51.9 2.6 %collective-permute-start.12 = (bf16[16,512]{1,0:T(8,128)(2,1)S(1)}, bf16[16,512]{1,0:T(8,128)(2,1)S(1)}, u32[]{:S(2)}, u32[]{:S(2)}) collective-permute-start(bf16[16,512]{1,0:T(8,128)(2,1)S(1)} %low_sums.1.rest_1_.rest_0_), channel_id=1, source_target_pairs={{0,3},{1,2},{2,1},{3,0},{4,7},{5,6},{6,5},{7,4},{8,11},{9,10},{10,... | collective-permute-start | bytes 49160 | tf_op jit(solution)/shard_map/ppermute | solution.py:377
  54.5 0.0 collective-permute-start.11
  54.5 2.4 %collective-permute-done.14.rest_0_ = bf16[512,512]{1,0:T(8,128)(2,1)S(1)} collective-permute-done((bf16[512,512]{1,0:T(8,128)(2,1)S(1)}, bf16[512,512]{1,0:T(8,128)(2,1)S(1)}, u32[]{:S(2)}, u32[]{:S(2)}) %collective-permute-start.14) | collective-permute-done | bytes 524320 | tf_op jit(solution)/shard_map/ppermute | solution.py:341
  56.9 0.4 collective-permute-start.10
  57.4 2.7 %block_product.20.rest_1_ = bf16[512,512]{1,0:T(8,128)(2,1)S(1)} custom-call(s32[1]{0:T(128)} %bitcast.12.first_ref, bf16[512,2048]{1,0:T(8,128)(2,1)S(1)} %copy-done, bf16[2048,4096]{1,0:T(8,128)(2,1)} %weight_ref.23, bf16[512,512]{1,0:T(8,128)(2,1)S(1)} %collective-permute-done.14.rest_0_, bf16[16,512]{1,0:T(8,128)(2,1)S(1)} %low_sums.1.rest_1_.rest_0_), custom_call_target="tpu_custom_call" | custom-call | flops 20000000000 | bytes 1000 | tf_op jit(solution)/shard_map/block_product/pallas_call | solution.py:41
  60.1 0.0 collective-permute-done.13.rest_0_
  60.1 1.6 %collective-permute-start.16 = (bf16[512,512]{1,0:T(8,128)(2,1)S(1)}, bf16[512,512]{1,0:T(8,128)(2,1)S(1)}, u32[]{:S(2)}, u32[]{:S(2)}) collective-permute-start(bf16[512,512]{1,0:T(8,128)(2,1)S(1)} %block_product.20.rest_1_), channel_id=1, source_target_pairs={{0,3},{1,0},{2,1},{3,2},{4,5},{5,6},{6,7},{7,4},{8,11},{9,8},{10,9... | collective-permute-start | bytes 1572872 | tf_op jit(solution)/shard_map/ppermute | solution.py:341
  61.7 1.9 %block_product.21.rest_11_ = bf16[512,256]{1,0:T(8,128)(2,1)S(1)} custom-call(s32[1]{0:T(128)} %bitcast.11.first_ref, bf16[512,2048]{1,0:T(8,128)(2,1)S(1)} %copy-done, bf16[2048,4096]{1,0:T(8,128)(2,1)} %weight_ref.23, bf16[512,256]{1,0:T(8,128)(2,1)S(1)} %collective-permute-done.13.rest_0_, bf16[512,512]{1,0:T(8,128)(2,1)S(1)} %block_product.20.rest_1_), custom_call_target="tpu_custom_call" | custom-call | flops 20000000000 | bytes 1000 | tf_op jit(solution)/shard_map/block_product/pallas_call | solution.py:41
  63.7 0.0 collective-permute-done.12.rest_3_
  63.7 0.5 collective-permute-start.15
  64.2 0.0 collective-permute-done.11.rest_2_
  64.2 0.0 collective-permute-done.10.rest_1_
  64.2 1.3 %adapter_term.1 = (f32[512,256]{1,0:T(8,128)S(1)}, f32[512,512]{1,0:T(8,128)S(1)}, f32[512,256]{1,0:T(8,128)S(1)}) custom-call(s32[24]{0:T(128)S(1)} %get-tuple-element.16.rest_0_.start_ref, s32[24]{0:T(128)S(1)} %get-tuple-element.17.end_ref, bf16[16,512]{1,0:T(8,128)(2,1)S(1)} %low_sums.1.rest_1_.rest_0_, ...), custom_call_target="tpu_custom_call" | custom-call | flops 1000 | bytes 1000 | tf_op jit(solution)/shard_map/adapter_term/pallas_call | solution.py:282
  65.5 0.0 collective-permute-done.17.rest_0_
  65.5 1.4 %finish.3.rest_1_ = bf16[512,1024]{1,0:T(8,128)(2,1)} custom-call(f32[512,256]{1,0:T(8,128)S(1)} %get-tuple-element.22.term_ref, bf16[512,256]{1,0:T(8,128)(2,1)S(1)} %collective-permute-done.17.rest_0_), custom_call_target="tpu_custom_call" | custom-call | flops 20000000000 | bytes 1000 | tf_op jit(solution)/shard_map/finish/pallas_call | solution.py:309
  66.8 13.7 %collective-permute-done.16.rest_0_ = bf16[512,512]{1,0:T(8,128)(2,1)S(1)} collective-permute-done((bf16[512,512]{1,0:T(8,128)(2,1)S(1)}, bf16[512,512]{1,0:T(8,128)(2,1)S(1)}, u32[]{:S(2)}, u32[]{:S(2)}) %collective-permute-start.16) | collective-permute-done | bytes 524320 | tf_op jit(solution)/shard_map/ppermute | solution.py:341
  80.6 1.4 %finish.4.rest_1_ = bf16[512,1024]{1,0:T(8,128)(2,1)} custom-call(f32[512,512]{1,0:T(8,128)S(1)} %get-tuple-element.21.term_ref, bf16[512,512]{1,0:T(8,128)(2,1)S(1)} %collective-permute-done.16.rest_0_, bf16[512,1024]{1,0:T(8,128)(2,1)} %finish.3.rest_1_), custom_call_target="tpu_custom_call", output_to_operand_aliasing={{}: (2, {})} | custom-call | flops 1000 | bytes 1000 | tf_op jit(solution)/shard_map/finish/pallas_call | solution.py:309
  82.0 0.0 collective-permute-done.15.rest_0_
  82.0 1.3 %finish.5 = bf16[512,1024]{1,0:T(8,128)(2,1)} custom-call(f32[512,256]{1,0:T(8,128)S(1)} %get-tuple-element.20.term_ref, bf16[512,256]{1,0:T(8,128)(2,1)S(1)} %collective-permute-done.15.rest_0_, bf16[512,1024]{1,0:T(8,128)(2,1)} %finish.4.rest_1_), custom_call_target="tpu_custom_call", output_to_operand_aliasing={{}: (2, {})} | custom-call | flops 1000 | bytes 1000 | tf_op jit(solution)/shard_map/finish/pallas_call | solution.py:309
Async XLA Ops:
  0.0 5.9 %copy-start = (bf16[512,2048]{1,0:T(8,128)(2,1)S(1)}, bf16[512,2048]{1,0:T(8,128)(2,1)}, u32[]{:S(2)}) copy-start(bf16[512,2048]{1,0:T(8,128)(2,1)} %rows_ref.25) | copy-start | bytes 6291460
  0.0 5.9 %copy-start.2 = (s32[1,12]{1,0:T(1,128)S(1)}, s32[1,12]{1,0:T(1,128)}, u32[]{:S(2)}) copy-start(s32[1,12]{1,0:T(1,128)} %rest_0_.1) | copy-start | bytes 148
  2.8 17.5 %collective-permute-start.6 = (bf16[512,256]{1,0:T(8,128)(2,1)S(1)}, bf16[512,256]{1,0:T(8,128)(2,1)S(1)}, u32[]{:S(2)}, u32[]{:S(2)}) collective-permute-start(bf16[512,256]{1,0:T(8,128)(2,1)S(1)} %first_product.1.rest_1_), channel_id=1, source_target_pairs={{0,1},{1,2},{2,3},{3,0},{4,7},{5,4},{6,5},{7,6},{8,9},{9,10},{10,1... | collective-permute-start | bytes 786440 | tf_op jit(solution)/shard_map/ppermute | solution.py:341
  9.2 6.3 %collective-permute-start.2 = (s32[1,12]{1,0:T(1,128)S(1)}, s32[1,12]{1,0:T(1,128)S(1)}, u32[]{:S(2)}, u32[]{:S(2)}) collective-permute-start(s32[1,12]{1,0:T(1,128)S(1)} %get-tuple-element.14.rest_0_), channel_id=1, source_target_pairs={{0,12},{4,8},{8,4},{12,0},{1,13},{5,9},{9,5},{13,1},{2,14},{6,10},... | collective-permute-start | bytes 152 | tf_op jit(solution)/shard_map/ppermute | solution.py:358
  12.0 3.5 %collective-permute-start.1 = (s32[1,12]{1,0:T(1,128)S(1)}, s32[1,12]{1,0:T(1,128)S(1)}, u32[]{:S(2)}, u32[]{:S(2)}) collective-permute-start(s32[1,12]{1,0:T(1,128)S(1)} %get-tuple-element.14.rest_0_), channel_id=1, source_target_pairs={{0,8},{4,12},{8,0},{12,4},{1,9},{5,13},{9,1},{13,5},{2,10},{6,14},... | collective-permute-start | bytes 152 | tf_op jit(solution)/shard_map/ppermute | solution.py:358
  12.5 3.0 %collective-permute-start = (s32[1,12]{1,0:T(1,128)S(1)}, s32[1,12]{1,0:T(1,128)S(1)}, u32[]{:S(2)}, u32[]{:S(2)}) collective-permute-start(s32[1,12]{1,0:T(1,128)S(1)} %get-tuple-element.14.rest_0_), channel_id=1, source_target_pairs={{0,4},{4,0},{8,12},{12,8},{1,5},{5,1},{9,13},{13,9},{2,6},{6,2},{1... | collective-permute-start | bytes 152 | tf_op jit(solution)/shard_map/ppermute | solution.py:358
  12.5 15.1 %collective-permute-start.9 = (bf16[512,512]{1,0:T(8,128)(2,1)S(1)}, bf16[512,512]{1,0:T(8,128)(2,1)}, u32[]{:S(2)}, u32[]{:S(2)}) collective-permute-start(bf16[512,512]{1,0:T(8,128)(2,1)S(1)} %get-tuple-element.15.rest_0_), channel_id=1, source_target_pairs={{0,3},{1,0},{2,1},{3,2},{4,5},{5,6},{6,7},{7,4},{8,11},{9,8},{10,9... | collective-permute-start | bytes 1572872 | tf_op jit(solution)/shard_map/ppermute | solution.py:341
  13.3 2.3 %copy-start.1 = (s32[512]{0:T(512)S(1)}, s32[512]{0:T(512)}, u32[]{:S(2)}) copy-start(s32[512]{0:T(512)} %table_ref.1) | copy-start | bytes 6148
  13.3 2.3 %copy-start.3 = (s32[1,12]{1,0:T(1,128)S(1)}, s32[1,12]{1,0:T(1,128)}, u32[]{:S(2)}) copy-start(s32[1,12]{1,0:T(1,128)} %lens_ref.1) | copy-start | bytes 148
  19.0 28.0 %collective-permute-start.4 = (bf16[2,6,16,3072]{3,2,1,0:T(8,128)(2,1)S(1)}, bf16[2,6,16,3072]{3,2,1,0:T(8,128)(2,1)S(1)}, u32[]{:S(2)}, u32[]{:S(2)}) collective-permute-start(bf16[2,6,16,3072]{3,2,1,0:T(8,128)(2,1)S(1)} %get-tuple-element.19), channel_id=1, source_target_pairs={{0,8},{4,12},{8,0},{12,4},{1,9},{5,13},{9,1},{13,5},{2,10},{6,14},... | collective-permute-start | bytes 3538952 | tf_op jit(solution)/shard_map/ppermute | solution.py:205
  20.3 30.0 %collective-permute-start.3 = (bf16[2,6,16,3072]{3,2,1,0:T(8,128)(2,1)S(1)}, bf16[2,6,16,3072]{3,2,1,0:T(8,128)(2,1)S(1)}, u32[]{:S(2)}, u32[]{:S(2)}) collective-permute-start(bf16[2,6,16,3072]{3,2,1,0:T(8,128)(2,1)S(1)} %get-tuple-element.18.rest_0_.rest_7_), channel_id=1, source_target_pairs={{0,4},{4,0},{8,12},{12,8},{1,5},{5,1},{9,13},{13,9},{2,6},{6,2},{1... | collective-permute-start | bytes 3538952 | tf_op jit(solution)/shard_map/ppermute | solution.py:206
  22.3 14.5 %collective-permute-start.8 = (bf16[512,256]{1,0:T(8,128)(2,1)S(1)}, bf16[512,256]{1,0:T(8,128)(2,1)S(1)}, u32[]{:S(2)}, u32[]{:S(2)}) collective-permute-start(bf16[512,256]{1,0:T(8,128)(2,1)S(1)} %block_product.13.rest_1_), channel_id=1, source_target_pairs={{0,1},{1,2},{2,3},{3,0},{4,7},{5,4},{6,5},{7,6},{8,9},{9,10},{10,1... | collective-permute-start | bytes 786440 | tf_op jit(solution)/shard_map/ppermute | solution.py:341
  25.4 21.7 %collective-permute-start.7 = (bf16[512,256]{1,0:T(8,128)(2,1)S(1)}, bf16[512,256]{1,0:T(8,128)(2,1)S(1)}, u32[]{:S(2)}, u32[]{:S(2)}) collective-permute-start(bf16[512,256]{1,0:T(8,128)(2,1)S(1)} %block_product.14.rest_0_), channel_id=1, source_target_pairs={{0,1},{1,2},{2,3},{3,0},{4,7},{5,4},{6,5},{7,6},{8,9},{9,10},{10,1... | collective-permute-start | bytes 786440 | tf_op jit(solution)/shard_map/ppermute | solution.py:341
  30.4 26.5 %collective-permute-start.14 = (bf16[512,512]{1,0:T(8,128)(2,1)S(1)}, bf16[512,512]{1,0:T(8,128)(2,1)S(1)}, u32[]{:S(2)}, u32[]{:S(2)}) collective-permute-start(bf16[512,512]{1,0:T(8,128)(2,1)S(1)} %block_product.16.rest_0_), channel_id=1, source_target_pairs={{0,3},{1,0},{2,1},{3,2},{4,5},{5,6},{6,7},{7,4},{8,11},{9,8},{10,9... | collective-permute-start | bytes 1572872 | tf_op jit(solution)/shard_map/ppermute | solution.py:341
  38.7 21.4 %collective-permute-start.13 = (bf16[512,256]{1,0:T(8,128)(2,1)S(1)}, bf16[512,256]{1,0:T(8,128)(2,1)S(1)}, u32[]{:S(2)}, u32[]{:S(2)}) collective-permute-start(bf16[512,256]{1,0:T(8,128)(2,1)S(1)} %block_product.18.rest_1_), channel_id=1, source_target_pairs={{0,1},{1,2},{2,3},{3,0},{4,7},{5,4},{6,5},{7,6},{8,9},{9,10},{10,1... | collective-permute-start | bytes 786440 | tf_op jit(solution)/shard_map/ppermute | solution.py:341
  47.1 3.3 %collective-permute-start.5 = (bf16[2,6,16,3072]{3,2,1,0:T(8,128)(2,1)S(1)}, bf16[2,6,16,3072]{3,2,1,0:T(8,128)(2,1)S(1)}, u32[]{:S(2)}, u32[]{:S(2)}) collective-permute-start(bf16[2,6,16,3072]{3,2,1,0:T(8,128)(2,1)S(1)} %collective-permute-done.4.rest_2_.rest_9_), channel_id=1, source_target_pairs={{0,4},{4,0},{8,12},{12,8},{1,5},{5,1},{9,13},{13,9},{2,6},{6,2},{1... | collective-permute-start | bytes 3538952 | tf_op jit(solution)/shard_map/ppermute | solution.py:206
  49.0 16.4 %collective-permute-start.17 = (bf16[512,256]{1,0:T(8,128)(2,1)S(1)}, bf16[512,256]{1,0:T(8,128)(2,1)S(1)}, u32[]{:S(2)}, u32[]{:S(2)}) collective-permute-start(bf16[512,256]{1,0:T(8,128)(2,1)S(1)} %block_product.19.rest_4_), channel_id=1, source_target_pairs={{0,1},{1,2},{2,3},{3,0},{4,7},{5,4},{6,5},{7,6},{8,9},{9,10},{10,1... | collective-permute-start | bytes 786440 | tf_op jit(solution)/shard_map/ppermute | solution.py:341
  51.9 11.7 %collective-permute-start.12 = (bf16[16,512]{1,0:T(8,128)(2,1)S(1)}, bf16[16,512]{1,0:T(8,128)(2,1)S(1)}, u32[]{:S(2)}, u32[]{:S(2)}) collective-permute-start(bf16[16,512]{1,0:T(8,128)(2,1)S(1)} %low_sums.1.rest_1_.rest_0_), channel_id=1, source_target_pairs={{0,3},{1,2},{2,1},{3,0},{4,7},{5,6},{6,5},{7,4},{8,11},{9,10},{10,... | collective-permute-start | bytes 49160 | tf_op jit(solution)/shard_map/ppermute | solution.py:377
  54.5 9.6 %collective-permute-start.11 = (bf16[16,512]{1,0:T(8,128)(2,1)S(1)}, bf16[16,512]{1,0:T(8,128)(2,1)S(1)}, u32[]{:S(2)}, u32[]{:S(2)}) collective-permute-start(bf16[16,512]{1,0:T(8,128)(2,1)S(1)} %low_sums.1.rest_1_.rest_0_), channel_id=1, source_target_pairs={{0,2},{1,3},{2,0},{3,1},{4,6},{5,7},{6,4},{7,5},{8,10},{9,11},{10,... | collective-permute-start | bytes 49160 | tf_op jit(solution)/shard_map/ppermute | solution.py:377
  56.9 7.3 %collective-permute-start.10 = (bf16[16,512]{1,0:T(8,128)(2,1)S(1)}, bf16[16,512]{1,0:T(8,128)(2,1)S(1)}, u32[]{:S(2)}, u32[]{:S(2)}) collective-permute-start(bf16[16,512]{1,0:T(8,128)(2,1)S(1)} %low_sums.1.rest_1_.rest_0_), channel_id=1, source_target_pairs={{0,1},{1,0},{2,3},{3,2},{4,5},{5,4},{6,7},{7,6},{8,9},{9,8},{10,11... | collective-permute-start | bytes 49160 | tf_op jit(solution)/shard_map/ppermute | solution.py:377
  60.1 20.5 %collective-permute-start.16 = (bf16[512,512]{1,0:T(8,128)(2,1)S(1)}, bf16[512,512]{1,0:T(8,128)(2,1)S(1)}, u32[]{:S(2)}, u32[]{:S(2)}) collective-permute-start(bf16[512,512]{1,0:T(8,128)(2,1)S(1)} %block_product.20.rest_1_), channel_id=1, source_target_pairs={{0,3},{1,0},{2,1},{3,2},{4,5},{5,6},{6,7},{7,4},{8,11},{9,8},{10,9... | collective-permute-start | bytes 1572872 | tf_op jit(solution)/shard_map/ppermute | solution.py:341
  63.7 18.3 %collective-permute-start.15 = (bf16[512,256]{1,0:T(8,128)(2,1)S(1)}, bf16[512,256]{1,0:T(8,128)(2,1)S(1)}, u32[]{:S(2)}, u32[]{:S(2)}) collective-permute-start(bf16[512,256]{1,0:T(8,128)(2,1)S(1)} %block_product.21.rest_11_), channel_id=1, source_target_pairs={{0,1},{1,2},{2,3},{3,0},{4,7},{5,4},{6,5},{7,6},{8,9},{9,10},{10,1... | collective-permute-start | bytes 786440 | tf_op jit(solution)/shard_map/ppermute | solution.py:341

commit v19 on v18

--- a/solution.py
+++ b/solution.py
@@ -364,11 +364,12 @@
 
     for step in range(1, steps):
         for piece in pieces:
-            cost = LARGE if step == steps - 1 else SMALL
-            last = partial(1 + step, piece, addends=[moving[piece]], after=[last], cost=cost)
+            last = partial(1 + step, piece, addends=[moving[piece]], after=[last])
             moving[piece] = move(last, piece)
-            if step == 1 and piece < 2:
-                last = owns[2 - piece] = partial(0, 2 - piece, after=[last], cost=LARGE if piece == 0 else SMALL)
+            if step == 1 and piece == 0:
+                last = owns[2] = partial(0, 2, after=[last], cost=LARGE)
+            if step == steps - 1 and piece == 0:
+                last = owns[1] = partial(0, 1, after=[last], cost=LARGE)
             if step == steps - 1 and piece == 0:
                 last = low = low_sums(starts, ends, rows, packs, rank, [last])
                 lows = [low]
@@ -378,7 +379,7 @@
 
     terms = adapter_term(starts, ends, lows, owns, packs, offsets, [last])
     result = None
-    for piece in pieces:
+    for piece in (0, 2, 1):
         cost = LARGE if piece == 0 else SMALL
         result = finish(terms[piece], [moving[piece]], offsets[piece], cols, result, cost)
     return result

time: 84 us -> 88.4 us (1.052)
  waiting for transfers between devices: 24.5 us -> 17.1 us
  Pallas kernels: 38.3 us -> 43.3 us
  local copies, waits for them, and re-layouts: 0.01 us -> 4.3 us
  starting transfers between devices: 20.1 us -> 22.2 us
    ppermute x9, waiting for transfers between devices: 16.1 us -> 11.5 us  [move(): return lax.ppermute(value, ('req', 'tp'), pairs)]
    unnamed x8 -> x48, local copies, waits for them, and re-layouts: 0.01 us -> 4.3 us
    ppermute x3, starting transfers between devices: 3.08 us -> 6.37 us  [local(): lows.append(lax.ppermute(low, 'tp', pairs))]
    ppermute x1, waiting for transfers between devices: 8.3 us -> 5.4 us  [exchange(): pair = lax.ppermute(pair, 'req', [(i, i ^ 2 * y) for i in range(peers)])]
    pallas_call x11, Pallas kernels: 25.1 us -> 27.4 us  [block_product(): pl.pallas_call(functools.partial(product_kernel, len(addends), with_ids),...]
    pallas_call x3, Pallas kernels: 4.1 us -> 5.7 us  [finish(): pl.pallas_call(functools.partial(finish_kernel, len(arrivals)), grid=(row...]
    ppermute x9, starting transfers between devices: 12.5 us -> 11 us  [move(): return lax.ppermute(value, ('req', 'tp'), pairs)]
  transfers between devices with their start and end apart: 18 -> 18, of which waited for: 3 -> 5; matrix products, arithmetic and copies ran while one was open for 0% -> 0% of each run, Pallas kernels for 41% -> 44%
where the time goes in v19:
time: 88.4 us; the launch traced here: 87.4 us
  Pallas kernels  43.3 us (49%)
  starting transfers between devices  22.2 us (25%)
  waiting for transfers between devices  17.1 us (19%)
  local copies, waits for them, and re-layouts  4.3 us (5%)
    pallas_call x11, Pallas kernels, block_product(): pl.pallas_call(functools.partial(product_kernel, len(addends), with_ids),...  27.4 us
    ppermute x9, waiting for transfers between devices, move(): return lax.ppermute(value, ('req', 'tp'), pairs)  11.5 us
    ppermute x9, starting transfers between devices, move(): return lax.ppermute(value, ('req', 'tp'), pairs)  11 us
    ppermute x3, starting transfers between devices, local(): lows.append(lax.ppermute(low, 'tp', pairs))  6.37 us
    pallas_call x3, Pallas kernels, finish(): pl.pallas_call(functools.partial(finish_kernel, len(arrivals)), grid=(row...  5.7 us
    ppermute x1, waiting for transfers between devices, exchange(): pair = lax.ppermute(pair, 'req', [(i, i ^ 2 * y) for i in range(peers)])  5.4 us
    unnamed x48, local copies, waits for them, and re-layouts  4.3 us
    pallas_call x1, Pallas kernels, pick_adapters(): pl.pallas_call(functools.partial(pick_kernel, peers, len(after)), in_spec...  3.68 us
  transfers between devices with their start and end apart: 18, of which 5 were waited for; matrix products, arithmetic and copies ran while one was open for 0% of the time, Pallas kernels for 44%

profile of v19, /device:TPU:0, one launch (start us, length us, event | category | flops | bytes accessed | tf_op | source)
XLA Modules:
  0.0 87.4 jit_solution(12903443544461605005)
XLA Ops:
  0.0 3.5 %first_product.1.rest_1_ = bf16[512,256]{1,0:T(8,128)(2,1)} custom-call(s32[1]{0:T(128)} %bitcast.2.first_ref, bf16[512,2048]{1,0:T(8,128)(2,1)} %rows_ref.25, bf16[2048,4096]{1,0:T(8,128)(2,1)} %weight_ref.23), custom_call_target="tpu_custom_call" | custom-call | flops 1000 | bytes 1000 | tf_op jit(solution)/shard_map/first_product/pallas_call | solution.py:94
  3.5 3.1 %collective-permute-start.6 = (bf16[512,256]{1,0:T(8,128)(2,1)}, bf16[512,256]{1,0:T(8,128)(2,1)}, u32[]{:S(2)}, u32[]{:S(2)}) collective-permute-start(bf16[512,256]{1,0:T(8,128)(2,1)} %first_product.1.rest_1_), channel_id=1, source_target_pairs={{0,1},{1,2},{2,3},{3,0},{4,7},{5,4},{6,5},{7,6},{8,9},{9,10},{10,1... | collective-permute-start | bytes 786440 | tf_op jit(solution)/shard_map/ppermute | solution.py:341
  6.6 0.0 copy-done
  6.6 3.4 %block_product.11 = (bf16[512,512]{1,0:T(8,128)(2,1)}, s32[1,12]{1,0:T(1,128)S(1)}) custom-call(s32[1]{0:T(128)} %bitcast.1.first_ref, bf16[512,2048]{1,0:T(8,128)(2,1)S(1)} %copy-done, bf16[2048,4096]{1,0:T(8,128)(2,1)} %weight_ref.23, s32[1,12]{1,0:T(1,128)S(1)} %copy-done.18, bf16[512,256]{1,0:T(8,128)(2,1)} %first_product.1.rest_1_), custom_call_target="tpu_custom_call" | custom-call | flops 1000 | bytes 1000 | tf_op jit(solution)/shard_map/block_product/pallas_call | solution.py:41
  10.0 2.7 %collective-permute-start.2 = (s32[1,12]{1,0:T(1,128)S(1)}, s32[1,12]{1,0:T(1,128)S(1)}, u32[]{:S(2)}, u32[]{:S(2)}) collective-permute-start(s32[1,12]{1,0:T(1,128)S(1)} %get-tuple-element.14.rest_0_), channel_id=1, source_target_pairs={{0,12},{4,8},{8,4},{12,0},{1,13},{5,9},{9,5},{13,1},{2,14},{6,10},... | collective-permute-start | bytes 152 | tf_op jit(solution)/shard_map/ppermute | solution.py:358
  12.7 0.5 collective-permute-start.1
  13.2 0.0 collective-permute-start
  13.2 0.7 collective-permute-start.9
  14.0 2.0 %block_product.12.rest_6_.rest_4_ = bf16[512,256]{1,0:T(8,128)(2,1)S(1)} custom-call(s32[1]{0:T(128)} %bitcast.3.first_ref, bf16[512,2048]{1,0:T(8,128)(2,1)S(1)} %copy-done, bf16[2048,4096]{1,0:T(8,128)(2,1)} %weight_ref.23, bf16[512,512]{1,0:T(8,128)(2,1)} %get-tuple-element.15.rest_0_), custom_call_target="tpu_custom_call" | custom-call | flops 1000 | bytes 1000 | tf_op jit(solution)/shard_map/block_product/pallas_call | solution.py:41
  16.1 0.0 collective-permute-done.2.rest_3_
  16.1 0.1 collective-permute-done.1.rest_2_
  16.2 0.6 copy-done.20
  16.8 0.0 collective-permute-done.rest_1_
  16.8 0.5 copy-done.22
  17.3 0.7 copy-done.21
  18.0 0.6 copy-done.23
  18.6 3.7 %pick_adapters.1 = (bf16[2,6,16,3072]{3,2,1,0:T(8,128)(2,1)S(1)}, bf16[2,6,16,3072]{3,2,1,0:T(8,128)(2,1)S(1)}, s32[24]{0:T(128)S(1)}, s32[24]{0:T(128)S(1)}) custom-call(s32[1]{0:T(128)} %bitcast.me_ref, s32[512]{0:T(512)S(1)} %copy-done.15, s32[1,12]{1,0:T(1,128)S(1)} %copy-done.19, s32[1,12]{1,0:T(1,128)S(1)} %get-tuple-element.14.rest_0_, ...), custom_call_target="tpu_custom_call" | custom-call | flops 1000 | bytes 1000 | tf_op jit(solution)/shard_map/pick_adapters/pallas_call | solution.py:183
  22.3 0.0 copy-start.13
  22.3 1.6 %collective-permute-start.4 = (bf16[2,6,16,3072]{3,2,1,0:T(8,128)(2,1)S(1)}, bf16[2,6,16,3072]{3,2,1,0:T(8,128)(2,1)S(1)}, u32[]{:S(2)}, u32[]{:S(2)}) collective-permute-start(bf16[2,6,16,3072]{3,2,1,0:T(8,128)(2,1)S(1)} %get-tuple-element.19), channel_id=1, source_target_pairs={{0,8},{4,12},{8,0},{12,4},{1,9},{5,13},{9,1},{13,5},{2,10},{6,14},... | collective-permute-start | bytes 3538952 | tf_op jit(solution)/shard_map/ppermute | solution.py:205
  23.9 0.0 collective-permute-start.3
  23.9 0.0 collective-permute-done.6.rest_1_.rest_0_
  23.9 1.9 %block_product.13.rest_1_ = bf16[512,256]{1,0:T(8,128)(2,1)S(1)} custom-call(s32[1]{0:T(128)} %bitcast.7.first_ref, bf16[512,2048]{1,0:T(8,128)(2,1)S(1)} %copy-done, bf16[2048,4096]{1,0:T(8,128)(2,1)} %weight_ref.23, s32[24]{0:T(128)S(1)} %get-tuple-element.16.rest_0_.start_ref, bf16[512,256]{1,0:T(8,128)(2,1)} %collective-permute-done.6.rest_1_.rest_0_), custom_call_target="tpu_custom_call" | custom-call | flops 1000 | bytes 1000 | tf_op jit(solution)/shard_map/block_product/pallas_call | solution.py:41
  25.8 1.2 %collective-permute-start.8 = (bf16[512,256]{1,0:T(8,128)(2,1)S(1)}, bf16[512,256]{1,0:T(8,128)(2,1)S(1)}, u32[]{:S(2)}, u32[]{:S(2)}) collective-permute-start(bf16[512,256]{1,0:T(8,128)(2,1)S(1)} %block_product.13.rest_1_), channel_id=1, source_target_pairs={{0,1},{1,2},{2,3},{3,0},{4,7},{5,4},{6,5},{7,6},{8,9},{9,10},{10,1... | collective-permute-start | bytes 786440 | tf_op jit(solution)/shard_map/ppermute | solution.py:341
  27.0 2.0 %block_product.14.rest_0_ = bf16[512,256]{1,0:T(8,128)(2,1)S(1)} custom-call(s32[1]{0:T(128)} %bitcast.6.first_ref, bf16[512,2048]{1,0:T(8,128)(2,1)S(1)} %copy-done, bf16[2048,4096]{1,0:T(8,128)(2,1)} %weight_ref.23, bf16[512,256]{1,0:T(8,128)(2,1)} %collective-permute-done.6.rest_1_.rest_0_, bf16[512,256]{1,0:T(8,128)(2,1)S(1)} %block_product.13.rest_1_), custom_call_target="tpu_custom_call" | custom-call | flops 1000 | bytes 1000 | tf_op jit(solution)/shard_map/block_product/pallas_call | solution.py:41
  29.0 0.3 collective-permute-start.7
  29.3 1.9 %block_product.15.rest_1_.rest_6_ = bf16[512,256]{1,0:T(8,128)(2,1)S(1)} custom-call(s32[1]{0:T(128)} %bitcast.10.first_ref, bf16[512,2048]{1,0:T(8,128)(2,1)S(1)} %copy-done, bf16[2048,4096]{1,0:T(8,128)(2,1)} %weight_ref.23, bf16[512,256]{1,0:T(8,128)(2,1)S(1)} %block_product.14.rest_0_), custom_call_target="tpu_custom_call" | custom-call | flops 20000000000 | bytes 1000 | tf_op jit(solution)/shard_map/block_product/pallas_call | solution.py:41
  31.2 0.0 collective-permute-done.9.rest_0_
  31.3 2.9 %block_product.16.rest_1_ = bf16[512,512]{1,0:T(8,128)(2,1)S(1)} custom-call(s32[1]{0:T(128)} %bitcast.9.first_ref, bf16[512,2048]{1,0:T(8,128)(2,1)S(1)} %copy-done, bf16[2048,4096]{1,0:T(8,128)(2,1)} %weight_ref.23, bf16[512,512]{1,0:T(8,128)(2,1)} %collective-permute-done.9.rest_0_, bf16[512,256]{1,0:T(8,128)(2,1)S(1)} %block_product.15.rest_1_.rest_6_), custom_call_target="tpu_custom_call" | custom-call | flops 1000 | bytes 1000 | tf_op jit(solution)/shard_map/block_product/pallas_call | solution.py:41
  34.1 3.6 %collective-permute-start.14 = (bf16[512,512]{1,0:T(8,128)(2,1)S(1)}, bf16[512,512]{1,0:T(8,128)(2,1)S(1)}, u32[]{:S(2)}, u32[]{:S(2)}) collective-permute-start(bf16[512,512]{1,0:T(8,128)(2,1)S(1)} %block_product.16.rest_1_), channel_id=1, source_target_pairs={{0,3},{1,0},{2,1},{3,2},{4,5},{5,6},{6,7},{7,4},{8,11},{9,8},{10,9... | collective-permute-start | bytes 1572872 | tf_op jit(solution)/shard_map/ppermute | solution.py:341
  37.8 0.0 collective-permute-done.8.rest_0_
  37.8 2.6 %block_product.17.rest_1_ = bf16[512,256]{1,0:T(8,128)(2,1)} custom-call(s32[1]{0:T(128)} %bitcast.8.first_ref, bf16[512,2048]{1,0:T(8,128)(2,1)S(1)} %copy-done, bf16[2048,4096]{1,0:T(8,128)(2,1)} %weight_ref.23, bf16[512,256]{1,0:T(8,128)(2,1)S(1)} %collective-permute-done.8.rest_0_, bf16[512,512]{1,0:T(8,128)(2,1)S(1)} %block_product.16.rest_1_), custom_call_target="tpu_custom_call" | custom-call | flops 1000 | bytes 1000 | tf_op jit(solution)/shard_map/block_product/pallas_call | solution.py:41
  40.4 0.0 collective-permute-start.13
  40.4 1.2 %collective-permute-done.7.rest_0_ = bf16[512,256]{1,0:T(8,128)(2,1)S(1)} collective-permute-done((bf16[512,256]{1,0:T(8,128)(2,1)S(1)}, bf16[512,256]{1,0:T(8,128)(2,1)S(1)}, u32[]{:S(2)}, u32[]{:S(2)}) %collective-permute-start.7) | collective-permute-done | bytes 262176 | tf_op jit(solution)/shard_map/ppermute | solution.py:341
  41.7 2.7 %block_product.18.rest_0_ = bf16[512,256]{1,0:T(8,128)(2,1)} custom-call(s32[1]{0:T(128)} %bitcast.5.first_ref, bf16[512,2048]{1,0:T(8,128)(2,1)S(1)} %copy-done, bf16[2048,4096]{1,0:T(8,128)(2,1)} %weight_ref.23, bf16[512,256]{1,0:T(8,128)(2,1)S(1)} %collective-permute-done.7.rest_0_, bf16[512,256]{1,0:T(8,128)(2,1)} %block_product.17.rest_1_), custom_call_target="tpu_custom_call" | custom-call | flops 1000 | bytes 1000 | tf_op jit(solution)/shard_map/block_product/pallas_call | solution.py:41
  44.3 0.0 collective-permute-start.17
  44.3 5.4 %collective-permute-done.4.rest_2_.rest_9_ = bf16[2,6,16,3072]{3,2,1,0:T(8,128)(2,1)S(1)} collective-permute-done((bf16[2,6,16,3072]{3,2,1,0:T(8,128)(2,1)S(1)}, bf16[2,6,16,3072]{3,2,1,0:T(8,128)(2,1)S(1)}, u32[]{:S(2)}, u32[]{:S(2)}) %collective-permute-start.4) | collective-permute-done | bytes 1179680 | tf_op jit(solution)/shard_map/ppermute | solution.py:205
  49.7 0.0 collective-permute-start.5
  49.7 3.1 %block_product.19.rest_4_.rest_5_ = bf16[512,512]{1,0:T(8,128)(2,1)S(1)} custom-call(s32[1]{0:T(128)} %bitcast.4.first_ref, bf16[512,2048]{1,0:T(8,128)(2,1)S(1)} %copy-done, bf16[2048,4096]{1,0:T(8,128)(2,1)} %weight_ref.23, bf16[512,256]{1,0:T(8,128)(2,1)} %block_product.18.rest_0_), custom_call_target="tpu_custom_call" | custom-call | flops 20000000000 | bytes 1000 | tf_op jit(solution)/shard_map/block_product/pallas_call | solution.py:41
  52.9 0.0 copy-start.7
  52.9 0.0 collective-permute-done.3.rest_1_.rest_8_
  52.9 0.0 collective-permute-done.5.rest_3_.rest_10_
  52.9 1.6 %low_sums.1.rest_1_.rest_0_ = bf16[16,512]{1,0:T(8,128)(2,1)S(1)} custom-call(s32[24]{0:T(128)S(1)} %get-tuple-element.16.rest_0_.start_ref, s32[24]{0:T(128)S(1)} %get-tuple-element.17.end_ref, bf16[512,2048]{1,0:T(8,128)(2,1)S(1)} %copy-done, bf16[2,6,16,3072]{3,2,1,0:T(8,128)(2,1)S(1)} %get-tuple-element.18.rest_0_.rest_7_, ...), custom_call_target="tpu_custom_call" | custom-call | flops 1000 | bytes 1000 | tf_op jit(solution)/shard_map/low_sums/pallas_call | solution.py:236
  54.5 3.2 %collective-permute-start.12 = (bf16[16,512]{1,0:T(8,128)(2,1)S(1)}, bf16[16,512]{1,0:T(8,128)(2,1)}, u32[]{:S(2)}, u32[]{:S(2)}) collective-permute-start(bf16[16,512]{1,0:T(8,128)(2,1)S(1)} %low_sums.1.rest_1_.rest_0_), channel_id=1, source_target_pairs={{0,3},{1,2},{2,1},{3,0},{4,7},{5,6},{6,5},{7,4},{8,11},{9,10},{10,... | collective-permute-start | bytes 49160 | tf_op jit(solution)/shard_map/ppermute | solution.py:378
  57.7 0.0 collective-permute-start.11
  57.7 3.5 %collective-permute-done.14.rest_0_ = bf16[512,512]{1,0:T(8,128)(2,1)S(1)} collective-permute-done((bf16[512,512]{1,0:T(8,128)(2,1)S(1)}, bf16[512,512]{1,0:T(8,128)(2,1)S(1)}, u32[]{:S(2)}, u32[]{:S(2)}) %collective-permute-start.14) | collective-permute-done | bytes 524320 | tf_op jit(solution)/shard_map/ppermute | solution.py:341
  61.3 0.8 copy-done.11
  62.1 3.2 %collective-permute-start.10 = (bf16[16,512]{1,0:T(8,128)(2,1)S(1)}, bf16[16,512]{1,0:T(8,128)(2,1)}, u32[]{:S(2)}, u32[]{:S(2)}) collective-permute-start(bf16[16,512]{1,0:T(8,128)(2,1)S(1)} %low_sums.1.rest_1_.rest_0_), channel_id=1, source_target_pairs={{0,1},{1,0},{2,3},{3,2},{4,5},{5,4},{6,7},{7,6},{8,9},{9,8},{10,11... | collective-permute-start | bytes 49160 | tf_op jit(solution)/shard_map/ppermute | solution.py:378
  65.2 1.0 %copy-done.12 = bf16[512,512]{1,0:T(8,128)(2,1)S(1)} copy-done((bf16[512,512]{1,0:T(8,128)(2,1)S(1)}, bf16[512,512]{1,0:T(8,128)(2,1)}, u32[]{:S(2)}) %copy-start.12) | copy-done | bytes 524312
  66.3 2.7 %block_product.20.rest_1_ = bf16[512,512]{1,0:T(8,128)(2,1)S(1)} custom-call(s32[1]{0:T(128)} %bitcast.12.first_ref, bf16[512,2048]{1,0:T(8,128)(2,1)S(1)} %copy-done, bf16[2048,4096]{1,0:T(8,128)(2,1)} %weight_ref.23, bf16[512,512]{1,0:T(8,128)(2,1)S(1)} %copy-done.12, bf16[16,512]{1,0:T(8,128)(2,1)S(1)} %low_sums.1.rest_1_.rest_0_), custom_call_target="tpu_custom_call" | custom-call | flops 1000 | bytes 1000 | tf_op jit(solution)/shard_map/block_product/pallas_call | solution.py:41
  69.0 0.0 collective-permute-done.13.rest_0_
  69.0 0.1 collective-permute-start.15
  69.1 0.0 copy-start.8
  69.1 2.1 %block_product.21.rest_11_ = bf16[512,256]{1,0:T(8,128)(2,1)S(1)} custom-call(s32[1]{0:T(128)} %bitcast.11.first_ref, bf16[512,2048]{1,0:T(8,128)(2,1)S(1)} %copy-done, bf16[2048,4096]{1,0:T(8,128)(2,1)} %weight_ref.23, bf16[512,256]{1,0:T(8,128)(2,1)} %collective-permute-done.13.rest_0_, bf16[512,512]{1,0:T(8,128)(2,1)S(1)} %block_product.20.rest_1_), custom_call_target="tpu_custom_call" | custom-call | flops 1000 | bytes 1000 | tf_op jit(solution)/shard_map/block_product/pallas_call | solution.py:41
  71.3 0.0 collective-permute-done.12.rest_3_
  71.3 2.0 %collective-permute-start.16 = (bf16[512,256]{1,0:T(8,128)(2,1)S(1)}, bf16[512,256]{1,0:T(8,128)(2,1)S(1)}, u32[]{:S(2)}, u32[]{:S(2)}) collective-permute-start(bf16[512,256]{1,0:T(8,128)(2,1)S(1)} %block_product.21.rest_11_), channel_id=1, source_target_pairs={{0,1},{1,2},{2,3},{3,0},{4,7},{5,4},{6,5},{7,6},{8,9},{9,10},{10,1... | collective-permute-start | bytes 786440 | tf_op jit(solution)/shard_map/ppermute | solution.py:341
  73.3 0.0 collective-permute-done.11.rest_2_
  73.3 0.0 collective-permute-done.10.rest_1_
  73.4 1.5 %adapter_term.1 = (f32[512,256]{1,0:T(8,128)S(1)}, f32[512,512]{1,0:T(8,128)S(1)}, f32[512,256]{1,0:T(8,128)S(1)}) custom-call(s32[24]{0:T(128)S(1)} %copy-done.14, s32[24]{0:T(128)S(1)} %copy-done.17, bf16[16,512]{1,0:T(8,128)(2,1)S(1)} %low_sums.1.rest_1_.rest_0_, bf16[16,512]{1,0:T(8,128)(2,1)} %collective-permute-done.10.rest_1_, ...), custom_call_target="tpu_custom_call" | custom-call | flops 1000 | bytes 1000 | tf_op jit(solution)/shard_map/adapter_term/pallas_call | solution.py:282
  74.9 0.0 collective-permute-done.17.rest_0_
  74.9 3.0 %finish.3.rest_1_ = bf16[512,1024]{1,0:T(8,128)(2,1)} custom-call(f32[512,256]{1,0:T(8,128)S(1)} %get-tuple-element.22.term_ref, bf16[512,256]{1,0:T(8,128)(2,1)} %collective-permute-done.17.rest_0_), custom_call_target="tpu_custom_call" | custom-call | flops 20000000000 | bytes 1000 | tf_op jit(solution)/shard_map/finish/pallas_call | solution.py:309
  77.9 6.8 %collective-permute-done.16.rest_0_ = bf16[512,256]{1,0:T(8,128)(2,1)S(1)} collective-permute-done((bf16[512,256]{1,0:T(8,128)(2,1)S(1)}, bf16[512,256]{1,0:T(8,128)(2,1)S(1)}, u32[]{:S(2)}, u32[]{:S(2)}) %collective-permute-start.16) | collective-permute-done | bytes 262176 | tf_op jit(solution)/shard_map/ppermute | solution.py:341
  84.7 1.3 %finish.4.rest_1_ = bf16[512,1024]{1,0:T(8,128)(2,1)} custom-call(f32[512,256]{1,0:T(8,128)S(1)} %get-tuple-element.21.term_ref, bf16[512,256]{1,0:T(8,128)(2,1)S(1)} %collective-permute-done.16.rest_0_, bf16[512,1024]{1,0:T(8,128)(2,1)} %finish.3.rest_1_), custom_call_target="tpu_custom_call", output_to_operand_aliasing={{}: (2, {})} | custom-call | flops 1000 | bytes 1000 | tf_op jit(solution)/shard_map/finish/pallas_call | solution.py:309
  86.0 0.0 collective-permute-done.15.rest_0_
  86.0 1.4 %finish.5 = bf16[512,1024]{1,0:T(8,128)(2,1)} custom-call(f32[512,512]{1,0:T(8,128)S(1)} %get-tuple-element.20.term_ref, bf16[512,512]{1,0:T(8,128)(2,1)S(1)} %collective-permute-done.15.rest_0_, bf16[512,1024]{1,0:T(8,128)(2,1)} %finish.4.rest_1_), custom_call_target="tpu_custom_call", output_to_operand_aliasing={{}: (2, {})} | custom-call | flops 1000 | bytes 1000 | tf_op jit(solution)/shard_map/finish/pallas_call | solution.py:309
  (38 shorter events, 0.1 us)
Async XLA Ops:
  0.0 6.6 %copy-start = (bf16[512,2048]{1,0:T(8,128)(2,1)S(1)}, bf16[512,2048]{1,0:T(8,128)(2,1)}, u32[]{:S(2)}) copy-start(bf16[512,2048]{1,0:T(8,128)(2,1)} %rows_ref.25) | copy-start | bytes 6291460
  0.0 6.6 %copy-start.18 = (s32[1,12]{1,0:T(1,128)S(1)}, s32[1,12]{1,0:T(1,128)}, u32[]{:S(2)}) copy-start(s32[1,12]{1,0:T(1,128)} %rest_0_.1) | copy-start | bytes 148
  3.5 20.4 %collective-permute-start.6 = (bf16[512,256]{1,0:T(8,128)(2,1)}, bf16[512,256]{1,0:T(8,128)(2,1)}, u32[]{:S(2)}, u32[]{:S(2)}) collective-permute-start(bf16[512,256]{1,0:T(8,128)(2,1)} %first_product.1.rest_1_), channel_id=1, source_target_pairs={{0,1},{1,2},{2,3},{3,0},{4,7},{5,4},{6,5},{7,6},{8,9},{9,10},{10,1... | collective-permute-start | bytes 786440 | tf_op jit(solution)/shard_map/ppermute | solution.py:341
  10.0 6.1 %collective-permute-start.2 = (s32[1,12]{1,0:T(1,128)S(1)}, s32[1,12]{1,0:T(1,128)S(1)}, u32[]{:S(2)}, u32[]{:S(2)}) collective-permute-start(s32[1,12]{1,0:T(1,128)S(1)} %get-tuple-element.14.rest_0_), channel_id=1, source_target_pairs={{0,12},{4,8},{8,4},{12,0},{1,13},{5,9},{9,5},{13,1},{2,14},{6,10},... | collective-permute-start | bytes 152 | tf_op jit(solution)/shard_map/ppermute | solution.py:358
  12.7 3.5 %collective-permute-start.1 = (s32[1,12]{1,0:T(1,128)S(1)}, s32[1,12]{1,0:T(1,128)S(1)}, u32[]{:S(2)}, u32[]{:S(2)}) collective-permute-start(s32[1,12]{1,0:T(1,128)S(1)} %get-tuple-element.14.rest_0_), channel_id=1, source_target_pairs={{0,8},{4,12},{8,0},{12,4},{1,9},{5,13},{9,1},{13,5},{2,10},{6,14},... | collective-permute-start | bytes 152 | tf_op jit(solution)/shard_map/ppermute | solution.py:358
  13.2 3.6 %collective-permute-start = (s32[1,12]{1,0:T(1,128)S(1)}, s32[1,12]{1,0:T(1,128)S(1)}, u32[]{:S(2)}, u32[]{:S(2)}) collective-permute-start(s32[1,12]{1,0:T(1,128)S(1)} %get-tuple-element.14.rest_0_), channel_id=1, source_target_pairs={{0,4},{4,0},{8,12},{12,8},{1,5},{5,1},{9,13},{13,9},{2,6},{6,2},{1... | collective-permute-start | bytes 152 | tf_op jit(solution)/shard_map/ppermute | solution.py:358
  13.2 18.0 %collective-permute-start.9 = (bf16[512,512]{1,0:T(8,128)(2,1)}, bf16[512,512]{1,0:T(8,128)(2,1)}, u32[]{:S(2)}, u32[]{:S(2)}) collective-permute-start(bf16[512,512]{1,0:T(8,128)(2,1)} %get-tuple-element.15.rest_0_), channel_id=1, source_target_pairs={{0,3},{1,0},{2,1},{3,2},{4,5},{5,6},{6,7},{7,4},{8,11},{9,8},{10,9... | collective-permute-start | bytes 1572872 | tf_op jit(solution)/shard_map/ppermute | solution.py:341
  14.0 3.4 %copy-start.15 = (s32[512]{0:T(512)S(1)}, s32[512]{0:T(512)}, u32[]{:S(2)}) copy-start(s32[512]{0:T(512)} %table_ref.1) | copy-start | bytes 6148
  14.0 3.4 %copy-start.19 = (s32[1,12]{1,0:T(1,128)S(1)}, s32[1,12]{1,0:T(1,128)}, u32[]{:S(2)}) copy-start(s32[1,12]{1,0:T(1,128)} %lens_ref.1) | copy-start | bytes 148
  16.2 0.6 copy-start.20
  16.8 0.5 copy-start.22
  17.3 0.7 copy-start.21
  18.0 0.6 copy-start.23
  22.3 30.6 %copy-start.13 = (s32[24]{0:T(128)}, s32[24]{0:T(128)S(1)}, u32[]{:S(2)}) copy-start(s32[24]{0:T(128)S(1)} %get-tuple-element.16.rest_0_.start_ref) | copy-start | bytes 292
  22.3 30.6 %copy-start.16 = (s32[24]{0:T(128)}, s32[24]{0:T(128)S(1)}, u32[]{:S(2)}) copy-start(s32[24]{0:T(128)S(1)} %get-tuple-element.17.end_ref) | copy-start | bytes 292
  22.3 27.4 %collective-permute-start.4 = (bf16[2,6,16,3072]{3,2,1,0:T(8,128)(2,1)S(1)}, bf16[2,6,16,3072]{3,2,1,0:T(8,128)(2,1)S(1)}, u32[]{:S(2)}, u32[]{:S(2)}) collective-permute-start(bf16[2,6,16,3072]{3,2,1,0:T(8,128)(2,1)S(1)} %get-tuple-element.19), channel_id=1, source_target_pairs={{0,8},{4,12},{8,0},{12,4},{1,9},{5,13},{9,1},{13,5},{2,10},{6,14},... | collective-permute-start | bytes 3538952 | tf_op jit(solution)/shard_map/ppermute | solution.py:205
  23.9 29.0 %collective-permute-start.3 = (bf16[2,6,16,3072]{3,2,1,0:T(8,128)(2,1)S(1)}, bf16[2,6,16,3072]{3,2,1,0:T(8,128)(2,1)S(1)}, u32[]{:S(2)}, u32[]{:S(2)}) collective-permute-start(bf16[2,6,16,3072]{3,2,1,0:T(8,128)(2,1)S(1)} %get-tuple-element.18.rest_0_.rest_7_), channel_id=1, source_target_pairs={{0,4},{4,0},{8,12},{12,8},{1,5},{5,1},{9,13},{13,9},{2,6},{6,2},{1... | collective-permute-start | bytes 3538952 | tf_op jit(solution)/shard_map/ppermute | solution.py:206
  25.8 11.9 %collective-permute-start.8 = (bf16[512,256]{1,0:T(8,128)(2,1)S(1)}, bf16[512,256]{1,0:T(8,128)(2,1)S(1)}, u32[]{:S(2)}, u32[]{:S(2)}) collective-permute-start(bf16[512,256]{1,0:T(8,128)(2,1)S(1)} %block_product.13.rest_1_), channel_id=1, source_target_pairs={{0,1},{1,2},{2,3},{3,0},{4,7},{5,4},{6,5},{7,6},{8,9},{9,10},{10,1... | collective-permute-start | bytes 786440 | tf_op jit(solution)/shard_map/ppermute | solution.py:341
  29.0 12.6 %collective-permute-start.7 = (bf16[512,256]{1,0:T(8,128)(2,1)S(1)}, bf16[512,256]{1,0:T(8,128)(2,1)S(1)}, u32[]{:S(2)}, u32[]{:S(2)}) collective-permute-start(bf16[512,256]{1,0:T(8,128)(2,1)S(1)} %block_product.14.rest_0_), channel_id=1, source_target_pairs={{0,1},{1,2},{2,3},{3,0},{4,7},{5,4},{6,5},{7,6},{8,9},{9,10},{10,1... | collective-permute-start | bytes 786440 | tf_op jit(solution)/shard_map/ppermute | solution.py:341
  31.2 2.9 %copy-start.9 = (bf16[512,256]{1,0:T(8,128)(2,1)}, bf16[512,256]{1,0:T(8,128)(2,1)S(1)}, u32[]{:S(2)}) copy-start(bf16[512,256]{1,0:T(8,128)(2,1)S(1)} %block_product.15.rest_1_.rest_6_) | copy-start | bytes 786436
  34.1 27.1 %collective-permute-start.14 = (bf16[512,512]{1,0:T(8,128)(2,1)S(1)}, bf16[512,512]{1,0:T(8,128)(2,1)S(1)}, u32[]{:S(2)}, u32[]{:S(2)}) collective-permute-start(bf16[512,512]{1,0:T(8,128)(2,1)S(1)} %block_product.16.rest_1_), channel_id=1, source_target_pairs={{0,3},{1,0},{2,1},{3,2},{4,5},{5,6},{6,7},{7,4},{8,11},{9,8},{10,9... | collective-permute-start | bytes 1572872 | tf_op jit(solution)/shard_map/ppermute | solution.py:341
  40.4 28.6 %collective-permute-start.13 = (bf16[512,256]{1,0:T(8,128)(2,1)}, bf16[512,256]{1,0:T(8,128)(2,1)}, u32[]{:S(2)}, u32[]{:S(2)}) collective-permute-start(bf16[512,256]{1,0:T(8,128)(2,1)} %block_product.17.rest_1_), channel_id=1, source_target_pairs={{0,1},{1,2},{2,3},{3,0},{4,7},{5,4},{6,5},{7,6},{8,9},{9,10},{10,1... | collective-permute-start | bytes 786440 | tf_op jit(solution)/shard_map/ppermute | solution.py:341
  44.3 30.6 %collective-permute-start.17 = (bf16[512,256]{1,0:T(8,128)(2,1)}, bf16[512,256]{1,0:T(8,128)(2,1)}, u32[]{:S(2)}, u32[]{:S(2)}) collective-permute-start(bf16[512,256]{1,0:T(8,128)(2,1)} %block_product.18.rest_0_), channel_id=1, source_target_pairs={{0,1},{1,2},{2,3},{3,0},{4,7},{5,4},{6,5},{7,6},{8,9},{9,10},{10,1... | collective-permute-start | bytes 786440 | tf_op jit(solution)/shard_map/ppermute | solution.py:341
  49.7 3.2 %copy-start.1 = (bf16[2,6,16,3072]{3,2,1,0:T(8,128)(2,1)}, bf16[2,6,16,3072]{3,2,1,0:T(8,128)(2,1)S(1)}, u32[]{:S(2)}) copy-start(bf16[2,6,16,3072]{3,2,1,0:T(8,128)(2,1)S(1)} %collective-permute-done.4.rest_2_.rest_9_) | copy-start | bytes 3538948
  49.7 3.2 %collective-permute-start.5 = (bf16[2,6,16,3072]{3,2,1,0:T(8,128)(2,1)S(1)}, bf16[2,6,16,3072]{3,2,1,0:T(8,128)(2,1)S(1)}, u32[]{:S(2)}, u32[]{:S(2)}) collective-permute-start(bf16[2,6,16,3072]{3,2,1,0:T(8,128)(2,1)S(1)} %collective-permute-done.4.rest_2_.rest_9_), channel_id=1, source_target_pairs={{0,4},{4,0},{8,12},{12,8},{1,5},{5,1},{9,13},{13,9},{2,6},{6,2},{1... | collective-permute-start | bytes 3538952 | tf_op jit(solution)/shard_map/ppermute | solution.py:206
  52.9 1.6 %copy-start.7 = (bf16[512,512]{1,0:T(8,128)(2,1)}, bf16[512,512]{1,0:T(8,128)(2,1)S(1)}, u32[]{:S(2)}) copy-start(bf16[512,512]{1,0:T(8,128)(2,1)S(1)} %block_product.19.rest_4_.rest_5_) | copy-start | bytes 1572868
  52.9 1.6 %copy-start.3 = (bf16[2,6,16,3072]{3,2,1,0:T(8,128)(2,1)}, bf16[2,6,16,3072]{3,2,1,0:T(8,128)(2,1)S(1)}, u32[]{:S(2)}) copy-start(bf16[2,6,16,3072]{3,2,1,0:T(8,128)(2,1)S(1)} %collective-permute-done.3.rest_1_.rest_8_) | copy-start | bytes 3538948
  52.9 1.6 %copy-start.5 = (bf16[2,6,16,3072]{3,2,1,0:T(8,128)(2,1)}, bf16[2,6,16,3072]{3,2,1,0:T(8,128)(2,1)S(1)}, u32[]{:S(2)}) copy-start(bf16[2,6,16,3072]{3,2,1,0:T(8,128)(2,1)S(1)} %collective-permute-done.5.rest_3_.rest_10_) | copy-start | bytes 3538948
  54.5 16.8 %collective-permute-start.12 = (bf16[16,512]{1,0:T(8,128)(2,1)S(1)}, bf16[16,512]{1,0:T(8,128)(2,1)}, u32[]{:S(2)}, u32[]{:S(2)}) collective-permute-start(bf16[16,512]{1,0:T(8,128)(2,1)S(1)} %low_sums.1.rest_1_.rest_0_), channel_id=1, source_target_pairs={{0,3},{1,2},{2,1},{3,0},{4,7},{5,6},{6,5},{7,4},{8,11},{9,10},{10,... | collective-permute-start | bytes 49160 | tf_op jit(solution)/shard_map/ppermute | solution.py:378
  57.7 15.6 %collective-permute-start.11 = (bf16[16,512]{1,0:T(8,128)(2,1)S(1)}, bf16[16,512]{1,0:T(8,128)(2,1)}, u32[]{:S(2)}, u32[]{:S(2)}) collective-permute-start(bf16[16,512]{1,0:T(8,128)(2,1)S(1)} %low_sums.1.rest_1_.rest_0_), channel_id=1, source_target_pairs={{0,2},{1,3},{2,0},{3,1},{4,6},{5,7},{6,4},{7,5},{8,10},{9,11},{10,... | collective-permute-start | bytes 49160 | tf_op jit(solution)/shard_map/ppermute | solution.py:378
  61.3 0.8 copy-start.11
  62.1 11.3 %collective-permute-start.10 = (bf16[16,512]{1,0:T(8,128)(2,1)S(1)}, bf16[16,512]{1,0:T(8,128)(2,1)}, u32[]{:S(2)}, u32[]{:S(2)}) collective-permute-start(bf16[16,512]{1,0:T(8,128)(2,1)S(1)} %low_sums.1.rest_1_.rest_0_), channel_id=1, source_target_pairs={{0,1},{1,0},{2,3},{3,2},{4,5},{5,4},{6,7},{7,6},{8,9},{9,8},{10,11... | collective-permute-start | bytes 49160 | tf_op jit(solution)/shard_map/ppermute | solution.py:378
  65.2 1.0 %copy-start.12 = (bf16[512,512]{1,0:T(8,128)(2,1)S(1)}, bf16[512,512]{1,0:T(8,128)(2,1)}, u32[]{:S(2)}) copy-start(bf16[512,512]{1,0:T(8,128)(2,1)} %copy-done.11) | copy-start | bytes 1572868
  69.0 17.0 %collective-permute-start.15 = (bf16[512,512]{1,0:T(8,128)(2,1)S(1)}, bf16[512,512]{1,0:T(8,128)(2,1)S(1)}, u32[]{:S(2)}, u32[]{:S(2)}) collective-permute-start(bf16[512,512]{1,0:T(8,128)(2,1)S(1)} %block_product.20.rest_1_), channel_id=1, source_target_pairs={{0,3},{1,0},{2,1},{3,2},{4,5},{5,6},{6,7},{7,4},{8,11},{9,8},{10,9... | collective-permute-start | bytes 1572872 | tf_op jit(solution)/shard_map/ppermute | solution.py:341
  69.1 4.3 %copy-start.2 = (bf16[2,6,16,3072]{3,2,1,0:T(8,128)(2,1)S(1)}, bf16[2,6,16,3072]{3,2,1,0:T(8,128)(2,1)}, u32[]{:S(2)}) copy-start(bf16[2,6,16,3072]{3,2,1,0:T(8,128)(2,1)} %copy-done.1) | copy-start | bytes 3538948
  69.1 4.3 %copy-start.4 = (bf16[2,6,16,3072]{3,2,1,0:T(8,128)(2,1)S(1)}, bf16[2,6,16,3072]{3,2,1,0:T(8,128)(2,1)}, u32[]{:S(2)}) copy-start(bf16[2,6,16,3072]{3,2,1,0:T(8,128)(2,1)} %copy-done.3) | copy-start | bytes 3538948
  69.1 4.3 %copy-start.6 = (bf16[2,6,16,3072]{3,2,1,0:T(8,128)(2,1)S(1)}, bf16[2,6,16,3072]{3,2,1,0:T(8,128)(2,1)}, u32[]{:S(2)}) copy-start(bf16[2,6,16,3072]{3,2,1,0:T(8,128)(2,1)} %copy-done.5) | copy-start | bytes 3538948
  69.1 4.3 %copy-start.8 = (bf16[512,512]{1,0:T(8,128)(2,1)S(1)}, bf16[512,512]{1,0:T(8,128)(2,1)}, u32[]{:S(2)}) copy-start(bf16[512,512]{1,0:T(8,128)(2,1)} %copy-done.7) | copy-start | bytes 1572868
  69.1 4.3 %copy-start.10 = (bf16[512,256]{1,0:T(8,128)(2,1)S(1)}, bf16[512,256]{1,0:T(8,128)(2,1)}, u32[]{:S(2)}) copy-start(bf16[512,256]{1,0:T(8,128)(2,1)} %copy-done.9) | copy-start | bytes 786436
  69.1 4.3 %copy-start.14 = (s32[24]{0:T(128)S(1)}, s32[24]{0:T(128)}, u32[]{:S(2)}) copy-start(s32[24]{0:T(128)} %copy-done.13) | copy-start | bytes 292
  69.1 4.3 %copy-start.17 = (s32[24]{0:T(128)S(1)}, s32[24]{0:T(128)}, u32[]{:S(2)}) copy-start(s32[24]{0:T(128)} %copy-done.16) | copy-start | bytes 292
  71.3 13.4 %collective-permute-start.16 = (bf16[512,256]{1,0:T(8,128)(2,1)S(1)}, bf16[512,256]{1,0:T(8,128)(2,1)S(1)}, u32[]{:S(2)}, u32[]{:S(2)}) collective-permute-start(bf16[512,256]{1,0:T(8,128)(2,1)S(1)} %block_product.21.rest_11_), channel_id=1, source_target_pairs={{0,1},{1,2},{2,3},{3,0},{4,7},{5,4},{6,5},{7,6},{8,9},{9,10},{10,1... | collective-permute-start | bytes 786440 | tf_op jit(solution)/shard_map/ppermute | solution.py:341

commit v20 on v16

--- a/solution.py
+++ b/solution.py
@@ -28,7 +28,9 @@
             ids_out_ref[0, s] = ids_ref[0, s]
 
 
-def block_product(rows, weight, first, width, addends=(), after=(), ids=None, cost=SMALL):
+def block_product(
+    rows, weight, first, width, addends=(), skip=0, after=(), ids=None, cost=SMALL
+):
     row_total, depth = rows.shape
     tile = min(256, width)
     with_ids = ids is not None
@@ -48,7 +50,7 @@
                 pl.BlockSpec((row_total, depth), lambda j, t: (0, 0)),
                 pl.BlockSpec((depth, tile), lambda j, t: (0, t[0] + j)),
             ]
-            + [columns] * len(addends)
+            + [pl.BlockSpec((row_total, tile), lambda j, t: (0, skip // tile + j))] * len(addends)
             + [smem] * with_ids
             + [hbm] * len(after),
             out_specs=out_specs,
@@ -294,22 +296,23 @@
     rest[-1][...] = total.astype(rest[-1].dtype)
 
 
-def finish(term, arrivals, piece, pieces, result, cost):
-    row_total, width = term.shape
+def finish(term, skip, arrived, offset, cols, result, cost):
+    row_total, width = arrived.shape
     height = min(row_total, 128)
     block = pl.BlockSpec((height, width), lambda i: (i, 0))
     held = [] if result is None else [result]
     return pl.pallas_call(
-        functools.partial(finish_kernel, len(arrivals)),
+        functools.partial(finish_kernel, 1),
         grid=(row_total // height,),
-        in_specs=[block] * (1 + len(arrivals)) + [pl.BlockSpec(memory_space=pl.ANY)] * len(held),
-        out_specs=pl.BlockSpec((height, width), lambda i: (i, piece)),
-        out_shape=jax.ShapeDtypeStruct((row_total, width * pieces), BF16),
-        input_output_aliases={1 + len(arrivals): 0} if held else {},
+        in_specs=[pl.BlockSpec((height, width), lambda i: (i, skip // width)), block]
+        + [pl.BlockSpec(memory_space=pl.ANY)] * len(held),
+        out_specs=pl.BlockSpec((height, width), lambda i: (i, offset // width)),
+        out_shape=jax.ShapeDtypeStruct((row_total, cols), BF16),
+        input_output_aliases={2: 0} if held else {},
         compiler_params=pltpu.CompilerParams(vmem_limit_bytes=VMEM_LIMIT),
         cost_estimate=cost,
         name="finish",
-    )(term, *arrivals, *held)
+    )(term, arrived, *held)
 
 
 def local(req_total, tp_total, rows, weight, down, up, table, ids, lens):
@@ -339,6 +342,10 @@
     def partial(back, piece, **options):
         return block_product(rows, weight, start_of(back, piece), width, **options)
 
+    def half_partial(back, piece, skip, **options):
+        first = start_of(back, piece) + skip
+        return block_product(rows, weight, first, width // 2, skip=skip, **options)
+
     last, rows = first_product(rows, weight, start_of(1, 0), width)
     rows = pltpu.with_memory_space_constraint(rows, pltpu.VMEM)
     moving = [move(last, 0)]
@@ -365,6 +372,14 @@
                     pairs = [(i, i ^ x) for i in range(tp_total)]
                     lows.append(lax.ppermute(low, "tp", pairs))
                 last = low
+            if step == steps - 1 and piece == PIECES - 1:
+                halves = []
+                for skip in (0, width // 2):
+                    last = half_partial(
+                        1 + step, piece, skip, addends=[moving[piece]], after=[last]
+                    )
+                    halves.append(move(last, piece))
+                break
             last = partial(1 + step, piece, addends=[moving[piece]], after=[last])
             moving[piece] = move(last, piece)
             if step == 1 and piece > 0:
@@ -372,11 +387,14 @@
                 owns.append(last)
 
     terms = adapter_term(starts, ends, lows, owns, packs, [last])
+    parts = [(piece, 0, moving[piece]) for piece in range(PIECES - 1)]
+    parts += [(PIECES - 1, skip, half) for skip, half in zip((0, width // 2), halves)]
     result = None
-    for piece in range(PIECES):
-        cost = SMALL if piece == PIECES - 1 else LARGE
-        arrived = pltpu.with_memory_space_constraint(moving[piece], pltpu.VMEM)
-        result = finish(terms[piece], [arrived], piece, PIECES, result, cost)
+    for piece, skip, arrived in parts:
+        arrived = pltpu.with_memory_space_constraint(arrived, pltpu.VMEM)
+        cost = LARGE if piece == 0 else SMALL
+        offset = piece * width + skip
+        result = finish(terms[piece], skip, arrived, offset, cols, result, cost)
     return result
 
 

time: 80.9 us -> 80.2 us (level)
  waiting for transfers between devices: 16.1 us -> 8.31 us
  starting transfers between devices: 27 us -> 32 us
  Pallas kernels: 36.1 us -> 38.2 us
    ppermute x6 -> x7, waiting for transfers between devices: 12.9 us -> 6.92 us  [move(): return lax.ppermute(value, ('req', 'tp'), pairs)]
    ppermute x6 -> x7, starting transfers between devices: 17.8 us -> 22.3 us  [move(): return lax.ppermute(value, ('req', 'tp'), pairs)]
    ppermute x3, waiting for transfers between devices: 3.23 us -> 1.37 us  [local(): lows.append(lax.ppermute(low, 'tp', pairs))]
    pallas_call x2 -> x3, Pallas kernels: 4.6 us -> 5.94 us  [finish(): pl.pallas_call(functools.partial(finish_kernel, 1), grid=(row_total // he...]
    pallas_call x7 -> x8, Pallas kernels: 21.5 us -> 22.6 us  [block_product(): pl.pallas_call(functools.partial(product_kernel, len(addends), with_ids),...]
  transfers between devices with their start and end apart: 15 -> 16, of which waited for: 6 -> 4; matrix products, arithmetic and copies ran while one was open for 0% -> 0% of each run, Pallas kernels for 39% -> 42%
where the time goes in v20:
time: 80.2 us; the launch traced here: 79.7 us
  Pallas kernels  38.2 us (48%)
  starting transfers between devices  32 us (40%)
  waiting for transfers between devices  8.31 us (10%)
  local copies, waits for them, and re-layouts  0.85 us (1%)
    pallas_call x8, Pallas kernels, block_product(): pl.pallas_call(functools.partial(product_kernel, len(addends), with_ids),...  22.6 us
    ppermute x7, starting transfers between devices, move(): return lax.ppermute(value, ('req', 'tp'), pairs)  22.3 us
    ppermute x7, waiting for transfers between devices, move(): return lax.ppermute(value, ('req', 'tp'), pairs)  6.92 us
    pallas_call x3, Pallas kernels, finish(): pl.pallas_call(functools.partial(finish_kernel, 1), grid=(row_total // he...  5.94 us
    ppermute x3, starting transfers between devices, local(): lows.append(lax.ppermute(low, 'tp', pairs))  5.32 us
    pallas_call x1, Pallas kernels, first_product(): pl.pallas_call(functools.partial(first_kernel, chunk), in_specs=[pl.Block...  3.49 us
    pallas_call x1, Pallas kernels, pick_adapters(): pl.pallas_call(functools.partial(pick_kernel, peers, len(after)), in_spec...  3.33 us
    ppermute x3, starting transfers between devices, local(): lax.ppermute(packs[x], 'req', [(i, i ^ x) for i in range(req_total)])  2.47 us
  transfers between devices with their start and end apart: 16, of which 4 were waited for; matrix products, arithmetic and copies ran while one was open for 0% of the time, Pallas kernels for 42%

profile of v20, /device:TPU:0, one launch (start us, length us, event | category | flops | bytes accessed | tf_op | source)
XLA Modules:
  0.0 79.7 jit_solution(10112776286531554608)
XLA Ops:
  0.0 3.5 %first_product.1 = (bf16[512,512]{1,0:T(8,128)(2,1)}, bf16[512,2048]{1,0:T(8,128)(2,1)S(1)}) custom-call(s32[1]{0:T(128)} %bitcast.2.first_ref, bf16[512,2048]{1,0:T(8,128)(2,1)} %rows_ref.1, bf16[2048,4096]{1,0:T(8,128)(2,1)} %weight_ref.17), custom_call_target="tpu_custom_call" | custom-call | flops 1000 | bytes 1000 | tf_op jit(solution)/shard_map/first_product/pallas_call | solution.py:98
  3.5 3.1 %collective-permute-start.6 = (bf16[512,512]{1,0:T(8,128)(2,1)}, bf16[512,512]{1,0:T(8,128)(2,1)}, u32[]{:S(2)}, u32[]{:S(2)}) collective-permute-start(bf16[512,512]{1,0:T(8,128)(2,1)} %get-tuple-element.18.rest_1_), channel_id=1, source_target_pairs={{0,1},{1,2},{2,3},{3,0},{4,7},{5,4},{6,5},{7,6},{8,9},{9,10},{10,1... | collective-permute-start | bytes 1572872 | tf_op jit(solution)/shard_map/ppermute | solution.py:335
  6.6 0.0 copy-done.9
  6.6 3.4 %block_product.8 = (bf16[512,512]{1,0:T(8,128)(2,1)}, s32[1,12]{1,0:T(1,128)S(1)}) custom-call(s32[1]{0:T(128)} %bitcast.1.first_ref, bf16[512,2048]{1,0:T(8,128)(2,1)S(1)} %get-tuple-element.17.rows_ref, bf16[2048,4096]{1,0:T(8,128)(2,1)} %weight_ref.17, s32[1,12]{1,0:T(1,128)S(1)} %copy-done.9, bf16[512,512]{1,0:T(8,128)(2,1)} %get-tuple-element.18.rest_1_), custom_call_target="tpu_custom_call" | custom-call | flops 1000 | bytes 1000 | tf_op jit(solution)/shard_map/block_product/pallas_call | solution.py:44
  10.0 2.1 %collective-permute-start.8 = (bf16[512,512]{1,0:T(8,128)(2,1)}, bf16[512,512]{1,0:T(8,128)(2,1)}, u32[]{:S(2)}, u32[]{:S(2)}) collective-permute-start(bf16[512,512]{1,0:T(8,128)(2,1)} %get-tuple-element.20.rest_0_), channel_id=1, source_target_pairs={{0,3},{1,0},{2,1},{3,2},{4,5},{5,6},{6,7},{7,4},{8,11},{9,8},{10,9... | collective-permute-start | bytes 1572872 | tf_op jit(solution)/shard_map/ppermute | solution.py:335
  12.1 0.0 collective-permute-start
  12.1 1.7 %collective-permute-start.1 = (s32[1,12]{1,0:T(1,128)S(1)}, s32[1,12]{1,0:T(1,128)S(1)}, u32[]{:S(2)}, u32[]{:S(2)}) collective-permute-start(s32[1,12]{1,0:T(1,128)S(1)} %get-tuple-element.19.rest_0_), channel_id=1, source_target_pairs={{0,8},{4,12},{8,0},{12,4},{1,9},{5,13},{9,1},{13,5},{2,10},{6,14},... | collective-permute-start | bytes 152 | tf_op jit(solution)/shard_map/ppermute | solution.py:358
  13.8 0.2 collective-permute-start.2
  14.0 2.7 %block_product.9.rest_6_.rest_4_ = bf16[512,512]{1,0:T(8,128)(2,1)S(1)} custom-call(s32[1]{0:T(128)} %bitcast.3.first_ref, bf16[512,2048]{1,0:T(8,128)(2,1)S(1)} %get-tuple-element.17.rows_ref, bf16[2048,4096]{1,0:T(8,128)(2,1)} %weight_ref.17, bf16[512,512]{1,0:T(8,128)(2,1)} %get-tuple-element.20.rest_0_), custom_call_target="tpu_custom_call" | custom-call | flops 1000 | bytes 1000 | tf_op jit(solution)/shard_map/block_product/pallas_call | solution.py:44
  16.8 0.0 collective-permute-done.rest_1_
  16.8 0.0 collective-permute-done.1.rest_2_
  16.8 0.0 collective-permute-done.2.rest_3_
  16.9 0.0 copy-done.8
  16.9 0.0 copy-done.10
  16.9 3.3 %pick_adapters.1 = (bf16[6,16,3072]{2,1,0:T(8,128)(2,1)S(1)}, bf16[6,16,3072]{2,1,0:T(8,128)(2,1)S(1)}, bf16[6,16,3072]{2,1,0:T(8,128)(2,1)S(1)}, bf16[6,16,3072...) custom-call(s32[1]{0:T(128)} %bitcast.me_ref, s32[512]{0:T(512)S(1)} %copy-done.8, s32[1,12]{1,0:T(1,128)S(1)} %copy-done.10, ...), custom_call_target="tpu_custom_call" | custom-call | flops 1000 | bytes 1000 | tf_op jit(solution)/shard_map/pick_adapters/pallas_call | solution.py:189
  20.2 1.0 %collective-permute-start.3 = (bf16[6,16,3072]{2,1,0:T(8,128)(2,1)S(1)}, bf16[6,16,3072]{2,1,0:T(8,128)(2,1)S(1)}, u32[]{:S(2)}, u32[]{:S(2)}) collective-permute-start(bf16[6,16,3072]{2,1,0:T(8,128)(2,1)S(1)} %get-tuple-element.24), channel_id=1, source_target_pairs={{0,4},{4,0},{8,12},{12,8},{1,5},{5,1},{9,13},{13,9},{2,6},{6,2},{1... | collective-permute-start | bytes 1769480 | tf_op jit(solution)/shard_map/ppermute | solution.py:363
  21.3 1.1 %collective-permute-start.4 = (bf16[6,16,3072]{2,1,0:T(8,128)(2,1)S(1)}, bf16[6,16,3072]{2,1,0:T(8,128)(2,1)S(1)}, u32[]{:S(2)}, u32[]{:S(2)}) collective-permute-start(bf16[6,16,3072]{2,1,0:T(8,128)(2,1)S(1)} %get-tuple-element.25), channel_id=1, source_target_pairs={{0,8},{4,12},{8,0},{12,4},{1,9},{5,13},{9,1},{13,5},{2,10},{6,14},... | collective-permute-start | bytes 1769480 | tf_op jit(solution)/shard_map/ppermute | solution.py:363
  22.4 0.3 collective-permute-start.5
  22.7 0.0 collective-permute-done.6.rest_0_
  22.7 2.8 %block_product.10.rest_1_ = bf16[512,512]{1,0:T(8,128)(2,1)S(1)} custom-call(s32[1]{0:T(128)} %bitcast.5.first_ref, bf16[512,2048]{1,0:T(8,128)(2,1)S(1)} %get-tuple-element.17.rows_ref, bf16[2048,4096]{1,0:T(8,128)(2,1)} %weight_ref.17, bf16[512,512]{1,0:T(8,128)(2,1)} %collective-permute-done.6.rest_0_, s32[24]{0:T(128)S(1)} %get-tuple-element.21.rest_1_.start_ref), custom_call_target="tpu_custom_call" | custom-call | flops 1000 | bytes 1000 | tf_op jit(solution)/shard_map/block_product/pallas_call | solution.py:44
  25.5 6.5 %collective-permute-start.7 = (bf16[512,512]{1,0:T(8,128)(2,1)S(1)}, bf16[512,512]{1,0:T(8,128)(2,1)S(1)}, u32[]{:S(2)}, u32[]{:S(2)}) collective-permute-start(bf16[512,512]{1,0:T(8,128)(2,1)S(1)} %block_product.10.rest_1_), channel_id=1, source_target_pairs={{0,1},{1,2},{2,3},{3,0},{4,7},{5,4},{6,5},{7,6},{8,9},{9,10},{10,1... | collective-permute-start | bytes 1572872 | tf_op jit(solution)/shard_map/ppermute | solution.py:335
  32.0 0.0 collective-permute-done.8.rest_0_
  32.0 3.5 %block_product.11.rest_0_ = bf16[512,512]{1,0:T(8,128)(2,1)} custom-call(s32[1]{0:T(128)} %bitcast.7.first_ref, bf16[512,2048]{1,0:T(8,128)(2,1)S(1)} %get-tuple-element.17.rows_ref, bf16[2048,4096]{1,0:T(8,128)(2,1)} %weight_ref.17, bf16[512,512]{1,0:T(8,128)(2,1)} %collective-permute-done.8.rest_0_, bf16[512,512]{1,0:T(8,128)(2,1)S(1)} %block_product.10.rest_1_), custom_call_target="tpu_custom_call" | custom-call | flops 1000 | bytes 1000 | tf_op jit(solution)/shard_map/block_product/pallas_call | solution.py:44
  35.4 3.7 %collective-permute-start.12 = (bf16[512,512]{1,0:T(8,128)(2,1)}, bf16[512,512]{1,0:T(8,128)(2,1)}, u32[]{:S(2)}, u32[]{:S(2)}) collective-permute-start(bf16[512,512]{1,0:T(8,128)(2,1)} %block_product.11.rest_0_), channel_id=1, source_target_pairs={{0,3},{1,0},{2,1},{3,2},{4,5},{5,6},{6,7},{7,4},{8,11},{9,8},{10,9... | collective-permute-start | bytes 1572872 | tf_op jit(solution)/shard_map/ppermute | solution.py:335
  39.1 2.7 %block_product.12.rest_1_.rest_5_ = bf16[512,512]{1,0:T(8,128)(2,1)S(1)} custom-call(s32[1]{0:T(128)} %bitcast.6.first_ref, bf16[512,2048]{1,0:T(8,128)(2,1)S(1)} %get-tuple-element.17.rows_ref, bf16[2048,4096]{1,0:T(8,128)(2,1)} %weight_ref.17, bf16[512,512]{1,0:T(8,128)(2,1)} %block_product.11.rest_0_), custom_call_target="tpu_custom_call" | custom-call | flops 20000000000 | bytes 1000 | tf_op jit(solution)/shard_map/block_product/pallas_call | solution.py:44
  41.8 0.0 copy-start.6
  41.8 2.6 %collective-permute-done.7.rest_0_ = bf16[512,512]{1,0:T(8,128)(2,1)S(1)} collective-permute-done((bf16[512,512]{1,0:T(8,128)(2,1)S(1)}, bf16[512,512]{1,0:T(8,128)(2,1)S(1)}, u32[]{:S(2)}, u32[]{:S(2)}) %collective-permute-start.7) | collective-permute-done | bytes 524320 | tf_op jit(solution)/shard_map/ppermute | solution.py:335
  44.4 3.4 %block_product.13.rest_4_ = bf16[512,512]{1,0:T(8,128)(2,1)} custom-call(s32[1]{0:T(128)} %bitcast.4.first_ref, bf16[512,2048]{1,0:T(8,128)(2,1)S(1)} %get-tuple-element.17.rows_ref, bf16[2048,4096]{1,0:T(8,128)(2,1)} %weight_ref.17, bf16[512,512]{1,0:T(8,128)(2,1)S(1)} %collective-permute-done.7.rest_0_, bf16[512,512]{1,0:T(8,128)(2,1)S(1)} %block_product.12.rest_1_.rest_5_), custom_call_target="tpu_custom_call" | custom-call | flops 1000 | bytes 1000 | tf_op jit(solution)/shard_map/block_product/pallas_call | solution.py:44
  47.8 0.0 copy-done.6
  47.8 2.4 %collective-permute-start.15 = (bf16[512,512]{1,0:T(8,128)(2,1)}, bf16[512,512]{1,0:T(8,128)(2,1)}, u32[]{:S(2)}, u32[]{:S(2)}) collective-permute-start(bf16[512,512]{1,0:T(8,128)(2,1)} %block_product.13.rest_4_), channel_id=1, source_target_pairs={{0,1},{1,2},{2,3},{3,0},{4,7},{5,4},{6,5},{7,6},{8,9},{9,10},{10,1... | collective-permute-start | bytes 1572872 | tf_op jit(solution)/shard_map/ppermute | solution.py:335
  50.2 0.0 collective-permute-done.3.rest_1_.rest_7_
  50.2 0.0 collective-permute-done.4.rest_2_.rest_8_
  50.2 0.0 collective-permute-done.5.rest_3_.rest_9_
  50.3 0.0 copy-start.4
  50.3 1.6 %low_sums.1.rest_1_.rest_0_ = bf16[16,512]{1,0:T(8,128)(2,1)S(1)} custom-call(s32[24]{0:T(128)S(1)} %get-tuple-element.21.rest_1_.start_ref, s32[24]{0:T(128)S(1)} %get-tuple-element.22.end_ref, bf16[512,2048]{1,0:T(8,128)(2,1)S(1)} %get-tuple-element.17.rows_ref, bf16[6,16,3072]{2,1,0:T(8,128)(2,1)S(1)} %get-tuple-element.23.rest_0_.rest_6_, ...), custom_call_target="tpu_custom_call" | custom-call | flops 1000 | bytes 1000 | tf_op jit(solution)/shard_map/low_sums/pallas_call | solution.py:231
  51.8 0.0 copy-done.2
  51.8 0.0 copy-start
  51.8 0.8 %copy-done = bf16[6,16,3072]{2,1,0:T(8,128)(2,1)} copy-done((bf16[6,16,3072]{2,1,0:T(8,128)(2,1)}, bf16[6,16,3072]{2,1,0:T(8,128)(2,1)S(1)}, u32[]{:S(2)}) %copy-start) | copy-done | bytes 589848
  52.6 2.8 %collective-permute-start.9 = (bf16[16,512]{1,0:T(8,128)(2,1)S(1)}, bf16[16,512]{1,0:T(8,128)(2,1)S(1)}, u32[]{:S(2)}, u32[]{:S(2)}) collective-permute-start(bf16[16,512]{1,0:T(8,128)(2,1)S(1)} %low_sums.1.rest_1_.rest_0_), channel_id=1, source_target_pairs={{0,1},{1,0},{2,3},{3,2},{4,5},{5,4},{6,7},{7,6},{8,9},{9,8},{10,11... | collective-permute-start | bytes 49160 | tf_op jit(solution)/shard_map/ppermute | solution.py:373
  55.4 0.0 copy-done.4
  55.4 1.1 %collective-permute-start.10 = (bf16[16,512]{1,0:T(8,128)(2,1)S(1)}, bf16[16,512]{1,0:T(8,128)(2,1)S(1)}, u32[]{:S(2)}, u32[]{:S(2)}) collective-permute-start(bf16[16,512]{1,0:T(8,128)(2,1)S(1)} %low_sums.1.rest_1_.rest_0_), channel_id=1, source_target_pairs={{0,2},{1,3},{2,0},{3,1},{4,6},{5,7},{6,4},{7,5},{8,10},{9,11},{10,... | collective-permute-start | bytes 49160 | tf_op jit(solution)/shard_map/ppermute | solution.py:373
  56.5 1.4 %collective-permute-start.11 = (bf16[16,512]{1,0:T(8,128)(2,1)S(1)}, bf16[16,512]{1,0:T(8,128)(2,1)S(1)}, u32[]{:S(2)}, u32[]{:S(2)}) collective-permute-start(bf16[16,512]{1,0:T(8,128)(2,1)S(1)} %low_sums.1.rest_1_.rest_0_), channel_id=1, source_target_pairs={{0,3},{1,2},{2,1},{3,0},{4,7},{5,6},{6,5},{7,4},{8,11},{9,10},{10,... | collective-permute-start | bytes 49160 | tf_op jit(solution)/shard_map/ppermute | solution.py:373
  58.0 3.6 %collective-permute-done.12.rest_0_ = bf16[512,512]{1,0:T(8,128)(2,1)} collective-permute-done((bf16[512,512]{1,0:T(8,128)(2,1)}, bf16[512,512]{1,0:T(8,128)(2,1)}, u32[]{:S(2)}, u32[]{:S(2)}) %collective-permute-start.12) | collective-permute-done | bytes 524320 | tf_op jit(solution)/shard_map/ppermute | solution.py:335
  61.6 2.0 %block_product.14.rest_1_ = bf16[512,256]{1,0:T(8,128)(2,1)S(1)} custom-call(s32[1]{0:T(128)} %bitcast.9.first_ref, bf16[512,2048]{1,0:T(8,128)(2,1)S(1)} %get-tuple-element.17.rows_ref, bf16[2048,4096]{1,0:T(8,128)(2,1)} %weight_ref.17, bf16[512,512]{1,0:T(8,128)(2,1)} %collective-permute-done.12.rest_0_, bf16[16,512]{1,0:T(8,128)(2,1)S(1)} %low_sums.1.rest_1_.rest_0_), custom_call_target="tpu_custom_call" | custom-call | flops 1000 | bytes 1000 | tf_op jit(solution)/shard_map/block_product/pallas_call | solution.py:44
  63.6 0.1 collective-permute-start.14
  63.7 0.0 copy-start.1
  63.7 0.0 copy-start.3
  63.7 0.0 copy-start.5
  63.7 0.0 copy-start.7
  63.7 2.1 %block_product.15.rest_10_ = bf16[512,256]{1,0:T(8,128)(2,1)S(1)} custom-call(s32[1]{0:T(128)} %bitcast.8.first_ref, bf16[512,2048]{1,0:T(8,128)(2,1)S(1)} %get-tuple-element.17.rows_ref, bf16[2048,4096]{1,0:T(8,128)(2,1)} %weight_ref.17, bf16[512,512]{1,0:T(8,128)(2,1)} %collective-permute-done.12.rest_0_, bf16[512,256]{1,0:T(8,128)(2,1)S(1)} %block_product.14.rest_1_), custom_call_target="tpu_custom_call" | custom-call | flops 1000 | bytes 1000 | tf_op jit(solution)/shard_map/block_product/pallas_call | solution.py:44
  65.8 1.4 %collective-permute-done.9.rest_1_ = bf16[16,512]{1,0:T(8,128)(2,1)S(1)} collective-permute-done((bf16[16,512]{1,0:T(8,128)(2,1)S(1)}, bf16[16,512]{1,0:T(8,128)(2,1)S(1)}, u32[]{:S(2)}, u32[]{:S(2)}) %collective-permute-start.9) | collective-permute-done | bytes 16416 | tf_op jit(solution)/shard_map/ppermute | solution.py:373
  67.2 4.5 %collective-permute-start.13 = (bf16[512,256]{1,0:T(8,128)(2,1)S(1)}, bf16[512,256]{1,0:T(8,128)(2,1)S(1)}, u32[]{:S(2)}, u32[]{:S(2)}) collective-permute-start(bf16[512,256]{1,0:T(8,128)(2,1)S(1)} %block_product.15.rest_10_), channel_id=1, source_target_pairs={{0,3},{1,0},{2,1},{3,2},{4,5},{5,6},{6,7},{7,4},{8,11},{9,8},{10,9... | collective-permute-start | bytes 786440 | tf_op jit(solution)/shard_map/ppermute | solution.py:335
  71.7 0.0 collective-permute-done.10.rest_2_
  71.7 0.0 collective-permute-done.11.rest_3_
  71.7 0.0 copy-done.1
  71.7 0.0 copy-done.3
  71.7 0.0 copy-done.5
  71.8 1.3 %adapter_term.1 = (f32[512,512]{1,0:T(8,128)S(1)}, f32[512,512]{1,0:T(8,128)S(1)}) custom-call(s32[24]{0:T(128)S(1)} %get-tuple-element.21.rest_1_.start_ref, s32[24]{0:T(128)S(1)} %get-tuple-element.22.end_ref, bf16[16,512]{1,0:T(8,128)(2,1)S(1)} %low_sums.1.rest_1_.rest_0_, bf16[16,512]{1,0:T(8,128)(2,1)S(1)} %collective-permute-done.9.rest_1_, ...), custom_call_target="tpu_custom_call" | custom-call | flops 1000 | bytes 1000 | tf_op jit(solution)/shard_map/adapter_term/pallas_call | solution.py:277
  73.0 0.0 collective-permute-done.15.rest_0_
  73.1 3.2 %finish.3.rest_1_ = bf16[512,1024]{1,0:T(8,128)(2,1)} custom-call(f32[512,512]{1,0:T(8,128)S(1)} %get-tuple-element.28.term_ref, bf16[512,512]{1,0:T(8,128)(2,1)} %collective-permute-done.15.rest_0_), custom_call_target="tpu_custom_call" | custom-call | flops 20000000000 | bytes 1000 | tf_op jit(solution)/shard_map/finish/pallas_call | solution.py:304
  76.2 0.0 collective-permute-done.14.rest_0_
  76.3 1.4 %finish.4.rest_1_ = bf16[512,1024]{1,0:T(8,128)(2,1)} custom-call(f32[512,512]{1,0:T(8,128)S(1)} %get-tuple-element.27.term_ref, bf16[512,256]{1,0:T(8,128)(2,1)S(1)} %collective-permute-done.14.rest_0_, bf16[512,1024]{1,0:T(8,128)(2,1)} %finish.3.rest_1_), custom_call_target="tpu_custom_call", output_to_operand_aliasing={{}: (2, {})} | custom-call | flops 1000 | bytes 1000 | tf_op jit(solution)/shard_map/finish/pallas_call | solution.py:304
  77.6 0.7 collective-permute-done.13.rest_0_
  78.3 1.4 %finish.5 = bf16[512,1024]{1,0:T(8,128)(2,1)} custom-call(f32[512,512]{1,0:T(8,128)S(1)} %get-tuple-element.27.term_ref, bf16[512,256]{1,0:T(8,128)(2,1)S(1)} %collective-permute-done.13.rest_0_, bf16[512,1024]{1,0:T(8,128)(2,1)} %finish.4.rest_1_), custom_call_target="tpu_custom_call", output_to_operand_aliasing={{}: (2, {})} | custom-call | flops 1000 | bytes 1000 | tf_op jit(solution)/shard_map/finish/pallas_call | solution.py:304
  (5 shorter events, 0.0 us)
Async XLA Ops:
  0.0 6.6 %copy-start.9 = (s32[1,12]{1,0:T(1,128)S(1)}, s32[1,12]{1,0:T(1,128)}, u32[]{:S(2)}) copy-start(s32[1,12]{1,0:T(1,128)} %rest_0_.1) | copy-start | bytes 148
  3.5 19.2 %collective-permute-start.6 = (bf16[512,512]{1,0:T(8,128)(2,1)}, bf16[512,512]{1,0:T(8,128)(2,1)}, u32[]{:S(2)}, u32[]{:S(2)}) collective-permute-start(bf16[512,512]{1,0:T(8,128)(2,1)} %get-tuple-element.18.rest_1_), channel_id=1, source_target_pairs={{0,1},{1,2},{2,3},{3,0},{4,7},{5,4},{6,5},{7,6},{8,9},{9,10},{10,1... | collective-permute-start | bytes 1572872 | tf_op jit(solution)/shard_map/ppermute | solution.py:335
  10.0 21.9 %collective-permute-start.8 = (bf16[512,512]{1,0:T(8,128)(2,1)}, bf16[512,512]{1,0:T(8,128)(2,1)}, u32[]{:S(2)}, u32[]{:S(2)}) collective-permute-start(bf16[512,512]{1,0:T(8,128)(2,1)} %get-tuple-element.20.rest_0_), channel_id=1, source_target_pairs={{0,3},{1,0},{2,1},{3,2},{4,5},{5,6},{6,7},{7,4},{8,11},{9,8},{10,9... | collective-permute-start | bytes 1572872 | tf_op jit(solution)/shard_map/ppermute | solution.py:335
  12.1 4.7 %collective-permute-start = (s32[1,12]{1,0:T(1,128)S(1)}, s32[1,12]{1,0:T(1,128)S(1)}, u32[]{:S(2)}, u32[]{:S(2)}) collective-permute-start(s32[1,12]{1,0:T(1,128)S(1)} %get-tuple-element.19.rest_0_), channel_id=1, source_target_pairs={{0,4},{4,0},{8,12},{12,8},{1,5},{5,1},{9,13},{13,9},{2,6},{6,2},{1... | collective-permute-start | bytes 152 | tf_op jit(solution)/shard_map/ppermute | solution.py:358
  12.1 4.7 %collective-permute-start.1 = (s32[1,12]{1,0:T(1,128)S(1)}, s32[1,12]{1,0:T(1,128)S(1)}, u32[]{:S(2)}, u32[]{:S(2)}) collective-permute-start(s32[1,12]{1,0:T(1,128)S(1)} %get-tuple-element.19.rest_0_), channel_id=1, source_target_pairs={{0,8},{4,12},{8,0},{12,4},{1,9},{5,13},{9,1},{13,5},{2,10},{6,14},... | collective-permute-start | bytes 152 | tf_op jit(solution)/shard_map/ppermute | solution.py:358
  13.8 3.1 %collective-permute-start.2 = (s32[1,12]{1,0:T(1,128)S(1)}, s32[1,12]{1,0:T(1,128)S(1)}, u32[]{:S(2)}, u32[]{:S(2)}) collective-permute-start(s32[1,12]{1,0:T(1,128)S(1)} %get-tuple-element.19.rest_0_), channel_id=1, source_target_pairs={{0,12},{4,8},{8,4},{12,0},{1,13},{5,9},{9,5},{13,1},{2,14},{6,10},... | collective-permute-start | bytes 152 | tf_op jit(solution)/shard_map/ppermute | solution.py:358
  14.0 2.9 %copy-start.8 = (s32[512]{0:T(512)S(1)}, s32[512]{0:T(512)}, u32[]{:S(2)}) copy-start(s32[512]{0:T(512)} %table_ref.1) | copy-start | bytes 6148
  14.0 2.9 %copy-start.10 = (s32[1,12]{1,0:T(1,128)S(1)}, s32[1,12]{1,0:T(1,128)}, u32[]{:S(2)}) copy-start(s32[1,12]{1,0:T(1,128)} %lens_ref.1) | copy-start | bytes 148
  20.2 30.0 %collective-permute-start.3 = (bf16[6,16,3072]{2,1,0:T(8,128)(2,1)S(1)}, bf16[6,16,3072]{2,1,0:T(8,128)(2,1)S(1)}, u32[]{:S(2)}, u32[]{:S(2)}) collective-permute-start(bf16[6,16,3072]{2,1,0:T(8,128)(2,1)S(1)} %get-tuple-element.24), channel_id=1, source_target_pairs={{0,4},{4,0},{8,12},{12,8},{1,5},{5,1},{9,13},{13,9},{2,6},{6,2},{1... | collective-permute-start | bytes 1769480 | tf_op jit(solution)/shard_map/ppermute | solution.py:363
  21.3 29.0 %collective-permute-start.4 = (bf16[6,16,3072]{2,1,0:T(8,128)(2,1)S(1)}, bf16[6,16,3072]{2,1,0:T(8,128)(2,1)S(1)}, u32[]{:S(2)}, u32[]{:S(2)}) collective-permute-start(bf16[6,16,3072]{2,1,0:T(8,128)(2,1)S(1)} %get-tuple-element.25), channel_id=1, source_target_pairs={{0,8},{4,12},{8,0},{12,4},{1,9},{5,13},{9,1},{13,5},{2,10},{6,14},... | collective-permute-start | bytes 1769480 | tf_op jit(solution)/shard_map/ppermute | solution.py:363
  22.4 27.9 %collective-permute-start.5 = (bf16[6,16,3072]{2,1,0:T(8,128)(2,1)S(1)}, bf16[6,16,3072]{2,1,0:T(8,128)(2,1)S(1)}, u32[]{:S(2)}, u32[]{:S(2)}) collective-permute-start(bf16[6,16,3072]{2,1,0:T(8,128)(2,1)S(1)} %get-tuple-element.26), channel_id=1, source_target_pairs={{0,12},{4,8},{8,4},{12,0},{1,13},{5,9},{9,5},{13,1},{2,14},{6,10},... | collective-permute-start | bytes 1769480 | tf_op jit(solution)/shard_map/ppermute | solution.py:363
  25.5 19.0 %collective-permute-start.7 = (bf16[512,512]{1,0:T(8,128)(2,1)S(1)}, bf16[512,512]{1,0:T(8,128)(2,1)S(1)}, u32[]{:S(2)}, u32[]{:S(2)}) collective-permute-start(bf16[512,512]{1,0:T(8,128)(2,1)S(1)} %block_product.10.rest_1_), channel_id=1, source_target_pairs={{0,1},{1,2},{2,3},{3,0},{4,7},{5,4},{6,5},{7,6},{8,9},{9,10},{10,1... | collective-permute-start | bytes 1572872 | tf_op jit(solution)/shard_map/ppermute | solution.py:335
  35.4 26.1 %collective-permute-start.12 = (bf16[512,512]{1,0:T(8,128)(2,1)}, bf16[512,512]{1,0:T(8,128)(2,1)}, u32[]{:S(2)}, u32[]{:S(2)}) collective-permute-start(bf16[512,512]{1,0:T(8,128)(2,1)} %block_product.11.rest_0_), channel_id=1, source_target_pairs={{0,3},{1,0},{2,1},{3,2},{4,5},{5,6},{6,7},{7,4},{8,11},{9,8},{10,9... | collective-permute-start | bytes 1572872 | tf_op jit(solution)/shard_map/ppermute | solution.py:335
  41.8 6.0 %copy-start.6 = (bf16[512,512]{1,0:T(8,128)(2,1)}, bf16[512,512]{1,0:T(8,128)(2,1)S(1)}, u32[]{:S(2)}) copy-start(bf16[512,512]{1,0:T(8,128)(2,1)S(1)} %block_product.12.rest_1_.rest_5_) | copy-start | bytes 1572868
  47.8 25.2 %collective-permute-start.15 = (bf16[512,512]{1,0:T(8,128)(2,1)}, bf16[512,512]{1,0:T(8,128)(2,1)}, u32[]{:S(2)}, u32[]{:S(2)}) collective-permute-start(bf16[512,512]{1,0:T(8,128)(2,1)} %block_product.13.rest_4_), channel_id=1, source_target_pairs={{0,1},{1,2},{2,3},{3,0},{4,7},{5,4},{6,5},{7,6},{8,9},{9,10},{10,1... | collective-permute-start | bytes 1572872 | tf_op jit(solution)/shard_map/ppermute | solution.py:335
  50.2 1.6 %copy-start.2 = (bf16[6,16,3072]{2,1,0:T(8,128)(2,1)}, bf16[6,16,3072]{2,1,0:T(8,128)(2,1)S(1)}, u32[]{:S(2)}) copy-start(bf16[6,16,3072]{2,1,0:T(8,128)(2,1)S(1)} %collective-permute-done.4.rest_2_.rest_8_) | copy-start | bytes 1769476
  50.3 5.2 %copy-start.4 = (bf16[6,16,3072]{2,1,0:T(8,128)(2,1)}, bf16[6,16,3072]{2,1,0:T(8,128)(2,1)S(1)}, u32[]{:S(2)}) copy-start(bf16[6,16,3072]{2,1,0:T(8,128)(2,1)S(1)} %collective-permute-done.5.rest_3_.rest_9_) | copy-start | bytes 1769476
  51.8 0.8 %copy-start = (bf16[6,16,3072]{2,1,0:T(8,128)(2,1)}, bf16[6,16,3072]{2,1,0:T(8,128)(2,1)S(1)}, u32[]{:S(2)}) copy-start(bf16[6,16,3072]{2,1,0:T(8,128)(2,1)S(1)} %collective-permute-done.3.rest_1_.rest_7_) | copy-start | bytes 1769476
  52.6 14.6 %collective-permute-start.9 = (bf16[16,512]{1,0:T(8,128)(2,1)S(1)}, bf16[16,512]{1,0:T(8,128)(2,1)S(1)}, u32[]{:S(2)}, u32[]{:S(2)}) collective-permute-start(bf16[16,512]{1,0:T(8,128)(2,1)S(1)} %low_sums.1.rest_1_.rest_0_), channel_id=1, source_target_pairs={{0,1},{1,0},{2,3},{3,2},{4,5},{5,4},{6,7},{7,6},{8,9},{9,8},{10,11... | collective-permute-start | bytes 49160 | tf_op jit(solution)/shard_map/ppermute | solution.py:373
  55.4 16.3 %collective-permute-start.10 = (bf16[16,512]{1,0:T(8,128)(2,1)S(1)}, bf16[16,512]{1,0:T(8,128)(2,1)S(1)}, u32[]{:S(2)}, u32[]{:S(2)}) collective-permute-start(bf16[16,512]{1,0:T(8,128)(2,1)S(1)} %low_sums.1.rest_1_.rest_0_), channel_id=1, source_target_pairs={{0,2},{1,3},{2,0},{3,1},{4,6},{5,7},{6,4},{7,5},{8,10},{9,11},{10,... | collective-permute-start | bytes 49160 | tf_op jit(solution)/shard_map/ppermute | solution.py:373
  56.5 15.2 %collective-permute-start.11 = (bf16[16,512]{1,0:T(8,128)(2,1)S(1)}, bf16[16,512]{1,0:T(8,128)(2,1)S(1)}, u32[]{:S(2)}, u32[]{:S(2)}) collective-permute-start(bf16[16,512]{1,0:T(8,128)(2,1)S(1)} %low_sums.1.rest_1_.rest_0_), channel_id=1, source_target_pairs={{0,3},{1,2},{2,1},{3,0},{4,7},{5,6},{6,5},{7,4},{8,11},{9,10},{10,... | collective-permute-start | bytes 49160 | tf_op jit(solution)/shard_map/ppermute | solution.py:373
  63.6 12.7 %collective-permute-start.14 = (bf16[512,256]{1,0:T(8,128)(2,1)S(1)}, bf16[512,256]{1,0:T(8,128)(2,1)S(1)}, u32[]{:S(2)}, u32[]{:S(2)}) collective-permute-start(bf16[512,256]{1,0:T(8,128)(2,1)S(1)} %block_product.14.rest_1_), channel_id=1, source_target_pairs={{0,3},{1,0},{2,1},{3,2},{4,5},{5,6},{6,7},{7,4},{8,11},{9,8},{10,9... | collective-permute-start | bytes 786440 | tf_op jit(solution)/shard_map/ppermute | solution.py:335
  63.7 8.1 %copy-start.1 = (bf16[6,16,3072]{2,1,0:T(8,128)(2,1)S(1)}, bf16[6,16,3072]{2,1,0:T(8,128)(2,1)}, u32[]{:S(2)}) copy-start(bf16[6,16,3072]{2,1,0:T(8,128)(2,1)} %copy-done) | copy-start | bytes 1769476
  63.7 8.1 %copy-start.3 = (bf16[6,16,3072]{2,1,0:T(8,128)(2,1)S(1)}, bf16[6,16,3072]{2,1,0:T(8,128)(2,1)}, u32[]{:S(2)}) copy-start(bf16[6,16,3072]{2,1,0:T(8,128)(2,1)} %copy-done.2) | copy-start | bytes 1769476
  63.7 8.1 %copy-start.5 = (bf16[6,16,3072]{2,1,0:T(8,128)(2,1)S(1)}, bf16[6,16,3072]{2,1,0:T(8,128)(2,1)}, u32[]{:S(2)}) copy-start(bf16[6,16,3072]{2,1,0:T(8,128)(2,1)} %copy-done.4) | copy-start | bytes 1769476
  63.7 8.1 %copy-start.7 = (bf16[512,512]{1,0:T(8,128)(2,1)S(1)}, bf16[512,512]{1,0:T(8,128)(2,1)}, u32[]{:S(2)}) copy-start(bf16[512,512]{1,0:T(8,128)(2,1)} %copy-done.6) | copy-start | bytes 1572868
  67.2 11.1 %collective-permute-start.13 = (bf16[512,256]{1,0:T(8,128)(2,1)S(1)}, bf16[512,256]{1,0:T(8,128)(2,1)S(1)}, u32[]{:S(2)}, u32[]{:S(2)}) collective-permute-start(bf16[512,256]{1,0:T(8,128)(2,1)S(1)} %block_product.15.rest_10_), channel_id=1, source_target_pairs={{0,3},{1,0},{2,1},{3,2},{4,5},{5,6},{6,7},{7,4},{8,11},{9,8},{10,9... | collective-permute-start | bytes 786440 | tf_op jit(solution)/shard_map/ppermute | solution.py:335

commit v21 on v20

--- a/solution.py
+++ b/solution.py
@@ -17,15 +17,24 @@
 
 
 def product_kernel(addends, with_ids, first_ref, rows_ref, weight_ref, *rest):
-    out_ref = rest[-1 - with_ids]
+    if with_ids:
+        out_ref, ids_out_ref, sem = rest[-3:]
+        ids_copy = pltpu.make_async_copy(rest[addends], ids_out_ref, sem)
+
+        @pl.when(pl.program_id(0) == 0)
+        def _():
+            ids_copy.start()
+    else:
+        out_ref = rest[-1]
     total = jnp.dot(rows_ref[...], weight_ref[...], preferred_element_type=F32)
     for ref in rest[:addends]:
         total = total + ref[...].astype(F32)
     out_ref[...] = total.astype(out_ref.dtype)
     if with_ids:
-        ids_ref, ids_out_ref = rest[addends], rest[-1]
-        for s in range(ids_ref.shape[1]):
-            ids_out_ref[0, s] = ids_ref[0, s]
+
+        @pl.when(pl.program_id(0) == pl.num_programs(0) - 1)
+        def _():
+            ids_copy.wait()
 
 
 def block_product(
@@ -39,7 +48,7 @@
     columns = pl.BlockSpec((row_total, tile), lambda j, t: (0, j))
     out_specs, out_shape = [columns], [jax.ShapeDtypeStruct((row_total, width), BF16)]
     if with_ids:
-        out_specs.append(smem)
+        out_specs.append(hbm)
         out_shape.append(jax.ShapeDtypeStruct(ids.shape, ids.dtype))
     out = pl.pallas_call(
         functools.partial(product_kernel, len(addends), with_ids),
@@ -51,9 +60,10 @@
                 pl.BlockSpec((depth, tile), lambda j, t: (0, t[0] + j)),
             ]
             + [pl.BlockSpec((row_total, tile), lambda j, t: (0, skip // tile + j))] * len(addends)
-            + [smem] * with_ids
+            + [hbm] * with_ids
             + [hbm] * len(after),
             out_specs=out_specs,
+            scratch_shapes=[pltpu.SemaphoreType.DMA] if with_ids else [],
         ),
         out_shape=out_shape,
         compiler_params=pltpu.CompilerParams(vmem_limit_bytes=VMEM_LIMIT),
@@ -298,7 +308,7 @@
 
 def finish(term, skip, arrived, offset, cols, result, cost):
     row_total, width = arrived.shape
-    height = min(row_total, 128)
+    height = min(row_total, 256)
     block = pl.BlockSpec((height, width), lambda i: (i, 0))
     held = [] if result is None else [result]
     return pl.pallas_call(

time: 80.2 us -> 79.5 us (level)
  Pallas kernels: 38.2 us -> 35.5 us
  waiting for transfers between devices: 8.31 us -> 10.2 us
    pallas_call x3, Pallas kernels: 5.94 us -> 3.38 us  [finish(): pl.pallas_call(functools.partial(finish_kernel, 1), grid=(row_total // he...]
    ppermute x7, waiting for transfers between devices: 6.92 us -> 8.85 us  [move(): return lax.ppermute(value, ('req', 'tp'), pairs)]
  transfers between devices with their start and end apart: 16 -> 16, of which waited for: 4 -> 4; matrix products, arithmetic and copies ran while one was open for 0% -> 0% of each run, Pallas kernels for 42% -> 39%
where the time goes in v21:
time: 79.5 us; the launch traced here: 79.1 us
  Pallas kernels  35.5 us (45%)
  starting transfers between devices  32.3 us (41%)
  waiting for transfers between devices  10.2 us (13%)
  local copies, waits for them, and re-layouts  0.85 us (1%)
    pallas_call x8, Pallas kernels, block_product(): pl.pallas_call(functools.partial(product_kernel, len(addends), with_ids),...  22.6 us
    ppermute x7, starting transfers between devices, move(): return lax.ppermute(value, ('req', 'tp'), pairs)  22.3 us
    ppermute x7, waiting for transfers between devices, move(): return lax.ppermute(value, ('req', 'tp'), pairs)  8.85 us
    ppermute x3, starting transfers between devices, local(): lows.append(lax.ppermute(low, 'tp', pairs))  5.5 us
    pallas_call x1, Pallas kernels, first_product(): pl.pallas_call(functools.partial(first_kernel, chunk), in_specs=[pl.Block...  3.49 us
    pallas_call x3, Pallas kernels, finish(): pl.pallas_call(functools.partial(finish_kernel, 1), grid=(row_total // he...  3.38 us
    pallas_call x1, Pallas kernels, pick_adapters(): pl.pallas_call(functools.partial(pick_kernel, peers, len(after)), in_spec...  3.14 us
    ppermute x3, starting transfers between devices, local(): lax.ppermute(packs[x], 'req', [(i, i ^ x) for i in range(req_total)])  2.59 us
  transfers between devices with their start and end apart: 16, of which 4 were waited for; matrix products, arithmetic and copies ran while one was open for 0% of the time, Pallas kernels for 39%

profile of v21, /device:TPU:0, one launch (start us, length us, event | category | flops | bytes accessed | tf_op | source)
XLA Modules:
  0.0 79.1 jit_solution(15620474848403871024)
XLA Ops:
  0.0 3.5 %first_product.1 = (bf16[512,512]{1,0:T(8,128)(2,1)}, bf16[512,2048]{1,0:T(8,128)(2,1)S(1)}) custom-call(s32[1]{0:T(128)} %bitcast.2.first_ref, bf16[512,2048]{1,0:T(8,128)(2,1)} %rows_ref.1, bf16[2048,4096]{1,0:T(8,128)(2,1)} %weight_ref.17), custom_call_target="tpu_custom_call" | custom-call | flops 1000 | bytes 1000 | tf_op jit(solution)/shard_map/first_product/pallas_call | solution.py:108
  3.5 3.1 %collective-permute-start.6 = (bf16[512,512]{1,0:T(8,128)(2,1)}, bf16[512,512]{1,0:T(8,128)(2,1)}, u32[]{:S(2)}, u32[]{:S(2)}) collective-permute-start(bf16[512,512]{1,0:T(8,128)(2,1)} %get-tuple-element.18.rest_1_), channel_id=1, source_target_pairs={{0,1},{1,2},{2,3},{3,0},{4,7},{5,4},{6,5},{7,6},{8,9},{9,10},{10,1... | collective-permute-start | bytes 1572872 | tf_op jit(solution)/shard_map/ppermute | solution.py:345
  6.6 0.0 copy-done.9
  6.6 3.4 %block_product.8 = (bf16[512,512]{1,0:T(8,128)(2,1)}, s32[1,12]{1,0:T(1,128)S(1)}) custom-call(s32[1]{0:T(128)} %bitcast.1.first_ref, bf16[512,2048]{1,0:T(8,128)(2,1)S(1)} %get-tuple-element.17.rows_ref, bf16[2048,4096]{1,0:T(8,128)(2,1)} %weight_ref.17, s32[1,12]{1,0:T(1,128)S(1)} %copy-done.9, bf16[512,512]{1,0:T(8,128)(2,1)} %get-tuple-element.18.rest_1_), custom_call_target="tpu_custom_call" | custom-call | flops 1000 | bytes 1000 | tf_op jit(solution)/shard_map/block_product/pallas_call | solution.py:53
  10.0 2.1 %collective-permute-start.8 = (bf16[512,512]{1,0:T(8,128)(2,1)}, bf16[512,512]{1,0:T(8,128)(2,1)}, u32[]{:S(2)}, u32[]{:S(2)}) collective-permute-start(bf16[512,512]{1,0:T(8,128)(2,1)} %get-tuple-element.20.rest_0_), channel_id=1, source_target_pairs={{0,3},{1,0},{2,1},{3,2},{4,5},{5,6},{6,7},{7,4},{8,11},{9,8},{10,9... | collective-permute-start | bytes 1572872 | tf_op jit(solution)/shard_map/ppermute | solution.py:345
  12.2 0.0 collective-permute-start
  12.2 1.7 %collective-permute-start.1 = (s32[1,12]{1,0:T(1,128)S(1)}, s32[1,12]{1,0:T(1,128)S(1)}, u32[]{:S(2)}, u32[]{:S(2)}) collective-permute-start(s32[1,12]{1,0:T(1,128)S(1)} %get-tuple-element.19.rest_0_), channel_id=1, source_target_pairs={{0,8},{4,12},{8,0},{12,4},{1,9},{5,13},{9,1},{13,5},{2,10},{6,14},... | collective-permute-start | bytes 152 | tf_op jit(solution)/shard_map/ppermute | solution.py:368
  13.8 0.2 collective-permute-start.2
  14.0 2.7 %block_product.9.rest_6_.rest_4_ = bf16[512,512]{1,0:T(8,128)(2,1)S(1)} custom-call(s32[1]{0:T(128)} %bitcast.3.first_ref, bf16[512,2048]{1,0:T(8,128)(2,1)S(1)} %get-tuple-element.17.rows_ref, bf16[2048,4096]{1,0:T(8,128)(2,1)} %weight_ref.17, bf16[512,512]{1,0:T(8,128)(2,1)} %get-tuple-element.20.rest_0_), custom_call_target="tpu_custom_call" | custom-call | flops 1000 | bytes 1000 | tf_op jit(solution)/shard_map/block_product/pallas_call | solution.py:53
  16.9 0.0 collective-permute-done.rest_1_
  16.9 0.0 collective-permute-done.1.rest_2_
  16.9 0.0 collective-permute-done.2.rest_3_
  16.9 0.0 copy-done.8
  16.9 0.0 copy-done.10
  16.9 3.1 %pick_adapters.1 = (bf16[6,16,3072]{2,1,0:T(8,128)(2,1)S(1)}, bf16[6,16,3072]{2,1,0:T(8,128)(2,1)S(1)}, bf16[6,16,3072]{2,1,0:T(8,128)(2,1)S(1)}, bf16[6,16,3072...) custom-call(s32[1]{0:T(128)} %bitcast.me_ref, s32[512]{0:T(512)S(1)} %copy-done.8, s32[1,12]{1,0:T(1,128)S(1)} %copy-done.10, ...), custom_call_target="tpu_custom_call" | custom-call | flops 1000 | bytes 1000 | tf_op jit(solution)/shard_map/pick_adapters/pallas_call | solution.py:199
  20.1 1.0 %collective-permute-start.3 = (bf16[6,16,3072]{2,1,0:T(8,128)(2,1)S(1)}, bf16[6,16,3072]{2,1,0:T(8,128)(2,1)S(1)}, u32[]{:S(2)}, u32[]{:S(2)}) collective-permute-start(bf16[6,16,3072]{2,1,0:T(8,128)(2,1)S(1)} %get-tuple-element.24), channel_id=1, source_target_pairs={{0,4},{4,0},{8,12},{12,8},{1,5},{5,1},{9,13},{13,9},{2,6},{6,2},{1... | collective-permute-start | bytes 1769480 | tf_op jit(solution)/shard_map/ppermute | solution.py:373
  21.1 1.5 %collective-permute-start.4 = (bf16[6,16,3072]{2,1,0:T(8,128)(2,1)S(1)}, bf16[6,16,3072]{2,1,0:T(8,128)(2,1)S(1)}, u32[]{:S(2)}, u32[]{:S(2)}) collective-permute-start(bf16[6,16,3072]{2,1,0:T(8,128)(2,1)S(1)} %get-tuple-element.25), channel_id=1, source_target_pairs={{0,8},{4,12},{8,0},{12,4},{1,9},{5,13},{9,1},{13,5},{2,10},{6,14},... | collective-permute-start | bytes 1769480 | tf_op jit(solution)/shard_map/ppermute | solution.py:373
  22.6 0.1 collective-permute-start.5
  22.7 0.0 collective-permute-done.6.rest_0_
  22.7 2.8 %block_product.10.rest_1_ = bf16[512,512]{1,0:T(8,128)(2,1)S(1)} custom-call(s32[1]{0:T(128)} %bitcast.5.first_ref, bf16[512,2048]{1,0:T(8,128)(2,1)S(1)} %get-tuple-element.17.rows_ref, bf16[2048,4096]{1,0:T(8,128)(2,1)} %weight_ref.17, bf16[512,512]{1,0:T(8,128)(2,1)} %collective-permute-done.6.rest_0_, s32[24]{0:T(128)S(1)} %get-tuple-element.21.rest_1_.start_ref), custom_call_target="tpu_custom_call" | custom-call | flops 1000 | bytes 1000 | tf_op jit(solution)/shard_map/block_product/pallas_call | solution.py:53
  25.4 6.5 %collective-permute-start.7 = (bf16[512,512]{1,0:T(8,128)(2,1)S(1)}, bf16[512,512]{1,0:T(8,128)(2,1)S(1)}, u32[]{:S(2)}, u32[]{:S(2)}) collective-permute-start(bf16[512,512]{1,0:T(8,128)(2,1)S(1)} %block_product.10.rest_1_), channel_id=1, source_target_pairs={{0,1},{1,2},{2,3},{3,0},{4,7},{5,4},{6,5},{7,6},{8,9},{9,10},{10,1... | collective-permute-start | bytes 1572872 | tf_op jit(solution)/shard_map/ppermute | solution.py:345
  31.9 0.0 collective-permute-done.8.rest_0_
  31.9 3.5 %block_product.11.rest_0_ = bf16[512,512]{1,0:T(8,128)(2,1)} custom-call(s32[1]{0:T(128)} %bitcast.7.first_ref, bf16[512,2048]{1,0:T(8,128)(2,1)S(1)} %get-tuple-element.17.rows_ref, bf16[2048,4096]{1,0:T(8,128)(2,1)} %weight_ref.17, bf16[512,512]{1,0:T(8,128)(2,1)} %collective-permute-done.8.rest_0_, bf16[512,512]{1,0:T(8,128)(2,1)S(1)} %block_product.10.rest_1_), custom_call_target="tpu_custom_call" | custom-call | flops 1000 | bytes 1000 | tf_op jit(solution)/shard_map/block_product/pallas_call | solution.py:53
  35.4 3.7 %collective-permute-start.12 = (bf16[512,512]{1,0:T(8,128)(2,1)}, bf16[512,512]{1,0:T(8,128)(2,1)}, u32[]{:S(2)}, u32[]{:S(2)}) collective-permute-start(bf16[512,512]{1,0:T(8,128)(2,1)} %block_product.11.rest_0_), channel_id=1, source_target_pairs={{0,3},{1,0},{2,1},{3,2},{4,5},{5,6},{6,7},{7,4},{8,11},{9,8},{10,9... | collective-permute-start | bytes 1572872 | tf_op jit(solution)/shard_map/ppermute | solution.py:345
  39.1 2.7 %block_product.12.rest_1_.rest_5_ = bf16[512,512]{1,0:T(8,128)(2,1)S(1)} custom-call(s32[1]{0:T(128)} %bitcast.6.first_ref, bf16[512,2048]{1,0:T(8,128)(2,1)S(1)} %get-tuple-element.17.rows_ref, bf16[2048,4096]{1,0:T(8,128)(2,1)} %weight_ref.17, bf16[512,512]{1,0:T(8,128)(2,1)} %block_product.11.rest_0_), custom_call_target="tpu_custom_call" | custom-call | flops 20000000000 | bytes 1000 | tf_op jit(solution)/shard_map/block_product/pallas_call | solution.py:53
  41.8 0.0 copy-start.6
  41.8 2.7 %collective-permute-done.7.rest_0_ = bf16[512,512]{1,0:T(8,128)(2,1)S(1)} collective-permute-done((bf16[512,512]{1,0:T(8,128)(2,1)S(1)}, bf16[512,512]{1,0:T(8,128)(2,1)S(1)}, u32[]{:S(2)}, u32[]{:S(2)}) %collective-permute-start.7) | collective-permute-done | bytes 524320 | tf_op jit(solution)/shard_map/ppermute | solution.py:345
  44.5 3.4 %block_product.13.rest_4_ = bf16[512,512]{1,0:T(8,128)(2,1)} custom-call(s32[1]{0:T(128)} %bitcast.4.first_ref, bf16[512,2048]{1,0:T(8,128)(2,1)S(1)} %get-tuple-element.17.rows_ref, bf16[2048,4096]{1,0:T(8,128)(2,1)} %weight_ref.17, bf16[512,512]{1,0:T(8,128)(2,1)S(1)} %collective-permute-done.7.rest_0_, bf16[512,512]{1,0:T(8,128)(2,1)S(1)} %block_product.12.rest_1_.rest_5_), custom_call_target="tpu_custom_call" | custom-call | flops 1000 | bytes 1000 | tf_op jit(solution)/shard_map/block_product/pallas_call | solution.py:53
  47.9 0.0 copy-done.6
  47.9 2.3 %collective-permute-start.15 = (bf16[512,512]{1,0:T(8,128)(2,1)}, bf16[512,512]{1,0:T(8,128)(2,1)}, u32[]{:S(2)}, u32[]{:S(2)}) collective-permute-start(bf16[512,512]{1,0:T(8,128)(2,1)} %block_product.13.rest_4_), channel_id=1, source_target_pairs={{0,1},{1,2},{2,3},{3,0},{4,7},{5,4},{6,5},{7,6},{8,9},{9,10},{10,1... | collective-permute-start | bytes 1572872 | tf_op jit(solution)/shard_map/ppermute | solution.py:345
  50.2 0.0 collective-permute-done.3.rest_1_.rest_7_
  50.2 0.0 collective-permute-done.4.rest_2_.rest_8_
  50.2 0.0 collective-permute-done.5.rest_3_.rest_9_
  50.2 0.0 copy-start.4
  50.2 1.6 %low_sums.1.rest_1_.rest_0_ = bf16[16,512]{1,0:T(8,128)(2,1)S(1)} custom-call(s32[24]{0:T(128)S(1)} %get-tuple-element.21.rest_1_.start_ref, s32[24]{0:T(128)S(1)} %get-tuple-element.22.end_ref, bf16[512,2048]{1,0:T(8,128)(2,1)S(1)} %get-tuple-element.17.rows_ref, bf16[6,16,3072]{2,1,0:T(8,128)(2,1)S(1)} %get-tuple-element.23.rest_0_.rest_6_, ...), custom_call_target="tpu_custom_call" | custom-call | flops 1000 | bytes 1000 | tf_op jit(solution)/shard_map/low_sums/pallas_call | solution.py:241
  51.8 0.0 copy-done.2
  51.8 0.0 copy-start
  51.8 0.8 %copy-done = bf16[6,16,3072]{2,1,0:T(8,128)(2,1)} copy-done((bf16[6,16,3072]{2,1,0:T(8,128)(2,1)}, bf16[6,16,3072]{2,1,0:T(8,128)(2,1)S(1)}, u32[]{:S(2)}) %copy-start) | copy-done | bytes 589848
  52.6 3.0 %collective-permute-start.9 = (bf16[16,512]{1,0:T(8,128)(2,1)S(1)}, bf16[16,512]{1,0:T(8,128)(2,1)S(1)}, u32[]{:S(2)}, u32[]{:S(2)}) collective-permute-start(bf16[16,512]{1,0:T(8,128)(2,1)S(1)} %low_sums.1.rest_1_.rest_0_), channel_id=1, source_target_pairs={{0,1},{1,0},{2,3},{3,2},{4,5},{5,4},{6,7},{7,6},{8,9},{9,8},{10,11... | collective-permute-start | bytes 49160 | tf_op jit(solution)/shard_map/ppermute | solution.py:383
  55.6 0.0 copy-done.4
  55.6 1.1 %collective-permute-start.10 = (bf16[16,512]{1,0:T(8,128)(2,1)S(1)}, bf16[16,512]{1,0:T(8,128)(2,1)S(1)}, u32[]{:S(2)}, u32[]{:S(2)}) collective-permute-start(bf16[16,512]{1,0:T(8,128)(2,1)S(1)} %low_sums.1.rest_1_.rest_0_), channel_id=1, source_target_pairs={{0,2},{1,3},{2,0},{3,1},{4,6},{5,7},{6,4},{7,5},{8,10},{9,11},{10,... | collective-permute-start | bytes 49160 | tf_op jit(solution)/shard_map/ppermute | solution.py:383
  56.7 1.4 %collective-permute-start.11 = (bf16[16,512]{1,0:T(8,128)(2,1)S(1)}, bf16[16,512]{1,0:T(8,128)(2,1)S(1)}, u32[]{:S(2)}, u32[]{:S(2)}) collective-permute-start(bf16[16,512]{1,0:T(8,128)(2,1)S(1)} %low_sums.1.rest_1_.rest_0_), channel_id=1, source_target_pairs={{0,3},{1,2},{2,1},{3,0},{4,7},{5,6},{6,5},{7,4},{8,11},{9,10},{10,... | collective-permute-start | bytes 49160 | tf_op jit(solution)/shard_map/ppermute | solution.py:383
  58.1 3.5 %collective-permute-done.12.rest_0_ = bf16[512,512]{1,0:T(8,128)(2,1)} collective-permute-done((bf16[512,512]{1,0:T(8,128)(2,1)}, bf16[512,512]{1,0:T(8,128)(2,1)}, u32[]{:S(2)}, u32[]{:S(2)}) %collective-permute-start.12) | collective-permute-done | bytes 524320 | tf_op jit(solution)/shard_map/ppermute | solution.py:345
  61.6 2.0 %block_product.14.rest_1_ = bf16[512,256]{1,0:T(8,128)(2,1)S(1)} custom-call(s32[1]{0:T(128)} %bitcast.9.first_ref, bf16[512,2048]{1,0:T(8,128)(2,1)S(1)} %get-tuple-element.17.rows_ref, bf16[2048,4096]{1,0:T(8,128)(2,1)} %weight_ref.17, bf16[512,512]{1,0:T(8,128)(2,1)} %collective-permute-done.12.rest_0_, bf16[16,512]{1,0:T(8,128)(2,1)S(1)} %low_sums.1.rest_1_.rest_0_), custom_call_target="tpu_custom_call" | custom-call | flops 1000 | bytes 1000 | tf_op jit(solution)/shard_map/block_product/pallas_call | solution.py:53
  63.6 0.1 collective-permute-start.14
  63.7 0.0 copy-start.1
  63.7 0.0 copy-start.3
  63.7 0.0 copy-start.5
  63.7 0.0 copy-start.7
  63.7 2.1 %block_product.15.rest_10_ = bf16[512,256]{1,0:T(8,128)(2,1)S(1)} custom-call(s32[1]{0:T(128)} %bitcast.8.first_ref, bf16[512,2048]{1,0:T(8,128)(2,1)S(1)} %get-tuple-element.17.rows_ref, bf16[2048,4096]{1,0:T(8,128)(2,1)} %weight_ref.17, bf16[512,512]{1,0:T(8,128)(2,1)} %collective-permute-done.12.rest_0_, bf16[512,256]{1,0:T(8,128)(2,1)S(1)} %block_product.14.rest_1_), custom_call_target="tpu_custom_call" | custom-call | flops 1000 | bytes 1000 | tf_op jit(solution)/shard_map/block_product/pallas_call | solution.py:53
  65.9 1.3 %collective-permute-done.9.rest_1_ = bf16[16,512]{1,0:T(8,128)(2,1)S(1)} collective-permute-done((bf16[16,512]{1,0:T(8,128)(2,1)S(1)}, bf16[16,512]{1,0:T(8,128)(2,1)S(1)}, u32[]{:S(2)}, u32[]{:S(2)}) %collective-permute-start.9) | collective-permute-done | bytes 16416 | tf_op jit(solution)/shard_map/ppermute | solution.py:383
  67.2 4.6 %collective-permute-start.13 = (bf16[512,256]{1,0:T(8,128)(2,1)S(1)}, bf16[512,256]{1,0:T(8,128)(2,1)S(1)}, u32[]{:S(2)}, u32[]{:S(2)}) collective-permute-start(bf16[512,256]{1,0:T(8,128)(2,1)S(1)} %block_product.15.rest_10_), channel_id=1, source_target_pairs={{0,3},{1,0},{2,1},{3,2},{4,5},{5,6},{6,7},{7,4},{8,11},{9,8},{10,9... | collective-permute-start | bytes 786440 | tf_op jit(solution)/shard_map/ppermute | solution.py:345
  71.8 0.0 collective-permute-done.10.rest_2_
  71.8 0.0 collective-permute-done.11.rest_3_
  71.8 0.0 copy-done.1
  71.8 0.0 copy-done.3
  71.8 0.0 copy-done.5
  71.8 1.3 %adapter_term.1 = (f32[512,512]{1,0:T(8,128)S(1)}, f32[512,512]{1,0:T(8,128)S(1)}) custom-call(s32[24]{0:T(128)S(1)} %get-tuple-element.21.rest_1_.start_ref, s32[24]{0:T(128)S(1)} %get-tuple-element.22.end_ref, bf16[16,512]{1,0:T(8,128)(2,1)S(1)} %low_sums.1.rest_1_.rest_0_, bf16[16,512]{1,0:T(8,128)(2,1)S(1)} %collective-permute-done.9.rest_1_, ...), custom_call_target="tpu_custom_call" | custom-call | flops 1000 | bytes 1000 | tf_op jit(solution)/shard_map/adapter_term/pallas_call | solution.py:287
  73.1 0.0 collective-permute-done.15.rest_0_
  73.1 1.8 %finish.3.rest_1_ = bf16[512,1024]{1,0:T(8,128)(2,1)} custom-call(f32[512,512]{1,0:T(8,128)S(1)} %get-tuple-element.28.term_ref, bf16[512,512]{1,0:T(8,128)(2,1)} %collective-permute-done.15.rest_0_), custom_call_target="tpu_custom_call" | custom-call | flops 20000000000 | bytes 1000 | tf_op jit(solution)/shard_map/finish/pallas_call | solution.py:314
  74.9 0.0 collective-permute-done.14.rest_0_
  74.9 0.8 finish.4.rest_1_
  75.7 2.6 %collective-permute-done.13.rest_0_ = bf16[512,256]{1,0:T(8,128)(2,1)S(1)} collective-permute-done((bf16[512,256]{1,0:T(8,128)(2,1)S(1)}, bf16[512,256]{1,0:T(8,128)(2,1)S(1)}, u32[]{:S(2)}, u32[]{:S(2)}) %collective-permute-start.13) | collective-permute-done | bytes 262176 | tf_op jit(solution)/shard_map/ppermute | solution.py:345
  78.3 0.8 %finish.5 = bf16[512,1024]{1,0:T(8,128)(2,1)} custom-call(f32[512,512]{1,0:T(8,128)S(1)} %get-tuple-element.27.term_ref, bf16[512,256]{1,0:T(8,128)(2,1)S(1)} %collective-permute-done.13.rest_0_, bf16[512,1024]{1,0:T(8,128)(2,1)} %finish.4.rest_1_), custom_call_target="tpu_custom_call", output_to_operand_aliasing={{}: (2, {})} | custom-call | flops 1000 | bytes 1000 | tf_op jit(solution)/shard_map/finish/pallas_call | solution.py:314
  (5 shorter events, 0.0 us)
Async XLA Ops:
  0.0 6.6 %copy-start.9 = (s32[1,12]{1,0:T(1,128)S(1)}, s32[1,12]{1,0:T(1,128)}, u32[]{:S(2)}) copy-start(s32[1,12]{1,0:T(1,128)} %rest_0_.1) | copy-start | bytes 148
  3.5 19.2 %collective-permute-start.6 = (bf16[512,512]{1,0:T(8,128)(2,1)}, bf16[512,512]{1,0:T(8,128)(2,1)}, u32[]{:S(2)}, u32[]{:S(2)}) collective-permute-start(bf16[512,512]{1,0:T(8,128)(2,1)} %get-tuple-element.18.rest_1_), channel_id=1, source_target_pairs={{0,1},{1,2},{2,3},{3,0},{4,7},{5,4},{6,5},{7,6},{8,9},{9,10},{10,1... | collective-permute-start | bytes 1572872 | tf_op jit(solution)/shard_map/ppermute | solution.py:345
  10.0 21.9 %collective-permute-start.8 = (bf16[512,512]{1,0:T(8,128)(2,1)}, bf16[512,512]{1,0:T(8,128)(2,1)}, u32[]{:S(2)}, u32[]{:S(2)}) collective-permute-start(bf16[512,512]{1,0:T(8,128)(2,1)} %get-tuple-element.20.rest_0_), channel_id=1, source_target_pairs={{0,3},{1,0},{2,1},{3,2},{4,5},{5,6},{6,7},{7,4},{8,11},{9,8},{10,9... | collective-permute-start | bytes 1572872 | tf_op jit(solution)/shard_map/ppermute | solution.py:345
  12.2 4.7 %collective-permute-start = (s32[1,12]{1,0:T(1,128)S(1)}, s32[1,12]{1,0:T(1,128)S(1)}, u32[]{:S(2)}, u32[]{:S(2)}) collective-permute-start(s32[1,12]{1,0:T(1,128)S(1)} %get-tuple-element.19.rest_0_), channel_id=1, source_target_pairs={{0,4},{4,0},{8,12},{12,8},{1,5},{5,1},{9,13},{13,9},{2,6},{6,2},{1... | collective-permute-start | bytes 152 | tf_op jit(solution)/shard_map/ppermute | solution.py:368
  12.2 4.7 %collective-permute-start.1 = (s32[1,12]{1,0:T(1,128)S(1)}, s32[1,12]{1,0:T(1,128)S(1)}, u32[]{:S(2)}, u32[]{:S(2)}) collective-permute-start(s32[1,12]{1,0:T(1,128)S(1)} %get-tuple-element.19.rest_0_), channel_id=1, source_target_pairs={{0,8},{4,12},{8,0},{12,4},{1,9},{5,13},{9,1},{13,5},{2,10},{6,14},... | collective-permute-start | bytes 152 | tf_op jit(solution)/shard_map/ppermute | solution.py:368
  13.8 3.0 %collective-permute-start.2 = (s32[1,12]{1,0:T(1,128)S(1)}, s32[1,12]{1,0:T(1,128)S(1)}, u32[]{:S(2)}, u32[]{:S(2)}) collective-permute-start(s32[1,12]{1,0:T(1,128)S(1)} %get-tuple-element.19.rest_0_), channel_id=1, source_target_pairs={{0,12},{4,8},{8,4},{12,0},{1,13},{5,9},{9,5},{13,1},{2,14},{6,10},... | collective-permute-start | bytes 152 | tf_op jit(solution)/shard_map/ppermute | solution.py:368
  14.0 2.9 %copy-start.8 = (s32[512]{0:T(512)S(1)}, s32[512]{0:T(512)}, u32[]{:S(2)}) copy-start(s32[512]{0:T(512)} %table_ref.1) | copy-start | bytes 6148
  14.0 2.9 %copy-start.10 = (s32[1,12]{1,0:T(1,128)S(1)}, s32[1,12]{1,0:T(1,128)}, u32[]{:S(2)}) copy-start(s32[1,12]{1,0:T(1,128)} %lens_ref.1) | copy-start | bytes 148
  20.1 30.1 %collective-permute-start.3 = (bf16[6,16,3072]{2,1,0:T(8,128)(2,1)S(1)}, bf16[6,16,3072]{2,1,0:T(8,128)(2,1)S(1)}, u32[]{:S(2)}, u32[]{:S(2)}) collective-permute-start(bf16[6,16,3072]{2,1,0:T(8,128)(2,1)S(1)} %get-tuple-element.24), channel_id=1, source_target_pairs={{0,4},{4,0},{8,12},{12,8},{1,5},{5,1},{9,13},{13,9},{2,6},{6,2},{1... | collective-permute-start | bytes 1769480 | tf_op jit(solution)/shard_map/ppermute | solution.py:373
  21.1 29.1 %collective-permute-start.4 = (bf16[6,16,3072]{2,1,0:T(8,128)(2,1)S(1)}, bf16[6,16,3072]{2,1,0:T(8,128)(2,1)S(1)}, u32[]{:S(2)}, u32[]{:S(2)}) collective-permute-start(bf16[6,16,3072]{2,1,0:T(8,128)(2,1)S(1)} %get-tuple-element.25), channel_id=1, source_target_pairs={{0,8},{4,12},{8,0},{12,4},{1,9},{5,13},{9,1},{13,5},{2,10},{6,14},... | collective-permute-start | bytes 1769480 | tf_op jit(solution)/shard_map/ppermute | solution.py:373
  22.6 27.6 %collective-permute-start.5 = (bf16[6,16,3072]{2,1,0:T(8,128)(2,1)S(1)}, bf16[6,16,3072]{2,1,0:T(8,128)(2,1)S(1)}, u32[]{:S(2)}, u32[]{:S(2)}) collective-permute-start(bf16[6,16,3072]{2,1,0:T(8,128)(2,1)S(1)} %get-tuple-element.26), channel_id=1, source_target_pairs={{0,12},{4,8},{8,4},{12,0},{1,13},{5,9},{9,5},{13,1},{2,14},{6,10},... | collective-permute-start | bytes 1769480 | tf_op jit(solution)/shard_map/ppermute | solution.py:373
  25.4 19.0 %collective-permute-start.7 = (bf16[512,512]{1,0:T(8,128)(2,1)S(1)}, bf16[512,512]{1,0:T(8,128)(2,1)S(1)}, u32[]{:S(2)}, u32[]{:S(2)}) collective-permute-start(bf16[512,512]{1,0:T(8,128)(2,1)S(1)} %block_product.10.rest_1_), channel_id=1, source_target_pairs={{0,1},{1,2},{2,3},{3,0},{4,7},{5,4},{6,5},{7,6},{8,9},{9,10},{10,1... | collective-permute-start | bytes 1572872 | tf_op jit(solution)/shard_map/ppermute | solution.py:345
  35.4 26.2 %collective-permute-start.12 = (bf16[512,512]{1,0:T(8,128)(2,1)}, bf16[512,512]{1,0:T(8,128)(2,1)}, u32[]{:S(2)}, u32[]{:S(2)}) collective-permute-start(bf16[512,512]{1,0:T(8,128)(2,1)} %block_product.11.rest_0_), channel_id=1, source_target_pairs={{0,3},{1,0},{2,1},{3,2},{4,5},{5,6},{6,7},{7,4},{8,11},{9,8},{10,9... | collective-permute-start | bytes 1572872 | tf_op jit(solution)/shard_map/ppermute | solution.py:345
  41.8 6.1 %copy-start.6 = (bf16[512,512]{1,0:T(8,128)(2,1)}, bf16[512,512]{1,0:T(8,128)(2,1)S(1)}, u32[]{:S(2)}) copy-start(bf16[512,512]{1,0:T(8,128)(2,1)S(1)} %block_product.12.rest_1_.rest_5_) | copy-start | bytes 1572868
  47.9 25.2 %collective-permute-start.15 = (bf16[512,512]{1,0:T(8,128)(2,1)}, bf16[512,512]{1,0:T(8,128)(2,1)}, u32[]{:S(2)}, u32[]{:S(2)}) collective-permute-start(bf16[512,512]{1,0:T(8,128)(2,1)} %block_product.13.rest_4_), channel_id=1, source_target_pairs={{0,1},{1,2},{2,3},{3,0},{4,7},{5,4},{6,5},{7,6},{8,9},{9,10},{10,1... | collective-permute-start | bytes 1572872 | tf_op jit(solution)/shard_map/ppermute | solution.py:345
  50.2 1.6 %copy-start.2 = (bf16[6,16,3072]{2,1,0:T(8,128)(2,1)}, bf16[6,16,3072]{2,1,0:T(8,128)(2,1)S(1)}, u32[]{:S(2)}) copy-start(bf16[6,16,3072]{2,1,0:T(8,128)(2,1)S(1)} %collective-permute-done.4.rest_2_.rest_8_) | copy-start | bytes 1769476
  50.2 5.4 %copy-start.4 = (bf16[6,16,3072]{2,1,0:T(8,128)(2,1)}, bf16[6,16,3072]{2,1,0:T(8,128)(2,1)S(1)}, u32[]{:S(2)}) copy-start(bf16[6,16,3072]{2,1,0:T(8,128)(2,1)S(1)} %collective-permute-done.5.rest_3_.rest_9_) | copy-start | bytes 1769476
  51.8 0.8 %copy-start = (bf16[6,16,3072]{2,1,0:T(8,128)(2,1)}, bf16[6,16,3072]{2,1,0:T(8,128)(2,1)S(1)}, u32[]{:S(2)}) copy-start(bf16[6,16,3072]{2,1,0:T(8,128)(2,1)S(1)} %collective-permute-done.3.rest_1_.rest_7_) | copy-start | bytes 1769476
  52.6 14.6 %collective-permute-start.9 = (bf16[16,512]{1,0:T(8,128)(2,1)S(1)}, bf16[16,512]{1,0:T(8,128)(2,1)S(1)}, u32[]{:S(2)}, u32[]{:S(2)}) collective-permute-start(bf16[16,512]{1,0:T(8,128)(2,1)S(1)} %low_sums.1.rest_1_.rest_0_), channel_id=1, source_target_pairs={{0,1},{1,0},{2,3},{3,2},{4,5},{5,4},{6,7},{7,6},{8,9},{9,8},{10,11... | collective-permute-start | bytes 49160 | tf_op jit(solution)/shard_map/ppermute | solution.py:383
  55.6 16.2 %collective-permute-start.10 = (bf16[16,512]{1,0:T(8,128)(2,1)S(1)}, bf16[16,512]{1,0:T(8,128)(2,1)S(1)}, u32[]{:S(2)}, u32[]{:S(2)}) collective-permute-start(bf16[16,512]{1,0:T(8,128)(2,1)S(1)} %low_sums.1.rest_1_.rest_0_), channel_id=1, source_target_pairs={{0,2},{1,3},{2,0},{3,1},{4,6},{5,7},{6,4},{7,5},{8,10},{9,11},{10,... | collective-permute-start | bytes 49160 | tf_op jit(solution)/shard_map/ppermute | solution.py:383
  56.7 15.1 %collective-permute-start.11 = (bf16[16,512]{1,0:T(8,128)(2,1)S(1)}, bf16[16,512]{1,0:T(8,128)(2,1)S(1)}, u32[]{:S(2)}, u32[]{:S(2)}) collective-permute-start(bf16[16,512]{1,0:T(8,128)(2,1)S(1)} %low_sums.1.rest_1_.rest_0_), channel_id=1, source_target_pairs={{0,3},{1,2},{2,1},{3,0},{4,7},{5,6},{6,5},{7,4},{8,11},{9,10},{10,... | collective-permute-start | bytes 49160 | tf_op jit(solution)/shard_map/ppermute | solution.py:383
  63.6 11.3 %collective-permute-start.14 = (bf16[512,256]{1,0:T(8,128)(2,1)S(1)}, bf16[512,256]{1,0:T(8,128)(2,1)S(1)}, u32[]{:S(2)}, u32[]{:S(2)}) collective-permute-start(bf16[512,256]{1,0:T(8,128)(2,1)S(1)} %block_product.14.rest_1_), channel_id=1, source_target_pairs={{0,3},{1,0},{2,1},{3,2},{4,5},{5,6},{6,7},{7,4},{8,11},{9,8},{10,9... | collective-permute-start | bytes 786440 | tf_op jit(solution)/shard_map/ppermute | solution.py:345
  63.7 8.1 %copy-start.1 = (bf16[6,16,3072]{2,1,0:T(8,128)(2,1)S(1)}, bf16[6,16,3072]{2,1,0:T(8,128)(2,1)}, u32[]{:S(2)}) copy-start(bf16[6,16,3072]{2,1,0:T(8,128)(2,1)} %copy-done) | copy-start | bytes 1769476
  63.7 8.1 %copy-start.3 = (bf16[6,16,3072]{2,1,0:T(8,128)(2,1)S(1)}, bf16[6,16,3072]{2,1,0:T(8,128)(2,1)}, u32[]{:S(2)}) copy-start(bf16[6,16,3072]{2,1,0:T(8,128)(2,1)} %copy-done.2) | copy-start | bytes 1769476
  63.7 8.1 %copy-start.5 = (bf16[6,16,3072]{2,1,0:T(8,128)(2,1)S(1)}, bf16[6,16,3072]{2,1,0:T(8,128)(2,1)}, u32[]{:S(2)}) copy-start(bf16[6,16,3072]{2,1,0:T(8,128)(2,1)} %copy-done.4) | copy-start | bytes 1769476
  63.7 8.1 %copy-start.7 = (bf16[512,512]{1,0:T(8,128)(2,1)S(1)}, bf16[512,512]{1,0:T(8,128)(2,1)}, u32[]{:S(2)}) copy-start(bf16[512,512]{1,0:T(8,128)(2,1)} %copy-done.6) | copy-start | bytes 1572868
  67.2 11.2 %collective-permute-start.13 = (bf16[512,256]{1,0:T(8,128)(2,1)S(1)}, bf16[512,256]{1,0:T(8,128)(2,1)S(1)}, u32[]{:S(2)}, u32[]{:S(2)}) collective-permute-start(bf16[512,256]{1,0:T(8,128)(2,1)S(1)} %block_product.15.rest_10_), channel_id=1, source_target_pairs={{0,3},{1,0},{2,1},{3,2},{4,5},{5,6},{6,7},{7,4},{8,11},{9,8},{10,9... | collective-permute-start | bytes 786440 | tf_op jit(solution)/shard_map/ppermute | solution.py:345

commit v22 on v21

--- a/solution.py
+++ b/solution.py
@@ -41,7 +41,7 @@
     rows, weight, first, width, addends=(), skip=0, after=(), ids=None, cost=SMALL
 ):
     row_total, depth = rows.shape
-    tile = min(256, width)
+    tile = 256 if width % 256 == 0 else 128
     with_ids = ids is not None
     smem = pl.BlockSpec(memory_space=pltpu.SMEM)
     hbm = pl.BlockSpec(memory_space=pl.ANY)
@@ -271,7 +271,8 @@
     spread = jnp.concatenate(spread, axis=0).astype(BF16)
     ups = jnp.concatenate([ref[...].reshape(CAP * rank, cols) for ref in up_refs], axis=0)
     for piece in range(pieces):
-        columns = slice(piece * width, (piece + 1) * width)
+        first = (pieces - 1 - piece) * width
+        columns = slice(first, first + width)
         term = lax.dot_general(
             spread, ups[:, columns], (((0,), (0,)), ((), ())), preferred_element_type=F32
         )
@@ -332,6 +333,7 @@
     rank = down.shape[1]
     cols = up.shape[2]
     width = cols // PIECES
+    offsets = [(PIECES - 1 - piece) * width for piece in range(PIECES)]
     me_req = lax.axis_index("req").astype(jnp.int32)
     me = lax.axis_index("tp").astype(jnp.int32)
     steps = tp_total - 1
@@ -347,14 +349,18 @@
     def start_of(back, piece):
         behind = jnp.where(lax.rem(me_req + piece, 2) == 0, tp_total - back, back)
         block = lax.rem(me + behind, tp_total)
-        return block * cols + piece * width
+        return block * cols + offsets[piece]
 
     def partial(back, piece, **options):
         return block_product(rows, weight, start_of(back, piece), width, **options)
 
-    def half_partial(back, piece, skip, **options):
+    cut = 3 * width // 4 // 128 * 128
+    last_parts = ((0, cut), (cut, width - cut))
+
+    def part_partial(back, piece, part, **options):
+        skip, part_width = part
         first = start_of(back, piece) + skip
-        return block_product(rows, weight, first, width // 2, skip=skip, **options)
+        return block_product(rows, weight, first, part_width, skip=skip, **options)
 
     last, rows = first_product(rows, weight, start_of(1, 0), width)
     rows = pltpu.with_memory_space_constraint(rows, pltpu.VMEM)
@@ -383,12 +389,12 @@
                     lows.append(lax.ppermute(low, "tp", pairs))
                 last = low
             if step == steps - 1 and piece == PIECES - 1:
-                halves = []
-                for skip in (0, width // 2):
-                    last = half_partial(
-                        1 + step, piece, skip, addends=[moving[piece]], after=[last]
+                last_moving = []
+                for part in last_parts:
+                    last = part_partial(
+                        1 + step, piece, part, addends=[moving[piece]], after=[last]
                     )
-                    halves.append(move(last, piece))
+                    last_moving.append(move(last, piece))
                 break
             last = partial(1 + step, piece, addends=[moving[piece]], after=[last])
             moving[piece] = move(last, piece)
@@ -398,12 +404,12 @@
 
     terms = adapter_term(starts, ends, lows, owns, packs, [last])
     parts = [(piece, 0, moving[piece]) for piece in range(PIECES - 1)]
-    parts += [(PIECES - 1, skip, half) for skip, half in zip((0, width // 2), halves)]
+    parts += [(PIECES - 1, part[0], came) for part, came in zip(last_parts, last_moving)]
     result = None
     for piece, skip, arrived in parts:
         arrived = pltpu.with_memory_space_constraint(arrived, pltpu.VMEM)
         cost = LARGE if piece == 0 else SMALL
-        offset = piece * width + skip
+        offset = offsets[piece] + skip
         result = finish(terms[piece], skip, arrived, offset, cols, result, cost)
     return result
 

time: 79.5 us -> 80.9 us (1.018)
  starting transfers between devices: 32.3 us -> 30.5 us
  waiting for transfers between devices: 10.2 us -> 11.8 us
  Pallas kernels: 35.5 us -> 36.9 us
    ppermute x7, waiting for transfers between devices: 8.85 us -> 11.8 us  [move(): return lax.ppermute(value, ('req', 'tp'), pairs)]
    ppermute x7, starting transfers between devices: 22.3 us -> 20.3 us  [move(): return lax.ppermute(value, ('req', 'tp'), pairs)]
    pallas_call x8, Pallas kernels: 22.6 us -> 24.1 us  [block_product(): pl.pallas_call(functools.partial(product_kernel, len(addends), with_ids),...]
    ppermute x3, waiting for transfers between devices: 1.29 us -> 0.01 us  [local(): lows.append(lax.ppermute(low, 'tp', pairs))]
  transfers between devices with their start and end apart: 16 -> 16, of which waited for: 4 -> 4; matrix products, arithmetic and copies ran while one was open for 0% -> 0% of each run, Pallas kernels for 39% -> 41%
where the time goes in v22:
time: 80.9 us; the launch traced here: 80.5 us
  Pallas kernels  36.9 us (46%)
  starting transfers between devices  30.5 us (38%)
  waiting for transfers between devices  11.8 us (15%)
  local copies, waits for them, and re-layouts  0.85 us (1%)
    pallas_call x8, Pallas kernels, block_product(): pl.pallas_call(functools.partial(product_kernel, len(addends), with_ids),...  24.1 us
    ppermute x7, starting transfers between devices, move(): return lax.ppermute(value, ('req', 'tp'), pairs)  20.3 us
    ppermute x7, waiting for transfers between devices, move(): return lax.ppermute(value, ('req', 'tp'), pairs)  11.8 us
    ppermute x3, starting transfers between devices, local(): lows.append(lax.ppermute(low, 'tp', pairs))  5.5 us
    pallas_call x1, Pallas kernels, first_product(): pl.pallas_call(functools.partial(first_kernel, chunk), in_specs=[pl.Block...  3.49 us
    pallas_call x3, Pallas kernels, finish(): pl.pallas_call(functools.partial(finish_kernel, 1), grid=(row_total // he...  3.39 us
    pallas_call x1, Pallas kernels, pick_adapters(): pl.pallas_call(functools.partial(pick_kernel, peers, len(after)), in_spec...  3.09 us
    ppermute x3, starting transfers between devices, local(): lax.ppermute(packs[x], 'req', [(i, i ^ x) for i in range(req_total)])  2.89 us
  transfers between devices with their start and end apart: 16, of which 4 were waited for; matrix products, arithmetic and copies ran while one was open for 0% of the time, Pallas kernels for 41%

profile of v22, /device:TPU:0, one launch (start us, length us, event | category | flops | bytes accessed | tf_op | source)
XLA Modules:
  0.0 80.5 jit_solution(13234775681366129170)
XLA Ops:
  0.0 3.5 %first_product.1 = (bf16[512,512]{1,0:T(8,128)(2,1)}, bf16[512,2048]{1,0:T(8,128)(2,1)S(1)}) custom-call(s32[1]{0:T(128)} %bitcast.2.first_ref, bf16[512,2048]{1,0:T(8,128)(2,1)} %rows_ref.1, bf16[2048,4096]{1,0:T(8,128)(2,1)} %weight_ref.17), custom_call_target="tpu_custom_call" | custom-call | flops 1000 | bytes 1000 | tf_op jit(solution)/shard_map/first_product/pallas_call | solution.py:108
  3.5 3.1 %collective-permute-start.6 = (bf16[512,512]{1,0:T(8,128)(2,1)}, bf16[512,512]{1,0:T(8,128)(2,1)}, u32[]{:S(2)}, u32[]{:S(2)}) collective-permute-start(bf16[512,512]{1,0:T(8,128)(2,1)} %get-tuple-element.18.rest_1_), channel_id=1, source_target_pairs={{0,1},{1,2},{2,3},{3,0},{4,7},{5,4},{6,5},{7,6},{8,9},{9,10},{10,1... | collective-permute-start | bytes 1572872 | tf_op jit(solution)/shard_map/ppermute | solution.py:347
  6.6 0.0 copy-done.9
  6.6 3.4 %block_product.8 = (bf16[512,512]{1,0:T(8,128)(2,1)}, s32[1,12]{1,0:T(1,128)S(1)}) custom-call(s32[1]{0:T(128)} %bitcast.1.first_ref, bf16[512,2048]{1,0:T(8,128)(2,1)S(1)} %get-tuple-element.17.rows_ref, bf16[2048,4096]{1,0:T(8,128)(2,1)} %weight_ref.17, s32[1,12]{1,0:T(1,128)S(1)} %copy-done.9, bf16[512,512]{1,0:T(8,128)(2,1)} %get-tuple-element.18.rest_1_), custom_call_target="tpu_custom_call" | custom-call | flops 1000 | bytes 1000 | tf_op jit(solution)/shard_map/block_product/pallas_call | solution.py:53
  10.0 2.1 %collective-permute-start.8 = (bf16[512,512]{1,0:T(8,128)(2,1)}, bf16[512,512]{1,0:T(8,128)(2,1)}, u32[]{:S(2)}, u32[]{:S(2)}) collective-permute-start(bf16[512,512]{1,0:T(8,128)(2,1)} %get-tuple-element.20.rest_0_), channel_id=1, source_target_pairs={{0,3},{1,0},{2,1},{3,2},{4,5},{5,6},{6,7},{7,4},{8,11},{9,8},{10,9... | collective-permute-start | bytes 1572872 | tf_op jit(solution)/shard_map/ppermute | solution.py:347
  12.2 0.0 collective-permute-start
  12.2 1.7 %collective-permute-start.1 = (s32[1,12]{1,0:T(1,128)S(1)}, s32[1,12]{1,0:T(1,128)S(1)}, u32[]{:S(2)}, u32[]{:S(2)}) collective-permute-start(s32[1,12]{1,0:T(1,128)S(1)} %get-tuple-element.19.rest_0_), channel_id=1, source_target_pairs={{0,8},{4,12},{8,0},{12,4},{1,9},{5,13},{9,1},{13,5},{2,10},{6,14},... | collective-permute-start | bytes 152 | tf_op jit(solution)/shard_map/ppermute | solution.py:374
  13.8 0.2 collective-permute-start.2
  14.0 2.7 %block_product.9.rest_6_.rest_4_ = bf16[512,512]{1,0:T(8,128)(2,1)S(1)} custom-call(s32[1]{0:T(128)} %bitcast.3.first_ref, bf16[512,2048]{1,0:T(8,128)(2,1)S(1)} %get-tuple-element.17.rows_ref, bf16[2048,4096]{1,0:T(8,128)(2,1)} %weight_ref.17, bf16[512,512]{1,0:T(8,128)(2,1)} %get-tuple-element.20.rest_0_), custom_call_target="tpu_custom_call" | custom-call | flops 1000 | bytes 1000 | tf_op jit(solution)/shard_map/block_product/pallas_call | solution.py:53
  16.9 0.0 collective-permute-done.rest_1_
  16.9 0.0 collective-permute-done.1.rest_2_
  16.9 0.0 collective-permute-done.2.rest_3_
  16.9 0.0 copy-done.8
  16.9 0.0 copy-done.10
  16.9 3.1 %pick_adapters.1 = (bf16[6,16,3072]{2,1,0:T(8,128)(2,1)S(1)}, bf16[6,16,3072]{2,1,0:T(8,128)(2,1)S(1)}, bf16[6,16,3072]{2,1,0:T(8,128)(2,1)S(1)}, bf16[6,16,3072...) custom-call(s32[1]{0:T(128)} %bitcast.me_ref, s32[512]{0:T(512)S(1)} %copy-done.8, s32[1,12]{1,0:T(1,128)S(1)} %copy-done.10, ...), custom_call_target="tpu_custom_call" | custom-call | flops 1000 | bytes 1000 | tf_op jit(solution)/shard_map/pick_adapters/pallas_call | solution.py:199
  20.0 0.6 collective-permute-start.3
  20.6 2.2 %collective-permute-start.4 = (bf16[6,16,3072]{2,1,0:T(8,128)(2,1)S(1)}, bf16[6,16,3072]{2,1,0:T(8,128)(2,1)S(1)}, u32[]{:S(2)}, u32[]{:S(2)}) collective-permute-start(bf16[6,16,3072]{2,1,0:T(8,128)(2,1)S(1)} %get-tuple-element.25), channel_id=1, source_target_pairs={{0,8},{4,12},{8,0},{12,4},{1,9},{5,13},{9,1},{13,5},{2,10},{6,14},... | collective-permute-start | bytes 1769480 | tf_op jit(solution)/shard_map/ppermute | solution.py:379
  22.8 0.1 collective-permute-start.5
  22.9 0.0 collective-permute-done.6.rest_0_
  22.9 2.8 %block_product.10.rest_1_ = bf16[512,512]{1,0:T(8,128)(2,1)S(1)} custom-call(s32[1]{0:T(128)} %bitcast.5.first_ref, bf16[512,2048]{1,0:T(8,128)(2,1)S(1)} %get-tuple-element.17.rows_ref, bf16[2048,4096]{1,0:T(8,128)(2,1)} %weight_ref.17, bf16[512,512]{1,0:T(8,128)(2,1)} %collective-permute-done.6.rest_0_, s32[24]{0:T(128)S(1)} %get-tuple-element.21.rest_1_.start_ref), custom_call_target="tpu_custom_call" | custom-call | flops 1000 | bytes 1000 | tf_op jit(solution)/shard_map/block_product/pallas_call | solution.py:53
  25.7 6.2 %collective-permute-start.7 = (bf16[512,512]{1,0:T(8,128)(2,1)S(1)}, bf16[512,512]{1,0:T(8,128)(2,1)S(1)}, u32[]{:S(2)}, u32[]{:S(2)}) collective-permute-start(bf16[512,512]{1,0:T(8,128)(2,1)S(1)} %block_product.10.rest_1_), channel_id=1, source_target_pairs={{0,1},{1,2},{2,3},{3,0},{4,7},{5,4},{6,5},{7,6},{8,9},{9,10},{10,1... | collective-permute-start | bytes 1572872 | tf_op jit(solution)/shard_map/ppermute | solution.py:347
  31.9 0.0 collective-permute-done.8.rest_0_
  31.9 3.5 %block_product.11.rest_0_ = bf16[512,512]{1,0:T(8,128)(2,1)} custom-call(s32[1]{0:T(128)} %bitcast.7.first_ref, bf16[512,2048]{1,0:T(8,128)(2,1)S(1)} %get-tuple-element.17.rows_ref, bf16[2048,4096]{1,0:T(8,128)(2,1)} %weight_ref.17, bf16[512,512]{1,0:T(8,128)(2,1)} %collective-permute-done.8.rest_0_, bf16[512,512]{1,0:T(8,128)(2,1)S(1)} %block_product.10.rest_1_), custom_call_target="tpu_custom_call" | custom-call | flops 1000 | bytes 1000 | tf_op jit(solution)/shard_map/block_product/pallas_call | solution.py:53
  35.4 3.7 %collective-permute-start.12 = (bf16[512,512]{1,0:T(8,128)(2,1)}, bf16[512,512]{1,0:T(8,128)(2,1)}, u32[]{:S(2)}, u32[]{:S(2)}) collective-permute-start(bf16[512,512]{1,0:T(8,128)(2,1)} %block_product.11.rest_0_), channel_id=1, source_target_pairs={{0,3},{1,0},{2,1},{3,2},{4,5},{5,6},{6,7},{7,4},{8,11},{9,8},{10,9... | collective-permute-start | bytes 1572872 | tf_op jit(solution)/shard_map/ppermute | solution.py:347
  39.1 2.7 %block_product.12.rest_1_.rest_5_ = bf16[512,512]{1,0:T(8,128)(2,1)S(1)} custom-call(s32[1]{0:T(128)} %bitcast.6.first_ref, bf16[512,2048]{1,0:T(8,128)(2,1)S(1)} %get-tuple-element.17.rows_ref, bf16[2048,4096]{1,0:T(8,128)(2,1)} %weight_ref.17, bf16[512,512]{1,0:T(8,128)(2,1)} %block_product.11.rest_0_), custom_call_target="tpu_custom_call" | custom-call | flops 20000000000 | bytes 1000 | tf_op jit(solution)/shard_map/block_product/pallas_call | solution.py:53
  41.8 0.0 copy-start.6
  41.8 2.7 %collective-permute-done.7.rest_0_ = bf16[512,512]{1,0:T(8,128)(2,1)S(1)} collective-permute-done((bf16[512,512]{1,0:T(8,128)(2,1)S(1)}, bf16[512,512]{1,0:T(8,128)(2,1)S(1)}, u32[]{:S(2)}, u32[]{:S(2)}) %collective-permute-start.7) | collective-permute-done | bytes 524320 | tf_op jit(solution)/shard_map/ppermute | solution.py:347
  44.5 3.4 %block_product.13.rest_4_ = bf16[512,512]{1,0:T(8,128)(2,1)} custom-call(s32[1]{0:T(128)} %bitcast.4.first_ref, bf16[512,2048]{1,0:T(8,128)(2,1)S(1)} %get-tuple-element.17.rows_ref, bf16[2048,4096]{1,0:T(8,128)(2,1)} %weight_ref.17, bf16[512,512]{1,0:T(8,128)(2,1)S(1)} %collective-permute-done.7.rest_0_, bf16[512,512]{1,0:T(8,128)(2,1)S(1)} %block_product.12.rest_1_.rest_5_), custom_call_target="tpu_custom_call" | custom-call | flops 1000 | bytes 1000 | tf_op jit(solution)/shard_map/block_product/pallas_call | solution.py:53
  47.9 0.0 copy-done.6
  47.9 2.3 %collective-permute-start.15 = (bf16[512,512]{1,0:T(8,128)(2,1)}, bf16[512,512]{1,0:T(8,128)(2,1)}, u32[]{:S(2)}, u32[]{:S(2)}) collective-permute-start(bf16[512,512]{1,0:T(8,128)(2,1)} %block_product.13.rest_4_), channel_id=1, source_target_pairs={{0,1},{1,2},{2,3},{3,0},{4,7},{5,4},{6,5},{7,6},{8,9},{9,10},{10,1... | collective-permute-start | bytes 1572872 | tf_op jit(solution)/shard_map/ppermute | solution.py:347
  50.2 0.0 collective-permute-done.3.rest_1_.rest_7_
  50.2 0.0 collective-permute-done.4.rest_2_.rest_8_
  50.2 0.0 collective-permute-done.5.rest_3_.rest_9_
  50.2 0.0 copy-start.4
  50.2 1.6 %low_sums.1.rest_1_.rest_0_ = bf16[16,512]{1,0:T(8,128)(2,1)S(1)} custom-call(s32[24]{0:T(128)S(1)} %get-tuple-element.21.rest_1_.start_ref, s32[24]{0:T(128)S(1)} %get-tuple-element.22.end_ref, bf16[512,2048]{1,0:T(8,128)(2,1)S(1)} %get-tuple-element.17.rows_ref, bf16[6,16,3072]{2,1,0:T(8,128)(2,1)S(1)} %get-tuple-element.23.rest_0_.rest_6_, ...), custom_call_target="tpu_custom_call" | custom-call | flops 1000 | bytes 1000 | tf_op jit(solution)/shard_map/low_sums/pallas_call | solution.py:241
  51.8 0.0 copy-done.2
  51.8 0.0 copy-start
  51.8 0.8 %copy-done = bf16[6,16,3072]{2,1,0:T(8,128)(2,1)} copy-done((bf16[6,16,3072]{2,1,0:T(8,128)(2,1)}, bf16[6,16,3072]{2,1,0:T(8,128)(2,1)S(1)}, u32[]{:S(2)}) %copy-start) | copy-done | bytes 589848
  52.6 3.0 %collective-permute-start.9 = (bf16[16,512]{1,0:T(8,128)(2,1)S(1)}, bf16[16,512]{1,0:T(8,128)(2,1)S(1)}, u32[]{:S(2)}, u32[]{:S(2)}) collective-permute-start(bf16[16,512]{1,0:T(8,128)(2,1)S(1)} %low_sums.1.rest_1_.rest_0_), channel_id=1, source_target_pairs={{0,1},{1,0},{2,3},{3,2},{4,5},{5,4},{6,7},{7,6},{8,9},{9,8},{10,11... | collective-permute-start | bytes 49160 | tf_op jit(solution)/shard_map/ppermute | solution.py:389
  55.6 0.0 copy-done.4
  55.6 1.1 %collective-permute-start.10 = (bf16[16,512]{1,0:T(8,128)(2,1)S(1)}, bf16[16,512]{1,0:T(8,128)(2,1)S(1)}, u32[]{:S(2)}, u32[]{:S(2)}) collective-permute-start(bf16[16,512]{1,0:T(8,128)(2,1)S(1)} %low_sums.1.rest_1_.rest_0_), channel_id=1, source_target_pairs={{0,2},{1,3},{2,0},{3,1},{4,6},{5,7},{6,4},{7,5},{8,10},{9,11},{10,... | collective-permute-start | bytes 49160 | tf_op jit(solution)/shard_map/ppermute | solution.py:389
  56.7 1.4 %collective-permute-start.11 = (bf16[16,512]{1,0:T(8,128)(2,1)S(1)}, bf16[16,512]{1,0:T(8,128)(2,1)S(1)}, u32[]{:S(2)}, u32[]{:S(2)}) collective-permute-start(bf16[16,512]{1,0:T(8,128)(2,1)S(1)} %low_sums.1.rest_1_.rest_0_), channel_id=1, source_target_pairs={{0,3},{1,2},{2,1},{3,0},{4,7},{5,6},{6,5},{7,4},{8,11},{9,10},{10,... | collective-permute-start | bytes 49160 | tf_op jit(solution)/shard_map/ppermute | solution.py:389
  58.1 3.5 %collective-permute-done.12.rest_0_ = bf16[512,512]{1,0:T(8,128)(2,1)} collective-permute-done((bf16[512,512]{1,0:T(8,128)(2,1)}, bf16[512,512]{1,0:T(8,128)(2,1)}, u32[]{:S(2)}, u32[]{:S(2)}) %collective-permute-start.12) | collective-permute-done | bytes 524320 | tf_op jit(solution)/shard_map/ppermute | solution.py:347
  61.6 3.6 %block_product.14.rest_1_ = bf16[512,384]{1,0:T(8,128)(2,1)S(1)} custom-call(s32[1]{0:T(128)} %bitcast.9.first_ref, bf16[512,2048]{1,0:T(8,128)(2,1)S(1)} %get-tuple-element.17.rows_ref, bf16[2048,4096]{1,0:T(8,128)(2,1)} %weight_ref.17, bf16[512,512]{1,0:T(8,128)(2,1)} %collective-permute-done.12.rest_0_, bf16[16,512]{1,0:T(8,128)(2,1)S(1)} %low_sums.1.rest_1_.rest_0_), custom_call_target="tpu_custom_call" | custom-call | flops 1000 | bytes 1000 | tf_op jit(solution)/shard_map/block_product/pallas_call | solution.py:53
  65.3 0.1 collective-permute-start.14
  65.3 0.0 copy-start.1
  65.3 0.0 copy-start.3
  65.4 0.0 copy-start.5
  65.4 0.0 copy-start.7
  65.4 1.9 %block_product.15.rest_10_ = bf16[512,128]{1,0:T(8,128)(2,1)S(1)} custom-call(s32[1]{0:T(128)} %bitcast.8.first_ref, bf16[512,2048]{1,0:T(8,128)(2,1)S(1)} %get-tuple-element.17.rows_ref, bf16[2048,4096]{1,0:T(8,128)(2,1)} %weight_ref.17, bf16[512,512]{1,0:T(8,128)(2,1)} %collective-permute-done.12.rest_0_, bf16[512,384]{1,0:T(8,128)(2,1)S(1)} %block_product.14.rest_1_), custom_call_target="tpu_custom_call" | custom-call | flops 1000 | bytes 1000 | tf_op jit(solution)/shard_map/block_product/pallas_call | solution.py:53
  67.3 0.0 collective-permute-done.9.rest_1_
  67.3 2.8 %collective-permute-start.13 = (bf16[512,128]{1,0:T(8,128)(2,1)S(1)}, bf16[512,128]{1,0:T(8,128)(2,1)S(1)}, u32[]{:S(2)}, u32[]{:S(2)}) collective-permute-start(bf16[512,128]{1,0:T(8,128)(2,1)S(1)} %block_product.15.rest_10_), channel_id=1, source_target_pairs={{0,3},{1,0},{2,1},{3,2},{4,5},{5,6},{6,7},{7,4},{8,11},{9,8},{10,9... | collective-permute-start | bytes 393224 | tf_op jit(solution)/shard_map/ppermute | solution.py:347
  70.1 0.0 collective-permute-done.10.rest_2_
  70.1 0.0 collective-permute-done.11.rest_3_
  70.1 0.0 copy-done.1
  70.1 0.0 copy-done.3
  70.1 0.0 copy-done.5
  70.2 1.3 %adapter_term.1 = (f32[512,512]{1,0:T(8,128)S(1)}, f32[512,512]{1,0:T(8,128)S(1)}) custom-call(s32[24]{0:T(128)S(1)} %get-tuple-element.21.rest_1_.start_ref, s32[24]{0:T(128)S(1)} %get-tuple-element.22.end_ref, bf16[16,512]{1,0:T(8,128)(2,1)S(1)} %low_sums.1.rest_1_.rest_0_, bf16[16,512]{1,0:T(8,128)(2,1)S(1)} %collective-permute-done.9.rest_1_, ...), custom_call_target="tpu_custom_call" | custom-call | flops 1000 | bytes 1000 | tf_op jit(solution)/shard_map/adapter_term/pallas_call | solution.py:288
  71.4 0.0 collective-permute-done.15.rest_0_
  71.5 1.8 %finish.3.rest_1_ = bf16[512,1024]{1,0:T(8,128)(2,1)} custom-call(f32[512,512]{1,0:T(8,128)S(1)} %get-tuple-element.28.term_ref, bf16[512,512]{1,0:T(8,128)(2,1)} %collective-permute-done.15.rest_0_), custom_call_target="tpu_custom_call" | custom-call | flops 20000000000 | bytes 1000 | tf_op jit(solution)/shard_map/finish/pallas_call | solution.py:315
  73.2 4.0 %collective-permute-done.14.rest_0_ = bf16[512,384]{1,0:T(8,128)(2,1)S(1)} collective-permute-done((bf16[512,384]{1,0:T(8,128)(2,1)S(1)}, bf16[512,384]{1,0:T(8,128)(2,1)S(1)}, u32[]{:S(2)}, u32[]{:S(2)}) %collective-permute-start.14) | collective-permute-done | bytes 393248 | tf_op jit(solution)/shard_map/ppermute | solution.py:347
  77.2 0.9 %finish.4.rest_1_ = bf16[512,1024]{1,0:T(8,128)(2,1)} custom-call(f32[512,512]{1,0:T(8,128)S(1)} %get-tuple-element.27.term_ref, bf16[512,384]{1,0:T(8,128)(2,1)S(1)} %collective-permute-done.14.rest_0_, bf16[512,1024]{1,0:T(8,128)(2,1)} %finish.3.rest_1_), custom_call_target="tpu_custom_call", output_to_operand_aliasing={{}: (2, {})} | custom-call | flops 1000 | bytes 1000 | tf_op jit(solution)/shard_map/finish/pallas_call | solution.py:315
  78.1 1.6 %collective-permute-done.13.rest_0_ = bf16[512,128]{1,0:T(8,128)(2,1)S(1)} collective-permute-done((bf16[512,128]{1,0:T(8,128)(2,1)S(1)}, bf16[512,128]{1,0:T(8,128)(2,1)S(1)}, u32[]{:S(2)}, u32[]{:S(2)}) %collective-permute-start.13) | collective-permute-done | bytes 131104 | tf_op jit(solution)/shard_map/ppermute | solution.py:347
  79.7 0.7 finish.5
  (5 shorter events, 0.0 us)
Async XLA Ops:
  0.0 6.6 %copy-start.9 = (s32[1,12]{1,0:T(1,128)S(1)}, s32[1,12]{1,0:T(1,128)}, u32[]{:S(2)}) copy-start(s32[1,12]{1,0:T(1,128)} %rest_0_.1) | copy-start | bytes 148
  3.5 19.4 %collective-permute-start.6 = (bf16[512,512]{1,0:T(8,128)(2,1)}, bf16[512,512]{1,0:T(8,128)(2,1)}, u32[]{:S(2)}, u32[]{:S(2)}) collective-permute-start(bf16[512,512]{1,0:T(8,128)(2,1)} %get-tuple-element.18.rest_1_), channel_id=1, source_target_pairs={{0,1},{1,2},{2,3},{3,0},{4,7},{5,4},{6,5},{7,6},{8,9},{9,10},{10,1... | collective-permute-start | bytes 1572872 | tf_op jit(solution)/shard_map/ppermute | solution.py:347
  10.0 21.9 %collective-permute-start.8 = (bf16[512,512]{1,0:T(8,128)(2,1)}, bf16[512,512]{1,0:T(8,128)(2,1)}, u32[]{:S(2)}, u32[]{:S(2)}) collective-permute-start(bf16[512,512]{1,0:T(8,128)(2,1)} %get-tuple-element.20.rest_0_), channel_id=1, source_target_pairs={{0,3},{1,0},{2,1},{3,2},{4,5},{5,6},{6,7},{7,4},{8,11},{9,8},{10,9... | collective-permute-start | bytes 1572872 | tf_op jit(solution)/shard_map/ppermute | solution.py:347
  12.2 4.7 %collective-permute-start = (s32[1,12]{1,0:T(1,128)S(1)}, s32[1,12]{1,0:T(1,128)S(1)}, u32[]{:S(2)}, u32[]{:S(2)}) collective-permute-start(s32[1,12]{1,0:T(1,128)S(1)} %get-tuple-element.19.rest_0_), channel_id=1, source_target_pairs={{0,4},{4,0},{8,12},{12,8},{1,5},{5,1},{9,13},{13,9},{2,6},{6,2},{1... | collective-permute-start | bytes 152 | tf_op jit(solution)/shard_map/ppermute | solution.py:374
  12.2 4.7 %collective-permute-start.1 = (s32[1,12]{1,0:T(1,128)S(1)}, s32[1,12]{1,0:T(1,128)S(1)}, u32[]{:S(2)}, u32[]{:S(2)}) collective-permute-start(s32[1,12]{1,0:T(1,128)S(1)} %get-tuple-element.19.rest_0_), channel_id=1, source_target_pairs={{0,8},{4,12},{8,0},{12,4},{1,9},{5,13},{9,1},{13,5},{2,10},{6,14},... | collective-permute-start | bytes 152 | tf_op jit(solution)/shard_map/ppermute | solution.py:374
  13.8 3.0 %collective-permute-start.2 = (s32[1,12]{1,0:T(1,128)S(1)}, s32[1,12]{1,0:T(1,128)S(1)}, u32[]{:S(2)}, u32[]{:S(2)}) collective-permute-start(s32[1,12]{1,0:T(1,128)S(1)} %get-tuple-element.19.rest_0_), channel_id=1, source_target_pairs={{0,12},{4,8},{8,4},{12,0},{1,13},{5,9},{9,5},{13,1},{2,14},{6,10},... | collective-permute-start | bytes 152 | tf_op jit(solution)/shard_map/ppermute | solution.py:374
  14.0 2.9 %copy-start.8 = (s32[512]{0:T(512)S(1)}, s32[512]{0:T(512)}, u32[]{:S(2)}) copy-start(s32[512]{0:T(512)} %table_ref.1) | copy-start | bytes 6148
  14.0 2.9 %copy-start.10 = (s32[1,12]{1,0:T(1,128)S(1)}, s32[1,12]{1,0:T(1,128)}, u32[]{:S(2)}) copy-start(s32[1,12]{1,0:T(1,128)} %lens_ref.1) | copy-start | bytes 148
  20.0 30.2 %collective-permute-start.3 = (bf16[6,16,3072]{2,1,0:T(8,128)(2,1)S(1)}, bf16[6,16,3072]{2,1,0:T(8,128)(2,1)S(1)}, u32[]{:S(2)}, u32[]{:S(2)}) collective-permute-start(bf16[6,16,3072]{2,1,0:T(8,128)(2,1)S(1)} %get-tuple-element.24), channel_id=1, source_target_pairs={{0,4},{4,0},{8,12},{12,8},{1,5},{5,1},{9,13},{13,9},{2,6},{6,2},{1... | collective-permute-start | bytes 1769480 | tf_op jit(solution)/shard_map/ppermute | solution.py:379
  20.6 29.6 %collective-permute-start.4 = (bf16[6,16,3072]{2,1,0:T(8,128)(2,1)S(1)}, bf16[6,16,3072]{2,1,0:T(8,128)(2,1)S(1)}, u32[]{:S(2)}, u32[]{:S(2)}) collective-permute-start(bf16[6,16,3072]{2,1,0:T(8,128)(2,1)S(1)} %get-tuple-element.25), channel_id=1, source_target_pairs={{0,8},{4,12},{8,0},{12,4},{1,9},{5,13},{9,1},{13,5},{2,10},{6,14},... | collective-permute-start | bytes 1769480 | tf_op jit(solution)/shard_map/ppermute | solution.py:379
  22.8 27.4 %collective-permute-start.5 = (bf16[6,16,3072]{2,1,0:T(8,128)(2,1)S(1)}, bf16[6,16,3072]{2,1,0:T(8,128)(2,1)S(1)}, u32[]{:S(2)}, u32[]{:S(2)}) collective-permute-start(bf16[6,16,3072]{2,1,0:T(8,128)(2,1)S(1)} %get-tuple-element.26), channel_id=1, source_target_pairs={{0,12},{4,8},{8,4},{12,0},{1,13},{5,9},{9,5},{13,1},{2,14},{6,10},... | collective-permute-start | bytes 1769480 | tf_op jit(solution)/shard_map/ppermute | solution.py:379
  25.7 18.8 %collective-permute-start.7 = (bf16[512,512]{1,0:T(8,128)(2,1)S(1)}, bf16[512,512]{1,0:T(8,128)(2,1)S(1)}, u32[]{:S(2)}, u32[]{:S(2)}) collective-permute-start(bf16[512,512]{1,0:T(8,128)(2,1)S(1)} %block_product.10.rest_1_), channel_id=1, source_target_pairs={{0,1},{1,2},{2,3},{3,0},{4,7},{5,4},{6,5},{7,6},{8,9},{9,10},{10,1... | collective-permute-start | bytes 1572872 | tf_op jit(solution)/shard_map/ppermute | solution.py:347
  35.4 26.2 %collective-permute-start.12 = (bf16[512,512]{1,0:T(8,128)(2,1)}, bf16[512,512]{1,0:T(8,128)(2,1)}, u32[]{:S(2)}, u32[]{:S(2)}) collective-permute-start(bf16[512,512]{1,0:T(8,128)(2,1)} %block_product.11.rest_0_), channel_id=1, source_target_pairs={{0,3},{1,0},{2,1},{3,2},{4,5},{5,6},{6,7},{7,4},{8,11},{9,8},{10,9... | collective-permute-start | bytes 1572872 | tf_op jit(solution)/shard_map/ppermute | solution.py:347
  41.8 6.1 %copy-start.6 = (bf16[512,512]{1,0:T(8,128)(2,1)}, bf16[512,512]{1,0:T(8,128)(2,1)S(1)}, u32[]{:S(2)}) copy-start(bf16[512,512]{1,0:T(8,128)(2,1)S(1)} %block_product.12.rest_1_.rest_5_) | copy-start | bytes 1572868
  47.9 23.6 %collective-permute-start.15 = (bf16[512,512]{1,0:T(8,128)(2,1)}, bf16[512,512]{1,0:T(8,128)(2,1)}, u32[]{:S(2)}, u32[]{:S(2)}) collective-permute-start(bf16[512,512]{1,0:T(8,128)(2,1)} %block_product.13.rest_4_), channel_id=1, source_target_pairs={{0,1},{1,2},{2,3},{3,0},{4,7},{5,4},{6,5},{7,6},{8,9},{9,10},{10,1... | collective-permute-start | bytes 1572872 | tf_op jit(solution)/shard_map/ppermute | solution.py:347
  50.2 1.6 %copy-start.2 = (bf16[6,16,3072]{2,1,0:T(8,128)(2,1)}, bf16[6,16,3072]{2,1,0:T(8,128)(2,1)S(1)}, u32[]{:S(2)}) copy-start(bf16[6,16,3072]{2,1,0:T(8,128)(2,1)S(1)} %collective-permute-done.4.rest_2_.rest_8_) | copy-start | bytes 1769476
  50.2 5.4 %copy-start.4 = (bf16[6,16,3072]{2,1,0:T(8,128)(2,1)}, bf16[6,16,3072]{2,1,0:T(8,128)(2,1)S(1)}, u32[]{:S(2)}) copy-start(bf16[6,16,3072]{2,1,0:T(8,128)(2,1)S(1)} %collective-permute-done.5.rest_3_.rest_9_) | copy-start | bytes 1769476
  51.8 0.8 %copy-start = (bf16[6,16,3072]{2,1,0:T(8,128)(2,1)}, bf16[6,16,3072]{2,1,0:T(8,128)(2,1)S(1)}, u32[]{:S(2)}) copy-start(bf16[6,16,3072]{2,1,0:T(8,128)(2,1)S(1)} %collective-permute-done.3.rest_1_.rest_7_) | copy-start | bytes 1769476
  52.6 14.7 %collective-permute-start.9 = (bf16[16,512]{1,0:T(8,128)(2,1)S(1)}, bf16[16,512]{1,0:T(8,128)(2,1)S(1)}, u32[]{:S(2)}, u32[]{:S(2)}) collective-permute-start(bf16[16,512]{1,0:T(8,128)(2,1)S(1)} %low_sums.1.rest_1_.rest_0_), channel_id=1, source_target_pairs={{0,1},{1,0},{2,3},{3,2},{4,5},{5,4},{6,7},{7,6},{8,9},{9,8},{10,11... | collective-permute-start | bytes 49160 | tf_op jit(solution)/shard_map/ppermute | solution.py:389
  55.6 14.6 %collective-permute-start.10 = (bf16[16,512]{1,0:T(8,128)(2,1)S(1)}, bf16[16,512]{1,0:T(8,128)(2,1)S(1)}, u32[]{:S(2)}, u32[]{:S(2)}) collective-permute-start(bf16[16,512]{1,0:T(8,128)(2,1)S(1)} %low_sums.1.rest_1_.rest_0_), channel_id=1, source_target_pairs={{0,2},{1,3},{2,0},{3,1},{4,6},{5,7},{6,4},{7,5},{8,10},{9,11},{10,... | collective-permute-start | bytes 49160 | tf_op jit(solution)/shard_map/ppermute | solution.py:389
  56.7 13.4 %collective-permute-start.11 = (bf16[16,512]{1,0:T(8,128)(2,1)S(1)}, bf16[16,512]{1,0:T(8,128)(2,1)S(1)}, u32[]{:S(2)}, u32[]{:S(2)}) collective-permute-start(bf16[16,512]{1,0:T(8,128)(2,1)S(1)} %low_sums.1.rest_1_.rest_0_), channel_id=1, source_target_pairs={{0,3},{1,2},{2,1},{3,0},{4,7},{5,6},{6,5},{7,4},{8,11},{9,10},{10,... | collective-permute-start | bytes 49160 | tf_op jit(solution)/shard_map/ppermute | solution.py:389
  65.3 12.0 %collective-permute-start.14 = (bf16[512,384]{1,0:T(8,128)(2,1)S(1)}, bf16[512,384]{1,0:T(8,128)(2,1)S(1)}, u32[]{:S(2)}, u32[]{:S(2)}) collective-permute-start(bf16[512,384]{1,0:T(8,128)(2,1)S(1)} %block_product.14.rest_1_), channel_id=1, source_target_pairs={{0,3},{1,0},{2,1},{3,2},{4,5},{5,6},{6,7},{7,4},{8,11},{9,8},{10,9... | collective-permute-start | bytes 1179656 | tf_op jit(solution)/shard_map/ppermute | solution.py:347
  65.3 4.8 %copy-start.1 = (bf16[6,16,3072]{2,1,0:T(8,128)(2,1)S(1)}, bf16[6,16,3072]{2,1,0:T(8,128)(2,1)}, u32[]{:S(2)}) copy-start(bf16[6,16,3072]{2,1,0:T(8,128)(2,1)} %copy-done) | copy-start | bytes 1769476
  65.3 4.8 %copy-start.3 = (bf16[6,16,3072]{2,1,0:T(8,128)(2,1)S(1)}, bf16[6,16,3072]{2,1,0:T(8,128)(2,1)}, u32[]{:S(2)}) copy-start(bf16[6,16,3072]{2,1,0:T(8,128)(2,1)} %copy-done.2) | copy-start | bytes 1769476
  65.4 4.8 %copy-start.5 = (bf16[6,16,3072]{2,1,0:T(8,128)(2,1)S(1)}, bf16[6,16,3072]{2,1,0:T(8,128)(2,1)}, u32[]{:S(2)}) copy-start(bf16[6,16,3072]{2,1,0:T(8,128)(2,1)} %copy-done.4) | copy-start | bytes 1769476
  65.4 4.8 %copy-start.7 = (bf16[512,512]{1,0:T(8,128)(2,1)S(1)}, bf16[512,512]{1,0:T(8,128)(2,1)}, u32[]{:S(2)}) copy-start(bf16[512,512]{1,0:T(8,128)(2,1)} %copy-done.6) | copy-start | bytes 1572868
  67.3 12.4 %collective-permute-start.13 = (bf16[512,128]{1,0:T(8,128)(2,1)S(1)}, bf16[512,128]{1,0:T(8,128)(2,1)S(1)}, u32[]{:S(2)}, u32[]{:S(2)}) collective-permute-start(bf16[512,128]{1,0:T(8,128)(2,1)S(1)} %block_product.15.rest_10_), channel_id=1, source_target_pairs={{0,3},{1,0},{2,1},{3,2},{4,5},{5,6},{6,7},{7,4},{8,11},{9,8},{10,9... | collective-permute-start | bytes 393224 | tf_op jit(solution)/shard_map/ppermute | solution.py:347

commit v23 on v21

--- a/solution.py
+++ b/solution.py
@@ -9,7 +9,7 @@
 
 CAP = 6
 PIECES = 2
-VMEM_LIMIT = 20 * 1024 * 1024
+VMEM_LIMIT = 12 * 1024 * 1024
 F32 = jnp.float32
 BF16 = jnp.bfloat16
 SMALL = pl.CostEstimate(flops=1000, bytes_accessed=1000, transcendentals=0)

time: 79.5 us -> 79.5 us (level)
  transfers between devices with their start and end apart: 16 -> 16, of which waited for: 4 -> 4; matrix products, arithmetic and copies ran while one was open for 0% -> 0% of each run, Pallas kernels for 39% -> 40%
where the time goes in v23:
time: 79.5 us; the launch traced here: 79.1 us
  Pallas kernels  35.7 us (45%)
  starting transfers between devices  32.1 us (40%)
  waiting for transfers between devices  10.2 us (13%)
  local copies, waits for them, and re-layouts  0.85 us (1%)
    pallas_call x8, Pallas kernels, block_product(): pl.pallas_call(functools.partial(product_kernel, len(addends), with_ids),...  22.6 us
    ppermute x7, starting transfers between devices, move(): return lax.ppermute(value, ('req', 'tp'), pairs)  22.3 us
    ppermute x7, waiting for transfers between devices, move(): return lax.ppermute(value, ('req', 'tp'), pairs)  8.85 us
    ppermute x3, starting transfers between devices, local(): lows.append(lax.ppermute(low, 'tp', pairs))  5.5 us
    pallas_call x1, Pallas kernels, first_product(): pl.pallas_call(functools.partial(first_kernel, chunk), in_specs=[pl.Block...  3.49 us
    pallas_call x3, Pallas kernels, finish(): pl.pallas_call(functools.partial(finish_kernel, 1), grid=(row_total // he...  3.38 us
    pallas_call x1, Pallas kernels, pick_adapters(): pl.pallas_call(functools.partial(pick_kernel, peers, len(after)), in_spec...  3.35 us
    ppermute x3, starting transfers between devices, local(): lax.ppermute(packs[x], 'req', [(i, i ^ x) for i in range(req_total)])  2.39 us
  transfers between devices with their start and end apart: 16, of which 4 were waited for; matrix products, arithmetic and copies ran while one was open for 0% of the time, Pallas kernels for 40%

profile of v23, /device:TPU:0, one launch (start us, length us, event | category | flops | bytes accessed | tf_op | source)
XLA Modules:
  0.0 79.1 jit_solution(637161032689755064)
XLA Ops:
  0.0 3.5 %first_product.1 = (bf16[512,512]{1,0:T(8,128)(2,1)}, bf16[512,2048]{1,0:T(8,128)(2,1)S(1)}) custom-call(s32[1]{0:T(128)} %bitcast.2.first_ref, bf16[512,2048]{1,0:T(8,128)(2,1)} %rows_ref.1, bf16[2048,4096]{1,0:T(8,128)(2,1)} %weight_ref.17), custom_call_target="tpu_custom_call" | custom-call | flops 1000 | bytes 1000 | tf_op jit(solution)/shard_map/first_product/pallas_call | solution.py:108
  3.5 3.1 %collective-permute-start.6 = (bf16[512,512]{1,0:T(8,128)(2,1)}, bf16[512,512]{1,0:T(8,128)(2,1)}, u32[]{:S(2)}, u32[]{:S(2)}) collective-permute-start(bf16[512,512]{1,0:T(8,128)(2,1)} %get-tuple-element.18.rest_1_), channel_id=1, source_target_pairs={{0,1},{1,2},{2,3},{3,0},{4,7},{5,4},{6,5},{7,6},{8,9},{9,10},{10,1... | collective-permute-start | bytes 1572872 | tf_op jit(solution)/shard_map/ppermute | solution.py:345
  6.6 0.0 copy-done.9
  6.6 3.4 %block_product.8 = (bf16[512,512]{1,0:T(8,128)(2,1)}, s32[1,12]{1,0:T(1,128)S(1)}) custom-call(s32[1]{0:T(128)} %bitcast.1.first_ref, bf16[512,2048]{1,0:T(8,128)(2,1)S(1)} %get-tuple-element.17.rows_ref, bf16[2048,4096]{1,0:T(8,128)(2,1)} %weight_ref.17, s32[1,12]{1,0:T(1,128)S(1)} %copy-done.9, bf16[512,512]{1,0:T(8,128)(2,1)} %get-tuple-element.18.rest_1_), custom_call_target="tpu_custom_call" | custom-call | flops 1000 | bytes 1000 | tf_op jit(solution)/shard_map/block_product/pallas_call | solution.py:53
  10.0 2.1 %collective-permute-start.8 = (bf16[512,512]{1,0:T(8,128)(2,1)}, bf16[512,512]{1,0:T(8,128)(2,1)}, u32[]{:S(2)}, u32[]{:S(2)}) collective-permute-start(bf16[512,512]{1,0:T(8,128)(2,1)} %get-tuple-element.20.rest_0_), channel_id=1, source_target_pairs={{0,3},{1,0},{2,1},{3,2},{4,5},{5,6},{6,7},{7,4},{8,11},{9,8},{10,9... | collective-permute-start | bytes 1572872 | tf_op jit(solution)/shard_map/ppermute | solution.py:345
  12.2 0.0 collective-permute-start
  12.2 1.7 %collective-permute-start.1 = (s32[1,12]{1,0:T(1,128)S(1)}, s32[1,12]{1,0:T(1,128)S(1)}, u32[]{:S(2)}, u32[]{:S(2)}) collective-permute-start(s32[1,12]{1,0:T(1,128)S(1)} %get-tuple-element.19.rest_0_), channel_id=1, source_target_pairs={{0,8},{4,12},{8,0},{12,4},{1,9},{5,13},{9,1},{13,5},{2,10},{6,14},... | collective-permute-start | bytes 152 | tf_op jit(solution)/shard_map/ppermute | solution.py:368
  13.8 0.2 collective-permute-start.2
  14.0 2.7 %block_product.9.rest_6_.rest_4_ = bf16[512,512]{1,0:T(8,128)(2,1)S(1)} custom-call(s32[1]{0:T(128)} %bitcast.3.first_ref, bf16[512,2048]{1,0:T(8,128)(2,1)S(1)} %get-tuple-element.17.rows_ref, bf16[2048,4096]{1,0:T(8,128)(2,1)} %weight_ref.17, bf16[512,512]{1,0:T(8,128)(2,1)} %get-tuple-element.20.rest_0_), custom_call_target="tpu_custom_call" | custom-call | flops 1000 | bytes 1000 | tf_op jit(solution)/shard_map/block_product/pallas_call | solution.py:53
  16.9 0.0 collective-permute-done.rest_1_
  16.9 0.0 collective-permute-done.1.rest_2_
  16.9 0.0 collective-permute-done.2.rest_3_
  16.9 0.0 copy-done.8
  16.9 0.0 copy-done.10
  16.9 3.3 %pick_adapters.1 = (bf16[6,16,3072]{2,1,0:T(8,128)(2,1)S(1)}, bf16[6,16,3072]{2,1,0:T(8,128)(2,1)S(1)}, bf16[6,16,3072]{2,1,0:T(8,128)(2,1)S(1)}, bf16[6,16,3072...) custom-call(s32[1]{0:T(128)} %bitcast.me_ref, s32[512]{0:T(512)S(1)} %copy-done.8, s32[1,12]{1,0:T(1,128)S(1)} %copy-done.10, ...), custom_call_target="tpu_custom_call" | custom-call | flops 1000 | bytes 1000 | tf_op jit(solution)/shard_map/pick_adapters/pallas_call | solution.py:199
  20.3 0.7 collective-permute-start.3
  20.9 1.7 %collective-permute-start.4 = (bf16[6,16,3072]{2,1,0:T(8,128)(2,1)S(1)}, bf16[6,16,3072]{2,1,0:T(8,128)(2,1)S(1)}, u32[]{:S(2)}, u32[]{:S(2)}) collective-permute-start(bf16[6,16,3072]{2,1,0:T(8,128)(2,1)S(1)} %get-tuple-element.25), channel_id=1, source_target_pairs={{0,8},{4,12},{8,0},{12,4},{1,9},{5,13},{9,1},{13,5},{2,10},{6,14},... | collective-permute-start | bytes 1769480 | tf_op jit(solution)/shard_map/ppermute | solution.py:373
  22.7 0.0 collective-permute-start.5
  22.7 0.0 collective-permute-done.6.rest_0_
  22.7 2.8 %block_product.10.rest_1_ = bf16[512,512]{1,0:T(8,128)(2,1)S(1)} custom-call(s32[1]{0:T(128)} %bitcast.5.first_ref, bf16[512,2048]{1,0:T(8,128)(2,1)S(1)} %get-tuple-element.17.rows_ref, bf16[2048,4096]{1,0:T(8,128)(2,1)} %weight_ref.17, bf16[512,512]{1,0:T(8,128)(2,1)} %collective-permute-done.6.rest_0_, s32[24]{0:T(128)S(1)} %get-tuple-element.21.rest_1_.start_ref), custom_call_target="tpu_custom_call" | custom-call | flops 1000 | bytes 1000 | tf_op jit(solution)/shard_map/block_product/pallas_call | solution.py:53
  25.5 6.5 %collective-permute-start.7 = (bf16[512,512]{1,0:T(8,128)(2,1)S(1)}, bf16[512,512]{1,0:T(8,128)(2,1)S(1)}, u32[]{:S(2)}, u32[]{:S(2)}) collective-permute-start(bf16[512,512]{1,0:T(8,128)(2,1)S(1)} %block_product.10.rest_1_), channel_id=1, source_target_pairs={{0,1},{1,2},{2,3},{3,0},{4,7},{5,4},{6,5},{7,6},{8,9},{9,10},{10,1... | collective-permute-start | bytes 1572872 | tf_op jit(solution)/shard_map/ppermute | solution.py:345
  31.9 0.0 collective-permute-done.8.rest_0_
  31.9 3.5 %block_product.11.rest_0_ = bf16[512,512]{1,0:T(8,128)(2,1)} custom-call(s32[1]{0:T(128)} %bitcast.7.first_ref, bf16[512,2048]{1,0:T(8,128)(2,1)S(1)} %get-tuple-element.17.rows_ref, bf16[2048,4096]{1,0:T(8,128)(2,1)} %weight_ref.17, bf16[512,512]{1,0:T(8,128)(2,1)} %collective-permute-done.8.rest_0_, bf16[512,512]{1,0:T(8,128)(2,1)S(1)} %block_product.10.rest_1_), custom_call_target="tpu_custom_call" | custom-call | flops 1000 | bytes 1000 | tf_op jit(solution)/shard_map/block_product/pallas_call | solution.py:53
  35.4 3.7 %collective-permute-start.12 = (bf16[512,512]{1,0:T(8,128)(2,1)}, bf16[512,512]{1,0:T(8,128)(2,1)}, u32[]{:S(2)}, u32[]{:S(2)}) collective-permute-start(bf16[512,512]{1,0:T(8,128)(2,1)} %block_product.11.rest_0_), channel_id=1, source_target_pairs={{0,3},{1,0},{2,1},{3,2},{4,5},{5,6},{6,7},{7,4},{8,11},{9,8},{10,9... | collective-permute-start | bytes 1572872 | tf_op jit(solution)/shard_map/ppermute | solution.py:345
  39.1 2.7 %block_product.12.rest_1_.rest_5_ = bf16[512,512]{1,0:T(8,128)(2,1)S(1)} custom-call(s32[1]{0:T(128)} %bitcast.6.first_ref, bf16[512,2048]{1,0:T(8,128)(2,1)S(1)} %get-tuple-element.17.rows_ref, bf16[2048,4096]{1,0:T(8,128)(2,1)} %weight_ref.17, bf16[512,512]{1,0:T(8,128)(2,1)} %block_product.11.rest_0_), custom_call_target="tpu_custom_call" | custom-call | flops 20000000000 | bytes 1000 | tf_op jit(solution)/shard_map/block_product/pallas_call | solution.py:53
  41.8 0.0 copy-start.6
  41.8 2.7 %collective-permute-done.7.rest_0_ = bf16[512,512]{1,0:T(8,128)(2,1)S(1)} collective-permute-done((bf16[512,512]{1,0:T(8,128)(2,1)S(1)}, bf16[512,512]{1,0:T(8,128)(2,1)S(1)}, u32[]{:S(2)}, u32[]{:S(2)}) %collective-permute-start.7) | collective-permute-done | bytes 524320 | tf_op jit(solution)/shard_map/ppermute | solution.py:345
  44.5 3.4 %block_product.13.rest_4_ = bf16[512,512]{1,0:T(8,128)(2,1)} custom-call(s32[1]{0:T(128)} %bitcast.4.first_ref, bf16[512,2048]{1,0:T(8,128)(2,1)S(1)} %get-tuple-element.17.rows_ref, bf16[2048,4096]{1,0:T(8,128)(2,1)} %weight_ref.17, bf16[512,512]{1,0:T(8,128)(2,1)S(1)} %collective-permute-done.7.rest_0_, bf16[512,512]{1,0:T(8,128)(2,1)S(1)} %block_product.12.rest_1_.rest_5_), custom_call_target="tpu_custom_call" | custom-call | flops 1000 | bytes 1000 | tf_op jit(solution)/shard_map/block_product/pallas_call | solution.py:53
  47.9 0.0 copy-done.6
  47.9 2.3 %collective-permute-start.15 = (bf16[512,512]{1,0:T(8,128)(2,1)}, bf16[512,512]{1,0:T(8,128)(2,1)}, u32[]{:S(2)}, u32[]{:S(2)}) collective-permute-start(bf16[512,512]{1,0:T(8,128)(2,1)} %block_product.13.rest_4_), channel_id=1, source_target_pairs={{0,1},{1,2},{2,3},{3,0},{4,7},{5,4},{6,5},{7,6},{8,9},{9,10},{10,1... | collective-permute-start | bytes 1572872 | tf_op jit(solution)/shard_map/ppermute | solution.py:345
  50.2 0.0 collective-permute-done.3.rest_1_.rest_7_
  50.2 0.0 collective-permute-done.4.rest_2_.rest_8_
  50.2 0.0 collective-permute-done.5.rest_3_.rest_9_
  50.2 0.0 copy-start.4
  50.2 1.6 %low_sums.1.rest_1_.rest_0_ = bf16[16,512]{1,0:T(8,128)(2,1)S(1)} custom-call(s32[24]{0:T(128)S(1)} %get-tuple-element.21.rest_1_.start_ref, s32[24]{0:T(128)S(1)} %get-tuple-element.22.end_ref, bf16[512,2048]{1,0:T(8,128)(2,1)S(1)} %get-tuple-element.17.rows_ref, bf16[6,16,3072]{2,1,0:T(8,128)(2,1)S(1)} %get-tuple-element.23.rest_0_.rest_6_, ...), custom_call_target="tpu_custom_call" | custom-call | flops 1000 | bytes 1000 | tf_op jit(solution)/shard_map/low_sums/pallas_call | solution.py:241
  51.8 0.0 copy-done.2
  51.8 0.0 copy-start
  51.8 0.8 %copy-done = bf16[6,16,3072]{2,1,0:T(8,128)(2,1)} copy-done((bf16[6,16,3072]{2,1,0:T(8,128)(2,1)}, bf16[6,16,3072]{2,1,0:T(8,128)(2,1)S(1)}, u32[]{:S(2)}) %copy-start) | copy-done | bytes 589848
  52.6 3.0 %collective-permute-start.9 = (bf16[16,512]{1,0:T(8,128)(2,1)S(1)}, bf16[16,512]{1,0:T(8,128)(2,1)S(1)}, u32[]{:S(2)}, u32[]{:S(2)}) collective-permute-start(bf16[16,512]{1,0:T(8,128)(2,1)S(1)} %low_sums.1.rest_1_.rest_0_), channel_id=1, source_target_pairs={{0,1},{1,0},{2,3},{3,2},{4,5},{5,4},{6,7},{7,6},{8,9},{9,8},{10,11... | collective-permute-start | bytes 49160 | tf_op jit(solution)/shard_map/ppermute | solution.py:383
  55.6 0.0 copy-done.4
  55.6 1.1 %collective-permute-start.10 = (bf16[16,512]{1,0:T(8,128)(2,1)S(1)}, bf16[16,512]{1,0:T(8,128)(2,1)S(1)}, u32[]{:S(2)}, u32[]{:S(2)}) collective-permute-start(bf16[16,512]{1,0:T(8,128)(2,1)S(1)} %low_sums.1.rest_1_.rest_0_), channel_id=1, source_target_pairs={{0,2},{1,3},{2,0},{3,1},{4,6},{5,7},{6,4},{7,5},{8,10},{9,11},{10,... | collective-permute-start | bytes 49160 | tf_op jit(solution)/shard_map/ppermute | solution.py:383
  56.7 1.4 %collective-permute-start.11 = (bf16[16,512]{1,0:T(8,128)(2,1)S(1)}, bf16[16,512]{1,0:T(8,128)(2,1)S(1)}, u32[]{:S(2)}, u32[]{:S(2)}) collective-permute-start(bf16[16,512]{1,0:T(8,128)(2,1)S(1)} %low_sums.1.rest_1_.rest_0_), channel_id=1, source_target_pairs={{0,3},{1,2},{2,1},{3,0},{4,7},{5,6},{6,5},{7,4},{8,11},{9,10},{10,... | collective-permute-start | bytes 49160 | tf_op jit(solution)/shard_map/ppermute | solution.py:383
  58.1 3.5 %collective-permute-done.12.rest_0_ = bf16[512,512]{1,0:T(8,128)(2,1)} collective-permute-done((bf16[512,512]{1,0:T(8,128)(2,1)}, bf16[512,512]{1,0:T(8,128)(2,1)}, u32[]{:S(2)}, u32[]{:S(2)}) %collective-permute-start.12) | collective-permute-done | bytes 524320 | tf_op jit(solution)/shard_map/ppermute | solution.py:345
  61.6 2.0 %block_product.14.rest_1_ = bf16[512,256]{1,0:T(8,128)(2,1)S(1)} custom-call(s32[1]{0:T(128)} %bitcast.9.first_ref, bf16[512,2048]{1,0:T(8,128)(2,1)S(1)} %get-tuple-element.17.rows_ref, bf16[2048,4096]{1,0:T(8,128)(2,1)} %weight_ref.17, bf16[512,512]{1,0:T(8,128)(2,1)} %collective-permute-done.12.rest_0_, bf16[16,512]{1,0:T(8,128)(2,1)S(1)} %low_sums.1.rest_1_.rest_0_), custom_call_target="tpu_custom_call" | custom-call | flops 1000 | bytes 1000 | tf_op jit(solution)/shard_map/block_product/pallas_call | solution.py:53
  63.6 0.1 collective-permute-start.14
  63.7 0.0 copy-start.1
  63.7 0.0 copy-start.3
  63.7 0.0 copy-start.5
  63.7 0.0 copy-start.7
  63.7 2.1 %block_product.15.rest_10_ = bf16[512,256]{1,0:T(8,128)(2,1)S(1)} custom-call(s32[1]{0:T(128)} %bitcast.8.first_ref, bf16[512,2048]{1,0:T(8,128)(2,1)S(1)} %get-tuple-element.17.rows_ref, bf16[2048,4096]{1,0:T(8,128)(2,1)} %weight_ref.17, bf16[512,512]{1,0:T(8,128)(2,1)} %collective-permute-done.12.rest_0_, bf16[512,256]{1,0:T(8,128)(2,1)S(1)} %block_product.14.rest_1_), custom_call_target="tpu_custom_call" | custom-call | flops 1000 | bytes 1000 | tf_op jit(solution)/shard_map/block_product/pallas_call | solution.py:53
  65.9 1.3 %collective-permute-done.9.rest_1_ = bf16[16,512]{1,0:T(8,128)(2,1)S(1)} collective-permute-done((bf16[16,512]{1,0:T(8,128)(2,1)S(1)}, bf16[16,512]{1,0:T(8,128)(2,1)S(1)}, u32[]{:S(2)}, u32[]{:S(2)}) %collective-permute-start.9) | collective-permute-done | bytes 16416 | tf_op jit(solution)/shard_map/ppermute | solution.py:383
  67.2 4.6 %collective-permute-start.13 = (bf16[512,256]{1,0:T(8,128)(2,1)S(1)}, bf16[512,256]{1,0:T(8,128)(2,1)S(1)}, u32[]{:S(2)}, u32[]{:S(2)}) collective-permute-start(bf16[512,256]{1,0:T(8,128)(2,1)S(1)} %block_product.15.rest_10_), channel_id=1, source_target_pairs={{0,3},{1,0},{2,1},{3,2},{4,5},{5,6},{6,7},{7,4},{8,11},{9,8},{10,9... | collective-permute-start | bytes 786440 | tf_op jit(solution)/shard_map/ppermute | solution.py:345
  71.8 0.0 collective-permute-done.10.rest_2_
  71.8 0.0 collective-permute-done.11.rest_3_
  71.8 0.0 copy-done.1
  71.8 0.0 copy-done.3
  71.8 0.0 copy-done.5
  71.8 1.3 %adapter_term.1 = (f32[512,512]{1,0:T(8,128)S(1)}, f32[512,512]{1,0:T(8,128)S(1)}) custom-call(s32[24]{0:T(128)S(1)} %get-tuple-element.21.rest_1_.start_ref, s32[24]{0:T(128)S(1)} %get-tuple-element.22.end_ref, bf16[16,512]{1,0:T(8,128)(2,1)S(1)} %low_sums.1.rest_1_.rest_0_, bf16[16,512]{1,0:T(8,128)(2,1)S(1)} %collective-permute-done.9.rest_1_, ...), custom_call_target="tpu_custom_call" | custom-call | flops 1000 | bytes 1000 | tf_op jit(solution)/shard_map/adapter_term/pallas_call | solution.py:287
  73.1 0.0 collective-permute-done.15.rest_0_
  73.1 1.8 %finish.3.rest_1_ = bf16[512,1024]{1,0:T(8,128)(2,1)} custom-call(f32[512,512]{1,0:T(8,128)S(1)} %get-tuple-element.28.term_ref, bf16[512,512]{1,0:T(8,128)(2,1)} %collective-permute-done.15.rest_0_), custom_call_target="tpu_custom_call" | custom-call | flops 20000000000 | bytes 1000 | tf_op jit(solution)/shard_map/finish/pallas_call | solution.py:314
  74.9 0.0 collective-permute-done.14.rest_0_
  74.9 0.8 finish.4.rest_1_
  75.7 2.6 %collective-permute-done.13.rest_0_ = bf16[512,256]{1,0:T(8,128)(2,1)S(1)} collective-permute-done((bf16[512,256]{1,0:T(8,128)(2,1)S(1)}, bf16[512,256]{1,0:T(8,128)(2,1)S(1)}, u32[]{:S(2)}, u32[]{:S(2)}) %collective-permute-start.13) | collective-permute-done | bytes 262176 | tf_op jit(solution)/shard_map/ppermute | solution.py:345
  78.3 0.8 %finish.5 = bf16[512,1024]{1,0:T(8,128)(2,1)} custom-call(f32[512,512]{1,0:T(8,128)S(1)} %get-tuple-element.27.term_ref, bf16[512,256]{1,0:T(8,128)(2,1)S(1)} %collective-permute-done.13.rest_0_, bf16[512,1024]{1,0:T(8,128)(2,1)} %finish.4.rest_1_), custom_call_target="tpu_custom_call", output_to_operand_aliasing={{}: (2, {})} | custom-call | flops 1000 | bytes 1000 | tf_op jit(solution)/shard_map/finish/pallas_call | solution.py:314
  (5 shorter events, 0.0 us)
Async XLA Ops:
  0.0 6.6 %copy-start.9 = (s32[1,12]{1,0:T(1,128)S(1)}, s32[1,12]{1,0:T(1,128)}, u32[]{:S(2)}) copy-start(s32[1,12]{1,0:T(1,128)} %rest_0_.1) | copy-start | bytes 148
  3.5 19.2 %collective-permute-start.6 = (bf16[512,512]{1,0:T(8,128)(2,1)}, bf16[512,512]{1,0:T(8,128)(2,1)}, u32[]{:S(2)}, u32[]{:S(2)}) collective-permute-start(bf16[512,512]{1,0:T(8,128)(2,1)} %get-tuple-element.18.rest_1_), channel_id=1, source_target_pairs={{0,1},{1,2},{2,3},{3,0},{4,7},{5,4},{6,5},{7,6},{8,9},{9,10},{10,1... | collective-permute-start | bytes 1572872 | tf_op jit(solution)/shard_map/ppermute | solution.py:345
  10.0 21.9 %collective-permute-start.8 = (bf16[512,512]{1,0:T(8,128)(2,1)}, bf16[512,512]{1,0:T(8,128)(2,1)}, u32[]{:S(2)}, u32[]{:S(2)}) collective-permute-start(bf16[512,512]{1,0:T(8,128)(2,1)} %get-tuple-element.20.rest_0_), channel_id=1, source_target_pairs={{0,3},{1,0},{2,1},{3,2},{4,5},{5,6},{6,7},{7,4},{8,11},{9,8},{10,9... | collective-permute-start | bytes 1572872 | tf_op jit(solution)/shard_map/ppermute | solution.py:345
  12.2 4.7 %collective-permute-start = (s32[1,12]{1,0:T(1,128)S(1)}, s32[1,12]{1,0:T(1,128)S(1)}, u32[]{:S(2)}, u32[]{:S(2)}) collective-permute-start(s32[1,12]{1,0:T(1,128)S(1)} %get-tuple-element.19.rest_0_), channel_id=1, source_target_pairs={{0,4},{4,0},{8,12},{12,8},{1,5},{5,1},{9,13},{13,9},{2,6},{6,2},{1... | collective-permute-start | bytes 152 | tf_op jit(solution)/shard_map/ppermute | solution.py:368
  12.2 4.7 %collective-permute-start.1 = (s32[1,12]{1,0:T(1,128)S(1)}, s32[1,12]{1,0:T(1,128)S(1)}, u32[]{:S(2)}, u32[]{:S(2)}) collective-permute-start(s32[1,12]{1,0:T(1,128)S(1)} %get-tuple-element.19.rest_0_), channel_id=1, source_target_pairs={{0,8},{4,12},{8,0},{12,4},{1,9},{5,13},{9,1},{13,5},{2,10},{6,14},... | collective-permute-start | bytes 152 | tf_op jit(solution)/shard_map/ppermute | solution.py:368
  13.8 3.0 %collective-permute-start.2 = (s32[1,12]{1,0:T(1,128)S(1)}, s32[1,12]{1,0:T(1,128)S(1)}, u32[]{:S(2)}, u32[]{:S(2)}) collective-permute-start(s32[1,12]{1,0:T(1,128)S(1)} %get-tuple-element.19.rest_0_), channel_id=1, source_target_pairs={{0,12},{4,8},{8,4},{12,0},{1,13},{5,9},{9,5},{13,1},{2,14},{6,10},... | collective-permute-start | bytes 152 | tf_op jit(solution)/shard_map/ppermute | solution.py:368
  14.0 2.9 %copy-start.8 = (s32[512]{0:T(512)S(1)}, s32[512]{0:T(512)}, u32[]{:S(2)}) copy-start(s32[512]{0:T(512)} %table_ref.1) | copy-start | bytes 6148
  14.0 2.9 %copy-start.10 = (s32[1,12]{1,0:T(1,128)S(1)}, s32[1,12]{1,0:T(1,128)}, u32[]{:S(2)}) copy-start(s32[1,12]{1,0:T(1,128)} %lens_ref.1) | copy-start | bytes 148
  20.3 29.9 %collective-permute-start.3 = (bf16[6,16,3072]{2,1,0:T(8,128)(2,1)S(1)}, bf16[6,16,3072]{2,1,0:T(8,128)(2,1)S(1)}, u32[]{:S(2)}, u32[]{:S(2)}) collective-permute-start(bf16[6,16,3072]{2,1,0:T(8,128)(2,1)S(1)} %get-tuple-element.24), channel_id=1, source_target_pairs={{0,4},{4,0},{8,12},{12,8},{1,5},{5,1},{9,13},{13,9},{2,6},{6,2},{1... | collective-permute-start | bytes 1769480 | tf_op jit(solution)/shard_map/ppermute | solution.py:373
  20.9 29.2 %collective-permute-start.4 = (bf16[6,16,3072]{2,1,0:T(8,128)(2,1)S(1)}, bf16[6,16,3072]{2,1,0:T(8,128)(2,1)S(1)}, u32[]{:S(2)}, u32[]{:S(2)}) collective-permute-start(bf16[6,16,3072]{2,1,0:T(8,128)(2,1)S(1)} %get-tuple-element.25), channel_id=1, source_target_pairs={{0,8},{4,12},{8,0},{12,4},{1,9},{5,13},{9,1},{13,5},{2,10},{6,14},... | collective-permute-start | bytes 1769480 | tf_op jit(solution)/shard_map/ppermute | solution.py:373
  22.7 27.5 %collective-permute-start.5 = (bf16[6,16,3072]{2,1,0:T(8,128)(2,1)S(1)}, bf16[6,16,3072]{2,1,0:T(8,128)(2,1)S(1)}, u32[]{:S(2)}, u32[]{:S(2)}) collective-permute-start(bf16[6,16,3072]{2,1,0:T(8,128)(2,1)S(1)} %get-tuple-element.26), channel_id=1, source_target_pairs={{0,12},{4,8},{8,4},{12,0},{1,13},{5,9},{9,5},{13,1},{2,14},{6,10},... | collective-permute-start | bytes 1769480 | tf_op jit(solution)/shard_map/ppermute | solution.py:373
  25.5 19.0 %collective-permute-start.7 = (bf16[512,512]{1,0:T(8,128)(2,1)S(1)}, bf16[512,512]{1,0:T(8,128)(2,1)S(1)}, u32[]{:S(2)}, u32[]{:S(2)}) collective-permute-start(bf16[512,512]{1,0:T(8,128)(2,1)S(1)} %block_product.10.rest_1_), channel_id=1, source_target_pairs={{0,1},{1,2},{2,3},{3,0},{4,7},{5,4},{6,5},{7,6},{8,9},{9,10},{10,1... | collective-permute-start | bytes 1572872 | tf_op jit(solution)/shard_map/ppermute | solution.py:345
  35.4 26.2 %collective-permute-start.12 = (bf16[512,512]{1,0:T(8,128)(2,1)}, bf16[512,512]{1,0:T(8,128)(2,1)}, u32[]{:S(2)}, u32[]{:S(2)}) collective-permute-start(bf16[512,512]{1,0:T(8,128)(2,1)} %block_product.11.rest_0_), channel_id=1, source_target_pairs={{0,3},{1,0},{2,1},{3,2},{4,5},{5,6},{6,7},{7,4},{8,11},{9,8},{10,9... | collective-permute-start | bytes 1572872 | tf_op jit(solution)/shard_map/ppermute | solution.py:345
  41.8 6.1 %copy-start.6 = (bf16[512,512]{1,0:T(8,128)(2,1)}, bf16[512,512]{1,0:T(8,128)(2,1)S(1)}, u32[]{:S(2)}) copy-start(bf16[512,512]{1,0:T(8,128)(2,1)S(1)} %block_product.12.rest_1_.rest_5_) | copy-start | bytes 1572868
  47.9 25.2 %collective-permute-start.15 = (bf16[512,512]{1,0:T(8,128)(2,1)}, bf16[512,512]{1,0:T(8,128)(2,1)}, u32[]{:S(2)}, u32[]{:S(2)}) collective-permute-start(bf16[512,512]{1,0:T(8,128)(2,1)} %block_product.13.rest_4_), channel_id=1, source_target_pairs={{0,1},{1,2},{2,3},{3,0},{4,7},{5,4},{6,5},{7,6},{8,9},{9,10},{10,1... | collective-permute-start | bytes 1572872 | tf_op jit(solution)/shard_map/ppermute | solution.py:345
  50.2 1.6 %copy-start.2 = (bf16[6,16,3072]{2,1,0:T(8,128)(2,1)}, bf16[6,16,3072]{2,1,0:T(8,128)(2,1)S(1)}, u32[]{:S(2)}) copy-start(bf16[6,16,3072]{2,1,0:T(8,128)(2,1)S(1)} %collective-permute-done.4.rest_2_.rest_8_) | copy-start | bytes 1769476
  50.2 5.4 %copy-start.4 = (bf16[6,16,3072]{2,1,0:T(8,128)(2,1)}, bf16[6,16,3072]{2,1,0:T(8,128)(2,1)S(1)}, u32[]{:S(2)}) copy-start(bf16[6,16,3072]{2,1,0:T(8,128)(2,1)S(1)} %collective-permute-done.5.rest_3_.rest_9_) | copy-start | bytes 1769476
  51.8 0.8 %copy-start = (bf16[6,16,3072]{2,1,0:T(8,128)(2,1)}, bf16[6,16,3072]{2,1,0:T(8,128)(2,1)S(1)}, u32[]{:S(2)}) copy-start(bf16[6,16,3072]{2,1,0:T(8,128)(2,1)S(1)} %collective-permute-done.3.rest_1_.rest_7_) | copy-start | bytes 1769476
  52.6 14.6 %collective-permute-start.9 = (bf16[16,512]{1,0:T(8,128)(2,1)S(1)}, bf16[16,512]{1,0:T(8,128)(2,1)S(1)}, u32[]{:S(2)}, u32[]{:S(2)}) collective-permute-start(bf16[16,512]{1,0:T(8,128)(2,1)S(1)} %low_sums.1.rest_1_.rest_0_), channel_id=1, source_target_pairs={{0,1},{1,0},{2,3},{3,2},{4,5},{5,4},{6,7},{7,6},{8,9},{9,8},{10,11... | collective-permute-start | bytes 49160 | tf_op jit(solution)/shard_map/ppermute | solution.py:383
  55.6 16.2 %collective-permute-start.10 = (bf16[16,512]{1,0:T(8,128)(2,1)S(1)}, bf16[16,512]{1,0:T(8,128)(2,1)S(1)}, u32[]{:S(2)}, u32[]{:S(2)}) collective-permute-start(bf16[16,512]{1,0:T(8,128)(2,1)S(1)} %low_sums.1.rest_1_.rest_0_), channel_id=1, source_target_pairs={{0,2},{1,3},{2,0},{3,1},{4,6},{5,7},{6,4},{7,5},{8,10},{9,11},{10,... | collective-permute-start | bytes 49160 | tf_op jit(solution)/shard_map/ppermute | solution.py:383
  56.7 15.1 %collective-permute-start.11 = (bf16[16,512]{1,0:T(8,128)(2,1)S(1)}, bf16[16,512]{1,0:T(8,128)(2,1)S(1)}, u32[]{:S(2)}, u32[]{:S(2)}) collective-permute-start(bf16[16,512]{1,0:T(8,128)(2,1)S(1)} %low_sums.1.rest_1_.rest_0_), channel_id=1, source_target_pairs={{0,3},{1,2},{2,1},{3,0},{4,7},{5,6},{6,5},{7,4},{8,11},{9,10},{10,... | collective-permute-start | bytes 49160 | tf_op jit(solution)/shard_map/ppermute | solution.py:383
  63.6 11.3 %collective-permute-start.14 = (bf16[512,256]{1,0:T(8,128)(2,1)S(1)}, bf16[512,256]{1,0:T(8,128)(2,1)S(1)}, u32[]{:S(2)}, u32[]{:S(2)}) collective-permute-start(bf16[512,256]{1,0:T(8,128)(2,1)S(1)} %block_product.14.rest_1_), channel_id=1, source_target_pairs={{0,3},{1,0},{2,1},{3,2},{4,5},{5,6},{6,7},{7,4},{8,11},{9,8},{10,9... | collective-permute-start | bytes 786440 | tf_op jit(solution)/shard_map/ppermute | solution.py:345
  63.7 8.1 %copy-start.1 = (bf16[6,16,3072]{2,1,0:T(8,128)(2,1)S(1)}, bf16[6,16,3072]{2,1,0:T(8,128)(2,1)}, u32[]{:S(2)}) copy-start(bf16[6,16,3072]{2,1,0:T(8,128)(2,1)} %copy-done) | copy-start | bytes 1769476
  63.7 8.1 %copy-start.3 = (bf16[6,16,3072]{2,1,0:T(8,128)(2,1)S(1)}, bf16[6,16,3072]{2,1,0:T(8,128)(2,1)}, u32[]{:S(2)}) copy-start(bf16[6,16,3072]{2,1,0:T(8,128)(2,1)} %copy-done.2) | copy-start | bytes 1769476
  63.7 8.1 %copy-start.5 = (bf16[6,16,3072]{2,1,0:T(8,128)(2,1)S(1)}, bf16[6,16,3072]{2,1,0:T(8,128)(2,1)}, u32[]{:S(2)}) copy-start(bf16[6,16,3072]{2,1,0:T(8,128)(2,1)} %copy-done.4) | copy-start | bytes 1769476
  63.7 8.1 %copy-start.7 = (bf16[512,512]{1,0:T(8,128)(2,1)S(1)}, bf16[512,512]{1,0:T(8,128)(2,1)}, u32[]{:S(2)}) copy-start(bf16[512,512]{1,0:T(8,128)(2,1)} %copy-done.6) | copy-start | bytes 1572868
  67.2 11.2 %collective-permute-start.13 = (bf16[512,256]{1,0:T(8,128)(2,1)S(1)}, bf16[512,256]{1,0:T(8,128)(2,1)S(1)}, u32[]{:S(2)}, u32[]{:S(2)}) collective-permute-start(bf16[512,256]{1,0:T(8,128)(2,1)S(1)} %block_product.15.rest_10_), channel_id=1, source_target_pairs={{0,3},{1,0},{2,1},{3,2},{4,5},{5,6},{6,7},{7,4},{8,11},{9,8},{10,9... | collective-permute-start | bytes 786440 | tf_op jit(solution)/shard_map/ppermute | solution.py:345

commit v24 on v21

--- a/solution.py
+++ b/solution.py
@@ -359,15 +359,15 @@
     last, rows = first_product(rows, weight, start_of(1, 0), width)
     rows = pltpu.with_memory_space_constraint(rows, pltpu.VMEM)
     moving = [move(last, 0)]
-    for piece in range(1, PIECES):
-        last, ids = partial(1, piece, after=[last], ids=ids)
-        moving.append(move(last, piece))
+    last, ids = partial(0, 0, after=[last], ids=ids)
+    owns = [last]
 
     all_ids = [ids]
     for x in range(1, req_total):
         all_ids.append(lax.ppermute(ids, "req", [(i, i ^ x) for i in range(req_total)]))
-    last = partial(0, 0, after=[last])
-    owns = [last]
+    for piece in range(1, PIECES):
+        last = partial(1, piece, after=[last])
+        moving.append(move(last, piece))
     packs, starts, ends = pick_adapters(me_req, table, all_ids, lens, down, up, [last])
     for x in range(1, req_total):
         packs[x] = lax.ppermute(packs[x], "req", [(i, i ^ x) for i in range(req_total)])

time: 79.5 us -> 80.5 us (1.013)
  waiting for transfers between devices: 10.2 us -> 12.6 us
  starting transfers between devices: 32.3 us -> 30 us
  Pallas kernels: 35.5 us -> 36.4 us
    ppermute x3, waiting for transfers between devices: 0.01 us -> 2.75 us  [local(): lax.ppermute(ids, 'req', [(i, i ^ x) for i in range(req_total)])]
    ppermute x7, starting transfers between devices: 22.3 us -> 20.4 us  [move(): return lax.ppermute(value, ('req', 'tp'), pairs)]
    ppermute x3, waiting for transfers between devices: 1.29 us -> 0.01 us  [local(): lows.append(lax.ppermute(low, 'tp', pairs))]
    ppermute x7, waiting for transfers between devices: 8.85 us -> 9.8 us  [move(): return lax.ppermute(value, ('req', 'tp'), pairs)]
  transfers between devices with their start and end apart: 16 -> 16, of which waited for: 4 -> 6; matrix products, arithmetic and copies ran while one was open for 0% -> 0% of each run, Pallas kernels for 39% -> 40%
where the time goes in v24:
time: 80.5 us; the launch traced here: 80 us
  Pallas kernels  36.4 us (45%)
  starting transfers between devices  30 us (37%)
  waiting for transfers between devices  12.6 us (16%)
  local copies, waits for them, and re-layouts  0.85 us (1%)
    pallas_call x8, Pallas kernels, block_product(): pl.pallas_call(functools.partial(product_kernel, len(addends), with_ids),...  22.8 us
    ppermute x7, starting transfers between devices, move(): return lax.ppermute(value, ('req', 'tp'), pairs)  20.4 us
    ppermute x7, waiting for transfers between devices, move(): return lax.ppermute(value, ('req', 'tp'), pairs)  9.8 us
    ppermute x3, starting transfers between devices, local(): lows.append(lax.ppermute(low, 'tp', pairs))  5.85 us
    pallas_call x1, Pallas kernels, pick_adapters(): pl.pallas_call(functools.partial(pick_kernel, peers, len(after)), in_spec...  3.84 us
    pallas_call x1, Pallas kernels, first_product(): pl.pallas_call(functools.partial(first_kernel, chunk), in_specs=[pl.Block...  3.49 us
    pallas_call x3, Pallas kernels, finish(): pl.pallas_call(functools.partial(finish_kernel, 1), grid=(row_total // he...  3.39 us
    ppermute x3, waiting for transfers between devices, local(): lax.ppermute(ids, 'req', [(i, i ^ x) for i in range(req_total)])  2.75 us
  transfers between devices with their start and end apart: 16, of which 6 were waited for; matrix products, arithmetic and copies ran while one was open for 0% of the time, Pallas kernels for 40%

profile of v24, /device:TPU:0, one launch (start us, length us, event | category | flops | bytes accessed | tf_op | source)
XLA Modules:
  0.0 80.0 jit_solution(11265985990483816298)
XLA Ops:
  0.0 3.5 %first_product.1 = (bf16[512,512]{1,0:T(8,128)(2,1)}, bf16[512,2048]{1,0:T(8,128)(2,1)S(1)}) custom-call(s32[1]{0:T(128)} %bitcast.2.first_ref, bf16[512,2048]{1,0:T(8,128)(2,1)} %rows_ref.1, bf16[2048,4096]{1,0:T(8,128)(2,1)} %weight_ref.17), custom_call_target="tpu_custom_call" | custom-call | flops 1000 | bytes 1000 | tf_op jit(solution)/shard_map/first_product/pallas_call | solution.py:108
  3.5 3.1 %collective-permute-start.6 = (bf16[512,512]{1,0:T(8,128)(2,1)}, bf16[512,512]{1,0:T(8,128)(2,1)}, u32[]{:S(2)}, u32[]{:S(2)}) collective-permute-start(bf16[512,512]{1,0:T(8,128)(2,1)} %get-tuple-element.18.rest_1_), channel_id=1, source_target_pairs={{0,1},{1,2},{2,3},{3,0},{4,7},{5,4},{6,5},{7,6},{8,9},{9,10},{10,1... | collective-permute-start | bytes 1572872 | tf_op jit(solution)/shard_map/ppermute | solution.py:345
  6.6 0.0 copy-done.9
  6.6 2.7 %block_product.8 = (bf16[512,512]{1,0:T(8,128)(2,1)S(1)}, s32[1,12]{1,0:T(1,128)S(1)}) custom-call(s32[1]{0:T(128)} %bitcast.1.first_ref, bf16[512,2048]{1,0:T(8,128)(2,1)S(1)} %get-tuple-element.17.rows_ref, bf16[2048,4096]{1,0:T(8,128)(2,1)} %weight_ref.17, s32[1,12]{1,0:T(1,128)S(1)} %copy-done.9, bf16[512,512]{1,0:T(8,128)(2,1)} %get-tuple-element.18.rest_1_), custom_call_target="tpu_custom_call" | custom-call | flops 1000 | bytes 1000 | tf_op jit(solution)/shard_map/block_product/pallas_call | solution.py:53
  9.3 0.0 copy-start.4
  9.3 0.0 copy-start.8
  9.4 0.0 copy-start.10
  9.4 3.6 %block_product.9.rest_6_ = bf16[512,512]{1,0:T(8,128)(2,1)} custom-call(s32[1]{0:T(128)} %bitcast.3.first_ref, bf16[512,2048]{1,0:T(8,128)(2,1)S(1)} %get-tuple-element.17.rows_ref, bf16[2048,4096]{1,0:T(8,128)(2,1)} %weight_ref.17, bf16[512,512]{1,0:T(8,128)(2,1)S(1)} %get-tuple-element.20.rest_0_.rest_4_), custom_call_target="tpu_custom_call" | custom-call | flops 1000 | bytes 1000 | tf_op jit(solution)/shard_map/block_product/pallas_call | solution.py:53
  13.0 0.0 copy-done.4
  13.0 2.1 %collective-permute-start.8 = (bf16[512,512]{1,0:T(8,128)(2,1)}, bf16[512,512]{1,0:T(8,128)(2,1)}, u32[]{:S(2)}, u32[]{:S(2)}) collective-permute-start(bf16[512,512]{1,0:T(8,128)(2,1)} %block_product.9.rest_6_), channel_id=1, source_target_pairs={{0,3},{1,0},{2,1},{3,2},{4,5},{5,6},{6,7},{7,4},{8,11},{9,8},{10,9... | collective-permute-start | bytes 1572872 | tf_op jit(solution)/shard_map/ppermute | solution.py:345
  15.1 0.0 collective-permute-start
  15.1 1.6 %collective-permute-start.1 = (s32[1,12]{1,0:T(1,128)S(1)}, s32[1,12]{1,0:T(1,128)S(1)}, u32[]{:S(2)}, u32[]{:S(2)}) collective-permute-start(s32[1,12]{1,0:T(1,128)S(1)} %get-tuple-element.19.rest_0_), channel_id=1, source_target_pairs={{0,8},{4,12},{8,0},{12,4},{1,9},{5,13},{9,1},{13,5},{2,10},{6,14},... | collective-permute-start | bytes 152 | tf_op jit(solution)/shard_map/ppermute | solution.py:367
  16.7 0.2 collective-permute-start.2
  16.9 0.0 collective-permute-done.rest_1_
  17.0 1.7 %collective-permute-done.1.rest_2_ = s32[1,12]{1,0:T(1,128)S(1)} collective-permute-done((s32[1,12]{1,0:T(1,128)S(1)}, s32[1,12]{1,0:T(1,128)S(1)}, u32[]{:S(2)}, u32[]{:S(2)}) %collective-permute-start.1) | collective-permute-done | bytes 80 | tf_op jit(solution)/shard_map/ppermute | solution.py:367
  18.6 1.1 %collective-permute-done.2.rest_3_ = s32[1,12]{1,0:T(1,128)S(1)} collective-permute-done((s32[1,12]{1,0:T(1,128)S(1)}, s32[1,12]{1,0:T(1,128)S(1)}, u32[]{:S(2)}, u32[]{:S(2)}) %collective-permute-start.2) | collective-permute-done | bytes 80 | tf_op jit(solution)/shard_map/ppermute | solution.py:367
  19.7 0.0 copy-done.8
  19.7 0.0 copy-done.10
  19.7 3.8 %pick_adapters.1 = (bf16[6,16,3072]{2,1,0:T(8,128)(2,1)S(1)}, bf16[6,16,3072]{2,1,0:T(8,128)(2,1)S(1)}, bf16[6,16,3072]{2,1,0:T(8,128)(2,1)S(1)}, bf16[6,16,3072...) custom-call(s32[1]{0:T(128)} %bitcast.me_ref, s32[512]{0:T(512)S(1)} %copy-done.8, s32[1,12]{1,0:T(1,128)S(1)} %copy-done.10, ...), custom_call_target="tpu_custom_call" | custom-call | flops 1000 | bytes 1000 | tf_op jit(solution)/shard_map/pick_adapters/pallas_call | solution.py:199
  23.6 0.3 collective-permute-start.3
  23.8 0.3 collective-permute-start.4
  24.1 1.4 %collective-permute-start.5 = (bf16[6,16,3072]{2,1,0:T(8,128)(2,1)S(1)}, bf16[6,16,3072]{2,1,0:T(8,128)(2,1)S(1)}, u32[]{:S(2)}, u32[]{:S(2)}) collective-permute-start(bf16[6,16,3072]{2,1,0:T(8,128)(2,1)S(1)} %get-tuple-element.26), channel_id=1, source_target_pairs={{0,12},{4,8},{8,4},{12,0},{1,13},{5,9},{9,5},{13,1},{2,14},{6,10},... | collective-permute-start | bytes 1769480 | tf_op jit(solution)/shard_map/ppermute | solution.py:373
  25.5 0.0 collective-permute-done.6.rest_0_
  25.5 2.8 %block_product.10.rest_1_ = bf16[512,512]{1,0:T(8,128)(2,1)S(1)} custom-call(s32[1]{0:T(128)} %bitcast.5.first_ref, bf16[512,2048]{1,0:T(8,128)(2,1)S(1)} %get-tuple-element.17.rows_ref, bf16[2048,4096]{1,0:T(8,128)(2,1)} %weight_ref.17, bf16[512,512]{1,0:T(8,128)(2,1)} %collective-permute-done.6.rest_0_, s32[24]{0:T(128)S(1)} %get-tuple-element.21.rest_1_.start_ref), custom_call_target="tpu_custom_call" | custom-call | flops 1000 | bytes 1000 | tf_op jit(solution)/shard_map/block_product/pallas_call | solution.py:53
  28.3 0.8 collective-permute-start.7
  29.0 0.5 collective-permute-done.8.rest_0_
  29.6 3.5 %block_product.11.rest_0_ = bf16[512,512]{1,0:T(8,128)(2,1)} custom-call(s32[1]{0:T(128)} %bitcast.7.first_ref, bf16[512,2048]{1,0:T(8,128)(2,1)S(1)} %get-tuple-element.17.rows_ref, bf16[2048,4096]{1,0:T(8,128)(2,1)} %weight_ref.17, bf16[512,512]{1,0:T(8,128)(2,1)} %collective-permute-done.8.rest_0_, bf16[512,512]{1,0:T(8,128)(2,1)S(1)} %block_product.10.rest_1_), custom_call_target="tpu_custom_call" | custom-call | flops 1000 | bytes 1000 | tf_op jit(solution)/shard_map/block_product/pallas_call | solution.py:53
  33.0 4.3 %collective-permute-start.12 = (bf16[512,512]{1,0:T(8,128)(2,1)}, bf16[512,512]{1,0:T(8,128)(2,1)}, u32[]{:S(2)}, u32[]{:S(2)}) collective-permute-start(bf16[512,512]{1,0:T(8,128)(2,1)} %block_product.11.rest_0_), channel_id=1, source_target_pairs={{0,3},{1,0},{2,1},{3,2},{4,5},{5,6},{6,7},{7,4},{8,11},{9,8},{10,9... | collective-permute-start | bytes 1572872 | tf_op jit(solution)/shard_map/ppermute | solution.py:345
  37.3 2.7 %block_product.12.rest_1_.rest_5_ = bf16[512,512]{1,0:T(8,128)(2,1)S(1)} custom-call(s32[1]{0:T(128)} %bitcast.6.first_ref, bf16[512,2048]{1,0:T(8,128)(2,1)S(1)} %get-tuple-element.17.rows_ref, bf16[2048,4096]{1,0:T(8,128)(2,1)} %weight_ref.17, bf16[512,512]{1,0:T(8,128)(2,1)} %block_product.11.rest_0_), custom_call_target="tpu_custom_call" | custom-call | flops 20000000000 | bytes 1000 | tf_op jit(solution)/shard_map/block_product/pallas_call | solution.py:53
  40.0 0.0 copy-start.6
  40.0 5.6 %collective-permute-done.7.rest_0_ = bf16[512,512]{1,0:T(8,128)(2,1)S(1)} collective-permute-done((bf16[512,512]{1,0:T(8,128)(2,1)S(1)}, bf16[512,512]{1,0:T(8,128)(2,1)S(1)}, u32[]{:S(2)}, u32[]{:S(2)}) %collective-permute-start.7) | collective-permute-done | bytes 524320 | tf_op jit(solution)/shard_map/ppermute | solution.py:345
  45.7 3.4 %block_product.13.rest_4_ = bf16[512,512]{1,0:T(8,128)(2,1)} custom-call(s32[1]{0:T(128)} %bitcast.4.first_ref, bf16[512,2048]{1,0:T(8,128)(2,1)S(1)} %get-tuple-element.17.rows_ref, bf16[2048,4096]{1,0:T(8,128)(2,1)} %weight_ref.17, bf16[512,512]{1,0:T(8,128)(2,1)S(1)} %collective-permute-done.7.rest_0_, bf16[512,512]{1,0:T(8,128)(2,1)S(1)} %block_product.12.rest_1_.rest_5_), custom_call_target="tpu_custom_call" | custom-call | flops 1000 | bytes 1000 | tf_op jit(solution)/shard_map/block_product/pallas_call | solution.py:53
  49.1 0.0 copy-done.6
  49.1 6.5 %collective-permute-start.15 = (bf16[512,512]{1,0:T(8,128)(2,1)}, bf16[512,512]{1,0:T(8,128)(2,1)}, u32[]{:S(2)}, u32[]{:S(2)}) collective-permute-start(bf16[512,512]{1,0:T(8,128)(2,1)} %block_product.13.rest_4_), channel_id=1, source_target_pairs={{0,1},{1,2},{2,3},{3,0},{4,7},{5,4},{6,5},{7,6},{8,9},{9,10},{10,1... | collective-permute-start | bytes 1572872 | tf_op jit(solution)/shard_map/ppermute | solution.py:345
  55.6 0.0 collective-permute-done.3.rest_1_.rest_7_
  55.6 0.0 collective-permute-done.4.rest_2_.rest_8_
  55.6 0.0 collective-permute-done.5.rest_3_.rest_9_
  55.6 0.0 copy-start.2
  55.6 1.6 %low_sums.1.rest_1_.rest_0_ = bf16[16,512]{1,0:T(8,128)(2,1)S(1)} custom-call(s32[24]{0:T(128)S(1)} %get-tuple-element.21.rest_1_.start_ref, s32[24]{0:T(128)S(1)} %get-tuple-element.22.end_ref, bf16[512,2048]{1,0:T(8,128)(2,1)S(1)} %get-tuple-element.17.rows_ref, bf16[6,16,3072]{2,1,0:T(8,128)(2,1)S(1)} %get-tuple-element.23.rest_0_.rest_6_, ...), custom_call_target="tpu_custom_call" | custom-call | flops 1000 | bytes 1000 | tf_op jit(solution)/shard_map/low_sums/pallas_call | solution.py:241
  57.2 0.0 copy-done.2
  57.2 0.0 copy-start
  57.2 0.8 %copy-done = bf16[6,16,3072]{2,1,0:T(8,128)(2,1)} copy-done((bf16[6,16,3072]{2,1,0:T(8,128)(2,1)}, bf16[6,16,3072]{2,1,0:T(8,128)(2,1)S(1)}, u32[]{:S(2)}) %copy-start) | copy-done | bytes 589848
  58.0 3.0 %collective-permute-start.9 = (bf16[16,512]{1,0:T(8,128)(2,1)S(1)}, bf16[16,512]{1,0:T(8,128)(2,1)S(1)}, u32[]{:S(2)}, u32[]{:S(2)}) collective-permute-start(bf16[16,512]{1,0:T(8,128)(2,1)S(1)} %low_sums.1.rest_1_.rest_0_), channel_id=1, source_target_pairs={{0,1},{1,0},{2,3},{3,2},{4,5},{5,4},{6,7},{7,6},{8,9},{9,8},{10,11... | collective-permute-start | bytes 49160 | tf_op jit(solution)/shard_map/ppermute | solution.py:383
  61.0 1.4 %collective-permute-start.10 = (bf16[16,512]{1,0:T(8,128)(2,1)S(1)}, bf16[16,512]{1,0:T(8,128)(2,1)S(1)}, u32[]{:S(2)}, u32[]{:S(2)}) collective-permute-start(bf16[16,512]{1,0:T(8,128)(2,1)S(1)} %low_sums.1.rest_1_.rest_0_), channel_id=1, source_target_pairs={{0,2},{1,3},{2,0},{3,1},{4,6},{5,7},{6,4},{7,5},{8,10},{9,11},{10,... | collective-permute-start | bytes 49160 | tf_op jit(solution)/shard_map/ppermute | solution.py:383
  62.4 1.4 %collective-permute-start.11 = (bf16[16,512]{1,0:T(8,128)(2,1)S(1)}, bf16[16,512]{1,0:T(8,128)(2,1)S(1)}, u32[]{:S(2)}, u32[]{:S(2)}) collective-permute-start(bf16[16,512]{1,0:T(8,128)(2,1)S(1)} %low_sums.1.rest_1_.rest_0_), channel_id=1, source_target_pairs={{0,3},{1,2},{2,1},{3,0},{4,7},{5,6},{6,5},{7,4},{8,11},{9,10},{10,... | collective-permute-start | bytes 49160 | tf_op jit(solution)/shard_map/ppermute | solution.py:383
  63.9 0.0 collective-permute-done.12.rest_0_
  63.9 2.0 %block_product.14.rest_1_ = bf16[512,256]{1,0:T(8,128)(2,1)S(1)} custom-call(s32[1]{0:T(128)} %bitcast.9.first_ref, bf16[512,2048]{1,0:T(8,128)(2,1)S(1)} %get-tuple-element.17.rows_ref, bf16[2048,4096]{1,0:T(8,128)(2,1)} %weight_ref.17, bf16[512,512]{1,0:T(8,128)(2,1)} %collective-permute-done.12.rest_0_, bf16[16,512]{1,0:T(8,128)(2,1)S(1)} %low_sums.1.rest_1_.rest_0_), custom_call_target="tpu_custom_call" | custom-call | flops 1000 | bytes 1000 | tf_op jit(solution)/shard_map/block_product/pallas_call | solution.py:53
  65.9 2.4 %collective-permute-start.14 = (bf16[512,256]{1,0:T(8,128)(2,1)S(1)}, bf16[512,256]{1,0:T(8,128)(2,1)S(1)}, u32[]{:S(2)}, u32[]{:S(2)}) collective-permute-start(bf16[512,256]{1,0:T(8,128)(2,1)S(1)} %block_product.14.rest_1_), channel_id=1, source_target_pairs={{0,3},{1,0},{2,1},{3,2},{4,5},{5,6},{6,7},{7,4},{8,11},{9,8},{10,9... | collective-permute-start | bytes 786440 | tf_op jit(solution)/shard_map/ppermute | solution.py:345
  68.3 2.1 %block_product.15.rest_10_ = bf16[512,256]{1,0:T(8,128)(2,1)S(1)} custom-call(s32[1]{0:T(128)} %bitcast.8.first_ref, bf16[512,2048]{1,0:T(8,128)(2,1)S(1)} %get-tuple-element.17.rows_ref, bf16[2048,4096]{1,0:T(8,128)(2,1)} %weight_ref.17, bf16[512,512]{1,0:T(8,128)(2,1)} %collective-permute-done.12.rest_0_, bf16[512,256]{1,0:T(8,128)(2,1)S(1)} %block_product.14.rest_1_), custom_call_target="tpu_custom_call" | custom-call | flops 1000 | bytes 1000 | tf_op jit(solution)/shard_map/block_product/pallas_call | solution.py:53
  70.5 0.0 collective-permute-done.9.rest_1_
  70.5 1.2 %collective-permute-start.13 = (bf16[512,256]{1,0:T(8,128)(2,1)S(1)}, bf16[512,256]{1,0:T(8,128)(2,1)S(1)}, u32[]{:S(2)}, u32[]{:S(2)}) collective-permute-start(bf16[512,256]{1,0:T(8,128)(2,1)S(1)} %block_product.15.rest_10_), channel_id=1, source_target_pairs={{0,3},{1,0},{2,1},{3,2},{4,5},{5,6},{6,7},{7,4},{8,11},{9,8},{10,9... | collective-permute-start | bytes 786440 | tf_op jit(solution)/shard_map/ppermute | solution.py:345
  71.6 0.0 collective-permute-done.10.rest_2_
  71.6 0.0 collective-permute-done.11.rest_3_
  71.6 0.0 copy-done.1
  71.6 0.0 copy-done.3
  71.7 0.0 copy-done.5
  71.7 0.0 copy-done.7
  71.7 1.3 %adapter_term.1 = (f32[512,512]{1,0:T(8,128)S(1)}, f32[512,512]{1,0:T(8,128)S(1)}) custom-call(s32[24]{0:T(128)S(1)} %get-tuple-element.21.rest_1_.start_ref, s32[24]{0:T(128)S(1)} %get-tuple-element.22.end_ref, bf16[16,512]{1,0:T(8,128)(2,1)S(1)} %low_sums.1.rest_1_.rest_0_, bf16[16,512]{1,0:T(8,128)(2,1)S(1)} %collective-permute-done.9.rest_1_, ...), custom_call_target="tpu_custom_call" | custom-call | flops 1000 | bytes 1000 | tf_op jit(solution)/shard_map/adapter_term/pallas_call | solution.py:287
  73.0 0.0 collective-permute-done.15.rest_0_
  73.0 1.8 %finish.3.rest_1_ = bf16[512,1024]{1,0:T(8,128)(2,1)} custom-call(f32[512,512]{1,0:T(8,128)S(1)} %get-tuple-element.28.term_ref, bf16[512,512]{1,0:T(8,128)(2,1)} %collective-permute-done.15.rest_0_), custom_call_target="tpu_custom_call" | custom-call | flops 20000000000 | bytes 1000 | tf_op jit(solution)/shard_map/finish/pallas_call | solution.py:314
  74.8 1.6 %collective-permute-done.14.rest_0_ = bf16[512,256]{1,0:T(8,128)(2,1)S(1)} collective-permute-done((bf16[512,256]{1,0:T(8,128)(2,1)S(1)}, bf16[512,256]{1,0:T(8,128)(2,1)S(1)}, u32[]{:S(2)}, u32[]{:S(2)}) %collective-permute-start.14) | collective-permute-done | bytes 262176 | tf_op jit(solution)/shard_map/ppermute | solution.py:345
  76.4 0.8 finish.4.rest_1_
  77.2 2.0 %collective-permute-done.13.rest_0_ = bf16[512,256]{1,0:T(8,128)(2,1)S(1)} collective-permute-done((bf16[512,256]{1,0:T(8,128)(2,1)S(1)}, bf16[512,256]{1,0:T(8,128)(2,1)S(1)}, u32[]{:S(2)}, u32[]{:S(2)}) %collective-permute-start.13) | collective-permute-done | bytes 262176 | tf_op jit(solution)/shard_map/ppermute | solution.py:345
  79.2 0.8 finish.5
  (5 shorter events, 0.0 us)
Async XLA Ops:
  0.0 6.6 %copy-start.9 = (s32[1,12]{1,0:T(1,128)S(1)}, s32[1,12]{1,0:T(1,128)}, u32[]{:S(2)}) copy-start(s32[1,12]{1,0:T(1,128)} %rest_0_.1) | copy-start | bytes 148
  3.5 22.0 %collective-permute-start.6 = (bf16[512,512]{1,0:T(8,128)(2,1)}, bf16[512,512]{1,0:T(8,128)(2,1)}, u32[]{:S(2)}, u32[]{:S(2)}) collective-permute-start(bf16[512,512]{1,0:T(8,128)(2,1)} %get-tuple-element.18.rest_1_), channel_id=1, source_target_pairs={{0,1},{1,2},{2,3},{3,0},{4,7},{5,4},{6,5},{7,6},{8,9},{9,10},{10,1... | collective-permute-start | bytes 1572872 | tf_op jit(solution)/shard_map/ppermute | solution.py:345
  9.3 3.6 %copy-start.4 = (bf16[512,512]{1,0:T(8,128)(2,1)}, bf16[512,512]{1,0:T(8,128)(2,1)S(1)}, u32[]{:S(2)}) copy-start(bf16[512,512]{1,0:T(8,128)(2,1)S(1)} %get-tuple-element.20.rest_0_.rest_4_) | copy-start | bytes 1572868
  9.3 10.4 %copy-start.8 = (s32[512]{0:T(512)S(1)}, s32[512]{0:T(512)}, u32[]{:S(2)}) copy-start(s32[512]{0:T(512)} %table_ref.1) | copy-start | bytes 6148
  9.4 10.3 %copy-start.10 = (s32[1,12]{1,0:T(1,128)S(1)}, s32[1,12]{1,0:T(1,128)}, u32[]{:S(2)}) copy-start(s32[1,12]{1,0:T(1,128)} %lens_ref.1) | copy-start | bytes 148
  13.0 16.6 %collective-permute-start.8 = (bf16[512,512]{1,0:T(8,128)(2,1)}, bf16[512,512]{1,0:T(8,128)(2,1)}, u32[]{:S(2)}, u32[]{:S(2)}) collective-permute-start(bf16[512,512]{1,0:T(8,128)(2,1)} %block_product.9.rest_6_), channel_id=1, source_target_pairs={{0,3},{1,0},{2,1},{3,2},{4,5},{5,6},{6,7},{7,4},{8,11},{9,8},{10,9... | collective-permute-start | bytes 1572872 | tf_op jit(solution)/shard_map/ppermute | solution.py:345
  15.1 1.9 %collective-permute-start = (s32[1,12]{1,0:T(1,128)S(1)}, s32[1,12]{1,0:T(1,128)S(1)}, u32[]{:S(2)}, u32[]{:S(2)}) collective-permute-start(s32[1,12]{1,0:T(1,128)S(1)} %get-tuple-element.19.rest_0_), channel_id=1, source_target_pairs={{0,4},{4,0},{8,12},{12,8},{1,5},{5,1},{9,13},{13,9},{2,6},{6,2},{1... | collective-permute-start | bytes 152 | tf_op jit(solution)/shard_map/ppermute | solution.py:367
  15.1 3.5 %collective-permute-start.1 = (s32[1,12]{1,0:T(1,128)S(1)}, s32[1,12]{1,0:T(1,128)S(1)}, u32[]{:S(2)}, u32[]{:S(2)}) collective-permute-start(s32[1,12]{1,0:T(1,128)S(1)} %get-tuple-element.19.rest_0_), channel_id=1, source_target_pairs={{0,8},{4,12},{8,0},{12,4},{1,9},{5,13},{9,1},{13,5},{2,10},{6,14},... | collective-permute-start | bytes 152 | tf_op jit(solution)/shard_map/ppermute | solution.py:367
  16.7 3.0 %collective-permute-start.2 = (s32[1,12]{1,0:T(1,128)S(1)}, s32[1,12]{1,0:T(1,128)S(1)}, u32[]{:S(2)}, u32[]{:S(2)}) collective-permute-start(s32[1,12]{1,0:T(1,128)S(1)} %get-tuple-element.19.rest_0_), channel_id=1, source_target_pairs={{0,12},{4,8},{8,4},{12,0},{1,13},{5,9},{9,5},{13,1},{2,14},{6,10},... | collective-permute-start | bytes 152 | tf_op jit(solution)/shard_map/ppermute | solution.py:367
  23.6 32.1 %collective-permute-start.3 = (bf16[6,16,3072]{2,1,0:T(8,128)(2,1)S(1)}, bf16[6,16,3072]{2,1,0:T(8,128)(2,1)S(1)}, u32[]{:S(2)}, u32[]{:S(2)}) collective-permute-start(bf16[6,16,3072]{2,1,0:T(8,128)(2,1)S(1)} %get-tuple-element.24), channel_id=1, source_target_pairs={{0,4},{4,0},{8,12},{12,8},{1,5},{5,1},{9,13},{13,9},{2,6},{6,2},{1... | collective-permute-start | bytes 1769480 | tf_op jit(solution)/shard_map/ppermute | solution.py:373
  23.8 31.8 %collective-permute-start.4 = (bf16[6,16,3072]{2,1,0:T(8,128)(2,1)S(1)}, bf16[6,16,3072]{2,1,0:T(8,128)(2,1)S(1)}, u32[]{:S(2)}, u32[]{:S(2)}) collective-permute-start(bf16[6,16,3072]{2,1,0:T(8,128)(2,1)S(1)} %get-tuple-element.25), channel_id=1, source_target_pairs={{0,8},{4,12},{8,0},{12,4},{1,9},{5,13},{9,1},{13,5},{2,10},{6,14},... | collective-permute-start | bytes 1769480 | tf_op jit(solution)/shard_map/ppermute | solution.py:373
  24.1 31.5 %collective-permute-start.5 = (bf16[6,16,3072]{2,1,0:T(8,128)(2,1)S(1)}, bf16[6,16,3072]{2,1,0:T(8,128)(2,1)S(1)}, u32[]{:S(2)}, u32[]{:S(2)}) collective-permute-start(bf16[6,16,3072]{2,1,0:T(8,128)(2,1)S(1)} %get-tuple-element.26), channel_id=1, source_target_pairs={{0,12},{4,8},{8,4},{12,0},{1,13},{5,9},{9,5},{13,1},{2,14},{6,10},... | collective-permute-start | bytes 1769480 | tf_op jit(solution)/shard_map/ppermute | solution.py:373
  28.3 17.4 %collective-permute-start.7 = (bf16[512,512]{1,0:T(8,128)(2,1)S(1)}, bf16[512,512]{1,0:T(8,128)(2,1)S(1)}, u32[]{:S(2)}, u32[]{:S(2)}) collective-permute-start(bf16[512,512]{1,0:T(8,128)(2,1)S(1)} %block_product.10.rest_1_), channel_id=1, source_target_pairs={{0,1},{1,2},{2,3},{3,0},{4,7},{5,4},{6,5},{7,6},{8,9},{9,10},{10,1... | collective-permute-start | bytes 1572872 | tf_op jit(solution)/shard_map/ppermute | solution.py:345
  33.0 30.8 %collective-permute-start.12 = (bf16[512,512]{1,0:T(8,128)(2,1)}, bf16[512,512]{1,0:T(8,128)(2,1)}, u32[]{:S(2)}, u32[]{:S(2)}) collective-permute-start(bf16[512,512]{1,0:T(8,128)(2,1)} %block_product.11.rest_0_), channel_id=1, source_target_pairs={{0,3},{1,0},{2,1},{3,2},{4,5},{5,6},{6,7},{7,4},{8,11},{9,8},{10,9... | collective-permute-start | bytes 1572872 | tf_op jit(solution)/shard_map/ppermute | solution.py:345
  40.0 9.0 %copy-start.6 = (bf16[512,512]{1,0:T(8,128)(2,1)}, bf16[512,512]{1,0:T(8,128)(2,1)S(1)}, u32[]{:S(2)}) copy-start(bf16[512,512]{1,0:T(8,128)(2,1)S(1)} %block_product.12.rest_1_.rest_5_) | copy-start | bytes 1572868
  49.1 23.9 %collective-permute-start.15 = (bf16[512,512]{1,0:T(8,128)(2,1)}, bf16[512,512]{1,0:T(8,128)(2,1)}, u32[]{:S(2)}, u32[]{:S(2)}) collective-permute-start(bf16[512,512]{1,0:T(8,128)(2,1)} %block_product.13.rest_4_), channel_id=1, source_target_pairs={{0,1},{1,2},{2,3},{3,0},{4,7},{5,4},{6,5},{7,6},{8,9},{9,10},{10,1... | collective-permute-start | bytes 1572872 | tf_op jit(solution)/shard_map/ppermute | solution.py:345
  55.6 1.6 %copy-start.2 = (bf16[6,16,3072]{2,1,0:T(8,128)(2,1)}, bf16[6,16,3072]{2,1,0:T(8,128)(2,1)S(1)}, u32[]{:S(2)}) copy-start(bf16[6,16,3072]{2,1,0:T(8,128)(2,1)S(1)} %collective-permute-done.5.rest_3_.rest_9_) | copy-start | bytes 1769476
  57.2 0.8 %copy-start = (bf16[6,16,3072]{2,1,0:T(8,128)(2,1)}, bf16[6,16,3072]{2,1,0:T(8,128)(2,1)S(1)}, u32[]{:S(2)}) copy-start(bf16[6,16,3072]{2,1,0:T(8,128)(2,1)S(1)} %collective-permute-done.4.rest_2_.rest_8_) | copy-start | bytes 1769476
  58.0 12.4 %collective-permute-start.9 = (bf16[16,512]{1,0:T(8,128)(2,1)S(1)}, bf16[16,512]{1,0:T(8,128)(2,1)S(1)}, u32[]{:S(2)}, u32[]{:S(2)}) collective-permute-start(bf16[16,512]{1,0:T(8,128)(2,1)S(1)} %low_sums.1.rest_1_.rest_0_), channel_id=1, source_target_pairs={{0,1},{1,0},{2,3},{3,2},{4,5},{5,4},{6,7},{7,6},{8,9},{9,8},{10,11... | collective-permute-start | bytes 49160 | tf_op jit(solution)/shard_map/ppermute | solution.py:383
  61.0 10.6 %collective-permute-start.10 = (bf16[16,512]{1,0:T(8,128)(2,1)S(1)}, bf16[16,512]{1,0:T(8,128)(2,1)S(1)}, u32[]{:S(2)}, u32[]{:S(2)}) collective-permute-start(bf16[16,512]{1,0:T(8,128)(2,1)S(1)} %low_sums.1.rest_1_.rest_0_), channel_id=1, source_target_pairs={{0,2},{1,3},{2,0},{3,1},{4,6},{5,7},{6,4},{7,5},{8,10},{9,11},{10,... | collective-permute-start | bytes 49160 | tf_op jit(solution)/shard_map/ppermute | solution.py:383
  62.4 9.2 %collective-permute-start.11 = (bf16[16,512]{1,0:T(8,128)(2,1)S(1)}, bf16[16,512]{1,0:T(8,128)(2,1)S(1)}, u32[]{:S(2)}, u32[]{:S(2)}) collective-permute-start(bf16[16,512]{1,0:T(8,128)(2,1)S(1)} %low_sums.1.rest_1_.rest_0_), channel_id=1, source_target_pairs={{0,3},{1,2},{2,1},{3,0},{4,7},{5,6},{6,5},{7,4},{8,11},{9,10},{10,... | collective-permute-start | bytes 49160 | tf_op jit(solution)/shard_map/ppermute | solution.py:383
  65.9 10.5 %collective-permute-start.14 = (bf16[512,256]{1,0:T(8,128)(2,1)S(1)}, bf16[512,256]{1,0:T(8,128)(2,1)S(1)}, u32[]{:S(2)}, u32[]{:S(2)}) collective-permute-start(bf16[512,256]{1,0:T(8,128)(2,1)S(1)} %block_product.14.rest_1_), channel_id=1, source_target_pairs={{0,3},{1,0},{2,1},{3,2},{4,5},{5,6},{6,7},{7,4},{8,11},{9,8},{10,9... | collective-permute-start | bytes 786440 | tf_op jit(solution)/shard_map/ppermute | solution.py:345
  68.3 3.3 %copy-start.1 = (bf16[6,16,3072]{2,1,0:T(8,128)(2,1)S(1)}, bf16[6,16,3072]{2,1,0:T(8,128)(2,1)}, u32[]{:S(2)}) copy-start(bf16[6,16,3072]{2,1,0:T(8,128)(2,1)} %copy-done) | copy-start | bytes 1769476
  68.3 3.3 %copy-start.3 = (bf16[6,16,3072]{2,1,0:T(8,128)(2,1)S(1)}, bf16[6,16,3072]{2,1,0:T(8,128)(2,1)}, u32[]{:S(2)}) copy-start(bf16[6,16,3072]{2,1,0:T(8,128)(2,1)} %copy-done.2) | copy-start | bytes 1769476
  68.3 3.4 %copy-start.5 = (bf16[512,512]{1,0:T(8,128)(2,1)S(1)}, bf16[512,512]{1,0:T(8,128)(2,1)}, u32[]{:S(2)}) copy-start(bf16[512,512]{1,0:T(8,128)(2,1)} %copy-done.4) | copy-start | bytes 1572868
  68.3 3.4 %copy-start.7 = (bf16[512,512]{1,0:T(8,128)(2,1)S(1)}, bf16[512,512]{1,0:T(8,128)(2,1)}, u32[]{:S(2)}) copy-start(bf16[512,512]{1,0:T(8,128)(2,1)} %copy-done.6) | copy-start | bytes 1572868
  70.5 8.7 %collective-permute-start.13 = (bf16[512,256]{1,0:T(8,128)(2,1)S(1)}, bf16[512,256]{1,0:T(8,128)(2,1)S(1)}, u32[]{:S(2)}, u32[]{:S(2)}) collective-permute-start(bf16[512,256]{1,0:T(8,128)(2,1)S(1)} %block_product.15.rest_10_), channel_id=1, source_target_pairs={{0,3},{1,0},{2,1},{3,2},{4,5},{5,6},{6,7},{7,4},{8,11},{9,8},{10,9... | collective-permute-start | bytes 786440 | tf_op jit(solution)/shard_map/ppermute | solution.py:345

commit v25 on v21

--- a/solution.py
+++ b/solution.py
@@ -13,7 +13,7 @@
 F32 = jnp.float32
 BF16 = jnp.bfloat16
 SMALL = pl.CostEstimate(flops=1000, bytes_accessed=1000, transcendentals=0)
-LARGE = pl.CostEstimate(flops=2 * 10**10, bytes_accessed=1000, transcendentals=0)
+LARGE = pl.CostEstimate(flops=8 * 10**9, bytes_accessed=1000, transcendentals=0)
 
 
 def product_kernel(addends, with_ids, first_ref, rows_ref, weight_ref, *rest):

time: 79.5 us -> 79.5 us (level)
  transfers between devices with their start and end apart: 16 -> 16, of which waited for: 4 -> 4; matrix products, arithmetic and copies ran while one was open for 0% -> 0% of each run, Pallas kernels for 39% -> 40%
where the time goes in v25:
time: 79.5 us; the launch traced here: 79.1 us
  Pallas kernels  36.1 us (45%)
  starting transfers between devices  31.7 us (40%)
  waiting for transfers between devices  10.2 us (13%)
  local copies, waits for them, and re-layouts  0.85 us (1%)
    pallas_call x8, Pallas kernels, block_product(): pl.pallas_call(functools.partial(product_kernel, len(addends), with_ids),...  22.6 us
    ppermute x7, starting transfers between devices, move(): return lax.ppermute(value, ('req', 'tp'), pairs)  22.4 us
    ppermute x7, waiting for transfers between devices, move(): return lax.ppermute(value, ('req', 'tp'), pairs)  8.85 us
    ppermute x3, starting transfers between devices, local(): lows.append(lax.ppermute(low, 'tp', pairs))  5.5 us
    pallas_call x1, Pallas kernels, pick_adapters(): pl.pallas_call(functools.partial(pick_kernel, peers, len(after)), in_spec...  3.75 us
    pallas_call x1, Pallas kernels, first_product(): pl.pallas_call(functools.partial(first_kernel, chunk), in_specs=[pl.Block...  3.49 us
    pallas_call x3, Pallas kernels, finish(): pl.pallas_call(functools.partial(finish_kernel, 1), grid=(row_total // he...  3.38 us
    ppermute x3, starting transfers between devices, local(): lax.ppermute(packs[x], 'req', [(i, i ^ x) for i in range(req_total)])  1.93 us
  transfers between devices with their start and end apart: 16, of which 4 were waited for; matrix products, arithmetic and copies ran while one was open for 0% of the time, Pallas kernels for 40%

profile of v25, /device:TPU:0, one launch (start us, length us, event | category | flops | bytes accessed | tf_op | source)
XLA Modules:
  0.0 79.1 jit_solution(15620474848403871024)
XLA Ops:
  0.0 3.5 %first_product.1 = (bf16[512,512]{1,0:T(8,128)(2,1)}, bf16[512,2048]{1,0:T(8,128)(2,1)S(1)}) custom-call(s32[1]{0:T(128)} %bitcast.2.first_ref, bf16[512,2048]{1,0:T(8,128)(2,1)} %rows_ref.1, bf16[2048,4096]{1,0:T(8,128)(2,1)} %weight_ref.17), custom_call_target="tpu_custom_call" | custom-call | flops 1000 | bytes 1000 | tf_op jit(solution)/shard_map/first_product/pallas_call | solution.py:108
  3.5 3.1 %collective-permute-start.6 = (bf16[512,512]{1,0:T(8,128)(2,1)}, bf16[512,512]{1,0:T(8,128)(2,1)}, u32[]{:S(2)}, u32[]{:S(2)}) collective-permute-start(bf16[512,512]{1,0:T(8,128)(2,1)} %get-tuple-element.18.rest_1_), channel_id=1, source_target_pairs={{0,1},{1,2},{2,3},{3,0},{4,7},{5,4},{6,5},{7,6},{8,9},{9,10},{10,1... | collective-permute-start | bytes 1572872 | tf_op jit(solution)/shard_map/ppermute | solution.py:345
  6.6 0.0 copy-done.9
  6.6 3.4 %block_product.8 = (bf16[512,512]{1,0:T(8,128)(2,1)}, s32[1,12]{1,0:T(1,128)S(1)}) custom-call(s32[1]{0:T(128)} %bitcast.1.first_ref, bf16[512,2048]{1,0:T(8,128)(2,1)S(1)} %get-tuple-element.17.rows_ref, bf16[2048,4096]{1,0:T(8,128)(2,1)} %weight_ref.17, s32[1,12]{1,0:T(1,128)S(1)} %copy-done.9, bf16[512,512]{1,0:T(8,128)(2,1)} %get-tuple-element.18.rest_1_), custom_call_target="tpu_custom_call" | custom-call | flops 1000 | bytes 1000 | tf_op jit(solution)/shard_map/block_product/pallas_call | solution.py:53
  10.0 2.1 %collective-permute-start.8 = (bf16[512,512]{1,0:T(8,128)(2,1)}, bf16[512,512]{1,0:T(8,128)(2,1)}, u32[]{:S(2)}, u32[]{:S(2)}) collective-permute-start(bf16[512,512]{1,0:T(8,128)(2,1)} %get-tuple-element.20.rest_0_), channel_id=1, source_target_pairs={{0,3},{1,0},{2,1},{3,2},{4,5},{5,6},{6,7},{7,4},{8,11},{9,8},{10,9... | collective-permute-start | bytes 1572872 | tf_op jit(solution)/shard_map/ppermute | solution.py:345
  12.2 0.0 collective-permute-start
  12.2 1.7 %collective-permute-start.1 = (s32[1,12]{1,0:T(1,128)S(1)}, s32[1,12]{1,0:T(1,128)S(1)}, u32[]{:S(2)}, u32[]{:S(2)}) collective-permute-start(s32[1,12]{1,0:T(1,128)S(1)} %get-tuple-element.19.rest_0_), channel_id=1, source_target_pairs={{0,8},{4,12},{8,0},{12,4},{1,9},{5,13},{9,1},{13,5},{2,10},{6,14},... | collective-permute-start | bytes 152 | tf_op jit(solution)/shard_map/ppermute | solution.py:368
  13.8 0.2 collective-permute-start.2
  14.0 2.7 %block_product.9.rest_6_.rest_4_ = bf16[512,512]{1,0:T(8,128)(2,1)S(1)} custom-call(s32[1]{0:T(128)} %bitcast.3.first_ref, bf16[512,2048]{1,0:T(8,128)(2,1)S(1)} %get-tuple-element.17.rows_ref, bf16[2048,4096]{1,0:T(8,128)(2,1)} %weight_ref.17, bf16[512,512]{1,0:T(8,128)(2,1)} %get-tuple-element.20.rest_0_), custom_call_target="tpu_custom_call" | custom-call | flops 1000 | bytes 1000 | tf_op jit(solution)/shard_map/block_product/pallas_call | solution.py:53
  16.9 0.0 collective-permute-done.rest_1_
  16.9 0.0 collective-permute-done.1.rest_2_
  16.9 0.0 collective-permute-done.2.rest_3_
  16.9 0.0 copy-done.8
  16.9 0.0 copy-done.10
  16.9 3.7 %pick_adapters.1 = (bf16[6,16,3072]{2,1,0:T(8,128)(2,1)S(1)}, bf16[6,16,3072]{2,1,0:T(8,128)(2,1)S(1)}, bf16[6,16,3072]{2,1,0:T(8,128)(2,1)S(1)}, bf16[6,16,3072...) custom-call(s32[1]{0:T(128)} %bitcast.me_ref, s32[512]{0:T(512)S(1)} %copy-done.8, s32[1,12]{1,0:T(1,128)S(1)} %copy-done.10, ...), custom_call_target="tpu_custom_call" | custom-call | flops 1000 | bytes 1000 | tf_op jit(solution)/shard_map/pick_adapters/pallas_call | solution.py:199
  20.7 0.4 collective-permute-start.3
  21.1 1.2 %collective-permute-start.4 = (bf16[6,16,3072]{2,1,0:T(8,128)(2,1)S(1)}, bf16[6,16,3072]{2,1,0:T(8,128)(2,1)S(1)}, u32[]{:S(2)}, u32[]{:S(2)}) collective-permute-start(bf16[6,16,3072]{2,1,0:T(8,128)(2,1)S(1)} %get-tuple-element.25), channel_id=1, source_target_pairs={{0,8},{4,12},{8,0},{12,4},{1,9},{5,13},{9,1},{13,5},{2,10},{6,14},... | collective-permute-start | bytes 1769480 | tf_op jit(solution)/shard_map/ppermute | solution.py:373
  22.2 0.4 collective-permute-start.5
  22.6 0.0 collective-permute-done.6.rest_0_
  22.6 2.8 %block_product.10.rest_1_ = bf16[512,512]{1,0:T(8,128)(2,1)S(1)} custom-call(s32[1]{0:T(128)} %bitcast.5.first_ref, bf16[512,2048]{1,0:T(8,128)(2,1)S(1)} %get-tuple-element.17.rows_ref, bf16[2048,4096]{1,0:T(8,128)(2,1)} %weight_ref.17, bf16[512,512]{1,0:T(8,128)(2,1)} %collective-permute-done.6.rest_0_, s32[24]{0:T(128)S(1)} %get-tuple-element.21.rest_1_.start_ref), custom_call_target="tpu_custom_call" | custom-call | flops 1000 | bytes 1000 | tf_op jit(solution)/shard_map/block_product/pallas_call | solution.py:53
  25.4 6.5 %collective-permute-start.7 = (bf16[512,512]{1,0:T(8,128)(2,1)S(1)}, bf16[512,512]{1,0:T(8,128)(2,1)S(1)}, u32[]{:S(2)}, u32[]{:S(2)}) collective-permute-start(bf16[512,512]{1,0:T(8,128)(2,1)S(1)} %block_product.10.rest_1_), channel_id=1, source_target_pairs={{0,1},{1,2},{2,3},{3,0},{4,7},{5,4},{6,5},{7,6},{8,9},{9,10},{10,1... | collective-permute-start | bytes 1572872 | tf_op jit(solution)/shard_map/ppermute | solution.py:345
  31.9 0.0 collective-permute-done.8.rest_0_
  31.9 3.5 %block_product.11.rest_0_ = bf16[512,512]{1,0:T(8,128)(2,1)} custom-call(s32[1]{0:T(128)} %bitcast.7.first_ref, bf16[512,2048]{1,0:T(8,128)(2,1)S(1)} %get-tuple-element.17.rows_ref, bf16[2048,4096]{1,0:T(8,128)(2,1)} %weight_ref.17, bf16[512,512]{1,0:T(8,128)(2,1)} %collective-permute-done.8.rest_0_, bf16[512,512]{1,0:T(8,128)(2,1)S(1)} %block_product.10.rest_1_), custom_call_target="tpu_custom_call" | custom-call | flops 1000 | bytes 1000 | tf_op jit(solution)/shard_map/block_product/pallas_call | solution.py:53
  35.4 3.7 %collective-permute-start.12 = (bf16[512,512]{1,0:T(8,128)(2,1)}, bf16[512,512]{1,0:T(8,128)(2,1)}, u32[]{:S(2)}, u32[]{:S(2)}) collective-permute-start(bf16[512,512]{1,0:T(8,128)(2,1)} %block_product.11.rest_0_), channel_id=1, source_target_pairs={{0,3},{1,0},{2,1},{3,2},{4,5},{5,6},{6,7},{7,4},{8,11},{9,8},{10,9... | collective-permute-start | bytes 1572872 | tf_op jit(solution)/shard_map/ppermute | solution.py:345
  39.1 2.7 %block_product.12.rest_1_.rest_5_ = bf16[512,512]{1,0:T(8,128)(2,1)S(1)} custom-call(s32[1]{0:T(128)} %bitcast.6.first_ref, bf16[512,2048]{1,0:T(8,128)(2,1)S(1)} %get-tuple-element.17.rows_ref, bf16[2048,4096]{1,0:T(8,128)(2,1)} %weight_ref.17, bf16[512,512]{1,0:T(8,128)(2,1)} %block_product.11.rest_0_), custom_call_target="tpu_custom_call" | custom-call | flops 8000000000 | bytes 1000 | tf_op jit(solution)/shard_map/block_product/pallas_call | solution.py:53
  41.8 0.0 copy-start.6
  41.8 2.7 %collective-permute-done.7.rest_0_ = bf16[512,512]{1,0:T(8,128)(2,1)S(1)} collective-permute-done((bf16[512,512]{1,0:T(8,128)(2,1)S(1)}, bf16[512,512]{1,0:T(8,128)(2,1)S(1)}, u32[]{:S(2)}, u32[]{:S(2)}) %collective-permute-start.7) | collective-permute-done | bytes 524320 | tf_op jit(solution)/shard_map/ppermute | solution.py:345
  44.5 3.4 %block_product.13.rest_4_ = bf16[512,512]{1,0:T(8,128)(2,1)} custom-call(s32[1]{0:T(128)} %bitcast.4.first_ref, bf16[512,2048]{1,0:T(8,128)(2,1)S(1)} %get-tuple-element.17.rows_ref, bf16[2048,4096]{1,0:T(8,128)(2,1)} %weight_ref.17, bf16[512,512]{1,0:T(8,128)(2,1)S(1)} %collective-permute-done.7.rest_0_, bf16[512,512]{1,0:T(8,128)(2,1)S(1)} %block_product.12.rest_1_.rest_5_), custom_call_target="tpu_custom_call" | custom-call | flops 1000 | bytes 1000 | tf_op jit(solution)/shard_map/block_product/pallas_call | solution.py:53
  47.9 0.0 copy-done.6
  47.9 2.3 %collective-permute-start.15 = (bf16[512,512]{1,0:T(8,128)(2,1)}, bf16[512,512]{1,0:T(8,128)(2,1)}, u32[]{:S(2)}, u32[]{:S(2)}) collective-permute-start(bf16[512,512]{1,0:T(8,128)(2,1)} %block_product.13.rest_4_), channel_id=1, source_target_pairs={{0,1},{1,2},{2,3},{3,0},{4,7},{5,4},{6,5},{7,6},{8,9},{9,10},{10,1... | collective-permute-start | bytes 1572872 | tf_op jit(solution)/shard_map/ppermute | solution.py:345
  50.2 0.0 collective-permute-done.3.rest_1_.rest_7_
  50.2 0.0 collective-permute-done.4.rest_2_.rest_8_
  50.2 0.0 collective-permute-done.5.rest_3_.rest_9_
  50.2 0.0 copy-start.4
  50.2 1.6 %low_sums.1.rest_1_.rest_0_ = bf16[16,512]{1,0:T(8,128)(2,1)S(1)} custom-call(s32[24]{0:T(128)S(1)} %get-tuple-element.21.rest_1_.start_ref, s32[24]{0:T(128)S(1)} %get-tuple-element.22.end_ref, bf16[512,2048]{1,0:T(8,128)(2,1)S(1)} %get-tuple-element.17.rows_ref, bf16[6,16,3072]{2,1,0:T(8,128)(2,1)S(1)} %get-tuple-element.23.rest_0_.rest_6_, ...), custom_call_target="tpu_custom_call" | custom-call | flops 1000 | bytes 1000 | tf_op jit(solution)/shard_map/low_sums/pallas_call | solution.py:241
  51.8 0.0 copy-done.2
  51.8 0.0 copy-start
  51.8 0.8 %copy-done = bf16[6,16,3072]{2,1,0:T(8,128)(2,1)} copy-done((bf16[6,16,3072]{2,1,0:T(8,128)(2,1)}, bf16[6,16,3072]{2,1,0:T(8,128)(2,1)S(1)}, u32[]{:S(2)}) %copy-start) | copy-done | bytes 589848
  52.6 3.0 %collective-permute-start.9 = (bf16[16,512]{1,0:T(8,128)(2,1)S(1)}, bf16[16,512]{1,0:T(8,128)(2,1)S(1)}, u32[]{:S(2)}, u32[]{:S(2)}) collective-permute-start(bf16[16,512]{1,0:T(8,128)(2,1)S(1)} %low_sums.1.rest_1_.rest_0_), channel_id=1, source_target_pairs={{0,1},{1,0},{2,3},{3,2},{4,5},{5,4},{6,7},{7,6},{8,9},{9,8},{10,11... | collective-permute-start | bytes 49160 | tf_op jit(solution)/shard_map/ppermute | solution.py:383
  55.6 0.0 copy-done.4
  55.6 1.1 %collective-permute-start.10 = (bf16[16,512]{1,0:T(8,128)(2,1)S(1)}, bf16[16,512]{1,0:T(8,128)(2,1)S(1)}, u32[]{:S(2)}, u32[]{:S(2)}) collective-permute-start(bf16[16,512]{1,0:T(8,128)(2,1)S(1)} %low_sums.1.rest_1_.rest_0_), channel_id=1, source_target_pairs={{0,2},{1,3},{2,0},{3,1},{4,6},{5,7},{6,4},{7,5},{8,10},{9,11},{10,... | collective-permute-start | bytes 49160 | tf_op jit(solution)/shard_map/ppermute | solution.py:383
  56.7 1.4 %collective-permute-start.11 = (bf16[16,512]{1,0:T(8,128)(2,1)S(1)}, bf16[16,512]{1,0:T(8,128)(2,1)S(1)}, u32[]{:S(2)}, u32[]{:S(2)}) collective-permute-start(bf16[16,512]{1,0:T(8,128)(2,1)S(1)} %low_sums.1.rest_1_.rest_0_), channel_id=1, source_target_pairs={{0,3},{1,2},{2,1},{3,0},{4,7},{5,6},{6,5},{7,4},{8,11},{9,10},{10,... | collective-permute-start | bytes 49160 | tf_op jit(solution)/shard_map/ppermute | solution.py:383
  58.1 3.5 %collective-permute-done.12.rest_0_ = bf16[512,512]{1,0:T(8,128)(2,1)} collective-permute-done((bf16[512,512]{1,0:T(8,128)(2,1)}, bf16[512,512]{1,0:T(8,128)(2,1)}, u32[]{:S(2)}, u32[]{:S(2)}) %collective-permute-start.12) | collective-permute-done | bytes 524320 | tf_op jit(solution)/shard_map/ppermute | solution.py:345
  61.6 2.0 %block_product.14.rest_1_ = bf16[512,256]{1,0:T(8,128)(2,1)S(1)} custom-call(s32[1]{0:T(128)} %bitcast.9.first_ref, bf16[512,2048]{1,0:T(8,128)(2,1)S(1)} %get-tuple-element.17.rows_ref, bf16[2048,4096]{1,0:T(8,128)(2,1)} %weight_ref.17, bf16[512,512]{1,0:T(8,128)(2,1)} %collective-permute-done.12.rest_0_, bf16[16,512]{1,0:T(8,128)(2,1)S(1)} %low_sums.1.rest_1_.rest_0_), custom_call_target="tpu_custom_call" | custom-call | flops 1000 | bytes 1000 | tf_op jit(solution)/shard_map/block_product/pallas_call | solution.py:53
  63.6 0.1 collective-permute-start.14
  63.7 0.0 copy-start.1
  63.7 0.0 copy-start.3
  63.7 0.0 copy-start.5
  63.7 0.0 copy-start.7
  63.7 2.1 %block_product.15.rest_10_ = bf16[512,256]{1,0:T(8,128)(2,1)S(1)} custom-call(s32[1]{0:T(128)} %bitcast.8.first_ref, bf16[512,2048]{1,0:T(8,128)(2,1)S(1)} %get-tuple-element.17.rows_ref, bf16[2048,4096]{1,0:T(8,128)(2,1)} %weight_ref.17, bf16[512,512]{1,0:T(8,128)(2,1)} %collective-permute-done.12.rest_0_, bf16[512,256]{1,0:T(8,128)(2,1)S(1)} %block_product.14.rest_1_), custom_call_target="tpu_custom_call" | custom-call | flops 1000 | bytes 1000 | tf_op jit(solution)/shard_map/block_product/pallas_call | solution.py:53
  65.9 1.3 %collective-permute-done.9.rest_1_ = bf16[16,512]{1,0:T(8,128)(2,1)S(1)} collective-permute-done((bf16[16,512]{1,0:T(8,128)(2,1)S(1)}, bf16[16,512]{1,0:T(8,128)(2,1)S(1)}, u32[]{:S(2)}, u32[]{:S(2)}) %collective-permute-start.9) | collective-permute-done | bytes 16416 | tf_op jit(solution)/shard_map/ppermute | solution.py:383
  67.2 4.6 %collective-permute-start.13 = (bf16[512,256]{1,0:T(8,128)(2,1)S(1)}, bf16[512,256]{1,0:T(8,128)(2,1)S(1)}, u32[]{:S(2)}, u32[]{:S(2)}) collective-permute-start(bf16[512,256]{1,0:T(8,128)(2,1)S(1)} %block_product.15.rest_10_), channel_id=1, source_target_pairs={{0,3},{1,0},{2,1},{3,2},{4,5},{5,6},{6,7},{7,4},{8,11},{9,8},{10,9... | collective-permute-start | bytes 786440 | tf_op jit(solution)/shard_map/ppermute | solution.py:345
  71.8 0.0 collective-permute-done.10.rest_2_
  71.8 0.0 collective-permute-done.11.rest_3_
  71.8 0.0 copy-done.1
  71.8 0.0 copy-done.3
  71.8 0.0 copy-done.5
  71.8 1.3 %adapter_term.1 = (f32[512,512]{1,0:T(8,128)S(1)}, f32[512,512]{1,0:T(8,128)S(1)}) custom-call(s32[24]{0:T(128)S(1)} %get-tuple-element.21.rest_1_.start_ref, s32[24]{0:T(128)S(1)} %get-tuple-element.22.end_ref, bf16[16,512]{1,0:T(8,128)(2,1)S(1)} %low_sums.1.rest_1_.rest_0_, bf16[16,512]{1,0:T(8,128)(2,1)S(1)} %collective-permute-done.9.rest_1_, ...), custom_call_target="tpu_custom_call" | custom-call | flops 1000 | bytes 1000 | tf_op jit(solution)/shard_map/adapter_term/pallas_call | solution.py:287
  73.1 0.0 collective-permute-done.15.rest_0_
  73.1 1.8 %finish.3.rest_1_ = bf16[512,1024]{1,0:T(8,128)(2,1)} custom-call(f32[512,512]{1,0:T(8,128)S(1)} %get-tuple-element.28.term_ref, bf16[512,512]{1,0:T(8,128)(2,1)} %collective-permute-done.15.rest_0_), custom_call_target="tpu_custom_call" | custom-call | flops 8000000000 | bytes 1000 | tf_op jit(solution)/shard_map/finish/pallas_call | solution.py:314
  74.9 0.0 collective-permute-done.14.rest_0_
  74.9 0.8 finish.4.rest_1_
  75.7 2.6 %collective-permute-done.13.rest_0_ = bf16[512,256]{1,0:T(8,128)(2,1)S(1)} collective-permute-done((bf16[512,256]{1,0:T(8,128)(2,1)S(1)}, bf16[512,256]{1,0:T(8,128)(2,1)S(1)}, u32[]{:S(2)}, u32[]{:S(2)}) %collective-permute-start.13) | collective-permute-done | bytes 262176 | tf_op jit(solution)/shard_map/ppermute | solution.py:345
  78.3 0.8 %finish.5 = bf16[512,1024]{1,0:T(8,128)(2,1)} custom-call(f32[512,512]{1,0:T(8,128)S(1)} %get-tuple-element.27.term_ref, bf16[512,256]{1,0:T(8,128)(2,1)S(1)} %collective-permute-done.13.rest_0_, bf16[512,1024]{1,0:T(8,128)(2,1)} %finish.4.rest_1_), custom_call_target="tpu_custom_call", output_to_operand_aliasing={{}: (2, {})} | custom-call | flops 1000 | bytes 1000 | tf_op jit(solution)/shard_map/finish/pallas_call | solution.py:314
  (5 shorter events, 0.0 us)
Async XLA Ops:
  0.0 6.6 %copy-start.9 = (s32[1,12]{1,0:T(1,128)S(1)}, s32[1,12]{1,0:T(1,128)}, u32[]{:S(2)}) copy-start(s32[1,12]{1,0:T(1,128)} %rest_0_.1) | copy-start | bytes 148
  3.5 19.1 %collective-permute-start.6 = (bf16[512,512]{1,0:T(8,128)(2,1)}, bf16[512,512]{1,0:T(8,128)(2,1)}, u32[]{:S(2)}, u32[]{:S(2)}) collective-permute-start(bf16[512,512]{1,0:T(8,128)(2,1)} %get-tuple-element.18.rest_1_), channel_id=1, source_target_pairs={{0,1},{1,2},{2,3},{3,0},{4,7},{5,4},{6,5},{7,6},{8,9},{9,10},{10,1... | collective-permute-start | bytes 1572872 | tf_op jit(solution)/shard_map/ppermute | solution.py:345
  10.0 21.9 %collective-permute-start.8 = (bf16[512,512]{1,0:T(8,128)(2,1)}, bf16[512,512]{1,0:T(8,128)(2,1)}, u32[]{:S(2)}, u32[]{:S(2)}) collective-permute-start(bf16[512,512]{1,0:T(8,128)(2,1)} %get-tuple-element.20.rest_0_), channel_id=1, source_target_pairs={{0,3},{1,0},{2,1},{3,2},{4,5},{5,6},{6,7},{7,4},{8,11},{9,8},{10,9... | collective-permute-start | bytes 1572872 | tf_op jit(solution)/shard_map/ppermute | solution.py:345
  12.2 4.7 %collective-permute-start = (s32[1,12]{1,0:T(1,128)S(1)}, s32[1,12]{1,0:T(1,128)S(1)}, u32[]{:S(2)}, u32[]{:S(2)}) collective-permute-start(s32[1,12]{1,0:T(1,128)S(1)} %get-tuple-element.19.rest_0_), channel_id=1, source_target_pairs={{0,4},{4,0},{8,12},{12,8},{1,5},{5,1},{9,13},{13,9},{2,6},{6,2},{1... | collective-permute-start | bytes 152 | tf_op jit(solution)/shard_map/ppermute | solution.py:368
  12.2 4.7 %collective-permute-start.1 = (s32[1,12]{1,0:T(1,128)S(1)}, s32[1,12]{1,0:T(1,128)S(1)}, u32[]{:S(2)}, u32[]{:S(2)}) collective-permute-start(s32[1,12]{1,0:T(1,128)S(1)} %get-tuple-element.19.rest_0_), channel_id=1, source_target_pairs={{0,8},{4,12},{8,0},{12,4},{1,9},{5,13},{9,1},{13,5},{2,10},{6,14},... | collective-permute-start | bytes 152 | tf_op jit(solution)/shard_map/ppermute | solution.py:368
  13.8 3.0 %collective-permute-start.2 = (s32[1,12]{1,0:T(1,128)S(1)}, s32[1,12]{1,0:T(1,128)S(1)}, u32[]{:S(2)}, u32[]{:S(2)}) collective-permute-start(s32[1,12]{1,0:T(1,128)S(1)} %get-tuple-element.19.rest_0_), channel_id=1, source_target_pairs={{0,12},{4,8},{8,4},{12,0},{1,13},{5,9},{9,5},{13,1},{2,14},{6,10},... | collective-permute-start | bytes 152 | tf_op jit(solution)/shard_map/ppermute | solution.py:368
  14.0 2.9 %copy-start.8 = (s32[512]{0:T(512)S(1)}, s32[512]{0:T(512)}, u32[]{:S(2)}) copy-start(s32[512]{0:T(512)} %table_ref.1) | copy-start | bytes 6148
  14.0 2.9 %copy-start.10 = (s32[1,12]{1,0:T(1,128)S(1)}, s32[1,12]{1,0:T(1,128)}, u32[]{:S(2)}) copy-start(s32[1,12]{1,0:T(1,128)} %lens_ref.1) | copy-start | bytes 148
  20.7 29.5 %collective-permute-start.3 = (bf16[6,16,3072]{2,1,0:T(8,128)(2,1)S(1)}, bf16[6,16,3072]{2,1,0:T(8,128)(2,1)S(1)}, u32[]{:S(2)}, u32[]{:S(2)}) collective-permute-start(bf16[6,16,3072]{2,1,0:T(8,128)(2,1)S(1)} %get-tuple-element.24), channel_id=1, source_target_pairs={{0,4},{4,0},{8,12},{12,8},{1,5},{5,1},{9,13},{13,9},{2,6},{6,2},{1... | collective-permute-start | bytes 1769480 | tf_op jit(solution)/shard_map/ppermute | solution.py:373
  21.1 29.1 %collective-permute-start.4 = (bf16[6,16,3072]{2,1,0:T(8,128)(2,1)S(1)}, bf16[6,16,3072]{2,1,0:T(8,128)(2,1)S(1)}, u32[]{:S(2)}, u32[]{:S(2)}) collective-permute-start(bf16[6,16,3072]{2,1,0:T(8,128)(2,1)S(1)} %get-tuple-element.25), channel_id=1, source_target_pairs={{0,8},{4,12},{8,0},{12,4},{1,9},{5,13},{9,1},{13,5},{2,10},{6,14},... | collective-permute-start | bytes 1769480 | tf_op jit(solution)/shard_map/ppermute | solution.py:373
  22.2 28.0 %collective-permute-start.5 = (bf16[6,16,3072]{2,1,0:T(8,128)(2,1)S(1)}, bf16[6,16,3072]{2,1,0:T(8,128)(2,1)S(1)}, u32[]{:S(2)}, u32[]{:S(2)}) collective-permute-start(bf16[6,16,3072]{2,1,0:T(8,128)(2,1)S(1)} %get-tuple-element.26), channel_id=1, source_target_pairs={{0,12},{4,8},{8,4},{12,0},{1,13},{5,9},{9,5},{13,1},{2,14},{6,10},... | collective-permute-start | bytes 1769480 | tf_op jit(solution)/shard_map/ppermute | solution.py:373
  25.4 19.1 %collective-permute-start.7 = (bf16[512,512]{1,0:T(8,128)(2,1)S(1)}, bf16[512,512]{1,0:T(8,128)(2,1)S(1)}, u32[]{:S(2)}, u32[]{:S(2)}) collective-permute-start(bf16[512,512]{1,0:T(8,128)(2,1)S(1)} %block_product.10.rest_1_), channel_id=1, source_target_pairs={{0,1},{1,2},{2,3},{3,0},{4,7},{5,4},{6,5},{7,6},{8,9},{9,10},{10,1... | collective-permute-start | bytes 1572872 | tf_op jit(solution)/shard_map/ppermute | solution.py:345
  35.4 26.2 %collective-permute-start.12 = (bf16[512,512]{1,0:T(8,128)(2,1)}, bf16[512,512]{1,0:T(8,128)(2,1)}, u32[]{:S(2)}, u32[]{:S(2)}) collective-permute-start(bf16[512,512]{1,0:T(8,128)(2,1)} %block_product.11.rest_0_), channel_id=1, source_target_pairs={{0,3},{1,0},{2,1},{3,2},{4,5},{5,6},{6,7},{7,4},{8,11},{9,8},{10,9... | collective-permute-start | bytes 1572872 | tf_op jit(solution)/shard_map/ppermute | solution.py:345
  41.8 6.1 %copy-start.6 = (bf16[512,512]{1,0:T(8,128)(2,1)}, bf16[512,512]{1,0:T(8,128)(2,1)S(1)}, u32[]{:S(2)}) copy-start(bf16[512,512]{1,0:T(8,128)(2,1)S(1)} %block_product.12.rest_1_.rest_5_) | copy-start | bytes 1572868
  47.9 25.2 %collective-permute-start.15 = (bf16[512,512]{1,0:T(8,128)(2,1)}, bf16[512,512]{1,0:T(8,128)(2,1)}, u32[]{:S(2)}, u32[]{:S(2)}) collective-permute-start(bf16[512,512]{1,0:T(8,128)(2,1)} %block_product.13.rest_4_), channel_id=1, source_target_pairs={{0,1},{1,2},{2,3},{3,0},{4,7},{5,4},{6,5},{7,6},{8,9},{9,10},{10,1... | collective-permute-start | bytes 1572872 | tf_op jit(solution)/shard_map/ppermute | solution.py:345
  50.2 1.6 %copy-start.2 = (bf16[6,16,3072]{2,1,0:T(8,128)(2,1)}, bf16[6,16,3072]{2,1,0:T(8,128)(2,1)S(1)}, u32[]{:S(2)}) copy-start(bf16[6,16,3072]{2,1,0:T(8,128)(2,1)S(1)} %collective-permute-done.4.rest_2_.rest_8_) | copy-start | bytes 1769476
  50.2 5.4 %copy-start.4 = (bf16[6,16,3072]{2,1,0:T(8,128)(2,1)}, bf16[6,16,3072]{2,1,0:T(8,128)(2,1)S(1)}, u32[]{:S(2)}) copy-start(bf16[6,16,3072]{2,1,0:T(8,128)(2,1)S(1)} %collective-permute-done.5.rest_3_.rest_9_) | copy-start | bytes 1769476
  51.8 0.8 %copy-start = (bf16[6,16,3072]{2,1,0:T(8,128)(2,1)}, bf16[6,16,3072]{2,1,0:T(8,128)(2,1)S(1)}, u32[]{:S(2)}) copy-start(bf16[6,16,3072]{2,1,0:T(8,128)(2,1)S(1)} %collective-permute-done.3.rest_1_.rest_7_) | copy-start | bytes 1769476
  52.6 14.6 %collective-permute-start.9 = (bf16[16,512]{1,0:T(8,128)(2,1)S(1)}, bf16[16,512]{1,0:T(8,128)(2,1)S(1)}, u32[]{:S(2)}, u32[]{:S(2)}) collective-permute-start(bf16[16,512]{1,0:T(8,128)(2,1)S(1)} %low_sums.1.rest_1_.rest_0_), channel_id=1, source_target_pairs={{0,1},{1,0},{2,3},{3,2},{4,5},{5,4},{6,7},{7,6},{8,9},{9,8},{10,11... | collective-permute-start | bytes 49160 | tf_op jit(solution)/shard_map/ppermute | solution.py:383
  55.6 16.2 %collective-permute-start.10 = (bf16[16,512]{1,0:T(8,128)(2,1)S(1)}, bf16[16,512]{1,0:T(8,128)(2,1)S(1)}, u32[]{:S(2)}, u32[]{:S(2)}) collective-permute-start(bf16[16,512]{1,0:T(8,128)(2,1)S(1)} %low_sums.1.rest_1_.rest_0_), channel_id=1, source_target_pairs={{0,2},{1,3},{2,0},{3,1},{4,6},{5,7},{6,4},{7,5},{8,10},{9,11},{10,... | collective-permute-start | bytes 49160 | tf_op jit(solution)/shard_map/ppermute | solution.py:383
  56.7 15.1 %collective-permute-start.11 = (bf16[16,512]{1,0:T(8,128)(2,1)S(1)}, bf16[16,512]{1,0:T(8,128)(2,1)S(1)}, u32[]{:S(2)}, u32[]{:S(2)}) collective-permute-start(bf16[16,512]{1,0:T(8,128)(2,1)S(1)} %low_sums.1.rest_1_.rest_0_), channel_id=1, source_target_pairs={{0,3},{1,2},{2,1},{3,0},{4,7},{5,6},{6,5},{7,4},{8,11},{9,10},{10,... | collective-permute-start | bytes 49160 | tf_op jit(solution)/shard_map/ppermute | solution.py:383
  63.6 11.3 %collective-permute-start.14 = (bf16[512,256]{1,0:T(8,128)(2,1)S(1)}, bf16[512,256]{1,0:T(8,128)(2,1)S(1)}, u32[]{:S(2)}, u32[]{:S(2)}) collective-permute-start(bf16[512,256]{1,0:T(8,128)(2,1)S(1)} %block_product.14.rest_1_), channel_id=1, source_target_pairs={{0,3},{1,0},{2,1},{3,2},{4,5},{5,6},{6,7},{7,4},{8,11},{9,8},{10,9... | collective-permute-start | bytes 786440 | tf_op jit(solution)/shard_map/ppermute | solution.py:345
  63.7 8.1 %copy-start.1 = (bf16[6,16,3072]{2,1,0:T(8,128)(2,1)S(1)}, bf16[6,16,3072]{2,1,0:T(8,128)(2,1)}, u32[]{:S(2)}) copy-start(bf16[6,16,3072]{2,1,0:T(8,128)(2,1)} %copy-done) | copy-start | bytes 1769476
  63.7 8.1 %copy-start.3 = (bf16[6,16,3072]{2,1,0:T(8,128)(2,1)S(1)}, bf16[6,16,3072]{2,1,0:T(8,128)(2,1)}, u32[]{:S(2)}) copy-start(bf16[6,16,3072]{2,1,0:T(8,128)(2,1)} %copy-done.2) | copy-start | bytes 1769476
  63.7 8.1 %copy-start.5 = (bf16[6,16,3072]{2,1,0:T(8,128)(2,1)S(1)}, bf16[6,16,3072]{2,1,0:T(8,128)(2,1)}, u32[]{:S(2)}) copy-start(bf16[6,16,3072]{2,1,0:T(8,128)(2,1)} %copy-done.4) | copy-start | bytes 1769476
  63.7 8.1 %copy-start.7 = (bf16[512,512]{1,0:T(8,128)(2,1)S(1)}, bf16[512,512]{1,0:T(8,128)(2,1)}, u32[]{:S(2)}) copy-start(bf16[512,512]{1,0:T(8,128)(2,1)} %copy-done.6) | copy-start | bytes 1572868
  67.2 11.2 %collective-permute-start.13 = (bf16[512,256]{1,0:T(8,128)(2,1)S(1)}, bf16[512,256]{1,0:T(8,128)(2,1)S(1)}, u32[]{:S(2)}, u32[]{:S(2)}) collective-permute-start(bf16[512,256]{1,0:T(8,128)(2,1)S(1)} %block_product.15.rest_10_), channel_id=1, source_target_pairs={{0,3},{1,0},{2,1},{3,2},{4,5},{5,6},{6,7},{7,4},{8,11},{9,8},{10,9... | collective-permute-start | bytes 786440 | tf_op jit(solution)/shard_map/ppermute | solution.py:345

commit v26 on v25

--- a/solution.py
+++ b/solution.py
@@ -46,7 +46,7 @@
     smem = pl.BlockSpec(memory_space=pltpu.SMEM)
     hbm = pl.BlockSpec(memory_space=pl.ANY)
     columns = pl.BlockSpec((row_total, tile), lambda j, t: (0, j))
-    out_specs, out_shape = [columns], [jax.ShapeDtypeStruct((row_total, width), BF16)]
+    out_specs, out_shape = [columns], [pltpu.VMEM((row_total, width), BF16)]
     if with_ids:
         out_specs.append(hbm)
         out_shape.append(jax.ShapeDtypeStruct(ids.shape, ids.dtype))
@@ -110,8 +110,8 @@
         in_specs=[pl.BlockSpec(memory_space=pltpu.SMEM), hbm, hbm],
         out_specs=[pl.BlockSpec(memory_space=pltpu.VMEM)] * 2,
         out_shape=[
-            jax.ShapeDtypeStruct((row_total, width), BF16),
-            jax.ShapeDtypeStruct((row_total, depth), BF16),
+            pltpu.VMEM((row_total, width), BF16),
+            pltpu.VMEM((row_total, depth), BF16),
         ],
         scratch_shapes=[
             pltpu.VMEM((chunks, chunk, width), BF16),

time: 79.5 us -> 79.5 us (level)
  no operation moved by 1% of the time
where the time goes in v26:
time: 79.5 us; the launch traced here: 79.1 us
  Pallas kernels  35.8 us (45%)
  starting transfers between devices  31.9 us (40%)
  waiting for transfers between devices  10.2 us (13%)
  local copies, waits for them, and re-layouts  0.85 us (1%)
    pallas_call x8, Pallas kernels, block_product(): pl.pallas_call(functools.partial(product_kernel, len(addends), with_ids),...  22.6 us
    ppermute x7, starting transfers between devices, move(): return lax.ppermute(value, ('req', 'tp'), pairs)  22.3 us
    ppermute x7, waiting for transfers between devices, move(): return lax.ppermute(value, ('req', 'tp'), pairs)  8.85 us
    ppermute x3, starting transfers between devices, local(): lows.append(lax.ppermute(low, 'tp', pairs))  5.5 us
    pallas_call x1, Pallas kernels, first_product(): pl.pallas_call(functools.partial(first_kernel, chunk), in_specs=[pl.Block...  3.49 us
    pallas_call x1, Pallas kernels, pick_adapters(): pl.pallas_call(functools.partial(pick_kernel, peers, len(after)), in_spec...  3.49 us
    pallas_call x3, Pallas kernels, finish(): pl.pallas_call(functools.partial(finish_kernel, 1), grid=(row_total // he...  3.38 us
    ppermute x3, starting transfers between devices, local(): lax.ppermute(packs[x], 'req', [(i, i ^ x) for i in range(req_total)])  2.31 us
  transfers between devices with their start and end apart: 16, of which 4 were waited for; matrix products, arithmetic and copies ran while one was open for 0% of the time, Pallas kernels for 40%

profile of v26, /device:TPU:0, one launch (start us, length us, event | category | flops | bytes accessed | tf_op | source)
XLA Modules:
  0.0 79.1 jit_solution(15620474848403871024)
XLA Ops:
  0.0 3.5 %first_product.1 = (bf16[512,512]{1,0:T(8,128)(2,1)}, bf16[512,2048]{1,0:T(8,128)(2,1)S(1)}) custom-call(s32[1]{0:T(128)} %bitcast.2.first_ref, bf16[512,2048]{1,0:T(8,128)(2,1)} %rows_ref.1, bf16[2048,4096]{1,0:T(8,128)(2,1)} %weight_ref.17), custom_call_target="tpu_custom_call" | custom-call | flops 1000 | bytes 1000 | tf_op jit(solution)/shard_map/first_product/pallas_call | solution.py:108
  3.5 3.1 %collective-permute-start.6 = (bf16[512,512]{1,0:T(8,128)(2,1)}, bf16[512,512]{1,0:T(8,128)(2,1)}, u32[]{:S(2)}, u32[]{:S(2)}) collective-permute-start(bf16[512,512]{1,0:T(8,128)(2,1)} %get-tuple-element.18.rest_1_), channel_id=1, source_target_pairs={{0,1},{1,2},{2,3},{3,0},{4,7},{5,4},{6,5},{7,6},{8,9},{9,10},{10,1... | collective-permute-start | bytes 1572872 | tf_op jit(solution)/shard_map/ppermute | solution.py:345
  6.6 0.0 copy-done.9
  6.6 3.4 %block_product.8 = (bf16[512,512]{1,0:T(8,128)(2,1)}, s32[1,12]{1,0:T(1,128)S(1)}) custom-call(s32[1]{0:T(128)} %bitcast.1.first_ref, bf16[512,2048]{1,0:T(8,128)(2,1)S(1)} %get-tuple-element.17.rows_ref, bf16[2048,4096]{1,0:T(8,128)(2,1)} %weight_ref.17, s32[1,12]{1,0:T(1,128)S(1)} %copy-done.9, bf16[512,512]{1,0:T(8,128)(2,1)} %get-tuple-element.18.rest_1_), custom_call_target="tpu_custom_call" | custom-call | flops 1000 | bytes 1000 | tf_op jit(solution)/shard_map/block_product/pallas_call | solution.py:53
  10.0 2.1 %collective-permute-start.8 = (bf16[512,512]{1,0:T(8,128)(2,1)}, bf16[512,512]{1,0:T(8,128)(2,1)}, u32[]{:S(2)}, u32[]{:S(2)}) collective-permute-start(bf16[512,512]{1,0:T(8,128)(2,1)} %get-tuple-element.20.rest_0_), channel_id=1, source_target_pairs={{0,3},{1,0},{2,1},{3,2},{4,5},{5,6},{6,7},{7,4},{8,11},{9,8},{10,9... | collective-permute-start | bytes 1572872 | tf_op jit(solution)/shard_map/ppermute | solution.py:345
  12.2 0.0 collective-permute-start
  12.2 1.7 %collective-permute-start.1 = (s32[1,12]{1,0:T(1,128)S(1)}, s32[1,12]{1,0:T(1,128)S(1)}, u32[]{:S(2)}, u32[]{:S(2)}) collective-permute-start(s32[1,12]{1,0:T(1,128)S(1)} %get-tuple-element.19.rest_0_), channel_id=1, source_target_pairs={{0,8},{4,12},{8,0},{12,4},{1,9},{5,13},{9,1},{13,5},{2,10},{6,14},... | collective-permute-start | bytes 152 | tf_op jit(solution)/shard_map/ppermute | solution.py:368
  13.8 0.2 collective-permute-start.2
  14.0 2.7 %block_product.9.rest_6_.rest_4_ = bf16[512,512]{1,0:T(8,128)(2,1)S(1)} custom-call(s32[1]{0:T(128)} %bitcast.3.first_ref, bf16[512,2048]{1,0:T(8,128)(2,1)S(1)} %get-tuple-element.17.rows_ref, bf16[2048,4096]{1,0:T(8,128)(2,1)} %weight_ref.17, bf16[512,512]{1,0:T(8,128)(2,1)} %get-tuple-element.20.rest_0_), custom_call_target="tpu_custom_call" | custom-call | flops 1000 | bytes 1000 | tf_op jit(solution)/shard_map/block_product/pallas_call | solution.py:53
  16.9 0.0 collective-permute-done.rest_1_
  16.9 0.0 collective-permute-done.1.rest_2_
  16.9 0.0 collective-permute-done.2.rest_3_
  16.9 0.0 copy-done.8
  16.9 0.0 copy-done.10
  16.9 3.5 %pick_adapters.1 = (bf16[6,16,3072]{2,1,0:T(8,128)(2,1)S(1)}, bf16[6,16,3072]{2,1,0:T(8,128)(2,1)S(1)}, bf16[6,16,3072]{2,1,0:T(8,128)(2,1)S(1)}, bf16[6,16,3072...) custom-call(s32[1]{0:T(128)} %bitcast.me_ref, s32[512]{0:T(512)S(1)} %copy-done.8, s32[1,12]{1,0:T(1,128)S(1)} %copy-done.10, ...), custom_call_target="tpu_custom_call" | custom-call | flops 1000 | bytes 1000 | tf_op jit(solution)/shard_map/pick_adapters/pallas_call | solution.py:199
  20.4 0.9 %collective-permute-start.3 = (bf16[6,16,3072]{2,1,0:T(8,128)(2,1)S(1)}, bf16[6,16,3072]{2,1,0:T(8,128)(2,1)S(1)}, u32[]{:S(2)}, u32[]{:S(2)}) collective-permute-start(bf16[6,16,3072]{2,1,0:T(8,128)(2,1)S(1)} %get-tuple-element.24), channel_id=1, source_target_pairs={{0,4},{4,0},{8,12},{12,8},{1,5},{5,1},{9,13},{13,9},{2,6},{6,2},{1... | collective-permute-start | bytes 1769480 | tf_op jit(solution)/shard_map/ppermute | solution.py:373
  21.3 1.1 %collective-permute-start.4 = (bf16[6,16,3072]{2,1,0:T(8,128)(2,1)S(1)}, bf16[6,16,3072]{2,1,0:T(8,128)(2,1)S(1)}, u32[]{:S(2)}, u32[]{:S(2)}) collective-permute-start(bf16[6,16,3072]{2,1,0:T(8,128)(2,1)S(1)} %get-tuple-element.25), channel_id=1, source_target_pairs={{0,8},{4,12},{8,0},{12,4},{1,9},{5,13},{9,1},{13,5},{2,10},{6,14},... | collective-permute-start | bytes 1769480 | tf_op jit(solution)/shard_map/ppermute | solution.py:373
  22.4 0.4 collective-permute-start.5
  22.7 0.0 collective-permute-done.6.rest_0_
  22.7 2.8 %block_product.10.rest_1_ = bf16[512,512]{1,0:T(8,128)(2,1)S(1)} custom-call(s32[1]{0:T(128)} %bitcast.5.first_ref, bf16[512,2048]{1,0:T(8,128)(2,1)S(1)} %get-tuple-element.17.rows_ref, bf16[2048,4096]{1,0:T(8,128)(2,1)} %weight_ref.17, bf16[512,512]{1,0:T(8,128)(2,1)} %collective-permute-done.6.rest_0_, s32[24]{0:T(128)S(1)} %get-tuple-element.21.rest_1_.start_ref), custom_call_target="tpu_custom_call" | custom-call | flops 1000 | bytes 1000 | tf_op jit(solution)/shard_map/block_product/pallas_call | solution.py:53
  25.5 6.4 %collective-permute-start.7 = (bf16[512,512]{1,0:T(8,128)(2,1)S(1)}, bf16[512,512]{1,0:T(8,128)(2,1)S(1)}, u32[]{:S(2)}, u32[]{:S(2)}) collective-permute-start(bf16[512,512]{1,0:T(8,128)(2,1)S(1)} %block_product.10.rest_1_), channel_id=1, source_target_pairs={{0,1},{1,2},{2,3},{3,0},{4,7},{5,4},{6,5},{7,6},{8,9},{9,10},{10,1... | collective-permute-start | bytes 1572872 | tf_op jit(solution)/shard_map/ppermute | solution.py:345
  31.9 0.0 collective-permute-done.8.rest_0_
  31.9 3.5 %block_product.11.rest_0_ = bf16[512,512]{1,0:T(8,128)(2,1)} custom-call(s32[1]{0:T(128)} %bitcast.7.first_ref, bf16[512,2048]{1,0:T(8,128)(2,1)S(1)} %get-tuple-element.17.rows_ref, bf16[2048,4096]{1,0:T(8,128)(2,1)} %weight_ref.17, bf16[512,512]{1,0:T(8,128)(2,1)} %collective-permute-done.8.rest_0_, bf16[512,512]{1,0:T(8,128)(2,1)S(1)} %block_product.10.rest_1_), custom_call_target="tpu_custom_call" | custom-call | flops 1000 | bytes 1000 | tf_op jit(solution)/shard_map/block_product/pallas_call | solution.py:53
  35.4 3.7 %collective-permute-start.12 = (bf16[512,512]{1,0:T(8,128)(2,1)}, bf16[512,512]{1,0:T(8,128)(2,1)}, u32[]{:S(2)}, u32[]{:S(2)}) collective-permute-start(bf16[512,512]{1,0:T(8,128)(2,1)} %block_product.11.rest_0_), channel_id=1, source_target_pairs={{0,3},{1,0},{2,1},{3,2},{4,5},{5,6},{6,7},{7,4},{8,11},{9,8},{10,9... | collective-permute-start | bytes 1572872 | tf_op jit(solution)/shard_map/ppermute | solution.py:345
  39.1 2.7 %block_product.12.rest_1_.rest_5_ = bf16[512,512]{1,0:T(8,128)(2,1)S(1)} custom-call(s32[1]{0:T(128)} %bitcast.6.first_ref, bf16[512,2048]{1,0:T(8,128)(2,1)S(1)} %get-tuple-element.17.rows_ref, bf16[2048,4096]{1,0:T(8,128)(2,1)} %weight_ref.17, bf16[512,512]{1,0:T(8,128)(2,1)} %block_product.11.rest_0_), custom_call_target="tpu_custom_call" | custom-call | flops 8000000000 | bytes 1000 | tf_op jit(solution)/shard_map/block_product/pallas_call | solution.py:53
  41.8 0.0 copy-start.6
  41.8 2.7 %collective-permute-done.7.rest_0_ = bf16[512,512]{1,0:T(8,128)(2,1)S(1)} collective-permute-done((bf16[512,512]{1,0:T(8,128)(2,1)S(1)}, bf16[512,512]{1,0:T(8,128)(2,1)S(1)}, u32[]{:S(2)}, u32[]{:S(2)}) %collective-permute-start.7) | collective-permute-done | bytes 524320 | tf_op jit(solution)/shard_map/ppermute | solution.py:345
  44.5 3.4 %block_product.13.rest_4_ = bf16[512,512]{1,0:T(8,128)(2,1)} custom-call(s32[1]{0:T(128)} %bitcast.4.first_ref, bf16[512,2048]{1,0:T(8,128)(2,1)S(1)} %get-tuple-element.17.rows_ref, bf16[2048,4096]{1,0:T(8,128)(2,1)} %weight_ref.17, bf16[512,512]{1,0:T(8,128)(2,1)S(1)} %collective-permute-done.7.rest_0_, bf16[512,512]{1,0:T(8,128)(2,1)S(1)} %block_product.12.rest_1_.rest_5_), custom_call_target="tpu_custom_call" | custom-call | flops 1000 | bytes 1000 | tf_op jit(solution)/shard_map/block_product/pallas_call | solution.py:53
  47.9 0.0 copy-done.6
  47.9 2.3 %collective-permute-start.15 = (bf16[512,512]{1,0:T(8,128)(2,1)}, bf16[512,512]{1,0:T(8,128)(2,1)}, u32[]{:S(2)}, u32[]{:S(2)}) collective-permute-start(bf16[512,512]{1,0:T(8,128)(2,1)} %block_product.13.rest_4_), channel_id=1, source_target_pairs={{0,1},{1,2},{2,3},{3,0},{4,7},{5,4},{6,5},{7,6},{8,9},{9,10},{10,1... | collective-permute-start | bytes 1572872 | tf_op jit(solution)/shard_map/ppermute | solution.py:345
  50.2 0.0 collective-permute-done.3.rest_1_.rest_7_
  50.2 0.0 collective-permute-done.4.rest_2_.rest_8_
  50.2 0.0 collective-permute-done.5.rest_3_.rest_9_
  50.2 0.0 copy-start.4
  50.2 1.6 %low_sums.1.rest_1_.rest_0_ = bf16[16,512]{1,0:T(8,128)(2,1)S(1)} custom-call(s32[24]{0:T(128)S(1)} %get-tuple-element.21.rest_1_.start_ref, s32[24]{0:T(128)S(1)} %get-tuple-element.22.end_ref, bf16[512,2048]{1,0:T(8,128)(2,1)S(1)} %get-tuple-element.17.rows_ref, bf16[6,16,3072]{2,1,0:T(8,128)(2,1)S(1)} %get-tuple-element.23.rest_0_.rest_6_, ...), custom_call_target="tpu_custom_call" | custom-call | flops 1000 | bytes 1000 | tf_op jit(solution)/shard_map/low_sums/pallas_call | solution.py:241
  51.8 0.0 copy-done.2
  51.8 0.0 copy-start
  51.8 0.8 %copy-done = bf16[6,16,3072]{2,1,0:T(8,128)(2,1)} copy-done((bf16[6,16,3072]{2,1,0:T(8,128)(2,1)}, bf16[6,16,3072]{2,1,0:T(8,128)(2,1)S(1)}, u32[]{:S(2)}) %copy-start) | copy-done | bytes 589848
  52.6 3.0 %collective-permute-start.9 = (bf16[16,512]{1,0:T(8,128)(2,1)S(1)}, bf16[16,512]{1,0:T(8,128)(2,1)S(1)}, u32[]{:S(2)}, u32[]{:S(2)}) collective-permute-start(bf16[16,512]{1,0:T(8,128)(2,1)S(1)} %low_sums.1.rest_1_.rest_0_), channel_id=1, source_target_pairs={{0,1},{1,0},{2,3},{3,2},{4,5},{5,4},{6,7},{7,6},{8,9},{9,8},{10,11... | collective-permute-start | bytes 49160 | tf_op jit(solution)/shard_map/ppermute | solution.py:383
  55.6 0.0 copy-done.4
  55.6 1.1 %collective-permute-start.10 = (bf16[16,512]{1,0:T(8,128)(2,1)S(1)}, bf16[16,512]{1,0:T(8,128)(2,1)S(1)}, u32[]{:S(2)}, u32[]{:S(2)}) collective-permute-start(bf16[16,512]{1,0:T(8,128)(2,1)S(1)} %low_sums.1.rest_1_.rest_0_), channel_id=1, source_target_pairs={{0,2},{1,3},{2,0},{3,1},{4,6},{5,7},{6,4},{7,5},{8,10},{9,11},{10,... | collective-permute-start | bytes 49160 | tf_op jit(solution)/shard_map/ppermute | solution.py:383
  56.7 1.4 %collective-permute-start.11 = (bf16[16,512]{1,0:T(8,128)(2,1)S(1)}, bf16[16,512]{1,0:T(8,128)(2,1)S(1)}, u32[]{:S(2)}, u32[]{:S(2)}) collective-permute-start(bf16[16,512]{1,0:T(8,128)(2,1)S(1)} %low_sums.1.rest_1_.rest_0_), channel_id=1, source_target_pairs={{0,3},{1,2},{2,1},{3,0},{4,7},{5,6},{6,5},{7,4},{8,11},{9,10},{10,... | collective-permute-start | bytes 49160 | tf_op jit(solution)/shard_map/ppermute | solution.py:383
  58.1 3.5 %collective-permute-done.12.rest_0_ = bf16[512,512]{1,0:T(8,128)(2,1)} collective-permute-done((bf16[512,512]{1,0:T(8,128)(2,1)}, bf16[512,512]{1,0:T(8,128)(2,1)}, u32[]{:S(2)}, u32[]{:S(2)}) %collective-permute-start.12) | collective-permute-done | bytes 524320 | tf_op jit(solution)/shard_map/ppermute | solution.py:345
  61.6 2.0 %block_product.14.rest_1_ = bf16[512,256]{1,0:T(8,128)(2,1)S(1)} custom-call(s32[1]{0:T(128)} %bitcast.9.first_ref, bf16[512,2048]{1,0:T(8,128)(2,1)S(1)} %get-tuple-element.17.rows_ref, bf16[2048,4096]{1,0:T(8,128)(2,1)} %weight_ref.17, bf16[512,512]{1,0:T(8,128)(2,1)} %collective-permute-done.12.rest_0_, bf16[16,512]{1,0:T(8,128)(2,1)S(1)} %low_sums.1.rest_1_.rest_0_), custom_call_target="tpu_custom_call" | custom-call | flops 1000 | bytes 1000 | tf_op jit(solution)/shard_map/block_product/pallas_call | solution.py:53
  63.6 0.1 collective-permute-start.14
  63.7 0.0 copy-start.1
  63.7 0.0 copy-start.3
  63.7 0.0 copy-start.5
  63.7 0.0 copy-start.7
  63.7 2.1 %block_product.15.rest_10_ = bf16[512,256]{1,0:T(8,128)(2,1)S(1)} custom-call(s32[1]{0:T(128)} %bitcast.8.first_ref, bf16[512,2048]{1,0:T(8,128)(2,1)S(1)} %get-tuple-element.17.rows_ref, bf16[2048,4096]{1,0:T(8,128)(2,1)} %weight_ref.17, bf16[512,512]{1,0:T(8,128)(2,1)} %collective-permute-done.12.rest_0_, bf16[512,256]{1,0:T(8,128)(2,1)S(1)} %block_product.14.rest_1_), custom_call_target="tpu_custom_call" | custom-call | flops 1000 | bytes 1000 | tf_op jit(solution)/shard_map/block_product/pallas_call | solution.py:53
  65.9 1.3 %collective-permute-done.9.rest_1_ = bf16[16,512]{1,0:T(8,128)(2,1)S(1)} collective-permute-done((bf16[16,512]{1,0:T(8,128)(2,1)S(1)}, bf16[16,512]{1,0:T(8,128)(2,1)S(1)}, u32[]{:S(2)}, u32[]{:S(2)}) %collective-permute-start.9) | collective-permute-done | bytes 16416 | tf_op jit(solution)/shard_map/ppermute | solution.py:383
  67.2 4.6 %collective-permute-start.13 = (bf16[512,256]{1,0:T(8,128)(2,1)S(1)}, bf16[512,256]{1,0:T(8,128)(2,1)S(1)}, u32[]{:S(2)}, u32[]{:S(2)}) collective-permute-start(bf16[512,256]{1,0:T(8,128)(2,1)S(1)} %block_product.15.rest_10_), channel_id=1, source_target_pairs={{0,3},{1,0},{2,1},{3,2},{4,5},{5,6},{6,7},{7,4},{8,11},{9,8},{10,9... | collective-permute-start | bytes 786440 | tf_op jit(solution)/shard_map/ppermute | solution.py:345
  71.8 0.0 collective-permute-done.10.rest_2_
  71.8 0.0 collective-permute-done.11.rest_3_
  71.8 0.0 copy-done.1
  71.8 0.0 copy-done.3
  71.8 0.0 copy-done.5
  71.8 1.3 %adapter_term.1 = (f32[512,512]{1,0:T(8,128)S(1)}, f32[512,512]{1,0:T(8,128)S(1)}) custom-call(s32[24]{0:T(128)S(1)} %get-tuple-element.21.rest_1_.start_ref, s32[24]{0:T(128)S(1)} %get-tuple-element.22.end_ref, bf16[16,512]{1,0:T(8,128)(2,1)S(1)} %low_sums.1.rest_1_.rest_0_, bf16[16,512]{1,0:T(8,128)(2,1)S(1)} %collective-permute-done.9.rest_1_, ...), custom_call_target="tpu_custom_call" | custom-call | flops 1000 | bytes 1000 | tf_op jit(solution)/shard_map/adapter_term/pallas_call | solution.py:287
  73.1 0.0 collective-permute-done.15.rest_0_
  73.1 1.8 %finish.3.rest_1_ = bf16[512,1024]{1,0:T(8,128)(2,1)} custom-call(f32[512,512]{1,0:T(8,128)S(1)} %get-tuple-element.28.term_ref, bf16[512,512]{1,0:T(8,128)(2,1)} %collective-permute-done.15.rest_0_), custom_call_target="tpu_custom_call" | custom-call | flops 8000000000 | bytes 1000 | tf_op jit(solution)/shard_map/finish/pallas_call | solution.py:314
  74.9 0.0 collective-permute-done.14.rest_0_
  74.9 0.8 finish.4.rest_1_
  75.7 2.6 %collective-permute-done.13.rest_0_ = bf16[512,256]{1,0:T(8,128)(2,1)S(1)} collective-permute-done((bf16[512,256]{1,0:T(8,128)(2,1)S(1)}, bf16[512,256]{1,0:T(8,128)(2,1)S(1)}, u32[]{:S(2)}, u32[]{:S(2)}) %collective-permute-start.13) | collective-permute-done | bytes 262176 | tf_op jit(solution)/shard_map/ppermute | solution.py:345
  78.3 0.8 %finish.5 = bf16[512,1024]{1,0:T(8,128)(2,1)} custom-call(f32[512,512]{1,0:T(8,128)S(1)} %get-tuple-element.27.term_ref, bf16[512,256]{1,0:T(8,128)(2,1)S(1)} %collective-permute-done.13.rest_0_, bf16[512,1024]{1,0:T(8,128)(2,1)} %finish.4.rest_1_), custom_call_target="tpu_custom_call", output_to_operand_aliasing={{}: (2, {})} | custom-call | flops 1000 | bytes 1000 | tf_op jit(solution)/shard_map/finish/pallas_call | solution.py:314
  (5 shorter events, 0.0 us)
Async XLA Ops:
  0.0 6.6 %copy-start.9 = (s32[1,12]{1,0:T(1,128)S(1)}, s32[1,12]{1,0:T(1,128)}, u32[]{:S(2)}) copy-start(s32[1,12]{1,0:T(1,128)} %rest_0_.1) | copy-start | bytes 148
  3.5 19.2 %collective-permute-start.6 = (bf16[512,512]{1,0:T(8,128)(2,1)}, bf16[512,512]{1,0:T(8,128)(2,1)}, u32[]{:S(2)}, u32[]{:S(2)}) collective-permute-start(bf16[512,512]{1,0:T(8,128)(2,1)} %get-tuple-element.18.rest_1_), channel_id=1, source_target_pairs={{0,1},{1,2},{2,3},{3,0},{4,7},{5,4},{6,5},{7,6},{8,9},{9,10},{10,1... | collective-permute-start | bytes 1572872 | tf_op jit(solution)/shard_map/ppermute | solution.py:345
  10.0 21.9 %collective-permute-start.8 = (bf16[512,512]{1,0:T(8,128)(2,1)}, bf16[512,512]{1,0:T(8,128)(2,1)}, u32[]{:S(2)}, u32[]{:S(2)}) collective-permute-start(bf16[512,512]{1,0:T(8,128)(2,1)} %get-tuple-element.20.rest_0_), channel_id=1, source_target_pairs={{0,3},{1,0},{2,1},{3,2},{4,5},{5,6},{6,7},{7,4},{8,11},{9,8},{10,9... | collective-permute-start | bytes 1572872 | tf_op jit(solution)/shard_map/ppermute | solution.py:345
  12.2 4.7 %collective-permute-start = (s32[1,12]{1,0:T(1,128)S(1)}, s32[1,12]{1,0:T(1,128)S(1)}, u32[]{:S(2)}, u32[]{:S(2)}) collective-permute-start(s32[1,12]{1,0:T(1,128)S(1)} %get-tuple-element.19.rest_0_), channel_id=1, source_target_pairs={{0,4},{4,0},{8,12},{12,8},{1,5},{5,1},{9,13},{13,9},{2,6},{6,2},{1... | collective-permute-start | bytes 152 | tf_op jit(solution)/shard_map/ppermute | solution.py:368
  12.2 4.7 %collective-permute-start.1 = (s32[1,12]{1,0:T(1,128)S(1)}, s32[1,12]{1,0:T(1,128)S(1)}, u32[]{:S(2)}, u32[]{:S(2)}) collective-permute-start(s32[1,12]{1,0:T(1,128)S(1)} %get-tuple-element.19.rest_0_), channel_id=1, source_target_pairs={{0,8},{4,12},{8,0},{12,4},{1,9},{5,13},{9,1},{13,5},{2,10},{6,14},... | collective-permute-start | bytes 152 | tf_op jit(solution)/shard_map/ppermute | solution.py:368
  13.8 3.0 %collective-permute-start.2 = (s32[1,12]{1,0:T(1,128)S(1)}, s32[1,12]{1,0:T(1,128)S(1)}, u32[]{:S(2)}, u32[]{:S(2)}) collective-permute-start(s32[1,12]{1,0:T(1,128)S(1)} %get-tuple-element.19.rest_0_), channel_id=1, source_target_pairs={{0,12},{4,8},{8,4},{12,0},{1,13},{5,9},{9,5},{13,1},{2,14},{6,10},... | collective-permute-start | bytes 152 | tf_op jit(solution)/shard_map/ppermute | solution.py:368
  14.0 2.9 %copy-start.8 = (s32[512]{0:T(512)S(1)}, s32[512]{0:T(512)}, u32[]{:S(2)}) copy-start(s32[512]{0:T(512)} %table_ref.1) | copy-start | bytes 6148
  14.0 2.9 %copy-start.10 = (s32[1,12]{1,0:T(1,128)S(1)}, s32[1,12]{1,0:T(1,128)}, u32[]{:S(2)}) copy-start(s32[1,12]{1,0:T(1,128)} %lens_ref.1) | copy-start | bytes 148
  20.4 29.8 %collective-permute-start.3 = (bf16[6,16,3072]{2,1,0:T(8,128)(2,1)S(1)}, bf16[6,16,3072]{2,1,0:T(8,128)(2,1)S(1)}, u32[]{:S(2)}, u32[]{:S(2)}) collective-permute-start(bf16[6,16,3072]{2,1,0:T(8,128)(2,1)S(1)} %get-tuple-element.24), channel_id=1, source_target_pairs={{0,4},{4,0},{8,12},{12,8},{1,5},{5,1},{9,13},{13,9},{2,6},{6,2},{1... | collective-permute-start | bytes 1769480 | tf_op jit(solution)/shard_map/ppermute | solution.py:373
  21.3 28.9 %collective-permute-start.4 = (bf16[6,16,3072]{2,1,0:T(8,128)(2,1)S(1)}, bf16[6,16,3072]{2,1,0:T(8,128)(2,1)S(1)}, u32[]{:S(2)}, u32[]{:S(2)}) collective-permute-start(bf16[6,16,3072]{2,1,0:T(8,128)(2,1)S(1)} %get-tuple-element.25), channel_id=1, source_target_pairs={{0,8},{4,12},{8,0},{12,4},{1,9},{5,13},{9,1},{13,5},{2,10},{6,14},... | collective-permute-start | bytes 1769480 | tf_op jit(solution)/shard_map/ppermute | solution.py:373
  22.4 27.8 %collective-permute-start.5 = (bf16[6,16,3072]{2,1,0:T(8,128)(2,1)S(1)}, bf16[6,16,3072]{2,1,0:T(8,128)(2,1)S(1)}, u32[]{:S(2)}, u32[]{:S(2)}) collective-permute-start(bf16[6,16,3072]{2,1,0:T(8,128)(2,1)S(1)} %get-tuple-element.26), channel_id=1, source_target_pairs={{0,12},{4,8},{8,4},{12,0},{1,13},{5,9},{9,5},{13,1},{2,14},{6,10},... | collective-permute-start | bytes 1769480 | tf_op jit(solution)/shard_map/ppermute | solution.py:373
  25.5 19.0 %collective-permute-start.7 = (bf16[512,512]{1,0:T(8,128)(2,1)S(1)}, bf16[512,512]{1,0:T(8,128)(2,1)S(1)}, u32[]{:S(2)}, u32[]{:S(2)}) collective-permute-start(bf16[512,512]{1,0:T(8,128)(2,1)S(1)} %block_product.10.rest_1_), channel_id=1, source_target_pairs={{0,1},{1,2},{2,3},{3,0},{4,7},{5,4},{6,5},{7,6},{8,9},{9,10},{10,1... | collective-permute-start | bytes 1572872 | tf_op jit(solution)/shard_map/ppermute | solution.py:345
  35.4 26.2 %collective-permute-start.12 = (bf16[512,512]{1,0:T(8,128)(2,1)}, bf16[512,512]{1,0:T(8,128)(2,1)}, u32[]{:S(2)}, u32[]{:S(2)}) collective-permute-start(bf16[512,512]{1,0:T(8,128)(2,1)} %block_product.11.rest_0_), channel_id=1, source_target_pairs={{0,3},{1,0},{2,1},{3,2},{4,5},{5,6},{6,7},{7,4},{8,11},{9,8},{10,9... | collective-permute-start | bytes 1572872 | tf_op jit(solution)/shard_map/ppermute | solution.py:345
  41.8 6.1 %copy-start.6 = (bf16[512,512]{1,0:T(8,128)(2,1)}, bf16[512,512]{1,0:T(8,128)(2,1)S(1)}, u32[]{:S(2)}) copy-start(bf16[512,512]{1,0:T(8,128)(2,1)S(1)} %block_product.12.rest_1_.rest_5_) | copy-start | bytes 1572868
  47.9 25.2 %collective-permute-start.15 = (bf16[512,512]{1,0:T(8,128)(2,1)}, bf16[512,512]{1,0:T(8,128)(2,1)}, u32[]{:S(2)}, u32[]{:S(2)}) collective-permute-start(bf16[512,512]{1,0:T(8,128)(2,1)} %block_product.13.rest_4_), channel_id=1, source_target_pairs={{0,1},{1,2},{2,3},{3,0},{4,7},{5,4},{6,5},{7,6},{8,9},{9,10},{10,1... | collective-permute-start | bytes 1572872 | tf_op jit(solution)/shard_map/ppermute | solution.py:345
  50.2 1.6 %copy-start.2 = (bf16[6,16,3072]{2,1,0:T(8,128)(2,1)}, bf16[6,16,3072]{2,1,0:T(8,128)(2,1)S(1)}, u32[]{:S(2)}) copy-start(bf16[6,16,3072]{2,1,0:T(8,128)(2,1)S(1)} %collective-permute-done.4.rest_2_.rest_8_) | copy-start | bytes 1769476
  50.2 5.4 %copy-start.4 = (bf16[6,16,3072]{2,1,0:T(8,128)(2,1)}, bf16[6,16,3072]{2,1,0:T(8,128)(2,1)S(1)}, u32[]{:S(2)}) copy-start(bf16[6,16,3072]{2,1,0:T(8,128)(2,1)S(1)} %collective-permute-done.5.rest_3_.rest_9_) | copy-start | bytes 1769476
  51.8 0.8 %copy-start = (bf16[6,16,3072]{2,1,0:T(8,128)(2,1)}, bf16[6,16,3072]{2,1,0:T(8,128)(2,1)S(1)}, u32[]{:S(2)}) copy-start(bf16[6,16,3072]{2,1,0:T(8,128)(2,1)S(1)} %collective-permute-done.3.rest_1_.rest_7_) | copy-start | bytes 1769476
  52.6 14.6 %collective-permute-start.9 = (bf16[16,512]{1,0:T(8,128)(2,1)S(1)}, bf16[16,512]{1,0:T(8,128)(2,1)S(1)}, u32[]{:S(2)}, u32[]{:S(2)}) collective-permute-start(bf16[16,512]{1,0:T(8,128)(2,1)S(1)} %low_sums.1.rest_1_.rest_0_), channel_id=1, source_target_pairs={{0,1},{1,0},{2,3},{3,2},{4,5},{5,4},{6,7},{7,6},{8,9},{9,8},{10,11... | collective-permute-start | bytes 49160 | tf_op jit(solution)/shard_map/ppermute | solution.py:383
  55.6 16.2 %collective-permute-start.10 = (bf16[16,512]{1,0:T(8,128)(2,1)S(1)}, bf16[16,512]{1,0:T(8,128)(2,1)S(1)}, u32[]{:S(2)}, u32[]{:S(2)}) collective-permute-start(bf16[16,512]{1,0:T(8,128)(2,1)S(1)} %low_sums.1.rest_1_.rest_0_), channel_id=1, source_target_pairs={{0,2},{1,3},{2,0},{3,1},{4,6},{5,7},{6,4},{7,5},{8,10},{9,11},{10,... | collective-permute-start | bytes 49160 | tf_op jit(solution)/shard_map/ppermute | solution.py:383
  56.7 15.1 %collective-permute-start.11 = (bf16[16,512]{1,0:T(8,128)(2,1)S(1)}, bf16[16,512]{1,0:T(8,128)(2,1)S(1)}, u32[]{:S(2)}, u32[]{:S(2)}) collective-permute-start(bf16[16,512]{1,0:T(8,128)(2,1)S(1)} %low_sums.1.rest_1_.rest_0_), channel_id=1, source_target_pairs={{0,3},{1,2},{2,1},{3,0},{4,7},{5,6},{6,5},{7,4},{8,11},{9,10},{10,... | collective-permute-start | bytes 49160 | tf_op jit(solution)/shard_map/ppermute | solution.py:383
  63.6 11.3 %collective-permute-start.14 = (bf16[512,256]{1,0:T(8,128)(2,1)S(1)}, bf16[512,256]{1,0:T(8,128)(2,1)S(1)}, u32[]{:S(2)}, u32[]{:S(2)}) collective-permute-start(bf16[512,256]{1,0:T(8,128)(2,1)S(1)} %block_product.14.rest_1_), channel_id=1, source_target_pairs={{0,3},{1,0},{2,1},{3,2},{4,5},{5,6},{6,7},{7,4},{8,11},{9,8},{10,9... | collective-permute-start | bytes 786440 | tf_op jit(solution)/shard_map/ppermute | solution.py:345
  63.7 8.1 %copy-start.1 = (bf16[6,16,3072]{2,1,0:T(8,128)(2,1)S(1)}, bf16[6,16,3072]{2,1,0:T(8,128)(2,1)}, u32[]{:S(2)}) copy-start(bf16[6,16,3072]{2,1,0:T(8,128)(2,1)} %copy-done) | copy-start | bytes 1769476
  63.7 8.1 %copy-start.3 = (bf16[6,16,3072]{2,1,0:T(8,128)(2,1)S(1)}, bf16[6,16,3072]{2,1,0:T(8,128)(2,1)}, u32[]{:S(2)}) copy-start(bf16[6,16,3072]{2,1,0:T(8,128)(2,1)} %copy-done.2) | copy-start | bytes 1769476
  63.7 8.1 %copy-start.5 = (bf16[6,16,3072]{2,1,0:T(8,128)(2,1)S(1)}, bf16[6,16,3072]{2,1,0:T(8,128)(2,1)}, u32[]{:S(2)}) copy-start(bf16[6,16,3072]{2,1,0:T(8,128)(2,1)} %copy-done.4) | copy-start | bytes 1769476
  63.7 8.1 %copy-start.7 = (bf16[512,512]{1,0:T(8,128)(2,1)S(1)}, bf16[512,512]{1,0:T(8,128)(2,1)}, u32[]{:S(2)}) copy-start(bf16[512,512]{1,0:T(8,128)(2,1)} %copy-done.6) | copy-start | bytes 1572868
  67.2 11.2 %collective-permute-start.13 = (bf16[512,256]{1,0:T(8,128)(2,1)S(1)}, bf16[512,256]{1,0:T(8,128)(2,1)S(1)}, u32[]{:S(2)}, u32[]{:S(2)}) collective-permute-start(bf16[512,256]{1,0:T(8,128)(2,1)S(1)} %block_product.15.rest_10_), channel_id=1, source_target_pairs={{0,3},{1,0},{2,1},{3,2},{4,5},{5,6},{6,7},{7,4},{8,11},{9,8},{10,9... | collective-permute-start | bytes 786440 | tf_op jit(solution)/shard_map/ppermute | solution.py:345

commit v27 on v26

--- a/solution.py
+++ b/solution.py
@@ -378,7 +378,7 @@
             if step == steps - 1 and piece == PIECES - 1:
                 low = low_sums(starts, ends, rows, packs, rank, [last])
                 lows = [low]
-                for x in range(1, tp_total):
+                for x in reversed(range(1, tp_total)):
                     pairs = [(i, i ^ x) for i in range(tp_total)]
                     lows.append(lax.ppermute(low, "tp", pairs))
                 last = low

time: 79.5 us -> 79.4 us (level)
  starting transfers between devices: 31.9 us -> 30.5 us
  waiting for transfers between devices: 10.2 us -> 11.3 us
    ppermute x7, waiting for transfers between devices: 8.85 us -> 9.92 us  [move(): return lax.ppermute(value, ('req', 'tp'), pairs)]
    ppermute x3, starting transfers between devices: 5.5 us -> 4.6 us  [local(): lows.append(lax.ppermute(low, 'tp', pairs))]
where the time goes in v27:
time: 79.4 us; the launch traced here: 79 us
  Pallas kernels  36.1 us (45%)
  starting transfers between devices  30.5 us (38%)
  waiting for transfers between devices  11.3 us (14%)
  local copies, waits for them, and re-layouts  0.85 us (1%)
    pallas_call x8, Pallas kernels, block_product(): pl.pallas_call(functools.partial(product_kernel, len(addends), with_ids),...  22.6 us
    ppermute x7, starting transfers between devices, move(): return lax.ppermute(value, ('req', 'tp'), pairs)  22.1 us
    ppermute x7, waiting for transfers between devices, move(): return lax.ppermute(value, ('req', 'tp'), pairs)  9.92 us
    ppermute x3, starting transfers between devices, local(): lows.append(lax.ppermute(low, 'tp', pairs))  4.6 us
    pallas_call x1, Pallas kernels, pick_adapters(): pl.pallas_call(functools.partial(pick_kernel, peers, len(after)), in_spec...  3.72 us
    pallas_call x1, Pallas kernels, first_product(): pl.pallas_call(functools.partial(first_kernel, chunk), in_specs=[pl.Block...  3.49 us
    pallas_call x3, Pallas kernels, finish(): pl.pallas_call(functools.partial(finish_kernel, 1), grid=(row_total // he...  3.38 us
    ppermute x3, starting transfers between devices, local(): lax.ppermute(packs[x], 'req', [(i, i ^ x) for i in range(req_total)])  1.93 us
  transfers between devices with their start and end apart: 16, of which 4 were waited for; matrix products, arithmetic and copies ran while one was open for 0% of the time, Pallas kernels for 40%

profile of v27, /device:TPU:0, one launch (start us, length us, event | category | flops | bytes accessed | tf_op | source)
XLA Modules:
  0.0 79.0 jit_solution(5687472442712845780)
XLA Ops:
  0.0 3.5 %first_product.1 = (bf16[512,512]{1,0:T(8,128)(2,1)}, bf16[512,2048]{1,0:T(8,128)(2,1)S(1)}) custom-call(s32[1]{0:T(128)} %bitcast.2.first_ref, bf16[512,2048]{1,0:T(8,128)(2,1)} %rows_ref.1, bf16[2048,4096]{1,0:T(8,128)(2,1)} %weight_ref.17), custom_call_target="tpu_custom_call" | custom-call | flops 1000 | bytes 1000 | tf_op jit(solution)/shard_map/first_product/pallas_call | solution.py:108
  3.5 3.1 %collective-permute-start.6 = (bf16[512,512]{1,0:T(8,128)(2,1)}, bf16[512,512]{1,0:T(8,128)(2,1)}, u32[]{:S(2)}, u32[]{:S(2)}) collective-permute-start(bf16[512,512]{1,0:T(8,128)(2,1)} %get-tuple-element.18.rest_1_), channel_id=1, source_target_pairs={{0,1},{1,2},{2,3},{3,0},{4,7},{5,4},{6,5},{7,6},{8,9},{9,10},{10,1... | collective-permute-start | bytes 1572872 | tf_op jit(solution)/shard_map/ppermute | solution.py:345
  6.6 0.0 copy-done.9
  6.6 3.4 %block_product.8 = (bf16[512,512]{1,0:T(8,128)(2,1)}, s32[1,12]{1,0:T(1,128)S(1)}) custom-call(s32[1]{0:T(128)} %bitcast.1.first_ref, bf16[512,2048]{1,0:T(8,128)(2,1)S(1)} %get-tuple-element.17.rows_ref, bf16[2048,4096]{1,0:T(8,128)(2,1)} %weight_ref.17, s32[1,12]{1,0:T(1,128)S(1)} %copy-done.9, bf16[512,512]{1,0:T(8,128)(2,1)} %get-tuple-element.18.rest_1_), custom_call_target="tpu_custom_call" | custom-call | flops 1000 | bytes 1000 | tf_op jit(solution)/shard_map/block_product/pallas_call | solution.py:53
  10.0 2.1 %collective-permute-start.8 = (bf16[512,512]{1,0:T(8,128)(2,1)}, bf16[512,512]{1,0:T(8,128)(2,1)}, u32[]{:S(2)}, u32[]{:S(2)}) collective-permute-start(bf16[512,512]{1,0:T(8,128)(2,1)} %get-tuple-element.20.rest_0_), channel_id=1, source_target_pairs={{0,3},{1,0},{2,1},{3,2},{4,5},{5,6},{6,7},{7,4},{8,11},{9,8},{10,9... | collective-permute-start | bytes 1572872 | tf_op jit(solution)/shard_map/ppermute | solution.py:345
  12.2 0.0 collective-permute-start
  12.2 1.7 %collective-permute-start.1 = (s32[1,12]{1,0:T(1,128)S(1)}, s32[1,12]{1,0:T(1,128)S(1)}, u32[]{:S(2)}, u32[]{:S(2)}) collective-permute-start(s32[1,12]{1,0:T(1,128)S(1)} %get-tuple-element.19.rest_0_), channel_id=1, source_target_pairs={{0,8},{4,12},{8,0},{12,4},{1,9},{5,13},{9,1},{13,5},{2,10},{6,14},... | collective-permute-start | bytes 152 | tf_op jit(solution)/shard_map/ppermute | solution.py:368
  13.8 0.2 collective-permute-start.2
  14.0 2.7 %block_product.9.rest_6_.rest_4_ = bf16[512,512]{1,0:T(8,128)(2,1)S(1)} custom-call(s32[1]{0:T(128)} %bitcast.3.first_ref, bf16[512,2048]{1,0:T(8,128)(2,1)S(1)} %get-tuple-element.17.rows_ref, bf16[2048,4096]{1,0:T(8,128)(2,1)} %weight_ref.17, bf16[512,512]{1,0:T(8,128)(2,1)} %get-tuple-element.20.rest_0_), custom_call_target="tpu_custom_call" | custom-call | flops 1000 | bytes 1000 | tf_op jit(solution)/shard_map/block_product/pallas_call | solution.py:53
  16.9 0.0 collective-permute-done.rest_1_
  16.9 0.0 collective-permute-done.1.rest_2_
  16.9 0.0 collective-permute-done.2.rest_3_
  16.9 0.0 copy-done.8
  16.9 0.0 copy-done.10
  16.9 3.7 %pick_adapters.1 = (bf16[6,16,3072]{2,1,0:T(8,128)(2,1)S(1)}, bf16[6,16,3072]{2,1,0:T(8,128)(2,1)S(1)}, bf16[6,16,3072]{2,1,0:T(8,128)(2,1)S(1)}, bf16[6,16,3072...) custom-call(s32[1]{0:T(128)} %bitcast.me_ref, s32[512]{0:T(512)S(1)} %copy-done.8, s32[1,12]{1,0:T(1,128)S(1)} %copy-done.10, ...), custom_call_target="tpu_custom_call" | custom-call | flops 1000 | bytes 1000 | tf_op jit(solution)/shard_map/pick_adapters/pallas_call | solution.py:199
  20.6 0.1 collective-permute-start.3
  20.7 1.8 %collective-permute-start.4 = (bf16[6,16,3072]{2,1,0:T(8,128)(2,1)S(1)}, bf16[6,16,3072]{2,1,0:T(8,128)(2,1)S(1)}, u32[]{:S(2)}, u32[]{:S(2)}) collective-permute-start(bf16[6,16,3072]{2,1,0:T(8,128)(2,1)S(1)} %get-tuple-element.25), channel_id=1, source_target_pairs={{0,8},{4,12},{8,0},{12,4},{1,9},{5,13},{9,1},{13,5},{2,10},{6,14},... | collective-permute-start | bytes 1769480 | tf_op jit(solution)/shard_map/ppermute | solution.py:373
  22.5 0.1 collective-permute-start.5
  22.6 0.0 collective-permute-done.6.rest_0_
  22.6 2.8 %block_product.10.rest_1_ = bf16[512,512]{1,0:T(8,128)(2,1)S(1)} custom-call(s32[1]{0:T(128)} %bitcast.5.first_ref, bf16[512,2048]{1,0:T(8,128)(2,1)S(1)} %get-tuple-element.17.rows_ref, bf16[2048,4096]{1,0:T(8,128)(2,1)} %weight_ref.17, bf16[512,512]{1,0:T(8,128)(2,1)} %collective-permute-done.6.rest_0_, s32[24]{0:T(128)S(1)} %get-tuple-element.21.rest_1_.start_ref), custom_call_target="tpu_custom_call" | custom-call | flops 1000 | bytes 1000 | tf_op jit(solution)/shard_map/block_product/pallas_call | solution.py:53
  25.4 6.5 %collective-permute-start.7 = (bf16[512,512]{1,0:T(8,128)(2,1)S(1)}, bf16[512,512]{1,0:T(8,128)(2,1)S(1)}, u32[]{:S(2)}, u32[]{:S(2)}) collective-permute-start(bf16[512,512]{1,0:T(8,128)(2,1)S(1)} %block_product.10.rest_1_), channel_id=1, source_target_pairs={{0,1},{1,2},{2,3},{3,0},{4,7},{5,4},{6,5},{7,6},{8,9},{9,10},{10,1... | collective-permute-start | bytes 1572872 | tf_op jit(solution)/shard_map/ppermute | solution.py:345
  31.9 0.0 collective-permute-done.8.rest_0_
  31.9 3.5 %block_product.11.rest_0_ = bf16[512,512]{1,0:T(8,128)(2,1)} custom-call(s32[1]{0:T(128)} %bitcast.7.first_ref, bf16[512,2048]{1,0:T(8,128)(2,1)S(1)} %get-tuple-element.17.rows_ref, bf16[2048,4096]{1,0:T(8,128)(2,1)} %weight_ref.17, bf16[512,512]{1,0:T(8,128)(2,1)} %collective-permute-done.8.rest_0_, bf16[512,512]{1,0:T(8,128)(2,1)S(1)} %block_product.10.rest_1_), custom_call_target="tpu_custom_call" | custom-call | flops 1000 | bytes 1000 | tf_op jit(solution)/shard_map/block_product/pallas_call | solution.py:53
  35.4 3.7 %collective-permute-start.12 = (bf16[512,512]{1,0:T(8,128)(2,1)}, bf16[512,512]{1,0:T(8,128)(2,1)}, u32[]{:S(2)}, u32[]{:S(2)}) collective-permute-start(bf16[512,512]{1,0:T(8,128)(2,1)} %block_product.11.rest_0_), channel_id=1, source_target_pairs={{0,3},{1,0},{2,1},{3,2},{4,5},{5,6},{6,7},{7,4},{8,11},{9,8},{10,9... | collective-permute-start | bytes 1572872 | tf_op jit(solution)/shard_map/ppermute | solution.py:345
  39.1 2.7 %block_product.12.rest_1_.rest_5_ = bf16[512,512]{1,0:T(8,128)(2,1)S(1)} custom-call(s32[1]{0:T(128)} %bitcast.6.first_ref, bf16[512,2048]{1,0:T(8,128)(2,1)S(1)} %get-tuple-element.17.rows_ref, bf16[2048,4096]{1,0:T(8,128)(2,1)} %weight_ref.17, bf16[512,512]{1,0:T(8,128)(2,1)} %block_product.11.rest_0_), custom_call_target="tpu_custom_call" | custom-call | flops 8000000000 | bytes 1000 | tf_op jit(solution)/shard_map/block_product/pallas_call | solution.py:53
  41.8 0.0 copy-start.6
  41.8 2.7 %collective-permute-done.7.rest_0_ = bf16[512,512]{1,0:T(8,128)(2,1)S(1)} collective-permute-done((bf16[512,512]{1,0:T(8,128)(2,1)S(1)}, bf16[512,512]{1,0:T(8,128)(2,1)S(1)}, u32[]{:S(2)}, u32[]{:S(2)}) %collective-permute-start.7) | collective-permute-done | bytes 524320 | tf_op jit(solution)/shard_map/ppermute | solution.py:345
  44.5 3.4 %block_product.13.rest_4_ = bf16[512,512]{1,0:T(8,128)(2,1)} custom-call(s32[1]{0:T(128)} %bitcast.4.first_ref, bf16[512,2048]{1,0:T(8,128)(2,1)S(1)} %get-tuple-element.17.rows_ref, bf16[2048,4096]{1,0:T(8,128)(2,1)} %weight_ref.17, bf16[512,512]{1,0:T(8,128)(2,1)S(1)} %collective-permute-done.7.rest_0_, bf16[512,512]{1,0:T(8,128)(2,1)S(1)} %block_product.12.rest_1_.rest_5_), custom_call_target="tpu_custom_call" | custom-call | flops 1000 | bytes 1000 | tf_op jit(solution)/shard_map/block_product/pallas_call | solution.py:53
  47.9 0.0 copy-done.6
  47.9 2.3 %collective-permute-start.15 = (bf16[512,512]{1,0:T(8,128)(2,1)}, bf16[512,512]{1,0:T(8,128)(2,1)}, u32[]{:S(2)}, u32[]{:S(2)}) collective-permute-start(bf16[512,512]{1,0:T(8,128)(2,1)} %block_product.13.rest_4_), channel_id=1, source_target_pairs={{0,1},{1,2},{2,3},{3,0},{4,7},{5,4},{6,5},{7,6},{8,9},{9,10},{10,1... | collective-permute-start | bytes 1572872 | tf_op jit(solution)/shard_map/ppermute | solution.py:345
  50.2 0.0 collective-permute-done.3.rest_1_.rest_7_
  50.2 0.0 collective-permute-done.4.rest_2_.rest_8_
  50.2 0.0 collective-permute-done.5.rest_3_.rest_9_
  50.2 0.0 copy-start.4
  50.2 1.6 %low_sums.1.rest_1_.rest_0_ = bf16[16,512]{1,0:T(8,128)(2,1)S(1)} custom-call(s32[24]{0:T(128)S(1)} %get-tuple-element.21.rest_1_.start_ref, s32[24]{0:T(128)S(1)} %get-tuple-element.22.end_ref, bf16[512,2048]{1,0:T(8,128)(2,1)S(1)} %get-tuple-element.17.rows_ref, bf16[6,16,3072]{2,1,0:T(8,128)(2,1)S(1)} %get-tuple-element.23.rest_0_.rest_6_, ...), custom_call_target="tpu_custom_call" | custom-call | flops 1000 | bytes 1000 | tf_op jit(solution)/shard_map/low_sums/pallas_call | solution.py:241
  51.8 0.0 copy-done.2
  51.8 0.0 copy-start
  51.8 0.8 %copy-done = bf16[6,16,3072]{2,1,0:T(8,128)(2,1)} copy-done((bf16[6,16,3072]{2,1,0:T(8,128)(2,1)}, bf16[6,16,3072]{2,1,0:T(8,128)(2,1)S(1)}, u32[]{:S(2)}) %copy-start) | copy-done | bytes 589848
  52.6 3.5 %collective-permute-start.9 = (bf16[16,512]{1,0:T(8,128)(2,1)S(1)}, bf16[16,512]{1,0:T(8,128)(2,1)S(1)}, u32[]{:S(2)}, u32[]{:S(2)}) collective-permute-start(bf16[16,512]{1,0:T(8,128)(2,1)S(1)} %low_sums.1.rest_1_.rest_0_), channel_id=1, source_target_pairs={{0,3},{1,2},{2,1},{3,0},{4,7},{5,6},{6,5},{7,4},{8,11},{9,10},{10,... | collective-permute-start | bytes 49160 | tf_op jit(solution)/shard_map/ppermute | solution.py:383
  56.1 0.0 copy-done.4
  56.1 0.9 %collective-permute-start.10 = (bf16[16,512]{1,0:T(8,128)(2,1)S(1)}, bf16[16,512]{1,0:T(8,128)(2,1)S(1)}, u32[]{:S(2)}, u32[]{:S(2)}) collective-permute-start(bf16[16,512]{1,0:T(8,128)(2,1)S(1)} %low_sums.1.rest_1_.rest_0_), channel_id=1, source_target_pairs={{0,2},{1,3},{2,0},{3,1},{4,6},{5,7},{6,4},{7,5},{8,10},{9,11},{10,... | collective-permute-start | bytes 49160 | tf_op jit(solution)/shard_map/ppermute | solution.py:383
  57.0 0.2 collective-permute-start.11
  57.2 4.4 %collective-permute-done.12.rest_0_ = bf16[512,512]{1,0:T(8,128)(2,1)} collective-permute-done((bf16[512,512]{1,0:T(8,128)(2,1)}, bf16[512,512]{1,0:T(8,128)(2,1)}, u32[]{:S(2)}, u32[]{:S(2)}) %collective-permute-start.12) | collective-permute-done | bytes 524320 | tf_op jit(solution)/shard_map/ppermute | solution.py:345
  61.6 2.0 %block_product.14.rest_1_ = bf16[512,256]{1,0:T(8,128)(2,1)S(1)} custom-call(s32[1]{0:T(128)} %bitcast.9.first_ref, bf16[512,2048]{1,0:T(8,128)(2,1)S(1)} %get-tuple-element.17.rows_ref, bf16[2048,4096]{1,0:T(8,128)(2,1)} %weight_ref.17, bf16[512,512]{1,0:T(8,128)(2,1)} %collective-permute-done.12.rest_0_, bf16[16,512]{1,0:T(8,128)(2,1)S(1)} %low_sums.1.rest_1_.rest_0_), custom_call_target="tpu_custom_call" | custom-call | flops 1000 | bytes 1000 | tf_op jit(solution)/shard_map/block_product/pallas_call | solution.py:53
  63.6 0.1 collective-permute-start.14
  63.7 0.0 copy-start.1
  63.7 0.0 copy-start.3
  63.7 0.0 copy-start.5
  63.7 2.1 %block_product.15.rest_10_ = bf16[512,256]{1,0:T(8,128)(2,1)S(1)} custom-call(s32[1]{0:T(128)} %bitcast.8.first_ref, bf16[512,2048]{1,0:T(8,128)(2,1)S(1)} %get-tuple-element.17.rows_ref, bf16[2048,4096]{1,0:T(8,128)(2,1)} %weight_ref.17, bf16[512,512]{1,0:T(8,128)(2,1)} %collective-permute-done.12.rest_0_, bf16[512,256]{1,0:T(8,128)(2,1)S(1)} %block_product.14.rest_1_), custom_call_target="tpu_custom_call" | custom-call | flops 1000 | bytes 1000 | tf_op jit(solution)/shard_map/block_product/pallas_call | solution.py:53
  65.9 1.3 %collective-permute-done.9.rest_1_ = bf16[16,512]{1,0:T(8,128)(2,1)S(1)} collective-permute-done((bf16[16,512]{1,0:T(8,128)(2,1)S(1)}, bf16[16,512]{1,0:T(8,128)(2,1)S(1)}, u32[]{:S(2)}, u32[]{:S(2)}) %collective-permute-start.9) | collective-permute-done | bytes 16416 | tf_op jit(solution)/shard_map/ppermute | solution.py:383
  67.2 4.2 %collective-permute-start.13 = (bf16[512,256]{1,0:T(8,128)(2,1)S(1)}, bf16[512,256]{1,0:T(8,128)(2,1)S(1)}, u32[]{:S(2)}, u32[]{:S(2)}) collective-permute-start(bf16[512,256]{1,0:T(8,128)(2,1)S(1)} %block_product.15.rest_10_), channel_id=1, source_target_pairs={{0,3},{1,0},{2,1},{3,2},{4,5},{5,6},{6,7},{7,4},{8,11},{9,8},{10,9... | collective-permute-start | bytes 786440 | tf_op jit(solution)/shard_map/ppermute | solution.py:345
  71.4 0.0 collective-permute-done.10.rest_2_
  71.5 0.0 collective-permute-done.11.rest_3_
  71.5 0.0 copy-done.1
  71.5 0.0 copy-done.3
  71.5 0.0 copy-done.5
  71.5 0.0 copy-done.7
  71.5 1.3 %adapter_term.1 = (f32[512,512]{1,0:T(8,128)S(1)}, f32[512,512]{1,0:T(8,128)S(1)}) custom-call(s32[24]{0:T(128)S(1)} %get-tuple-element.21.rest_1_.start_ref, s32[24]{0:T(128)S(1)} %get-tuple-element.22.end_ref, bf16[16,512]{1,0:T(8,128)(2,1)S(1)} %low_sums.1.rest_1_.rest_0_, bf16[16,512]{1,0:T(8,128)(2,1)S(1)} %collective-permute-done.9.rest_1_, ...), custom_call_target="tpu_custom_call" | custom-call | flops 1000 | bytes 1000 | tf_op jit(solution)/shard_map/adapter_term/pallas_call | solution.py:287
  72.8 0.0 collective-permute-done.15.rest_0_
  72.8 1.8 %finish.3.rest_1_ = bf16[512,1024]{1,0:T(8,128)(2,1)} custom-call(f32[512,512]{1,0:T(8,128)S(1)} %get-tuple-element.28.term_ref, bf16[512,512]{1,0:T(8,128)(2,1)} %collective-permute-done.15.rest_0_), custom_call_target="tpu_custom_call" | custom-call | flops 8000000000 | bytes 1000 | tf_op jit(solution)/shard_map/finish/pallas_call | solution.py:314
  74.6 0.0 collective-permute-done.14.rest_0_
  74.6 0.8 finish.4.rest_1_
  75.4 2.8 %collective-permute-done.13.rest_0_ = bf16[512,256]{1,0:T(8,128)(2,1)S(1)} collective-permute-done((bf16[512,256]{1,0:T(8,128)(2,1)S(1)}, bf16[512,256]{1,0:T(8,128)(2,1)S(1)}, u32[]{:S(2)}, u32[]{:S(2)}) %collective-permute-start.13) | collective-permute-done | bytes 262176 | tf_op jit(solution)/shard_map/ppermute | solution.py:345
  78.2 0.8 %finish.5 = bf16[512,1024]{1,0:T(8,128)(2,1)} custom-call(f32[512,512]{1,0:T(8,128)S(1)} %get-tuple-element.27.term_ref, bf16[512,256]{1,0:T(8,128)(2,1)S(1)} %collective-permute-done.13.rest_0_, bf16[512,1024]{1,0:T(8,128)(2,1)} %finish.4.rest_1_), custom_call_target="tpu_custom_call", output_to_operand_aliasing={{}: (2, {})} | custom-call | flops 1000 | bytes 1000 | tf_op jit(solution)/shard_map/finish/pallas_call | solution.py:314
  (5 shorter events, 0.0 us)
Async XLA Ops:
  0.0 6.6 %copy-start.9 = (s32[1,12]{1,0:T(1,128)S(1)}, s32[1,12]{1,0:T(1,128)}, u32[]{:S(2)}) copy-start(s32[1,12]{1,0:T(1,128)} %rest_0_.1) | copy-start | bytes 148
  3.5 19.1 %collective-permute-start.6 = (bf16[512,512]{1,0:T(8,128)(2,1)}, bf16[512,512]{1,0:T(8,128)(2,1)}, u32[]{:S(2)}, u32[]{:S(2)}) collective-permute-start(bf16[512,512]{1,0:T(8,128)(2,1)} %get-tuple-element.18.rest_1_), channel_id=1, source_target_pairs={{0,1},{1,2},{2,3},{3,0},{4,7},{5,4},{6,5},{7,6},{8,9},{9,10},{10,1... | collective-permute-start | bytes 1572872 | tf_op jit(solution)/shard_map/ppermute | solution.py:345
  10.0 21.9 %collective-permute-start.8 = (bf16[512,512]{1,0:T(8,128)(2,1)}, bf16[512,512]{1,0:T(8,128)(2,1)}, u32[]{:S(2)}, u32[]{:S(2)}) collective-permute-start(bf16[512,512]{1,0:T(8,128)(2,1)} %get-tuple-element.20.rest_0_), channel_id=1, source_target_pairs={{0,3},{1,0},{2,1},{3,2},{4,5},{5,6},{6,7},{7,4},{8,11},{9,8},{10,9... | collective-permute-start | bytes 1572872 | tf_op jit(solution)/shard_map/ppermute | solution.py:345
  12.2 4.7 %collective-permute-start = (s32[1,12]{1,0:T(1,128)S(1)}, s32[1,12]{1,0:T(1,128)S(1)}, u32[]{:S(2)}, u32[]{:S(2)}) collective-permute-start(s32[1,12]{1,0:T(1,128)S(1)} %get-tuple-element.19.rest_0_), channel_id=1, source_target_pairs={{0,4},{4,0},{8,12},{12,8},{1,5},{5,1},{9,13},{13,9},{2,6},{6,2},{1... | collective-permute-start | bytes 152 | tf_op jit(solution)/shard_map/ppermute | solution.py:368
  12.2 4.7 %collective-permute-start.1 = (s32[1,12]{1,0:T(1,128)S(1)}, s32[1,12]{1,0:T(1,128)S(1)}, u32[]{:S(2)}, u32[]{:S(2)}) collective-permute-start(s32[1,12]{1,0:T(1,128)S(1)} %get-tuple-element.19.rest_0_), channel_id=1, source_target_pairs={{0,8},{4,12},{8,0},{12,4},{1,9},{5,13},{9,1},{13,5},{2,10},{6,14},... | collective-permute-start | bytes 152 | tf_op jit(solution)/shard_map/ppermute | solution.py:368
  13.8 3.0 %collective-permute-start.2 = (s32[1,12]{1,0:T(1,128)S(1)}, s32[1,12]{1,0:T(1,128)S(1)}, u32[]{:S(2)}, u32[]{:S(2)}) collective-permute-start(s32[1,12]{1,0:T(1,128)S(1)} %get-tuple-element.19.rest_0_), channel_id=1, source_target_pairs={{0,12},{4,8},{8,4},{12,0},{1,13},{5,9},{9,5},{13,1},{2,14},{6,10},... | collective-permute-start | bytes 152 | tf_op jit(solution)/shard_map/ppermute | solution.py:368
  14.0 2.9 %copy-start.8 = (s32[512]{0:T(512)S(1)}, s32[512]{0:T(512)}, u32[]{:S(2)}) copy-start(s32[512]{0:T(512)} %table_ref.1) | copy-start | bytes 6148
  14.0 2.9 %copy-start.10 = (s32[1,12]{1,0:T(1,128)S(1)}, s32[1,12]{1,0:T(1,128)}, u32[]{:S(2)}) copy-start(s32[1,12]{1,0:T(1,128)} %lens_ref.1) | copy-start | bytes 148
  20.6 29.5 %collective-permute-start.3 = (bf16[6,16,3072]{2,1,0:T(8,128)(2,1)S(1)}, bf16[6,16,3072]{2,1,0:T(8,128)(2,1)S(1)}, u32[]{:S(2)}, u32[]{:S(2)}) collective-permute-start(bf16[6,16,3072]{2,1,0:T(8,128)(2,1)S(1)} %get-tuple-element.24), channel_id=1, source_target_pairs={{0,4},{4,0},{8,12},{12,8},{1,5},{5,1},{9,13},{13,9},{2,6},{6,2},{1... | collective-permute-start | bytes 1769480 | tf_op jit(solution)/shard_map/ppermute | solution.py:373
  20.7 29.5 %collective-permute-start.4 = (bf16[6,16,3072]{2,1,0:T(8,128)(2,1)S(1)}, bf16[6,16,3072]{2,1,0:T(8,128)(2,1)S(1)}, u32[]{:S(2)}, u32[]{:S(2)}) collective-permute-start(bf16[6,16,3072]{2,1,0:T(8,128)(2,1)S(1)} %get-tuple-element.25), channel_id=1, source_target_pairs={{0,8},{4,12},{8,0},{12,4},{1,9},{5,13},{9,1},{13,5},{2,10},{6,14},... | collective-permute-start | bytes 1769480 | tf_op jit(solution)/shard_map/ppermute | solution.py:373
  22.5 27.7 %collective-permute-start.5 = (bf16[6,16,3072]{2,1,0:T(8,128)(2,1)S(1)}, bf16[6,16,3072]{2,1,0:T(8,128)(2,1)S(1)}, u32[]{:S(2)}, u32[]{:S(2)}) collective-permute-start(bf16[6,16,3072]{2,1,0:T(8,128)(2,1)S(1)} %get-tuple-element.26), channel_id=1, source_target_pairs={{0,12},{4,8},{8,4},{12,0},{1,13},{5,9},{9,5},{13,1},{2,14},{6,10},... | collective-permute-start | bytes 1769480 | tf_op jit(solution)/shard_map/ppermute | solution.py:373
  25.4 19.1 %collective-permute-start.7 = (bf16[512,512]{1,0:T(8,128)(2,1)S(1)}, bf16[512,512]{1,0:T(8,128)(2,1)S(1)}, u32[]{:S(2)}, u32[]{:S(2)}) collective-permute-start(bf16[512,512]{1,0:T(8,128)(2,1)S(1)} %block_product.10.rest_1_), channel_id=1, source_target_pairs={{0,1},{1,2},{2,3},{3,0},{4,7},{5,4},{6,5},{7,6},{8,9},{9,10},{10,1... | collective-permute-start | bytes 1572872 | tf_op jit(solution)/shard_map/ppermute | solution.py:345
  35.4 26.2 %collective-permute-start.12 = (bf16[512,512]{1,0:T(8,128)(2,1)}, bf16[512,512]{1,0:T(8,128)(2,1)}, u32[]{:S(2)}, u32[]{:S(2)}) collective-permute-start(bf16[512,512]{1,0:T(8,128)(2,1)} %block_product.11.rest_0_), channel_id=1, source_target_pairs={{0,3},{1,0},{2,1},{3,2},{4,5},{5,6},{6,7},{7,4},{8,11},{9,8},{10,9... | collective-permute-start | bytes 1572872 | tf_op jit(solution)/shard_map/ppermute | solution.py:345
  41.8 6.1 %copy-start.6 = (bf16[512,512]{1,0:T(8,128)(2,1)}, bf16[512,512]{1,0:T(8,128)(2,1)S(1)}, u32[]{:S(2)}) copy-start(bf16[512,512]{1,0:T(8,128)(2,1)S(1)} %block_product.12.rest_1_.rest_5_) | copy-start | bytes 1572868
  47.9 24.9 %collective-permute-start.15 = (bf16[512,512]{1,0:T(8,128)(2,1)}, bf16[512,512]{1,0:T(8,128)(2,1)}, u32[]{:S(2)}, u32[]{:S(2)}) collective-permute-start(bf16[512,512]{1,0:T(8,128)(2,1)} %block_product.13.rest_4_), channel_id=1, source_target_pairs={{0,1},{1,2},{2,3},{3,0},{4,7},{5,4},{6,5},{7,6},{8,9},{9,10},{10,1... | collective-permute-start | bytes 1572872 | tf_op jit(solution)/shard_map/ppermute | solution.py:345
  50.2 1.6 %copy-start.2 = (bf16[6,16,3072]{2,1,0:T(8,128)(2,1)}, bf16[6,16,3072]{2,1,0:T(8,128)(2,1)S(1)}, u32[]{:S(2)}) copy-start(bf16[6,16,3072]{2,1,0:T(8,128)(2,1)S(1)} %collective-permute-done.4.rest_2_.rest_8_) | copy-start | bytes 1769476
  50.2 5.9 %copy-start.4 = (bf16[6,16,3072]{2,1,0:T(8,128)(2,1)}, bf16[6,16,3072]{2,1,0:T(8,128)(2,1)S(1)}, u32[]{:S(2)}) copy-start(bf16[6,16,3072]{2,1,0:T(8,128)(2,1)S(1)} %collective-permute-done.5.rest_3_.rest_9_) | copy-start | bytes 1769476
  51.8 0.8 %copy-start = (bf16[6,16,3072]{2,1,0:T(8,128)(2,1)}, bf16[6,16,3072]{2,1,0:T(8,128)(2,1)S(1)}, u32[]{:S(2)}) copy-start(bf16[6,16,3072]{2,1,0:T(8,128)(2,1)S(1)} %collective-permute-done.3.rest_1_.rest_7_) | copy-start | bytes 1769476
  52.6 14.6 %collective-permute-start.9 = (bf16[16,512]{1,0:T(8,128)(2,1)S(1)}, bf16[16,512]{1,0:T(8,128)(2,1)S(1)}, u32[]{:S(2)}, u32[]{:S(2)}) collective-permute-start(bf16[16,512]{1,0:T(8,128)(2,1)S(1)} %low_sums.1.rest_1_.rest_0_), channel_id=1, source_target_pairs={{0,3},{1,2},{2,1},{3,0},{4,7},{5,6},{6,5},{7,4},{8,11},{9,10},{10,... | collective-permute-start | bytes 49160 | tf_op jit(solution)/shard_map/ppermute | solution.py:383
  56.1 15.3 %collective-permute-start.10 = (bf16[16,512]{1,0:T(8,128)(2,1)S(1)}, bf16[16,512]{1,0:T(8,128)(2,1)S(1)}, u32[]{:S(2)}, u32[]{:S(2)}) collective-permute-start(bf16[16,512]{1,0:T(8,128)(2,1)S(1)} %low_sums.1.rest_1_.rest_0_), channel_id=1, source_target_pairs={{0,2},{1,3},{2,0},{3,1},{4,6},{5,7},{6,4},{7,5},{8,10},{9,11},{10,... | collective-permute-start | bytes 49160 | tf_op jit(solution)/shard_map/ppermute | solution.py:383
  57.0 14.4 %collective-permute-start.11 = (bf16[16,512]{1,0:T(8,128)(2,1)S(1)}, bf16[16,512]{1,0:T(8,128)(2,1)S(1)}, u32[]{:S(2)}, u32[]{:S(2)}) collective-permute-start(bf16[16,512]{1,0:T(8,128)(2,1)S(1)} %low_sums.1.rest_1_.rest_0_), channel_id=1, source_target_pairs={{0,1},{1,0},{2,3},{3,2},{4,5},{5,4},{6,7},{7,6},{8,9},{9,8},{10,11... | collective-permute-start | bytes 49160 | tf_op jit(solution)/shard_map/ppermute | solution.py:383
  63.6 11.0 %collective-permute-start.14 = (bf16[512,256]{1,0:T(8,128)(2,1)S(1)}, bf16[512,256]{1,0:T(8,128)(2,1)S(1)}, u32[]{:S(2)}, u32[]{:S(2)}) collective-permute-start(bf16[512,256]{1,0:T(8,128)(2,1)S(1)} %block_product.14.rest_1_), channel_id=1, source_target_pairs={{0,3},{1,0},{2,1},{3,2},{4,5},{5,6},{6,7},{7,4},{8,11},{9,8},{10,9... | collective-permute-start | bytes 786440 | tf_op jit(solution)/shard_map/ppermute | solution.py:345
  63.7 7.8 %copy-start.1 = (bf16[6,16,3072]{2,1,0:T(8,128)(2,1)S(1)}, bf16[6,16,3072]{2,1,0:T(8,128)(2,1)}, u32[]{:S(2)}) copy-start(bf16[6,16,3072]{2,1,0:T(8,128)(2,1)} %copy-done) | copy-start | bytes 1769476
  63.7 7.8 %copy-start.3 = (bf16[6,16,3072]{2,1,0:T(8,128)(2,1)S(1)}, bf16[6,16,3072]{2,1,0:T(8,128)(2,1)}, u32[]{:S(2)}) copy-start(bf16[6,16,3072]{2,1,0:T(8,128)(2,1)} %copy-done.2) | copy-start | bytes 1769476
  63.7 7.8 %copy-start.5 = (bf16[6,16,3072]{2,1,0:T(8,128)(2,1)S(1)}, bf16[6,16,3072]{2,1,0:T(8,128)(2,1)}, u32[]{:S(2)}) copy-start(bf16[6,16,3072]{2,1,0:T(8,128)(2,1)} %copy-done.4) | copy-start | bytes 1769476
  63.7 7.8 %copy-start.7 = (bf16[512,512]{1,0:T(8,128)(2,1)S(1)}, bf16[512,512]{1,0:T(8,128)(2,1)}, u32[]{:S(2)}) copy-start(bf16[512,512]{1,0:T(8,128)(2,1)} %copy-done.6) | copy-start | bytes 1572868
  67.2 11.0 %collective-permute-start.13 = (bf16[512,256]{1,0:T(8,128)(2,1)S(1)}, bf16[512,256]{1,0:T(8,128)(2,1)S(1)}, u32[]{:S(2)}, u32[]{:S(2)}) collective-permute-start(bf16[512,256]{1,0:T(8,128)(2,1)S(1)} %block_product.15.rest_10_), channel_id=1, source_target_pairs={{0,3},{1,0},{2,1},{3,2},{4,5},{5,6},{6,7},{7,4},{8,11},{9,8},{10,9... | collective-permute-start | bytes 786440 | tf_op jit(solution)/shard_map/ppermute | solution.py:345

commit v28 on v26

--- a/solution.py
+++ b/solution.py
@@ -102,7 +102,7 @@
 
 def first_product(rows, weight, first, width):
     row_total, depth = rows.shape
-    chunk = min(512, depth // 2)
+    chunk = depth // 2
     chunks = depth // chunk
     hbm = pl.BlockSpec(memory_space=pltpu.HBM)
     return pl.pallas_call(
@@ -369,7 +369,7 @@
     last = partial(0, 0, after=[last])
     owns = [last]
     packs, starts, ends = pick_adapters(me_req, table, all_ids, lens, down, up, [last])
-    for x in range(1, req_total):
+    for x in reversed(range(1, req_total)):
         packs[x] = lax.ppermute(packs[x], "req", [(i, i ^ x) for i in range(req_total)])
 
     last = starts

time: 79.5 us -> 79.8 us (level)
  no operation moved by 1% of the time
where the time goes in v28:
time: 79.8 us; the launch traced here: 79.4 us
  Pallas kernels  36.3 us (45%)
  starting transfers between devices  31.7 us (40%)
  waiting for transfers between devices  10.2 us (13%)
  local copies, waits for them, and re-layouts  0.85 us (1%)
    pallas_call x8, Pallas kernels, block_product(): pl.pallas_call(functools.partial(product_kernel, len(addends), with_ids),...  22.6 us
    ppermute x7, starting transfers between devices, move(): return lax.ppermute(value, ('req', 'tp'), pairs)  22.4 us
    ppermute x7, waiting for transfers between devices, move(): return lax.ppermute(value, ('req', 'tp'), pairs)  8.85 us
    ppermute x3, starting transfers between devices, local(): lows.append(lax.ppermute(low, 'tp', pairs))  5.5 us
    pallas_call x1, Pallas kernels, first_product(): pl.pallas_call(functools.partial(first_kernel, chunk), in_specs=[pl.Block...  3.73 us
    pallas_call x1, Pallas kernels, pick_adapters(): pl.pallas_call(functools.partial(pick_kernel, peers, len(after)), in_spec...  3.71 us
    pallas_call x3, Pallas kernels, finish(): pl.pallas_call(functools.partial(finish_kernel, 1), grid=(row_total // he...  3.38 us
    ppermute x3, starting transfers between devices, local(): lax.ppermute(packs[x], 'req', [(i, i ^ x) for i in range(req_total)])  1.93 us
  transfers between devices with their start and end apart: 16, of which 4 were waited for; matrix products, arithmetic and copies ran while one was open for 0% of the time, Pallas kernels for 40%

profile of v28, /device:TPU:0, one launch (start us, length us, event | category | flops | bytes accessed | tf_op | source)
XLA Modules:
  0.0 79.4 jit_solution(13014676296276750587)
XLA Ops:
  0.0 3.7 %first_product.1 = (bf16[512,512]{1,0:T(8,128)(2,1)}, bf16[512,2048]{1,0:T(8,128)(2,1)S(1)}) custom-call(s32[1]{0:T(128)} %bitcast.2.first_ref, bf16[512,2048]{1,0:T(8,128)(2,1)} %rows_ref.1, bf16[2048,4096]{1,0:T(8,128)(2,1)} %weight_ref.17), custom_call_target="tpu_custom_call" | custom-call | flops 1000 | bytes 1000 | tf_op jit(solution)/shard_map/first_product/pallas_call | solution.py:108
  3.7 3.1 %collective-permute-start.6 = (bf16[512,512]{1,0:T(8,128)(2,1)}, bf16[512,512]{1,0:T(8,128)(2,1)}, u32[]{:S(2)}, u32[]{:S(2)}) collective-permute-start(bf16[512,512]{1,0:T(8,128)(2,1)} %get-tuple-element.18.rest_1_), channel_id=1, source_target_pairs={{0,1},{1,2},{2,3},{3,0},{4,7},{5,4},{6,5},{7,6},{8,9},{9,10},{10,1... | collective-permute-start | bytes 1572872 | tf_op jit(solution)/shard_map/ppermute | solution.py:345
  6.8 0.0 copy-done.9
  6.8 3.4 %block_product.8 = (bf16[512,512]{1,0:T(8,128)(2,1)}, s32[1,12]{1,0:T(1,128)S(1)}) custom-call(s32[1]{0:T(128)} %bitcast.1.first_ref, bf16[512,2048]{1,0:T(8,128)(2,1)S(1)} %get-tuple-element.17.rows_ref, bf16[2048,4096]{1,0:T(8,128)(2,1)} %weight_ref.17, s32[1,12]{1,0:T(1,128)S(1)} %copy-done.9, bf16[512,512]{1,0:T(8,128)(2,1)} %get-tuple-element.18.rest_1_), custom_call_target="tpu_custom_call" | custom-call | flops 1000 | bytes 1000 | tf_op jit(solution)/shard_map/block_product/pallas_call | solution.py:53
  10.3 2.2 %collective-permute-start.8 = (bf16[512,512]{1,0:T(8,128)(2,1)}, bf16[512,512]{1,0:T(8,128)(2,1)}, u32[]{:S(2)}, u32[]{:S(2)}) collective-permute-start(bf16[512,512]{1,0:T(8,128)(2,1)} %get-tuple-element.20.rest_0_), channel_id=1, source_target_pairs={{0,3},{1,0},{2,1},{3,2},{4,5},{5,6},{6,7},{7,4},{8,11},{9,8},{10,9... | collective-permute-start | bytes 1572872 | tf_op jit(solution)/shard_map/ppermute | solution.py:345
  12.4 0.0 collective-permute-start
  12.4 1.7 %collective-permute-start.1 = (s32[1,12]{1,0:T(1,128)S(1)}, s32[1,12]{1,0:T(1,128)S(1)}, u32[]{:S(2)}, u32[]{:S(2)}) collective-permute-start(s32[1,12]{1,0:T(1,128)S(1)} %get-tuple-element.19.rest_0_), channel_id=1, source_target_pairs={{0,8},{4,12},{8,0},{12,4},{1,9},{5,13},{9,1},{13,5},{2,10},{6,14},... | collective-permute-start | bytes 152 | tf_op jit(solution)/shard_map/ppermute | solution.py:368
  14.1 0.2 collective-permute-start.2
  14.3 2.7 %block_product.9.rest_6_.rest_4_ = bf16[512,512]{1,0:T(8,128)(2,1)S(1)} custom-call(s32[1]{0:T(128)} %bitcast.3.first_ref, bf16[512,2048]{1,0:T(8,128)(2,1)S(1)} %get-tuple-element.17.rows_ref, bf16[2048,4096]{1,0:T(8,128)(2,1)} %weight_ref.17, bf16[512,512]{1,0:T(8,128)(2,1)} %get-tuple-element.20.rest_0_), custom_call_target="tpu_custom_call" | custom-call | flops 1000 | bytes 1000 | tf_op jit(solution)/shard_map/block_product/pallas_call | solution.py:53
  17.1 0.0 collective-permute-done.rest_1_
  17.1 0.0 collective-permute-done.1.rest_2_
  17.1 0.0 collective-permute-done.2.rest_3_
  17.1 0.0 copy-done.8
  17.1 0.0 copy-done.10
  17.2 3.7 %pick_adapters.1 = (bf16[6,16,3072]{2,1,0:T(8,128)(2,1)S(1)}, bf16[6,16,3072]{2,1,0:T(8,128)(2,1)S(1)}, bf16[6,16,3072]{2,1,0:T(8,128)(2,1)S(1)}, bf16[6,16,3072...) custom-call(s32[1]{0:T(128)} %bitcast.me_ref, s32[512]{0:T(512)S(1)} %copy-done.8, s32[1,12]{1,0:T(1,128)S(1)} %copy-done.10, ...), custom_call_target="tpu_custom_call" | custom-call | flops 1000 | bytes 1000 | tf_op jit(solution)/shard_map/pick_adapters/pallas_call | solution.py:199
  20.9 0.3 collective-permute-start.3
  21.2 1.5 %collective-permute-start.4 = (bf16[6,16,3072]{2,1,0:T(8,128)(2,1)S(1)}, bf16[6,16,3072]{2,1,0:T(8,128)(2,1)S(1)}, u32[]{:S(2)}, u32[]{:S(2)}) collective-permute-start(bf16[6,16,3072]{2,1,0:T(8,128)(2,1)S(1)} %get-tuple-element.25), channel_id=1, source_target_pairs={{0,8},{4,12},{8,0},{12,4},{1,9},{5,13},{9,1},{13,5},{2,10},{6,14},... | collective-permute-start | bytes 1769480 | tf_op jit(solution)/shard_map/ppermute | solution.py:373
  22.7 0.1 collective-permute-start.5
  22.8 0.0 collective-permute-done.6.rest_0_
  22.8 2.8 %block_product.10.rest_1_ = bf16[512,512]{1,0:T(8,128)(2,1)S(1)} custom-call(s32[1]{0:T(128)} %bitcast.5.first_ref, bf16[512,2048]{1,0:T(8,128)(2,1)S(1)} %get-tuple-element.17.rows_ref, bf16[2048,4096]{1,0:T(8,128)(2,1)} %weight_ref.17, bf16[512,512]{1,0:T(8,128)(2,1)} %collective-permute-done.6.rest_0_, s32[24]{0:T(128)S(1)} %get-tuple-element.21.rest_1_.start_ref), custom_call_target="tpu_custom_call" | custom-call | flops 1000 | bytes 1000 | tf_op jit(solution)/shard_map/block_product/pallas_call | solution.py:53
  25.6 6.6 %collective-permute-start.7 = (bf16[512,512]{1,0:T(8,128)(2,1)S(1)}, bf16[512,512]{1,0:T(8,128)(2,1)S(1)}, u32[]{:S(2)}, u32[]{:S(2)}) collective-permute-start(bf16[512,512]{1,0:T(8,128)(2,1)S(1)} %block_product.10.rest_1_), channel_id=1, source_target_pairs={{0,1},{1,2},{2,3},{3,0},{4,7},{5,4},{6,5},{7,6},{8,9},{9,10},{10,1... | collective-permute-start | bytes 1572872 | tf_op jit(solution)/shard_map/ppermute | solution.py:345
  32.2 0.0 collective-permute-done.8.rest_0_
  32.2 3.5 %block_product.11.rest_0_ = bf16[512,512]{1,0:T(8,128)(2,1)} custom-call(s32[1]{0:T(128)} %bitcast.7.first_ref, bf16[512,2048]{1,0:T(8,128)(2,1)S(1)} %get-tuple-element.17.rows_ref, bf16[2048,4096]{1,0:T(8,128)(2,1)} %weight_ref.17, bf16[512,512]{1,0:T(8,128)(2,1)} %collective-permute-done.8.rest_0_, bf16[512,512]{1,0:T(8,128)(2,1)S(1)} %block_product.10.rest_1_), custom_call_target="tpu_custom_call" | custom-call | flops 1000 | bytes 1000 | tf_op jit(solution)/shard_map/block_product/pallas_call | solution.py:53
  35.6 3.7 %collective-permute-start.12 = (bf16[512,512]{1,0:T(8,128)(2,1)}, bf16[512,512]{1,0:T(8,128)(2,1)}, u32[]{:S(2)}, u32[]{:S(2)}) collective-permute-start(bf16[512,512]{1,0:T(8,128)(2,1)} %block_product.11.rest_0_), channel_id=1, source_target_pairs={{0,3},{1,0},{2,1},{3,2},{4,5},{5,6},{6,7},{7,4},{8,11},{9,8},{10,9... | collective-permute-start | bytes 1572872 | tf_op jit(solution)/shard_map/ppermute | solution.py:345
  39.3 2.7 %block_product.12.rest_1_.rest_5_ = bf16[512,512]{1,0:T(8,128)(2,1)S(1)} custom-call(s32[1]{0:T(128)} %bitcast.6.first_ref, bf16[512,2048]{1,0:T(8,128)(2,1)S(1)} %get-tuple-element.17.rows_ref, bf16[2048,4096]{1,0:T(8,128)(2,1)} %weight_ref.17, bf16[512,512]{1,0:T(8,128)(2,1)} %block_product.11.rest_0_), custom_call_target="tpu_custom_call" | custom-call | flops 8000000000 | bytes 1000 | tf_op jit(solution)/shard_map/block_product/pallas_call | solution.py:53
  42.0 0.0 copy-start.6
  42.0 2.7 %collective-permute-done.7.rest_0_ = bf16[512,512]{1,0:T(8,128)(2,1)S(1)} collective-permute-done((bf16[512,512]{1,0:T(8,128)(2,1)S(1)}, bf16[512,512]{1,0:T(8,128)(2,1)S(1)}, u32[]{:S(2)}, u32[]{:S(2)}) %collective-permute-start.7) | collective-permute-done | bytes 524320 | tf_op jit(solution)/shard_map/ppermute | solution.py:345
  44.7 3.4 %block_product.13.rest_4_ = bf16[512,512]{1,0:T(8,128)(2,1)} custom-call(s32[1]{0:T(128)} %bitcast.4.first_ref, bf16[512,2048]{1,0:T(8,128)(2,1)S(1)} %get-tuple-element.17.rows_ref, bf16[2048,4096]{1,0:T(8,128)(2,1)} %weight_ref.17, bf16[512,512]{1,0:T(8,128)(2,1)S(1)} %collective-permute-done.7.rest_0_, bf16[512,512]{1,0:T(8,128)(2,1)S(1)} %block_product.12.rest_1_.rest_5_), custom_call_target="tpu_custom_call" | custom-call | flops 1000 | bytes 1000 | tf_op jit(solution)/shard_map/block_product/pallas_call | solution.py:53
  48.1 0.0 copy-done.6
  48.1 2.3 %collective-permute-start.15 = (bf16[512,512]{1,0:T(8,128)(2,1)}, bf16[512,512]{1,0:T(8,128)(2,1)}, u32[]{:S(2)}, u32[]{:S(2)}) collective-permute-start(bf16[512,512]{1,0:T(8,128)(2,1)} %block_product.13.rest_4_), channel_id=1, source_target_pairs={{0,1},{1,2},{2,3},{3,0},{4,7},{5,4},{6,5},{7,6},{8,9},{9,10},{10,1... | collective-permute-start | bytes 1572872 | tf_op jit(solution)/shard_map/ppermute | solution.py:345
  50.4 0.0 collective-permute-done.3.rest_1_.rest_7_
  50.4 0.0 collective-permute-done.4.rest_2_.rest_8_
  50.4 0.0 collective-permute-done.5.rest_3_.rest_9_
  50.4 0.0 copy-start.4
  50.5 1.6 %low_sums.1.rest_1_.rest_0_ = bf16[16,512]{1,0:T(8,128)(2,1)S(1)} custom-call(s32[24]{0:T(128)S(1)} %get-tuple-element.21.rest_1_.start_ref, s32[24]{0:T(128)S(1)} %get-tuple-element.22.end_ref, bf16[512,2048]{1,0:T(8,128)(2,1)S(1)} %get-tuple-element.17.rows_ref, bf16[6,16,3072]{2,1,0:T(8,128)(2,1)S(1)} %get-tuple-element.23.rest_0_.rest_6_, ...), custom_call_target="tpu_custom_call" | custom-call | flops 1000 | bytes 1000 | tf_op jit(solution)/shard_map/low_sums/pallas_call | solution.py:241
  52.0 0.0 copy-done.2
  52.0 0.0 copy-start
  52.0 0.8 %copy-done = bf16[6,16,3072]{2,1,0:T(8,128)(2,1)} copy-done((bf16[6,16,3072]{2,1,0:T(8,128)(2,1)}, bf16[6,16,3072]{2,1,0:T(8,128)(2,1)S(1)}, u32[]{:S(2)}) %copy-start) | copy-done | bytes 589848
  52.8 3.0 %collective-permute-start.9 = (bf16[16,512]{1,0:T(8,128)(2,1)S(1)}, bf16[16,512]{1,0:T(8,128)(2,1)S(1)}, u32[]{:S(2)}, u32[]{:S(2)}) collective-permute-start(bf16[16,512]{1,0:T(8,128)(2,1)S(1)} %low_sums.1.rest_1_.rest_0_), channel_id=1, source_target_pairs={{0,1},{1,0},{2,3},{3,2},{4,5},{5,4},{6,7},{7,6},{8,9},{9,8},{10,11... | collective-permute-start | bytes 49160 | tf_op jit(solution)/shard_map/ppermute | solution.py:383
  55.8 0.0 copy-done.4
  55.8 1.1 %collective-permute-start.10 = (bf16[16,512]{1,0:T(8,128)(2,1)S(1)}, bf16[16,512]{1,0:T(8,128)(2,1)S(1)}, u32[]{:S(2)}, u32[]{:S(2)}) collective-permute-start(bf16[16,512]{1,0:T(8,128)(2,1)S(1)} %low_sums.1.rest_1_.rest_0_), channel_id=1, source_target_pairs={{0,2},{1,3},{2,0},{3,1},{4,6},{5,7},{6,4},{7,5},{8,10},{9,11},{10,... | collective-permute-start | bytes 49160 | tf_op jit(solution)/shard_map/ppermute | solution.py:383
  56.9 1.4 %collective-permute-start.11 = (bf16[16,512]{1,0:T(8,128)(2,1)S(1)}, bf16[16,512]{1,0:T(8,128)(2,1)S(1)}, u32[]{:S(2)}, u32[]{:S(2)}) collective-permute-start(bf16[16,512]{1,0:T(8,128)(2,1)S(1)} %low_sums.1.rest_1_.rest_0_), channel_id=1, source_target_pairs={{0,3},{1,2},{2,1},{3,0},{4,7},{5,6},{6,5},{7,4},{8,11},{9,10},{10,... | collective-permute-start | bytes 49160 | tf_op jit(solution)/shard_map/ppermute | solution.py:383
  58.3 3.5 %collective-permute-done.12.rest_0_ = bf16[512,512]{1,0:T(8,128)(2,1)} collective-permute-done((bf16[512,512]{1,0:T(8,128)(2,1)}, bf16[512,512]{1,0:T(8,128)(2,1)}, u32[]{:S(2)}, u32[]{:S(2)}) %collective-permute-start.12) | collective-permute-done | bytes 524320 | tf_op jit(solution)/shard_map/ppermute | solution.py:345
  61.9 2.0 %block_product.14.rest_1_ = bf16[512,256]{1,0:T(8,128)(2,1)S(1)} custom-call(s32[1]{0:T(128)} %bitcast.9.first_ref, bf16[512,2048]{1,0:T(8,128)(2,1)S(1)} %get-tuple-element.17.rows_ref, bf16[2048,4096]{1,0:T(8,128)(2,1)} %weight_ref.17, bf16[512,512]{1,0:T(8,128)(2,1)} %collective-permute-done.12.rest_0_, bf16[16,512]{1,0:T(8,128)(2,1)S(1)} %low_sums.1.rest_1_.rest_0_), custom_call_target="tpu_custom_call" | custom-call | flops 1000 | bytes 1000 | tf_op jit(solution)/shard_map/block_product/pallas_call | solution.py:53
  63.9 0.1 collective-permute-start.14
  63.9 0.0 copy-start.1
  63.9 0.0 copy-start.3
  63.9 0.0 copy-start.5
  64.0 0.0 copy-start.7
  64.0 2.1 %block_product.15.rest_10_ = bf16[512,256]{1,0:T(8,128)(2,1)S(1)} custom-call(s32[1]{0:T(128)} %bitcast.8.first_ref, bf16[512,2048]{1,0:T(8,128)(2,1)S(1)} %get-tuple-element.17.rows_ref, bf16[2048,4096]{1,0:T(8,128)(2,1)} %weight_ref.17, bf16[512,512]{1,0:T(8,128)(2,1)} %collective-permute-done.12.rest_0_, bf16[512,256]{1,0:T(8,128)(2,1)S(1)} %block_product.14.rest_1_), custom_call_target="tpu_custom_call" | custom-call | flops 1000 | bytes 1000 | tf_op jit(solution)/shard_map/block_product/pallas_call | solution.py:53
  66.1 1.3 %collective-permute-done.9.rest_1_ = bf16[16,512]{1,0:T(8,128)(2,1)S(1)} collective-permute-done((bf16[16,512]{1,0:T(8,128)(2,1)S(1)}, bf16[16,512]{1,0:T(8,128)(2,1)S(1)}, u32[]{:S(2)}, u32[]{:S(2)}) %collective-permute-start.9) | collective-permute-done | bytes 16416 | tf_op jit(solution)/shard_map/ppermute | solution.py:383
  67.4 4.6 %collective-permute-start.13 = (bf16[512,256]{1,0:T(8,128)(2,1)S(1)}, bf16[512,256]{1,0:T(8,128)(2,1)S(1)}, u32[]{:S(2)}, u32[]{:S(2)}) collective-permute-start(bf16[512,256]{1,0:T(8,128)(2,1)S(1)} %block_product.15.rest_10_), channel_id=1, source_target_pairs={{0,3},{1,0},{2,1},{3,2},{4,5},{5,6},{6,7},{7,4},{8,11},{9,8},{10,9... | collective-permute-start | bytes 786440 | tf_op jit(solution)/shard_map/ppermute | solution.py:345
  72.0 0.0 collective-permute-done.10.rest_2_
  72.0 0.0 collective-permute-done.11.rest_3_
  72.0 0.0 copy-done.1
  72.0 0.0 copy-done.3
  72.0 0.0 copy-done.5
  72.0 1.3 %adapter_term.1 = (f32[512,512]{1,0:T(8,128)S(1)}, f32[512,512]{1,0:T(8,128)S(1)}) custom-call(s32[24]{0:T(128)S(1)} %get-tuple-element.21.rest_1_.start_ref, s32[24]{0:T(128)S(1)} %get-tuple-element.22.end_ref, bf16[16,512]{1,0:T(8,128)(2,1)S(1)} %low_sums.1.rest_1_.rest_0_, bf16[16,512]{1,0:T(8,128)(2,1)S(1)} %collective-permute-done.9.rest_1_, ...), custom_call_target="tpu_custom_call" | custom-call | flops 1000 | bytes 1000 | tf_op jit(solution)/shard_map/adapter_term/pallas_call | solution.py:287
  73.3 0.0 collective-permute-done.15.rest_0_
  73.3 1.8 %finish.3.rest_1_ = bf16[512,1024]{1,0:T(8,128)(2,1)} custom-call(f32[512,512]{1,0:T(8,128)S(1)} %get-tuple-element.28.term_ref, bf16[512,512]{1,0:T(8,128)(2,1)} %collective-permute-done.15.rest_0_), custom_call_target="tpu_custom_call" | custom-call | flops 8000000000 | bytes 1000 | tf_op jit(solution)/shard_map/finish/pallas_call | solution.py:314
  75.1 0.0 collective-permute-done.14.rest_0_
  75.1 0.8 finish.4.rest_1_
  75.9 2.6 %collective-permute-done.13.rest_0_ = bf16[512,256]{1,0:T(8,128)(2,1)S(1)} collective-permute-done((bf16[512,256]{1,0:T(8,128)(2,1)S(1)}, bf16[512,256]{1,0:T(8,128)(2,1)S(1)}, u32[]{:S(2)}, u32[]{:S(2)}) %collective-permute-start.13) | collective-permute-done | bytes 262176 | tf_op jit(solution)/shard_map/ppermute | solution.py:345
  78.6 0.8 finish.5
  (5 shorter events, 0.0 us)
Async XLA Ops:
  0.0 6.8 %copy-start.9 = (s32[1,12]{1,0:T(1,128)S(1)}, s32[1,12]{1,0:T(1,128)}, u32[]{:S(2)}) copy-start(s32[1,12]{1,0:T(1,128)} %rest_0_.1) | copy-start | bytes 148
  3.7 19.1 %collective-permute-start.6 = (bf16[512,512]{1,0:T(8,128)(2,1)}, bf16[512,512]{1,0:T(8,128)(2,1)}, u32[]{:S(2)}, u32[]{:S(2)}) collective-permute-start(bf16[512,512]{1,0:T(8,128)(2,1)} %get-tuple-element.18.rest_1_), channel_id=1, source_target_pairs={{0,1},{1,2},{2,3},{3,0},{4,7},{5,4},{6,5},{7,6},{8,9},{9,10},{10,1... | collective-permute-start | bytes 1572872 | tf_op jit(solution)/shard_map/ppermute | solution.py:345
  10.3 21.9 %collective-permute-start.8 = (bf16[512,512]{1,0:T(8,128)(2,1)}, bf16[512,512]{1,0:T(8,128)(2,1)}, u32[]{:S(2)}, u32[]{:S(2)}) collective-permute-start(bf16[512,512]{1,0:T(8,128)(2,1)} %get-tuple-element.20.rest_0_), channel_id=1, source_target_pairs={{0,3},{1,0},{2,1},{3,2},{4,5},{5,6},{6,7},{7,4},{8,11},{9,8},{10,9... | collective-permute-start | bytes 1572872 | tf_op jit(solution)/shard_map/ppermute | solution.py:345
  12.4 4.7 %collective-permute-start = (s32[1,12]{1,0:T(1,128)S(1)}, s32[1,12]{1,0:T(1,128)S(1)}, u32[]{:S(2)}, u32[]{:S(2)}) collective-permute-start(s32[1,12]{1,0:T(1,128)S(1)} %get-tuple-element.19.rest_0_), channel_id=1, source_target_pairs={{0,4},{4,0},{8,12},{12,8},{1,5},{5,1},{9,13},{13,9},{2,6},{6,2},{1... | collective-permute-start | bytes 152 | tf_op jit(solution)/shard_map/ppermute | solution.py:368
  12.4 4.7 %collective-permute-start.1 = (s32[1,12]{1,0:T(1,128)S(1)}, s32[1,12]{1,0:T(1,128)S(1)}, u32[]{:S(2)}, u32[]{:S(2)}) collective-permute-start(s32[1,12]{1,0:T(1,128)S(1)} %get-tuple-element.19.rest_0_), channel_id=1, source_target_pairs={{0,8},{4,12},{8,0},{12,4},{1,9},{5,13},{9,1},{13,5},{2,10},{6,14},... | collective-permute-start | bytes 152 | tf_op jit(solution)/shard_map/ppermute | solution.py:368
  14.1 3.1 %collective-permute-start.2 = (s32[1,12]{1,0:T(1,128)S(1)}, s32[1,12]{1,0:T(1,128)S(1)}, u32[]{:S(2)}, u32[]{:S(2)}) collective-permute-start(s32[1,12]{1,0:T(1,128)S(1)} %get-tuple-element.19.rest_0_), channel_id=1, source_target_pairs={{0,12},{4,8},{8,4},{12,0},{1,13},{5,9},{9,5},{13,1},{2,14},{6,10},... | collective-permute-start | bytes 152 | tf_op jit(solution)/shard_map/ppermute | solution.py:368
  14.3 2.9 %copy-start.8 = (s32[512]{0:T(512)S(1)}, s32[512]{0:T(512)}, u32[]{:S(2)}) copy-start(s32[512]{0:T(512)} %table_ref.1) | copy-start | bytes 6148
  14.3 2.9 %copy-start.10 = (s32[1,12]{1,0:T(1,128)S(1)}, s32[1,12]{1,0:T(1,128)}, u32[]{:S(2)}) copy-start(s32[1,12]{1,0:T(1,128)} %lens_ref.1) | copy-start | bytes 148
  20.9 29.6 %collective-permute-start.3 = (bf16[6,16,3072]{2,1,0:T(8,128)(2,1)S(1)}, bf16[6,16,3072]{2,1,0:T(8,128)(2,1)S(1)}, u32[]{:S(2)}, u32[]{:S(2)}) collective-permute-start(bf16[6,16,3072]{2,1,0:T(8,128)(2,1)S(1)} %get-tuple-element.24), channel_id=1, source_target_pairs={{0,4},{4,0},{8,12},{12,8},{1,5},{5,1},{9,13},{13,9},{2,6},{6,2},{1... | collective-permute-start | bytes 1769480 | tf_op jit(solution)/shard_map/ppermute | solution.py:373
  21.2 29.3 %collective-permute-start.4 = (bf16[6,16,3072]{2,1,0:T(8,128)(2,1)S(1)}, bf16[6,16,3072]{2,1,0:T(8,128)(2,1)S(1)}, u32[]{:S(2)}, u32[]{:S(2)}) collective-permute-start(bf16[6,16,3072]{2,1,0:T(8,128)(2,1)S(1)} %get-tuple-element.25), channel_id=1, source_target_pairs={{0,8},{4,12},{8,0},{12,4},{1,9},{5,13},{9,1},{13,5},{2,10},{6,14},... | collective-permute-start | bytes 1769480 | tf_op jit(solution)/shard_map/ppermute | solution.py:373
  22.7 27.7 %collective-permute-start.5 = (bf16[6,16,3072]{2,1,0:T(8,128)(2,1)S(1)}, bf16[6,16,3072]{2,1,0:T(8,128)(2,1)S(1)}, u32[]{:S(2)}, u32[]{:S(2)}) collective-permute-start(bf16[6,16,3072]{2,1,0:T(8,128)(2,1)S(1)} %get-tuple-element.26), channel_id=1, source_target_pairs={{0,12},{4,8},{8,4},{12,0},{1,13},{5,9},{9,5},{13,1},{2,14},{6,10},... | collective-permute-start | bytes 1769480 | tf_op jit(solution)/shard_map/ppermute | solution.py:373
  25.6 19.1 %collective-permute-start.7 = (bf16[512,512]{1,0:T(8,128)(2,1)S(1)}, bf16[512,512]{1,0:T(8,128)(2,1)S(1)}, u32[]{:S(2)}, u32[]{:S(2)}) collective-permute-start(bf16[512,512]{1,0:T(8,128)(2,1)S(1)} %block_product.10.rest_1_), channel_id=1, source_target_pairs={{0,1},{1,2},{2,3},{3,0},{4,7},{5,4},{6,5},{7,6},{8,9},{9,10},{10,1... | collective-permute-start | bytes 1572872 | tf_op jit(solution)/shard_map/ppermute | solution.py:345
  35.6 26.2 %collective-permute-start.12 = (bf16[512,512]{1,0:T(8,128)(2,1)}, bf16[512,512]{1,0:T(8,128)(2,1)}, u32[]{:S(2)}, u32[]{:S(2)}) collective-permute-start(bf16[512,512]{1,0:T(8,128)(2,1)} %block_product.11.rest_0_), channel_id=1, source_target_pairs={{0,3},{1,0},{2,1},{3,2},{4,5},{5,6},{6,7},{7,4},{8,11},{9,8},{10,9... | collective-permute-start | bytes 1572872 | tf_op jit(solution)/shard_map/ppermute | solution.py:345
  42.0 6.1 %copy-start.6 = (bf16[512,512]{1,0:T(8,128)(2,1)}, bf16[512,512]{1,0:T(8,128)(2,1)S(1)}, u32[]{:S(2)}) copy-start(bf16[512,512]{1,0:T(8,128)(2,1)S(1)} %block_product.12.rest_1_.rest_5_) | copy-start | bytes 1572868
  48.1 25.2 %collective-permute-start.15 = (bf16[512,512]{1,0:T(8,128)(2,1)}, bf16[512,512]{1,0:T(8,128)(2,1)}, u32[]{:S(2)}, u32[]{:S(2)}) collective-permute-start(bf16[512,512]{1,0:T(8,128)(2,1)} %block_product.13.rest_4_), channel_id=1, source_target_pairs={{0,1},{1,2},{2,3},{3,0},{4,7},{5,4},{6,5},{7,6},{8,9},{9,10},{10,1... | collective-permute-start | bytes 1572872 | tf_op jit(solution)/shard_map/ppermute | solution.py:345
  50.4 1.6 %copy-start.2 = (bf16[6,16,3072]{2,1,0:T(8,128)(2,1)}, bf16[6,16,3072]{2,1,0:T(8,128)(2,1)S(1)}, u32[]{:S(2)}) copy-start(bf16[6,16,3072]{2,1,0:T(8,128)(2,1)S(1)} %collective-permute-done.4.rest_2_.rest_8_) | copy-start | bytes 1769476
  50.4 5.4 %copy-start.4 = (bf16[6,16,3072]{2,1,0:T(8,128)(2,1)}, bf16[6,16,3072]{2,1,0:T(8,128)(2,1)S(1)}, u32[]{:S(2)}) copy-start(bf16[6,16,3072]{2,1,0:T(8,128)(2,1)S(1)} %collective-permute-done.5.rest_3_.rest_9_) | copy-start | bytes 1769476
  52.0 0.8 %copy-start = (bf16[6,16,3072]{2,1,0:T(8,128)(2,1)}, bf16[6,16,3072]{2,1,0:T(8,128)(2,1)S(1)}, u32[]{:S(2)}) copy-start(bf16[6,16,3072]{2,1,0:T(8,128)(2,1)S(1)} %collective-permute-done.3.rest_1_.rest_7_) | copy-start | bytes 1769476
  52.8 14.6 %collective-permute-start.9 = (bf16[16,512]{1,0:T(8,128)(2,1)S(1)}, bf16[16,512]{1,0:T(8,128)(2,1)S(1)}, u32[]{:S(2)}, u32[]{:S(2)}) collective-permute-start(bf16[16,512]{1,0:T(8,128)(2,1)S(1)} %low_sums.1.rest_1_.rest_0_), channel_id=1, source_target_pairs={{0,1},{1,0},{2,3},{3,2},{4,5},{5,4},{6,7},{7,6},{8,9},{9,8},{10,11... | collective-permute-start | bytes 49160 | tf_op jit(solution)/shard_map/ppermute | solution.py:383
  55.8 16.2 %collective-permute-start.10 = (bf16[16,512]{1,0:T(8,128)(2,1)S(1)}, bf16[16,512]{1,0:T(8,128)(2,1)S(1)}, u32[]{:S(2)}, u32[]{:S(2)}) collective-permute-start(bf16[16,512]{1,0:T(8,128)(2,1)S(1)} %low_sums.1.rest_1_.rest_0_), channel_id=1, source_target_pairs={{0,2},{1,3},{2,0},{3,1},{4,6},{5,7},{6,4},{7,5},{8,10},{9,11},{10,... | collective-permute-start | bytes 49160 | tf_op jit(solution)/shard_map/ppermute | solution.py:383
  56.9 15.1 %collective-permute-start.11 = (bf16[16,512]{1,0:T(8,128)(2,1)S(1)}, bf16[16,512]{1,0:T(8,128)(2,1)S(1)}, u32[]{:S(2)}, u32[]{:S(2)}) collective-permute-start(bf16[16,512]{1,0:T(8,128)(2,1)S(1)} %low_sums.1.rest_1_.rest_0_), channel_id=1, source_target_pairs={{0,3},{1,2},{2,1},{3,0},{4,7},{5,6},{6,5},{7,4},{8,11},{9,10},{10,... | collective-permute-start | bytes 49160 | tf_op jit(solution)/shard_map/ppermute | solution.py:383
  63.9 11.3 %collective-permute-start.14 = (bf16[512,256]{1,0:T(8,128)(2,1)S(1)}, bf16[512,256]{1,0:T(8,128)(2,1)S(1)}, u32[]{:S(2)}, u32[]{:S(2)}) collective-permute-start(bf16[512,256]{1,0:T(8,128)(2,1)S(1)} %block_product.14.rest_1_), channel_id=1, source_target_pairs={{0,3},{1,0},{2,1},{3,2},{4,5},{5,6},{6,7},{7,4},{8,11},{9,8},{10,9... | collective-permute-start | bytes 786440 | tf_op jit(solution)/shard_map/ppermute | solution.py:345
  63.9 8.1 %copy-start.1 = (bf16[6,16,3072]{2,1,0:T(8,128)(2,1)S(1)}, bf16[6,16,3072]{2,1,0:T(8,128)(2,1)}, u32[]{:S(2)}) copy-start(bf16[6,16,3072]{2,1,0:T(8,128)(2,1)} %copy-done) | copy-start | bytes 1769476
  63.9 8.1 %copy-start.3 = (bf16[6,16,3072]{2,1,0:T(8,128)(2,1)S(1)}, bf16[6,16,3072]{2,1,0:T(8,128)(2,1)}, u32[]{:S(2)}) copy-start(bf16[6,16,3072]{2,1,0:T(8,128)(2,1)} %copy-done.2) | copy-start | bytes 1769476
  63.9 8.1 %copy-start.5 = (bf16[6,16,3072]{2,1,0:T(8,128)(2,1)S(1)}, bf16[6,16,3072]{2,1,0:T(8,128)(2,1)}, u32[]{:S(2)}) copy-start(bf16[6,16,3072]{2,1,0:T(8,128)(2,1)} %copy-done.4) | copy-start | bytes 1769476
  64.0 8.1 %copy-start.7 = (bf16[512,512]{1,0:T(8,128)(2,1)S(1)}, bf16[512,512]{1,0:T(8,128)(2,1)}, u32[]{:S(2)}) copy-start(bf16[512,512]{1,0:T(8,128)(2,1)} %copy-done.6) | copy-start | bytes 1572868
  67.4 11.2 %collective-permute-start.13 = (bf16[512,256]{1,0:T(8,128)(2,1)S(1)}, bf16[512,256]{1,0:T(8,128)(2,1)S(1)}, u32[]{:S(2)}, u32[]{:S(2)}) collective-permute-start(bf16[512,256]{1,0:T(8,128)(2,1)S(1)} %block_product.15.rest_10_), channel_id=1, source_target_pairs={{0,3},{1,0},{2,1},{3,2},{4,5},{5,6},{6,7},{7,4},{8,11},{9,8},{10,9... | collective-permute-start | bytes 786440 | tf_op jit(solution)/shard_map/ppermute | solution.py:345
